TPU v7x, 32 devices: a whole 2x2x4 slice. The times are simulated.
32 devices in a mesh: dp: 2 (over x), dep: 4 (over z), hgt: 4 (over y, core).
Axes of the slice: x: 2, y: 2, z: 4, core: 2. Of those that a mesh axis runs over, the one named last changes fastest.
Arguments:
- volume: bfloat16 [2, 32, 8, 32, 128], P('dp', None, 'dep', 'hgt'), may hold values from -6 to 6
- kernel_first: bfloat16 [27, 64, 32], replicated, may hold values from -0.21875 to 0.21875
- kernel_second: bfloat16 [27, 128, 64], replicated, may hold values from -0.15625 to 0.15625
- cotangent: bfloat16 [2, 128, 8, 32, 128], P('dp', None, 'dep', 'hgt'), may hold values from -0.03125 to 0.03125
Outputs:
- features: bfloat16 [2, 128, 8, 32, 128], P('dp', None, 'dep', 'hgt')
- grad_first: float32 [27, 64, 32], P(None, 'dp')
- grad_second: float32 [27, 128, 64], P(None, 'dp')
All inputs are finite; a program needn't handle non-finite values.
Results may differ from a plain program's by a relative error of at most 0.0049.
Values may be sent and summed in bfloat16 or wider, within the bound.
No kernel may reach another device: no remote copies, remote signals or barrier semaphores. Data moves between devices by JAX's collectives and lax.ppermute only.
A program may use at most 64 MiB of HBM per device.

v0:
```python
import jax
import jax.numpy as jnp
from jax import lax
from jax.sharding import PartitionSpec as P

OFFSETS = [
    (first, second, third) for first in (-1, 0, 1) for second in (-1, 0, 1) for third in (-1, 0, 1)
]


def extended_2(x, sides, width):
    for axis, dim in sides:
        size, length = (lax.axis_size(axis), x.shape[dim])
        up = [(i, (i + 1) % size) for i in range(size - 1)]
        down = [(j, i) for i, j in up]
        last = lax.slice_in_dim(x, length - width, length, axis=dim)
        leading = lax.slice_in_dim(x, 0, width, axis=dim)
        before = lax.ppermute(last, axis, up)
        after = lax.ppermute(leading, axis, down)
        x = jnp.concatenate([before, x, after], axis=dim)
    return x


def widen(field):
    return jnp.pad(field, ((0, 0), (0, 0), (0, 0), (0, 0), (1, 1)))


def window(padded, shift_d, shift_h, shift_w, depth, height, width):
    return padded[
        :,
        :,
        1 + shift_d : 1 + shift_d + depth,
        1 + shift_h : 1 + shift_h + height,
        1 + shift_w : 1 + shift_w + width,
    ]


def convolve(extended, kernel, depth, height, width):
    padded = widen(extended)
    total = None
    for number, shift in enumerate(OFFSETS):
        piece = window(padded, shift[0], shift[1], shift[2], depth, height, width)
        term = jnp.einsum(
            "oi,bidhw->bodhw", kernel[number], piece, preferred_element_type=jnp.float32
        )
        total = term if total is None else total + term
    return total


def kernel_grad(upstream, extended, depth, height, width):
    padded = widen(extended)
    parts = []
    for shift in OFFSETS:
        piece = window(padded, shift[0], shift[1], shift[2], depth, height, width)
        parts.append(
            jnp.einsum("bodhw,bidhw->oi", upstream, piece, preferred_element_type=jnp.float32)
        )
    return jnp.stack(parts)


def per_device(volume, kernel_first, kernel_second, cotangent):
    depth, height, width = (volume.shape[2], volume.shape[3], volume.shape[4])
    vol_rim = extended_2(volume, (("dep", 2), ("hgt", 3)), 1)
    pre = convolve(vol_rim, kernel_first, depth, height, width)
    hidden = jax.nn.silu(pre).astype(jnp.bfloat16)
    hidden_rim = extended_2(hidden, (("dep", 2), ("hgt", 3)), 1)
    features = convolve(hidden_rim, kernel_second, depth, height, width).astype(jnp.bfloat16)
    cot_rim = extended_2(cotangent, (("dep", 2), ("hgt", 3)), 1)
    grad_second = kernel_grad(cotangent, hidden_rim, depth, height, width)
    padded_cot = widen(cot_rim)
    back = None
    for number, shift in enumerate(OFFSETS):
        piece = window(padded_cot, -shift[0], -shift[1], -shift[2], depth, height, width)
        term = jnp.einsum(
            "oi,bodhw->bidhw", kernel_second[number], piece, preferred_element_type=jnp.float32
        )
        back = term if back is None else back + term
    sigma = jax.nn.sigmoid(pre)
    delta = (back * (sigma * (1.0 + pre * (1.0 - sigma)))).astype(jnp.bfloat16)
    grad_first = kernel_grad(delta, vol_rim, depth, height, width)
    summed = lax.psum((grad_first, grad_second), ("dep", "hgt"))
    grad_first, grad_second = (
        lax.psum_scatter(summed[0], "dp", scatter_dimension=1, tiled=True),
        lax.psum_scatter(summed[1], "dp", scatter_dimension=1, tiled=True),
    )
    return (features, grad_first, grad_second)


def solution(mesh):
    placed = (P("dp", None, "dep", "hgt", None), P(), P(), P("dp", None, "dep", "hgt", None))
    return jax.shard_map(
        per_device,
        mesh=mesh,
        in_specs=placed,
        out_specs=(P("dp", None, "dep", "hgt", None), P(None, "dp", None), P(None, "dp", None)),
        check_vma=False,
    )
```

profile of v0, /device:TPU:0, one launch (start us, length us, event | category | flops | bytes accessed | tf_op | source)
XLA Modules:
  0.0 259.4 jit_solution(10118163500701807690)
XLA Ops:
  8.2 5.1 %collective-permute-start = (bf16[1,32,1,8,128]{4,1,3,2,0:T(8,128)(2,1)S(1)}, bf16[1,32,1,8,128]{4,1,3,2,0:T(8,128)(2,1)S(1)}, u32[]{:S(2)}, u32[]{:S(2)}) collective-permute-start(bf16[1,32,1,8,128]{4,1,3,2,0:T(8,128)(2,1)S(1)} %get-tuple-element.24), channel_id=1, source_target_pairs={{0,4},{4,8},{8,12},{1,5},{5,9},{9,13},{2,6},{6,10},{10,14},{3,7},{... | collective-permute-start | bytes 196616 | tf_op jit(solution)/shard_map/ppermute | solution.py:18
  15.9 4.6 %collective-permute-start.8 = (bf16[1,128,1,8,128]{4,1,3,2,0:T(8,128)(2,1)S(1)}, bf16[1,128,1,8,128]{4,1,3,2,0:T(8,128)(2,1)S(1)}, u32[]{:S(2)}, u32[]{:S(2)}) collective-permute-start(bf16[1,128,1,8,128]{4,1,3,2,0:T(8,128)(2,1)S(1)} %get-tuple-element.14), channel_id=1, source_target_pairs={{0,4},{4,8},{8,12},{1,5},{5,9},{9,13},{2,6},{6,10},{10,14},{3,7},{... | collective-permute-start | bytes 786440 | tf_op jit(solution)/shard_map/ppermute | solution.py:18
  23.2 3.0 %collective-permute-start.2 = (bf16[1,32,4,1,128]{4,1,3,2,0:T(8,128)(2,1)S(1)}, bf16[1,32,4,1,128]{4,1,3,2,0:T(8,128)(2,1)S(1)}, u32[]{:S(2)}, u32[]{:S(2)}) collective-permute-start(bf16[1,32,4,1,128]{4,1,3,2,0:T(8,128)(2,1)S(1)} %get-tuple-element.21), channel_id=1, source_target_pairs={{0,1},{1,2},{2,3},{4,5},{5,6},{6,7},{8,9},{9,10},{10,11},{12,13},{... | collective-permute-start | bytes 98312 | tf_op jit(solution)/shard_map/ppermute | solution.py:18
  36.6 5.2 %collective-permute-start.4 = (bf16[1,64,1,8,128]{4,1,3,2,0:T(8,128)(2,1)S(1)}, bf16[1,64,1,8,128]{4,1,3,2,0:T(8,128)(2,1)S(1)}, u32[]{:S(2)}, u32[]{:S(2)}) collective-permute-start(bf16[1,64,1,8,128]{4,1,3,2,0:T(8,128)(2,1)S(1)} %get-tuple-element.19), channel_id=1, source_target_pairs={{0,4},{4,8},{8,12},{1,5},{5,9},{9,13},{2,6},{6,10},{10,14},{3,7},{... | collective-permute-start | bytes 393224 | tf_op jit(solution)/shard_map/ppermute | solution.py:18
  43.7 1.7 collective-permute-done.4
  46.7 3.0 %collective-permute-start.6 = (bf16[1,64,4,1,128]{4,1,3,2,0:T(8,128)(2,1)S(1)}, bf16[1,64,4,1,128]{4,1,3,2,0:T(8,128)(2,1)S(1)}, u32[]{:S(2)}, u32[]{:S(2)}) collective-permute-start(bf16[1,64,4,1,128]{4,1,3,2,0:T(8,128)(2,1)S(1)} %get-tuple-element.17), channel_id=1, source_target_pairs={{0,1},{1,2},{2,3},{4,5},{5,6},{6,7},{8,9},{9,10},{10,11},{12,13},{... | collective-permute-start | bytes 196616 | tf_op jit(solution)/shard_map/ppermute | solution.py:18
  51.7 4.8 %collective-permute-start.10 = (bf16[1,128,4,1,128]{4,1,3,2,0:T(8,128)(2,1)S(1)}, bf16[1,128,4,1,128]{4,1,3,2,0:T(8,128)(2,1)S(1)}, u32[]{:S(2)}, u32[]{:S(2)}) collective-permute-start(bf16[1,128,4,1,128]{4,1,3,2,0:T(8,128)(2,1)S(1)} %get-tuple-element.11), channel_id=1, source_target_pairs={{0,1},{1,2},{2,3},{4,5},{5,6},{6,7},{8,9},{9,10},{10,11},{12,13},{... | collective-permute-start | bytes 393224 | tf_op jit(solution)/shard_map/ppermute | solution.py:18
  77.9 2.0 fusion.5
  109.8 2.9 %copy.201 = f32[27,64,32]{2,0,1:T(8,128)} copy(f32[27,64,32]{1,2,0:T(8,128)} %fusion.86) | data formatting | bytes 442368
  112.7 2.3 reshape.675
  115.0 2.3 convolution_bitcast_fusion.6
  117.3 4.0 %copy.203 = f32[27,128,64]{2,0,1:T(8,128)} copy(f32[27,128,64]{1,2,0:T(8,128)} %copy-done.10) | data formatting | bytes 1769472
  121.3 2.9 %reshape.677 = f32[128,1728]{1,0:T(8,128)} reshape(f32[128,27,64]{2,1,0:T(8,128)} %bitcast.1536) | data formatting | bytes 1769472
  124.2 2.1 convolution_bitcast_fusion.7
  126.3 2.1 convolution_add_fusion.6
  128.7 2.1 convolution_bitcast_fusion.8
  130.8 2.2 convolution_bitcast_fusion.9
  141.9 8.6 %reduce-scatter.9.cloned.1.call-done = f32[64,1728]{1,0:T(8,128)} async-done(((f32[128,1728]{1,0:T(8,128)}), f32[64,1728]{1,0:T(8,128)}) %reduce-scatter.9.cloned.1.call-update) | async-done | bytes 442384
  150.5 2.4 reshape.678
  153.0 2.7 %copy.204 = f32[27,64,64]{1,2,0:T(8,128)} copy(f32[27,64,64]{2,0,1:T(8,128)} %bitcast.1566) | data formatting | bytes 884736
  155.7 5.0 %fusion.27 = bf16[1,128,2,8,128]{1,4,3,2,0:T(8,128)(2,1)} fusion(f32[1,128,2,8,128]{1,4,3,2,0:T(8,128)S(1)} %copy-done.1, f32[1,128,2,8,128]{1,4,3,2,0:T(8,128)} %convolution_bitcast_fusion.1, f32[1,128,2,8,128]{1,4,3,2,0:T(8,128)} %convolution_bitcast_fusion.2, f32[1,128,2,8,128]{1,4,3,2,0:T(8,128)} %convolution_bitcast_fusion.3, ...), kind=kOutput, calls=%fused_computation.64 | convolution fusion | flops 36700160 | bytes 12337152 | tf_op jit(solution)/shard_map/oi,bidhw->bodhw/dot_general | solution.py:43
  160.7 2.2 copy.90
  163.0 86.6 %all-reduce.6.cloned.1.call-done = (f32[27,32,32]{1,2,0:T(8,128)}, f32[27,64,64]{1,2,0:T(8,128)}) async-done(((f32[27,32,32]{1,2,0:T(8,128)}, f32[27,64,64]{1,2,0:T(8,128)}), (f32[27,32,32]{1,2,0:T(8,128)}, f32[27,64,64]{1,2,0:T(8,128)})) %all-reduce.6.cloned.1.call-update) | async-done | bytes 552976 | tf_op jit(solution)/shard_map/psum | solution.py:81
  249.6 2.0 copy.91
  (197 shorter events, 82.8 us)
Async XLA Ops:
  7.2 132.6 %reduce-scatter.7.cloned.1.call-start = ((), (), s32[]{:S(2)}) async-start(), calls=%async_computation.2 | async-start | bytes 344064
  8.2 13.7 %copy-start.7 = (bf16[1,32,2,8,128]{4,3,2,1,0:T(8,128)(2,1)S(1)}, bf16[1,32,2,8,128]{4,3,2,1,0:T(8,128)(2,1)}, u32[]{:S(2)}) copy-start(bf16[1,32,2,8,128]{4,3,2,1,0:T(8,128)(2,1)} %param.4) | copy-start | bytes 393220
  8.2 13.6 %collective-permute-start = (bf16[1,32,1,8,128]{4,1,3,2,0:T(8,128)(2,1)S(1)}, bf16[1,32,1,8,128]{4,1,3,2,0:T(8,128)(2,1)S(1)}, u32[]{:S(2)}, u32[]{:S(2)}) collective-permute-start(bf16[1,32,1,8,128]{4,1,3,2,0:T(8,128)(2,1)S(1)} %get-tuple-element.24), channel_id=1, source_target_pairs={{0,4},{4,8},{8,12},{1,5},{5,9},{9,13},{2,6},{6,10},{10,14},{3,7},{... | collective-permute-start | bytes 196616 | tf_op jit(solution)/shard_map/ppermute | solution.py:18
  13.3 13.0 %copy-start.11 = (bf16[27,64,32]{1,2,0:T(8,128)(2,1)S(1)}, bf16[27,64,32]{1,2,0:T(8,128)(2,1)}, u32[]{:S(2)}) copy-start(bf16[27,64,32]{1,2,0:T(8,128)(2,1)} %param.5) | copy-start | bytes 331780
  13.3 8.6 %collective-permute-start.1 = (bf16[1,32,1,8,128]{4,1,3,2,0:T(8,128)(2,1)S(1)}, bf16[1,32,1,8,128]{4,1,3,2,0:T(8,128)(2,1)S(1)}, u32[]{:S(2)}, u32[]{:S(2)}) collective-permute-start(bf16[1,32,1,8,128]{4,1,3,2,0:T(8,128)(2,1)S(1)} %get-tuple-element.23), channel_id=1, source_target_pairs={{4,0},{8,4},{12,8},{5,1},{9,5},{13,9},{6,2},{10,6},{14,10},{7,3},{... | collective-permute-start | bytes 196616 | tf_op jit(solution)/shard_map/ppermute | solution.py:19
  15.9 34.1 %collective-permute-start.8 = (bf16[1,128,1,8,128]{4,1,3,2,0:T(8,128)(2,1)S(1)}, bf16[1,128,1,8,128]{4,1,3,2,0:T(8,128)(2,1)S(1)}, u32[]{:S(2)}, u32[]{:S(2)}) collective-permute-start(bf16[1,128,1,8,128]{4,1,3,2,0:T(8,128)(2,1)S(1)} %get-tuple-element.14), channel_id=1, source_target_pairs={{0,4},{4,8},{8,12},{1,5},{5,9},{9,13},{2,6},{6,10},{10,14},{3,7},{... | collective-permute-start | bytes 786440 | tf_op jit(solution)/shard_map/ppermute | solution.py:18
  20.5 29.8 %collective-permute-start.9 = (bf16[1,128,1,8,128]{4,1,3,2,0:T(8,128)(2,1)S(1)}, bf16[1,128,1,8,128]{4,1,3,2,0:T(8,128)(2,1)S(1)}, u32[]{:S(2)}, u32[]{:S(2)}) collective-permute-start(bf16[1,128,1,8,128]{4,1,3,2,0:T(8,128)(2,1)S(1)} %get-tuple-element.13), channel_id=1, source_target_pairs={{4,0},{8,4},{12,8},{5,1},{9,5},{13,9},{6,2},{10,6},{14,10},{7,3},{... | collective-permute-start | bytes 786440 | tf_op jit(solution)/shard_map/ppermute | solution.py:19
  21.9 4.6 %collective-permute-start.3 = (bf16[1,32,4,1,128]{4,1,3,2,0:T(8,128)(2,1)S(1)}, bf16[1,32,4,1,128]{4,1,3,2,0:T(8,128)(2,1)S(1)}, u32[]{:S(2)}, u32[]{:S(2)}) collective-permute-start(bf16[1,32,4,1,128]{4,1,3,2,0:T(8,128)(2,1)S(1)} %get-tuple-element.22), channel_id=1, source_target_pairs={{1,0},{2,1},{3,2},{5,4},{6,5},{7,6},{9,8},{10,9},{11,10},{13,12},{... | collective-permute-start | bytes 98312 | tf_op jit(solution)/shard_map/ppermute | solution.py:19
  23.2 3.9 %collective-permute-start.2 = (bf16[1,32,4,1,128]{4,1,3,2,0:T(8,128)(2,1)S(1)}, bf16[1,32,4,1,128]{4,1,3,2,0:T(8,128)(2,1)S(1)}, u32[]{:S(2)}, u32[]{:S(2)}) collective-permute-start(bf16[1,32,4,1,128]{4,1,3,2,0:T(8,128)(2,1)S(1)} %get-tuple-element.21), channel_id=1, source_target_pairs={{0,1},{1,2},{2,3},{4,5},{5,6},{6,7},{8,9},{9,10},{10,11},{12,13},{... | collective-permute-start | bytes 98312 | tf_op jit(solution)/shard_map/ppermute | solution.py:18
  34.7 7.2 %copy-start = (bf16[1,128,2,8,128]{4,3,2,1,0:T(8,128)(2,1)S(1)}, bf16[1,128,2,8,128]{4,3,2,1,0:T(8,128)(2,1)}, u32[]{:S(2)}) copy-start(bf16[1,128,2,8,128]{4,3,2,1,0:T(8,128)(2,1)} %param.7) | copy-start | bytes 1572868
  34.7 7.2 %copy-start.8 = (bf16[27,128,64]{1,2,0:T(8,128)(2,1)S(1)}, bf16[27,128,64]{1,2,0:T(8,128)(2,1)}, u32[]{:S(2)}) copy-start(bf16[27,128,64]{1,2,0:T(8,128)(2,1)} %param.6) | copy-start | bytes 1327108
  35.3 8.3 %collective-permute-start.5 = (bf16[1,64,1,8,128]{4,1,3,2,0:T(8,128)(2,1)S(1)}, bf16[1,64,1,8,128]{4,1,3,2,0:T(8,128)(2,1)S(1)}, u32[]{:S(2)}, u32[]{:S(2)}) collective-permute-start(bf16[1,64,1,8,128]{4,1,3,2,0:T(8,128)(2,1)S(1)} %get-tuple-element.20), channel_id=1, source_target_pairs={{4,0},{8,4},{12,8},{5,1},{9,5},{13,9},{6,2},{10,6},{14,10},{7,3},{... | collective-permute-start | bytes 393224 | tf_op jit(solution)/shard_map/ppermute | solution.py:19
  36.6 8.7 %collective-permute-start.4 = (bf16[1,64,1,8,128]{4,1,3,2,0:T(8,128)(2,1)S(1)}, bf16[1,64,1,8,128]{4,1,3,2,0:T(8,128)(2,1)S(1)}, u32[]{:S(2)}, u32[]{:S(2)}) collective-permute-start(bf16[1,64,1,8,128]{4,1,3,2,0:T(8,128)(2,1)S(1)} %get-tuple-element.19), channel_id=1, source_target_pairs={{0,4},{4,8},{8,12},{1,5},{5,9},{9,13},{2,6},{6,10},{10,14},{3,7},{... | collective-permute-start | bytes 393224 | tf_op jit(solution)/shard_map/ppermute | solution.py:18
  45.4 11.3 %collective-permute-start.7 = (bf16[1,64,4,1,128]{4,1,3,2,0:T(8,128)(2,1)S(1)}, bf16[1,64,4,1,128]{4,1,3,2,0:T(8,128)(2,1)S(1)}, u32[]{:S(2)}, u32[]{:S(2)}) collective-permute-start(bf16[1,64,4,1,128]{4,1,3,2,0:T(8,128)(2,1)S(1)} %get-tuple-element.18), channel_id=1, source_target_pairs={{1,0},{2,1},{3,2},{5,4},{6,5},{7,6},{9,8},{10,9},{11,10},{13,12},{... | collective-permute-start | bytes 196616 | tf_op jit(solution)/shard_map/ppermute | solution.py:19
  46.7 10.0 %collective-permute-start.6 = (bf16[1,64,4,1,128]{4,1,3,2,0:T(8,128)(2,1)S(1)}, bf16[1,64,4,1,128]{4,1,3,2,0:T(8,128)(2,1)S(1)}, u32[]{:S(2)}, u32[]{:S(2)}) collective-permute-start(bf16[1,64,4,1,128]{4,1,3,2,0:T(8,128)(2,1)S(1)} %get-tuple-element.17), channel_id=1, source_target_pairs={{0,1},{1,2},{2,3},{4,5},{5,6},{6,7},{8,9},{9,10},{10,11},{12,13},{... | collective-permute-start | bytes 196616 | tf_op jit(solution)/shard_map/ppermute | solution.py:18
  50.4 27.5 %collective-permute-start.11 = (bf16[1,128,4,1,128]{4,1,3,2,0:T(8,128)(2,1)S(1)}, bf16[1,128,4,1,128]{4,1,3,2,0:T(8,128)(2,1)S(1)}, u32[]{:S(2)}, u32[]{:S(2)}) collective-permute-start(bf16[1,128,4,1,128]{4,1,3,2,0:T(8,128)(2,1)S(1)} %get-tuple-element.12), channel_id=1, source_target_pairs={{1,0},{2,1},{3,2},{5,4},{6,5},{7,6},{9,8},{10,9},{11,10},{13,12},{... | collective-permute-start | bytes 393224 | tf_op jit(solution)/shard_map/ppermute | solution.py:19
  51.7 26.2 %collective-permute-start.10 = (bf16[1,128,4,1,128]{4,1,3,2,0:T(8,128)(2,1)S(1)}, bf16[1,128,4,1,128]{4,1,3,2,0:T(8,128)(2,1)S(1)}, u32[]{:S(2)}, u32[]{:S(2)}) collective-permute-start(bf16[1,128,4,1,128]{4,1,3,2,0:T(8,128)(2,1)S(1)} %get-tuple-element.11), channel_id=1, source_target_pairs={{0,1},{1,2},{2,3},{4,5},{5,6},{6,7},{8,9},{9,10},{10,11},{12,13},{... | collective-permute-start | bytes 393224 | tf_op jit(solution)/shard_map/ppermute | solution.py:18
  61.5 11.0 %copy-start.5 = (bf16[1,64,4,9,128]{4,1,3,2,0:T(8,128)(2,1)}, bf16[1,64,4,9,128]{4,1,3,2,0:T(8,128)(2,1)S(1)}, u32[]{:S(2)}) copy-start(bf16[1,64,4,9,128]{4,1,3,2,0:T(8,128)(2,1)S(1)} %get-tuple-element.15) | copy-start | bytes 1769476
  61.6 12.9 %copy-start.4 = (bf16[1,64,4,9,128]{4,1,3,2,0:T(8,128)(2,1)}, bf16[1,64,4,9,128]{4,1,3,2,0:T(8,128)(2,1)S(1)}, u32[]{:S(2)}) copy-start(bf16[1,64,4,9,128]{4,1,3,2,0:T(8,128)(2,1)S(1)} %get-tuple-element.16) | copy-start | bytes 1769476
  75.1 2.8 %copy-start.10 = (f32[27,128,64]{1,2,0:T(8,128)}, f32[27,128,64]{1,2,0:T(8,128)S(1)}, u32[]{:S(2)}) copy-start(f32[27,128,64]{1,2,0:T(8,128)S(1)} %fusion.59) | copy-start | bytes 2654212
  115.0 35.6 %reduce-scatter.9.cloned.1.call-start = ((), (), s32[]{:S(2)}) async-start(), calls=%async_computation.3 | async-start | bytes 1376256
  121.3 2.9 %copy-start.6 = (bf16[1,64,4,9,128]{4,1,3,2,0:T(8,128)(2,1)S(1)}, bf16[1,64,4,9,128]{4,1,3,2,0:T(8,128)(2,1)}, u32[]{:S(2)}) copy-start(bf16[1,64,4,9,128]{4,1,3,2,0:T(8,128)(2,1)} %copy-done.5) | copy-start | bytes 1769476
  128.4 121.2 %all-reduce.6.cloned.1.call-start = ((), (), s32[]{:S(2)}) async-start(), calls=%async_computation.4 | async-start | bytes 2654208 | tf_op jit(solution)/shard_map/psum | solution.py:81
  128.7 4.4 %copy-start.3 = (f32[2,8,128,128]{3,2,1,0:T(8,128)S(1)}, f32[2,8,128,128]{3,2,1,0:T(8,128)}, u32[]{:S(2)}) copy-start(f32[2,8,128,128]{3,2,1,0:T(8,128)} %convolution_add_fusion.6) | copy-start | bytes 3145732
  (3 other events, 6.9 us)
Sparse Core Ops, SparseCore 0:
  115.1 14.2 reduce-scatter.6
  131.6 18.8 reduce-scatter.8
  155.8 93.7 all-reduce.5
where the time goes:
time: 261 us; the launch traced here: 259 us
  waiting for transfers between devices  99.2 us (38%)
  matrix products  81 us (31%)
  starting transfers between devices  34 us (13%)
  local copies, waits for them, and re-layouts  27.4 us (10%)
  between operations  14.7 us (6%)
  other arithmetic  3.19 us (1%)
    psum x1, waiting for transfers between devices, per_device(): summed = lax.psum((grad_first, grad_second), ('dep', 'hgt'))  86.6 us
    dot_general x54, matrix products, convolve(): jnp.einsum('oi,bidhw->bodhw', kernel[number], piece, preferred_element_ty...  42.3 us
    dot_general x54, matrix products, kernel_grad(): jnp.einsum('bodhw,bidhw->oi', upstream, piece, preferred_element_type=jnp...  30.9 us
    unnamed x41, local copies, waits for them, and re-layouts  27.2 us
    ppermute x6, starting transfers between devices, extended_2(): before = lax.ppermute(last, axis, up)  25.7 us
    unnamed x5, waiting for transfers between devices  8.71 us
    ppermute x6, starting transfers between devices, extended_2(): after = lax.ppermute(leading, axis, down)  7.88 us
    dot_general x27, matrix products, per_device(): jnp.einsum('oi,bodhw->bidhw', kernel_second[number], piece, preferred_ele...  7.87 us
  transfers between devices with their start and end apart: 15, of which 5 were waited for; matrix products, arithmetic and copies ran while one was open for 25% of the time, Pallas kernels for 0%

commit v1 on v0

v1 whole, which is shorter than its diff:
```python
import functools

import jax
import jax.numpy as jnp
from jax import lax
from jax.experimental import pallas as pl
from jax.experimental.pallas import tpu as pltpu
from jax.sharding import PartitionSpec as P

BF, F32 = jnp.bfloat16, jnp.float32
LANES = 128
VMEM_BYTES = 48 * 2**20


def call(body, outs, args, scratch=(), flops=0):
    moved = sum(x.size * x.dtype.itemsize for x in (*outs, *args))
    return pl.pallas_call(
        body,
        out_shape=outs,
        in_specs=[pl.BlockSpec(memory_space=pltpu.VMEM)] * len(args),
        out_specs=[pl.BlockSpec(memory_space=pltpu.VMEM)] * len(outs),
        scratch_shapes=list(scratch),
        compiler_params=pltpu.CompilerParams(vmem_limit_bytes=VMEM_BYTES),
        cost_estimate=pl.CostEstimate(flops=flops, bytes_accessed=moved, transcendentals=0),
    )(*args)


def shape(dims, dtype):
    return jax.ShapeDtypeStruct(dims, dtype)


def moved_along_width(x, c):
    if c == 0:
        return x
    pieces = []
    for start in range(0, x.shape[1], LANES):
        piece = x[:, start : start + LANES]
        lane = lax.broadcasted_iota(jnp.int32, piece.shape, 1)
        rolled = pltpu.roll(piece, c % LANES, 1)
        pieces.append(jnp.where(lane == (0 if c == 1 else LANES - 1), 0.0, rolled))
    return pieces[0] if len(pieces) == 1 else jnp.concatenate(pieces, axis=1)


def by_rows(ref, scratch, store):
    channels, depth, height, width = ref.shape
    rows = depth * height
    scratch[...] = ref[...].astype(F32).reshape(channels * rows, width)
    for d in range(depth):
        for h in range(height):
            store(d, h, scratch[pl.ds(d * height + h, channels, stride=rows), :])


def volume_kernel(vol_ref, out_ref, scratch):
    def store(d, h, row):
        out_ref[d, :, h * LANES : (h + 1) * LANES] = row.astype(BF)

    by_rows(vol_ref, scratch, store)


def cotangent_kernel(cot_ref, k1_ref, k2_ref, lo_ref, hi_ref, moved_ref, w1_ref, w2_ref, scratch):
    def store(d, h, row):
        lanes = slice(h * LANES, (h + 1) * LANES)
        (lo_ref, hi_ref)[d][:, lanes] = row.astype(BF)
        channels = row.shape[0]
        for n, c in enumerate((-1, 0, 1)):
            moved_ref[d, n * channels : (n + 1) * channels, lanes] = moved_along_width(row, c).astype(BF)

    by_rows(cot_ref, scratch, store)
    mid, out = k1_ref.shape[2], k2_ref.shape[2]
    for c in range(3):
        one = jnp.concatenate([k1_ref[3 * ab + c] for ab in range(9)], axis=0)
        w1_ref[c * mid : (c + 1) * mid, :] = one.astype(F32).T.astype(BF)
        two = jnp.concatenate([k2_ref[3 * ab + c] for ab in range(9)], axis=0)
        w2_ref[c * out : (c + 1) * out, :] = two.astype(F32).T.astype(BF)


def rim_kernel(own_ref, before_ref, after_ref, first_ref, last_ref):
    n = first_ref.shape[2]
    rows = [before_ref[0], before_ref[1], own_ref[0], own_ref[1], after_ref[0], after_ref[1]]
    for d, row in enumerate(rows):
        first_ref[d] = row[:, :n]
        last_ref[d] = row[:, row.shape[1] - n :]


def cot_rim_kernel(lo_ref, hi_ref, before_ref, after_ref, first_ref, last_ref):
    n = first_ref.shape[2]
    for d, ref in enumerate((before_ref, lo_ref, hi_ref, after_ref)):
        first_ref[d] = ref[:, :n]
        last_ref[d] = ref[:, ref.shape[1] - n :]


def volume_rows(own_ref, before_ref, after_ref, left_ref, right_ref):
    middle = [before_ref[0], before_ref[1], own_ref[0], own_ref[1], after_ref[0], after_ref[1]]
    return [
        jnp.concatenate([left_ref[d], middle[d], right_ref[d]], axis=1) for d in range(len(middle))
    ]


def hidden_kernel(
    own_ref, before_ref, after_ref, left_ref, right_ref, w1_ref, moved_ref, hidden_ref, slope_ref, g2_ref
):
    rows = volume_rows(own_ref, before_ref, after_ref, left_ref, right_ref)
    mid = w1_ref.shape[0] // 3
    dep, deps = lax.axis_index("dep"), lax.axis_size("dep")
    hgt, hgts = lax.axis_index("hgt"), lax.axis_size("hgt")
    depth, height = hidden_ref.shape[0], hidden_ref.shape[2] // LANES
    w1 = w1_ref[...]
    for d in range(depth):
        for h in range(0, height, 2):
            rhs = jnp.concatenate(
                [rows[d + a][:, (h + b) * LANES : (h + b + 2) * LANES] for a in range(3) for b in range(3)], axis=0
            )
            y = jnp.dot(w1, rhs, preferred_element_type=F32)
            pre = sum(moved_along_width(y[n * mid : (n + 1) * mid], 1 - n) for n in range(3))
            s = 1.0 / (1.0 + jnp.exp(-pre))
            for r in range(2):
                lanes = slice(r * LANES, (r + 1) * LANES)
                p, q = pre[:, lanes], s[:, lanes]
                value = (p * q).astype(BF)
                outside = []
                if d == 0:
                    outside.append(dep == 0)
                if d == depth - 1:
                    outside.append(dep == deps - 1)
                if h + r == 0:
                    outside.append(hgt == 0)
                if h + r == height - 1:
                    outside.append(hgt == hgts - 1)
                for far in outside:
                    value = jnp.where(far, jnp.zeros_like(value), value)
                hidden_ref[d, :, (h + r) * LANES : (h + r + 1) * LANES] = value
                if 0 < d < depth - 1 and 0 < h + r < height - 1:
                    at = (h + r - 1) * LANES
                    slope_ref[d - 1, :, at : at + LANES] = q * (1.0 + p * (1.0 - q))
    cells = (height - 2) * LANES
    own = depth - 2
    out = moved_ref.shape[1] // 3
    left = jnp.concatenate([moved_ref[d] for d in range(own)], axis=1)
    tails = []
    for first in (0, 4, 8):
        group = range(first, min(first + 4, 9))
        right = jnp.concatenate(
            [
                jnp.concatenate(
                    [hidden_ref[d + ab // 3, :, (ab % 3) * LANES : (ab % 3) * LANES + cells] for ab in group], axis=0
                )
                for d in range(own)
            ],
            axis=1,
        )
        g = lax.dot_general(left, right, (((1,), (1,)), ((), ())), preferred_element_type=F32)
        for n in range(3):
            part = g[n * out : (n + 1) * out]
            if first < 8:
                for m in range(2):
                    g2_ref[4 * n + first // 2 + m] = part[:, m * LANES : (m + 1) * LANES].astype(BF)
            else:
                tails.append(part)
    tails.append(jnp.zeros_like(tails[0]))
    for m in range(2):
        g2_ref[12 + m] = jnp.concatenate(tails[2 * m : 2 * m + 2], axis=1).astype(BF)


def features_kernel(hidden_ref, w2_ref, out_ref, scratch):
    out = w2_ref.shape[0] // 3
    _, depth, height, _ = out_ref.shape
    w2 = w2_ref[...]
    for d in range(depth):
        for h in range(0, height, 2):
            rhs = jnp.concatenate(
                [
                    hidden_ref[d + a, :, (h + b) * LANES : (h + b + 2) * LANES]
                    for a in range(3)
                    for b in range(3)
                ],
                axis=0,
            )
            y = jnp.dot(w2, rhs, preferred_element_type=F32)
            total = sum(moved_along_width(y[n * out : (n + 1) * out], 1 - n) for n in range(3))
            for r in range(2):
                row = total[:, r * LANES : (r + 1) * LANES]
                scratch[pl.ds(d * height + h + r, out, stride=depth * height), :] = row
    out_ref[...] = scratch[...].reshape(out_ref.shape).astype(BF)


def delta_kernel(
    direct, own_ref, before_ref, after_ref, left_ref, right_ref,
    lo_ref, hi_ref, cot_before_ref, cot_after_ref, cot_left_ref, cot_right_ref,
    k2_ref, slope_ref, g2_ref, *outs_and_scratch,
):
    *out_refs, delta_ref = outs_and_scratch
    rows = volume_rows(own_ref, before_ref, after_ref, left_ref, right_ref)
    middle = (cot_before_ref, lo_ref, hi_ref, cot_after_ref)
    cots = [
        jnp.concatenate([cot_left_ref[d], middle[d][...], cot_right_ref[d]], axis=1) for d in range(len(middle))
    ]
    mid = k2_ref.shape[1]
    own, cells = slope_ref.shape[0], slope_ref.shape[2]
    w = jnp.concatenate([k2_ref[3 * ab : 3 * ab + 3].reshape(3 * mid, k2_ref.shape[2]) for ab in range(9)], axis=1)
    for d in range(own):
        for at in range(0, cells, 2 * LANES):
            rhs = jnp.concatenate(
                [
                    cots[d + 2 - a][:, at + (2 - b) * LANES : at + (4 - b) * LANES]
                    for a in range(3)
                    for b in range(3)
                ],
                axis=0,
            )
            y = jnp.dot(w, rhs, preferred_element_type=F32)
            back = sum(moved_along_width(y[n * mid : (n + 1) * mid], n - 1) for n in range(3))
            delta = back * slope_ref[d, :, at : at + 2 * LANES]
            for n in range(3):
                delta_ref[n * mid : (n + 1) * mid, d * cells + at : d * cells + at + 2 * LANES] = moved_along_width(
                    delta, n - 1
                ).astype(BF)
    left = delta_ref[...]
    blocks, tails = [None] * 6, []
    inner = own_ref.shape[1]
    for first in (0, 8):
        group = range(first, min(first + 8, 9))
        right = jnp.concatenate(
            [
                jnp.concatenate(
                    [rows[d + 1 + ab // 3][:, (1 + ab % 3) * LANES : (1 + ab % 3) * LANES + cells] for ab in group],
                    axis=0,
                )
                for d in range(own)
            ],
            axis=1,
        )
        g = lax.dot_general(left, right, (((1,), (1,)), ((), ())), preferred_element_type=F32)
        for n in range(3):
            part = g[n * mid : (n + 1) * mid]
            if first == 0:
                for m in range(2):
                    blocks[2 * n + m] = part[:, m * LANES : (m + 1) * LANES]
            else:
                tails.append(part)
    tails.append(jnp.zeros((mid, LANES - 3 * inner), F32))
    blocks.append(jnp.concatenate(tails, axis=1))
    if not direct:
        for j, block in enumerate(blocks):
            out_refs[0][j] = block.astype(BF)
        return
    packed_ref = out_refs[0]
    parts, quarters, units, size, _ = packed_ref.shape

    def put(part, unit, value):
        packed_ref[part, unit // units, unit % units] = value

    for part in range(parts):
        for j in range(14):
            for half in range(2):
                start = (2 * part + half) * size
                put(part, 2 * j + half, g2_ref[j, start : start + size, :])
        for j, block in enumerate(blocks):
            put(part, 28 + j, block[part * size : (part + 1) * size].astype(BF))
        for unit in range(35, quarters * units):
            put(part, unit, jnp.zeros((size, LANES), BF))


def sum_kernel(in_ref, out_ref):
    total = in_ref[0].astype(F32)
    for n in range(1, in_ref.shape[0]):
        total = total + in_ref[n].astype(F32)
    out_ref[...] = total.astype(out_ref.dtype)


def sum_four_kernel(a_ref, b_ref, c_ref, d_ref, out_ref):
    one = a_ref[...].astype(F32) + b_ref[...].astype(F32)
    two = c_ref[...].astype(F32) + d_ref[...].astype(F32)
    out_ref[...] = (one + two).astype(out_ref.dtype)


def unpack_kernel(in_ref, g1_ref, g2_ref):
    quarters, units, size, _ = in_ref.shape

    def get(unit):
        return in_ref[unit // units, unit % units].astype(F32)

    for j in range(14):
        for half in range(2):
            rows = slice(half * size, (half + 1) * size)
            value = get(2 * j + half)
            for m in range(2):
                if j < 12:
                    c, ab = j // 4, 2 * (j % 4) + m
                else:
                    c, ab = 2 * (j - 12) + m, 8
                if c < 3:
                    g2_ref[3 * ab + c, rows, :] = value[:, m * 64 : (m + 1) * 64]
    for j in range(7):
        value = get(28 + j)
        for m in range(4):
            c, ab = (j // 2, 4 * (j % 2) + m) if j < 6 else (m, 8)
            if c < 3:
                g1_ref[3 * ab + c] = value[:, m * 32 : (m + 1) * 32]


def exchange(up, down, axis):
    size = lax.axis_size(axis)
    rising = [(i, i + 1) for i in range(size - 1)]
    falling = [(j, i) for i, j in rising]
    return lax.ppermute(up, axis, rising), lax.ppermute(down, axis, falling)


def gathered_by_xor(x, axis):
    size = lax.axis_size(axis)
    return [x] + [lax.ppermute(x, axis, [(i, i ^ k) for i in range(size)]) for k in range(1, size)]


def per_device(volume, kernel_first, kernel_second, cotangent):
    _, inner, depth, height, width = volume.shape
    mid, out = kernel_first.shape[1], kernel_second.shape[1]
    cells = height * width
    parts, quarters = lax.axis_size("dp"), lax.axis_size("hgt")
    k1, k2 = jnp.swapaxes(kernel_first, 1, 2), jnp.swapaxes(kernel_second, 1, 2)
    rows = depth * height

    (vol,) = call(
        volume_kernel, [shape((depth, inner, cells), BF)], [volume[0]], [pltpu.VMEM((inner * rows, width), F32)]
    )
    before, after = exchange(vol, vol, "dep")
    lo, hi, moved, w1, w2 = call(
        cotangent_kernel,
        [shape((out, cells), BF)] * 2
        + [shape((depth, 3 * out, cells), BF), shape((3 * mid, 9 * inner), BF), shape((3 * out, 9 * mid), BF)],
        [cotangent[0], k1, k2],
        [pltpu.VMEM((out * rows, width), F32)],
    )
    first, last = call(rim_kernel, [shape((depth + 4, inner, 2 * width), BF)] * 2, [vol, before, after])
    left, right = exchange(last, first, "hgt")
    cot_before, cot_after = exchange(hi, lo, "dep")
    cot_first, cot_last = call(
        cot_rim_kernel, [shape((depth + 2, out, width), BF)] * 2, [lo, hi, cot_before, cot_after]
    )
    cot_left, cot_right = exchange(cot_last, cot_first, "hgt")

    volumes = [vol, before, after, left, right]
    hidden, slope, g2 = call(
        hidden_kernel,
        [
            shape((depth + 2, mid, cells + 2 * width), BF),
            shape((depth, mid, cells), F32),
            shape((14, out, LANES), BF),
        ],
        [*volumes, w1, moved],
        flops=1_500_000_000,
    )
    size = mid // parts
    direct = size % 16 == 0
    packed = (parts, quarters, 9, size, LANES)
    (grads,) = call(
        functools.partial(delta_kernel, direct),
        [shape(packed if direct else (7, mid, LANES), BF)],
        [*volumes, lo, hi, cot_before, cot_after, cot_left, cot_right, k2, slope, g2],
        [pltpu.VMEM((3 * mid, depth * cells), BF)],
        flops=1_100_000_000,
    )
    if not direct:
        one = jnp.swapaxes(grads.reshape(7, parts, size, LANES), 0, 1)
        two = jnp.swapaxes(g2.reshape(14, parts, 2, size, LANES), 0, 1).reshape(parts, 28, size, LANES)
        grads = jnp.pad(jnp.concatenate([two, one], axis=1), ((0, 0), (0, quarters * 9 - 35), (0, 0), (0, 0)))
        grads = grads.reshape(packed)
    grads = grads.reshape(parts * quarters, 9 * size, LANES)
    swapped = lax.all_to_all(grads, ("dp", "hgt"), 0, 0, tiled=True)
    (features,) = call(
        features_kernel, [shape(cotangent.shape[1:], BF)], [hidden, w2], [pltpu.VMEM((out * rows, width), F32)],
        flops=900_000_000,
    )
    (share,) = call(sum_kernel, [shape(grads.shape[1:], BF)], [swapped])
    (share,) = call(sum_four_kernel, [shape(grads.shape[1:], BF)], gathered_by_xor(share, "dep"))
    near = jnp.stack(gathered_by_xor(share, "hgt"))
    me = lax.axis_index("hgt")
    whole = jnp.stack([lax.dynamic_index_in_dim(near, me ^ q, 0, False) for q in range(quarters)])
    grad_first, grad_second = call(
        unpack_kernel,
        [shape((27, size, inner), F32), shape((27, 2 * size, mid), F32)],
        [whole.reshape(quarters, 9, size, LANES)],
    )
    return features[None], grad_first, grad_second


def solution(mesh):
    placed = (P("dp", None, "dep", "hgt", None), P(), P(), P("dp", None, "dep", "hgt", None))
    return jax.shard_map(
        per_device,
        mesh=mesh,
        in_specs=placed,
        out_specs=(P("dp", None, "dep", "hgt", None), P(None, "dp", None), P(None, "dp", None)),
        check_vma=False,
    )
```

time: 261 us -> 70.5 us (0.27)
  waiting for transfers between devices: 99.2 us -> 12.9 us
  matrix products: 81 us -> 0 us
  local copies, waits for them, and re-layouts: 27.4 us -> 3.92 us
  blocking collectives: 0 us -> 16.1 us
  between operations: 14.7 us -> 0.83 us
  Pallas kernels: 0 us -> 9.1 us
  starting transfers between devices: 34 us -> 27.1 us
  other arithmetic: 3.19 us -> 0.08 us
    psum x1 -> x0, waiting for transfers between devices: 86.6 us -> none  [per_device(): summed = lax.psum((grad_first, grad_second), ('dep', 'hgt'))]
    dot_general x135 -> x0, matrix products: 81 us -> none  [the longest x54 42.3 us: convolve(): jnp.einsum('oi,bidhw->bodhw', kernel[number], piece, preferred_element_ty...]
    unnamed x41 -> x10, local copies, waits for them, and re-layouts: 27.2 us -> 3.89 us
    all_to_all x0 -> x1, blocking collectives: none -> 16.1 us  [per_device(): swapped = lax.all_to_all(grads, ('dp', 'hgt'), 0, 0, tiled=True)]
    pallas_call x0 -> x10, Pallas kernels: none -> 9.1 us  [call(): pl.pallas_call(body, out_shape=outs, in_specs=[pl.BlockSpec(memory_space=...]
    ppermute x12 -> x14, waiting for transfers between devices: 3.86 us -> 12.9 us  [the longest x6 6.74 us: gathered_by_xor(): lax.ppermute(x, axis, [(i, i ^ k) for i in range(size)])]
    unnamed x5 -> x0, waiting for transfers between devices: 8.71 us -> none
    ppermute x12 -> x14, starting transfers between devices: 33.6 us -> 27.1 us  [the longest x8 20.7 us: exchange(): return (lax.ppermute(up, axis, rising), lax.ppermute(down, axis, falling))]
  transfers between devices with their start and end apart: 15 -> 14, of which waited for: 5 -> 7; matrix products, arithmetic and copies ran while one was open for 25% -> 0% of each run, Pallas kernels for 0% -> 7%
where the time goes in v1:
time: 70.5 us; the launch traced here: 70.1 us
  starting transfers between devices  27.1 us (38%)
  blocking collectives  16.1 us (23%)
  waiting for transfers between devices  12.9 us (18%)
  Pallas kernels  9.1 us (13%)
  local copies, waits for them, and re-layouts  3.92 us (6%)
  between operations  0.83 us (1%)
    ppermute x8, starting transfers between devices, exchange(): return (lax.ppermute(up, axis, rising), lax.ppermute(down, axis, falling))  20.7 us
    all_to_all x1, blocking collectives, per_device(): swapped = lax.all_to_all(grads, ('dp', 'hgt'), 0, 0, tiled=True)  16.1 us
    pallas_call x10, Pallas kernels, call(): pl.pallas_call(body, out_shape=outs, in_specs=[pl.BlockSpec(memory_space=...  9.1 us
    ppermute x6, waiting for transfers between devices, gathered_by_xor(): lax.ppermute(x, axis, [(i, i ^ k) for i in range(size)])  6.74 us
    ppermute x6, starting transfers between devices, gathered_by_xor(): lax.ppermute(x, axis, [(i, i ^ k) for i in range(size)])  6.39 us
    ppermute x8, waiting for transfers between devices, exchange(): return (lax.ppermute(up, axis, rising), lax.ppermute(down, axis, falling))  6.17 us
    unnamed x10, local copies, waits for them, and re-layouts  3.89 us
  transfers between devices with their start and end apart: 14, of which 7 were waited for; matrix products, arithmetic and copies ran while one was open for 0% of the time, Pallas kernels for 7%

profile of v1, /device:TPU:0, one launch (start us, length us, event | category | flops | bytes accessed | tf_op | source)
XLA Modules:
  0.0 70.1 jit_solution(10788931097930315460)
XLA Ops:
  0.6 1.0 %copy-done = bf16[1,128,2,8,128]{4,3,2,1,0:T(8,128)(2,1)S(1)} copy-done((bf16[1,128,2,8,128]{4,3,2,1,0:T(8,128)(2,1)S(1)}, bf16[1,128,2,8,128]{4,3,2,1,0:T(8,128)(2,1)}, u32[]{:S(2)}) %copy-start) | copy-done | bytes 524312
  1.7 1.0 %copy-done.1 = bf16[27,128,64]{1,2,0:T(8,128)(2,1)S(1)} copy-done((bf16[27,128,64]{1,2,0:T(8,128)(2,1)S(1)}, bf16[27,128,64]{1,2,0:T(8,128)(2,1)}, u32[]{:S(2)}) %copy-start.1) | copy-done | bytes 442392
  2.7 0.9 %copy-done.3 = bf16[27,64,32]{1,2,0:T(8,128)(2,1)S(1)} copy-done((bf16[27,64,32]{1,2,0:T(8,128)(2,1)S(1)}, bf16[27,64,32]{1,2,0:T(8,128)(2,1)}, u32[]{:S(2)}) %copy-start.3) | copy-done | bytes 110616
  4.5 4.9 %collective-permute-start.4 = (bf16[128,1024]{1,0:T(8,128)(2,1)S(1)}, bf16[128,1024]{1,0:T(8,128)(2,1)S(1)}, u32[]{:S(2)}, u32[]{:S(2)}) collective-permute-start(bf16[128,1024]{1,0:T(8,128)(2,1)S(1)} %get-tuple-element.24.hi_ref), channel_id=1, source_target_pairs={{0,4},{4,8},{8,12},{1,5},{5,9},{9,13},{2,6},{6,10},{10,14},{3,7},{... | collective-permute-start | bytes 786440 | tf_op jit(solution)/shard_map/ppermute | solution.py:305
  9.4 1.3 %collective-permute-start.5 = (bf16[128,1024]{1,0:T(8,128)(2,1)S(1)}, bf16[128,1024]{1,0:T(8,128)(2,1)S(1)}, u32[]{:S(2)}, u32[]{:S(2)}) collective-permute-start(bf16[128,1024]{1,0:T(8,128)(2,1)S(1)} %get-tuple-element.23.lo_ref), channel_id=1, source_target_pairs={{4,0},{8,4},{12,8},{5,1},{9,5},{13,9},{6,2},{10,6},{14,10},{7,3},{... | collective-permute-start | bytes 786440 | tf_op jit(solution)/shard_map/ppermute | solution.py:305
  11.8 4.6 %collective-permute-start = (bf16[2,32,1024]{2,1,0:T(8,128)(2,1)S(1)}, bf16[2,32,1024]{2,1,0:T(8,128)(2,1)S(1)}, u32[]{:S(2)}, u32[]{:S(2)}) collective-permute-start(bf16[2,32,1024]{2,1,0:T(8,128)(2,1)S(1)} %shard_map.67.own_ref), channel_id=1, source_target_pairs={{0,4},{4,8},{8,12},{1,5},{5,9},{9,13},{2,6},{6,10},{10,14},{3,7},{... | collective-permute-start | bytes 393224 | tf_op jit(solution)/shard_map/ppermute | solution.py:305
  16.3 1.3 %collective-permute-start.1 = (bf16[2,32,1024]{2,1,0:T(8,128)(2,1)S(1)}, bf16[2,32,1024]{2,1,0:T(8,128)(2,1)S(1)}, u32[]{:S(2)}, u32[]{:S(2)}) collective-permute-start(bf16[2,32,1024]{2,1,0:T(8,128)(2,1)S(1)} %shard_map.67.own_ref), channel_id=1, source_target_pairs={{4,0},{8,4},{12,8},{5,1},{9,5},{13,9},{6,2},{10,6},{14,10},{7,3},{... | collective-permute-start | bytes 393224 | tf_op jit(solution)/shard_map/ppermute | solution.py:305
  17.6 1.2 %collective-permute-done.before_ref = bf16[2,32,1024]{2,1,0:T(8,128)(2,1)S(1)} collective-permute-done((bf16[2,32,1024]{2,1,0:T(8,128)(2,1)S(1)}, bf16[2,32,1024]{2,1,0:T(8,128)(2,1)S(1)}, u32[]{:S(2)}, u32[]{:S(2)}) %collective-permute-start) | collective-permute-done | bytes 131104 | tf_op jit(solution)/shard_map/ppermute | solution.py:305
  18.8 4.4 %collective-permute-done.1.after_ref = bf16[2,32,1024]{2,1,0:T(8,128)(2,1)S(1)} collective-permute-done((bf16[2,32,1024]{2,1,0:T(8,128)(2,1)S(1)}, bf16[2,32,1024]{2,1,0:T(8,128)(2,1)S(1)}, u32[]{:S(2)}, u32[]{:S(2)}) %collective-permute-start.1) | collective-permute-done | bytes 131104 | tf_op jit(solution)/shard_map/ppermute | solution.py:305
  23.2 1.3 %collective-permute-start.2 = (bf16[6,32,256]{2,1,0:T(8,128)(2,1)S(1)}, bf16[6,32,256]{2,1,0:T(8,128)(2,1)S(1)}, u32[]{:S(2)}, u32[]{:S(2)}) collective-permute-start(bf16[6,32,256]{2,1,0:T(8,128)(2,1)S(1)} %get-tuple-element.17), channel_id=1, source_target_pairs={{0,1},{1,2},{2,3},{4,5},{5,6},{6,7},{8,9},{9,10},{10,11},{12,13},{... | collective-permute-start | bytes 294920 | tf_op jit(solution)/shard_map/ppermute | solution.py:305
  24.5 1.3 %collective-permute-start.3 = (bf16[6,32,256]{2,1,0:T(8,128)(2,1)S(1)}, bf16[6,32,256]{2,1,0:T(8,128)(2,1)S(1)}, u32[]{:S(2)}, u32[]{:S(2)}) collective-permute-start(bf16[6,32,256]{2,1,0:T(8,128)(2,1)S(1)} %get-tuple-element.18), channel_id=1, source_target_pairs={{1,0},{2,1},{3,2},{5,4},{6,5},{7,6},{9,8},{10,9},{11,10},{13,12},{... | collective-permute-start | bytes 294920 | tf_op jit(solution)/shard_map/ppermute | solution.py:305
  25.9 4.8 %collective-permute-start.6 = (bf16[4,128,128]{2,1,0:T(8,128)(2,1)S(1)}, bf16[4,128,128]{2,1,0:T(8,128)(2,1)S(1)}, u32[]{:S(2)}, u32[]{:S(2)}) collective-permute-start(bf16[4,128,128]{2,1,0:T(8,128)(2,1)S(1)} %get-tuple-element.25), channel_id=1, source_target_pairs={{0,1},{1,2},{2,3},{4,5},{5,6},{6,7},{8,9},{9,10},{10,11},{12,13},{... | collective-permute-start | bytes 393224 | tf_op jit(solution)/shard_map/ppermute | solution.py:305
  30.7 1.3 %collective-permute-start.7 = (bf16[4,128,128]{2,1,0:T(8,128)(2,1)S(1)}, bf16[4,128,128]{2,1,0:T(8,128)(2,1)S(1)}, u32[]{:S(2)}, u32[]{:S(2)}) collective-permute-start(bf16[4,128,128]{2,1,0:T(8,128)(2,1)S(1)} %get-tuple-element.26), channel_id=1, source_target_pairs={{1,0},{2,1},{3,2},{5,4},{6,5},{7,6},{9,8},{10,9},{11,10},{13,12},{... | collective-permute-start | bytes 393224 | tf_op jit(solution)/shard_map/ppermute | solution.py:305
  32.0 2.5 %shard_map.70 = (bf16[4,64,1280]{2,1,0:T(8,128)(2,1)S(1)}, f32[2,64,1024]{2,1,0:T(8,128)S(1)}, bf16[14,128,128]{2,1,0:T(8,128)(2,1)S(1)}) custom-call(bf16[2,32,1024]{2,1,0:T(8,128)(2,1)S(1)} %shard_map.67.own_ref, bf16[2,32,1024]{2,1,0:T(8,128)(2,1)S(1)} %collective-permute-done.before_ref, bf16[2,32,1024]{2,1,0:T(8,128)(2,1)S(1)} %collective-permute-done.1.after_ref, ...), custom_call_target="tpu_custom_call" | custom-call | flops 1500000000 | bytes 3911680 | tf_op jit(solution)/shard_map/pallas_call | solution.py:17
  35.1 1.8 %shard_map.73 = bf16[2,4,9,32,128]{4,3,2,1,0:T(8,128)(2,1)S(1)} custom-call(bf16[2,32,1024]{2,1,0:T(8,128)(2,1)S(1)} %shard_map.67.own_ref, bf16[2,32,1024]{2,1,0:T(8,128)(2,1)S(1)} %collective-permute-done.before_ref, bf16[2,32,1024]{2,1,0:T(8,128)(2,1)S(1)} %collective-permute-done.1.after_ref, bf16[6,32,256]{2,1,0:T(8,128)(2,1)S(1)} %collective-permute-done.2.left_ref, ...), custom_call_target="tpu_custom_call" | custom-call | flops 1100000000 | bytes 3915776 | tf_op jit(solution)/shard_map/pallas_call | solution.py:17
  36.9 16.1 %all_to_all.5.in_ref = bf16[8,288,128]{2,1,0:T(8,128)(2,1)S(1)} all-to-all(bf16[8,288,128]{2,1,0:T(8,128)(2,1)S(1)} %bitcast.12), channel_id=1, replica_groups=mesh['dp'=2,'dep'=4,'hgt'=4] {'dp','hgt'}, dimensions={0} | all-to-all | bytes 1179648 | tf_op jit(solution)/shard_map/all_to_all | solution.py:367
  53.1 1.7 %collective-permute-start.10 = (bf16[288,128]{1,0:T(8,128)(2,1)S(1)}, bf16[288,128]{1,0:T(8,128)(2,1)S(1)}, u32[]{:S(2)}, u32[]{:S(2)}) collective-permute-start(bf16[288,128]{1,0:T(8,128)(2,1)S(1)} %shard_map.74.a_ref), channel_id=1, source_target_pairs={{0,12},{4,8},{8,4},{12,0},{1,13},{5,9},{9,5},{13,1},{2,14},{6,10},... | collective-permute-start | bytes 221192 | tf_op jit(solution)/shard_map/ppermute | solution.py:310
  54.7 1.6 %collective-permute-start.8 = (bf16[288,128]{1,0:T(8,128)(2,1)S(1)}, bf16[288,128]{1,0:T(8,128)(2,1)S(1)}, u32[]{:S(2)}, u32[]{:S(2)}) collective-permute-start(bf16[288,128]{1,0:T(8,128)(2,1)S(1)} %shard_map.74.a_ref), channel_id=1, source_target_pairs={{0,4},{4,0},{8,12},{12,8},{1,5},{5,1},{9,13},{13,9},{2,6},{6,2},{1... | collective-permute-start | bytes 221192 | tf_op jit(solution)/shard_map/ppermute | solution.py:310
  56.3 1.2 %collective-permute-start.9 = (bf16[288,128]{1,0:T(8,128)(2,1)S(1)}, bf16[288,128]{1,0:T(8,128)(2,1)S(1)}, u32[]{:S(2)}, u32[]{:S(2)}) collective-permute-start(bf16[288,128]{1,0:T(8,128)(2,1)S(1)} %shard_map.74.a_ref), channel_id=1, source_target_pairs={{0,8},{4,12},{8,0},{12,4},{1,9},{5,13},{9,1},{13,5},{2,10},{6,14},... | collective-permute-start | bytes 221192 | tf_op jit(solution)/shard_map/ppermute | solution.py:310
  57.5 2.7 %collective-permute-done.10.d_ref = bf16[288,128]{1,0:T(8,128)(2,1)S(1)} collective-permute-done((bf16[288,128]{1,0:T(8,128)(2,1)S(1)}, bf16[288,128]{1,0:T(8,128)(2,1)S(1)}, u32[]{:S(2)}, u32[]{:S(2)}) %collective-permute-start.10) | collective-permute-done | bytes 73760 | tf_op jit(solution)/shard_map/ppermute | solution.py:310
  60.2 2.6 %collective-permute-done.9.c_ref = bf16[288,128]{1,0:T(8,128)(2,1)S(1)} collective-permute-done((bf16[288,128]{1,0:T(8,128)(2,1)S(1)}, bf16[288,128]{1,0:T(8,128)(2,1)S(1)}, u32[]{:S(2)}, u32[]{:S(2)}) %collective-permute-start.9) | collective-permute-done | bytes 73760 | tf_op jit(solution)/shard_map/ppermute | solution.py:310
  62.9 1.0 %collective-permute-start.12 = (bf16[288,128]{1,0:T(8,128)(2,1)S(1)}, bf16[288,128]{1,0:T(8,128)(2,1)S(1)}, u32[]{:S(2)}, u32[]{:S(2)}) collective-permute-start(bf16[288,128]{1,0:T(8,128)(2,1)S(1)} %shard_map.75), channel_id=1, source_target_pairs={{0,2},{1,3},{2,0},{3,1},{4,6},{5,7},{6,4},{7,5},{8,10},{9,11},{10,... | collective-permute-start | bytes 221192 | tf_op jit(solution)/shard_map/ppermute | solution.py:310
  64.8 2.5 %shard_map.71 = bf16[128,2,8,128]{3,2,1,0:T(8,128)(2,1)} custom-call(bf16[4,64,1280]{2,1,0:T(8,128)(2,1)S(1)} %get-tuple-element.21.hidden_ref, bf16[384,576]{1,0:T(8,128)(2,1)S(1)} %get-tuple-element.22.w2_ref), custom_call_target="tpu_custom_call" | custom-call | flops 900000000 | bytes 1622016 | tf_op jit(solution)/shard_map/pallas_call | solution.py:17
  68.9 1.2 %shard_map.76 = (f32[27,32,32]{2,1,0:T(8,128)}, f32[27,64,64]{2,1,0:T(8,128)}) custom-call(bf16[4,9,32,128]{3,2,1,0:T(8,128)(2,1)S(1)} %bitcast.11), custom_call_target="tpu_custom_call" | custom-call | bytes 847872 | tf_op jit(solution)/shard_map/pallas_call | solution.py:17
  (28 shorter events, 5.2 us)
Async XLA Ops:
  0.6 1.0 %copy-start = (bf16[1,128,2,8,128]{4,3,2,1,0:T(8,128)(2,1)S(1)}, bf16[1,128,2,8,128]{4,3,2,1,0:T(8,128)(2,1)}, u32[]{:S(2)}) copy-start(bf16[1,128,2,8,128]{4,3,2,1,0:T(8,128)(2,1)} %param.7) | copy-start | bytes 1572868
  1.7 1.0 %copy-start.1 = (bf16[27,128,64]{1,2,0:T(8,128)(2,1)S(1)}, bf16[27,128,64]{1,2,0:T(8,128)(2,1)}, u32[]{:S(2)}) copy-start(bf16[27,128,64]{1,2,0:T(8,128)(2,1)} %param.6) | copy-start | bytes 1327108
  2.7 0.9 %copy-start.3 = (bf16[27,64,32]{1,2,0:T(8,128)(2,1)S(1)}, bf16[27,64,32]{1,2,0:T(8,128)(2,1)}, u32[]{:S(2)}) copy-start(bf16[27,64,32]{1,2,0:T(8,128)(2,1)} %param.5) | copy-start | bytes 331780
  4.5 21.3 %collective-permute-start.4 = (bf16[128,1024]{1,0:T(8,128)(2,1)S(1)}, bf16[128,1024]{1,0:T(8,128)(2,1)S(1)}, u32[]{:S(2)}, u32[]{:S(2)}) collective-permute-start(bf16[128,1024]{1,0:T(8,128)(2,1)S(1)} %get-tuple-element.24.hi_ref), channel_id=1, source_target_pairs={{0,4},{4,8},{8,12},{1,5},{5,9},{9,13},{2,6},{6,10},{10,14},{3,7},{... | collective-permute-start | bytes 786440 | tf_op jit(solution)/shard_map/ppermute | solution.py:305
  9.4 16.4 %collective-permute-start.5 = (bf16[128,1024]{1,0:T(8,128)(2,1)S(1)}, bf16[128,1024]{1,0:T(8,128)(2,1)S(1)}, u32[]{:S(2)}, u32[]{:S(2)}) collective-permute-start(bf16[128,1024]{1,0:T(8,128)(2,1)S(1)} %get-tuple-element.23.lo_ref), channel_id=1, source_target_pairs={{4,0},{8,4},{12,8},{5,1},{9,5},{13,9},{6,2},{10,6},{14,10},{7,3},{... | collective-permute-start | bytes 786440 | tf_op jit(solution)/shard_map/ppermute | solution.py:305
  10.7 0.9 %copy-start.4 = (bf16[1,32,2,8,128]{4,3,2,1,0:T(8,128)(2,1)S(1)}, bf16[1,32,2,8,128]{4,3,2,1,0:T(8,128)(2,1)}, u32[]{:S(2)}) copy-start(bf16[1,32,2,8,128]{4,3,2,1,0:T(8,128)(2,1)} %param.4) | copy-start | bytes 393220
  11.8 7.1 %collective-permute-start = (bf16[2,32,1024]{2,1,0:T(8,128)(2,1)S(1)}, bf16[2,32,1024]{2,1,0:T(8,128)(2,1)S(1)}, u32[]{:S(2)}, u32[]{:S(2)}) collective-permute-start(bf16[2,32,1024]{2,1,0:T(8,128)(2,1)S(1)} %shard_map.67.own_ref), channel_id=1, source_target_pairs={{0,4},{4,8},{8,12},{1,5},{5,9},{9,13},{2,6},{6,10},{10,14},{3,7},{... | collective-permute-start | bytes 393224 | tf_op jit(solution)/shard_map/ppermute | solution.py:305
  16.3 6.9 %collective-permute-start.1 = (bf16[2,32,1024]{2,1,0:T(8,128)(2,1)S(1)}, bf16[2,32,1024]{2,1,0:T(8,128)(2,1)S(1)}, u32[]{:S(2)}, u32[]{:S(2)}) collective-permute-start(bf16[2,32,1024]{2,1,0:T(8,128)(2,1)S(1)} %shard_map.67.own_ref), channel_id=1, source_target_pairs={{4,0},{8,4},{12,8},{5,1},{9,5},{13,9},{6,2},{10,6},{14,10},{7,3},{... | collective-permute-start | bytes 393224 | tf_op jit(solution)/shard_map/ppermute | solution.py:305
  23.2 8.8 %collective-permute-start.2 = (bf16[6,32,256]{2,1,0:T(8,128)(2,1)S(1)}, bf16[6,32,256]{2,1,0:T(8,128)(2,1)S(1)}, u32[]{:S(2)}, u32[]{:S(2)}) collective-permute-start(bf16[6,32,256]{2,1,0:T(8,128)(2,1)S(1)} %get-tuple-element.17), channel_id=1, source_target_pairs={{0,1},{1,2},{2,3},{4,5},{5,6},{6,7},{8,9},{9,10},{10,11},{12,13},{... | collective-permute-start | bytes 294920 | tf_op jit(solution)/shard_map/ppermute | solution.py:305
  24.5 7.5 %collective-permute-start.3 = (bf16[6,32,256]{2,1,0:T(8,128)(2,1)S(1)}, bf16[6,32,256]{2,1,0:T(8,128)(2,1)S(1)}, u32[]{:S(2)}, u32[]{:S(2)}) collective-permute-start(bf16[6,32,256]{2,1,0:T(8,128)(2,1)S(1)} %get-tuple-element.18), channel_id=1, source_target_pairs={{1,0},{2,1},{3,2},{5,4},{6,5},{7,6},{9,8},{10,9},{11,10},{13,12},{... | collective-permute-start | bytes 294920 | tf_op jit(solution)/shard_map/ppermute | solution.py:305
  25.9 8.7 %collective-permute-start.6 = (bf16[4,128,128]{2,1,0:T(8,128)(2,1)S(1)}, bf16[4,128,128]{2,1,0:T(8,128)(2,1)S(1)}, u32[]{:S(2)}, u32[]{:S(2)}) collective-permute-start(bf16[4,128,128]{2,1,0:T(8,128)(2,1)S(1)} %get-tuple-element.25), channel_id=1, source_target_pairs={{0,1},{1,2},{2,3},{4,5},{5,6},{6,7},{8,9},{9,10},{10,11},{12,13},{... | collective-permute-start | bytes 393224 | tf_op jit(solution)/shard_map/ppermute | solution.py:305
  30.7 4.5 %collective-permute-start.7 = (bf16[4,128,128]{2,1,0:T(8,128)(2,1)S(1)}, bf16[4,128,128]{2,1,0:T(8,128)(2,1)S(1)}, u32[]{:S(2)}, u32[]{:S(2)}) collective-permute-start(bf16[4,128,128]{2,1,0:T(8,128)(2,1)S(1)} %get-tuple-element.26), channel_id=1, source_target_pairs={{1,0},{2,1},{3,2},{5,4},{6,5},{7,6},{9,8},{10,9},{11,10},{13,12},{... | collective-permute-start | bytes 393224 | tf_op jit(solution)/shard_map/ppermute | solution.py:305
  32.0 3.2 %copy-start.2 = (bf16[27,128,64]{1,2,0:T(8,128)(2,1)S(1)}, bf16[27,128,64]{1,2,0:T(8,128)(2,1)}, u32[]{:S(2)}) copy-start(bf16[27,128,64]{1,2,0:T(8,128)(2,1)} %param.6) | copy-start | bytes 1327108
  53.1 7.1 %collective-permute-start.10 = (bf16[288,128]{1,0:T(8,128)(2,1)S(1)}, bf16[288,128]{1,0:T(8,128)(2,1)S(1)}, u32[]{:S(2)}, u32[]{:S(2)}) collective-permute-start(bf16[288,128]{1,0:T(8,128)(2,1)S(1)} %shard_map.74.a_ref), channel_id=1, source_target_pairs={{0,12},{4,8},{8,4},{12,0},{1,13},{5,9},{9,5},{13,1},{2,14},{6,10},... | collective-permute-start | bytes 221192 | tf_op jit(solution)/shard_map/ppermute | solution.py:310
  54.7 5.5 %collective-permute-start.8 = (bf16[288,128]{1,0:T(8,128)(2,1)S(1)}, bf16[288,128]{1,0:T(8,128)(2,1)S(1)}, u32[]{:S(2)}, u32[]{:S(2)}) collective-permute-start(bf16[288,128]{1,0:T(8,128)(2,1)S(1)} %shard_map.74.a_ref), channel_id=1, source_target_pairs={{0,4},{4,0},{8,12},{12,8},{1,5},{5,1},{9,13},{13,9},{2,6},{6,2},{1... | collective-permute-start | bytes 221192 | tf_op jit(solution)/shard_map/ppermute | solution.py:310
  56.3 6.5 %collective-permute-start.9 = (bf16[288,128]{1,0:T(8,128)(2,1)S(1)}, bf16[288,128]{1,0:T(8,128)(2,1)S(1)}, u32[]{:S(2)}, u32[]{:S(2)}) collective-permute-start(bf16[288,128]{1,0:T(8,128)(2,1)S(1)} %shard_map.74.a_ref), channel_id=1, source_target_pairs={{0,8},{4,12},{8,0},{12,4},{1,9},{5,13},{9,1},{13,5},{2,10},{6,14},... | collective-permute-start | bytes 221192 | tf_op jit(solution)/shard_map/ppermute | solution.py:310
  62.8 4.4 %collective-permute-start.11 = (bf16[288,128]{1,0:T(8,128)(2,1)S(1)}, bf16[288,128]{1,0:T(8,128)(2,1)S(1)}, u32[]{:S(2)}, u32[]{:S(2)}) collective-permute-start(bf16[288,128]{1,0:T(8,128)(2,1)S(1)} %shard_map.75), channel_id=1, source_target_pairs={{0,1},{1,0},{2,3},{3,2},{4,5},{5,4},{6,7},{7,6},{8,9},{9,8},{10,11... | collective-permute-start | bytes 221192 | tf_op jit(solution)/shard_map/ppermute | solution.py:310
  62.9 5.1 %collective-permute-start.12 = (bf16[288,128]{1,0:T(8,128)(2,1)S(1)}, bf16[288,128]{1,0:T(8,128)(2,1)S(1)}, u32[]{:S(2)}, u32[]{:S(2)}) collective-permute-start(bf16[288,128]{1,0:T(8,128)(2,1)S(1)} %shard_map.75), channel_id=1, source_target_pairs={{0,2},{1,3},{2,0},{3,1},{4,6},{5,7},{6,4},{7,5},{8,10},{9,11},{10,... | collective-permute-start | bytes 221192 | tf_op jit(solution)/shard_map/ppermute | solution.py:310
  63.9 4.8 %collective-permute-start.13 = (bf16[288,128]{1,0:T(8,128)(2,1)S(1)}, bf16[288,128]{1,0:T(8,128)(2,1)S(1)}, u32[]{:S(2)}, u32[]{:S(2)}) collective-permute-start(bf16[288,128]{1,0:T(8,128)(2,1)S(1)} %shard_map.75), channel_id=1, source_target_pairs={{0,3},{1,2},{2,1},{3,0},{4,7},{5,6},{6,5},{7,4},{8,11},{9,10},{10,... | collective-permute-start | bytes 221192 | tf_op jit(solution)/shard_map/ppermute | solution.py:310

commit v2 on v1

v2 whole, which is shorter than its diff:
```python
import functools

import jax
import jax.numpy as jnp
from jax import lax
from jax.experimental import pallas as pl
from jax.experimental.pallas import tpu as pltpu
from jax.sharding import PartitionSpec as P

BF, F32 = jnp.bfloat16, jnp.float32
LANES = 128
VMEM_BYTES = 48 * 2**20


def call(body, outs, args, scratch=(), flops=0, far=()):
    moved = sum(x.size * x.dtype.itemsize for x in (*outs, *args))
    return pl.pallas_call(
        body,
        out_shape=outs,
        in_specs=[pl.BlockSpec(memory_space=pl.ANY if n in far else pltpu.VMEM) for n in range(len(args))],
        out_specs=[pl.BlockSpec(memory_space=pltpu.VMEM)] * len(outs),
        scratch_shapes=list(scratch),
        compiler_params=pltpu.CompilerParams(vmem_limit_bytes=VMEM_BYTES),
        cost_estimate=pl.CostEstimate(flops=flops, bytes_accessed=moved, transcendentals=0),
    )(*args)


def shape(dims, dtype):
    return jax.ShapeDtypeStruct(dims, dtype)


def moved_along_width(x, c):
    if c == 0:
        return x
    pieces = []
    for start in range(0, x.shape[1], LANES):
        piece = x[:, start : start + LANES]
        lane = lax.broadcasted_iota(jnp.int32, piece.shape, 1)
        rolled = pltpu.roll(piece, c % LANES, 1)
        pieces.append(jnp.where(lane == (0 if c == 1 else LANES - 1), 0.0, rolled))
    return pieces[0] if len(pieces) == 1 else jnp.concatenate(pieces, axis=1)


def by_rows(ref, scratch, store):
    channels, depth, height, width = ref.shape
    rows = depth * height
    scratch[...] = ref[...].astype(F32).reshape(channels * rows, width)
    for d in range(depth):
        for h in range(height):
            store(d, h, scratch[pl.ds(d * height + h, channels, stride=rows), :])


def odd(axis):
    return lax.rem(lax.axis_index(axis), 2) == 1


def begin_copies(pairs, sems):
    copies = [pltpu.make_async_copy(src, dst, sems.at[n]) for n, (src, dst) in enumerate(pairs)]
    for copy in copies:
        copy.start()
    return copies


def volume_kernel(vol_ref, out_ref, held, scratch, sems):
    (copy,) = begin_copies([(vol_ref, held)], sems)
    copy.wait()

    def store(d, h, row):
        out_ref[d, :, h * LANES : (h + 1) * LANES] = row.astype(BF)

    by_rows(held, scratch, store)


def cotangent_kernel(
    _, cot_ref, k1_ref, k2_ref, own_ref, one_ref, two_ref, moved_ref, w1_ref, w2_ref, held, k1, k2, scratch, sems
):
    copies = begin_copies([(cot_ref, held), (k1_ref, k1), (k2_ref, k2)], sems)
    copies[0].wait()

    def store(d, h, row):
        lanes = slice(h * LANES, (h + 1) * LANES)
        own_ref[d, :, lanes] = row.astype(BF)
        channels = row.shape[0]
        for n, c in enumerate((-1, 0, 1)):
            moved_ref[d, n * channels : (n + 1) * channels, lanes] = moved_along_width(row, c).astype(BF)

    by_rows(held, scratch, store)
    is_odd = odd("dep")
    one_ref[...] = jnp.where(is_odd, own_ref[0], own_ref[own_ref.shape[0] - 1])
    two_ref[...] = jnp.where(is_odd, own_ref[own_ref.shape[0] - 1], own_ref[0])
    copies[1].wait()
    copies[2].wait()
    mid, out = k1.shape[2], k2.shape[2]
    for c in range(3):
        one = jnp.concatenate([k1[3 * ab + c] for ab in range(9)], axis=0)
        w1_ref[c * mid : (c + 1) * mid, :] = one.astype(F32).T.astype(BF)
        two = jnp.concatenate([k2[3 * ab + c] for ab in range(9)], axis=0)
        w2_ref[c * out : (c + 1) * out, :] = two.astype(F32).T.astype(BF)


def sides(axis, one, two):
    me, size = lax.axis_index(axis), lax.axis_size(axis)
    is_odd = odd(axis)
    none = jnp.zeros_like(one)
    before = jnp.where(me == 0, none, jnp.where(is_odd, one, two))
    after = jnp.where(me == size - 1, none, jnp.where(is_odd, two, one))
    return before, after


def rim_kernel(own_ref, one_ref, two_ref, deep_ref, send_one_ref, send_two_ref):
    before, after = sides("dep", one_ref[...], two_ref[...])
    edge, own = one_ref.shape[0], own_ref.shape[0]
    deep_ref[:edge] = before
    deep_ref[edge : edge + own] = own_ref[...]
    deep_ref[edge + own :] = after
    n, cells = send_one_ref.shape[2], deep_ref.shape[2]
    first, last = deep_ref[:, :, :n], deep_ref[:, :, cells - n :]
    is_odd = odd("hgt")
    send_one_ref[...] = jnp.where(is_odd, first, last)
    send_two_ref[...] = jnp.where(is_odd, last, first)


def widened(deep_ref, one_ref, two_ref):
    left, right = sides("hgt", one_ref[...], two_ref[...])
    return [jnp.concatenate([left[d], deep_ref[d], right[d]], axis=1) for d in range(deep_ref.shape[0])]


def hidden_kernel(deep_ref, one_ref, two_ref, w1_ref, moved_ref, hidden_ref, slope_ref, g2_ref, rows_ref):
    for d, row in enumerate(widened(deep_ref, one_ref, two_ref)):
        rows_ref[d] = row
    rows = rows_ref
    mid = w1_ref.shape[0] // 3
    dep, deps = lax.axis_index("dep"), lax.axis_size("dep")
    hgt, hgts = lax.axis_index("hgt"), lax.axis_size("hgt")
    depth, height = hidden_ref.shape[0], hidden_ref.shape[2] // LANES
    w1 = w1_ref[...]
    for d in range(depth):
        for h in range(0, height, 2):
            rhs = jnp.concatenate(
                [rows[d + a, :, (h + b) * LANES : (h + b + 2) * LANES] for a in range(3) for b in range(3)], axis=0
            )
            y = jnp.dot(w1, rhs, preferred_element_type=F32)
            pre = sum(moved_along_width(y[n * mid : (n + 1) * mid], 1 - n) for n in range(3))
            s = 1.0 / (1.0 + jnp.exp(-pre))
            for r in range(2):
                lanes = slice(r * LANES, (r + 1) * LANES)
                p, q = pre[:, lanes], s[:, lanes]
                value = (p * q).astype(BF)
                outside = []
                if d == 0:
                    outside.append(dep == 0)
                if d == depth - 1:
                    outside.append(dep == deps - 1)
                if h + r == 0:
                    outside.append(hgt == 0)
                if h + r == height - 1:
                    outside.append(hgt == hgts - 1)
                for far in outside:
                    value = jnp.where(far, jnp.zeros_like(value), value)
                hidden_ref[d, :, (h + r) * LANES : (h + r + 1) * LANES] = value
                if 0 < d < depth - 1 and 0 < h + r < height - 1:
                    at = (h + r - 1) * LANES
                    slope_ref[d - 1, :, at : at + LANES] = q * (1.0 + p * (1.0 - q))
    cells = (height - 2) * LANES
    own = depth - 2
    out = moved_ref.shape[1] // 3
    left = jnp.concatenate([moved_ref[d] for d in range(own)], axis=1)
    tails = []
    for first in (0, 4, 8):
        group = range(first, min(first + 4, 9))
        right = jnp.concatenate(
            [
                jnp.concatenate(
                    [hidden_ref[d + ab // 3, :, (ab % 3) * LANES : (ab % 3) * LANES + cells] for ab in group], axis=0
                )
                for d in range(own)
            ],
            axis=1,
        )
        g = lax.dot_general(left, right, (((1,), (1,)), ((), ())), preferred_element_type=F32)
        for n in range(3):
            part = g[n * out : (n + 1) * out]
            if first < 8:
                for m in range(2):
                    g2_ref[4 * n + first // 2 + m] = part[:, m * LANES : (m + 1) * LANES]
            else:
                tails.append(part)
    tails.append(jnp.zeros_like(tails[0]))
    for m in range(2):
        g2_ref[12 + m] = jnp.concatenate(tails[2 * m : 2 * m + 2], axis=1)


def features_kernel(hidden_ref, w2_ref, out_ref, scratch):
    out = w2_ref.shape[0] // 3
    _, depth, height, _ = out_ref.shape
    w2 = w2_ref[...]
    for d in range(depth):
        for h in range(0, height, 2):
            rhs = jnp.concatenate(
                [
                    hidden_ref[d + a, :, (h + b) * LANES : (h + b + 2) * LANES]
                    for a in range(3)
                    for b in range(3)
                ],
                axis=0,
            )
            y = jnp.dot(w2, rhs, preferred_element_type=F32)
            total = sum(moved_along_width(y[n * out : (n + 1) * out], 1 - n) for n in range(3))
            for r in range(2):
                row = total[:, r * LANES : (r + 1) * LANES]
                scratch[pl.ds(d * height + h + r, out, stride=depth * height), :] = row
    out_ref[...] = scratch[...].reshape(out_ref.shape).astype(BF)


def delta_kernel(direct, rows_ref, cot_ref, one_ref, two_ref, k2_ref, slope_ref, g2_ref, *outs_and_scratch):
    *out_refs, delta_ref = outs_and_scratch
    cots = widened(cot_ref, one_ref, two_ref)
    mid = k2_ref.shape[1]
    own, cells = slope_ref.shape[0], slope_ref.shape[2]
    w = jnp.concatenate([k2_ref[3 * ab : 3 * ab + 3].reshape(3 * mid, k2_ref.shape[2]) for ab in range(9)], axis=1)
    for d in range(own):
        for at in range(0, cells, 2 * LANES):
            rhs = jnp.concatenate(
                [
                    cots[d + 2 - a][:, at + (2 - b) * LANES : at + (4 - b) * LANES]
                    for a in range(3)
                    for b in range(3)
                ],
                axis=0,
            )
            y = jnp.dot(w, rhs, preferred_element_type=F32)
            back = sum(moved_along_width(y[n * mid : (n + 1) * mid], n - 1) for n in range(3))
            delta = back * slope_ref[d, :, at : at + 2 * LANES]
            for n in range(3):
                delta_ref[n * mid : (n + 1) * mid, d * cells + at : d * cells + at + 2 * LANES] = moved_along_width(
                    delta, n - 1
                ).astype(BF)
    left = delta_ref[...]
    blocks, tails = [None] * 6, []
    inner = rows_ref.shape[1]
    for first in (0, 8):
        group = range(first, min(first + 8, 9))
        right = jnp.concatenate(
            [
                jnp.concatenate(
                    [
                        rows_ref[d + 1 + ab // 3, :, (1 + ab % 3) * LANES : (1 + ab % 3) * LANES + cells]
                        for ab in group
                    ],
                    axis=0,
                )
                for d in range(own)
            ],
            axis=1,
        )
        g = lax.dot_general(left, right, (((1,), (1,)), ((), ())), preferred_element_type=F32)
        for n in range(3):
            part = g[n * mid : (n + 1) * mid]
            if first == 0:
                for m in range(2):
                    blocks[2 * n + m] = part[:, m * LANES : (m + 1) * LANES]
            else:
                tails.append(part)
    tails.append(jnp.zeros((mid, LANES - 3 * inner), F32))
    blocks.append(jnp.concatenate(tails, axis=1))
    if not direct:
        for j, block in enumerate(blocks):
            out_refs[0][j] = block
        return
    keep_ref, send_ref = out_refs
    parts, halves, units, size, _ = keep_ref.shape
    core = odd("hgt")

    def value(part, unit):
        if unit < 28:
            start = (2 * part + unit % 2) * size
            return g2_ref[unit // 2, start : start + size, :]
        if unit < 35:
            return blocks[unit - 28][part * size : (part + 1) * size]
        return jnp.zeros((size, LANES), F32)

    for part in range(parts):
        for half in range(halves):
            for unit in range(units):
                one, two = (value(part, (2 * half + c) * units + unit) for c in range(2))
                keep_ref[part, half, unit] = jnp.where(core, two, one)
                send_ref[part, half, unit] = jnp.where(core, one, two).astype(BF)


def halve_kernel(axis, bit, keep_ref, got_ref, kept_ref, send_ref):
    mine = lax.rem(lax.div(lax.axis_index(axis), bit), 2)
    kept_ref[...] = keep_ref[mine] + got_ref[mine].astype(F32)
    send_ref[...] = (keep_ref[1 - mine] + got_ref[1 - mine].astype(F32)).astype(BF)


def add_kernel(one_ref, two_ref, out_ref):
    out_ref[...] = (one_ref[...].astype(F32) + two_ref[...].astype(F32)).astype(BF)


def order_kernel(axis, bit, own_ref, got_ref, out_ref):
    mine = lax.rem(lax.div(lax.axis_index(axis), bit), 2)
    out_ref[mine] = own_ref[...]
    out_ref[1 - mine] = got_ref[...]


def unpack_kernel(own_ref, got_ref, g1_ref, g2_ref):
    _, units, size, _ = own_ref.shape
    core = odd("hgt")

    def get(unit):
        quarter = unit // units
        at = quarter // 2, unit % units
        one, two = (got_ref, own_ref) if quarter % 2 else (own_ref, got_ref)
        return jnp.where(core, two[at], one[at]).astype(F32)

    for j in range(14):
        for half in range(2):
            rows = slice(half * size, (half + 1) * size)
            value = get(2 * j + half)
            for m in range(2):
                if j < 12:
                    c, ab = j // 4, 2 * (j % 4) + m
                else:
                    c, ab = 2 * (j - 12) + m, 8
                if c < 3:
                    g2_ref[3 * ab + c, rows, :] = value[:, m * 64 : (m + 1) * 64]
    for j in range(7):
        value = get(28 + j)
        for m in range(4):
            c, ab = (j // 2, 4 * (j % 2) + m) if j < 6 else (m, 8)
            if c < 3:
                g1_ref[3 * ab + c] = value[:, m * 32 : (m + 1) * 32]


def swapped(x, axis, pattern):
    size = lax.axis_size(axis)
    first = {"one": 0, "two": 1, "inner": 1}[pattern]
    pairs = [(i, (i + 1) % size) for i in range(first, size, 2)]
    if pattern == "inner":
        pairs = pairs[:-1]
    return lax.ppermute(x, axis, pairs + [(j, i) for i, j in pairs])


def across(x, axis, bit):
    return lax.ppermute(x, axis, [(i, i ^ bit) for i in range(lax.axis_size(axis))])


def per_device(volume, kernel_first, kernel_second, cotangent):
    _, inner, depth, height, width = volume.shape
    mid, out = kernel_first.shape[1], kernel_second.shape[1]
    cells = height * width
    parts, quarters = lax.axis_size("dp"), lax.axis_size("hgt")
    k1, k2 = jnp.swapaxes(kernel_first, 1, 2), jnp.swapaxes(kernel_second, 1, 2)
    rows = depth * height

    (vol,) = call(
        volume_kernel,
        [shape((depth, inner, cells), BF)],
        [volume[0]],
        [
            pltpu.VMEM(volume.shape[1:], BF),
            pltpu.VMEM((inner * rows, width), F32),
            pltpu.SemaphoreType.DMA((1,)),
        ],
        far=(0,),
    )
    one, two = swapped(vol, "dep", "one"), swapped(vol, "dep", "two")
    cot, cot_one, cot_two, moved, w1, w2 = call(
        cotangent_kernel,
        [
            shape((depth, out, cells), BF),
            shape((out, cells), BF),
            shape((out, cells), BF),
            shape((depth, 3 * out, cells), BF),
            shape((3 * mid, 9 * inner), BF),
            shape((3 * out, 9 * mid), BF),
        ],
        [vol, cotangent[0], k1, k2],
        [
            pltpu.VMEM(cotangent.shape[1:], BF),
            pltpu.VMEM(k1.shape, BF),
            pltpu.VMEM(k2.shape, BF),
            pltpu.VMEM((out * rows, width), F32),
            pltpu.SemaphoreType.DMA((3,)),
        ],
        far=(0, 1, 2, 3),
    )
    deep, one, two = call(
        rim_kernel,
        [shape((depth + 4, inner, cells), BF)] + [shape((depth + 4, inner, 2 * width), BF)] * 2,
        [vol, one, two],
    )
    one, two = swapped(one, "hgt", "one"), swapped(two, "hgt", "two")
    cot_one, cot_two = swapped(cot_one, "dep", "one"), swapped(cot_two, "dep", "inner")
    cot_deep, cot_one, cot_two = call(
        rim_kernel,
        [shape((depth + 2, out, cells), BF)] + [shape((depth + 2, out, width), BF)] * 2,
        [cot, cot_one[None], cot_two[None]],
    )
    cot_one, cot_two = swapped(cot_one, "hgt", "one"), swapped(cot_two, "hgt", "inner")

    hidden, slope, g2, wide = call(
        hidden_kernel,
        [
            shape((depth + 2, mid, cells + 2 * width), BF),
            shape((depth, mid, cells), F32),
            shape((14, out, LANES), F32),
            shape((depth + 4, inner, cells + 4 * width), BF),
        ],
        [deep, one, two, w1, moved],
        flops=1_500_000_000,
    )
    size = mid // parts
    direct = parts == 2 and size % 16 == 0
    half = (parts, quarters // 2, 9, size, LANES)
    grads = call(
        functools.partial(delta_kernel, direct),
        [shape(half, F32), shape(half, BF)] if direct else [shape((7, mid, LANES), F32)],
        [wide, cot_deep, cot_one, cot_two, k2, slope, g2],
        [pltpu.VMEM((3 * mid, depth * cells), BF)],
        flops=1_100_000_000,
    )
    if direct:
        keep, send = grads
    else:
        grad = jnp.swapaxes(grads[0].reshape(7, parts, size, LANES), 0, 1)
        grad2 = jnp.swapaxes(g2.reshape(14, parts, 2, size, LANES), 0, 1).reshape(parts, 28, size, LANES)
        grad = jnp.pad(jnp.concatenate([grad2, grad], axis=1), ((0, 0), (0, quarters * 9 - 35), (0, 0), (0, 0)))
        grad = lax.psum_scatter(grad, "dp", scatter_dimension=0, tiled=True)
        grad = grad.reshape(quarters // 2, 2, 9, size, LANES)
        core = lax.rem(lax.axis_index("hgt"), 2)
        keep = lax.dynamic_index_in_dim(grad, core, 1, False)
        send = lax.dynamic_index_in_dim(grad, 1 - core, 1, False).astype(BF)
    (features,) = call(
        features_kernel, [shape(cotangent.shape[1:], BF)], [hidden, w2], [pltpu.VMEM((out * rows, width), F32)],
        flops=900_000_000,
    )
    got = across(send, "hgt", 1)
    if direct:
        keep, send = call(
            functools.partial(halve_kernel, "dp", 1), [shape(half[1:], F32), shape(half[1:], BF)], [keep, got]
        )
        got = across(send, "dp", 1)
    keep, send = call(
        functools.partial(halve_kernel, "hgt", 2), [shape(half[2:], F32), shape(half[2:], BF)], [keep, got]
    )
    got = across(send, "hgt", 2)
    (share,) = call(add_kernel, [shape(half[2:], BF)], [keep, got])
    (share,) = call(add_kernel, [shape(half[2:], BF)], [share, across(share, "dep", 1)])
    (share,) = call(add_kernel, [shape(half[2:], BF)], [share, across(share, "dep", 3)])
    (pair,) = call(
        functools.partial(order_kernel, "hgt", 2), [shape(half[1:], BF)], [share, across(share, "hgt", 2)]
    )
    grad_first, grad_second = call(
        unpack_kernel,
        [shape((27, size, inner), F32), shape((27, 2 * size, mid), F32)],
        [pair, across(pair, "hgt", 1)],
    )
    return features[None], grad_first, grad_second


def solution(mesh):
    placed = (P("dp", None, "dep", "hgt", None), P(), P(), P("dp", None, "dep", "hgt", None))
    return jax.shard_map(
        per_device,
        mesh=mesh,
        in_specs=placed,
        out_specs=(P("dp", None, "dep", "hgt", None), P(None, "dp", None), P(None, "dp", None)),
        check_vma=False,
    )
```

time: 70.5 us -> 66.1 us (0.938)
  waiting for transfers between devices: 12.9 us -> 29.6 us
  blocking collectives: 16.1 us -> 0 us
  starting transfers between devices: 27.1 us -> 21.2 us
  Pallas kernels: 9.1 us -> 10.4 us
    ppermute x14 -> x15, waiting for transfers between devices: 12.9 us -> 29.6 us  [the longest x7 19.5 us: across(): lax.ppermute(x, axis, [(i, i ^ bit) for i in range(lax.axis_size(axis))])]
    all_to_all x1 -> x0, blocking collectives: 16.1 us -> none  [per_device(): swapped = lax.all_to_all(grads, ('dp', 'hgt'), 0, 0, tiled=True)]
    ppermute x14 -> x15, starting transfers between devices: 27.1 us -> 21.2 us  [the longest x8 11.6 us: swapped(): return lax.ppermute(x, axis, pairs + [(j, i) for i, j in pairs])]
    pallas_call x10 -> x14, Pallas kernels: 9.1 us -> 10.4 us  [call(): pl.pallas_call(body, out_shape=outs, in_specs=[pl.BlockSpec(memory_space=...]
  transfers between devices with their start and end apart: 14 -> 15, of which waited for: 7 -> 9; matrix products, arithmetic and copies ran while one was open for 0% -> 0% of each run, Pallas kernels for 7% -> 8%
where the time goes in v2:
time: 66.1 us; the launch traced here: 65.8 us
  waiting for transfers between devices  29.6 us (45%)
  starting transfers between devices  21.2 us (32%)
  Pallas kernels  10.4 us (16%)
  local copies, waits for them, and re-layouts  3.89 us (6%)
  between operations  0.78 us (1%)
    ppermute x7, waiting for transfers between devices, across(): lax.ppermute(x, axis, [(i, i ^ bit) for i in range(lax.axis_size(axis))])  19.5 us
    ppermute x8, starting transfers between devices, swapped(): return lax.ppermute(x, axis, pairs + [(j, i) for i, j in pairs])  11.6 us
    pallas_call x14, Pallas kernels, call(): pl.pallas_call(body, out_shape=outs, in_specs=[pl.BlockSpec(memory_space=...  10.4 us
    ppermute x8, waiting for transfers between devices, swapped(): return lax.ppermute(x, axis, pairs + [(j, i) for i, j in pairs])  10.2 us
    ppermute x7, starting transfers between devices, across(): lax.ppermute(x, axis, [(i, i ^ bit) for i in range(lax.axis_size(axis))])  9.55 us
    unnamed x10, local copies, waits for them, and re-layouts  3.89 us
  transfers between devices with their start and end apart: 15, of which 9 were waited for; matrix products, arithmetic and copies ran while one was open for 0% of the time, Pallas kernels for 8%

profile of v2, /device:TPU:0, one launch (start us, length us, event | category | flops | bytes accessed | tf_op | source)
XLA Modules:
  0.0 65.8 jit_solution(11159886802662252377)
XLA Ops:
  1.8 1.0 %copy-done = bf16[1,128,2,8,128]{4,3,2,1,0:T(8,128)(2,1)S(1)} copy-done((bf16[1,128,2,8,128]{4,3,2,1,0:T(8,128)(2,1)S(1)}, bf16[1,128,2,8,128]{4,3,2,1,0:T(8,128)(2,1)}, u32[]{:S(2)}) %copy-start) | copy-done | bytes 524312
  2.8 1.0 %copy-done.1 = bf16[27,128,64]{1,2,0:T(8,128)(2,1)S(1)} copy-done((bf16[27,128,64]{1,2,0:T(8,128)(2,1)S(1)}, bf16[27,128,64]{1,2,0:T(8,128)(2,1)}, u32[]{:S(2)}) %copy-start.1) | copy-done | bytes 442392
  3.9 0.9 %copy-done.3 = bf16[27,64,32]{1,2,0:T(8,128)(2,1)S(1)} copy-done((bf16[27,64,32]{1,2,0:T(8,128)(2,1)S(1)}, bf16[27,64,32]{1,2,0:T(8,128)(2,1)}, u32[]{:S(2)}) %copy-start.3) | copy-done | bytes 110616
  4.8 1.7 %shard_map.69 = (bf16[2,128,1024]{2,1,0:T(8,128)(2,1)S(1)}, bf16[128,1024]{1,0:T(8,128)(2,1)S(1)}, bf16[128,1024]{1,0:T(8,128)(2,1)S(1)}, bf16[2,384,1024]{2,1,0...) custom-call(bf16[2,32,1024]{2,1,0:T(8,128)(2,1)S(1)} %shard_map.67.own_ref._, ...), custom_call_target="tpu_custom_call" | custom-call | bytes 4382720 | tf_op jit(solution)/shard_map/pallas_call | solution.py:17
  6.5 3.1 %collective-permute-start.4 = (bf16[128,1024]{1,0:T(8,128)(2,1)S(1)}, bf16[128,1024]{1,0:T(8,128)(2,1)S(1)}, u32[]{:S(2)}, u32[]{:S(2)}) collective-permute-start(bf16[128,1024]{1,0:T(8,128)(2,1)S(1)} %get-tuple-element.36), channel_id=1, source_target_pairs={{0,4},{8,12},{4,0},{12,8},{1,5},{9,13},{5,1},{13,9},{2,6},{10,14},... | collective-permute-start | bytes 786440 | tf_op jit(solution)/shard_map/ppermute | solution.py:341
  10.2 4.5 %collective-permute-start = (bf16[2,32,1024]{2,1,0:T(8,128)(2,1)S(1)}, bf16[2,32,1024]{2,1,0:T(8,128)(2,1)S(1)}, u32[]{:S(2)}, u32[]{:S(2)}) collective-permute-start(bf16[2,32,1024]{2,1,0:T(8,128)(2,1)S(1)} %shard_map.67.own_ref._), channel_id=1, source_target_pairs={{0,4},{8,12},{4,0},{12,8},{1,5},{9,13},{5,1},{13,9},{2,6},{10,14},... | collective-permute-start | bytes 393224 | tf_op jit(solution)/shard_map/ppermute | solution.py:341
  15.6 3.3 %collective-permute-done.one_ref = bf16[2,32,1024]{2,1,0:T(8,128)(2,1)S(1)} collective-permute-done((bf16[2,32,1024]{2,1,0:T(8,128)(2,1)S(1)}, bf16[2,32,1024]{2,1,0:T(8,128)(2,1)S(1)}, u32[]{:S(2)}, u32[]{:S(2)}) %collective-permute-start) | collective-permute-done | bytes 131104 | tf_op jit(solution)/shard_map/ppermute | solution.py:341
  18.9 4.9 %collective-permute-done.1.two_ref = bf16[2,32,1024]{2,1,0:T(8,128)(2,1)S(1)} collective-permute-done((bf16[2,32,1024]{2,1,0:T(8,128)(2,1)S(1)}, bf16[2,32,1024]{2,1,0:T(8,128)(2,1)S(1)}, u32[]{:S(2)}, u32[]{:S(2)}) %collective-permute-start.1) | collective-permute-done | bytes 131104 | tf_op jit(solution)/shard_map/ppermute | solution.py:341
  23.9 1.6 %collective-permute-start.3 = (bf16[6,32,256]{2,1,0:T(8,128)(2,1)S(1)}, bf16[6,32,256]{2,1,0:T(8,128)(2,1)S(1)}, u32[]{:S(2)}, u32[]{:S(2)}) collective-permute-start(bf16[6,32,256]{2,1,0:T(8,128)(2,1)S(1)} %get-tuple-element.29), channel_id=1, source_target_pairs={{1,2},{3,0},{2,1},{0,3},{5,6},{7,4},{6,5},{4,7},{9,10},{11,8},{10,... | collective-permute-start | bytes 294920 | tf_op jit(solution)/shard_map/ppermute | solution.py:341
  26.5 2.0 %collective-permute-done.3.two_ref = bf16[6,32,256]{2,1,0:T(8,128)(2,1)S(1)} collective-permute-done((bf16[6,32,256]{2,1,0:T(8,128)(2,1)S(1)}, bf16[6,32,256]{2,1,0:T(8,128)(2,1)S(1)}, u32[]{:S(2)}, u32[]{:S(2)}) %collective-permute-start.3) | collective-permute-done | bytes 98336 | tf_op jit(solution)/shard_map/ppermute | solution.py:341
  28.5 2.6 %shard_map.70 = (bf16[4,64,1280]{2,1,0:T(8,128)(2,1)S(1)}, f32[2,64,1024]{2,1,0:T(8,128)S(1)}, f32[14,128,128]{2,1,0:T(8,128)S(1)}, bf16[6,32,1536]{2,1,0:T(8,128)(2,1)S(1)}) custom-call(bf16[6,32,1024]{2,1,0:T(8,128)(2,1)S(1)} %get-tuple-element.27.deep_ref, bf16[6,32,256]{2,1,0:T(8,128)(2,1)S(1)} %collective-permute-done.2.one_ref, ...), custom_call_target="tpu_custom_call" | custom-call | flops 1500000000 | bytes 4960256 | tf_op jit(solution)/shard_map/pallas_call | solution.py:17
  31.1 1.8 %shard_map.73 = (f32[2,2,9,32,128]{4,3,2,1,0:T(8,128)S(1)}, bf16[2,2,9,32,128]{4,3,2,1,0:T(8,128)(2,1)S(1)}) custom-call(bf16[6,32,1536]{2,1,0:T(8,128)(2,1)S(1)} %get-tuple-element.34.rows_ref, bf16[4,128,1024]{2,1,0:T(8,128)(2,1)S(1)} %get-tuple-element.38.cot_ref, bf16[4,128,128]{2,1,0:T(8,128)(2,1)S(1)} %collective-permute-done.6.one_ref, ...), custom_call_target="tpu_custom_call" | custom-call | flops 1100000000 | bytes 4669440 | tf_op jit(solution)/shard_map/pallas_call | solution.py:17
  32.9 1.5 %collective-permute-start.8 = (bf16[2,2,9,32,128]{4,3,2,1,0:T(8,128)(2,1)S(1)}, bf16[2,2,9,32,128]{4,3,2,1,0:T(8,128)(2,1)S(1)}, u32[]{:S(2)}, u32[]{:S(2)}) collective-permute-start(bf16[2,2,9,32,128]{4,3,2,1,0:T(8,128)(2,1)S(1)} %get-tuple-element.44), channel_id=1, source_target_pairs={{0,1},{1,0},{2,3},{3,2},{4,5},{5,4},{6,7},{7,6},{8,9},{9,8},{10,11... | collective-permute-start | bytes 884744 | tf_op jit(solution)/shard_map/ppermute | solution.py:345
  34.4 1.2 %collective-permute-done.8.got_ref = bf16[2,2,9,32,128]{4,3,2,1,0:T(8,128)(2,1)S(1)} collective-permute-done((bf16[2,2,9,32,128]{4,3,2,1,0:T(8,128)(2,1)S(1)}, bf16[2,2,9,32,128]{4,3,2,1,0:T(8,128)(2,1)S(1)}, u32[]{:S(2)}, u32[]{:S(2)}) %collective-permute-start.8) | collective-permute-done | bytes 294944 | tf_op jit(solution)/shard_map/ppermute | solution.py:345
  35.7 1.6 %collective-permute-start.9 = (bf16[2,9,32,128]{3,2,1,0:T(8,128)(2,1)S(1)}, bf16[2,9,32,128]{3,2,1,0:T(8,128)(2,1)S(1)}, u32[]{:S(2)}, u32[]{:S(2)}) collective-permute-start(bf16[2,9,32,128]{3,2,1,0:T(8,128)(2,1)S(1)} %get-tuple-element.46), channel_id=1, source_target_pairs={{0,16},{16,0},{1,17},{17,1},{2,18},{18,2},{3,19},{19,3},{4,20},{20... | collective-permute-start | bytes 442376 | tf_op jit(solution)/shard_map/ppermute | solution.py:345
  37.3 4.6 %collective-permute-done.9.got_ref = bf16[2,9,32,128]{3,2,1,0:T(8,128)(2,1)S(1)} collective-permute-done((bf16[2,9,32,128]{3,2,1,0:T(8,128)(2,1)S(1)}, bf16[2,9,32,128]{3,2,1,0:T(8,128)(2,1)S(1)}, u32[]{:S(2)}, u32[]{:S(2)}) %collective-permute-start.9) | collective-permute-done | bytes 147488 | tf_op jit(solution)/shard_map/ppermute | solution.py:345
  42.4 3.9 %collective-permute-done.10.two_ref = bf16[9,32,128]{2,1,0:T(8,128)(2,1)S(1)} collective-permute-done((bf16[9,32,128]{2,1,0:T(8,128)(2,1)S(1)}, bf16[9,32,128]{2,1,0:T(8,128)(2,1)S(1)}, u32[]{:S(2)}, u32[]{:S(2)}) %collective-permute-start.10) | collective-permute-done | bytes 73760 | tf_op jit(solution)/shard_map/ppermute | solution.py:345
  46.4 2.5 %collective-permute-start.11 = (bf16[9,32,128]{2,1,0:T(8,128)(2,1)S(1)}, bf16[9,32,128]{2,1,0:T(8,128)(2,1)S(1)}, u32[]{:S(2)}, u32[]{:S(2)}) collective-permute-start(bf16[9,32,128]{2,1,0:T(8,128)(2,1)S(1)} %shard_map.76.one_ref), channel_id=1, source_target_pairs={{0,4},{4,0},{8,12},{12,8},{1,5},{5,1},{9,13},{13,9},{2,6},{6,2},{1... | collective-permute-start | bytes 221192 | tf_op jit(solution)/shard_map/ppermute | solution.py:345
  48.9 2.3 %collective-permute-done.11.two_ref = bf16[9,32,128]{2,1,0:T(8,128)(2,1)S(1)} collective-permute-done((bf16[9,32,128]{2,1,0:T(8,128)(2,1)S(1)}, bf16[9,32,128]{2,1,0:T(8,128)(2,1)S(1)}, u32[]{:S(2)}, u32[]{:S(2)}) %collective-permute-start.11) | collective-permute-done | bytes 73760 | tf_op jit(solution)/shard_map/ppermute | solution.py:345
  51.3 2.8 %collective-permute-start.12 = (bf16[9,32,128]{2,1,0:T(8,128)(2,1)S(1)}, bf16[9,32,128]{2,1,0:T(8,128)(2,1)S(1)}, u32[]{:S(2)}, u32[]{:S(2)}) collective-permute-start(bf16[9,32,128]{2,1,0:T(8,128)(2,1)S(1)} %shard_map.77.one_ref), channel_id=1, source_target_pairs={{0,12},{4,8},{8,4},{12,0},{1,13},{5,9},{9,5},{13,1},{2,14},{6,10},... | collective-permute-start | bytes 221192 | tf_op jit(solution)/shard_map/ppermute | solution.py:345
  54.1 3.5 %collective-permute-done.12.two_ref = bf16[9,32,128]{2,1,0:T(8,128)(2,1)S(1)} collective-permute-done((bf16[9,32,128]{2,1,0:T(8,128)(2,1)S(1)}, bf16[9,32,128]{2,1,0:T(8,128)(2,1)S(1)}, u32[]{:S(2)}, u32[]{:S(2)}) %collective-permute-start.12) | collective-permute-done | bytes 73760 | tf_op jit(solution)/shard_map/ppermute | solution.py:345
  58.1 3.9 %collective-permute-done.13.got_ref = bf16[9,32,128]{2,1,0:T(8,128)(2,1)S(1)} collective-permute-done((bf16[9,32,128]{2,1,0:T(8,128)(2,1)S(1)}, bf16[9,32,128]{2,1,0:T(8,128)(2,1)S(1)}, u32[]{:S(2)}, u32[]{:S(2)}) %collective-permute-start.13) | collective-permute-done | bytes 73760 | tf_op jit(solution)/shard_map/ppermute | solution.py:345
  62.1 2.5 %shard_map.71 = bf16[128,2,8,128]{3,2,1,0:T(8,128)(2,1)} custom-call(bf16[4,64,1280]{2,1,0:T(8,128)(2,1)S(1)} %get-tuple-element.32.hidden_ref, bf16[384,576]{1,0:T(8,128)(2,1)S(1)} %get-tuple-element.33.w2_ref), custom_call_target="tpu_custom_call" | custom-call | flops 900000000 | bytes 1622016 | tf_op jit(solution)/shard_map/pallas_call | solution.py:17
  64.6 1.2 %shard_map.80 = (f32[27,32,32]{2,1,0:T(8,128)}, f32[27,64,64]{2,1,0:T(8,128)}) custom-call(bf16[2,9,32,128]{3,2,1,0:T(8,128)(2,1)S(1)} %shard_map.79.own_ref, bf16[2,9,32,128]{3,2,1,0:T(8,128)(2,1)S(1)} %collective-permute-done.14.got_ref), custom_call_target="tpu_custom_call" | custom-call | bytes 847872 | tf_op jit(solution)/shard_map/pallas_call | solution.py:17
  (30 shorter events, 5.1 us)
Async XLA Ops:
  0.6 0.9 %copy-start.4 = (bf16[1,32,2,8,128]{4,3,2,1,0:T(8,128)(2,1)S(1)}, bf16[1,32,2,8,128]{4,3,2,1,0:T(8,128)(2,1)}, u32[]{:S(2)}) copy-start(bf16[1,32,2,8,128]{4,3,2,1,0:T(8,128)(2,1)} %param.4) | copy-start | bytes 393220
  1.8 1.0 %copy-start = (bf16[1,128,2,8,128]{4,3,2,1,0:T(8,128)(2,1)S(1)}, bf16[1,128,2,8,128]{4,3,2,1,0:T(8,128)(2,1)}, u32[]{:S(2)}) copy-start(bf16[1,128,2,8,128]{4,3,2,1,0:T(8,128)(2,1)} %param.7) | copy-start | bytes 1572868
  2.8 1.0 %copy-start.1 = (bf16[27,128,64]{1,2,0:T(8,128)(2,1)S(1)}, bf16[27,128,64]{1,2,0:T(8,128)(2,1)}, u32[]{:S(2)}) copy-start(bf16[27,128,64]{1,2,0:T(8,128)(2,1)} %param.6) | copy-start | bytes 1327108
  3.9 0.9 %copy-start.3 = (bf16[27,64,32]{1,2,0:T(8,128)(2,1)S(1)}, bf16[27,64,32]{1,2,0:T(8,128)(2,1)}, u32[]{:S(2)}) copy-start(bf16[27,64,32]{1,2,0:T(8,128)(2,1)} %param.5) | copy-start | bytes 331780
  6.5 19.1 %collective-permute-start.4 = (bf16[128,1024]{1,0:T(8,128)(2,1)S(1)}, bf16[128,1024]{1,0:T(8,128)(2,1)S(1)}, u32[]{:S(2)}, u32[]{:S(2)}) collective-permute-start(bf16[128,1024]{1,0:T(8,128)(2,1)S(1)} %get-tuple-element.36), channel_id=1, source_target_pairs={{0,4},{8,12},{4,0},{12,8},{1,5},{9,13},{5,1},{13,9},{2,6},{10,14},... | collective-permute-start | bytes 786440 | tf_op jit(solution)/shard_map/ppermute | solution.py:341
  9.5 16.0 %collective-permute-start.5 = (bf16[128,1024]{1,0:T(8,128)(2,1)S(1)}, bf16[128,1024]{1,0:T(8,128)(2,1)S(1)}, u32[]{:S(2)}, u32[]{:S(2)}) collective-permute-start(bf16[128,1024]{1,0:T(8,128)(2,1)S(1)} %get-tuple-element.37), channel_id=1, source_target_pairs={{4,8},{8,4},{5,9},{9,5},{6,10},{10,6},{7,11},{11,7},{20,24},{24,20... | collective-permute-start | bytes 786440 | tf_op jit(solution)/shard_map/ppermute | solution.py:341
  10.2 8.7 %collective-permute-start = (bf16[2,32,1024]{2,1,0:T(8,128)(2,1)S(1)}, bf16[2,32,1024]{2,1,0:T(8,128)(2,1)S(1)}, u32[]{:S(2)}, u32[]{:S(2)}) collective-permute-start(bf16[2,32,1024]{2,1,0:T(8,128)(2,1)S(1)} %shard_map.67.own_ref._), channel_id=1, source_target_pairs={{0,4},{8,12},{4,0},{12,8},{1,5},{9,13},{5,1},{13,9},{2,6},{10,14},... | collective-permute-start | bytes 393224 | tf_op jit(solution)/shard_map/ppermute | solution.py:341
  14.7 9.1 %collective-permute-start.1 = (bf16[2,32,1024]{2,1,0:T(8,128)(2,1)S(1)}, bf16[2,32,1024]{2,1,0:T(8,128)(2,1)S(1)}, u32[]{:S(2)}, u32[]{:S(2)}) collective-permute-start(bf16[2,32,1024]{2,1,0:T(8,128)(2,1)S(1)} %shard_map.67.own_ref._), channel_id=1, source_target_pairs={{4,8},{12,0},{8,4},{0,12},{5,9},{13,1},{9,5},{1,13},{6,10},{14,2},... | collective-permute-start | bytes 393224 | tf_op jit(solution)/shard_map/ppermute | solution.py:341
  23.8 2.7 %collective-permute-start.2 = (bf16[6,32,256]{2,1,0:T(8,128)(2,1)S(1)}, bf16[6,32,256]{2,1,0:T(8,128)(2,1)S(1)}, u32[]{:S(2)}, u32[]{:S(2)}) collective-permute-start(bf16[6,32,256]{2,1,0:T(8,128)(2,1)S(1)} %get-tuple-element.28), channel_id=1, source_target_pairs={{0,1},{2,3},{1,0},{3,2},{4,5},{6,7},{5,4},{7,6},{8,9},{10,11},{9,8... | collective-permute-start | bytes 294920 | tf_op jit(solution)/shard_map/ppermute | solution.py:341
  23.9 4.6 %collective-permute-start.3 = (bf16[6,32,256]{2,1,0:T(8,128)(2,1)S(1)}, bf16[6,32,256]{2,1,0:T(8,128)(2,1)S(1)}, u32[]{:S(2)}, u32[]{:S(2)}) collective-permute-start(bf16[6,32,256]{2,1,0:T(8,128)(2,1)S(1)} %get-tuple-element.29), channel_id=1, source_target_pairs={{1,2},{3,0},{2,1},{0,3},{5,6},{7,4},{6,5},{4,7},{9,10},{11,8},{10,... | collective-permute-start | bytes 294920 | tf_op jit(solution)/shard_map/ppermute | solution.py:341
  25.7 5.3 %collective-permute-start.6 = (bf16[4,128,128]{2,1,0:T(8,128)(2,1)S(1)}, bf16[4,128,128]{2,1,0:T(8,128)(2,1)S(1)}, u32[]{:S(2)}, u32[]{:S(2)}) collective-permute-start(bf16[4,128,128]{2,1,0:T(8,128)(2,1)S(1)} %get-tuple-element.39), channel_id=1, source_target_pairs={{0,1},{2,3},{1,0},{3,2},{4,5},{6,7},{5,4},{7,6},{8,9},{10,11},{9,8... | collective-permute-start | bytes 393224 | tf_op jit(solution)/shard_map/ppermute | solution.py:341
  25.9 5.2 %collective-permute-start.7 = (bf16[4,128,128]{2,1,0:T(8,128)(2,1)S(1)}, bf16[4,128,128]{2,1,0:T(8,128)(2,1)S(1)}, u32[]{:S(2)}, u32[]{:S(2)}) collective-permute-start(bf16[4,128,128]{2,1,0:T(8,128)(2,1)S(1)} %get-tuple-element.40), channel_id=1, source_target_pairs={{1,2},{2,1},{5,6},{6,5},{9,10},{10,9},{13,14},{14,13},{17,18},{18,... | collective-permute-start | bytes 393224 | tf_op jit(solution)/shard_map/ppermute | solution.py:341
  28.5 2.6 %copy-start.2 = (bf16[27,128,64]{1,2,0:T(8,128)(2,1)S(1)}, bf16[27,128,64]{1,2,0:T(8,128)(2,1)}, u32[]{:S(2)}) copy-start(bf16[27,128,64]{1,2,0:T(8,128)(2,1)} %param.6) | copy-start | bytes 1327108
  32.9 2.7 %collective-permute-start.8 = (bf16[2,2,9,32,128]{4,3,2,1,0:T(8,128)(2,1)S(1)}, bf16[2,2,9,32,128]{4,3,2,1,0:T(8,128)(2,1)S(1)}, u32[]{:S(2)}, u32[]{:S(2)}) collective-permute-start(bf16[2,2,9,32,128]{4,3,2,1,0:T(8,128)(2,1)S(1)} %get-tuple-element.44), channel_id=1, source_target_pairs={{0,1},{1,0},{2,3},{3,2},{4,5},{5,4},{6,7},{7,6},{8,9},{9,8},{10,11... | collective-permute-start | bytes 884744 | tf_op jit(solution)/shard_map/ppermute | solution.py:345
  35.7 6.2 %collective-permute-start.9 = (bf16[2,9,32,128]{3,2,1,0:T(8,128)(2,1)S(1)}, bf16[2,9,32,128]{3,2,1,0:T(8,128)(2,1)S(1)}, u32[]{:S(2)}, u32[]{:S(2)}) collective-permute-start(bf16[2,9,32,128]{3,2,1,0:T(8,128)(2,1)S(1)} %get-tuple-element.46), channel_id=1, source_target_pairs={{0,16},{16,0},{1,17},{17,1},{2,18},{18,2},{3,19},{19,3},{4,20},{20... | collective-permute-start | bytes 442376 | tf_op jit(solution)/shard_map/ppermute | solution.py:345
  41.9 4.4 %collective-permute-start.10 = (bf16[9,32,128]{2,1,0:T(8,128)(2,1)S(1)}, bf16[9,32,128]{2,1,0:T(8,128)(2,1)S(1)}, u32[]{:S(2)}, u32[]{:S(2)}) collective-permute-start(bf16[9,32,128]{2,1,0:T(8,128)(2,1)S(1)} %get-tuple-element.48), channel_id=1, source_target_pairs={{0,2},{1,3},{2,0},{3,1},{4,6},{5,7},{6,4},{7,5},{8,10},{9,11},{10,... | collective-permute-start | bytes 221192 | tf_op jit(solution)/shard_map/ppermute | solution.py:345
  46.4 4.9 %collective-permute-start.11 = (bf16[9,32,128]{2,1,0:T(8,128)(2,1)S(1)}, bf16[9,32,128]{2,1,0:T(8,128)(2,1)S(1)}, u32[]{:S(2)}, u32[]{:S(2)}) collective-permute-start(bf16[9,32,128]{2,1,0:T(8,128)(2,1)S(1)} %shard_map.76.one_ref), channel_id=1, source_target_pairs={{0,4},{4,0},{8,12},{12,8},{1,5},{5,1},{9,13},{13,9},{2,6},{6,2},{1... | collective-permute-start | bytes 221192 | tf_op jit(solution)/shard_map/ppermute | solution.py:345
  51.3 6.3 %collective-permute-start.12 = (bf16[9,32,128]{2,1,0:T(8,128)(2,1)S(1)}, bf16[9,32,128]{2,1,0:T(8,128)(2,1)S(1)}, u32[]{:S(2)}, u32[]{:S(2)}) collective-permute-start(bf16[9,32,128]{2,1,0:T(8,128)(2,1)S(1)} %shard_map.77.one_ref), channel_id=1, source_target_pairs={{0,12},{4,8},{8,4},{12,0},{1,13},{5,9},{9,5},{13,1},{2,14},{6,10},... | collective-permute-start | bytes 221192 | tf_op jit(solution)/shard_map/ppermute | solution.py:345
  57.6 4.4 %collective-permute-start.13 = (bf16[9,32,128]{2,1,0:T(8,128)(2,1)S(1)}, bf16[9,32,128]{2,1,0:T(8,128)(2,1)S(1)}, u32[]{:S(2)}, u32[]{:S(2)}) collective-permute-start(bf16[9,32,128]{2,1,0:T(8,128)(2,1)S(1)} %shard_map.78.own_ref), channel_id=1, source_target_pairs={{0,2},{1,3},{2,0},{3,1},{4,6},{5,7},{6,4},{7,5},{8,10},{9,11},{10,... | collective-permute-start | bytes 221192 | tf_op jit(solution)/shard_map/ppermute | solution.py:345
  62.0 2.6 %collective-permute-start.14 = (bf16[2,9,32,128]{3,2,1,0:T(8,128)(2,1)S(1)}, bf16[2,9,32,128]{3,2,1,0:T(8,128)(2,1)S(1)}, u32[]{:S(2)}, u32[]{:S(2)}) collective-permute-start(bf16[2,9,32,128]{3,2,1,0:T(8,128)(2,1)S(1)} %shard_map.79.own_ref), channel_id=1, source_target_pairs={{0,1},{1,0},{2,3},{3,2},{4,5},{5,4},{6,7},{7,6},{8,9},{9,8},{10,11... | collective-permute-start | bytes 442376 | tf_op jit(solution)/shard_map/ppermute | solution.py:345

commit v3 on v2

--- a/solution.py
+++ b/solution.py
@@ -17,7 +17,7 @@
     return pl.pallas_call(
         body,
         out_shape=outs,
-        in_specs=[pl.BlockSpec(memory_space=pl.ANY if n in far else pltpu.VMEM) for n in range(len(args))],
+        in_specs=[pl.BlockSpec(memory_space=pltpu.HBM if n in far else pltpu.VMEM) for n in range(len(args))],
         out_specs=[pl.BlockSpec(memory_space=pltpu.VMEM)] * len(outs),
         scratch_shapes=list(scratch),
         compiler_params=pltpu.CompilerParams(vmem_limit_bytes=VMEM_BYTES),
@@ -61,41 +61,63 @@
     return copies
 
 
-def volume_kernel(vol_ref, out_ref, held, scratch, sems):
-    (copy,) = begin_copies([(vol_ref, held)], sems)
-    copy.wait()
-
-    def store(d, h, row):
-        out_ref[d, :, h * LANES : (h + 1) * LANES] = row.astype(BF)
-
-    by_rows(held, scratch, store)
-
-
-def cotangent_kernel(
-    _, cot_ref, k1_ref, k2_ref, own_ref, one_ref, two_ref, moved_ref, w1_ref, w2_ref, held, k1, k2, scratch, sems
+def prepare_kernel(
+    vol_ref, cot_ref, k1_ref, k2_ref, own_ref, moved_ref, w1_ref, w2_ref, back_ref, one_ref, two_ref,
+    vol, cot, k1, k2, vol_scratch, cot_scratch, sems,
 ):
-    copies = begin_copies([(cot_ref, held), (k1_ref, k1), (k2_ref, k2)], sems)
+    copies = begin_copies([(cot_ref, cot), (k2_ref, k2), (vol_ref, vol), (k1_ref, k1)], sems)
     copies[0].wait()
+    out, depth, height, _ = cot.shape
+    rows = [[None] * height for _ in range(depth)]
 
     def store(d, h, row):
         lanes = slice(h * LANES, (h + 1) * LANES)
-        own_ref[d, :, lanes] = row.astype(BF)
-        channels = row.shape[0]
+        rows[d][h] = row.astype(BF)
         for n, c in enumerate((-1, 0, 1)):
-            moved_ref[d, n * channels : (n + 1) * channels, lanes] = moved_along_width(row, c).astype(BF)
-
-    by_rows(held, scratch, store)
+            moved_ref[d, n * out : (n + 1) * out, lanes] = moved_along_width(row, c).astype(BF)
+
+    by_rows(cot, cot_scratch, store)
+    copies[1].wait()
+    mid = k2.shape[1]
+    none = jnp.zeros((out, 2 * LANES), BF)
+    padded = [jnp.concatenate([none, *rows[d], none], axis=1) for d in range(depth)]
     is_odd = odd("dep")
-    one_ref[...] = jnp.where(is_odd, own_ref[0], own_ref[own_ref.shape[0] - 1])
-    two_ref[...] = jnp.where(is_odd, own_ref[own_ref.shape[0] - 1], own_ref[0])
-    copies[1].wait()
-    copies[2].wait()
-    mid, out = k1.shape[2], k2.shape[2]
+    faces = [[], []]
+    for e in range(depth + 2):
+        reached = [(d, e - 1 - d) for d in range(depth) if abs(e - 1 - d) <= 1]
+        w = jnp.concatenate(
+            [
+                k2[9 * (a + 1) + 3 * b : 9 * (a + 1) + 3 * b + 3].reshape(3 * mid, out)
+                for _, a in reached
+                for b in range(3)
+            ],
+            axis=1,
+        )
+        for j in range(0, height + 2, 2):
+            rhs = jnp.concatenate(
+                [padded[d][:, (j + 2 - b) * LANES : (j + 4 - b) * LANES] for d, _ in reached for b in range(3)], axis=0
+            )
+            y = jnp.dot(w, rhs, preferred_element_type=F32)
+            back = sum(moved_along_width(y[n * mid : (n + 1) * mid], n - 1) for n in range(3))
+            if 0 < e < depth + 1:
+                back_ref[e - 1, :, j * LANES : (j + 2) * LANES] = back
+            else:
+                faces[e > 0].append(back.astype(BF))
+    low, high = (jnp.concatenate(face, axis=1) for face in faces)
+    one_ref[...] = jnp.where(is_odd, low, high)
+    two_ref[...] = jnp.where(is_odd, high, low)
+    copies[3].wait()
     for c in range(3):
         one = jnp.concatenate([k1[3 * ab + c] for ab in range(9)], axis=0)
         w1_ref[c * mid : (c + 1) * mid, :] = one.astype(F32).T.astype(BF)
         two = jnp.concatenate([k2[3 * ab + c] for ab in range(9)], axis=0)
         w2_ref[c * out : (c + 1) * out, :] = two.astype(F32).T.astype(BF)
+    copies[2].wait()
+
+    def store_own(d, h, row):
+        own_ref[d, :, h * LANES : (h + 1) * LANES] = row.astype(BF)
+
+    by_rows(vol, vol_scratch, store_own)
 
 
 def sides(axis, one, two):
@@ -107,17 +129,39 @@
     return before, after
 
 
-def rim_kernel(own_ref, one_ref, two_ref, deep_ref, send_one_ref, send_two_ref):
-    before, after = sides("dep", one_ref[...], two_ref[...])
-    edge, own = one_ref.shape[0], own_ref.shape[0]
-    deep_ref[:edge] = before
-    deep_ref[edge : edge + own] = own_ref[...]
-    deep_ref[edge + own :] = after
+def rim_kernel(own_ref, one_ref, two_ref, deep_ref, send_one_ref, send_two_ref, scratch):
+    depth = own_ref.shape[0]
+    deep_ref[depth : 2 * depth] = own_ref[...]
+    for at, side in zip((0, 2 * depth), sides("dep", one_ref[...], two_ref[...]), strict=True):
+
+        def store(d, h, row, at=at):
+            deep_ref[at + d, :, h * LANES : (h + 1) * LANES] = row.astype(BF)
+
+        by_rows(side, scratch, store)
     n, cells = send_one_ref.shape[2], deep_ref.shape[2]
     first, last = deep_ref[:, :, :n], deep_ref[:, :, cells - n :]
     is_odd = odd("hgt")
     send_one_ref[...] = jnp.where(is_odd, first, last)
     send_two_ref[...] = jnp.where(is_odd, last, first)
+
+
+def back_rim_kernel(own_ref, one_ref, two_ref, back_ref, send_one_ref, send_two_ref):
+    before, after = sides("dep", one_ref[...], two_ref[...])
+    last = own_ref.shape[0] - 1
+    cells = back_ref.shape[2]
+    ends = []
+    for d in range(last + 1):
+        total = own_ref[d]
+        if d == 0:
+            total = total + before.astype(F32)
+        if d == last:
+            total = total + after.astype(F32)
+        back_ref[d] = total[:, LANES : LANES + cells]
+        ends.append((total[:, :LANES].astype(BF), total[:, LANES + cells :].astype(BF)))
+    is_odd = odd("hgt")
+    for d, (low, high) in enumerate(ends):
+        send_one_ref[d] = jnp.where(is_odd, low, high)
+        send_two_ref[d] = jnp.where(is_odd, high, low)
 
 
 def widened(deep_ref, one_ref, two_ref):
@@ -212,27 +256,20 @@
     out_ref[...] = scratch[...].reshape(out_ref.shape).astype(BF)
 
 
-def delta_kernel(direct, rows_ref, cot_ref, one_ref, two_ref, k2_ref, slope_ref, g2_ref, *outs_and_scratch):
+def delta_kernel(direct, rows_ref, back_ref, one_ref, two_ref, slope_ref, g2_ref, *outs_and_scratch):
     *out_refs, delta_ref = outs_and_scratch
-    cots = widened(cot_ref, one_ref, two_ref)
-    mid = k2_ref.shape[1]
-    own, cells = slope_ref.shape[0], slope_ref.shape[2]
-    w = jnp.concatenate([k2_ref[3 * ab : 3 * ab + 3].reshape(3 * mid, k2_ref.shape[2]) for ab in range(9)], axis=1)
+    before, after = sides("hgt", one_ref[...], two_ref[...])
+    own, mid, cells = slope_ref.shape
     for d in range(own):
-        for at in range(0, cells, 2 * LANES):
-            rhs = jnp.concatenate(
-                [
-                    cots[d + 2 - a][:, at + (2 - b) * LANES : at + (4 - b) * LANES]
-                    for a in range(3)
-                    for b in range(3)
-                ],
-                axis=0,
-            )
-            y = jnp.dot(w, rhs, preferred_element_type=F32)
-            back = sum(moved_along_width(y[n * mid : (n + 1) * mid], n - 1) for n in range(3))
-            delta = back * slope_ref[d, :, at : at + 2 * LANES]
+        for at in range(0, cells, LANES):
+            back = back_ref[d, :, at : at + LANES]
+            if at == 0:
+                back = back + before[d].astype(F32)
+            if at == cells - LANES:
+                back = back + after[d].astype(F32)
+            delta = back * slope_ref[d, :, at : at + LANES]
             for n in range(3):
-                delta_ref[n * mid : (n + 1) * mid, d * cells + at : d * cells + at + 2 * LANES] = moved_along_width(
+                delta_ref[n * mid : (n + 1) * mid, d * cells + at : d * cells + at + LANES] = moved_along_width(
                     delta, n - 1
                 ).astype(BF)
     left = delta_ref[...]
@@ -268,50 +305,86 @@
             out_refs[0][j] = block
         return
     keep_ref, send_ref = out_refs
-    parts, halves, units, size, _ = keep_ref.shape
+    parts, halves, deps, units, size, _ = keep_ref.shape
+    each = mid // parts
     core = odd("hgt")
 
-    def value(part, unit):
+    def value(part, number):
+        unit, start = divmod(number * size, each)
         if unit < 28:
-            start = (2 * part + unit % 2) * size
+            start += (2 * part + unit % 2) * each
             return g2_ref[unit // 2, start : start + size, :]
         if unit < 35:
-            return blocks[unit - 28][part * size : (part + 1) * size]
+            start += part * each
+            return blocks[unit - 28][start : start + size]
         return jnp.zeros((size, LANES), F32)
 
     for part in range(parts):
         for half in range(halves):
-            for unit in range(units):
-                one, two = (value(part, (2 * half + c) * units + unit) for c in range(2))
-                keep_ref[part, half, unit] = jnp.where(core, two, one)
-                send_ref[part, half, unit] = jnp.where(core, one, two).astype(BF)
-
-
-def halve_kernel(axis, bit, keep_ref, got_ref, kept_ref, send_ref):
-    mine = lax.rem(lax.div(lax.axis_index(axis), bit), 2)
-    kept_ref[...] = keep_ref[mine] + got_ref[mine].astype(F32)
-    send_ref[...] = (keep_ref[1 - mine] + got_ref[1 - mine].astype(F32)).astype(BF)
-
-
-def add_kernel(one_ref, two_ref, out_ref):
-    out_ref[...] = (one_ref[...].astype(F32) + two_ref[...].astype(F32)).astype(BF)
-
-
-def order_kernel(axis, bit, own_ref, got_ref, out_ref):
-    mine = lax.rem(lax.div(lax.axis_index(axis), bit), 2)
-    out_ref[mine] = own_ref[...]
-    out_ref[1 - mine] = got_ref[...]
+            for dep in range(deps):
+                for unit in range(units):
+                    one, two = (value(part, ((2 * half + c) * deps + dep) * units + unit) for c in range(2))
+                    keep_ref[part, half, dep, unit] = jnp.where(core, two, one)
+                    send_ref[part, half, dep, unit] = jnp.where(core, one, two).astype(BF)
+
+
+def plane_kernel(moves, keep_ref, got_ref, kept_ref, *send_refs):
+    part = lax.rem(lax.axis_index("dp"), keep_ref.shape[0])
+    half = lax.div(lax.axis_index("hgt"), 2)
+    kept_ref[...] = keep_ref[part, half] + got_ref[part, half].astype(F32)
+    for (x, y), send_ref in zip(moves, send_refs, strict=True):
+        p = 1 - part if x else part
+        h = 1 - half if y else half
+        send_ref[...] = (keep_ref[p, h] + got_ref[p, h].astype(F32)).astype(BF)
+
+
+def depth_kernel(n_got, *refs):
+    kept_ref, got_refs, (_, out_ref, *send_refs) = refs[0], refs[1 : 1 + n_got], refs[1 + n_got :]
+    me = lax.axis_index("dep")
+
+    def total(at):
+        value = kept_ref[at]
+        for ref in got_refs:
+            value = value + ref[at].astype(F32)
+        return value
+
+    out_ref[...] = total(me)
+    for n, ref in enumerate(send_refs):
+        ref[...] = total(lax.bitwise_xor(me, n + 1)).astype(BF)
+
+
+def finish_kernel(kept_ref, *refs):
+    *got_refs, out_ref = refs
+    value = kept_ref[...]
+    for ref in got_refs:
+        value = value + ref[...].astype(F32)
+    out_ref[...] = value.astype(BF)
+
+
+def order_kernel(axis, bit, own_ref, *refs):
+    *got_refs, out_ref = refs
+    me = lax.div(lax.axis_index(axis), bit)
+    out_ref[me] = own_ref[...]
+    for n, ref in enumerate(got_refs):
+        out_ref[lax.bitwise_xor(me, n + 1)] = ref[...]
 
 
 def unpack_kernel(own_ref, got_ref, g1_ref, g2_ref):
-    _, units, size, _ = own_ref.shape
+    _, deps, units, block, _ = own_ref.shape
+    size = g1_ref.shape[1]
     core = odd("hgt")
 
-    def get(unit):
-        quarter = unit // units
-        at = quarter // 2, unit % units
+    def block_at(number):
+        quarter, number = divmod(number, deps * units)
+        at = quarter // 2, number // units, number % units
         one, two = (got_ref, own_ref) if quarter % 2 else (own_ref, got_ref)
         return jnp.where(core, two[at], one[at]).astype(F32)
+
+    def get(unit):
+        first, start = divmod(unit * size, block)
+        if size < block:
+            return block_at(first)[start : start + size]
+        return jnp.concatenate([block_at(first + n) for n in range(size // block)], axis=0)
 
     for j in range(14):
         for half in range(2):
@@ -345,59 +418,64 @@
     return lax.ppermute(x, axis, [(i, i ^ bit) for i in range(lax.axis_size(axis))])
 
 
+def across_plane(x, moves):
+    dp, hgt = moves
+    if not dp:
+        return across(x, "hgt", 2)
+    if not hgt:
+        return across(x, "dp", 1)
+    size = lax.axis_size("dp") * lax.axis_size("hgt")
+    flip = lax.axis_size("hgt") + 2
+    return lax.ppermute(x, ("dp", "hgt"), [(i, i ^ flip) for i in range(size)])
+
+
 def per_device(volume, kernel_first, kernel_second, cotangent):
     _, inner, depth, height, width = volume.shape
     mid, out = kernel_first.shape[1], kernel_second.shape[1]
     cells = height * width
-    parts, quarters = lax.axis_size("dp"), lax.axis_size("hgt")
+    parts, quarters, deps = lax.axis_size("dp"), lax.axis_size("hgt"), lax.axis_size("dep")
     k1, k2 = jnp.swapaxes(kernel_first, 1, 2), jnp.swapaxes(kernel_second, 1, 2)
     rows = depth * height
 
-    (vol,) = call(
-        volume_kernel,
-        [shape((depth, inner, cells), BF)],
-        [volume[0]],
+    one, two = swapped(volume[0], "dep", "one"), swapped(volume[0], "dep", "inner")
+    vol, moved, w1, w2, back, back_one, back_two = call(
+        prepare_kernel,
         [
-            pltpu.VMEM(volume.shape[1:], BF),
-            pltpu.VMEM((inner * rows, width), F32),
-            pltpu.SemaphoreType.DMA((1,)),
-        ],
-        far=(0,),
-    )
-    one, two = swapped(vol, "dep", "one"), swapped(vol, "dep", "two")
-    cot, cot_one, cot_two, moved, w1, w2 = call(
-        cotangent_kernel,
-        [
-            shape((depth, out, cells), BF),
-            shape((out, cells), BF),
-            shape((out, cells), BF),
+            shape((depth, inner, cells), BF),
             shape((depth, 3 * out, cells), BF),
             shape((3 * mid, 9 * inner), BF),
             shape((3 * out, 9 * mid), BF),
+            shape((depth, mid, cells + 2 * width), F32),
+            shape((mid, cells + 2 * width), BF),
+            shape((mid, cells + 2 * width), BF),
         ],
-        [vol, cotangent[0], k1, k2],
+        [volume[0], cotangent[0], k1, k2],
         [
+            pltpu.VMEM(volume.shape[1:], BF),
             pltpu.VMEM(cotangent.shape[1:], BF),
             pltpu.VMEM(k1.shape, BF),
             pltpu.VMEM(k2.shape, BF),
+            pltpu.VMEM((inner * rows, width), F32),
             pltpu.VMEM((out * rows, width), F32),
-            pltpu.SemaphoreType.DMA((3,)),
+            pltpu.SemaphoreType.DMA((4,)),
         ],
         far=(0, 1, 2, 3),
+        flops=1_100_000_000,
     )
     deep, one, two = call(
         rim_kernel,
-        [shape((depth + 4, inner, cells), BF)] + [shape((depth + 4, inner, 2 * width), BF)] * 2,
+        [shape((3 * depth, inner, cells), BF)] + [shape((3 * depth, inner, 2 * width), BF)] * 2,
         [vol, one, two],
-    )
-    one, two = swapped(one, "hgt", "one"), swapped(two, "hgt", "two")
-    cot_one, cot_two = swapped(cot_one, "dep", "one"), swapped(cot_two, "dep", "inner")
-    cot_deep, cot_one, cot_two = call(
-        rim_kernel,
-        [shape((depth + 2, out, cells), BF)] + [shape((depth + 2, out, width), BF)] * 2,
-        [cot, cot_one[None], cot_two[None]],
-    )
-    cot_one, cot_two = swapped(cot_one, "hgt", "one"), swapped(cot_two, "hgt", "inner")
+        [pltpu.VMEM((inner * rows, width), F32)],
+    )
+    one, two = swapped(one, "hgt", "one"), swapped(two, "hgt", "inner")
+    back_one, back_two = swapped(back_one, "dep", "one"), swapped(back_two, "dep", "inner")
+    back, back_one, back_two = call(
+        back_rim_kernel,
+        [shape((depth, mid, cells), F32)] + [shape((depth, mid, width), BF)] * 2,
+        [back, back_one, back_two],
+    )
+    back_one, back_two = swapped(back_one, "hgt", "one"), swapped(back_two, "hgt", "inner")
 
     hidden, slope, g2, wide = call(
         hidden_kernel,
@@ -405,56 +483,71 @@
             shape((depth + 2, mid, cells + 2 * width), BF),
             shape((depth, mid, cells), F32),
             shape((14, out, LANES), F32),
-            shape((depth + 4, inner, cells + 4 * width), BF),
+            shape((3 * depth, inner, cells + 4 * width), BF),
         ],
         [deep, one, two, w1, moved],
         flops=1_500_000_000,
     )
     size = mid // parts
     direct = parts == 2 and size % 16 == 0
-    half = (parts, quarters // 2, 9, size, LANES)
+    units = -(-35 * size // (16 * deps * quarters))
+    block = (units, 16, width)
+    packed = (parts if direct else 1, quarters // 2, deps, *block)
     grads = call(
         functools.partial(delta_kernel, direct),
-        [shape(half, F32), shape(half, BF)] if direct else [shape((7, mid, LANES), F32)],
-        [wide, cot_deep, cot_one, cot_two, k2, slope, g2],
+        [shape(packed, F32), shape(packed, BF)] if direct else [shape((7, mid, LANES), F32)],
+        [wide, back, back_one, back_two, slope, g2],
         [pltpu.VMEM((3 * mid, depth * cells), BF)],
-        flops=1_100_000_000,
+        flops=300_000_000,
     )
     if direct:
         keep, send = grads
+        moves = [(1, 0), (0, 1), (1, 1)]
     else:
         grad = jnp.swapaxes(grads[0].reshape(7, parts, size, LANES), 0, 1)
         grad2 = jnp.swapaxes(g2.reshape(14, parts, 2, size, LANES), 0, 1).reshape(parts, 28, size, LANES)
-        grad = jnp.pad(jnp.concatenate([grad2, grad], axis=1), ((0, 0), (0, quarters * 9 - 35), (0, 0), (0, 0)))
+        grad = jnp.concatenate([grad2, grad], axis=1).reshape(parts, 35 * size, LANES)
+        grad = jnp.pad(grad, ((0, 0), (0, quarters * deps * units * 16 - 35 * size), (0, 0)))
         grad = lax.psum_scatter(grad, "dp", scatter_dimension=0, tiled=True)
-        grad = grad.reshape(quarters // 2, 2, 9, size, LANES)
+        grad = grad.reshape(1, quarters // 2, 2, deps, *block)
         core = lax.rem(lax.axis_index("hgt"), 2)
-        keep = lax.dynamic_index_in_dim(grad, core, 1, False)
-        send = lax.dynamic_index_in_dim(grad, 1 - core, 1, False).astype(BF)
+        keep = lax.dynamic_index_in_dim(grad, core, 2, False)
+        send = lax.dynamic_index_in_dim(grad, 1 - core, 2, False).astype(BF)
+        moves = [(0, 1)]
     (features,) = call(
         features_kernel, [shape(cotangent.shape[1:], BF)], [hidden, w2], [pltpu.VMEM((out * rows, width), F32)],
         flops=900_000_000,
     )
     got = across(send, "hgt", 1)
-    if direct:
-        keep, send = call(
-            functools.partial(halve_kernel, "dp", 1), [shape(half[1:], F32), shape(half[1:], BF)], [keep, got]
-        )
-        got = across(send, "dp", 1)
-    keep, send = call(
-        functools.partial(halve_kernel, "hgt", 2), [shape(half[2:], F32), shape(half[2:], BF)], [keep, got]
-    )
-    got = across(send, "hgt", 2)
-    (share,) = call(add_kernel, [shape(half[2:], BF)], [keep, got])
-    (share,) = call(add_kernel, [shape(half[2:], BF)], [share, across(share, "dep", 1)])
-    (share,) = call(add_kernel, [shape(half[2:], BF)], [share, across(share, "dep", 3)])
-    (pair,) = call(
-        functools.partial(order_kernel, "hgt", 2), [shape(half[1:], BF)], [share, across(share, "hgt", 2)]
+    kept, *sends = call(
+        functools.partial(plane_kernel, moves),
+        [shape((deps, *block), F32)] + [shape((deps, *block), BF)] * len(moves),
+        [keep, got],
+    )
+    gots = [across_plane(send, move) for send, move in zip(sends, moves, strict=True)]
+    kept, *sends = call(
+        functools.partial(depth_kernel, len(gots)),
+        [shape(block, F32)] + [shape(block, BF)] * (deps - 1),
+        [kept, *gots, features],
+        far=(1 + len(gots),),
+    )
+    (share,) = call(
+        finish_kernel, [shape(block, BF)], [kept, *(across(send, "dep", n + 1) for n, send in enumerate(sends))]
+    )
+    (share,) = call(
+        functools.partial(order_kernel, "dep", 1),
+        [shape((deps, *block), BF)],
+        [share, *(across(share, "dep", n) for n in range(1, deps))],
+    )
+    (share,) = call(
+        functools.partial(order_kernel, "hgt", 2),
+        [shape((quarters // 2, deps, *block), BF)],
+        [share, across(share, "hgt", 2)],
     )
     grad_first, grad_second = call(
         unpack_kernel,
         [shape((27, size, inner), F32), shape((27, 2 * size, mid), F32)],
-        [pair, across(pair, "hgt", 1)],
+        [share, across(share, "hgt", 1)],
     )
     return features[None], grad_first, grad_second
 

time: 66.1 us -> 61.7 us (0.933)
  waiting for transfers between devices: 29.6 us -> 17.4 us
  starting transfers between devices: 21.2 us -> 27.3 us
  local copies, waits for them, and re-layouts: 3.89 us -> 4.93 us
    ppermute x7 -> x11, starting transfers between devices: 9.55 us -> 17.5 us  [across(): lax.ppermute(x, axis, [(i, i ^ bit) for i in range(lax.axis_size(axis))])]
    ppermute x7 -> x11, waiting for transfers between devices: 19.5 us -> 12.8 us  [across(): lax.ppermute(x, axis, [(i, i ^ bit) for i in range(lax.axis_size(axis))])]
    ppermute x8, waiting for transfers between devices: 10.2 us -> 3.61 us  [swapped(): return lax.ppermute(x, axis, pairs + [(j, i) for i, j in pairs])]
    ppermute x8, starting transfers between devices: 11.6 us -> 8.79 us  [swapped(): return lax.ppermute(x, axis, pairs + [(j, i) for i, j in pairs])]
    unnamed x10, local copies, waits for them, and re-layouts: 3.89 us -> 4.93 us
    ppermute x0 -> x1, waiting for transfers between devices: none -> 1.02 us  [across_plane(): return lax.ppermute(x, ('dp', 'hgt'), [(i, i ^ flip) for i in range(size)])]
    ppermute x0 -> x1, starting transfers between devices: none -> 1 us  [across_plane(): return lax.ppermute(x, ('dp', 'hgt'), [(i, i ^ flip) for i in range(size)])]
    pallas_call x14 -> x12, Pallas kernels: 10.4 us -> 10.9 us  [call(): pl.pallas_call(body, out_shape=outs, in_specs=[pl.BlockSpec(memory_space=...]
  transfers between devices with their start and end apart: 15 -> 20, of which waited for: 9 -> 10; matrix products, arithmetic and copies ran while one was open for 0% -> 0% of each run, Pallas kernels for 8% -> 14%
where the time goes in v3:
time: 61.7 us; the launch traced here: 61.3 us
  starting transfers between devices  27.3 us (44%)
  waiting for transfers between devices  17.4 us (28%)
  Pallas kernels  10.9 us (18%)
  local copies, waits for them, and re-layouts  4.93 us (8%)
  between operations  0.81 us (1%)
    ppermute x11, starting transfers between devices, across(): lax.ppermute(x, axis, [(i, i ^ bit) for i in range(lax.axis_size(axis))])  17.5 us
    ppermute x11, waiting for transfers between devices, across(): lax.ppermute(x, axis, [(i, i ^ bit) for i in range(lax.axis_size(axis))])  12.8 us
    pallas_call x12, Pallas kernels, call(): pl.pallas_call(body, out_shape=outs, in_specs=[pl.BlockSpec(memory_space=...  10.9 us
    ppermute x8, starting transfers between devices, swapped(): return lax.ppermute(x, axis, pairs + [(j, i) for i, j in pairs])  8.79 us
    unnamed x10, local copies, waits for them, and re-layouts  4.93 us
    ppermute x8, waiting for transfers between devices, swapped(): return lax.ppermute(x, axis, pairs + [(j, i) for i, j in pairs])  3.61 us
  transfers between devices with their start and end apart: 20, of which 10 were waited for; matrix products, arithmetic and copies ran while one was open for 0% of the time, Pallas kernels for 14%

profile of v3, /device:TPU:0, one launch (start us, length us, event | category | flops | bytes accessed | tf_op | source)
XLA Modules:
  0.0 61.3 jit_solution(17055153022564508716)
XLA Ops:
  1.3 5.9 %collective-permute-start = (bf16[32,2,8,128]{3,2,1,0:T(8,128)(2,1)}, bf16[32,2,8,128]{3,2,1,0:T(8,128)(2,1)S(1)}, u32[]{:S(2)}, u32[]{:S(2)}) collective-permute-start(bf16[32,2,8,128]{3,2,1,0:T(8,128)(2,1)} %bitcast.10), channel_id=1, source_target_pairs={{0,4},{8,12},{4,0},{12,8},{1,5},{9,13},{5,1},{13,9},{2,6},{10,14},... | collective-permute-start | bytes 393224 | tf_op jit(solution)/shard_map/ppermute | solution.py:414
  7.2 1.0 %copy-done.1 = bf16[1,128,2,8,128]{4,3,2,1,0:T(8,128)(2,1)S(1)} copy-done((bf16[1,128,2,8,128]{4,3,2,1,0:T(8,128)(2,1)S(1)}, bf16[1,128,2,8,128]{4,3,2,1,0:T(8,128)(2,1)}, u32[]{:S(2)}) %copy-start.1) | copy-done | bytes 524312
  8.3 1.0 %copy-done.2 = bf16[27,128,64]{1,2,0:T(8,128)(2,1)S(1)} copy-done((bf16[27,128,64]{1,2,0:T(8,128)(2,1)S(1)}, bf16[27,128,64]{1,2,0:T(8,128)(2,1)}, u32[]{:S(2)}) %copy-start.2) | copy-done | bytes 442392
  11.1 3.4 %shard_map.67 = (bf16[2,32,1024]{2,1,0:T(8,128)(2,1)S(1)}, bf16[2,384,1024]{2,1,0:T(8,128)(2,1)S(1)}, bf16[192,288]{1,0:T(8,128)(2,1)S(1)}, bf16[384,576]{1,0:T(...) custom-call(bf16[32,2,8,128]{3,2,1,0:T(8,128)(2,1)S(1)} %bitcast.11, ...), custom_call_target="tpu_custom_call" | custom-call | flops 1100000000 | bytes 4448256 | tf_op jit(solution)/shard_map/pallas_call | solution.py:17
  16.3 3.6 %collective-permute-done.4.one_ref = bf16[64,1280]{1,0:T(8,128)(2,1)S(1)} collective-permute-done((bf16[64,1280]{1,0:T(8,128)(2,1)S(1)}, bf16[64,1280]{1,0:T(8,128)(2,1)S(1)}, u32[]{:S(2)}, u32[]{:S(2)}) %collective-permute-start.4) | collective-permute-done | bytes 163872 | tf_op jit(solution)/shard_map/ppermute | solution.py:414
  20.8 2.5 %shard_map.69 = (bf16[4,64,1280]{2,1,0:T(8,128)(2,1)S(1)}, f32[2,64,1024]{2,1,0:T(8,128)S(1)}, f32[14,128,128]{2,1,0:T(8,128)S(1)}, bf16[6,32,1536]{2,1,0:T(8,128)(2,1)S(1)}) custom-call(bf16[6,32,1024]{2,1,0:T(8,128)(2,1)S(1)} %get-tuple-element.33.deep_ref, bf16[6,32,256]{2,1,0:T(8,128)(2,1)S(1)} %collective-permute-done.2.one_ref, ...), custom_call_target="tpu_custom_call" | custom-call | flops 1500000000 | bytes 4960256 | tf_op jit(solution)/shard_map/pallas_call | solution.py:17
  24.1 2.9 %collective-permute-start.8 = (bf16[2,2,4,5,16,128]{5,4,3,2,1,0:T(8,128)(2,1)S(1)}, bf16[2,2,4,5,16,128]{5,4,3,2,1,0:T(8,128)(2,1)S(1)}, u32[]{:S(2)}, u32[]{:S(2)}) collective-permute-start(bf16[2,2,4,5,16,128]{5,4,3,2,1,0:T(8,128)(2,1)S(1)} %get-tuple-element.50), channel_id=1, source_target_pairs={{0,1},{1,0},{2,3},{3,2},{4,5},{5,4},{6,7},{7,6},{8,9},{9,8},{10,11... | collective-permute-start | bytes 983048 | tf_op jit(solution)/shard_map/ppermute | solution.py:418
  27.1 1.3 %collective-permute-done.8.got_ref = bf16[2,2,4,5,16,128]{5,4,3,2,1,0:T(8,128)(2,1)S(1)} collective-permute-done((bf16[2,2,4,5,16,128]{5,4,3,2,1,0:T(8,128)(2,1)S(1)}, bf16[2,2,4,5,16,128]{5,4,3,2,1,0:T(8,128)(2,1)S(1)}, u32[]{:S(2)}, u32[]{:S(2)}) %collective-permute-start.8) | collective-permute-done | bytes 327712 | tf_op jit(solution)/shard_map/ppermute | solution.py:418
  28.4 1.6 %collective-permute-start.9 = (bf16[4,5,16,128]{3,2,1,0:T(8,128)(2,1)S(1)}, bf16[4,5,16,128]{3,2,1,0:T(8,128)(2,1)S(1)}, u32[]{:S(2)}, u32[]{:S(2)}) collective-permute-start(bf16[4,5,16,128]{3,2,1,0:T(8,128)(2,1)S(1)} %get-tuple-element.52), channel_id=1, source_target_pairs={{0,16},{16,0},{1,17},{17,1},{2,18},{18,2},{3,19},{19,3},{4,20},{20... | collective-permute-start | bytes 245768 | tf_op jit(solution)/shard_map/ppermute | solution.py:418
  31.0 1.0 %collective-permute-start.11 = (bf16[4,5,16,128]{3,2,1,0:T(8,128)(2,1)S(1)}, bf16[4,5,16,128]{3,2,1,0:T(8,128)(2,1)S(1)}, u32[]{:S(2)}, u32[]{:S(2)}) collective-permute-start(bf16[4,5,16,128]{3,2,1,0:T(8,128)(2,1)S(1)} %get-tuple-element.54), channel_id=1, source_target_pairs={{0,18},{1,19},{2,16},{3,17},{16,2},{17,3},{18,0},{19,1},{4,22},{5,... | collective-permute-start | bytes 245768 | tf_op jit(solution)/shard_map/ppermute | solution.py:429
  32.0 2.5 %shard_map.70.refs_4_ = bf16[128,2,8,128]{3,2,1,0:T(8,128)(2,1)} custom-call(bf16[4,64,1280]{2,1,0:T(8,128)(2,1)S(1)} %get-tuple-element.38.hidden_ref, bf16[384,576]{1,0:T(8,128)(2,1)S(1)} %get-tuple-element.39.w2_ref), custom_call_target="tpu_custom_call" | custom-call | flops 900000000 | bytes 1622016 | tf_op jit(solution)/shard_map/pallas_call | solution.py:17
  35.3 1.0 %collective-permute-done.11.refs_3_ = bf16[4,5,16,128]{3,2,1,0:T(8,128)(2,1)S(1)} collective-permute-done((bf16[4,5,16,128]{3,2,1,0:T(8,128)(2,1)S(1)}, bf16[4,5,16,128]{3,2,1,0:T(8,128)(2,1)S(1)}, u32[]{:S(2)}, u32[]{:S(2)}) %collective-permute-start.11) | collective-permute-done | bytes 81952 | tf_op jit(solution)/shard_map/ppermute | solution.py:429
  36.3 1.0 %copy-done = bf16[128,2,8,128]{3,2,1,0:T(8,128)(2,1)S(1)} copy-done((bf16[128,2,8,128]{3,2,1,0:T(8,128)(2,1)S(1)}, bf16[128,2,8,128]{3,2,1,0:T(8,128)(2,1)}, u32[]{:S(2)}) %copy-start) | copy-done | bytes 524312
  37.4 3.9 %collective-permute-start.12 = (bf16[5,16,128]{2,1,0:T(8,128)(2,1)S(1)}, bf16[5,16,128]{2,1,0:T(8,128)(2,1)S(1)}, u32[]{:S(2)}, u32[]{:S(2)}) collective-permute-start(bf16[5,16,128]{2,1,0:T(8,128)(2,1)S(1)} %get-tuple-element.56), channel_id=1, source_target_pairs={{0,4},{4,0},{8,12},{12,8},{1,5},{5,1},{9,13},{13,9},{2,6},{6,2},{1... | collective-permute-start | bytes 61448 | tf_op jit(solution)/shard_map/ppermute | solution.py:418
  41.3 2.4 %collective-permute-start.14 = (bf16[5,16,128]{2,1,0:T(8,128)(2,1)S(1)}, bf16[5,16,128]{2,1,0:T(8,128)(2,1)S(1)}, u32[]{:S(2)}, u32[]{:S(2)}) collective-permute-start(bf16[5,16,128]{2,1,0:T(8,128)(2,1)S(1)} %get-tuple-element.58), channel_id=1, source_target_pairs={{0,12},{4,8},{8,4},{12,0},{1,13},{5,9},{9,5},{13,1},{2,14},{6,10},... | collective-permute-start | bytes 61448 | tf_op jit(solution)/shard_map/ppermute | solution.py:418
  43.7 2.2 %collective-permute-done.13.refs_1_ = bf16[5,16,128]{2,1,0:T(8,128)(2,1)S(1)} collective-permute-done((bf16[5,16,128]{2,1,0:T(8,128)(2,1)S(1)}, bf16[5,16,128]{2,1,0:T(8,128)(2,1)S(1)}, u32[]{:S(2)}, u32[]{:S(2)}) %collective-permute-start.13) | collective-permute-done | bytes 20512 | tf_op jit(solution)/shard_map/ppermute | solution.py:418
  46.9 2.5 %collective-permute-start.17 = (bf16[5,16,128]{2,1,0:T(8,128)(2,1)S(1)}, bf16[5,16,128]{2,1,0:T(8,128)(2,1)S(1)}, u32[]{:S(2)}, u32[]{:S(2)}) collective-permute-start(bf16[5,16,128]{2,1,0:T(8,128)(2,1)S(1)} %shard_map.75.own_ref), channel_id=1, source_target_pairs={{0,12},{4,8},{8,4},{12,0},{1,13},{5,9},{9,5},{13,1},{2,14},{6,10},... | collective-permute-start | bytes 61448 | tf_op jit(solution)/shard_map/ppermute | solution.py:418
  49.4 1.9 %collective-permute-start.15 = (bf16[5,16,128]{2,1,0:T(8,128)(2,1)S(1)}, bf16[5,16,128]{2,1,0:T(8,128)(2,1)S(1)}, u32[]{:S(2)}, u32[]{:S(2)}) collective-permute-start(bf16[5,16,128]{2,1,0:T(8,128)(2,1)S(1)} %shard_map.75.own_ref), channel_id=1, source_target_pairs={{0,4},{4,0},{8,12},{12,8},{1,5},{5,1},{9,13},{13,9},{2,6},{6,2},{1... | collective-permute-start | bytes 61448 | tf_op jit(solution)/shard_map/ppermute | solution.py:418
  51.4 1.2 %collective-permute-done.17.refs_2_ = bf16[5,16,128]{2,1,0:T(8,128)(2,1)S(1)} collective-permute-done((bf16[5,16,128]{2,1,0:T(8,128)(2,1)S(1)}, bf16[5,16,128]{2,1,0:T(8,128)(2,1)S(1)}, u32[]{:S(2)}, u32[]{:S(2)}) %collective-permute-start.17) | collective-permute-done | bytes 20512 | tf_op jit(solution)/shard_map/ppermute | solution.py:418
  52.6 1.5 %collective-permute-done.16.refs_1_ = bf16[5,16,128]{2,1,0:T(8,128)(2,1)S(1)} collective-permute-done((bf16[5,16,128]{2,1,0:T(8,128)(2,1)S(1)}, bf16[5,16,128]{2,1,0:T(8,128)(2,1)S(1)}, u32[]{:S(2)}, u32[]{:S(2)}) %collective-permute-start.16) | collective-permute-done | bytes 20512 | tf_op jit(solution)/shard_map/ppermute | solution.py:418
  54.1 1.1 %collective-permute-start.18 = (bf16[4,5,16,128]{3,2,1,0:T(8,128)(2,1)S(1)}, bf16[4,5,16,128]{3,2,1,0:T(8,128)(2,1)S(1)}, u32[]{:S(2)}, u32[]{:S(2)}) collective-permute-start(bf16[4,5,16,128]{3,2,1,0:T(8,128)(2,1)S(1)} %shard_map.76.own_ref), channel_id=1, source_target_pairs={{0,2},{1,3},{2,0},{3,1},{4,6},{5,7},{6,4},{7,5},{8,10},{9,11},{10,... | collective-permute-start | bytes 245768 | tf_op jit(solution)/shard_map/ppermute | solution.py:418
  55.2 3.4 %collective-permute-done.18.refs_0_ = bf16[4,5,16,128]{3,2,1,0:T(8,128)(2,1)S(1)} collective-permute-done((bf16[4,5,16,128]{3,2,1,0:T(8,128)(2,1)S(1)}, bf16[4,5,16,128]{3,2,1,0:T(8,128)(2,1)S(1)}, u32[]{:S(2)}, u32[]{:S(2)}) %collective-permute-start.18) | collective-permute-done | bytes 81952 | tf_op jit(solution)/shard_map/ppermute | solution.py:418
  58.7 1.4 %collective-permute-done.19.got_ref = bf16[2,4,5,16,128]{4,3,2,1,0:T(8,128)(2,1)S(1)} collective-permute-done((bf16[2,4,5,16,128]{4,3,2,1,0:T(8,128)(2,1)S(1)}, bf16[2,4,5,16,128]{4,3,2,1,0:T(8,128)(2,1)S(1)}, u32[]{:S(2)}, u32[]{:S(2)}) %collective-permute-start.19) | collective-permute-done | bytes 163872 | tf_op jit(solution)/shard_map/ppermute | solution.py:418
  60.1 1.2 %shard_map.78 = (f32[27,32,32]{2,1,0:T(8,128)}, f32[27,64,64]{2,1,0:T(8,128)}) custom-call(bf16[2,4,5,16,128]{4,3,2,1,0:T(8,128)(2,1)S(1)} %shard_map.77.own_ref, bf16[2,4,5,16,128]{4,3,2,1,0:T(8,128)(2,1)S(1)} %collective-permute-done.19.got_ref), custom_call_target="tpu_custom_call" | custom-call | bytes 880640 | tf_op jit(solution)/shard_map/pallas_call | solution.py:17
  (38 shorter events, 8.9 us)
Async XLA Ops:
  0.6 14.6 %collective-permute-start.1 = (bf16[32,2,8,128]{3,2,1,0:T(8,128)(2,1)}, bf16[32,2,8,128]{3,2,1,0:T(8,128)(2,1)S(1)}, u32[]{:S(2)}, u32[]{:S(2)}) collective-permute-start(bf16[32,2,8,128]{3,2,1,0:T(8,128)(2,1)} %bitcast.9), channel_id=1, source_target_pairs={{4,8},{8,4},{5,9},{9,5},{6,10},{10,6},{7,11},{11,7},{20,24},{24,20... | collective-permute-start | bytes 393224 | tf_op jit(solution)/shard_map/ppermute | solution.py:414
  1.3 14.0 %collective-permute-start = (bf16[32,2,8,128]{3,2,1,0:T(8,128)(2,1)}, bf16[32,2,8,128]{3,2,1,0:T(8,128)(2,1)S(1)}, u32[]{:S(2)}, u32[]{:S(2)}) collective-permute-start(bf16[32,2,8,128]{3,2,1,0:T(8,128)(2,1)} %bitcast.10), channel_id=1, source_target_pairs={{0,4},{8,12},{4,0},{12,8},{1,5},{9,13},{5,1},{13,9},{2,6},{10,14},... | collective-permute-start | bytes 393224 | tf_op jit(solution)/shard_map/ppermute | solution.py:414
  7.2 1.0 %copy-start.1 = (bf16[1,128,2,8,128]{4,3,2,1,0:T(8,128)(2,1)S(1)}, bf16[1,128,2,8,128]{4,3,2,1,0:T(8,128)(2,1)}, u32[]{:S(2)}) copy-start(bf16[1,128,2,8,128]{4,3,2,1,0:T(8,128)(2,1)} %param.7) | copy-start | bytes 1572868
  8.3 1.0 %copy-start.2 = (bf16[27,128,64]{1,2,0:T(8,128)(2,1)S(1)}, bf16[27,128,64]{1,2,0:T(8,128)(2,1)}, u32[]{:S(2)}) copy-start(bf16[27,128,64]{1,2,0:T(8,128)(2,1)} %param.6) | copy-start | bytes 1327108
  9.3 0.9 %copy-start.3 = (bf16[27,64,32]{1,2,0:T(8,128)(2,1)S(1)}, bf16[27,64,32]{1,2,0:T(8,128)(2,1)}, u32[]{:S(2)}) copy-start(bf16[27,64,32]{1,2,0:T(8,128)(2,1)} %param.5) | copy-start | bytes 331780
  14.5 5.4 %collective-permute-start.4 = (bf16[64,1280]{1,0:T(8,128)(2,1)S(1)}, bf16[64,1280]{1,0:T(8,128)(2,1)S(1)}, u32[]{:S(2)}, u32[]{:S(2)}) collective-permute-start(bf16[64,1280]{1,0:T(8,128)(2,1)S(1)} %get-tuple-element.42), channel_id=1, source_target_pairs={{0,4},{8,12},{4,0},{12,8},{1,5},{9,13},{5,1},{13,9},{2,6},{10,14},... | collective-permute-start | bytes 491528 | tf_op jit(solution)/shard_map/ppermute | solution.py:414
  14.6 5.4 %collective-permute-start.5 = (bf16[64,1280]{1,0:T(8,128)(2,1)S(1)}, bf16[64,1280]{1,0:T(8,128)(2,1)S(1)}, u32[]{:S(2)}, u32[]{:S(2)}) collective-permute-start(bf16[64,1280]{1,0:T(8,128)(2,1)S(1)} %get-tuple-element.43), channel_id=1, source_target_pairs={{4,8},{8,4},{5,9},{9,5},{6,10},{10,6},{7,11},{11,7},{20,24},{24,20... | collective-permute-start | bytes 491528 | tf_op jit(solution)/shard_map/ppermute | solution.py:414
  15.6 5.2 %collective-permute-start.2 = (bf16[6,32,256]{2,1,0:T(8,128)(2,1)S(1)}, bf16[6,32,256]{2,1,0:T(8,128)(2,1)S(1)}, u32[]{:S(2)}, u32[]{:S(2)}) collective-permute-start(bf16[6,32,256]{2,1,0:T(8,128)(2,1)S(1)} %get-tuple-element.34), channel_id=1, source_target_pairs={{0,1},{2,3},{1,0},{3,2},{4,5},{6,7},{5,4},{7,6},{8,9},{10,11},{9,8... | collective-permute-start | bytes 294920 | tf_op jit(solution)/shard_map/ppermute | solution.py:414
  15.7 5.1 %collective-permute-start.3 = (bf16[6,32,256]{2,1,0:T(8,128)(2,1)S(1)}, bf16[6,32,256]{2,1,0:T(8,128)(2,1)S(1)}, u32[]{:S(2)}, u32[]{:S(2)}) collective-permute-start(bf16[6,32,256]{2,1,0:T(8,128)(2,1)S(1)} %get-tuple-element.35), channel_id=1, source_target_pairs={{1,2},{2,1},{5,6},{6,5},{9,10},{10,9},{13,14},{14,13},{17,18},{18,... | collective-permute-start | bytes 294920 | tf_op jit(solution)/shard_map/ppermute | solution.py:414
  20.0 3.3 %collective-permute-start.6 = (bf16[2,64,128]{2,1,0:T(8,128)(2,1)S(1)}, bf16[2,64,128]{2,1,0:T(8,128)(2,1)S(1)}, u32[]{:S(2)}, u32[]{:S(2)}) collective-permute-start(bf16[2,64,128]{2,1,0:T(8,128)(2,1)S(1)} %get-tuple-element.45), channel_id=1, source_target_pairs={{0,1},{2,3},{1,0},{3,2},{4,5},{6,7},{5,4},{7,6},{8,9},{10,11},{9,8... | collective-permute-start | bytes 98312 | tf_op jit(solution)/shard_map/ppermute | solution.py:414
  20.1 3.2 %collective-permute-start.7 = (bf16[2,64,128]{2,1,0:T(8,128)(2,1)S(1)}, bf16[2,64,128]{2,1,0:T(8,128)(2,1)S(1)}, u32[]{:S(2)}, u32[]{:S(2)}) collective-permute-start(bf16[2,64,128]{2,1,0:T(8,128)(2,1)S(1)} %get-tuple-element.46), channel_id=1, source_target_pairs={{1,2},{2,1},{5,6},{6,5},{9,10},{10,9},{13,14},{14,13},{17,18},{18,... | collective-permute-start | bytes 98312 | tf_op jit(solution)/shard_map/ppermute | solution.py:414
  24.1 4.2 %collective-permute-start.8 = (bf16[2,2,4,5,16,128]{5,4,3,2,1,0:T(8,128)(2,1)S(1)}, bf16[2,2,4,5,16,128]{5,4,3,2,1,0:T(8,128)(2,1)S(1)}, u32[]{:S(2)}, u32[]{:S(2)}) collective-permute-start(bf16[2,2,4,5,16,128]{5,4,3,2,1,0:T(8,128)(2,1)S(1)} %get-tuple-element.50), channel_id=1, source_target_pairs={{0,1},{1,0},{2,3},{3,2},{4,5},{5,4},{6,7},{7,6},{8,9},{9,8},{10,11... | collective-permute-start | bytes 983048 | tf_op jit(solution)/shard_map/ppermute | solution.py:418
  28.4 6.0 %collective-permute-start.9 = (bf16[4,5,16,128]{3,2,1,0:T(8,128)(2,1)S(1)}, bf16[4,5,16,128]{3,2,1,0:T(8,128)(2,1)S(1)}, u32[]{:S(2)}, u32[]{:S(2)}) collective-permute-start(bf16[4,5,16,128]{3,2,1,0:T(8,128)(2,1)S(1)} %get-tuple-element.52), channel_id=1, source_target_pairs={{0,16},{16,0},{1,17},{17,1},{2,18},{18,2},{3,19},{19,3},{4,20},{20... | collective-permute-start | bytes 245768 | tf_op jit(solution)/shard_map/ppermute | solution.py:418
  30.0 5.3 %collective-permute-start.10 = (bf16[4,5,16,128]{3,2,1,0:T(8,128)(2,1)S(1)}, bf16[4,5,16,128]{3,2,1,0:T(8,128)(2,1)S(1)}, u32[]{:S(2)}, u32[]{:S(2)}) collective-permute-start(bf16[4,5,16,128]{3,2,1,0:T(8,128)(2,1)S(1)} %get-tuple-element.53), channel_id=1, source_target_pairs={{0,2},{1,3},{2,0},{3,1},{4,6},{5,7},{6,4},{7,5},{8,10},{9,11},{10,... | collective-permute-start | bytes 245768 | tf_op jit(solution)/shard_map/ppermute | solution.py:418
  31.0 5.3 %collective-permute-start.11 = (bf16[4,5,16,128]{3,2,1,0:T(8,128)(2,1)S(1)}, bf16[4,5,16,128]{3,2,1,0:T(8,128)(2,1)S(1)}, u32[]{:S(2)}, u32[]{:S(2)}) collective-permute-start(bf16[4,5,16,128]{3,2,1,0:T(8,128)(2,1)S(1)} %get-tuple-element.54), channel_id=1, source_target_pairs={{0,18},{1,19},{2,16},{3,17},{16,2},{17,3},{18,0},{19,1},{4,22},{5,... | collective-permute-start | bytes 245768 | tf_op jit(solution)/shard_map/ppermute | solution.py:429
  36.3 1.0 %copy-start = (bf16[128,2,8,128]{3,2,1,0:T(8,128)(2,1)S(1)}, bf16[128,2,8,128]{3,2,1,0:T(8,128)(2,1)}, u32[]{:S(2)}) copy-start(bf16[128,2,8,128]{3,2,1,0:T(8,128)(2,1)} %shard_map.70.refs_4_) | copy-start | bytes 1572868
  37.4 6.4 %collective-permute-start.12 = (bf16[5,16,128]{2,1,0:T(8,128)(2,1)S(1)}, bf16[5,16,128]{2,1,0:T(8,128)(2,1)S(1)}, u32[]{:S(2)}, u32[]{:S(2)}) collective-permute-start(bf16[5,16,128]{2,1,0:T(8,128)(2,1)S(1)} %get-tuple-element.56), channel_id=1, source_target_pairs={{0,4},{4,0},{8,12},{12,8},{1,5},{5,1},{9,13},{13,9},{2,6},{6,2},{1... | collective-permute-start | bytes 61448 | tf_op jit(solution)/shard_map/ppermute | solution.py:418
  41.3 4.7 %collective-permute-start.13 = (bf16[5,16,128]{2,1,0:T(8,128)(2,1)S(1)}, bf16[5,16,128]{2,1,0:T(8,128)(2,1)S(1)}, u32[]{:S(2)}, u32[]{:S(2)}) collective-permute-start(bf16[5,16,128]{2,1,0:T(8,128)(2,1)S(1)} %get-tuple-element.57), channel_id=1, source_target_pairs={{0,8},{4,12},{8,0},{12,4},{1,9},{5,13},{9,1},{13,5},{2,10},{6,14},... | collective-permute-start | bytes 61448 | tf_op jit(solution)/shard_map/ppermute | solution.py:418
  41.3 5.6 %collective-permute-start.14 = (bf16[5,16,128]{2,1,0:T(8,128)(2,1)S(1)}, bf16[5,16,128]{2,1,0:T(8,128)(2,1)S(1)}, u32[]{:S(2)}, u32[]{:S(2)}) collective-permute-start(bf16[5,16,128]{2,1,0:T(8,128)(2,1)S(1)} %get-tuple-element.58), channel_id=1, source_target_pairs={{0,12},{4,8},{8,4},{12,0},{1,13},{5,9},{9,5},{13,1},{2,14},{6,10},... | collective-permute-start | bytes 61448 | tf_op jit(solution)/shard_map/ppermute | solution.py:418
  46.9 5.6 %collective-permute-start.17 = (bf16[5,16,128]{2,1,0:T(8,128)(2,1)S(1)}, bf16[5,16,128]{2,1,0:T(8,128)(2,1)S(1)}, u32[]{:S(2)}, u32[]{:S(2)}) collective-permute-start(bf16[5,16,128]{2,1,0:T(8,128)(2,1)S(1)} %shard_map.75.own_ref), channel_id=1, source_target_pairs={{0,12},{4,8},{8,4},{12,0},{1,13},{5,9},{9,5},{13,1},{2,14},{6,10},... | collective-permute-start | bytes 61448 | tf_op jit(solution)/shard_map/ppermute | solution.py:418
  49.4 4.7 %collective-permute-start.16 = (bf16[5,16,128]{2,1,0:T(8,128)(2,1)S(1)}, bf16[5,16,128]{2,1,0:T(8,128)(2,1)S(1)}, u32[]{:S(2)}, u32[]{:S(2)}) collective-permute-start(bf16[5,16,128]{2,1,0:T(8,128)(2,1)S(1)} %shard_map.75.own_ref), channel_id=1, source_target_pairs={{0,8},{4,12},{8,0},{12,4},{1,9},{5,13},{9,1},{13,5},{2,10},{6,14},... | collective-permute-start | bytes 61448 | tf_op jit(solution)/shard_map/ppermute | solution.py:418
  49.4 4.7 %collective-permute-start.15 = (bf16[5,16,128]{2,1,0:T(8,128)(2,1)S(1)}, bf16[5,16,128]{2,1,0:T(8,128)(2,1)S(1)}, u32[]{:S(2)}, u32[]{:S(2)}) collective-permute-start(bf16[5,16,128]{2,1,0:T(8,128)(2,1)S(1)} %shard_map.75.own_ref), channel_id=1, source_target_pairs={{0,4},{4,0},{8,12},{12,8},{1,5},{5,1},{9,13},{13,9},{2,6},{6,2},{1... | collective-permute-start | bytes 61448 | tf_op jit(solution)/shard_map/ppermute | solution.py:418
  54.1 4.5 %collective-permute-start.18 = (bf16[4,5,16,128]{3,2,1,0:T(8,128)(2,1)S(1)}, bf16[4,5,16,128]{3,2,1,0:T(8,128)(2,1)S(1)}, u32[]{:S(2)}, u32[]{:S(2)}) collective-permute-start(bf16[4,5,16,128]{3,2,1,0:T(8,128)(2,1)S(1)} %shard_map.76.own_ref), channel_id=1, source_target_pairs={{0,2},{1,3},{2,0},{3,1},{4,6},{5,7},{6,4},{7,5},{8,10},{9,11},{10,... | collective-permute-start | bytes 245768 | tf_op jit(solution)/shard_map/ppermute | solution.py:418
  58.6 1.5 %collective-permute-start.19 = (bf16[2,4,5,16,128]{4,3,2,1,0:T(8,128)(2,1)S(1)}, bf16[2,4,5,16,128]{4,3,2,1,0:T(8,128)(2,1)S(1)}, u32[]{:S(2)}, u32[]{:S(2)}) collective-permute-start(bf16[2,4,5,16,128]{4,3,2,1,0:T(8,128)(2,1)S(1)} %shard_map.77.own_ref), channel_id=1, source_target_pairs={{0,1},{1,0},{2,3},{3,2},{4,5},{5,4},{6,7},{7,6},{8,9},{9,8},{10,11... | collective-permute-start | bytes 491528 | tf_op jit(solution)/shard_map/ppermute | solution.py:418
  (1 other events, 0.9 us)

commit v4 on v3

v4 whole, which is shorter than its diff:
```python
import functools

import jax
import jax.numpy as jnp
from jax import lax
from jax.experimental import pallas as pl
from jax.experimental.pallas import tpu as pltpu
from jax.sharding import PartitionSpec as P

BF, F32 = jnp.bfloat16, jnp.float32
LANES = 128
HGT = ("y", "core")
VMEM_BYTES = 48 * 2**20


def call(body, outs, args, scratch=(), flops=0, far=()):
    moved = sum(x.size * x.dtype.itemsize for x in (*outs, *args))
    return pl.pallas_call(
        body,
        out_shape=outs,
        in_specs=[pl.BlockSpec(memory_space=pl.ANY if n in far else pltpu.VMEM) for n in range(len(args))],
        out_specs=[pl.BlockSpec(memory_space=pltpu.VMEM)] * len(outs),
        scratch_shapes=list(scratch),
        compiler_params=pltpu.CompilerParams(vmem_limit_bytes=VMEM_BYTES),
        cost_estimate=pl.CostEstimate(flops=flops, bytes_accessed=moved, transcendentals=0),
    )(*args)


def shape(dims, dtype):
    return jax.ShapeDtypeStruct(dims, dtype)


def moved_along_width(x, c):
    if c == 0:
        return x
    pieces = []
    for start in range(0, x.shape[1], LANES):
        piece = x[:, start : start + LANES]
        lane = lax.broadcasted_iota(jnp.int32, piece.shape, 1)
        rolled = pltpu.roll(piece, c % LANES, 1)
        pieces.append(jnp.where(lane == (0 if c == 1 else LANES - 1), 0.0, rolled))
    return pieces[0] if len(pieces) == 1 else jnp.concatenate(pieces, axis=1)


def by_rows(ref, scratch, store):
    channels, depth, height, width = ref.shape
    rows = depth * height
    scratch[...] = ref[...].astype(F32).reshape(channels * rows, width)
    for d in range(depth):
        for h in range(height):
            store(d, h, scratch[pl.ds(d * height + h, channels, stride=rows), :])


def odd(axis):
    return lax.rem(lax.axis_index(axis), 2) == 1


def spread_kernel(cot_ref, k2_ref, cot_rows_ref, back_ref, one_ref, two_ref, scratch):
    out, depth, height, _ = cot_ref.shape
    rows = [[None] * height for _ in range(depth)]

    def store(d, h, row):
        rows[d][h] = row.astype(BF)
        cot_rows_ref[d, :, h * LANES : (h + 1) * LANES] = rows[d][h]

    by_rows(cot_ref, scratch, store)
    mid = k2_ref.shape[1]
    none = jnp.zeros((out, 2 * LANES), BF)
    padded = [jnp.concatenate([none, *rows[d], none], axis=1) for d in range(depth)]
    is_odd = odd("dep")
    faces = [[], []]
    for e in range(depth + 2):
        reached = [(d, e - 1 - d) for d in range(depth) if abs(e - 1 - d) <= 1]
        w = jnp.concatenate(
            [
                k2_ref[9 * (a + 1) + 3 * b : 9 * (a + 1) + 3 * b + 3].reshape(3 * mid, out)
                for _, a in reached
                for b in range(3)
            ],
            axis=1,
        )
        for j in range(0, height + 2, 2):
            rhs = jnp.concatenate(
                [padded[d][:, (j + 2 - b) * LANES : (j + 4 - b) * LANES] for d, _ in reached for b in range(3)], axis=0
            )
            y = jnp.dot(w, rhs, preferred_element_type=F32)
            back = sum(moved_along_width(y[n * mid : (n + 1) * mid], n - 1) for n in range(3))
            if 0 < e < depth + 1:
                back_ref[e - 1, :, j * LANES : (j + 2) * LANES] = back
            else:
                faces[e > 0].append(back.astype(BF))
    low, high = (jnp.concatenate(face, axis=1) for face in faces)
    one_ref[...] = jnp.where(is_odd, low, high)
    two_ref[...] = jnp.where(is_odd, high, low)


def arrange_kernel(cot_rows_ref, k1_ref, k2_ref, _, moved_ref, w1_ref, w2_ref):
    depth, out, cells = cot_rows_ref.shape
    for d in range(depth):
        for h in range(0, cells, LANES):
            row = cot_rows_ref[d, :, h : h + LANES]
            for n, c in enumerate((-1, 0, 1)):
                value = row if c == 0 else moved_along_width(row.astype(F32), c).astype(BF)
                moved_ref[d, n * out : (n + 1) * out, h : h + LANES] = value
    mid = k1_ref.shape[2]
    for c in range(3):
        one = jnp.concatenate([k1_ref[3 * ab + c] for ab in range(9)], axis=0)
        w1_ref[c * mid : (c + 1) * mid, :] = one.astype(F32).T.astype(BF)
        two = jnp.concatenate([k2_ref[3 * ab + c] for ab in range(9)], axis=0)
        w2_ref[c * out : (c + 1) * out, :] = two.astype(F32).T.astype(BF)


def sides(axis, one, two):
    me, size = lax.axis_index(axis), lax.axis_size(axis)
    is_odd = odd(axis)
    none = jnp.zeros_like(one)
    before = jnp.where(me == 0, none, jnp.where(is_odd, one, two))
    after = jnp.where(me == size - 1, none, jnp.where(is_odd, two, one))
    return before, after


def rim_kernel(own_ref, one_ref, two_ref, _, deep_ref, send_one_ref, send_two_ref, scratch):
    depth = own_ref.shape[1]
    before, after = sides("dep", one_ref[...], two_ref[...])
    for n, part in enumerate((before, own_ref[...], after)):

        def store(d, h, row, at=n * depth):
            deep_ref[at + d, :, h * LANES : (h + 1) * LANES] = row.astype(BF)

        by_rows(part, scratch, store)
    n, cells = send_one_ref.shape[2], deep_ref.shape[2]
    first, last = deep_ref[:, :, :n], deep_ref[:, :, cells - n :]
    is_odd = odd(HGT)
    send_one_ref[...] = jnp.where(is_odd, first, last)
    send_two_ref[...] = jnp.where(is_odd, last, first)


def back_rim_kernel(own_ref, one_ref, two_ref, back_ref, send_one_ref, send_two_ref):
    before, after = sides("dep", one_ref[...], two_ref[...])
    last = own_ref.shape[0] - 1
    cells = back_ref.shape[2]
    ends = []
    for d in range(last + 1):
        total = own_ref[d]
        if d == 0:
            total = total + before.astype(F32)
        if d == last:
            total = total + after.astype(F32)
        back_ref[d] = total[:, LANES : LANES + cells]
        ends.append((total[:, :LANES].astype(BF), total[:, LANES + cells :].astype(BF)))
    is_odd = odd(HGT)
    for d, (low, high) in enumerate(ends):
        send_one_ref[d] = jnp.where(is_odd, low, high)
        send_two_ref[d] = jnp.where(is_odd, high, low)


def widened(deep_ref, one_ref, two_ref):
    left, right = sides(HGT, one_ref[...], two_ref[...])
    return [jnp.concatenate([left[d], deep_ref[d], right[d]], axis=1) for d in range(deep_ref.shape[0])]


def hidden_kernel(deep_ref, one_ref, two_ref, w1_ref, moved_ref, _, hidden_ref, slope_ref, g2_ref, rows_ref):
    for d, row in enumerate(widened(deep_ref, one_ref, two_ref)):
        rows_ref[d] = row
    rows = rows_ref
    mid = w1_ref.shape[0] // 3
    dep, deps = lax.axis_index("dep"), lax.axis_size("dep")
    hgt, hgts = lax.axis_index(HGT), lax.axis_size(HGT)
    depth, height = hidden_ref.shape[0], hidden_ref.shape[2] // LANES
    w1 = w1_ref[...]
    for d in range(depth):
        for h in range(0, height, 2):
            rhs = jnp.concatenate(
                [rows[d + a, :, (h + b) * LANES : (h + b + 2) * LANES] for a in range(3) for b in range(3)], axis=0
            )
            y = jnp.dot(w1, rhs, preferred_element_type=F32)
            pre = sum(moved_along_width(y[n * mid : (n + 1) * mid], 1 - n) for n in range(3))
            s = 1.0 / (1.0 + jnp.exp(-pre))
            for r in range(2):
                lanes = slice(r * LANES, (r + 1) * LANES)
                p, q = pre[:, lanes], s[:, lanes]
                value = (p * q).astype(BF)
                outside = []
                if d == 0:
                    outside.append(dep == 0)
                if d == depth - 1:
                    outside.append(dep == deps - 1)
                if h + r == 0:
                    outside.append(hgt == 0)
                if h + r == height - 1:
                    outside.append(hgt == hgts - 1)
                for far in outside:
                    value = jnp.where(far, jnp.zeros_like(value), value)
                hidden_ref[d, :, (h + r) * LANES : (h + r + 1) * LANES] = value
                if 0 < d < depth - 1 and 0 < h + r < height - 1:
                    at = (h + r - 1) * LANES
                    slope_ref[d - 1, :, at : at + LANES] = q * (1.0 + p * (1.0 - q))
    cells = (height - 2) * LANES
    own = depth - 2
    out = moved_ref.shape[1] // 3
    left = jnp.concatenate([moved_ref[d] for d in range(own)], axis=1)
    tails = []
    for first in (0, 4, 8):
        group = range(first, min(first + 4, 9))
        right = jnp.concatenate(
            [
                jnp.concatenate(
                    [hidden_ref[d + ab // 3, :, (ab % 3) * LANES : (ab % 3) * LANES + cells] for ab in group], axis=0
                )
                for d in range(own)
            ],
            axis=1,
        )
        g = lax.dot_general(left, right, (((1,), (1,)), ((), ())), preferred_element_type=F32)
        for n in range(3):
            part = g[n * out : (n + 1) * out]
            if first < 8:
                for m in range(2):
                    g2_ref[4 * n + first // 2 + m] = part[:, m * LANES : (m + 1) * LANES]
            else:
                tails.append(part)
    tails.append(jnp.zeros_like(tails[0]))
    for m in range(2):
        g2_ref[12 + m] = jnp.concatenate(tails[2 * m : 2 * m + 2], axis=1)


def features_kernel(hidden_ref, w2_ref, out_ref, token_ref, scratch):
    out = w2_ref.shape[0] // 3
    _, depth, height, _ = out_ref.shape
    w2 = w2_ref[...]
    for d in range(depth):
        for h in range(0, height, 2):
            rhs = jnp.concatenate(
                [
                    hidden_ref[d + a, :, (h + b) * LANES : (h + b + 2) * LANES]
                    for a in range(3)
                    for b in range(3)
                ],
                axis=0,
            )
            y = jnp.dot(w2, rhs, preferred_element_type=F32)
            total = sum(moved_along_width(y[n * out : (n + 1) * out], 1 - n) for n in range(3))
            for r in range(2):
                row = total[:, r * LANES : (r + 1) * LANES]
                scratch[pl.ds(d * height + h + r, out, stride=depth * height), :] = row
    out_ref[...] = scratch[...].reshape(out_ref.shape).astype(BF)
    token_ref[...] = scratch[:8]


def delta_kernel(direct, rows_ref, back_ref, one_ref, two_ref, slope_ref, g2_ref, *outs_and_scratch):
    *out_refs, delta_ref = outs_and_scratch
    before, after = sides(HGT, one_ref[...], two_ref[...])
    own, mid, cells = slope_ref.shape
    for d in range(own):
        for at in range(0, cells, LANES):
            back = back_ref[d, :, at : at + LANES]
            if at == 0:
                back = back + before[d].astype(F32)
            if at == cells - LANES:
                back = back + after[d].astype(F32)
            delta = back * slope_ref[d, :, at : at + LANES]
            for n in range(3):
                delta_ref[n * mid : (n + 1) * mid, d * cells + at : d * cells + at + LANES] = moved_along_width(
                    delta, n - 1
                ).astype(BF)
    left = delta_ref[...]
    blocks, tails = [None] * 6, []
    inner = rows_ref.shape[1]
    for first in (0, 8):
        group = range(first, min(first + 8, 9))
        right = jnp.concatenate(
            [
                jnp.concatenate(
                    [
                        rows_ref[d + 1 + ab // 3, :, (1 + ab % 3) * LANES : (1 + ab % 3) * LANES + cells]
                        for ab in group
                    ],
                    axis=0,
                )
                for d in range(own)
            ],
            axis=1,
        )
        g = lax.dot_general(left, right, (((1,), (1,)), ((), ())), preferred_element_type=F32)
        for n in range(3):
            part = g[n * mid : (n + 1) * mid]
            if first == 0:
                for m in range(2):
                    blocks[2 * n + m] = part[:, m * LANES : (m + 1) * LANES]
            else:
                tails.append(part)
    tails.append(jnp.zeros((mid, LANES - 3 * inner), F32))
    blocks.append(jnp.concatenate(tails, axis=1))
    if not direct:
        for j, block in enumerate(blocks):
            out_refs[0][j] = block
        return
    keep_ref, send_ref = out_refs
    parts, deps, halves, length, _ = keep_ref.shape
    size = mid // parts
    core = lax.axis_index("core") == 1

    def piece(part, number):
        values, row = [], number * length
        while row < (number + 1) * length:
            unit, start = divmod(row, size)
            stop = min(size, start + (number + 1) * length - row)
            if unit < 28:
                first = (2 * part + unit % 2) * size
                values.append(g2_ref[unit // 2, first + start : first + stop, :])
            elif unit < 35:
                values.append(blocks[unit - 28][part * size + start : part * size + stop])
            else:
                values.append(jnp.zeros((stop - start, LANES), F32))
            row += stop - start
        return jnp.concatenate(values, axis=0)

    for part in range(parts):
        for dep in range(deps):
            for half in range(halves):
                one, two = (piece(part, 2 * (dep * halves + half) + c) for c in range(2))
                keep_ref[part, dep, half] = jnp.where(core, two, one)
                send_ref[part, dep, half] = jnp.where(core, one, two).astype(BF)


def join_kernel(keep_ref, got_ref, _, out_ref):
    out_ref[...] = (keep_ref[...] + got_ref[...].astype(F32)).astype(BF)


def total_kernel(in_ref, out_ref):
    value = in_ref[0].astype(F32)
    for n in range(1, in_ref.shape[0]):
        value = value + in_ref[n].astype(F32)
    for n in range(out_ref.shape[0]):
        out_ref[n] = value.astype(BF)


def unpack_kernel(own_ref, got_ref, g1_ref, g2_ref):
    pieces, length, _ = own_ref.shape
    size, inner = g1_ref.shape[1:]
    mid = g2_ref.shape[2]
    core = lax.axis_index("core") == 1
    whole = []
    for n in range(pieces):
        own, got = own_ref[n].astype(F32), got_ref[n].astype(F32)
        whole += [jnp.where(core, got, own), jnp.where(core, own, got)]

    def get(unit):
        values, row = [], unit * size
        while row < (unit + 1) * size:
            number, start = divmod(row, length)
            stop = min(length, start + (unit + 1) * size - row)
            values.append(whole[number][start:stop])
            row += stop - start
        return values[0] if len(values) == 1 else jnp.concatenate(values, axis=0)

    for j in range(14):
        for half in range(2):
            value = get(2 * j + half)
            for m in range(2):
                c, ab = (j // 4, 2 * (j % 4) + m) if j < 12 else (2 * (j - 12) + m, 8)
                if c < 3:
                    g2_ref[3 * ab + c, half * size : (half + 1) * size, :] = value[:, m * mid : (m + 1) * mid]
    for j in range(7):
        value = get(28 + j)
        for m in range(4):
            c, ab = (j // 2, 4 * (j % 2) + m) if j < 6 else (m, 8)
            if c < 3:
                g1_ref[3 * ab + c] = value[:, m * inner : (m + 1) * inner]


def swapped(x, axis, first):
    size = lax.axis_size(axis)
    partner = list(range(size))
    for i in range(first, size - 1, 2):
        partner[i], partner[i + 1] = i + 1, i
    return lax.ppermute(x, axis, list(enumerate(partner)))


def from_other_core(x):
    return lax.ppermute(x, "core", [(0, 1), (1, 0)])


def per_device(volume, kernel_first, kernel_second, cotangent):
    _, inner, depth, height, width = volume.shape
    mid, out = kernel_first.shape[1], kernel_second.shape[1]
    cells = height * width
    parts = lax.axis_size("dp")
    k1, k2 = jnp.swapaxes(kernel_first, 1, 2), jnp.swapaxes(kernel_second, 1, 2)
    rows = depth * height

    one, two = swapped(volume[0], "dep", 0), swapped(volume[0], "dep", 1)
    cot_rows, back, back_one, back_two = call(
        spread_kernel,
        [
            shape((depth, out, cells), BF),
            shape((depth, mid, cells + 2 * width), F32),
            shape((mid, cells + 2 * width), BF),
            shape((mid, cells + 2 * width), BF),
        ],
        [cotangent[0], k2],
        [pltpu.VMEM((out * rows, width), F32)],
        flops=1_100_000_000,
    )
    deep, one, two = call(
        rim_kernel,
        [shape((3 * depth, inner, cells), BF)] + [shape((3 * depth, inner, 2 * width), BF)] * 2,
        [volume[0], one, two, cot_rows],
        [pltpu.VMEM((inner * rows, width), F32)],
    )
    one, two = swapped(one, HGT, 0), swapped(two, HGT, 1)
    moved, w1, w2 = call(
        arrange_kernel,
        [shape((depth, 3 * out, cells), BF), shape((3 * mid, 9 * inner), BF), shape((3 * out, 9 * mid), BF)],
        [cot_rows, k1, k2, deep],
        flops=500_000_000,
    )
    back_one, back_two = swapped(back_one, "dep", 0), swapped(back_two, "dep", 1)
    back, back_one, back_two = call(
        back_rim_kernel,
        [shape((depth, mid, cells), F32)] + [shape((depth, mid, width), BF)] * 2,
        [back, back_one, back_two],
    )
    back_one, back_two = swapped(back_one, HGT, 0), swapped(back_two, HGT, 1)

    hidden, slope, g2, wide = call(
        hidden_kernel,
        [
            shape((depth + 2, mid, cells + 2 * width), BF),
            shape((depth, mid, cells), F32),
            shape((14, out, LANES), F32),
            shape((3 * depth, inner, cells + 4 * width), BF),
        ],
        [deep, one, two, w1, moved, back],
        flops=1_500_000_000,
    )
    size = mid // parts
    direct = parts == 2 and size % 16 == 0
    deps, halves = lax.axis_size("dep"), lax.axis_size("y")
    pieces = deps * halves
    length = -(-35 * size // (16 * pieces)) * 8
    packed = (parts, deps, halves, length, width)
    grads = call(
        functools.partial(delta_kernel, direct),
        [shape(packed, F32), shape(packed, BF)] if direct else [shape((7, mid, LANES), F32)],
        [wide, back, back_one, back_two, slope, g2],
        [pltpu.VMEM((3 * mid, depth * cells), BF)],
        flops=300_000_000,
    )
    if direct:
        keep, send = grads
        group = ("dp", "dep", "y")
    else:
        grad = jnp.swapaxes(grads[0].reshape(7, parts, size, LANES), 0, 1)
        grad2 = jnp.swapaxes(g2.reshape(14, parts, 2, size, LANES), 0, 1).reshape(parts, 28, size, LANES)
        grad = jnp.concatenate([grad2, grad], axis=1).reshape(parts, 35 * size, LANES)
        grad = jnp.pad(grad, ((0, 0), (0, 2 * pieces * length - 35 * size), (0, 0)))
        grad = lax.psum_scatter(grad, "dp", scatter_dimension=0, tiled=True)
        grad = grad.reshape(1, deps, halves, 2, length, LANES)
        core = lax.axis_index("core")
        keep = lax.dynamic_index_in_dim(grad, core, 3, False)
        send = lax.dynamic_index_in_dim(grad, 1 - core, 3, False).astype(BF)
        group = ("dep", "y")
    features, token = call(
        features_kernel,
        [shape(cotangent.shape[1:], BF), shape((8, width), F32)],
        [hidden, w2],
        [pltpu.VMEM((out * rows, width), F32)],
        flops=900_000_000,
    )
    (joined,) = call(join_kernel, [shape(keep.shape, BF)], [keep, from_other_core(send), token])
    arrived = lax.all_to_all(joined.reshape(-1, length, width), group, 0, 0, tiled=True)
    (share,) = call(total_kernel, [shape((pieces, length, width), BF)], [arrived])
    own = lax.all_to_all(share, ("dep", "y"), 0, 0, tiled=True)
    grad_first, grad_second = call(
        unpack_kernel,
        [shape((27, size, inner), F32), shape((27, 2 * size, mid), F32)],
        [own, from_other_core(own)],
    )
    return features[None], grad_first, grad_second


def solution(mesh):
    dp, dep, hgt = (mesh.shape[axis] for axis in ("dp", "dep", "hgt"))
    split = jax.sharding.Mesh(mesh.devices.reshape(dp, dep, hgt // 2, 2), ("dp", "dep", *HGT))
    block = P("dp", None, "dep", HGT, None)
    return jax.shard_map(
        per_device,
        mesh=split,
        in_specs=(block, P(), P(), block),
        out_specs=(block, P(None, "dp", None), P(None, "dp", None)),
        check_vma=False,
    )
```

time: 61.7 us -> 57.1 us (0.925)
  blocking collectives: 0 us -> 28 us
  starting transfers between devices: 27.3 us -> 11.8 us
  waiting for transfers between devices: 17.4 us -> 4.25 us
  local copies, waits for them, and re-layouts: 4.93 us -> 2.06 us
  Pallas kernels: 10.9 us -> 9.9 us
    all_to_all x0 -> x2, blocking collectives: none -> 28 us  [the longest x1 17.6 us: per_device(): lax.all_to_all(joined.reshape(-1, length, width), group, 0, 0, tiled=True)]
    ppermute x20 -> x10, starting transfers between devices: 27.3 us -> 11.8 us  [the longest x8 8.83 us: swapped(): return lax.ppermute(x, axis, list(enumerate(partner)))]
    ppermute x20 -> x10, waiting for transfers between devices: 17.4 us -> 4.25 us  [the longest x8 2.88 us: swapped(): return lax.ppermute(x, axis, list(enumerate(partner)))]
    unnamed x10, local copies, waits for them, and re-layouts: 4.93 us -> 2.06 us
    pallas_call x12 -> x10, Pallas kernels: 10.9 us -> 9.9 us  [call(): pl.pallas_call(body, out_shape=outs, in_specs=[pl.BlockSpec(memory_space=...]
  transfers between devices with their start and end apart: 20 -> 10, of which waited for: 10 -> 2; matrix products, arithmetic and copies ran while one was open for 0% -> 0% of each run, Pallas kernels for 14% -> 14%
where the time goes in v4:
time: 57.1 us; the launch traced here: 56.8 us
  blocking collectives  28 us (49%)
  starting transfers between devices  11.8 us (21%)
  Pallas kernels  9.9 us (17%)
  waiting for transfers between devices  4.25 us (7%)
  local copies, waits for them, and re-layouts  2.06 us (4%)
  between operations  0.78 us (1%)
    all_to_all x1, blocking collectives, per_device(): lax.all_to_all(joined.reshape(-1, length, width), group, 0, 0, tiled=True)  17.6 us
    all_to_all x1, blocking collectives, per_device(): own = lax.all_to_all(share, ('dep', 'y'), 0, 0, tiled=True)  10.4 us
    pallas_call x10, Pallas kernels, call(): pl.pallas_call(body, out_shape=outs, in_specs=[pl.BlockSpec(memory_space=...  9.9 us
    ppermute x8, starting transfers between devices, swapped(): return lax.ppermute(x, axis, list(enumerate(partner)))  8.83 us
    ppermute x2, starting transfers between devices, from_other_core(): return lax.ppermute(x, 'core', [(0, 1), (1, 0)])  2.94 us
    ppermute x8, waiting for transfers between devices, swapped(): return lax.ppermute(x, axis, list(enumerate(partner)))  2.88 us
    unnamed x10, local copies, waits for them, and re-layouts  2.06 us
    ppermute x2, waiting for transfers between devices, from_other_core(): return lax.ppermute(x, 'core', [(0, 1), (1, 0)])  1.37 us
  transfers between devices with their start and end apart: 10, of which 2 were waited for; matrix products, arithmetic and copies ran while one was open for 0% of the time, Pallas kernels for 14%

profile of v4, /device:TPU:0, one launch (start us, length us, event | category | flops | bytes accessed | tf_op | source)
XLA Modules:
  0.0 56.8 jit_solution(4349442261370549862)
XLA Ops:
  0.6 1.6 %collective-permute-start.1 = (bf16[32,2,8,128]{3,2,1,0:T(8,128)(2,1)}, bf16[32,2,8,128]{3,2,1,0:T(8,128)(2,1)S(1)}, u32[]{:S(2)}, u32[]{:S(2)}) collective-permute-start(bf16[32,2,8,128]{3,2,1,0:T(8,128)(2,1)} %bitcast.7), channel_id=1, source_target_pairs={{0,0},{4,8},{8,4},{12,12},{1,1},{5,9},{9,5},{13,13},{2,2},{6,10},{... | collective-permute-start | bytes 393224 | tf_op jit(solution)/shard_map/ppermute | solution.py:377
  2.2 5.0 %collective-permute-start = (bf16[32,2,8,128]{3,2,1,0:T(8,128)(2,1)}, bf16[32,2,8,128]{3,2,1,0:T(8,128)(2,1)S(1)}, u32[]{:S(2)}, u32[]{:S(2)}) collective-permute-start(bf16[32,2,8,128]{3,2,1,0:T(8,128)(2,1)} %bitcast.8), channel_id=1, source_target_pairs={{0,4},{4,0},{8,12},{12,8},{1,5},{5,1},{9,13},{13,9},{2,6},{6,2},{1... | collective-permute-start | bytes 393224 | tf_op jit(solution)/shard_map/ppermute | solution.py:377
  7.2 1.0 %copy-done.1 = bf16[1,128,2,8,128]{4,3,2,1,0:T(8,128)(2,1)S(1)} copy-done((bf16[1,128,2,8,128]{4,3,2,1,0:T(8,128)(2,1)S(1)}, bf16[1,128,2,8,128]{4,3,2,1,0:T(8,128)(2,1)}, u32[]{:S(2)}) %copy-start.1) | copy-done | bytes 524312
  8.3 1.0 %copy-done.2 = bf16[27,128,64]{1,2,0:T(8,128)(2,1)S(1)} copy-done((bf16[27,128,64]{1,2,0:T(8,128)(2,1)S(1)}, bf16[27,128,64]{1,2,0:T(8,128)(2,1)}, u32[]{:S(2)}) %copy-start.2) | copy-done | bytes 442392
  9.3 1.7 %shard_map.67 = (bf16[2,128,1024]{2,1,0:T(8,128)(2,1)S(1)}, f32[2,64,1280]{2,1,0:T(8,128)S(1)}, bf16[64,1280]{1,0:T(8,128)(2,1)S(1)}, bf16[64,1280]{1,0:T(8,128)(2,1)S(1)}) custom-call(bf16[128,2,8,128]{3,2,1,0:T(8,128)(2,1)S(1)} %bitcast.10, bf16[27,64,128]{2,1,0:T(8,128)(2,1)S(1)} %bitcast.11), custom_call_target="tpu_custom_call" | custom-call | flops 1100000000 | bytes 2473984 | tf_op jit(solution)/shard_map/pallas_call | solution.py:18
  11.0 0.1 collective-permute-start.4
  11.1 0.7 %collective-permute-start.5 = (bf16[64,1280]{1,0:T(8,128)(2,1)S(1)}, bf16[64,1280]{1,0:T(8,128)(2,1)S(1)}, u32[]{:S(2)}, u32[]{:S(2)}) collective-permute-start(bf16[64,1280]{1,0:T(8,128)(2,1)S(1)} %get-tuple-element.34), channel_id=1, source_target_pairs={{0,0},{4,8},{8,4},{12,12},{1,1},{5,9},{9,5},{13,13},{2,2},{6,10},{... | collective-permute-start | bytes 491528 | tf_op jit(solution)/shard_map/ppermute | solution.py:377
  11.8 0.4 shard_map.68
  12.2 0.1 collective-permute-start.2
  12.2 0.7 %collective-permute-start.3 = (bf16[6,32,256]{2,1,0:T(8,128)(2,1)S(1)}, bf16[6,32,256]{2,1,0:T(8,128)(2,1)S(1)}, u32[]{:S(2)}, u32[]{:S(2)}) collective-permute-start(bf16[6,32,256]{2,1,0:T(8,128)(2,1)S(1)} %get-tuple-element.29), channel_id=1, source_target_pairs={{0,0},{1,2},{2,1},{3,3},{4,4},{5,6},{6,5},{7,7},{8,8},{9,10},{10,9... | collective-permute-start | bytes 294920 | tf_op jit(solution)/shard_map/ppermute | solution.py:377
  12.9 0.6 %shard_map.69 = (bf16[2,384,1024]{2,1,0:T(8,128)(2,1)S(1)}, bf16[192,288]{1,0:T(8,128)(2,1)S(1)}, bf16[384,576]{1,0:T(8,128)(2,1)S(1)}) custom-call(bf16[2,128,1024]{2,1,0:T(8,128)(2,1)S(1)} %get-tuple-element.26._.cot_rows_ref, bf16[27,32,64]{2,1,0:T(8,128)(2,1)S(1)} %bitcast.13, bf16[27,64,128]{2,1,0:T(8,128)(2,1)S(1)} %bitcast.12, ...), custom_call_target="tpu_custom_call" | custom-call | flops 500000000 | bytes 3596288 | tf_op jit(solution)/shard_map/pallas_call | solution.py:18
  13.6 2.9 %collective-permute-done.4.one_ref = bf16[64,1280]{1,0:T(8,128)(2,1)S(1)} collective-permute-done((bf16[64,1280]{1,0:T(8,128)(2,1)S(1)}, bf16[64,1280]{1,0:T(8,128)(2,1)S(1)}, u32[]{:S(2)}, u32[]{:S(2)}) %collective-permute-start.4) | collective-permute-done | bytes 163872 | tf_op jit(solution)/shard_map/ppermute | solution.py:377
  16.4 0.1 shard_map.70
  16.5 0.1 collective-permute-start.6
  16.6 0.7 %collective-permute-start.7 = (bf16[2,64,128]{2,1,0:T(8,128)(2,1)S(1)}, bf16[2,64,128]{2,1,0:T(8,128)(2,1)S(1)}, u32[]{:S(2)}, u32[]{:S(2)}) collective-permute-start(bf16[2,64,128]{2,1,0:T(8,128)(2,1)S(1)} %get-tuple-element.41), channel_id=1, source_target_pairs={{0,0},{1,2},{2,1},{3,3},{4,4},{5,6},{6,5},{7,7},{8,8},{9,10},{10,9... | collective-permute-start | bytes 98312 | tf_op jit(solution)/shard_map/ppermute | solution.py:377
  17.3 2.5 %shard_map.71 = (bf16[4,64,1280]{2,1,0:T(8,128)(2,1)S(1)}, f32[2,64,1024]{2,1,0:T(8,128)S(1)}, f32[14,128,128]{2,1,0:T(8,128)S(1)}, bf16[6,32,1536]{2,1,0:T(8,128)(2,1)S(1)}) custom-call(bf16[6,32,1024]{2,1,0:T(8,128)(2,1)S(1)} %get-tuple-element.27._.deep_ref, bf16[6,32,256]{2,1,0:T(8,128)(2,1)S(1)} %collective-permute-done.2.one_ref, ...), custom_call_target="tpu_custom_call" | custom-call | flops 1500000000 | bytes 5484544 | tf_op jit(solution)/shard_map/pallas_call | solution.py:18
  19.9 0.8 %shard_map.73 = (f32[2,4,2,72,128]{4,3,2,1,0:T(8,128)S(1)}, bf16[2,4,2,72,128]{4,3,2,1,0:T(8,128)(2,1)S(1)}) custom-call(bf16[6,32,1536]{2,1,0:T(8,128)(2,1)S(1)} %get-tuple-element.39.rows_ref, f32[2,64,1024]{2,1,0:T(8,128)S(1)} %get-tuple-element.35._.back_ref, bf16[2,64,128]{2,1,0:T(8,128)(2,1)S(1)} %collective-permute-done.6.one_ref, ...), custom_call_target="tpu_custom_call" | custom-call | flops 300000000 | bytes 3506176 | tf_op jit(solution)/shard_map/pallas_call | solution.py:18
  20.6 2.9 %collective-permute-start.8 = (bf16[2,4,2,72,128]{4,3,2,1,0:T(8,128)(2,1)S(1)}, bf16[2,4,2,72,128]{4,3,2,1,0:T(8,128)(2,1)S(1)}, u32[]{:S(2)}, u32[]{:S(2)}) collective-permute-start(bf16[2,4,2,72,128]{4,3,2,1,0:T(8,128)(2,1)S(1)} %get-tuple-element.45), channel_id=1, source_target_pairs={{0,1},{1,0},{2,3},{3,2},{4,5},{5,4},{6,7},{7,6},{8,9},{9,8},{10,11... | collective-permute-start | bytes 884744 | tf_op jit(solution)/shard_map/ppermute | solution.py:381
  23.6 2.5 %shard_map.72 = (bf16[128,2,8,128]{3,2,1,0:T(8,128)(2,1)}, f32[8,128]{1,0:T(8,128)S(1)}) custom-call(bf16[4,64,1280]{2,1,0:T(8,128)(2,1)S(1)} %get-tuple-element.36.hidden_ref, bf16[384,576]{1,0:T(8,128)(2,1)S(1)} %get-tuple-element.37.w2_ref), custom_call_target="tpu_custom_call" | custom-call | flops 900000000 | bytes 1626112 | tf_op jit(solution)/shard_map/pallas_call | solution.py:18
  26.1 0.1 shard_map.74
  26.1 17.6 %all_to_all.10.in_ref = bf16[16,72,128]{2,1,0:T(8,128)(2,1)S(1)} all-to-all(bf16[16,72,128]{2,1,0:T(8,128)(2,1)S(1)} %bitcast.6), channel_id=1, replica_groups=mesh['dp'=2,'dep'=4,'y'=2,'core'=2] {'dp','dep','y'}, dimensions={0} | all-to-all | bytes 589824 | tf_op jit(solution)/shard_map/all_to_all | solution.py:472
  43.8 10.4 %all_to_all.11.own_ref = bf16[8,72,128]{2,1,0:T(8,128)(2,1)S(1)} all-to-all(bf16[8,72,128]{2,1,0:T(8,128)(2,1)S(1)} %shard_map.75), channel_id=1, replica_groups=mesh['dp'=2,'dep'=4,'y'=2,'core'=2] {'dep','y'}, dimensions={0} | all-to-all | bytes 294912 | tf_op jit(solution)/shard_map/all_to_all | solution.py:474
  54.2 1.4 %collective-permute-done.9.got_ref = bf16[8,72,128]{2,1,0:T(8,128)(2,1)S(1)} collective-permute-done((bf16[8,72,128]{2,1,0:T(8,128)(2,1)S(1)}, bf16[8,72,128]{2,1,0:T(8,128)(2,1)S(1)}, u32[]{:S(2)}, u32[]{:S(2)}) %collective-permute-start.9) | collective-permute-done | bytes 147488 | tf_op jit(solution)/shard_map/ppermute | solution.py:381
  55.6 1.2 %shard_map.76 = (f32[27,32,32]{2,1,0:T(8,128)}, f32[27,64,64]{2,1,0:T(8,128)}) custom-call(bf16[8,72,128]{2,1,0:T(8,128)(2,1)S(1)} %all_to_all.11.own_ref, bf16[8,72,128]{2,1,0:T(8,128)(2,1)S(1)} %collective-permute-done.9.got_ref), custom_call_target="tpu_custom_call" | custom-call | bytes 847872 | tf_op jit(solution)/shard_map/pallas_call | solution.py:18
  (18 shorter events, 0.1 us)
Async XLA Ops:
  0.6 11.1 %collective-permute-start.1 = (bf16[32,2,8,128]{3,2,1,0:T(8,128)(2,1)}, bf16[32,2,8,128]{3,2,1,0:T(8,128)(2,1)S(1)}, u32[]{:S(2)}, u32[]{:S(2)}) collective-permute-start(bf16[32,2,8,128]{3,2,1,0:T(8,128)(2,1)} %bitcast.7), channel_id=1, source_target_pairs={{0,0},{4,8},{8,4},{12,12},{1,1},{5,9},{9,5},{13,13},{2,2},{6,10},{... | collective-permute-start | bytes 393224 | tf_op jit(solution)/shard_map/ppermute | solution.py:377
  2.2 9.6 %collective-permute-start = (bf16[32,2,8,128]{3,2,1,0:T(8,128)(2,1)}, bf16[32,2,8,128]{3,2,1,0:T(8,128)(2,1)S(1)}, u32[]{:S(2)}, u32[]{:S(2)}) collective-permute-start(bf16[32,2,8,128]{3,2,1,0:T(8,128)(2,1)} %bitcast.8), channel_id=1, source_target_pairs={{0,4},{4,0},{8,12},{12,8},{1,5},{5,1},{9,13},{13,9},{2,6},{6,2},{1... | collective-permute-start | bytes 393224 | tf_op jit(solution)/shard_map/ppermute | solution.py:377
  7.2 1.0 %copy-start.1 = (bf16[1,128,2,8,128]{4,3,2,1,0:T(8,128)(2,1)S(1)}, bf16[1,128,2,8,128]{4,3,2,1,0:T(8,128)(2,1)}, u32[]{:S(2)}) copy-start(bf16[1,128,2,8,128]{4,3,2,1,0:T(8,128)(2,1)} %param.7) | copy-start | bytes 1572868
  8.3 1.0 %copy-start.2 = (bf16[27,128,64]{1,2,0:T(8,128)(2,1)S(1)}, bf16[27,128,64]{1,2,0:T(8,128)(2,1)}, u32[]{:S(2)}) copy-start(bf16[27,128,64]{1,2,0:T(8,128)(2,1)} %param.6) | copy-start | bytes 1327108
  9.3 2.5 %copy-start = (bf16[1,32,2,8,128]{4,3,2,1,0:T(8,128)(2,1)S(1)}, bf16[1,32,2,8,128]{4,3,2,1,0:T(8,128)(2,1)}, u32[]{:S(2)}) copy-start(bf16[1,32,2,8,128]{4,3,2,1,0:T(8,128)(2,1)} %param.4) | copy-start | bytes 393220
  9.3 3.7 %copy-start.3 = (bf16[27,128,64]{1,2,0:T(8,128)(2,1)S(1)}, bf16[27,128,64]{1,2,0:T(8,128)(2,1)}, u32[]{:S(2)}) copy-start(bf16[27,128,64]{1,2,0:T(8,128)(2,1)} %param.6) | copy-start | bytes 1327108
  9.3 3.7 %copy-start.4 = (bf16[27,64,32]{1,2,0:T(8,128)(2,1)S(1)}, bf16[27,64,32]{1,2,0:T(8,128)(2,1)}, u32[]{:S(2)}) copy-start(bf16[27,64,32]{1,2,0:T(8,128)(2,1)} %param.5) | copy-start | bytes 331780
  11.0 5.4 %collective-permute-start.4 = (bf16[64,1280]{1,0:T(8,128)(2,1)S(1)}, bf16[64,1280]{1,0:T(8,128)(2,1)S(1)}, u32[]{:S(2)}, u32[]{:S(2)}) collective-permute-start(bf16[64,1280]{1,0:T(8,128)(2,1)S(1)} %get-tuple-element.33), channel_id=1, source_target_pairs={{0,4},{4,0},{8,12},{12,8},{1,5},{5,1},{9,13},{13,9},{2,6},{6,2},{1... | collective-permute-start | bytes 491528 | tf_op jit(solution)/shard_map/ppermute | solution.py:377
  11.1 5.4 %collective-permute-start.5 = (bf16[64,1280]{1,0:T(8,128)(2,1)S(1)}, bf16[64,1280]{1,0:T(8,128)(2,1)S(1)}, u32[]{:S(2)}, u32[]{:S(2)}) collective-permute-start(bf16[64,1280]{1,0:T(8,128)(2,1)S(1)} %get-tuple-element.34), channel_id=1, source_target_pairs={{0,0},{4,8},{8,4},{12,12},{1,1},{5,9},{9,5},{13,13},{2,2},{6,10},{... | collective-permute-start | bytes 491528 | tf_op jit(solution)/shard_map/ppermute | solution.py:377
  12.2 5.1 %collective-permute-start.2 = (bf16[6,32,256]{2,1,0:T(8,128)(2,1)S(1)}, bf16[6,32,256]{2,1,0:T(8,128)(2,1)S(1)}, u32[]{:S(2)}, u32[]{:S(2)}) collective-permute-start(bf16[6,32,256]{2,1,0:T(8,128)(2,1)S(1)} %get-tuple-element.28), channel_id=1, source_target_pairs={{0,1},{1,0},{2,3},{3,2},{4,5},{5,4},{6,7},{7,6},{8,9},{9,8},{10,11... | collective-permute-start | bytes 294920 | tf_op jit(solution)/shard_map/ppermute | solution.py:377
  12.2 5.1 %collective-permute-start.3 = (bf16[6,32,256]{2,1,0:T(8,128)(2,1)S(1)}, bf16[6,32,256]{2,1,0:T(8,128)(2,1)S(1)}, u32[]{:S(2)}, u32[]{:S(2)}) collective-permute-start(bf16[6,32,256]{2,1,0:T(8,128)(2,1)S(1)} %get-tuple-element.29), channel_id=1, source_target_pairs={{0,0},{1,2},{2,1},{3,3},{4,4},{5,6},{6,5},{7,7},{8,8},{9,10},{10,9... | collective-permute-start | bytes 294920 | tf_op jit(solution)/shard_map/ppermute | solution.py:377
  16.5 3.3 %collective-permute-start.6 = (bf16[2,64,128]{2,1,0:T(8,128)(2,1)S(1)}, bf16[2,64,128]{2,1,0:T(8,128)(2,1)S(1)}, u32[]{:S(2)}, u32[]{:S(2)}) collective-permute-start(bf16[2,64,128]{2,1,0:T(8,128)(2,1)S(1)} %get-tuple-element.40), channel_id=1, source_target_pairs={{0,1},{1,0},{2,3},{3,2},{4,5},{5,4},{6,7},{7,6},{8,9},{9,8},{10,11... | collective-permute-start | bytes 98312 | tf_op jit(solution)/shard_map/ppermute | solution.py:377
  16.6 3.2 %collective-permute-start.7 = (bf16[2,64,128]{2,1,0:T(8,128)(2,1)S(1)}, bf16[2,64,128]{2,1,0:T(8,128)(2,1)S(1)}, u32[]{:S(2)}, u32[]{:S(2)}) collective-permute-start(bf16[2,64,128]{2,1,0:T(8,128)(2,1)S(1)} %get-tuple-element.41), channel_id=1, source_target_pairs={{0,0},{1,2},{2,1},{3,3},{4,4},{5,6},{6,5},{7,7},{8,8},{9,10},{10,9... | collective-permute-start | bytes 98312 | tf_op jit(solution)/shard_map/ppermute | solution.py:377
  20.6 5.4 %collective-permute-start.8 = (bf16[2,4,2,72,128]{4,3,2,1,0:T(8,128)(2,1)S(1)}, bf16[2,4,2,72,128]{4,3,2,1,0:T(8,128)(2,1)S(1)}, u32[]{:S(2)}, u32[]{:S(2)}) collective-permute-start(bf16[2,4,2,72,128]{4,3,2,1,0:T(8,128)(2,1)S(1)} %get-tuple-element.45), channel_id=1, source_target_pairs={{0,1},{1,0},{2,3},{3,2},{4,5},{5,4},{6,7},{7,6},{8,9},{9,8},{10,11... | collective-permute-start | bytes 884744 | tf_op jit(solution)/shard_map/ppermute | solution.py:381
  54.2 1.4 %collective-permute-start.9 = (bf16[8,72,128]{2,1,0:T(8,128)(2,1)S(1)}, bf16[8,72,128]{2,1,0:T(8,128)(2,1)S(1)}, u32[]{:S(2)}, u32[]{:S(2)}) collective-permute-start(bf16[8,72,128]{2,1,0:T(8,128)(2,1)S(1)} %all_to_all.11.own_ref), channel_id=1, source_target_pairs={{0,1},{1,0},{2,3},{3,2},{4,5},{5,4},{6,7},{7,6},{8,9},{9,8},{10,11... | collective-permute-start | bytes 442376 | tf_op jit(solution)/shard_map/ppermute | solution.py:381

commit v5 on v4

--- a/solution.py
+++ b/solution.py
@@ -296,7 +296,7 @@
             out_refs[0][j] = block
         return
     keep_ref, send_ref = out_refs
-    parts, deps, halves, length, _ = keep_ref.shape
+    parts, halves, length, _ = keep_ref.shape
     size = mid // parts
     core = lax.axis_index("core") == 1
 
@@ -316,23 +316,38 @@
         return jnp.concatenate(values, axis=0)
 
     for part in range(parts):
-        for dep in range(deps):
-            for half in range(halves):
-                one, two = (piece(part, 2 * (dep * halves + half) + c) for c in range(2))
-                keep_ref[part, dep, half] = jnp.where(core, two, one)
-                send_ref[part, dep, half] = jnp.where(core, one, two).astype(BF)
-
-
-def join_kernel(keep_ref, got_ref, _, out_ref):
-    out_ref[...] = (keep_ref[...] + got_ref[...].astype(F32)).astype(BF)
-
-
-def total_kernel(in_ref, out_ref):
-    value = in_ref[0].astype(F32)
-    for n in range(1, in_ref.shape[0]):
-        value = value + in_ref[n].astype(F32)
-    for n in range(out_ref.shape[0]):
-        out_ref[n] = value.astype(BF)
+        for half in range(halves):
+            one, two = (piece(part, 2 * half + c) for c in range(2))
+            keep_ref[part, half] = jnp.where(core, two, one)
+            send_ref[part, half] = jnp.where(core, one, two).astype(BF)
+
+
+def plane_kernel(moves, keep_ref, got_ref, kept_ref, *send_refs):
+    part = lax.rem(lax.axis_index("dp"), keep_ref.shape[0])
+    half = lax.axis_index("y")
+    kept_ref[...] = keep_ref[part, half] + got_ref[part, half].astype(F32)
+    for (x, y), send_ref in zip(moves, send_refs, strict=True):
+        p = 1 - part if x else part
+        h = 1 - half if y else half
+        send_ref[...] = (keep_ref[p, h] + got_ref[p, h].astype(F32)).astype(BF)
+
+
+def total_kernel(kept_ref, *refs):
+    *got_refs, _, out_ref = refs
+    value = kept_ref[...]
+    for ref in got_refs:
+        value = value + ref[...].astype(F32)
+    out_ref[...] = value.astype(BF)
+
+
+def add_kernel(one_ref, two_ref, out_ref):
+    out_ref[...] = (one_ref[...].astype(F32) + two_ref[...].astype(F32)).astype(BF)
+
+
+def order_kernel(own_ref, got_ref, out_ref):
+    mine = lax.axis_index("y")
+    out_ref[mine] = own_ref[...]
+    out_ref[1 - mine] = got_ref[...]
 
 
 def unpack_kernel(own_ref, got_ref, g1_ref, g2_ref):
@@ -370,15 +385,24 @@
 
 
 def swapped(x, axis, first):
-    size = lax.axis_size(axis)
-    partner = list(range(size))
-    for i in range(first, size - 1, 2):
-        partner[i], partner[i + 1] = i + 1, i
-    return lax.ppermute(x, axis, list(enumerate(partner)))
-
-
-def from_other_core(x):
-    return lax.ppermute(x, "core", [(0, 1), (1, 0)])
+    axes = (axis,) if isinstance(axis, str) else axis
+    parts, size = lax.axis_size("dp"), lax.axis_size(axis)
+    partner = list(range(parts * size))
+    for i in partner:
+        part, at = divmod(i, size)
+        if first <= at < size - (size - first) % 2:
+            partner[i] = part * size + (at - first ^ 1) + first
+        elif parts % 2 == 0:
+            partner[i] = (part ^ 1) * size + at
+    return lax.ppermute(x, ("dp", *axes), list(enumerate(partner)))
+
+
+def across(x, *moves):
+    axes = tuple(axis for axis, _ in moves)
+    flip = 0
+    for axis, bit in moves:
+        flip = flip * lax.axis_size(axis) + bit
+    return lax.ppermute(x, axes, [(i, i ^ flip) for i in range(lax.axis_size(axes))])
 
 
 def per_device(volume, kernel_first, kernel_second, cotangent):
@@ -436,10 +460,9 @@
     )
     size = mid // parts
     direct = parts == 2 and size % 16 == 0
-    deps, halves = lax.axis_size("dep"), lax.axis_size("y")
-    pieces = deps * halves
-    length = -(-35 * size // (16 * pieces)) * 8
-    packed = (parts, deps, halves, length, width)
+    halves = lax.axis_size("y")
+    length = -(-35 * size // (32 * halves)) * 16
+    packed = (parts, halves, length, width)
     grads = call(
         functools.partial(delta_kernel, direct),
         [shape(packed, F32), shape(packed, BF)] if direct else [shape((7, mid, LANES), F32)],
@@ -449,18 +472,18 @@
     )
     if direct:
         keep, send = grads
-        group = ("dp", "dep", "y")
+        moves = [(1, 0), (0, 1), (1, 1)]
     else:
         grad = jnp.swapaxes(grads[0].reshape(7, parts, size, LANES), 0, 1)
         grad2 = jnp.swapaxes(g2.reshape(14, parts, 2, size, LANES), 0, 1).reshape(parts, 28, size, LANES)
         grad = jnp.concatenate([grad2, grad], axis=1).reshape(parts, 35 * size, LANES)
-        grad = jnp.pad(grad, ((0, 0), (0, 2 * pieces * length - 35 * size), (0, 0)))
+        grad = jnp.pad(grad, ((0, 0), (0, 2 * halves * length - 35 * size), (0, 0)))
         grad = lax.psum_scatter(grad, "dp", scatter_dimension=0, tiled=True)
-        grad = grad.reshape(1, deps, halves, 2, length, LANES)
+        grad = grad.reshape(1, halves, 2, length, LANES)
         core = lax.axis_index("core")
-        keep = lax.dynamic_index_in_dim(grad, core, 3, False)
-        send = lax.dynamic_index_in_dim(grad, 1 - core, 3, False).astype(BF)
-        group = ("dep", "y")
+        keep = lax.dynamic_index_in_dim(grad, core, 2, False)
+        send = lax.dynamic_index_in_dim(grad, 1 - core, 2, False).astype(BF)
+        moves = [(0, 1)]
     features, token = call(
         features_kernel,
         [shape(cotangent.shape[1:], BF), shape((8, width), F32)],
@@ -468,14 +491,20 @@
         [pltpu.VMEM((out * rows, width), F32)],
         flops=900_000_000,
     )
-    (joined,) = call(join_kernel, [shape(keep.shape, BF)], [keep, from_other_core(send), token])
-    arrived = lax.all_to_all(joined.reshape(-1, length, width), group, 0, 0, tiled=True)
-    (share,) = call(total_kernel, [shape((pieces, length, width), BF)], [arrived])
-    own = lax.all_to_all(share, ("dep", "y"), 0, 0, tiled=True)
+    kept, *sends = call(
+        functools.partial(plane_kernel, moves),
+        [shape((length, width), F32)] + [shape((length, width), BF)] * len(moves),
+        [keep, across(send, ("core", 1))],
+    )
+    gots = [across(send, ("dp", x), ("y", y)) for send, (x, y) in zip(sends, moves, strict=True)]
+    (share,) = call(total_kernel, [shape((length, width), BF)], [kept, *gots, token])
+    for bit in (1, 2):
+        (share,) = call(add_kernel, [shape((length, width), BF)], [share, across(share, ("dep", bit))])
+    (own,) = call(order_kernel, [shape((halves, length, width), BF)], [share, across(share, ("y", 1))])
     grad_first, grad_second = call(
         unpack_kernel,
         [shape((27, size, inner), F32), shape((27, 2 * size, mid), F32)],
-        [own, from_other_core(own)],
+        [own, across(own, ("core", 1))],
     )
     return features[None], grad_first, grad_second
 

time: 57.1 us -> 47.9 us (0.84)
  blocking collectives: 28 us -> 0 us
  waiting for transfers between devices: 4.25 us -> 17.8 us
  starting transfers between devices: 11.8 us -> 17.2 us
    all_to_all x2 -> x0, blocking collectives: 28 us -> none  [the longest x1 17.6 us: per_device(): lax.all_to_all(joined.reshape(-1, length, width), group, 0, 0, tiled=True)]
    ppermute x10 -> x16, waiting for transfers between devices: 4.25 us -> 17.8 us  [the longest x8 15.6 us: across(): lax.ppermute(x, axes, [(i, i ^ flip) for i in range(lax.axis_size(axes))])]
    ppermute x10 -> x16, starting transfers between devices: 11.8 us -> 17.2 us  [the longest x8 8.66 us: swapped(): return lax.ppermute(x, ('dp', *axes), list(enumerate(partner)))]
    pallas_call x10 -> x13, Pallas kernels: 9.9 us -> 9.93 us  [call(): pl.pallas_call(body, out_shape=outs, in_specs=[pl.BlockSpec(memory_space=...]
  transfers between devices with their start and end apart: 10 -> 16, of which waited for: 2 -> 10; matrix products, arithmetic and copies ran while one was open for 0% -> 0% of each run, Pallas kernels for 14% -> 16%
where the time goes in v5:
time: 47.9 us; the launch traced here: 47.7 us
  waiting for transfers between devices  17.8 us (37%)
  starting transfers between devices  17.2 us (36%)
  Pallas kernels  9.93 us (21%)
  local copies, waits for them, and re-layouts  2.06 us (4%)
  between operations  0.73 us (2%)
    ppermute x8, waiting for transfers between devices, across(): lax.ppermute(x, axes, [(i, i ^ flip) for i in range(lax.axis_size(axes))])  15.6 us
    pallas_call x13, Pallas kernels, call(): pl.pallas_call(body, out_shape=outs, in_specs=[pl.BlockSpec(memory_space=...  9.93 us
    ppermute x8, starting transfers between devices, swapped(): return lax.ppermute(x, ('dp', *axes), list(enumerate(partner)))  8.66 us
    ppermute x8, starting transfers between devices, across(): lax.ppermute(x, axes, [(i, i ^ flip) for i in range(lax.axis_size(axes))])  8.51 us
    ppermute x8, waiting for transfers between devices, swapped(): return lax.ppermute(x, ('dp', *axes), list(enumerate(partner)))  2.24 us
    unnamed x10, local copies, waits for them, and re-layouts  2.06 us
  transfers between devices with their start and end apart: 16, of which 10 were waited for; matrix products, arithmetic and copies ran while one was open for 0% of the time, Pallas kernels for 16%

profile of v5, /device:TPU:0, one launch (start us, length us, event | category | flops | bytes accessed | tf_op | source)
XLA Modules:
  0.0 47.7 jit_solution(13716671949974926562)
XLA Ops:
  0.6 3.0 %collective-permute-start.1 = (bf16[32,2,8,128]{3,2,1,0:T(8,128)(2,1)}, bf16[32,2,8,128]{3,2,1,0:T(8,128)(2,1)S(1)}, u32[]{:S(2)}, u32[]{:S(2)}) collective-permute-start(bf16[32,2,8,128]{3,2,1,0:T(8,128)(2,1)} %bitcast.5), channel_id=1, source_target_pairs={{0,16},{4,8},{8,4},{12,28},{16,0},{20,24},{24,20},{28,12},{1,17},{... | collective-permute-start | bytes 393224 | tf_op jit(solution)/shard_map/ppermute | solution.py:397
  3.6 1.7 %collective-permute-start = (bf16[32,2,8,128]{3,2,1,0:T(8,128)(2,1)}, bf16[32,2,8,128]{3,2,1,0:T(8,128)(2,1)S(1)}, u32[]{:S(2)}, u32[]{:S(2)}) collective-permute-start(bf16[32,2,8,128]{3,2,1,0:T(8,128)(2,1)} %bitcast.6), channel_id=1, source_target_pairs={{0,4},{4,0},{8,12},{12,8},{16,20},{20,16},{24,28},{28,24},{1,5},{5... | collective-permute-start | bytes 393224 | tf_op jit(solution)/shard_map/ppermute | solution.py:397
  5.3 1.0 %copy-done.1 = bf16[1,128,2,8,128]{4,3,2,1,0:T(8,128)(2,1)S(1)} copy-done((bf16[1,128,2,8,128]{4,3,2,1,0:T(8,128)(2,1)S(1)}, bf16[1,128,2,8,128]{4,3,2,1,0:T(8,128)(2,1)}, u32[]{:S(2)}) %copy-start.1) | copy-done | bytes 524312
  6.3 1.0 %copy-done.2 = bf16[27,128,64]{1,2,0:T(8,128)(2,1)S(1)} copy-done((bf16[27,128,64]{1,2,0:T(8,128)(2,1)S(1)}, bf16[27,128,64]{1,2,0:T(8,128)(2,1)}, u32[]{:S(2)}) %copy-start.2) | copy-done | bytes 442392
  7.4 1.7 %shard_map.67 = (bf16[2,128,1024]{2,1,0:T(8,128)(2,1)S(1)}, f32[2,64,1280]{2,1,0:T(8,128)S(1)}, bf16[64,1280]{1,0:T(8,128)(2,1)S(1)}, bf16[64,1280]{1,0:T(8,128)(2,1)S(1)}) custom-call(bf16[128,2,8,128]{3,2,1,0:T(8,128)(2,1)S(1)} %bitcast.8, bf16[27,64,128]{2,1,0:T(8,128)(2,1)S(1)} %bitcast.9), custom_call_target="tpu_custom_call" | custom-call | flops 1100000000 | bytes 2473984 | tf_op jit(solution)/shard_map/pallas_call | solution.py:18
  9.5 1.2 %collective-permute-start.5 = (bf16[64,1280]{1,0:T(8,128)(2,1)S(1)}, bf16[64,1280]{1,0:T(8,128)(2,1)S(1)}, u32[]{:S(2)}, u32[]{:S(2)}) collective-permute-start(bf16[64,1280]{1,0:T(8,128)(2,1)S(1)} %get-tuple-element.38), channel_id=1, source_target_pairs={{0,16},{4,8},{8,4},{12,28},{16,0},{20,24},{24,20},{28,12},{1,17},{... | collective-permute-start | bytes 491528 | tf_op jit(solution)/shard_map/ppermute | solution.py:397
  11.2 0.9 %collective-permute-start.3 = (bf16[6,32,256]{2,1,0:T(8,128)(2,1)S(1)}, bf16[6,32,256]{2,1,0:T(8,128)(2,1)S(1)}, u32[]{:S(2)}, u32[]{:S(2)}) collective-permute-start(bf16[6,32,256]{2,1,0:T(8,128)(2,1)S(1)} %get-tuple-element.33), channel_id=1, source_target_pairs={{0,16},{1,2},{2,1},{3,19},{16,0},{17,18},{18,17},{19,3},{4,20},{5,... | collective-permute-start | bytes 294920 | tf_op jit(solution)/shard_map/ppermute | solution.py:397
  12.7 1.8 %collective-permute-done.4.one_ref = bf16[64,1280]{1,0:T(8,128)(2,1)S(1)} collective-permute-done((bf16[64,1280]{1,0:T(8,128)(2,1)S(1)}, bf16[64,1280]{1,0:T(8,128)(2,1)S(1)}, u32[]{:S(2)}, u32[]{:S(2)}) %collective-permute-start.4) | collective-permute-done | bytes 163872 | tf_op jit(solution)/shard_map/ppermute | solution.py:397
  15.0 1.3 %collective-permute-start.7 = (bf16[2,64,128]{2,1,0:T(8,128)(2,1)S(1)}, bf16[2,64,128]{2,1,0:T(8,128)(2,1)S(1)}, u32[]{:S(2)}, u32[]{:S(2)}) collective-permute-start(bf16[2,64,128]{2,1,0:T(8,128)(2,1)S(1)} %get-tuple-element.45), channel_id=1, source_target_pairs={{0,16},{1,2},{2,1},{3,19},{16,0},{17,18},{18,17},{19,3},{4,20},{5,... | collective-permute-start | bytes 98312 | tf_op jit(solution)/shard_map/ppermute | solution.py:397
  16.3 2.5 %shard_map.71 = (bf16[4,64,1280]{2,1,0:T(8,128)(2,1)S(1)}, f32[2,64,1024]{2,1,0:T(8,128)S(1)}, f32[14,128,128]{2,1,0:T(8,128)S(1)}, bf16[6,32,1536]{2,1,0:T(8,128)(2,1)S(1)}) custom-call(bf16[6,32,1024]{2,1,0:T(8,128)(2,1)S(1)} %get-tuple-element.31._.deep_ref, bf16[6,32,256]{2,1,0:T(8,128)(2,1)S(1)} %collective-permute-done.2.one_ref, ...), custom_call_target="tpu_custom_call" | custom-call | flops 1500000000 | bytes 5484544 | tf_op jit(solution)/shard_map/pallas_call | solution.py:18
  20.6 1.2 %collective-permute-done.8.got_ref = bf16[2,2,288,128]{3,2,1,0:T(8,128)(2,1)S(1)} collective-permute-done((bf16[2,2,288,128]{3,2,1,0:T(8,128)(2,1)S(1)}, bf16[2,2,288,128]{3,2,1,0:T(8,128)(2,1)S(1)}, u32[]{:S(2)}, u32[]{:S(2)}) %collective-permute-start.8) | collective-permute-done | bytes 294944 | tf_op jit(solution)/shard_map/ppermute | solution.py:405
  21.9 1.8 %collective-permute-start.9 = (bf16[288,128]{1,0:T(8,128)(2,1)S(1)}, bf16[288,128]{1,0:T(8,128)(2,1)S(1)}, u32[]{:S(2)}, u32[]{:S(2)}) collective-permute-start(bf16[288,128]{1,0:T(8,128)(2,1)S(1)} %get-tuple-element.51), channel_id=1, source_target_pairs={{0,16},{2,18},{16,0},{18,2},{1,17},{3,19},{17,1},{19,3},{4,20},{6,... | collective-permute-start | bytes 221192 | tf_op jit(solution)/shard_map/ppermute | solution.py:405
  23.7 1.0 %collective-permute-start.10 = (bf16[288,128]{1,0:T(8,128)(2,1)S(1)}, bf16[288,128]{1,0:T(8,128)(2,1)S(1)}, u32[]{:S(2)}, u32[]{:S(2)}) collective-permute-start(bf16[288,128]{1,0:T(8,128)(2,1)S(1)} %get-tuple-element.52), channel_id=1, source_target_pairs={{0,2},{2,0},{16,18},{18,16},{1,3},{3,1},{17,19},{19,17},{4,6},{6,4... | collective-permute-start | bytes 221192 | tf_op jit(solution)/shard_map/ppermute | solution.py:405
  25.4 2.5 %shard_map.72 = (bf16[128,2,8,128]{3,2,1,0:T(8,128)(2,1)}, f32[8,128]{1,0:T(8,128)S(1)}) custom-call(bf16[4,64,1280]{2,1,0:T(8,128)(2,1)S(1)} %get-tuple-element.40.hidden_ref, bf16[384,576]{1,0:T(8,128)(2,1)S(1)} %get-tuple-element.41.w2_ref), custom_call_target="tpu_custom_call" | custom-call | flops 900000000 | bytes 1626112 | tf_op jit(solution)/shard_map/pallas_call | solution.py:18
  27.9 0.9 %collective-permute-done.10.refs_1_ = bf16[288,128]{1,0:T(8,128)(2,1)S(1)} collective-permute-done((bf16[288,128]{1,0:T(8,128)(2,1)S(1)}, bf16[288,128]{1,0:T(8,128)(2,1)S(1)}, u32[]{:S(2)}, u32[]{:S(2)}) %collective-permute-start.10) | collective-permute-done | bytes 73760 | tf_op jit(solution)/shard_map/ppermute | solution.py:405
  28.8 1.1 %collective-permute-done.11.refs_2_ = bf16[288,128]{1,0:T(8,128)(2,1)S(1)} collective-permute-done((bf16[288,128]{1,0:T(8,128)(2,1)S(1)}, bf16[288,128]{1,0:T(8,128)(2,1)S(1)}, u32[]{:S(2)}, u32[]{:S(2)}) %collective-permute-start.11) | collective-permute-done | bytes 73760 | tf_op jit(solution)/shard_map/ppermute | solution.py:405
  30.0 1.0 %collective-permute-start.12 = (bf16[288,128]{1,0:T(8,128)(2,1)S(1)}, bf16[288,128]{1,0:T(8,128)(2,1)S(1)}, u32[]{:S(2)}, u32[]{:S(2)}) collective-permute-start(bf16[288,128]{1,0:T(8,128)(2,1)S(1)} %shard_map.75.one_ref), channel_id=1, source_target_pairs={{0,4},{4,0},{8,12},{12,8},{1,5},{5,1},{9,13},{13,9},{2,6},{6,2},{1... | collective-permute-start | bytes 221192 | tf_op jit(solution)/shard_map/ppermute | solution.py:405
  31.0 3.5 %collective-permute-done.12.two_ref = bf16[288,128]{1,0:T(8,128)(2,1)S(1)} collective-permute-done((bf16[288,128]{1,0:T(8,128)(2,1)S(1)}, bf16[288,128]{1,0:T(8,128)(2,1)S(1)}, u32[]{:S(2)}, u32[]{:S(2)}) %collective-permute-start.12) | collective-permute-done | bytes 73760 | tf_op jit(solution)/shard_map/ppermute | solution.py:405
  34.5 2.0 %collective-permute-start.13 = (bf16[288,128]{1,0:T(8,128)(2,1)S(1)}, bf16[288,128]{1,0:T(8,128)(2,1)S(1)}, u32[]{:S(2)}, u32[]{:S(2)}) collective-permute-start(bf16[288,128]{1,0:T(8,128)(2,1)S(1)} %shard_map.76.one_ref), channel_id=1, source_target_pairs={{0,8},{4,12},{8,0},{12,4},{1,9},{5,13},{9,1},{13,5},{2,10},{6,14},... | collective-permute-start | bytes 221192 | tf_op jit(solution)/shard_map/ppermute | solution.py:405
  36.5 4.1 %collective-permute-done.13.two_ref = bf16[288,128]{1,0:T(8,128)(2,1)S(1)} collective-permute-done((bf16[288,128]{1,0:T(8,128)(2,1)S(1)}, bf16[288,128]{1,0:T(8,128)(2,1)S(1)}, u32[]{:S(2)}, u32[]{:S(2)}) %collective-permute-start.13) | collective-permute-done | bytes 73760 | tf_op jit(solution)/shard_map/ppermute | solution.py:405
  40.6 1.1 %collective-permute-start.14 = (bf16[288,128]{1,0:T(8,128)(2,1)S(1)}, bf16[288,128]{1,0:T(8,128)(2,1)S(1)}, u32[]{:S(2)}, u32[]{:S(2)}) collective-permute-start(bf16[288,128]{1,0:T(8,128)(2,1)S(1)} %shard_map.77.own_ref), channel_id=1, source_target_pairs={{0,2},{2,0},{1,3},{3,1},{4,6},{6,4},{5,7},{7,5},{8,10},{10,8},{9,1... | collective-permute-start | bytes 221192 | tf_op jit(solution)/shard_map/ppermute | solution.py:405
  41.7 3.4 %collective-permute-done.14.got_ref = bf16[288,128]{1,0:T(8,128)(2,1)S(1)} collective-permute-done((bf16[288,128]{1,0:T(8,128)(2,1)S(1)}, bf16[288,128]{1,0:T(8,128)(2,1)S(1)}, u32[]{:S(2)}, u32[]{:S(2)}) %collective-permute-start.14) | collective-permute-done | bytes 73760 | tf_op jit(solution)/shard_map/ppermute | solution.py:405
  45.1 1.4 %collective-permute-done.15.got_ref = bf16[2,288,128]{2,1,0:T(8,128)(2,1)S(1)} collective-permute-done((bf16[2,288,128]{2,1,0:T(8,128)(2,1)S(1)}, bf16[2,288,128]{2,1,0:T(8,128)(2,1)S(1)}, u32[]{:S(2)}, u32[]{:S(2)}) %collective-permute-start.15) | collective-permute-done | bytes 147488 | tf_op jit(solution)/shard_map/ppermute | solution.py:405
  46.5 1.2 %shard_map.79 = (f32[27,32,32]{2,1,0:T(8,128)}, f32[27,64,64]{2,1,0:T(8,128)}) custom-call(bf16[2,288,128]{2,1,0:T(8,128)(2,1)S(1)} %shard_map.78.own_ref, bf16[2,288,128]{2,1,0:T(8,128)(2,1)S(1)} %collective-permute-done.15.got_ref), custom_call_target="tpu_custom_call" | custom-call | bytes 847872 | tf_op jit(solution)/shard_map/pallas_call | solution.py:18
  (31 shorter events, 4.7 us)
Async XLA Ops:
  0.6 10.1 %collective-permute-start.1 = (bf16[32,2,8,128]{3,2,1,0:T(8,128)(2,1)}, bf16[32,2,8,128]{3,2,1,0:T(8,128)(2,1)S(1)}, u32[]{:S(2)}, u32[]{:S(2)}) collective-permute-start(bf16[32,2,8,128]{3,2,1,0:T(8,128)(2,1)} %bitcast.5), channel_id=1, source_target_pairs={{0,16},{4,8},{8,4},{12,28},{16,0},{20,24},{24,20},{28,12},{1,17},{... | collective-permute-start | bytes 393224 | tf_op jit(solution)/shard_map/ppermute | solution.py:397
  3.6 7.1 %collective-permute-start = (bf16[32,2,8,128]{3,2,1,0:T(8,128)(2,1)}, bf16[32,2,8,128]{3,2,1,0:T(8,128)(2,1)S(1)}, u32[]{:S(2)}, u32[]{:S(2)}) collective-permute-start(bf16[32,2,8,128]{3,2,1,0:T(8,128)(2,1)} %bitcast.6), channel_id=1, source_target_pairs={{0,4},{4,0},{8,12},{12,8},{16,20},{20,16},{24,28},{28,24},{1,5},{5... | collective-permute-start | bytes 393224 | tf_op jit(solution)/shard_map/ppermute | solution.py:397
  5.3 1.0 %copy-start.1 = (bf16[1,128,2,8,128]{4,3,2,1,0:T(8,128)(2,1)S(1)}, bf16[1,128,2,8,128]{4,3,2,1,0:T(8,128)(2,1)}, u32[]{:S(2)}) copy-start(bf16[1,128,2,8,128]{4,3,2,1,0:T(8,128)(2,1)} %param.7) | copy-start | bytes 1572868
  6.3 1.0 %copy-start.2 = (bf16[27,128,64]{1,2,0:T(8,128)(2,1)S(1)}, bf16[27,128,64]{1,2,0:T(8,128)(2,1)}, u32[]{:S(2)}) copy-start(bf16[27,128,64]{1,2,0:T(8,128)(2,1)} %param.6) | copy-start | bytes 1327108
  7.4 3.4 %copy-start = (bf16[1,32,2,8,128]{4,3,2,1,0:T(8,128)(2,1)S(1)}, bf16[1,32,2,8,128]{4,3,2,1,0:T(8,128)(2,1)}, u32[]{:S(2)}) copy-start(bf16[1,32,2,8,128]{4,3,2,1,0:T(8,128)(2,1)} %param.4) | copy-start | bytes 393220
  7.4 4.7 %copy-start.3 = (bf16[27,128,64]{1,2,0:T(8,128)(2,1)S(1)}, bf16[27,128,64]{1,2,0:T(8,128)(2,1)}, u32[]{:S(2)}) copy-start(bf16[27,128,64]{1,2,0:T(8,128)(2,1)} %param.6) | copy-start | bytes 1327108
  7.4 4.7 %copy-start.4 = (bf16[27,64,32]{1,2,0:T(8,128)(2,1)S(1)}, bf16[27,64,32]{1,2,0:T(8,128)(2,1)}, u32[]{:S(2)}) copy-start(bf16[27,64,32]{1,2,0:T(8,128)(2,1)} %param.5) | copy-start | bytes 331780
  9.1 5.4 %collective-permute-start.4 = (bf16[64,1280]{1,0:T(8,128)(2,1)S(1)}, bf16[64,1280]{1,0:T(8,128)(2,1)S(1)}, u32[]{:S(2)}, u32[]{:S(2)}) collective-permute-start(bf16[64,1280]{1,0:T(8,128)(2,1)S(1)} %get-tuple-element.37), channel_id=1, source_target_pairs={{0,4},{4,0},{8,12},{12,8},{16,20},{20,16},{24,28},{28,24},{1,5},{5... | collective-permute-start | bytes 491528 | tf_op jit(solution)/shard_map/ppermute | solution.py:397
  9.5 5.3 %collective-permute-start.5 = (bf16[64,1280]{1,0:T(8,128)(2,1)S(1)}, bf16[64,1280]{1,0:T(8,128)(2,1)S(1)}, u32[]{:S(2)}, u32[]{:S(2)}) collective-permute-start(bf16[64,1280]{1,0:T(8,128)(2,1)S(1)} %get-tuple-element.38), channel_id=1, source_target_pairs={{0,16},{4,8},{8,4},{12,28},{16,0},{20,24},{24,20},{28,12},{1,17},{... | collective-permute-start | bytes 491528 | tf_op jit(solution)/shard_map/ppermute | solution.py:397
  11.1 5.2 %collective-permute-start.2 = (bf16[6,32,256]{2,1,0:T(8,128)(2,1)S(1)}, bf16[6,32,256]{2,1,0:T(8,128)(2,1)S(1)}, u32[]{:S(2)}, u32[]{:S(2)}) collective-permute-start(bf16[6,32,256]{2,1,0:T(8,128)(2,1)S(1)} %get-tuple-element.32), channel_id=1, source_target_pairs={{0,1},{1,0},{2,3},{3,2},{16,17},{17,16},{18,19},{19,18},{4,5},{5,4... | collective-permute-start | bytes 294920 | tf_op jit(solution)/shard_map/ppermute | solution.py:397
  11.2 5.1 %collective-permute-start.3 = (bf16[6,32,256]{2,1,0:T(8,128)(2,1)S(1)}, bf16[6,32,256]{2,1,0:T(8,128)(2,1)S(1)}, u32[]{:S(2)}, u32[]{:S(2)}) collective-permute-start(bf16[6,32,256]{2,1,0:T(8,128)(2,1)S(1)} %get-tuple-element.33), channel_id=1, source_target_pairs={{0,16},{1,2},{2,1},{3,19},{16,0},{17,18},{18,17},{19,3},{4,20},{5,... | collective-permute-start | bytes 294920 | tf_op jit(solution)/shard_map/ppermute | solution.py:397
  14.9 3.9 %collective-permute-start.6 = (bf16[2,64,128]{2,1,0:T(8,128)(2,1)S(1)}, bf16[2,64,128]{2,1,0:T(8,128)(2,1)S(1)}, u32[]{:S(2)}, u32[]{:S(2)}) collective-permute-start(bf16[2,64,128]{2,1,0:T(8,128)(2,1)S(1)} %get-tuple-element.44), channel_id=1, source_target_pairs={{0,1},{1,0},{2,3},{3,2},{16,17},{17,16},{18,19},{19,18},{4,5},{5,4... | collective-permute-start | bytes 98312 | tf_op jit(solution)/shard_map/ppermute | solution.py:397
  15.0 4.0 %collective-permute-start.7 = (bf16[2,64,128]{2,1,0:T(8,128)(2,1)S(1)}, bf16[2,64,128]{2,1,0:T(8,128)(2,1)S(1)}, u32[]{:S(2)}, u32[]{:S(2)}) collective-permute-start(bf16[2,64,128]{2,1,0:T(8,128)(2,1)S(1)} %get-tuple-element.45), channel_id=1, source_target_pairs={{0,16},{1,2},{2,1},{3,19},{16,0},{17,18},{18,17},{19,3},{4,20},{5,... | collective-permute-start | bytes 98312 | tf_op jit(solution)/shard_map/ppermute | solution.py:397
  19.8 2.0 %collective-permute-start.8 = (bf16[2,2,288,128]{3,2,1,0:T(8,128)(2,1)S(1)}, bf16[2,2,288,128]{3,2,1,0:T(8,128)(2,1)S(1)}, u32[]{:S(2)}, u32[]{:S(2)}) collective-permute-start(bf16[2,2,288,128]{3,2,1,0:T(8,128)(2,1)S(1)} %get-tuple-element.49), channel_id=1, source_target_pairs={{0,1},{1,0},{2,3},{3,2},{4,5},{5,4},{6,7},{7,6},{8,9},{9,8},{10,11... | collective-permute-start | bytes 884744 | tf_op jit(solution)/shard_map/ppermute | solution.py:405
  21.9 6.0 %collective-permute-start.9 = (bf16[288,128]{1,0:T(8,128)(2,1)S(1)}, bf16[288,128]{1,0:T(8,128)(2,1)S(1)}, u32[]{:S(2)}, u32[]{:S(2)}) collective-permute-start(bf16[288,128]{1,0:T(8,128)(2,1)S(1)} %get-tuple-element.51), channel_id=1, source_target_pairs={{0,16},{2,18},{16,0},{18,2},{1,17},{3,19},{17,1},{19,3},{4,20},{6,... | collective-permute-start | bytes 221192 | tf_op jit(solution)/shard_map/ppermute | solution.py:405
  23.7 5.1 %collective-permute-start.10 = (bf16[288,128]{1,0:T(8,128)(2,1)S(1)}, bf16[288,128]{1,0:T(8,128)(2,1)S(1)}, u32[]{:S(2)}, u32[]{:S(2)}) collective-permute-start(bf16[288,128]{1,0:T(8,128)(2,1)S(1)} %get-tuple-element.52), channel_id=1, source_target_pairs={{0,2},{2,0},{16,18},{18,16},{1,3},{3,1},{17,19},{19,17},{4,6},{6,4... | collective-permute-start | bytes 221192 | tf_op jit(solution)/shard_map/ppermute | solution.py:405
  24.7 5.3 %collective-permute-start.11 = (bf16[288,128]{1,0:T(8,128)(2,1)S(1)}, bf16[288,128]{1,0:T(8,128)(2,1)S(1)}, u32[]{:S(2)}, u32[]{:S(2)}) collective-permute-start(bf16[288,128]{1,0:T(8,128)(2,1)S(1)} %get-tuple-element.53), channel_id=1, source_target_pairs={{0,18},{2,16},{16,2},{18,0},{1,19},{3,17},{17,3},{19,1},{4,22},{6,... | collective-permute-start | bytes 221192 | tf_op jit(solution)/shard_map/ppermute | solution.py:405
  30.0 4.4 %collective-permute-start.12 = (bf16[288,128]{1,0:T(8,128)(2,1)S(1)}, bf16[288,128]{1,0:T(8,128)(2,1)S(1)}, u32[]{:S(2)}, u32[]{:S(2)}) collective-permute-start(bf16[288,128]{1,0:T(8,128)(2,1)S(1)} %shard_map.75.one_ref), channel_id=1, source_target_pairs={{0,4},{4,0},{8,12},{12,8},{1,5},{5,1},{9,13},{13,9},{2,6},{6,2},{1... | collective-permute-start | bytes 221192 | tf_op jit(solution)/shard_map/ppermute | solution.py:405
  34.5 6.1 %collective-permute-start.13 = (bf16[288,128]{1,0:T(8,128)(2,1)S(1)}, bf16[288,128]{1,0:T(8,128)(2,1)S(1)}, u32[]{:S(2)}, u32[]{:S(2)}) collective-permute-start(bf16[288,128]{1,0:T(8,128)(2,1)S(1)} %shard_map.76.one_ref), channel_id=1, source_target_pairs={{0,8},{4,12},{8,0},{12,4},{1,9},{5,13},{9,1},{13,5},{2,10},{6,14},... | collective-permute-start | bytes 221192 | tf_op jit(solution)/shard_map/ppermute | solution.py:405
  40.6 4.4 %collective-permute-start.14 = (bf16[288,128]{1,0:T(8,128)(2,1)S(1)}, bf16[288,128]{1,0:T(8,128)(2,1)S(1)}, u32[]{:S(2)}, u32[]{:S(2)}) collective-permute-start(bf16[288,128]{1,0:T(8,128)(2,1)S(1)} %shard_map.77.own_ref), channel_id=1, source_target_pairs={{0,2},{2,0},{1,3},{3,1},{4,6},{6,4},{5,7},{7,5},{8,10},{10,8},{9,1... | collective-permute-start | bytes 221192 | tf_op jit(solution)/shard_map/ppermute | solution.py:405
  45.1 1.4 %collective-permute-start.15 = (bf16[2,288,128]{2,1,0:T(8,128)(2,1)S(1)}, bf16[2,288,128]{2,1,0:T(8,128)(2,1)S(1)}, u32[]{:S(2)}, u32[]{:S(2)}) collective-permute-start(bf16[2,288,128]{2,1,0:T(8,128)(2,1)S(1)} %shard_map.78.own_ref), channel_id=1, source_target_pairs={{0,1},{1,0},{2,3},{3,2},{4,5},{5,4},{6,7},{7,6},{8,9},{9,8},{10,11... | collective-permute-start | bytes 442376 | tf_op jit(solution)/shard_map/ppermute | solution.py:405

commit v6 on v5

--- a/solution.py
+++ b/solution.py
@@ -55,7 +55,11 @@
     return lax.rem(lax.axis_index(axis), 2) == 1
 
 
-def spread_kernel(cot_ref, k2_ref, cot_rows_ref, back_ref, one_ref, two_ref, scratch):
+def blank_kernel(out_ref):
+    out_ref[...] = jnp.zeros(out_ref.shape, BF)
+
+
+def spread_kernel(cot_ref, k2_ref, blank_ref, cot_rows_ref, back_ref, one_ref, two_ref, scratch):
     out, depth, height, _ = cot_ref.shape
     rows = [[None] * height for _ in range(depth)]
 
@@ -65,7 +69,7 @@
 
     by_rows(cot_ref, scratch, store)
     mid = k2_ref.shape[1]
-    none = jnp.zeros((out, 2 * LANES), BF)
+    none = blank_ref[...]
     padded = [jnp.concatenate([none, *rows[d], none], axis=1) for d in range(depth)]
     is_odd = odd("dep")
     faces = [[], []]
@@ -159,7 +163,40 @@
     return [jnp.concatenate([left[d], deep_ref[d], right[d]], axis=1) for d in range(deep_ref.shape[0])]
 
 
-def hidden_kernel(deep_ref, one_ref, two_ref, w1_ref, moved_ref, _, hidden_ref, slope_ref, g2_ref, rows_ref):
+def pack(direct, blocks, size, refs):
+    if not direct:
+        for j, block in enumerate(blocks):
+            refs[0][j] = block
+        return
+    keep_ref, send_ref = refs
+    parts, halves, length, _ = keep_ref.shape
+    fold = blocks[0].shape[0] // (parts * size)
+    core = lax.axis_index("core") == 1
+
+    def quarter(part, number):
+        values, row = [], number * length
+        while row < (number + 1) * length:
+            unit, start = divmod(row, size)
+            if unit < fold * len(blocks):
+                stop = min(size, start + (number + 1) * length - row)
+                first = (fold * part + unit % fold) * size
+                values.append(blocks[unit // fold][first + start : first + stop])
+                row += stop - start
+            else:
+                values.append(jnp.zeros(((number + 1) * length - row, LANES), F32))
+                row = (number + 1) * length
+        return jnp.concatenate(values, axis=0)
+
+    for part in range(parts):
+        for half in range(halves):
+            one, two = (quarter(part, 2 * half + c) for c in range(2))
+            keep_ref[part, half] = jnp.where(core, two, one)
+            send_ref[part, half] = jnp.where(core, one, two).astype(BF)
+
+
+def hidden_kernel(
+    direct, deep_ref, one_ref, two_ref, w1_ref, moved_ref, _, hidden_ref, slope_ref, rows_ref, *grad_refs
+):
     for d, row in enumerate(widened(deep_ref, one_ref, two_ref)):
         rows_ref[d] = row
     rows = rows_ref
@@ -199,7 +236,7 @@
     own = depth - 2
     out = moved_ref.shape[1] // 3
     left = jnp.concatenate([moved_ref[d] for d in range(own)], axis=1)
-    tails = []
+    blocks, tails = [None] * 12, []
     for first in (0, 4, 8):
         group = range(first, min(first + 4, 9))
         right = jnp.concatenate(
@@ -216,12 +253,12 @@
             part = g[n * out : (n + 1) * out]
             if first < 8:
                 for m in range(2):
-                    g2_ref[4 * n + first // 2 + m] = part[:, m * LANES : (m + 1) * LANES]
+                    blocks[4 * n + first // 2 + m] = part[:, m * LANES : (m + 1) * LANES]
             else:
                 tails.append(part)
     tails.append(jnp.zeros_like(tails[0]))
-    for m in range(2):
-        g2_ref[12 + m] = jnp.concatenate(tails[2 * m : 2 * m + 2], axis=1)
+    blocks += [jnp.concatenate(tails[2 * m : 2 * m + 2], axis=1) for m in range(2)]
+    pack(direct, blocks, mid // lax.axis_size("dp"), grad_refs)
 
 
 def features_kernel(hidden_ref, w2_ref, out_ref, token_ref, scratch):
@@ -247,8 +284,8 @@
     token_ref[...] = scratch[:8]
 
 
-def delta_kernel(direct, rows_ref, back_ref, one_ref, two_ref, slope_ref, g2_ref, *outs_and_scratch):
-    *out_refs, delta_ref = outs_and_scratch
+def delta_kernel(direct, rows_ref, back_ref, one_ref, two_ref, slope_ref, *outs_and_scratch):
+    *grad_refs, delta_ref = outs_and_scratch
     before, after = sides(HGT, one_ref[...], two_ref[...])
     own, mid, cells = slope_ref.shape
     for d in range(own):
@@ -291,76 +328,66 @@
                 tails.append(part)
     tails.append(jnp.zeros((mid, LANES - 3 * inner), F32))
     blocks.append(jnp.concatenate(tails, axis=1))
-    if not direct:
-        for j, block in enumerate(blocks):
-            out_refs[0][j] = block
-        return
-    keep_ref, send_ref = out_refs
-    parts, halves, length, _ = keep_ref.shape
-    size = mid // parts
-    core = lax.axis_index("core") == 1
-
-    def piece(part, number):
-        values, row = [], number * length
-        while row < (number + 1) * length:
-            unit, start = divmod(row, size)
-            stop = min(size, start + (number + 1) * length - row)
-            if unit < 28:
-                first = (2 * part + unit % 2) * size
-                values.append(g2_ref[unit // 2, first + start : first + stop, :])
-            elif unit < 35:
-                values.append(blocks[unit - 28][part * size + start : part * size + stop])
-            else:
-                values.append(jnp.zeros((stop - start, LANES), F32))
-            row += stop - start
-        return jnp.concatenate(values, axis=0)
-
-    for part in range(parts):
-        for half in range(halves):
-            one, two = (piece(part, 2 * half + c) for c in range(2))
-            keep_ref[part, half] = jnp.where(core, two, one)
-            send_ref[part, half] = jnp.where(core, one, two).astype(BF)
-
-
-def plane_kernel(moves, keep_ref, got_ref, kept_ref, *send_refs):
-    part = lax.rem(lax.axis_index("dp"), keep_ref.shape[0])
+    pack(direct, blocks, mid // lax.axis_size("dp"), grad_refs)
+
+
+def plane_kernel(moves, *refs):
+    keep_second, got_second, keep_first, got_first, kept_ref, *send_refs = refs
+    part = lax.rem(lax.axis_index("dp"), keep_first.shape[0])
     half = lax.axis_index("y")
-    kept_ref[...] = keep_ref[part, half] + got_ref[part, half].astype(F32)
-    for (x, y), send_ref in zip(moves, send_refs, strict=True):
+
+    def total(x, y):
         p = 1 - part if x else part
         h = 1 - half if y else half
-        send_ref[...] = (keep_ref[p, h] + got_ref[p, h].astype(F32)).astype(BF)
-
-
-def total_kernel(kept_ref, *refs):
-    *got_refs, _, out_ref = refs
-    value = kept_ref[...]
-    for ref in got_refs:
-        value = value + ref[...].astype(F32)
-    out_ref[...] = value.astype(BF)
+        second = keep_second[p, h] + got_second[p, h].astype(F32)
+        first = keep_first[p, h] + got_first[p, h].astype(F32)
+        return jnp.concatenate([second, first], axis=0).reshape(kept_ref.shape)
+
+    kept_ref[...] = total(0, 0)
+    for (x, y), send_ref in zip(moves, send_refs, strict=True):
+        send_ref[...] = total(x, y).astype(BF)
+
+
+def depth_kernel(kept_ref, *refs):
+    *got_refs, _, own_ref, send_ref = refs
+    mine = lax.rem(lax.axis_index("dep"), 2)
+
+    def total(at):
+        value = kept_ref[at]
+        for ref in got_refs:
+            value = value + ref[at].astype(F32)
+        return value
+
+    own_ref[...] = total(mine)
+    send_ref[...] = total(1 - mine).astype(BF)
 
 
 def add_kernel(one_ref, two_ref, out_ref):
     out_ref[...] = (one_ref[...].astype(F32) + two_ref[...].astype(F32)).astype(BF)
 
 
-def order_kernel(own_ref, got_ref, out_ref):
-    mine = lax.axis_index("y")
-    out_ref[mine] = own_ref[...]
-    out_ref[1 - mine] = got_ref[...]
-
-
-def unpack_kernel(own_ref, got_ref, g1_ref, g2_ref):
-    pieces, length, _ = own_ref.shape
+def order_kernel(own_ref, depth_ref, height_ref, both_ref, out_ref):
+    y, z = lax.axis_index("y"), lax.rem(lax.axis_index("dep"), 2)
+    out_ref[y, z] = own_ref[...]
+    out_ref[y, 1 - z] = depth_ref[...]
+    out_ref[1 - y, z] = height_ref[...]
+    out_ref[1 - y, 1 - z] = both_ref[...]
+
+
+def unpack_kernel(length_second, own_ref, got_ref, g1_ref, g2_ref):
+    halves, _, half, _ = own_ref.shape
     size, inner = g1_ref.shape[1:]
     mid = g2_ref.shape[2]
     core = lax.axis_index("core") == 1
-    whole = []
-    for n in range(pieces):
-        own, got = own_ref[n].astype(F32), got_ref[n].astype(F32)
-        whole += [jnp.where(core, got, own), jnp.where(core, own, got)]
-
-    def get(unit):
+    quarters = []
+    for n in range(halves):
+        own, got = (ref[n].astype(F32).reshape(2 * half, LANES) for ref in (own_ref, got_ref))
+        quarters += [jnp.where(core, got, own), jnp.where(core, own, got)]
+    second = [quarter[:length_second] for quarter in quarters]
+    first = [quarter[length_second:] for quarter in quarters]
+
+    def get(unit, whole=second):
+        length = whole[0].shape[0]
         values, row = [], unit * size
         while row < (unit + 1) * size:
             number, start = divmod(row, length)
@@ -377,7 +404,7 @@
                 if c < 3:
                     g2_ref[3 * ab + c, half * size : (half + 1) * size, :] = value[:, m * mid : (m + 1) * mid]
     for j in range(7):
-        value = get(28 + j)
+        value = get(j, first)
         for m in range(4):
             c, ab = (j // 2, 4 * (j % 2) + m) if j < 6 else (m, 8)
             if c < 3:
@@ -405,6 +432,15 @@
     return lax.ppermute(x, axes, [(i, i ^ flip) for i in range(lax.axis_size(axes))])
 
 
+def scattered(grad, parts, halves, size, length):
+    grad = jnp.swapaxes(grad.reshape(grad.shape[0], parts, -1, LANES), 0, 1).reshape(parts, -1, LANES)
+    grad = jnp.pad(grad, ((0, 0), (0, 2 * halves * length - grad.shape[1]), (0, 0)))
+    grad = lax.psum_scatter(grad, "dp", scatter_dimension=0, tiled=True).reshape(1, halves, 2, length, LANES)
+    core = lax.axis_index("core")
+    keep, send = (lax.dynamic_index_in_dim(grad, at, 2, False) for at in (core, 1 - core))
+    return keep, send.astype(BF)
+
+
 def per_device(volume, kernel_first, kernel_second, cotangent):
     _, inner, depth, height, width = volume.shape
     mid, out = kernel_first.shape[1], kernel_second.shape[1]
@@ -414,6 +450,7 @@
     rows = depth * height
 
     one, two = swapped(volume[0], "dep", 0), swapped(volume[0], "dep", 1)
+    (blank,) = call(blank_kernel, [shape((out, 2 * width), BF)], [], flops=3_000_000_000)
     cot_rows, back, back_one, back_two = call(
         spread_kernel,
         [
@@ -422,7 +459,7 @@
             shape((mid, cells + 2 * width), BF),
             shape((mid, cells + 2 * width), BF),
         ],
-        [cotangent[0], k2],
+        [cotangent[0], k2, blank],
         [pltpu.VMEM((out * rows, width), F32)],
         flops=1_100_000_000,
     )
@@ -447,43 +484,44 @@
     )
     back_one, back_two = swapped(back_one, HGT, 0), swapped(back_two, HGT, 1)
 
-    hidden, slope, g2, wide = call(
-        hidden_kernel,
+    size = mid // parts
+    direct = parts == 2 and size % 16 == 0
+    halves = lax.axis_size("y")
+    length_second, length_first = (-(-units * size // (32 * halves)) * 16 for units in (28, 7))
+    length = length_second + length_first
+    hidden, slope, wide, *second = call(
+        functools.partial(hidden_kernel, direct),
         [
             shape((depth + 2, mid, cells + 2 * width), BF),
             shape((depth, mid, cells), F32),
-            shape((14, out, LANES), F32),
             shape((3 * depth, inner, cells + 4 * width), BF),
-        ],
+        ]
+        + (
+            [shape((parts, halves, length_second, width), kind) for kind in (F32, BF)]
+            if direct
+            else [shape((14, out, LANES), F32)]
+        ),
         [deep, one, two, w1, moved, back],
         flops=1_500_000_000,
     )
-    size = mid // parts
-    direct = parts == 2 and size % 16 == 0
-    halves = lax.axis_size("y")
-    length = -(-35 * size // (32 * halves)) * 16
-    packed = (parts, halves, length, width)
-    grads = call(
+    first = call(
         functools.partial(delta_kernel, direct),
-        [shape(packed, F32), shape(packed, BF)] if direct else [shape((7, mid, LANES), F32)],
-        [wide, back, back_one, back_two, slope, g2],
+        [shape((parts, halves, length_first, width), kind) for kind in (F32, BF)]
+        if direct
+        else [shape((7, mid, LANES), F32)],
+        [wide, back, back_one, back_two, slope],
         [pltpu.VMEM((3 * mid, depth * cells), BF)],
-        flops=300_000_000,
+        flops=4_000_000_000,
     )
     if direct:
-        keep, send = grads
         moves = [(1, 0), (0, 1), (1, 1)]
     else:
-        grad = jnp.swapaxes(grads[0].reshape(7, parts, size, LANES), 0, 1)
-        grad2 = jnp.swapaxes(g2.reshape(14, parts, 2, size, LANES), 0, 1).reshape(parts, 28, size, LANES)
-        grad = jnp.concatenate([grad2, grad], axis=1).reshape(parts, 35 * size, LANES)
-        grad = jnp.pad(grad, ((0, 0), (0, 2 * halves * length - 35 * size), (0, 0)))
-        grad = lax.psum_scatter(grad, "dp", scatter_dimension=0, tiled=True)
-        grad = grad.reshape(1, halves, 2, length, LANES)
-        core = lax.axis_index("core")
-        keep = lax.dynamic_index_in_dim(grad, core, 2, False)
-        send = lax.dynamic_index_in_dim(grad, 1 - core, 2, False).astype(BF)
         moves = [(0, 1)]
+        first, second = (
+            scattered(grad[0], parts, halves, size, rows)
+            for grad, rows in ((first, length_first), (second, length_second))
+        )
+    got_second, got_first = (across(send, ("core", 1)) for _, send in (second, first))
     features, token = call(
         features_kernel,
         [shape(cotangent.shape[1:], BF), shape((8, width), F32)],
@@ -491,18 +529,23 @@
         [pltpu.VMEM((out * rows, width), F32)],
         flops=900_000_000,
     )
+    block = (2, length // 2, width)
     kept, *sends = call(
         functools.partial(plane_kernel, moves),
-        [shape((length, width), F32)] + [shape((length, width), BF)] * len(moves),
-        [keep, across(send, ("core", 1))],
+        [shape(block, F32)] + [shape(block, BF)] * len(moves),
+        [second[0], got_second, first[0], got_first],
     )
     gots = [across(send, ("dp", x), ("y", y)) for send, (x, y) in zip(sends, moves, strict=True)]
-    (share,) = call(total_kernel, [shape((length, width), BF)], [kept, *gots, token])
-    for bit in (1, 2):
-        (share,) = call(add_kernel, [shape((length, width), BF)], [share, across(share, ("dep", bit))])
-    (own,) = call(order_kernel, [shape((halves, length, width), BF)], [share, across(share, ("y", 1))])
+    own, send = call(depth_kernel, [shape(block[1:], F32), shape(block[1:], BF)], [kept, *gots, token])
+    (share,) = call(add_kernel, [shape(block[1:], BF)], [own, across(send, ("dep", 1))])
+    (share,) = call(add_kernel, [shape(block[1:], BF)], [share, across(share, ("dep", 2))])
+    (own,) = call(
+        order_kernel,
+        [shape((halves, *block), BF)],
+        [share, *(across(share, ("dep", z), ("y", y)) for z, y in ((1, 0), (0, 1), (1, 1)))],
+    )
     grad_first, grad_second = call(
-        unpack_kernel,
+        functools.partial(unpack_kernel, length_second),
         [shape((27, size, inner), F32), shape((27, 2 * size, mid), F32)],
         [own, across(own, ("core", 1))],
     )

time: 47.9 us -> 46.9 us (0.979)
  starting transfers between devices: 17.2 us -> 21.5 us
  waiting for transfers between devices: 17.8 us -> 14.4 us
  local copies, waits for them, and re-layouts: 2.06 us -> 0.02 us
    ppermute x8 -> x11, starting transfers between devices: 8.51 us -> 12.2 us  [across(): lax.ppermute(x, axes, [(i, i ^ flip) for i in range(lax.axis_size(axes))])]
    ppermute x8 -> x11, waiting for transfers between devices: 15.6 us -> 12.9 us  [across(): lax.ppermute(x, axes, [(i, i ^ flip) for i in range(lax.axis_size(axes))])]
    unnamed x10 -> x8, local copies, waits for them, and re-layouts: 2.06 us -> 0.02 us
    ppermute x8, waiting for transfers between devices: 2.24 us -> 1.5 us  [swapped(): return lax.ppermute(x, ('dp', *axes), list(enumerate(partner)))]
    ppermute x8, starting transfers between devices: 8.66 us -> 9.31 us  [swapped(): return lax.ppermute(x, ('dp', *axes), list(enumerate(partner)))]
    pallas_call x13 -> x14, Pallas kernels: 9.93 us -> 10.1 us  [call(): pl.pallas_call(body, out_shape=outs, in_specs=[pl.BlockSpec(memory_space=...]
  transfers between devices with their start and end apart: 16 -> 19, of which waited for: 10 -> 12; matrix products, arithmetic and copies ran while one was open for 0% -> 0% of each run, Pallas kernels for 16% -> 19%
where the time goes in v6:
time: 46.9 us; the launch traced here: 46.7 us
  starting transfers between devices  21.5 us (46%)
  waiting for transfers between devices  14.4 us (31%)
  Pallas kernels  10.1 us (22%)
  between operations  0.77 us (2%)
    ppermute x11, waiting for transfers between devices, across(): lax.ppermute(x, axes, [(i, i ^ flip) for i in range(lax.axis_size(axes))])  12.9 us
    ppermute x11, starting transfers between devices, across(): lax.ppermute(x, axes, [(i, i ^ flip) for i in range(lax.axis_size(axes))])  12.2 us
    pallas_call x14, Pallas kernels, call(): pl.pallas_call(body, out_shape=outs, in_specs=[pl.BlockSpec(memory_space=...  10.1 us
    ppermute x8, starting transfers between devices, swapped(): return lax.ppermute(x, ('dp', *axes), list(enumerate(partner)))  9.31 us
    ppermute x8, waiting for transfers between devices, swapped(): return lax.ppermute(x, ('dp', *axes), list(enumerate(partner)))  1.5 us
  transfers between devices with their start and end apart: 19, of which 12 were waited for; matrix products, arithmetic and copies ran while one was open for 0% of the time, Pallas kernels for 19%

profile of v6, /device:TPU:0, one launch (start us, length us, event | category | flops | bytes accessed | tf_op | source)
XLA Modules:
  0.0 46.7 jit_solution(10202685499638313826)
XLA Ops:
  0.7 3.0 %collective-permute-start.1 = (bf16[32,2,8,128]{3,2,1,0:T(8,128)(2,1)}, bf16[32,2,8,128]{3,2,1,0:T(8,128)(2,1)S(1)}, u32[]{:S(2)}, u32[]{:S(2)}) collective-permute-start(bf16[32,2,8,128]{3,2,1,0:T(8,128)(2,1)} %bitcast.5), channel_id=1, source_target_pairs={{0,16},{4,8},{8,4},{12,28},{16,0},{20,24},{24,20},{28,12},{1,17},{... | collective-permute-start | bytes 393224 | tf_op jit(solution)/shard_map/ppermute | solution.py:424
  3.7 1.7 %collective-permute-start = (bf16[32,2,8,128]{3,2,1,0:T(8,128)(2,1)}, bf16[32,2,8,128]{3,2,1,0:T(8,128)(2,1)S(1)}, u32[]{:S(2)}, u32[]{:S(2)}) collective-permute-start(bf16[32,2,8,128]{3,2,1,0:T(8,128)(2,1)} %bitcast.6), channel_id=1, source_target_pairs={{0,4},{4,0},{8,12},{12,8},{16,20},{20,16},{24,28},{28,24},{1,5},{5... | collective-permute-start | bytes 393224 | tf_op jit(solution)/shard_map/ppermute | solution.py:424
  5.4 1.8 %shard_map.68 = (bf16[2,128,1024]{2,1,0:T(8,128)(2,1)S(1)}, f32[2,64,1280]{2,1,0:T(8,128)S(1)}, bf16[64,1280]{1,0:T(8,128)(2,1)S(1)}, bf16[64,1280]{1,0:T(8,128)(2,1)S(1)}) custom-call(bf16[128,2,8,128]{3,2,1,0:T(8,128)(2,1)S(1)} %bitcast.8, bf16[27,64,128]{2,1,0:T(8,128)(2,1)S(1)} %bitcast.9, bf16[128,256]{1,0:T(8,128)(2,1)S(1)} %shard_map.67.blank_ref), custom_call_target="tpu_custom_call" | custom-call | flops 1100000000 | bytes 2539520 | tf_op jit(solution)/shard_map/pallas_call | solution.py:18
  7.6 1.2 %collective-permute-start.5 = (bf16[64,1280]{1,0:T(8,128)(2,1)S(1)}, bf16[64,1280]{1,0:T(8,128)(2,1)S(1)}, u32[]{:S(2)}, u32[]{:S(2)}) collective-permute-start(bf16[64,1280]{1,0:T(8,128)(2,1)S(1)} %get-tuple-element.41), channel_id=1, source_target_pairs={{0,16},{4,8},{8,4},{12,28},{16,0},{20,24},{24,20},{28,12},{1,17},{... | collective-permute-start | bytes 491528 | tf_op jit(solution)/shard_map/ppermute | solution.py:424
  9.7 1.5 %collective-permute-start.3 = (bf16[6,32,256]{2,1,0:T(8,128)(2,1)S(1)}, bf16[6,32,256]{2,1,0:T(8,128)(2,1)S(1)}, u32[]{:S(2)}, u32[]{:S(2)}) collective-permute-start(bf16[6,32,256]{2,1,0:T(8,128)(2,1)S(1)} %get-tuple-element.36), channel_id=1, source_target_pairs={{0,16},{1,2},{2,1},{3,19},{16,0},{17,18},{18,17},{19,3},{4,20},{5,... | collective-permute-start | bytes 294920 | tf_op jit(solution)/shard_map/ppermute | solution.py:424
  11.9 0.7 %collective-permute-done.4.one_ref = bf16[64,1280]{1,0:T(8,128)(2,1)S(1)} collective-permute-done((bf16[64,1280]{1,0:T(8,128)(2,1)S(1)}, bf16[64,1280]{1,0:T(8,128)(2,1)S(1)}, u32[]{:S(2)}, u32[]{:S(2)}) %collective-permute-start.4) | collective-permute-done | bytes 163872 | tf_op jit(solution)/shard_map/ppermute | solution.py:424
  13.1 1.3 %collective-permute-start.8 = (bf16[2,64,128]{2,1,0:T(8,128)(2,1)S(1)}, bf16[2,64,128]{2,1,0:T(8,128)(2,1)S(1)}, u32[]{:S(2)}, u32[]{:S(2)}) collective-permute-start(bf16[2,64,128]{2,1,0:T(8,128)(2,1)S(1)} %get-tuple-element.50), channel_id=1, source_target_pairs={{0,16},{1,2},{2,1},{3,19},{16,0},{17,18},{18,17},{19,3},{4,20},{5,... | collective-permute-start | bytes 98312 | tf_op jit(solution)/shard_map/ppermute | solution.py:424
  14.4 2.6 %shard_map.72 = (bf16[4,64,1280]{2,1,0:T(8,128)(2,1)S(1)}, f32[2,64,1024]{2,1,0:T(8,128)S(1)}, bf16[6,32,1536]{2,1,0:T(8,128)(2,1)S(1)}, f32[2,2,224,128]{3,2,1,0:T(8,128)S(1)}, bf16[2,2,224,128]{3,2,1,0:T(8,128)(2,1)S(1)}) custom-call(bf16[6,32,1024]{2,1,0:T(8,128)(2,1)S(1)} %get-tuple-element.34._.deep_ref, ...), custom_call_target="tpu_custom_call" | custom-call | flops 1500000000 | bytes 5255168 | tf_op jit(solution)/shard_map/pallas_call | solution.py:18
  17.5 0.8 %shard_map.74 = (f32[2,2,64,128]{3,2,1,0:T(8,128)S(1)}, bf16[2,2,64,128]{3,2,1,0:T(8,128)(2,1)S(1)}) custom-call(bf16[6,32,1536]{2,1,0:T(8,128)(2,1)S(1)} %get-tuple-element.48.rows_ref, f32[2,64,1024]{2,1,0:T(8,128)S(1)} %get-tuple-element.42._.back_ref, bf16[2,64,128]{2,1,0:T(8,128)(2,1)S(1)} %collective-permute-done.7.one_ref, ...), custom_call_target="tpu_custom_call" | custom-call | flops 4000000000 | bytes 1900544 | tf_op jit(solution)/shard_map/pallas_call | solution.py:18
  18.5 1.1 %collective-permute-done.9.refs_3_ = bf16[2,2,64,128]{3,2,1,0:T(8,128)(2,1)S(1)} collective-permute-done((bf16[2,2,64,128]{3,2,1,0:T(8,128)(2,1)S(1)}, bf16[2,2,64,128]{3,2,1,0:T(8,128)(2,1)S(1)}, u32[]{:S(2)}, u32[]{:S(2)}) %collective-permute-start.9) | collective-permute-done | bytes 65568 | tf_op jit(solution)/shard_map/ppermute | solution.py:432
  19.6 1.3 %collective-permute-start.10 = (bf16[2,144,128]{2,1,0:T(8,128)(2,1)S(1)}, bf16[2,144,128]{2,1,0:T(8,128)(2,1)S(1)}, u32[]{:S(2)}, u32[]{:S(2)}) collective-permute-start(bf16[2,144,128]{2,1,0:T(8,128)(2,1)S(1)} %get-tuple-element.55), channel_id=1, source_target_pairs={{0,16},{2,18},{16,0},{18,2},{1,17},{3,19},{17,1},{19,3},{4,20},{6,... | collective-permute-start | bytes 221192 | tf_op jit(solution)/shard_map/ppermute | solution.py:432
  21.0 0.9 %collective-permute-start.11 = (bf16[2,144,128]{2,1,0:T(8,128)(2,1)S(1)}, bf16[2,144,128]{2,1,0:T(8,128)(2,1)S(1)}, u32[]{:S(2)}, u32[]{:S(2)}) collective-permute-start(bf16[2,144,128]{2,1,0:T(8,128)(2,1)S(1)} %get-tuple-element.56), channel_id=1, source_target_pairs={{0,2},{2,0},{16,18},{18,16},{1,3},{3,1},{17,19},{19,17},{4,6},{6,4... | collective-permute-start | bytes 221192 | tf_op jit(solution)/shard_map/ppermute | solution.py:432
  21.9 1.3 %collective-permute-start.12 = (bf16[2,144,128]{2,1,0:T(8,128)(2,1)S(1)}, bf16[2,144,128]{2,1,0:T(8,128)(2,1)S(1)}, u32[]{:S(2)}, u32[]{:S(2)}) collective-permute-start(bf16[2,144,128]{2,1,0:T(8,128)(2,1)S(1)} %get-tuple-element.57), channel_id=1, source_target_pairs={{0,18},{2,16},{16,2},{18,0},{1,19},{3,17},{17,3},{19,1},{4,22},{6,... | collective-permute-start | bytes 221192 | tf_op jit(solution)/shard_map/ppermute | solution.py:432
  23.2 2.5 %shard_map.73 = (bf16[128,2,8,128]{3,2,1,0:T(8,128)(2,1)}, f32[8,128]{1,0:T(8,128)S(1)}) custom-call(bf16[4,64,1280]{2,1,0:T(8,128)(2,1)S(1)} %get-tuple-element.43.hidden_ref, bf16[384,576]{1,0:T(8,128)(2,1)S(1)} %get-tuple-element.44.w2_ref), custom_call_target="tpu_custom_call" | custom-call | flops 900000000 | bytes 1626112 | tf_op jit(solution)/shard_map/pallas_call | solution.py:18
  26.1 1.1 %collective-permute-done.12.refs_2_ = bf16[2,144,128]{2,1,0:T(8,128)(2,1)S(1)} collective-permute-done((bf16[2,144,128]{2,1,0:T(8,128)(2,1)S(1)}, bf16[2,144,128]{2,1,0:T(8,128)(2,1)S(1)}, u32[]{:S(2)}, u32[]{:S(2)}) %collective-permute-start.12) | collective-permute-done | bytes 73760 | tf_op jit(solution)/shard_map/ppermute | solution.py:432
  27.2 2.4 %collective-permute-start.13 = (bf16[144,128]{1,0:T(8,128)(2,1)S(1)}, bf16[144,128]{1,0:T(8,128)(2,1)S(1)}, u32[]{:S(2)}, u32[]{:S(2)}) collective-permute-start(bf16[144,128]{1,0:T(8,128)(2,1)S(1)} %get-tuple-element.60), channel_id=1, source_target_pairs={{0,4},{4,0},{8,12},{12,8},{1,5},{5,1},{9,13},{13,9},{2,6},{6,2},{1... | collective-permute-start | bytes 110600 | tf_op jit(solution)/shard_map/ppermute | solution.py:432
  29.7 1.9 %collective-permute-done.13.two_ref = bf16[144,128]{1,0:T(8,128)(2,1)S(1)} collective-permute-done((bf16[144,128]{1,0:T(8,128)(2,1)S(1)}, bf16[144,128]{1,0:T(8,128)(2,1)S(1)}, u32[]{:S(2)}, u32[]{:S(2)}) %collective-permute-start.13) | collective-permute-done | bytes 36896 | tf_op jit(solution)/shard_map/ppermute | solution.py:432
  31.6 1.8 %collective-permute-start.14 = (bf16[144,128]{1,0:T(8,128)(2,1)S(1)}, bf16[144,128]{1,0:T(8,128)(2,1)S(1)}, u32[]{:S(2)}, u32[]{:S(2)}) collective-permute-start(bf16[144,128]{1,0:T(8,128)(2,1)S(1)} %shard_map.77.one_ref), channel_id=1, source_target_pairs={{0,8},{4,12},{8,0},{12,4},{1,9},{5,13},{9,1},{13,5},{2,10},{6,14},... | collective-permute-start | bytes 110600 | tf_op jit(solution)/shard_map/ppermute | solution.py:432
  33.4 3.1 %collective-permute-done.14.two_ref = bf16[144,128]{1,0:T(8,128)(2,1)S(1)} collective-permute-done((bf16[144,128]{1,0:T(8,128)(2,1)S(1)}, bf16[144,128]{1,0:T(8,128)(2,1)S(1)}, u32[]{:S(2)}, u32[]{:S(2)}) %collective-permute-start.14) | collective-permute-done | bytes 36896 | tf_op jit(solution)/shard_map/ppermute | solution.py:432
  36.6 3.0 %collective-permute-start.17 = (bf16[144,128]{1,0:T(8,128)(2,1)S(1)}, bf16[144,128]{1,0:T(8,128)(2,1)S(1)}, u32[]{:S(2)}, u32[]{:S(2)}) collective-permute-start(bf16[144,128]{1,0:T(8,128)(2,1)S(1)} %shard_map.78.own_ref), channel_id=1, source_target_pairs={{0,6},{2,4},{4,2},{6,0},{8,14},{10,12},{12,10},{14,8},{1,7},{3,5},... | collective-permute-start | bytes 110600 | tf_op jit(solution)/shard_map/ppermute | solution.py:432
  40.2 1.3 %collective-permute-done.17.both_ref = bf16[144,128]{1,0:T(8,128)(2,1)S(1)} collective-permute-done((bf16[144,128]{1,0:T(8,128)(2,1)S(1)}, bf16[144,128]{1,0:T(8,128)(2,1)S(1)}, u32[]{:S(2)}, u32[]{:S(2)}) %collective-permute-start.17) | collective-permute-done | bytes 36896 | tf_op jit(solution)/shard_map/ppermute | solution.py:432
  41.5 2.0 %collective-permute-done.16.height_ref = bf16[144,128]{1,0:T(8,128)(2,1)S(1)} collective-permute-done((bf16[144,128]{1,0:T(8,128)(2,1)S(1)}, bf16[144,128]{1,0:T(8,128)(2,1)S(1)}, u32[]{:S(2)}, u32[]{:S(2)}) %collective-permute-start.16) | collective-permute-done | bytes 36896 | tf_op jit(solution)/shard_map/ppermute | solution.py:432
  44.2 1.4 %collective-permute-done.18.got_ref = bf16[2,2,144,128]{3,2,1,0:T(8,128)(2,1)S(1)} collective-permute-done((bf16[2,2,144,128]{3,2,1,0:T(8,128)(2,1)S(1)}, bf16[2,2,144,128]{3,2,1,0:T(8,128)(2,1)S(1)}, u32[]{:S(2)}, u32[]{:S(2)}) %collective-permute-start.18) | collective-permute-done | bytes 147488 | tf_op jit(solution)/shard_map/ppermute | solution.py:432
  45.5 1.2 %shard_map.80 = (f32[27,32,32]{2,1,0:T(8,128)}, f32[27,64,64]{2,1,0:T(8,128)}) custom-call(bf16[2,2,144,128]{3,2,1,0:T(8,128)(2,1)S(1)} %shard_map.79.own_ref, bf16[2,2,144,128]{3,2,1,0:T(8,128)(2,1)S(1)} %collective-permute-done.18.got_ref), custom_call_target="tpu_custom_call" | custom-call | bytes 847872 | tf_op jit(solution)/shard_map/pallas_call | solution.py:18
  (36 shorter events, 5.0 us)
Async XLA Ops:
  0.6 4.7 %copy-start.1 = (bf16[1,128,2,8,128]{4,3,2,1,0:T(8,128)(2,1)S(1)}, bf16[1,128,2,8,128]{4,3,2,1,0:T(8,128)(2,1)}, u32[]{:S(2)}) copy-start(bf16[1,128,2,8,128]{4,3,2,1,0:T(8,128)(2,1)} %param.7) | copy-start | bytes 1572868
  0.6 4.7 %copy-start.2 = (bf16[27,128,64]{1,2,0:T(8,128)(2,1)S(1)}, bf16[27,128,64]{1,2,0:T(8,128)(2,1)}, u32[]{:S(2)}) copy-start(bf16[27,128,64]{1,2,0:T(8,128)(2,1)} %param.6) | copy-start | bytes 1327108
  0.7 8.1 %collective-permute-start.1 = (bf16[32,2,8,128]{3,2,1,0:T(8,128)(2,1)}, bf16[32,2,8,128]{3,2,1,0:T(8,128)(2,1)S(1)}, u32[]{:S(2)}, u32[]{:S(2)}) collective-permute-start(bf16[32,2,8,128]{3,2,1,0:T(8,128)(2,1)} %bitcast.5), channel_id=1, source_target_pairs={{0,16},{4,8},{8,4},{12,28},{16,0},{20,24},{24,20},{28,12},{1,17},{... | collective-permute-start | bytes 393224 | tf_op jit(solution)/shard_map/ppermute | solution.py:424
  3.7 5.6 %collective-permute-start = (bf16[32,2,8,128]{3,2,1,0:T(8,128)(2,1)}, bf16[32,2,8,128]{3,2,1,0:T(8,128)(2,1)S(1)}, u32[]{:S(2)}, u32[]{:S(2)}) collective-permute-start(bf16[32,2,8,128]{3,2,1,0:T(8,128)(2,1)} %bitcast.6), channel_id=1, source_target_pairs={{0,4},{4,0},{8,12},{12,8},{16,20},{20,16},{24,28},{28,24},{1,5},{5... | collective-permute-start | bytes 393224 | tf_op jit(solution)/shard_map/ppermute | solution.py:424
  5.3 3.9 %copy-start = (bf16[1,32,2,8,128]{4,3,2,1,0:T(8,128)(2,1)S(1)}, bf16[1,32,2,8,128]{4,3,2,1,0:T(8,128)(2,1)}, u32[]{:S(2)}) copy-start(bf16[1,32,2,8,128]{4,3,2,1,0:T(8,128)(2,1)} %param.4) | copy-start | bytes 393220
  5.3 5.9 %copy-start.3 = (bf16[27,64,32]{1,2,0:T(8,128)(2,1)S(1)}, bf16[27,64,32]{1,2,0:T(8,128)(2,1)}, u32[]{:S(2)}) copy-start(bf16[27,64,32]{1,2,0:T(8,128)(2,1)} %param.5) | copy-start | bytes 331780
  7.1 5.4 %collective-permute-start.4 = (bf16[64,1280]{1,0:T(8,128)(2,1)S(1)}, bf16[64,1280]{1,0:T(8,128)(2,1)S(1)}, u32[]{:S(2)}, u32[]{:S(2)}) collective-permute-start(bf16[64,1280]{1,0:T(8,128)(2,1)S(1)} %get-tuple-element.40), channel_id=1, source_target_pairs={{0,4},{4,0},{8,12},{12,8},{16,20},{20,16},{24,28},{28,24},{1,5},{5... | collective-permute-start | bytes 491528 | tf_op jit(solution)/shard_map/ppermute | solution.py:424
  7.6 5.3 %collective-permute-start.5 = (bf16[64,1280]{1,0:T(8,128)(2,1)S(1)}, bf16[64,1280]{1,0:T(8,128)(2,1)S(1)}, u32[]{:S(2)}, u32[]{:S(2)}) collective-permute-start(bf16[64,1280]{1,0:T(8,128)(2,1)S(1)} %get-tuple-element.41), channel_id=1, source_target_pairs={{0,16},{4,8},{8,4},{12,28},{16,0},{20,24},{24,20},{28,12},{1,17},{... | collective-permute-start | bytes 491528 | tf_op jit(solution)/shard_map/ppermute | solution.py:424
  9.7 4.7 %collective-permute-start.2 = (bf16[6,32,256]{2,1,0:T(8,128)(2,1)S(1)}, bf16[6,32,256]{2,1,0:T(8,128)(2,1)S(1)}, u32[]{:S(2)}, u32[]{:S(2)}) collective-permute-start(bf16[6,32,256]{2,1,0:T(8,128)(2,1)S(1)} %get-tuple-element.35), channel_id=1, source_target_pairs={{0,1},{1,0},{2,3},{3,2},{16,17},{17,16},{18,19},{19,18},{4,5},{5,4... | collective-permute-start | bytes 294920 | tf_op jit(solution)/shard_map/ppermute | solution.py:424
  9.7 4.7 %collective-permute-start.3 = (bf16[6,32,256]{2,1,0:T(8,128)(2,1)S(1)}, bf16[6,32,256]{2,1,0:T(8,128)(2,1)S(1)}, u32[]{:S(2)}, u32[]{:S(2)}) collective-permute-start(bf16[6,32,256]{2,1,0:T(8,128)(2,1)S(1)} %get-tuple-element.36), channel_id=1, source_target_pairs={{0,16},{1,2},{2,1},{3,19},{16,0},{17,18},{18,17},{19,3},{4,20},{5,... | collective-permute-start | bytes 294920 | tf_op jit(solution)/shard_map/ppermute | solution.py:424
  13.0 4.5 %collective-permute-start.7 = (bf16[2,64,128]{2,1,0:T(8,128)(2,1)S(1)}, bf16[2,64,128]{2,1,0:T(8,128)(2,1)S(1)}, u32[]{:S(2)}, u32[]{:S(2)}) collective-permute-start(bf16[2,64,128]{2,1,0:T(8,128)(2,1)S(1)} %get-tuple-element.49), channel_id=1, source_target_pairs={{0,1},{1,0},{2,3},{3,2},{16,17},{17,16},{18,19},{19,18},{4,5},{5,4... | collective-permute-start | bytes 98312 | tf_op jit(solution)/shard_map/ppermute | solution.py:424
  13.1 4.4 %collective-permute-start.8 = (bf16[2,64,128]{2,1,0:T(8,128)(2,1)S(1)}, bf16[2,64,128]{2,1,0:T(8,128)(2,1)S(1)}, u32[]{:S(2)}, u32[]{:S(2)}) collective-permute-start(bf16[2,64,128]{2,1,0:T(8,128)(2,1)S(1)} %get-tuple-element.50), channel_id=1, source_target_pairs={{0,16},{1,2},{2,1},{3,19},{16,0},{17,18},{18,17},{19,3},{4,20},{5,... | collective-permute-start | bytes 98312 | tf_op jit(solution)/shard_map/ppermute | solution.py:424
  17.0 2.5 %collective-permute-start.6 = (bf16[2,2,224,128]{3,2,1,0:T(8,128)(2,1)S(1)}, bf16[2,2,224,128]{3,2,1,0:T(8,128)(2,1)S(1)}, u32[]{:S(2)}, u32[]{:S(2)}) collective-permute-start(bf16[2,2,224,128]{3,2,1,0:T(8,128)(2,1)S(1)} %get-tuple-element.47), channel_id=1, source_target_pairs={{0,1},{1,0},{2,3},{3,2},{4,5},{5,4},{6,7},{7,6},{8,9},{9,8},{10,11... | collective-permute-start | bytes 688136 | tf_op jit(solution)/shard_map/ppermute | solution.py:432
  18.2 1.3 %collective-permute-start.9 = (bf16[2,2,64,128]{3,2,1,0:T(8,128)(2,1)S(1)}, bf16[2,2,64,128]{3,2,1,0:T(8,128)(2,1)S(1)}, u32[]{:S(2)}, u32[]{:S(2)}) collective-permute-start(bf16[2,2,64,128]{3,2,1,0:T(8,128)(2,1)S(1)} %get-tuple-element.53), channel_id=1, source_target_pairs={{0,1},{1,0},{2,3},{3,2},{4,5},{5,4},{6,7},{7,6},{8,9},{9,8},{10,11... | collective-permute-start | bytes 196616 | tf_op jit(solution)/shard_map/ppermute | solution.py:432
  19.6 6.0 %collective-permute-start.10 = (bf16[2,144,128]{2,1,0:T(8,128)(2,1)S(1)}, bf16[2,144,128]{2,1,0:T(8,128)(2,1)S(1)}, u32[]{:S(2)}, u32[]{:S(2)}) collective-permute-start(bf16[2,144,128]{2,1,0:T(8,128)(2,1)S(1)} %get-tuple-element.55), channel_id=1, source_target_pairs={{0,16},{2,18},{16,0},{18,2},{1,17},{3,19},{17,1},{19,3},{4,20},{6,... | collective-permute-start | bytes 221192 | tf_op jit(solution)/shard_map/ppermute | solution.py:432
  21.0 5.1 %collective-permute-start.11 = (bf16[2,144,128]{2,1,0:T(8,128)(2,1)S(1)}, bf16[2,144,128]{2,1,0:T(8,128)(2,1)S(1)}, u32[]{:S(2)}, u32[]{:S(2)}) collective-permute-start(bf16[2,144,128]{2,1,0:T(8,128)(2,1)S(1)} %get-tuple-element.56), channel_id=1, source_target_pairs={{0,2},{2,0},{16,18},{18,16},{1,3},{3,1},{17,19},{19,17},{4,6},{6,4... | collective-permute-start | bytes 221192 | tf_op jit(solution)/shard_map/ppermute | solution.py:432
  21.9 5.3 %collective-permute-start.12 = (bf16[2,144,128]{2,1,0:T(8,128)(2,1)S(1)}, bf16[2,144,128]{2,1,0:T(8,128)(2,1)S(1)}, u32[]{:S(2)}, u32[]{:S(2)}) collective-permute-start(bf16[2,144,128]{2,1,0:T(8,128)(2,1)S(1)} %get-tuple-element.57), channel_id=1, source_target_pairs={{0,18},{2,16},{16,2},{18,0},{1,19},{3,17},{17,3},{19,1},{4,22},{6,... | collective-permute-start | bytes 221192 | tf_op jit(solution)/shard_map/ppermute | solution.py:432
  27.2 4.4 %collective-permute-start.13 = (bf16[144,128]{1,0:T(8,128)(2,1)S(1)}, bf16[144,128]{1,0:T(8,128)(2,1)S(1)}, u32[]{:S(2)}, u32[]{:S(2)}) collective-permute-start(bf16[144,128]{1,0:T(8,128)(2,1)S(1)} %get-tuple-element.60), channel_id=1, source_target_pairs={{0,4},{4,0},{8,12},{12,8},{1,5},{5,1},{9,13},{13,9},{2,6},{6,2},{1... | collective-permute-start | bytes 110600 | tf_op jit(solution)/shard_map/ppermute | solution.py:432
  31.6 4.9 %collective-permute-start.14 = (bf16[144,128]{1,0:T(8,128)(2,1)S(1)}, bf16[144,128]{1,0:T(8,128)(2,1)S(1)}, u32[]{:S(2)}, u32[]{:S(2)}) collective-permute-start(bf16[144,128]{1,0:T(8,128)(2,1)S(1)} %shard_map.77.one_ref), channel_id=1, source_target_pairs={{0,8},{4,12},{8,0},{12,4},{1,9},{5,13},{9,1},{13,5},{2,10},{6,14},... | collective-permute-start | bytes 110600 | tf_op jit(solution)/shard_map/ppermute | solution.py:432
  36.6 4.9 %collective-permute-start.17 = (bf16[144,128]{1,0:T(8,128)(2,1)S(1)}, bf16[144,128]{1,0:T(8,128)(2,1)S(1)}, u32[]{:S(2)}, u32[]{:S(2)}) collective-permute-start(bf16[144,128]{1,0:T(8,128)(2,1)S(1)} %shard_map.78.own_ref), channel_id=1, source_target_pairs={{0,6},{2,4},{4,2},{6,0},{8,14},{10,12},{12,10},{14,8},{1,7},{3,5},... | collective-permute-start | bytes 110600 | tf_op jit(solution)/shard_map/ppermute | solution.py:432
  39.5 4.0 %collective-permute-start.16 = (bf16[144,128]{1,0:T(8,128)(2,1)S(1)}, bf16[144,128]{1,0:T(8,128)(2,1)S(1)}, u32[]{:S(2)}, u32[]{:S(2)}) collective-permute-start(bf16[144,128]{1,0:T(8,128)(2,1)S(1)} %shard_map.78.own_ref), channel_id=1, source_target_pairs={{0,2},{2,0},{4,6},{6,4},{8,10},{10,8},{12,14},{14,12},{1,3},{3,1},... | collective-permute-start | bytes 110600 | tf_op jit(solution)/shard_map/ppermute | solution.py:432
  40.1 4.0 %collective-permute-start.15 = (bf16[144,128]{1,0:T(8,128)(2,1)S(1)}, bf16[144,128]{1,0:T(8,128)(2,1)S(1)}, u32[]{:S(2)}, u32[]{:S(2)}) collective-permute-start(bf16[144,128]{1,0:T(8,128)(2,1)S(1)} %shard_map.78.own_ref), channel_id=1, source_target_pairs={{0,4},{2,6},{4,0},{6,2},{8,12},{10,14},{12,8},{14,10},{1,5},{3,7},... | collective-permute-start | bytes 110600 | tf_op jit(solution)/shard_map/ppermute | solution.py:432
  44.1 1.4 %collective-permute-start.18 = (bf16[2,2,144,128]{3,2,1,0:T(8,128)(2,1)S(1)}, bf16[2,2,144,128]{3,2,1,0:T(8,128)(2,1)S(1)}, u32[]{:S(2)}, u32[]{:S(2)}) collective-permute-start(bf16[2,2,144,128]{3,2,1,0:T(8,128)(2,1)S(1)} %shard_map.79.own_ref), channel_id=1, source_target_pairs={{0,1},{1,0},{2,3},{3,2},{4,5},{5,4},{6,7},{7,6},{8,9},{9,8},{10,11... | collective-permute-start | bytes 442376 | tf_op jit(solution)/shard_map/ppermute | solution.py:432

commit v7 on v6

--- a/solution.py
+++ b/solution.py
@@ -98,7 +98,12 @@
     two_ref[...] = jnp.where(is_odd, high, low)
 
 
-def arrange_kernel(cot_rows_ref, k1_ref, k2_ref, _, moved_ref, w1_ref, w2_ref):
+def as_matrix(ref, c):
+    stacked = jnp.concatenate([ref[3 * ab + c] for ab in range(9)], axis=0)
+    return stacked.astype(F32).T.astype(BF)
+
+
+def arrange_kernel(cot_rows_ref, k1_ref, _, moved_ref, w1_ref):
     depth, out, cells = cot_rows_ref.shape
     for d in range(depth):
         for h in range(0, cells, LANES):
@@ -108,10 +113,7 @@
                 moved_ref[d, n * out : (n + 1) * out, h : h + LANES] = value
     mid = k1_ref.shape[2]
     for c in range(3):
-        one = jnp.concatenate([k1_ref[3 * ab + c] for ab in range(9)], axis=0)
-        w1_ref[c * mid : (c + 1) * mid, :] = one.astype(F32).T.astype(BF)
-        two = jnp.concatenate([k2_ref[3 * ab + c] for ab in range(9)], axis=0)
-        w2_ref[c * out : (c + 1) * out, :] = two.astype(F32).T.astype(BF)
+        w1_ref[c * mid : (c + 1) * mid, :] = as_matrix(k1_ref, c)
 
 
 def sides(axis, one, two):
@@ -261,10 +263,9 @@
     pack(direct, blocks, mid // lax.axis_size("dp"), grad_refs)
 
 
-def features_kernel(hidden_ref, w2_ref, out_ref, token_ref, scratch):
-    out = w2_ref.shape[0] // 3
-    _, depth, height, _ = out_ref.shape
-    w2 = w2_ref[...]
+def features_kernel(hidden_ref, k2_ref, out_ref, token_ref, scratch):
+    out, depth, height, _ = out_ref.shape
+    w2 = jnp.concatenate([as_matrix(k2_ref, c) for c in range(3)], axis=0)
     for d in range(depth):
         for h in range(0, height, 2):
             rhs = jnp.concatenate(
@@ -341,47 +342,41 @@
         h = 1 - half if y else half
         second = keep_second[p, h] + got_second[p, h].astype(F32)
         first = keep_first[p, h] + got_first[p, h].astype(F32)
-        return jnp.concatenate([second, first], axis=0).reshape(kept_ref.shape)
+        return jnp.concatenate([second, first], axis=0)
 
     kept_ref[...] = total(0, 0)
     for (x, y), send_ref in zip(moves, send_refs, strict=True):
         send_ref[...] = total(x, y).astype(BF)
 
 
-def depth_kernel(kept_ref, *refs):
-    *got_refs, _, own_ref, send_ref = refs
-    mine = lax.rem(lax.axis_index("dep"), 2)
-
-    def total(at):
-        value = kept_ref[at]
-        for ref in got_refs:
-            value = value + ref[at].astype(F32)
-        return value
-
-    own_ref[...] = total(mine)
-    send_ref[...] = total(1 - mine).astype(BF)
-
-
-def add_kernel(one_ref, two_ref, out_ref):
-    out_ref[...] = (one_ref[...].astype(F32) + two_ref[...].astype(F32)).astype(BF)
-
-
-def order_kernel(own_ref, depth_ref, height_ref, both_ref, out_ref):
-    y, z = lax.axis_index("y"), lax.rem(lax.axis_index("dep"), 2)
-    out_ref[y, z] = own_ref[...]
-    out_ref[y, 1 - z] = depth_ref[...]
-    out_ref[1 - y, z] = height_ref[...]
-    out_ref[1 - y, 1 - z] = both_ref[...]
+def total_kernel(kept_ref, *refs):
+    *got_refs, out_ref = refs
+    value = kept_ref[...]
+    for ref in got_refs:
+        value = value + ref[...].astype(F32)
+    out_ref[...] = value.astype(BF)
+
+
+def depth_kernel(a_ref, b_ref, c_ref, d_ref, _, out_ref):
+    one = a_ref[...].astype(F32) + b_ref[...].astype(F32)
+    two = c_ref[...].astype(F32) + d_ref[...].astype(F32)
+    out_ref[...] = (one + two).astype(BF)
+
+
+def order_kernel(own_ref, got_ref, out_ref):
+    mine = lax.axis_index("y")
+    out_ref[mine] = own_ref[...]
+    out_ref[1 - mine] = got_ref[...]
 
 
 def unpack_kernel(length_second, own_ref, got_ref, g1_ref, g2_ref):
-    halves, _, half, _ = own_ref.shape
+    halves = own_ref.shape[0]
     size, inner = g1_ref.shape[1:]
     mid = g2_ref.shape[2]
     core = lax.axis_index("core") == 1
     quarters = []
     for n in range(halves):
-        own, got = (ref[n].astype(F32).reshape(2 * half, LANES) for ref in (own_ref, got_ref))
+        own, got = (ref[n].astype(F32) for ref in (own_ref, got_ref))
         quarters += [jnp.where(core, got, own), jnp.where(core, own, got)]
     second = [quarter[:length_second] for quarter in quarters]
     first = [quarter[length_second:] for quarter in quarters]
@@ -470,10 +465,10 @@
         [pltpu.VMEM((inner * rows, width), F32)],
     )
     one, two = swapped(one, HGT, 0), swapped(two, HGT, 1)
-    moved, w1, w2 = call(
+    moved, w1 = call(
         arrange_kernel,
-        [shape((depth, 3 * out, cells), BF), shape((3 * mid, 9 * inner), BF), shape((3 * out, 9 * mid), BF)],
-        [cot_rows, k1, k2, deep],
+        [shape((depth, 3 * out, cells), BF), shape((3 * mid, 9 * inner), BF)],
+        [cot_rows, k1, deep],
         flops=500_000_000,
     )
     back_one, back_two = swapped(back_one, "dep", 0), swapped(back_two, "dep", 1)
@@ -525,25 +520,21 @@
     features, token = call(
         features_kernel,
         [shape(cotangent.shape[1:], BF), shape((8, width), F32)],
-        [hidden, w2],
+        [hidden, k2],
         [pltpu.VMEM((out * rows, width), F32)],
         flops=900_000_000,
     )
-    block = (2, length // 2, width)
+    block = (length, width)
     kept, *sends = call(
         functools.partial(plane_kernel, moves),
         [shape(block, F32)] + [shape(block, BF)] * len(moves),
         [second[0], got_second, first[0], got_first],
     )
     gots = [across(send, ("dp", x), ("y", y)) for send, (x, y) in zip(sends, moves, strict=True)]
-    own, send = call(depth_kernel, [shape(block[1:], F32), shape(block[1:], BF)], [kept, *gots, token])
-    (share,) = call(add_kernel, [shape(block[1:], BF)], [own, across(send, ("dep", 1))])
-    (share,) = call(add_kernel, [shape(block[1:], BF)], [share, across(share, ("dep", 2))])
-    (own,) = call(
-        order_kernel,
-        [shape((halves, *block), BF)],
-        [share, *(across(share, ("dep", z), ("y", y)) for z, y in ((1, 0), (0, 1), (1, 1)))],
-    )
+    (share,) = call(total_kernel, [shape(block, BF)], [kept, *gots])
+    gots = [across(share, ("dep", bits)) for bits in (1, 2, 3)]
+    (share,) = call(depth_kernel, [shape(block, BF)], [share, *gots, token])
+    (own,) = call(order_kernel, [shape((halves, *block), BF)], [share, across(share, ("y", 1))])
     grad_first, grad_second = call(
         functools.partial(unpack_kernel, length_second),
         [shape((27, size, inner), F32), shape((27, 2 * size, mid), F32)],

time: 46.9 us -> 44 us (0.938)
  starting transfers between devices: 21.5 us -> 19.2 us
    ppermute x11 -> x10, starting transfers between devices: 12.2 us -> 9.81 us  [across(): lax.ppermute(x, axes, [(i, i ^ flip) for i in range(lax.axis_size(axes))])]
    ppermute x11 -> x10, waiting for transfers between devices: 12.9 us -> 12.5 us  [across(): lax.ppermute(x, axes, [(i, i ^ flip) for i in range(lax.axis_size(axes))])]
    pallas_call x14 -> x13, Pallas kernels: 10.1 us -> 9.88 us  [call(): pl.pallas_call(body, out_shape=outs, in_specs=[pl.BlockSpec(memory_space=...]
  transfers between devices with their start and end apart: 19 -> 18, of which waited for: 12 -> 10; matrix products, arithmetic and copies ran while one was open for 0% -> 0% of each run, Pallas kernels for 19% -> 19%
where the time goes in v7:
time: 44 us; the launch traced here: 43.9 us
  starting transfers between devices  19.2 us (44%)
  waiting for transfers between devices  14 us (32%)
  Pallas kernels  9.88 us (22%)
  between operations  0.77 us (2%)
    ppermute x10, waiting for transfers between devices, across(): lax.ppermute(x, axes, [(i, i ^ flip) for i in range(lax.axis_size(axes))])  12.5 us
    pallas_call x13, Pallas kernels, call(): pl.pallas_call(body, out_shape=outs, in_specs=[pl.BlockSpec(memory_space=...  9.88 us
    ppermute x10, starting transfers between devices, across(): lax.ppermute(x, axes, [(i, i ^ flip) for i in range(lax.axis_size(axes))])  9.81 us
    ppermute x8, starting transfers between devices, swapped(): return lax.ppermute(x, ('dp', *axes), list(enumerate(partner)))  9.4 us
    ppermute x8, waiting for transfers between devices, swapped(): return lax.ppermute(x, ('dp', *axes), list(enumerate(partner)))  1.54 us
  transfers between devices with their start and end apart: 18, of which 10 were waited for; matrix products, arithmetic and copies ran while one was open for 0% of the time, Pallas kernels for 19%

profile of v7, /device:TPU:0, one launch (start us, length us, event | category | flops | bytes accessed | tf_op | source)
XLA Modules:
  0.0 43.9 jit_solution(12569991301775114616)
XLA Ops:
  0.7 3.0 %collective-permute-start.1 = (bf16[32,2,8,128]{3,2,1,0:T(8,128)(2,1)}, bf16[32,2,8,128]{3,2,1,0:T(8,128)(2,1)S(1)}, u32[]{:S(2)}, u32[]{:S(2)}) collective-permute-start(bf16[32,2,8,128]{3,2,1,0:T(8,128)(2,1)} %bitcast.5), channel_id=1, source_target_pairs={{0,16},{4,8},{8,4},{12,28},{16,0},{20,24},{24,20},{28,12},{1,17},{... | collective-permute-start | bytes 393224 | tf_op jit(solution)/shard_map/ppermute | solution.py:419
  3.7 1.7 %collective-permute-start = (bf16[32,2,8,128]{3,2,1,0:T(8,128)(2,1)}, bf16[32,2,8,128]{3,2,1,0:T(8,128)(2,1)S(1)}, u32[]{:S(2)}, u32[]{:S(2)}) collective-permute-start(bf16[32,2,8,128]{3,2,1,0:T(8,128)(2,1)} %bitcast.6), channel_id=1, source_target_pairs={{0,4},{4,0},{8,12},{12,8},{16,20},{20,16},{24,28},{28,24},{1,5},{5... | collective-permute-start | bytes 393224 | tf_op jit(solution)/shard_map/ppermute | solution.py:419
  5.4 1.7 %shard_map.68 = (bf16[2,128,1024]{2,1,0:T(8,128)(2,1)S(1)}, f32[2,64,1280]{2,1,0:T(8,128)S(1)}, bf16[64,1280]{1,0:T(8,128)(2,1)S(1)}, bf16[64,1280]{1,0:T(8,128)(2,1)S(1)}) custom-call(bf16[128,2,8,128]{3,2,1,0:T(8,128)(2,1)S(1)} %bitcast.8, bf16[27,64,128]{2,1,0:T(8,128)(2,1)S(1)} %bitcast.9, bf16[128,256]{1,0:T(8,128)(2,1)S(1)} %shard_map.67.blank_ref), custom_call_target="tpu_custom_call" | custom-call | flops 1100000000 | bytes 2539520 | tf_op jit(solution)/shard_map/pallas_call | solution.py:18
  7.5 1.2 %collective-permute-start.5 = (bf16[64,1280]{1,0:T(8,128)(2,1)S(1)}, bf16[64,1280]{1,0:T(8,128)(2,1)S(1)}, u32[]{:S(2)}, u32[]{:S(2)}) collective-permute-start(bf16[64,1280]{1,0:T(8,128)(2,1)S(1)} %get-tuple-element.38), channel_id=1, source_target_pairs={{0,16},{4,8},{8,4},{12,28},{16,0},{20,24},{24,20},{28,12},{1,17},{... | collective-permute-start | bytes 491528 | tf_op jit(solution)/shard_map/ppermute | solution.py:419
  9.7 1.6 %collective-permute-start.3 = (bf16[6,32,256]{2,1,0:T(8,128)(2,1)S(1)}, bf16[6,32,256]{2,1,0:T(8,128)(2,1)S(1)}, u32[]{:S(2)}, u32[]{:S(2)}) collective-permute-start(bf16[6,32,256]{2,1,0:T(8,128)(2,1)S(1)} %get-tuple-element.33), channel_id=1, source_target_pairs={{0,16},{1,2},{2,1},{3,19},{16,0},{17,18},{18,17},{19,3},{4,20},{5,... | collective-permute-start | bytes 294920 | tf_op jit(solution)/shard_map/ppermute | solution.py:419
  11.8 0.7 %collective-permute-done.4.one_ref = bf16[64,1280]{1,0:T(8,128)(2,1)S(1)} collective-permute-done((bf16[64,1280]{1,0:T(8,128)(2,1)S(1)}, bf16[64,1280]{1,0:T(8,128)(2,1)S(1)}, u32[]{:S(2)}, u32[]{:S(2)}) %collective-permute-start.4) | collective-permute-done | bytes 163872 | tf_op jit(solution)/shard_map/ppermute | solution.py:419
  13.0 1.3 %collective-permute-start.8 = (bf16[2,64,128]{2,1,0:T(8,128)(2,1)S(1)}, bf16[2,64,128]{2,1,0:T(8,128)(2,1)S(1)}, u32[]{:S(2)}, u32[]{:S(2)}) collective-permute-start(bf16[2,64,128]{2,1,0:T(8,128)(2,1)S(1)} %get-tuple-element.46), channel_id=1, source_target_pairs={{0,16},{1,2},{2,1},{3,19},{16,0},{17,18},{18,17},{19,3},{4,20},{5,... | collective-permute-start | bytes 98312 | tf_op jit(solution)/shard_map/ppermute | solution.py:419
  14.4 2.5 %shard_map.72 = (bf16[4,64,1280]{2,1,0:T(8,128)(2,1)S(1)}, f32[2,64,1024]{2,1,0:T(8,128)S(1)}, bf16[6,32,1536]{2,1,0:T(8,128)(2,1)S(1)}, f32[2,2,224,128]{3,2,1,0:T(8,128)S(1)}, bf16[2,2,224,128]{3,2,1,0:T(8,128)(2,1)S(1)}) custom-call(bf16[6,32,1024]{2,1,0:T(8,128)(2,1)S(1)} %get-tuple-element.31._.deep_ref, ...), custom_call_target="tpu_custom_call" | custom-call | flops 1500000000 | bytes 5255168 | tf_op jit(solution)/shard_map/pallas_call | solution.py:18
  17.3 0.8 %shard_map.74 = (f32[2,2,64,128]{3,2,1,0:T(8,128)S(1)}, bf16[2,2,64,128]{3,2,1,0:T(8,128)(2,1)S(1)}) custom-call(bf16[6,32,1536]{2,1,0:T(8,128)(2,1)S(1)} %get-tuple-element.44.rows_ref, f32[2,64,1024]{2,1,0:T(8,128)S(1)} %get-tuple-element.39._.back_ref, bf16[2,64,128]{2,1,0:T(8,128)(2,1)S(1)} %collective-permute-done.7.one_ref, ...), custom_call_target="tpu_custom_call" | custom-call | flops 4000000000 | bytes 1900544 | tf_op jit(solution)/shard_map/pallas_call | solution.py:18
  18.3 1.1 %collective-permute-done.9.refs_3_ = bf16[2,2,64,128]{3,2,1,0:T(8,128)(2,1)S(1)} collective-permute-done((bf16[2,2,64,128]{3,2,1,0:T(8,128)(2,1)S(1)}, bf16[2,2,64,128]{3,2,1,0:T(8,128)(2,1)S(1)}, u32[]{:S(2)}, u32[]{:S(2)}) %collective-permute-start.9) | collective-permute-done | bytes 65568 | tf_op jit(solution)/shard_map/ppermute | solution.py:427
  19.5 1.4 %collective-permute-start.10 = (bf16[288,128]{1,0:T(8,128)(2,1)S(1)}, bf16[288,128]{1,0:T(8,128)(2,1)S(1)}, u32[]{:S(2)}, u32[]{:S(2)}) collective-permute-start(bf16[288,128]{1,0:T(8,128)(2,1)S(1)} %get-tuple-element.51), channel_id=1, source_target_pairs={{0,16},{2,18},{16,0},{18,2},{1,17},{3,19},{17,1},{19,3},{4,20},{6,... | collective-permute-start | bytes 221192 | tf_op jit(solution)/shard_map/ppermute | solution.py:427
  20.9 0.9 %collective-permute-start.11 = (bf16[288,128]{1,0:T(8,128)(2,1)S(1)}, bf16[288,128]{1,0:T(8,128)(2,1)S(1)}, u32[]{:S(2)}, u32[]{:S(2)}) collective-permute-start(bf16[288,128]{1,0:T(8,128)(2,1)S(1)} %get-tuple-element.52), channel_id=1, source_target_pairs={{0,2},{2,0},{16,18},{18,16},{1,3},{3,1},{17,19},{19,17},{4,6},{6,4... | collective-permute-start | bytes 221192 | tf_op jit(solution)/shard_map/ppermute | solution.py:427
  21.9 1.2 %collective-permute-start.12 = (bf16[288,128]{1,0:T(8,128)(2,1)S(1)}, bf16[288,128]{1,0:T(8,128)(2,1)S(1)}, u32[]{:S(2)}, u32[]{:S(2)}) collective-permute-start(bf16[288,128]{1,0:T(8,128)(2,1)S(1)} %get-tuple-element.53), channel_id=1, source_target_pairs={{0,18},{2,16},{16,2},{18,0},{1,19},{3,17},{17,3},{19,1},{4,22},{6,... | collective-permute-start | bytes 221192 | tf_op jit(solution)/shard_map/ppermute | solution.py:427
  23.1 0.9 %collective-permute-done.10.refs_0_ = bf16[288,128]{1,0:T(8,128)(2,1)S(1)} collective-permute-done((bf16[288,128]{1,0:T(8,128)(2,1)S(1)}, bf16[288,128]{1,0:T(8,128)(2,1)S(1)}, u32[]{:S(2)}, u32[]{:S(2)}) %collective-permute-start.10) | collective-permute-done | bytes 73760 | tf_op jit(solution)/shard_map/ppermute | solution.py:427
  23.9 2.2 %collective-permute-done.11.refs_1_ = bf16[288,128]{1,0:T(8,128)(2,1)S(1)} collective-permute-done((bf16[288,128]{1,0:T(8,128)(2,1)S(1)}, bf16[288,128]{1,0:T(8,128)(2,1)S(1)}, u32[]{:S(2)}, u32[]{:S(2)}) %collective-permute-start.11) | collective-permute-done | bytes 73760 | tf_op jit(solution)/shard_map/ppermute | solution.py:427
  26.1 1.0 %collective-permute-done.12.refs_2_ = bf16[288,128]{1,0:T(8,128)(2,1)S(1)} collective-permute-done((bf16[288,128]{1,0:T(8,128)(2,1)S(1)}, bf16[288,128]{1,0:T(8,128)(2,1)S(1)}, u32[]{:S(2)}, u32[]{:S(2)}) %collective-permute-start.12) | collective-permute-done | bytes 73760 | tf_op jit(solution)/shard_map/ppermute | solution.py:427
  27.2 3.4 %collective-permute-start.15 = (bf16[288,128]{1,0:T(8,128)(2,1)S(1)}, bf16[288,128]{1,0:T(8,128)(2,1)S(1)}, u32[]{:S(2)}, u32[]{:S(2)}) collective-permute-start(bf16[288,128]{1,0:T(8,128)(2,1)S(1)} %shard_map.76.a_ref), channel_id=1, source_target_pairs={{0,12},{4,8},{8,4},{12,0},{1,13},{5,9},{9,5},{13,1},{2,14},{6,10},... | collective-permute-start | bytes 221192 | tf_op jit(solution)/shard_map/ppermute | solution.py:427
  31.1 0.5 %collective-permute-start.13 = (bf16[288,128]{1,0:T(8,128)(2,1)S(1)}, bf16[288,128]{1,0:T(8,128)(2,1)S(1)}, u32[]{:S(2)}, u32[]{:S(2)}) collective-permute-start(bf16[288,128]{1,0:T(8,128)(2,1)S(1)} %shard_map.76.a_ref), channel_id=1, source_target_pairs={{0,4},{4,0},{8,12},{12,8},{1,5},{5,1},{9,13},{13,9},{2,6},{6,2},{1... | collective-permute-start | bytes 221192 | tf_op jit(solution)/shard_map/ppermute | solution.py:427
  31.6 2.5 %shard_map.73 = (bf16[128,2,8,128]{3,2,1,0:T(8,128)(2,1)}, f32[8,128]{1,0:T(8,128)S(1)}) custom-call(bf16[4,64,1280]{2,1,0:T(8,128)(2,1)S(1)} %get-tuple-element.40.hidden_ref, bf16[27,64,128]{2,1,0:T(8,128)(2,1)S(1)} %bitcast.10), custom_call_target="tpu_custom_call" | custom-call | flops 900000000 | bytes 1626112 | tf_op jit(solution)/shard_map/pallas_call | solution.py:18
  34.2 2.6 %collective-permute-done.14.c_ref = bf16[288,128]{1,0:T(8,128)(2,1)S(1)} collective-permute-done((bf16[288,128]{1,0:T(8,128)(2,1)S(1)}, bf16[288,128]{1,0:T(8,128)(2,1)S(1)}, u32[]{:S(2)}, u32[]{:S(2)}) %collective-permute-start.14) | collective-permute-done | bytes 73760 | tf_op jit(solution)/shard_map/ppermute | solution.py:427
  36.8 1.1 %collective-permute-start.16 = (bf16[288,128]{1,0:T(8,128)(2,1)S(1)}, bf16[288,128]{1,0:T(8,128)(2,1)S(1)}, u32[]{:S(2)}, u32[]{:S(2)}) collective-permute-start(bf16[288,128]{1,0:T(8,128)(2,1)S(1)} %shard_map.77.own_ref), channel_id=1, source_target_pairs={{0,2},{2,0},{1,3},{3,1},{4,6},{6,4},{5,7},{7,5},{8,10},{10,8},{9,1... | collective-permute-start | bytes 221192 | tf_op jit(solution)/shard_map/ppermute | solution.py:427
  37.9 3.3 %collective-permute-done.16.got_ref = bf16[288,128]{1,0:T(8,128)(2,1)S(1)} collective-permute-done((bf16[288,128]{1,0:T(8,128)(2,1)S(1)}, bf16[288,128]{1,0:T(8,128)(2,1)S(1)}, u32[]{:S(2)}, u32[]{:S(2)}) %collective-permute-start.16) | collective-permute-done | bytes 73760 | tf_op jit(solution)/shard_map/ppermute | solution.py:427
  41.3 1.4 %collective-permute-done.17.got_ref = bf16[2,288,128]{2,1,0:T(8,128)(2,1)S(1)} collective-permute-done((bf16[2,288,128]{2,1,0:T(8,128)(2,1)S(1)}, bf16[2,288,128]{2,1,0:T(8,128)(2,1)S(1)}, u32[]{:S(2)}, u32[]{:S(2)}) %collective-permute-start.17) | collective-permute-done | bytes 147488 | tf_op jit(solution)/shard_map/ppermute | solution.py:427
  42.7 1.2 %shard_map.79 = (f32[27,32,32]{2,1,0:T(8,128)}, f32[27,64,64]{2,1,0:T(8,128)}) custom-call(bf16[2,288,128]{2,1,0:T(8,128)(2,1)S(1)} %shard_map.78.own_ref, bf16[2,288,128]{2,1,0:T(8,128)(2,1)S(1)} %collective-permute-done.17.got_ref), custom_call_target="tpu_custom_call" | custom-call | bytes 847872 | tf_op jit(solution)/shard_map/pallas_call | solution.py:18
  (33 shorter events, 3.7 us)
Async XLA Ops:
  0.6 4.7 %copy-start.1 = (bf16[1,128,2,8,128]{4,3,2,1,0:T(8,128)(2,1)S(1)}, bf16[1,128,2,8,128]{4,3,2,1,0:T(8,128)(2,1)}, u32[]{:S(2)}) copy-start(bf16[1,128,2,8,128]{4,3,2,1,0:T(8,128)(2,1)} %param.7) | copy-start | bytes 1572868
  0.6 4.7 %copy-start.2 = (bf16[27,128,64]{1,2,0:T(8,128)(2,1)S(1)}, bf16[27,128,64]{1,2,0:T(8,128)(2,1)}, u32[]{:S(2)}) copy-start(bf16[27,128,64]{1,2,0:T(8,128)(2,1)} %param.6) | copy-start | bytes 1327108
  0.7 8.1 %collective-permute-start.1 = (bf16[32,2,8,128]{3,2,1,0:T(8,128)(2,1)}, bf16[32,2,8,128]{3,2,1,0:T(8,128)(2,1)S(1)}, u32[]{:S(2)}, u32[]{:S(2)}) collective-permute-start(bf16[32,2,8,128]{3,2,1,0:T(8,128)(2,1)} %bitcast.5), channel_id=1, source_target_pairs={{0,16},{4,8},{8,4},{12,28},{16,0},{20,24},{24,20},{28,12},{1,17},{... | collective-permute-start | bytes 393224 | tf_op jit(solution)/shard_map/ppermute | solution.py:419
  3.7 5.6 %collective-permute-start = (bf16[32,2,8,128]{3,2,1,0:T(8,128)(2,1)}, bf16[32,2,8,128]{3,2,1,0:T(8,128)(2,1)S(1)}, u32[]{:S(2)}, u32[]{:S(2)}) collective-permute-start(bf16[32,2,8,128]{3,2,1,0:T(8,128)(2,1)} %bitcast.6), channel_id=1, source_target_pairs={{0,4},{4,0},{8,12},{12,8},{16,20},{20,16},{24,28},{28,24},{1,5},{5... | collective-permute-start | bytes 393224 | tf_op jit(solution)/shard_map/ppermute | solution.py:419
  5.3 3.9 %copy-start = (bf16[1,32,2,8,128]{4,3,2,1,0:T(8,128)(2,1)S(1)}, bf16[1,32,2,8,128]{4,3,2,1,0:T(8,128)(2,1)}, u32[]{:S(2)}) copy-start(bf16[1,32,2,8,128]{4,3,2,1,0:T(8,128)(2,1)} %param.4) | copy-start | bytes 393220
  5.3 6.0 %copy-start.3 = (bf16[27,64,32]{1,2,0:T(8,128)(2,1)S(1)}, bf16[27,64,32]{1,2,0:T(8,128)(2,1)}, u32[]{:S(2)}) copy-start(bf16[27,64,32]{1,2,0:T(8,128)(2,1)} %param.5) | copy-start | bytes 331780
  7.1 5.4 %collective-permute-start.4 = (bf16[64,1280]{1,0:T(8,128)(2,1)S(1)}, bf16[64,1280]{1,0:T(8,128)(2,1)S(1)}, u32[]{:S(2)}, u32[]{:S(2)}) collective-permute-start(bf16[64,1280]{1,0:T(8,128)(2,1)S(1)} %get-tuple-element.37), channel_id=1, source_target_pairs={{0,4},{4,0},{8,12},{12,8},{16,20},{20,16},{24,28},{28,24},{1,5},{5... | collective-permute-start | bytes 491528 | tf_op jit(solution)/shard_map/ppermute | solution.py:419
  7.5 5.3 %collective-permute-start.5 = (bf16[64,1280]{1,0:T(8,128)(2,1)S(1)}, bf16[64,1280]{1,0:T(8,128)(2,1)S(1)}, u32[]{:S(2)}, u32[]{:S(2)}) collective-permute-start(bf16[64,1280]{1,0:T(8,128)(2,1)S(1)} %get-tuple-element.38), channel_id=1, source_target_pairs={{0,16},{4,8},{8,4},{12,28},{16,0},{20,24},{24,20},{28,12},{1,17},{... | collective-permute-start | bytes 491528 | tf_op jit(solution)/shard_map/ppermute | solution.py:419
  9.6 4.7 %collective-permute-start.2 = (bf16[6,32,256]{2,1,0:T(8,128)(2,1)S(1)}, bf16[6,32,256]{2,1,0:T(8,128)(2,1)S(1)}, u32[]{:S(2)}, u32[]{:S(2)}) collective-permute-start(bf16[6,32,256]{2,1,0:T(8,128)(2,1)S(1)} %get-tuple-element.32), channel_id=1, source_target_pairs={{0,1},{1,0},{2,3},{3,2},{16,17},{17,16},{18,19},{19,18},{4,5},{5,4... | collective-permute-start | bytes 294920 | tf_op jit(solution)/shard_map/ppermute | solution.py:419
  9.7 4.7 %collective-permute-start.3 = (bf16[6,32,256]{2,1,0:T(8,128)(2,1)S(1)}, bf16[6,32,256]{2,1,0:T(8,128)(2,1)S(1)}, u32[]{:S(2)}, u32[]{:S(2)}) collective-permute-start(bf16[6,32,256]{2,1,0:T(8,128)(2,1)S(1)} %get-tuple-element.33), channel_id=1, source_target_pairs={{0,16},{1,2},{2,1},{3,19},{16,0},{17,18},{18,17},{19,3},{4,20},{5,... | collective-permute-start | bytes 294920 | tf_op jit(solution)/shard_map/ppermute | solution.py:419
  12.9 4.4 %collective-permute-start.7 = (bf16[2,64,128]{2,1,0:T(8,128)(2,1)S(1)}, bf16[2,64,128]{2,1,0:T(8,128)(2,1)S(1)}, u32[]{:S(2)}, u32[]{:S(2)}) collective-permute-start(bf16[2,64,128]{2,1,0:T(8,128)(2,1)S(1)} %get-tuple-element.45), channel_id=1, source_target_pairs={{0,1},{1,0},{2,3},{3,2},{16,17},{17,16},{18,19},{19,18},{4,5},{5,4... | collective-permute-start | bytes 98312 | tf_op jit(solution)/shard_map/ppermute | solution.py:419
  13.0 4.3 %collective-permute-start.8 = (bf16[2,64,128]{2,1,0:T(8,128)(2,1)S(1)}, bf16[2,64,128]{2,1,0:T(8,128)(2,1)S(1)}, u32[]{:S(2)}, u32[]{:S(2)}) collective-permute-start(bf16[2,64,128]{2,1,0:T(8,128)(2,1)S(1)} %get-tuple-element.46), channel_id=1, source_target_pairs={{0,16},{1,2},{2,1},{3,19},{16,0},{17,18},{18,17},{19,3},{4,20},{5,... | collective-permute-start | bytes 98312 | tf_op jit(solution)/shard_map/ppermute | solution.py:419
  16.9 2.5 %collective-permute-start.6 = (bf16[2,2,224,128]{3,2,1,0:T(8,128)(2,1)S(1)}, bf16[2,2,224,128]{3,2,1,0:T(8,128)(2,1)S(1)}, u32[]{:S(2)}, u32[]{:S(2)}) collective-permute-start(bf16[2,2,224,128]{3,2,1,0:T(8,128)(2,1)S(1)} %get-tuple-element.43), channel_id=1, source_target_pairs={{0,1},{1,0},{2,3},{3,2},{4,5},{5,4},{6,7},{7,6},{8,9},{9,8},{10,11... | collective-permute-start | bytes 688136 | tf_op jit(solution)/shard_map/ppermute | solution.py:427
  18.1 1.3 %collective-permute-start.9 = (bf16[2,2,64,128]{3,2,1,0:T(8,128)(2,1)S(1)}, bf16[2,2,64,128]{3,2,1,0:T(8,128)(2,1)S(1)}, u32[]{:S(2)}, u32[]{:S(2)}) collective-permute-start(bf16[2,2,64,128]{3,2,1,0:T(8,128)(2,1)S(1)} %get-tuple-element.49), channel_id=1, source_target_pairs={{0,1},{1,0},{2,3},{3,2},{4,5},{5,4},{6,7},{7,6},{8,9},{9,8},{10,11... | collective-permute-start | bytes 196616 | tf_op jit(solution)/shard_map/ppermute | solution.py:427
  19.5 4.4 %collective-permute-start.10 = (bf16[288,128]{1,0:T(8,128)(2,1)S(1)}, bf16[288,128]{1,0:T(8,128)(2,1)S(1)}, u32[]{:S(2)}, u32[]{:S(2)}) collective-permute-start(bf16[288,128]{1,0:T(8,128)(2,1)S(1)} %get-tuple-element.51), channel_id=1, source_target_pairs={{0,16},{2,18},{16,0},{18,2},{1,17},{3,19},{17,1},{19,3},{4,20},{6,... | collective-permute-start | bytes 221192 | tf_op jit(solution)/shard_map/ppermute | solution.py:427
  20.9 5.1 %collective-permute-start.11 = (bf16[288,128]{1,0:T(8,128)(2,1)S(1)}, bf16[288,128]{1,0:T(8,128)(2,1)S(1)}, u32[]{:S(2)}, u32[]{:S(2)}) collective-permute-start(bf16[288,128]{1,0:T(8,128)(2,1)S(1)} %get-tuple-element.52), channel_id=1, source_target_pairs={{0,2},{2,0},{16,18},{18,16},{1,3},{3,1},{17,19},{19,17},{4,6},{6,4... | collective-permute-start | bytes 221192 | tf_op jit(solution)/shard_map/ppermute | solution.py:427
  21.9 5.3 %collective-permute-start.12 = (bf16[288,128]{1,0:T(8,128)(2,1)S(1)}, bf16[288,128]{1,0:T(8,128)(2,1)S(1)}, u32[]{:S(2)}, u32[]{:S(2)}) collective-permute-start(bf16[288,128]{1,0:T(8,128)(2,1)S(1)} %get-tuple-element.53), channel_id=1, source_target_pairs={{0,18},{2,16},{16,2},{18,0},{1,19},{3,17},{17,3},{19,1},{4,22},{6,... | collective-permute-start | bytes 221192 | tf_op jit(solution)/shard_map/ppermute | solution.py:427
  27.2 7.0 %collective-permute-start.15 = (bf16[288,128]{1,0:T(8,128)(2,1)S(1)}, bf16[288,128]{1,0:T(8,128)(2,1)S(1)}, u32[]{:S(2)}, u32[]{:S(2)}) collective-permute-start(bf16[288,128]{1,0:T(8,128)(2,1)S(1)} %shard_map.76.a_ref), channel_id=1, source_target_pairs={{0,12},{4,8},{8,4},{12,0},{1,13},{5,9},{9,5},{13,1},{2,14},{6,10},... | collective-permute-start | bytes 221192 | tf_op jit(solution)/shard_map/ppermute | solution.py:427
  30.6 6.2 %collective-permute-start.14 = (bf16[288,128]{1,0:T(8,128)(2,1)S(1)}, bf16[288,128]{1,0:T(8,128)(2,1)S(1)}, u32[]{:S(2)}, u32[]{:S(2)}) collective-permute-start(bf16[288,128]{1,0:T(8,128)(2,1)S(1)} %shard_map.76.a_ref), channel_id=1, source_target_pairs={{0,8},{4,12},{8,0},{12,4},{1,9},{5,13},{9,1},{13,5},{2,10},{6,14},... | collective-permute-start | bytes 221192 | tf_op jit(solution)/shard_map/ppermute | solution.py:427
  31.1 5.7 %collective-permute-start.13 = (bf16[288,128]{1,0:T(8,128)(2,1)S(1)}, bf16[288,128]{1,0:T(8,128)(2,1)S(1)}, u32[]{:S(2)}, u32[]{:S(2)}) collective-permute-start(bf16[288,128]{1,0:T(8,128)(2,1)S(1)} %shard_map.76.a_ref), channel_id=1, source_target_pairs={{0,4},{4,0},{8,12},{12,8},{1,5},{5,1},{9,13},{13,9},{2,6},{6,2},{1... | collective-permute-start | bytes 221192 | tf_op jit(solution)/shard_map/ppermute | solution.py:427
  36.8 4.4 %collective-permute-start.16 = (bf16[288,128]{1,0:T(8,128)(2,1)S(1)}, bf16[288,128]{1,0:T(8,128)(2,1)S(1)}, u32[]{:S(2)}, u32[]{:S(2)}) collective-permute-start(bf16[288,128]{1,0:T(8,128)(2,1)S(1)} %shard_map.77.own_ref), channel_id=1, source_target_pairs={{0,2},{2,0},{1,3},{3,1},{4,6},{6,4},{5,7},{7,5},{8,10},{10,8},{9,1... | collective-permute-start | bytes 221192 | tf_op jit(solution)/shard_map/ppermute | solution.py:427
  41.2 1.4 %collective-permute-start.17 = (bf16[2,288,128]{2,1,0:T(8,128)(2,1)S(1)}, bf16[2,288,128]{2,1,0:T(8,128)(2,1)S(1)}, u32[]{:S(2)}, u32[]{:S(2)}) collective-permute-start(bf16[2,288,128]{2,1,0:T(8,128)(2,1)S(1)} %shard_map.78.own_ref), channel_id=1, source_target_pairs={{0,1},{1,0},{2,3},{3,2},{4,5},{5,4},{6,7},{7,6},{8,9},{9,8},{10,11... | collective-permute-start | bytes 442376 | tf_op jit(solution)/shard_map/ppermute | solution.py:427

commit v8 on v7

--- a/solution.py
+++ b/solution.py
@@ -165,33 +165,29 @@
     return [jnp.concatenate([left[d], deep_ref[d], right[d]], axis=1) for d in range(deep_ref.shape[0])]
 
 
-def pack(direct, blocks, size, refs):
+def pack(direct, blocks, refs, units_of):
     if not direct:
         for j, block in enumerate(blocks):
             refs[0][j] = block
         return
     keep_ref, send_ref = refs
     parts, halves, length, _ = keep_ref.shape
-    fold = blocks[0].shape[0] // (parts * size)
     core = lax.axis_index("core") == 1
-
-    def quarter(part, number):
-        values, row = [], number * length
-        while row < (number + 1) * length:
-            unit, start = divmod(row, size)
-            if unit < fold * len(blocks):
+    for part in range(parts):
+        whole = units_of(part)
+        size = whole[0].shape[0]
+
+        def quarter(number, whole=whole, size=size):
+            values, row = [], number * length
+            while row < (number + 1) * length:
+                unit, start = divmod(row, size)
                 stop = min(size, start + (number + 1) * length - row)
-                first = (fold * part + unit % fold) * size
-                values.append(blocks[unit // fold][first + start : first + stop])
+                values.append(whole[unit][start:stop])
                 row += stop - start
-            else:
-                values.append(jnp.zeros(((number + 1) * length - row, LANES), F32))
-                row = (number + 1) * length
-        return jnp.concatenate(values, axis=0)
-
-    for part in range(parts):
+            return jnp.concatenate(values, axis=0)
+
         for half in range(halves):
-            one, two = (quarter(part, 2 * half + c) for c in range(2))
+            one, two = (quarter(2 * half + c) for c in range(2))
             keep_ref[part, half] = jnp.where(core, two, one)
             send_ref[part, half] = jnp.where(core, one, two).astype(BF)
 
@@ -260,10 +256,18 @@
                 tails.append(part)
     tails.append(jnp.zeros_like(tails[0]))
     blocks += [jnp.concatenate(tails[2 * m : 2 * m + 2], axis=1) for m in range(2)]
-    pack(direct, blocks, mid // lax.axis_size("dp"), grad_refs)
-
-
-def features_kernel(hidden_ref, k2_ref, out_ref, token_ref, scratch):
+    size = mid // lax.axis_size("dp")
+
+    def units_of(part):
+        rows = [slice((2 * part + half) * size, (2 * part + half + 1) * size) for half in range(2)]
+        return [block[at] for block in blocks[:13] for at in rows] + [
+            jnp.concatenate([tails[2][at] for at in rows], axis=1)
+        ]
+
+    pack(direct, blocks, grad_refs, units_of)
+
+
+def features_kernel(hidden_ref, k2_ref, _, out_ref, token_ref, scratch):
     out, depth, height, _ = out_ref.shape
     w2 = jnp.concatenate([as_matrix(k2_ref, c) for c in range(3)], axis=0)
     for d in range(depth):
@@ -329,20 +333,17 @@
                 tails.append(part)
     tails.append(jnp.zeros((mid, LANES - 3 * inner), F32))
     blocks.append(jnp.concatenate(tails, axis=1))
-    pack(direct, blocks, mid // lax.axis_size("dp"), grad_refs)
-
-
-def plane_kernel(moves, *refs):
-    keep_second, got_second, keep_first, got_first, kept_ref, *send_refs = refs
-    part = lax.rem(lax.axis_index("dp"), keep_first.shape[0])
+    size = mid // lax.axis_size("dp")
+    pack(direct, blocks, grad_refs, lambda part: [block[part * size : (part + 1) * size] for block in blocks])
+
+
+def plane_kernel(moves, keep_ref, got_ref, _, kept_ref, *send_refs):
+    part = lax.rem(lax.axis_index("dp"), keep_ref.shape[0])
     half = lax.axis_index("y")
 
     def total(x, y):
-        p = 1 - part if x else part
-        h = 1 - half if y else half
-        second = keep_second[p, h] + got_second[p, h].astype(F32)
-        first = keep_first[p, h] + got_first[p, h].astype(F32)
-        return jnp.concatenate([second, first], axis=0)
+        at = 1 - part if x else part, 1 - half if y else half
+        return keep_ref[at] + got_ref[at].astype(F32)
 
     kept_ref[...] = total(0, 0)
     for (x, y), send_ref in zip(moves, send_refs, strict=True):
@@ -350,60 +351,73 @@
 
 
 def total_kernel(kept_ref, *refs):
-    *got_refs, out_ref = refs
+    *got_refs, _, out_ref = refs
     value = kept_ref[...]
     for ref in got_refs:
         value = value + ref[...].astype(F32)
     out_ref[...] = value.astype(BF)
 
 
-def depth_kernel(a_ref, b_ref, c_ref, d_ref, _, out_ref):
-    one = a_ref[...].astype(F32) + b_ref[...].astype(F32)
-    two = c_ref[...].astype(F32) + d_ref[...].astype(F32)
-    out_ref[...] = (one + two).astype(BF)
-
-
-def order_kernel(own_ref, got_ref, out_ref):
+def depth_kernel(*refs):
+    *in_refs, out_ref = refs
+    sums = []
+    for n in range(0, len(in_refs), 4):
+        a, b, c, d = (ref[...].astype(F32) for ref in in_refs[n : n + 4])
+        sums.append((a + b) + (c + d))
+    out_ref[...] = jnp.concatenate(sums, axis=0).astype(BF)
+
+
+def order_kernel(own_ref, got_ref, _, out_ref):
     mine = lax.axis_index("y")
     out_ref[mine] = own_ref[...]
     out_ref[1 - mine] = got_ref[...]
 
 
-def unpack_kernel(length_second, own_ref, got_ref, g1_ref, g2_ref):
-    halves = own_ref.shape[0]
-    size, inner = g1_ref.shape[1:]
-    mid = g2_ref.shape[2]
+def quarters_of(own_ref, got_ref):
     core = lax.axis_index("core") == 1
     quarters = []
-    for n in range(halves):
+    for n in range(own_ref.shape[0]):
         own, got = (ref[n].astype(F32) for ref in (own_ref, got_ref))
         quarters += [jnp.where(core, got, own), jnp.where(core, own, got)]
-    second = [quarter[:length_second] for quarter in quarters]
-    first = [quarter[length_second:] for quarter in quarters]
-
-    def get(unit, whole=second):
-        length = whole[0].shape[0]
+    return quarters
+
+
+def units_in(quarters, size):
+    length = quarters[0].shape[0]
+
+    def get(unit):
         values, row = [], unit * size
         while row < (unit + 1) * size:
             number, start = divmod(row, length)
             stop = min(length, start + (unit + 1) * size - row)
-            values.append(whole[number][start:stop])
+            values.append(quarters[number][start:stop])
             row += stop - start
         return values[0] if len(values) == 1 else jnp.concatenate(values, axis=0)
 
-    for j in range(14):
+    return get
+
+
+def unpack_kernel(length, own_ref, got_ref, first_ref, second_ref):
+    quarters = quarters_of(own_ref, got_ref)
+    size, inner = first_ref.shape[1:]
+    mid = second_ref.shape[2]
+    get = units_in([quarter[:length] for quarter in quarters], size)
+    for j in range(13):
         for half in range(2):
             value = get(2 * j + half)
             for m in range(2):
-                c, ab = (j // 4, 2 * (j % 4) + m) if j < 12 else (2 * (j - 12) + m, 8)
-                if c < 3:
-                    g2_ref[3 * ab + c, half * size : (half + 1) * size, :] = value[:, m * mid : (m + 1) * mid]
+                c, ab = (j // 4, 2 * (j % 4) + m) if j < 12 else (m, 8)
+                second_ref[3 * ab + c, half * size : (half + 1) * size, :] = value[:, m * mid : (m + 1) * mid]
+    value = get(26)
+    for half in range(2):
+        second_ref[26, half * size : (half + 1) * size, :] = value[:, half * mid : (half + 1) * mid]
+    get = units_in([quarter[length:] for quarter in quarters], size)
     for j in range(7):
-        value = get(j, first)
+        value = get(j)
         for m in range(4):
             c, ab = (j // 2, 4 * (j % 2) + m) if j < 6 else (m, 8)
             if c < 3:
-                g1_ref[3 * ab + c] = value[:, m * inner : (m + 1) * inner]
+                first_ref[3 * ab + c] = value[:, m * inner : (m + 1) * inner]
 
 
 def swapped(x, axis, first):
@@ -427,8 +441,9 @@
     return lax.ppermute(x, axes, [(i, i ^ flip) for i in range(lax.axis_size(axes))])
 
 
-def scattered(grad, parts, halves, size, length):
-    grad = jnp.swapaxes(grad.reshape(grad.shape[0], parts, -1, LANES), 0, 1).reshape(parts, -1, LANES)
+def scattered(units, length):
+    parts, halves = units.shape[0], lax.axis_size("y")
+    grad = units.reshape(parts, -1, LANES)
     grad = jnp.pad(grad, ((0, 0), (0, 2 * halves * length - grad.shape[1]), (0, 0)))
     grad = lax.psum_scatter(grad, "dp", scatter_dimension=0, tiled=True).reshape(1, halves, 2, length, LANES)
     core = lax.axis_index("core")
@@ -482,8 +497,7 @@
     size = mid // parts
     direct = parts == 2 and size % 16 == 0
     halves = lax.axis_size("y")
-    length_second, length_first = (-(-units * size // (32 * halves)) * 16 for units in (28, 7))
-    length = length_second + length_first
+    length_second, length_first = (-(-units * size // (16 * halves)) * 8 for units in (27, 7))
     hidden, slope, wide, *second = call(
         functools.partial(hidden_kernel, direct),
         [
@@ -512,29 +526,40 @@
         moves = [(1, 0), (0, 1), (1, 1)]
     else:
         moves = [(0, 1)]
-        first, second = (
-            scattered(grad[0], parts, halves, size, rows)
-            for grad, rows in ((first, length_first), (second, length_second))
+        blocks = jnp.swapaxes(second[0].reshape(14, parts, 2, size, LANES), 0, 1)
+        tail = jnp.concatenate([blocks[:, 13, half, :, :mid] for half in range(2)], axis=-1)
+        units = jnp.concatenate([blocks[:, :13].reshape(parts, 26, size, LANES), tail[:, None]], axis=1)
+        second = scattered(units, length_second)
+        first = scattered(jnp.swapaxes(first[0].reshape(7, parts, size, LANES), 0, 1), length_first)
+    grads = []
+    after = slope
+    for keep, send in (second, first):
+        block = keep.shape[2:]
+        kept, *sends = call(
+            functools.partial(plane_kernel, moves),
+            [shape(block, F32)] + [shape(block, BF)] * len(moves),
+            [keep, across(send, ("core", 1)), after],
         )
-    got_second, got_first = (across(send, ("core", 1)) for _, send in (second, first))
+        after = kept
+        grads.append((kept, [across(send, ("dp", x), ("y", y)) for send, (x, y) in zip(sends, moves, strict=True)]))
+    shares, weights, orders = [], (0, 4_000_000_000), ((1, 3, 2), (3, 2, 1))
+    for (kept, gots), weight, order in zip(grads, weights, orders, strict=True):
+        (share,) = call(total_kernel, [shape(kept.shape, BF)], [kept, *gots, after], flops=weight)
+        after = share
+        shares.append((share, [across(share, ("dep", bits)) for bits in order]))
+    (share,) = call(
+        depth_kernel,
+        [shape((length_second + length_first, width), BF)],
+        [x for share, gots in shares for x in (share, *gots)],
+    )
     features, token = call(
         features_kernel,
         [shape(cotangent.shape[1:], BF), shape((8, width), F32)],
-        [hidden, k2],
+        [hidden, k2, share],
         [pltpu.VMEM((out * rows, width), F32)],
         flops=900_000_000,
     )
-    block = (length, width)
-    kept, *sends = call(
-        functools.partial(plane_kernel, moves),
-        [shape(block, F32)] + [shape(block, BF)] * len(moves),
-        [second[0], got_second, first[0], got_first],
-    )
-    gots = [across(send, ("dp", x), ("y", y)) for send, (x, y) in zip(sends, moves, strict=True)]
-    (share,) = call(total_kernel, [shape(block, BF)], [kept, *gots])
-    gots = [across(share, ("dep", bits)) for bits in (1, 2, 3)]
-    (share,) = call(depth_kernel, [shape(block, BF)], [share, *gots, token])
-    (own,) = call(order_kernel, [shape((halves, *block), BF)], [share, across(share, ("y", 1))])
+    (own,) = call(order_kernel, [shape((halves, *share.shape), BF)], [share, across(share, ("y", 1)), token])
     grad_first, grad_second = call(
         functools.partial(unpack_kernel, length_second),
         [shape((27, size, inner), F32), shape((27, 2 * size, mid), F32)],

time: 44 us -> 48.2 us (1.095)
  starting transfers between devices: 19.2 us -> 28.4 us
  waiting for transfers between devices: 14 us -> 8.76 us
    ppermute x10 -> x16, starting transfers between devices: 9.81 us -> 19.1 us  [across(): lax.ppermute(x, axes, [(i, i ^ flip) for i in range(lax.axis_size(axes))])]
    ppermute x10 -> x16, waiting for transfers between devices: 12.5 us -> 7.14 us  [across(): lax.ppermute(x, axes, [(i, i ^ flip) for i in range(lax.axis_size(axes))])]
    pallas_call x13 -> x15, Pallas kernels: 9.88 us -> 10 us  [call(): pl.pallas_call(body, out_shape=outs, in_specs=[pl.BlockSpec(memory_space=...]
  transfers between devices with their start and end apart: 18 -> 24, of which waited for: 10 -> 10; matrix products, arithmetic and copies ran while one was open for 0% -> 0% of each run, Pallas kernels for 19% -> 18%
where the time goes in v8:
time: 48.2 us; the launch traced here: 48 us
  starting transfers between devices  28.4 us (59%)
  Pallas kernels  10 us (21%)
  waiting for transfers between devices  8.76 us (18%)
  between operations  0.79 us (2%)
    ppermute x16, starting transfers between devices, across(): lax.ppermute(x, axes, [(i, i ^ flip) for i in range(lax.axis_size(axes))])  19.1 us
    pallas_call x15, Pallas kernels, call(): pl.pallas_call(body, out_shape=outs, in_specs=[pl.BlockSpec(memory_space=...  10 us
    ppermute x8, starting transfers between devices, swapped(): return lax.ppermute(x, ('dp', *axes), list(enumerate(partner)))  9.31 us
    ppermute x16, waiting for transfers between devices, across(): lax.ppermute(x, axes, [(i, i ^ flip) for i in range(lax.axis_size(axes))])  7.14 us
    ppermute x8, waiting for transfers between devices, swapped(): return lax.ppermute(x, ('dp', *axes), list(enumerate(partner)))  1.63 us
  transfers between devices with their start and end apart: 24, of which 10 were waited for; matrix products, arithmetic and copies ran while one was open for 0% of the time, Pallas kernels for 18%

profile of v8, /device:TPU:0, one launch (start us, length us, event | category | flops | bytes accessed | tf_op | source)
XLA Modules:
  0.0 48.0 jit_solution(6385531401961746954)
XLA Ops:
  0.7 3.0 %collective-permute-start.1 = (bf16[32,2,8,128]{3,2,1,0:T(8,128)(2,1)}, bf16[32,2,8,128]{3,2,1,0:T(8,128)(2,1)S(1)}, u32[]{:S(2)}, u32[]{:S(2)}) collective-permute-start(bf16[32,2,8,128]{3,2,1,0:T(8,128)(2,1)} %bitcast.5), channel_id=1, source_target_pairs={{0,16},{4,8},{8,4},{12,28},{16,0},{20,24},{24,20},{28,12},{1,17},{... | collective-permute-start | bytes 393224 | tf_op jit(solution)/shard_map/ppermute | solution.py:433
  3.7 1.7 %collective-permute-start = (bf16[32,2,8,128]{3,2,1,0:T(8,128)(2,1)}, bf16[32,2,8,128]{3,2,1,0:T(8,128)(2,1)S(1)}, u32[]{:S(2)}, u32[]{:S(2)}) collective-permute-start(bf16[32,2,8,128]{3,2,1,0:T(8,128)(2,1)} %bitcast.6), channel_id=1, source_target_pairs={{0,4},{4,0},{8,12},{12,8},{16,20},{20,16},{24,28},{28,24},{1,5},{5... | collective-permute-start | bytes 393224 | tf_op jit(solution)/shard_map/ppermute | solution.py:433
  5.4 1.8 %shard_map.68 = (bf16[2,128,1024]{2,1,0:T(8,128)(2,1)S(1)}, f32[2,64,1280]{2,1,0:T(8,128)S(1)}, bf16[64,1280]{1,0:T(8,128)(2,1)S(1)}, bf16[64,1280]{1,0:T(8,128)(2,1)S(1)}) custom-call(bf16[128,2,8,128]{3,2,1,0:T(8,128)(2,1)S(1)} %bitcast.8, bf16[27,64,128]{2,1,0:T(8,128)(2,1)S(1)} %bitcast.9, bf16[128,256]{1,0:T(8,128)(2,1)S(1)} %shard_map.67.blank_ref), custom_call_target="tpu_custom_call" | custom-call | flops 1100000000 | bytes 2539520 | tf_op jit(solution)/shard_map/pallas_call | solution.py:18
  7.6 1.2 %collective-permute-start.5 = (bf16[64,1280]{1,0:T(8,128)(2,1)S(1)}, bf16[64,1280]{1,0:T(8,128)(2,1)S(1)}, u32[]{:S(2)}, u32[]{:S(2)}) collective-permute-start(bf16[64,1280]{1,0:T(8,128)(2,1)S(1)} %get-tuple-element.42), channel_id=1, source_target_pairs={{0,16},{4,8},{8,4},{12,28},{16,0},{20,24},{24,20},{28,12},{1,17},{... | collective-permute-start | bytes 491528 | tf_op jit(solution)/shard_map/ppermute | solution.py:433
  9.7 1.5 %collective-permute-start.3 = (bf16[6,32,256]{2,1,0:T(8,128)(2,1)S(1)}, bf16[6,32,256]{2,1,0:T(8,128)(2,1)S(1)}, u32[]{:S(2)}, u32[]{:S(2)}) collective-permute-start(bf16[6,32,256]{2,1,0:T(8,128)(2,1)S(1)} %get-tuple-element.37), channel_id=1, source_target_pairs={{0,16},{1,2},{2,1},{3,19},{16,0},{17,18},{18,17},{19,3},{4,20},{5,... | collective-permute-start | bytes 294920 | tf_op jit(solution)/shard_map/ppermute | solution.py:433
  13.1 1.3 %collective-permute-start.11 = (bf16[2,64,128]{2,1,0:T(8,128)(2,1)S(1)}, bf16[2,64,128]{2,1,0:T(8,128)(2,1)S(1)}, u32[]{:S(2)}, u32[]{:S(2)}) collective-permute-start(bf16[2,64,128]{2,1,0:T(8,128)(2,1)S(1)} %get-tuple-element.54), channel_id=1, source_target_pairs={{0,16},{1,2},{2,1},{3,19},{16,0},{17,18},{18,17},{19,3},{4,20},{5,... | collective-permute-start | bytes 98312 | tf_op jit(solution)/shard_map/ppermute | solution.py:433
  14.4 2.6 %shard_map.72 = (bf16[4,64,1280]{2,1,0:T(8,128)(2,1)S(1)}, f32[2,64,1024]{2,1,0:T(8,128)S(1)}, bf16[6,32,1536]{2,1,0:T(8,128)(2,1)S(1)}, f32[2,2,216,128]{3,2,1,0:T(8,128)S(1)}, bf16[2,2,216,128]{3,2,1,0:T(8,128)(2,1)S(1)}) custom-call(bf16[6,32,1024]{2,1,0:T(8,128)(2,1)S(1)} %get-tuple-element.35._.deep_ref, ...), custom_call_target="tpu_custom_call" | custom-call | flops 1500000000 | bytes 5230592 | tf_op jit(solution)/shard_map/pallas_call | solution.py:18
  18.6 1.5 %collective-permute-start.7 = (bf16[216,128]{1,0:T(8,128)(2,1)S(1)}, bf16[216,128]{1,0:T(8,128)(2,1)S(1)}, u32[]{:S(2)}, u32[]{:S(2)}) collective-permute-start(bf16[216,128]{1,0:T(8,128)(2,1)S(1)} %get-tuple-element.49), channel_id=1, source_target_pairs={{0,16},{2,18},{16,0},{18,2},{1,17},{3,19},{17,1},{19,3},{4,20},{6,... | collective-permute-start | bytes 165896 | tf_op jit(solution)/shard_map/ppermute | solution.py:441
  20.2 1.0 %collective-permute-start.8 = (bf16[216,128]{1,0:T(8,128)(2,1)S(1)}, bf16[216,128]{1,0:T(8,128)(2,1)S(1)}, u32[]{:S(2)}, u32[]{:S(2)}) collective-permute-start(bf16[216,128]{1,0:T(8,128)(2,1)S(1)} %get-tuple-element.50), channel_id=1, source_target_pairs={{0,2},{2,0},{16,18},{18,16},{1,3},{3,1},{17,19},{19,17},{4,6},{6,4... | collective-permute-start | bytes 165896 | tf_op jit(solution)/shard_map/ppermute | solution.py:441
  21.1 1.1 %collective-permute-start.9 = (bf16[216,128]{1,0:T(8,128)(2,1)S(1)}, bf16[216,128]{1,0:T(8,128)(2,1)S(1)}, u32[]{:S(2)}, u32[]{:S(2)}) collective-permute-start(bf16[216,128]{1,0:T(8,128)(2,1)S(1)} %get-tuple-element.51), channel_id=1, source_target_pairs={{0,18},{2,16},{16,2},{18,0},{1,19},{3,17},{17,3},{19,1},{4,22},{6,... | collective-permute-start | bytes 165896 | tf_op jit(solution)/shard_map/ppermute | solution.py:441
  22.2 1.5 %collective-permute-start.16 = (bf16[56,128]{1,0:T(8,128)(2,1)S(1)}, bf16[56,128]{1,0:T(8,128)(2,1)S(1)}, u32[]{:S(2)}, u32[]{:S(2)}) collective-permute-start(bf16[56,128]{1,0:T(8,128)(2,1)S(1)} %get-tuple-element.58), channel_id=1, source_target_pairs={{0,16},{2,18},{16,0},{18,2},{1,17},{3,19},{17,1},{19,3},{4,20},{6,... | collective-permute-start | bytes 43016 | tf_op jit(solution)/shard_map/ppermute | solution.py:441
  23.7 1.0 %collective-permute-start.17 = (bf16[56,128]{1,0:T(8,128)(2,1)S(1)}, bf16[56,128]{1,0:T(8,128)(2,1)S(1)}, u32[]{:S(2)}, u32[]{:S(2)}) collective-permute-start(bf16[56,128]{1,0:T(8,128)(2,1)S(1)} %get-tuple-element.59), channel_id=1, source_target_pairs={{0,2},{2,0},{16,18},{18,16},{1,3},{3,1},{17,19},{19,17},{4,6},{6,4... | collective-permute-start | bytes 43016 | tf_op jit(solution)/shard_map/ppermute | solution.py:441
  24.7 1.1 %collective-permute-start.18 = (bf16[56,128]{1,0:T(8,128)(2,1)S(1)}, bf16[56,128]{1,0:T(8,128)(2,1)S(1)}, u32[]{:S(2)}, u32[]{:S(2)}) collective-permute-start(bf16[56,128]{1,0:T(8,128)(2,1)S(1)} %get-tuple-element.60), channel_id=1, source_target_pairs={{0,18},{2,16},{16,2},{18,0},{1,19},{3,17},{17,3},{19,1},{4,22},{6,... | collective-permute-start | bytes 43016 | tf_op jit(solution)/shard_map/ppermute | solution.py:441
  26.2 2.2 %collective-permute-start.15 = (bf16[216,128]{1,0:T(8,128)(2,1)S(1)}, bf16[216,128]{1,0:T(8,128)(2,1)S(1)}, u32[]{:S(2)}, u32[]{:S(2)}) collective-permute-start(bf16[216,128]{1,0:T(8,128)(2,1)S(1)} %shard_map.76.refs_3_.refs_0_), channel_id=1, source_target_pairs={{0,8},{4,12},{8,0},{12,4},{1,9},{5,13},{9,1},{13,5},{2,10},{6,14},... | collective-permute-start | bytes 165896 | tf_op jit(solution)/shard_map/ppermute | solution.py:441
  28.4 2.6 %collective-permute-start.14 = (bf16[216,128]{1,0:T(8,128)(2,1)S(1)}, bf16[216,128]{1,0:T(8,128)(2,1)S(1)}, u32[]{:S(2)}, u32[]{:S(2)}) collective-permute-start(bf16[216,128]{1,0:T(8,128)(2,1)S(1)} %shard_map.76.refs_3_.refs_0_), channel_id=1, source_target_pairs={{0,12},{4,8},{8,4},{12,0},{1,13},{5,9},{9,5},{13,1},{2,14},{6,10},... | collective-permute-start | bytes 165896 | tf_op jit(solution)/shard_map/ppermute | solution.py:441
  31.0 2.1 %collective-permute-start.21 = (bf16[56,128]{1,0:T(8,128)(2,1)S(1)}, bf16[56,128]{1,0:T(8,128)(2,1)S(1)}, u32[]{:S(2)}, u32[]{:S(2)}) collective-permute-start(bf16[56,128]{1,0:T(8,128)(2,1)S(1)} %shard_map.77.refs_4_), channel_id=1, source_target_pairs={{0,4},{4,0},{8,12},{12,8},{1,5},{5,1},{9,13},{13,9},{2,6},{6,2},{1... | collective-permute-start | bytes 43016 | tf_op jit(solution)/shard_map/ppermute | solution.py:441
  33.1 1.2 %collective-permute-start.20 = (bf16[56,128]{1,0:T(8,128)(2,1)S(1)}, bf16[56,128]{1,0:T(8,128)(2,1)S(1)}, u32[]{:S(2)}, u32[]{:S(2)}) collective-permute-start(bf16[56,128]{1,0:T(8,128)(2,1)S(1)} %shard_map.77.refs_4_), channel_id=1, source_target_pairs={{0,8},{4,12},{8,0},{12,4},{1,9},{5,13},{9,1},{13,5},{2,10},{6,14},... | collective-permute-start | bytes 43016 | tf_op jit(solution)/shard_map/ppermute | solution.py:441
  34.3 1.1 %collective-permute-done.21.refs_7_ = bf16[56,128]{1,0:T(8,128)(2,1)S(1)} collective-permute-done((bf16[56,128]{1,0:T(8,128)(2,1)S(1)}, bf16[56,128]{1,0:T(8,128)(2,1)S(1)}, u32[]{:S(2)}, u32[]{:S(2)}) %collective-permute-start.21) | collective-permute-done | bytes 14368 | tf_op jit(solution)/shard_map/ppermute | solution.py:441
  35.4 2.0 %collective-permute-start.19 = (bf16[56,128]{1,0:T(8,128)(2,1)S(1)}, bf16[56,128]{1,0:T(8,128)(2,1)S(1)}, u32[]{:S(2)}, u32[]{:S(2)}) collective-permute-start(bf16[56,128]{1,0:T(8,128)(2,1)S(1)} %shard_map.77.refs_4_), channel_id=1, source_target_pairs={{0,12},{4,8},{8,4},{12,0},{1,13},{5,9},{9,5},{13,1},{2,14},{6,10},... | collective-permute-start | bytes 43016 | tf_op jit(solution)/shard_map/ppermute | solution.py:441
  37.7 3.2 %collective-permute-done.19.refs_5_ = bf16[56,128]{1,0:T(8,128)(2,1)S(1)} collective-permute-done((bf16[56,128]{1,0:T(8,128)(2,1)S(1)}, bf16[56,128]{1,0:T(8,128)(2,1)S(1)}, u32[]{:S(2)}, u32[]{:S(2)}) %collective-permute-start.19) | collective-permute-done | bytes 14368 | tf_op jit(solution)/shard_map/ppermute | solution.py:441
  41.0 1.2 %collective-permute-start.22 = (bf16[272,128]{1,0:T(8,128)(2,1)S(1)}, bf16[272,128]{1,0:T(8,128)(2,1)S(1)}, u32[]{:S(2)}, u32[]{:S(2)}) collective-permute-start(bf16[272,128]{1,0:T(8,128)(2,1)S(1)} %shard_map.78._.own_ref), channel_id=1, source_target_pairs={{0,2},{2,0},{1,3},{3,1},{4,6},{6,4},{5,7},{7,5},{8,10},{10,8},{9,1... | collective-permute-start | bytes 208904 | tf_op jit(solution)/shard_map/ppermute | solution.py:441
  42.2 2.5 %shard_map.79 = (bf16[128,2,8,128]{3,2,1,0:T(8,128)(2,1)}, f32[8,128]{1,0:T(8,128)S(1)}) custom-call(bf16[4,64,1280]{2,1,0:T(8,128)(2,1)S(1)} %get-tuple-element.44.hidden_ref, bf16[27,64,128]{2,1,0:T(8,128)(2,1)S(1)} %bitcast.10, bf16[272,128]{1,0:T(8,128)(2,1)S(1)} %shard_map.78._.own_ref), custom_call_target="tpu_custom_call" | custom-call | flops 900000000 | bytes 1695744 | tf_op jit(solution)/shard_map/pallas_call | solution.py:18
  45.5 1.3 %collective-permute-done.23.got_ref = bf16[2,272,128]{2,1,0:T(8,128)(2,1)S(1)} collective-permute-done((bf16[2,272,128]{2,1,0:T(8,128)(2,1)S(1)}, bf16[2,272,128]{2,1,0:T(8,128)(2,1)S(1)}, u32[]{:S(2)}, u32[]{:S(2)}) %collective-permute-start.23) | collective-permute-done | bytes 139296 | tf_op jit(solution)/shard_map/ppermute | solution.py:441
  46.8 1.2 %shard_map.81 = (f32[27,32,32]{2,1,0:T(8,128)}, f32[27,64,64]{2,1,0:T(8,128)}) custom-call(bf16[2,272,128]{2,1,0:T(8,128)(2,1)S(1)} %shard_map.80.own_ref, bf16[2,272,128]{2,1,0:T(8,128)(2,1)S(1)} %collective-permute-done.23.got_ref), custom_call_target="tpu_custom_call" | custom-call | bytes 831488 | tf_op jit(solution)/shard_map/pallas_call | solution.py:18
  (47 shorter events, 6.3 us)
Async XLA Ops:
  0.7 8.1 %collective-permute-start.1 = (bf16[32,2,8,128]{3,2,1,0:T(8,128)(2,1)}, bf16[32,2,8,128]{3,2,1,0:T(8,128)(2,1)S(1)}, u32[]{:S(2)}, u32[]{:S(2)}) collective-permute-start(bf16[32,2,8,128]{3,2,1,0:T(8,128)(2,1)} %bitcast.5), channel_id=1, source_target_pairs={{0,16},{4,8},{8,4},{12,28},{16,0},{20,24},{24,20},{28,12},{1,17},{... | collective-permute-start | bytes 393224 | tf_op jit(solution)/shard_map/ppermute | solution.py:433
  3.7 5.6 %collective-permute-start = (bf16[32,2,8,128]{3,2,1,0:T(8,128)(2,1)}, bf16[32,2,8,128]{3,2,1,0:T(8,128)(2,1)S(1)}, u32[]{:S(2)}, u32[]{:S(2)}) collective-permute-start(bf16[32,2,8,128]{3,2,1,0:T(8,128)(2,1)} %bitcast.6), channel_id=1, source_target_pairs={{0,4},{4,0},{8,12},{12,8},{16,20},{20,16},{24,28},{28,24},{1,5},{5... | collective-permute-start | bytes 393224 | tf_op jit(solution)/shard_map/ppermute | solution.py:433
  7.1 5.4 %collective-permute-start.4 = (bf16[64,1280]{1,0:T(8,128)(2,1)S(1)}, bf16[64,1280]{1,0:T(8,128)(2,1)S(1)}, u32[]{:S(2)}, u32[]{:S(2)}) collective-permute-start(bf16[64,1280]{1,0:T(8,128)(2,1)S(1)} %get-tuple-element.41), channel_id=1, source_target_pairs={{0,4},{4,0},{8,12},{12,8},{16,20},{20,16},{24,28},{28,24},{1,5},{5... | collective-permute-start | bytes 491528 | tf_op jit(solution)/shard_map/ppermute | solution.py:433
  7.6 5.3 %collective-permute-start.5 = (bf16[64,1280]{1,0:T(8,128)(2,1)S(1)}, bf16[64,1280]{1,0:T(8,128)(2,1)S(1)}, u32[]{:S(2)}, u32[]{:S(2)}) collective-permute-start(bf16[64,1280]{1,0:T(8,128)(2,1)S(1)} %get-tuple-element.42), channel_id=1, source_target_pairs={{0,16},{4,8},{8,4},{12,28},{16,0},{20,24},{24,20},{28,12},{1,17},{... | collective-permute-start | bytes 491528 | tf_op jit(solution)/shard_map/ppermute | solution.py:433
  9.7 4.7 %collective-permute-start.2 = (bf16[6,32,256]{2,1,0:T(8,128)(2,1)S(1)}, bf16[6,32,256]{2,1,0:T(8,128)(2,1)S(1)}, u32[]{:S(2)}, u32[]{:S(2)}) collective-permute-start(bf16[6,32,256]{2,1,0:T(8,128)(2,1)S(1)} %get-tuple-element.36), channel_id=1, source_target_pairs={{0,1},{1,0},{2,3},{3,2},{16,17},{17,16},{18,19},{19,18},{4,5},{5,4... | collective-permute-start | bytes 294920 | tf_op jit(solution)/shard_map/ppermute | solution.py:433
  9.7 4.7 %collective-permute-start.3 = (bf16[6,32,256]{2,1,0:T(8,128)(2,1)S(1)}, bf16[6,32,256]{2,1,0:T(8,128)(2,1)S(1)}, u32[]{:S(2)}, u32[]{:S(2)}) collective-permute-start(bf16[6,32,256]{2,1,0:T(8,128)(2,1)S(1)} %get-tuple-element.37), channel_id=1, source_target_pairs={{0,16},{1,2},{2,1},{3,19},{16,0},{17,18},{18,17},{19,3},{4,20},{5,... | collective-permute-start | bytes 294920 | tf_op jit(solution)/shard_map/ppermute | solution.py:433
  13.0 4.5 %collective-permute-start.10 = (bf16[2,64,128]{2,1,0:T(8,128)(2,1)S(1)}, bf16[2,64,128]{2,1,0:T(8,128)(2,1)S(1)}, u32[]{:S(2)}, u32[]{:S(2)}) collective-permute-start(bf16[2,64,128]{2,1,0:T(8,128)(2,1)S(1)} %get-tuple-element.53), channel_id=1, source_target_pairs={{0,1},{1,0},{2,3},{3,2},{16,17},{17,16},{18,19},{19,18},{4,5},{5,4... | collective-permute-start | bytes 98312 | tf_op jit(solution)/shard_map/ppermute | solution.py:433
  13.1 4.4 %collective-permute-start.11 = (bf16[2,64,128]{2,1,0:T(8,128)(2,1)S(1)}, bf16[2,64,128]{2,1,0:T(8,128)(2,1)S(1)}, u32[]{:S(2)}, u32[]{:S(2)}) collective-permute-start(bf16[2,64,128]{2,1,0:T(8,128)(2,1)S(1)} %get-tuple-element.54), channel_id=1, source_target_pairs={{0,16},{1,2},{2,1},{3,19},{16,0},{17,18},{18,17},{19,3},{4,20},{5,... | collective-permute-start | bytes 98312 | tf_op jit(solution)/shard_map/ppermute | solution.py:433
  17.0 1.5 %collective-permute-start.6 = (bf16[2,2,216,128]{3,2,1,0:T(8,128)(2,1)S(1)}, bf16[2,2,216,128]{3,2,1,0:T(8,128)(2,1)S(1)}, u32[]{:S(2)}, u32[]{:S(2)}) collective-permute-start(bf16[2,2,216,128]{3,2,1,0:T(8,128)(2,1)S(1)} %get-tuple-element.46), channel_id=1, source_target_pairs={{0,1},{1,0},{2,3},{3,2},{4,5},{5,4},{6,7},{7,6},{8,9},{9,8},{10,11... | collective-permute-start | bytes 663560 | tf_op jit(solution)/shard_map/ppermute | solution.py:441
  18.2 4.0 %collective-permute-start.12 = (bf16[2,2,56,128]{3,2,1,0:T(8,128)(2,1)S(1)}, bf16[2,2,56,128]{3,2,1,0:T(8,128)(2,1)S(1)}, u32[]{:S(2)}, u32[]{:S(2)}) collective-permute-start(bf16[2,2,56,128]{3,2,1,0:T(8,128)(2,1)S(1)} %get-tuple-element.56), channel_id=1, source_target_pairs={{0,1},{1,0},{2,3},{3,2},{4,5},{5,4},{6,7},{7,6},{8,9},{9,8},{10,11... | collective-permute-start | bytes 172040 | tf_op jit(solution)/shard_map/ppermute | solution.py:441
  18.6 6.1 %collective-permute-start.7 = (bf16[216,128]{1,0:T(8,128)(2,1)S(1)}, bf16[216,128]{1,0:T(8,128)(2,1)S(1)}, u32[]{:S(2)}, u32[]{:S(2)}) collective-permute-start(bf16[216,128]{1,0:T(8,128)(2,1)S(1)} %get-tuple-element.49), channel_id=1, source_target_pairs={{0,16},{2,18},{16,0},{18,2},{1,17},{3,19},{17,1},{19,3},{4,20},{6,... | collective-permute-start | bytes 165896 | tf_op jit(solution)/shard_map/ppermute | solution.py:441
  20.2 5.6 %collective-permute-start.8 = (bf16[216,128]{1,0:T(8,128)(2,1)S(1)}, bf16[216,128]{1,0:T(8,128)(2,1)S(1)}, u32[]{:S(2)}, u32[]{:S(2)}) collective-permute-start(bf16[216,128]{1,0:T(8,128)(2,1)S(1)} %get-tuple-element.50), channel_id=1, source_target_pairs={{0,2},{2,0},{16,18},{18,16},{1,3},{3,1},{17,19},{19,17},{4,6},{6,4... | collective-permute-start | bytes 165896 | tf_op jit(solution)/shard_map/ppermute | solution.py:441
  21.1 5.1 %collective-permute-start.9 = (bf16[216,128]{1,0:T(8,128)(2,1)S(1)}, bf16[216,128]{1,0:T(8,128)(2,1)S(1)}, u32[]{:S(2)}, u32[]{:S(2)}) collective-permute-start(bf16[216,128]{1,0:T(8,128)(2,1)S(1)} %get-tuple-element.51), channel_id=1, source_target_pairs={{0,18},{2,16},{16,2},{18,0},{1,19},{3,17},{17,3},{19,1},{4,22},{6,... | collective-permute-start | bytes 165896 | tf_op jit(solution)/shard_map/ppermute | solution.py:441
  22.2 8.8 %collective-permute-start.16 = (bf16[56,128]{1,0:T(8,128)(2,1)S(1)}, bf16[56,128]{1,0:T(8,128)(2,1)S(1)}, u32[]{:S(2)}, u32[]{:S(2)}) collective-permute-start(bf16[56,128]{1,0:T(8,128)(2,1)S(1)} %get-tuple-element.58), channel_id=1, source_target_pairs={{0,16},{2,18},{16,0},{18,2},{1,17},{3,19},{17,1},{19,3},{4,20},{6,... | collective-permute-start | bytes 43016 | tf_op jit(solution)/shard_map/ppermute | solution.py:441
  23.7 7.3 %collective-permute-start.17 = (bf16[56,128]{1,0:T(8,128)(2,1)S(1)}, bf16[56,128]{1,0:T(8,128)(2,1)S(1)}, u32[]{:S(2)}, u32[]{:S(2)}) collective-permute-start(bf16[56,128]{1,0:T(8,128)(2,1)S(1)} %get-tuple-element.59), channel_id=1, source_target_pairs={{0,2},{2,0},{16,18},{18,16},{1,3},{3,1},{17,19},{19,17},{4,6},{6,4... | collective-permute-start | bytes 43016 | tf_op jit(solution)/shard_map/ppermute | solution.py:441
  24.7 6.3 %collective-permute-start.18 = (bf16[56,128]{1,0:T(8,128)(2,1)S(1)}, bf16[56,128]{1,0:T(8,128)(2,1)S(1)}, u32[]{:S(2)}, u32[]{:S(2)}) collective-permute-start(bf16[56,128]{1,0:T(8,128)(2,1)S(1)} %get-tuple-element.60), channel_id=1, source_target_pairs={{0,18},{2,16},{16,2},{18,0},{1,19},{3,17},{17,3},{19,1},{4,22},{6,... | collective-permute-start | bytes 43016 | tf_op jit(solution)/shard_map/ppermute | solution.py:441
  26.2 14.7 %collective-permute-start.15 = (bf16[216,128]{1,0:T(8,128)(2,1)S(1)}, bf16[216,128]{1,0:T(8,128)(2,1)S(1)}, u32[]{:S(2)}, u32[]{:S(2)}) collective-permute-start(bf16[216,128]{1,0:T(8,128)(2,1)S(1)} %shard_map.76.refs_3_.refs_0_), channel_id=1, source_target_pairs={{0,8},{4,12},{8,0},{12,4},{1,9},{5,13},{9,1},{13,5},{2,10},{6,14},... | collective-permute-start | bytes 165896 | tf_op jit(solution)/shard_map/ppermute | solution.py:441
  28.4 12.6 %collective-permute-start.14 = (bf16[216,128]{1,0:T(8,128)(2,1)S(1)}, bf16[216,128]{1,0:T(8,128)(2,1)S(1)}, u32[]{:S(2)}, u32[]{:S(2)}) collective-permute-start(bf16[216,128]{1,0:T(8,128)(2,1)S(1)} %shard_map.76.refs_3_.refs_0_), channel_id=1, source_target_pairs={{0,12},{4,8},{8,4},{12,0},{1,13},{5,9},{9,5},{13,1},{2,14},{6,10},... | collective-permute-start | bytes 165896 | tf_op jit(solution)/shard_map/ppermute | solution.py:441
  31.0 9.9 %collective-permute-start.13 = (bf16[216,128]{1,0:T(8,128)(2,1)S(1)}, bf16[216,128]{1,0:T(8,128)(2,1)S(1)}, u32[]{:S(2)}, u32[]{:S(2)}) collective-permute-start(bf16[216,128]{1,0:T(8,128)(2,1)S(1)} %shard_map.76.refs_3_.refs_0_), channel_id=1, source_target_pairs={{0,4},{4,0},{8,12},{12,8},{1,5},{5,1},{9,13},{13,9},{2,6},{6,2},{1... | collective-permute-start | bytes 165896 | tf_op jit(solution)/shard_map/ppermute | solution.py:441
  31.0 4.4 %collective-permute-start.21 = (bf16[56,128]{1,0:T(8,128)(2,1)S(1)}, bf16[56,128]{1,0:T(8,128)(2,1)S(1)}, u32[]{:S(2)}, u32[]{:S(2)}) collective-permute-start(bf16[56,128]{1,0:T(8,128)(2,1)S(1)} %shard_map.77.refs_4_), channel_id=1, source_target_pairs={{0,4},{4,0},{8,12},{12,8},{1,5},{5,1},{9,13},{13,9},{2,6},{6,2},{1... | collective-permute-start | bytes 43016 | tf_op jit(solution)/shard_map/ppermute | solution.py:441
  33.1 4.6 %collective-permute-start.20 = (bf16[56,128]{1,0:T(8,128)(2,1)S(1)}, bf16[56,128]{1,0:T(8,128)(2,1)S(1)}, u32[]{:S(2)}, u32[]{:S(2)}) collective-permute-start(bf16[56,128]{1,0:T(8,128)(2,1)S(1)} %shard_map.77.refs_4_), channel_id=1, source_target_pairs={{0,8},{4,12},{8,0},{12,4},{1,9},{5,13},{9,1},{13,5},{2,10},{6,14},... | collective-permute-start | bytes 43016 | tf_op jit(solution)/shard_map/ppermute | solution.py:441
  35.4 5.5 %collective-permute-start.19 = (bf16[56,128]{1,0:T(8,128)(2,1)S(1)}, bf16[56,128]{1,0:T(8,128)(2,1)S(1)}, u32[]{:S(2)}, u32[]{:S(2)}) collective-permute-start(bf16[56,128]{1,0:T(8,128)(2,1)S(1)} %shard_map.77.refs_4_), channel_id=1, source_target_pairs={{0,12},{4,8},{8,4},{12,0},{1,13},{5,9},{9,5},{13,1},{2,14},{6,10},... | collective-permute-start | bytes 43016 | tf_op jit(solution)/shard_map/ppermute | solution.py:441
  41.0 4.4 %collective-permute-start.22 = (bf16[272,128]{1,0:T(8,128)(2,1)S(1)}, bf16[272,128]{1,0:T(8,128)(2,1)S(1)}, u32[]{:S(2)}, u32[]{:S(2)}) collective-permute-start(bf16[272,128]{1,0:T(8,128)(2,1)S(1)} %shard_map.78._.own_ref), channel_id=1, source_target_pairs={{0,2},{2,0},{1,3},{3,1},{4,6},{6,4},{5,7},{7,5},{8,10},{10,8},{9,1... | collective-permute-start | bytes 208904 | tf_op jit(solution)/shard_map/ppermute | solution.py:441
  45.4 1.4 %collective-permute-start.23 = (bf16[2,272,128]{2,1,0:T(8,128)(2,1)S(1)}, bf16[2,272,128]{2,1,0:T(8,128)(2,1)S(1)}, u32[]{:S(2)}, u32[]{:S(2)}) collective-permute-start(bf16[2,272,128]{2,1,0:T(8,128)(2,1)S(1)} %shard_map.80.own_ref), channel_id=1, source_target_pairs={{0,1},{1,0},{2,3},{3,2},{4,5},{5,4},{6,7},{7,6},{8,9},{9,8},{10,11... | collective-permute-start | bytes 417800 | tf_op jit(solution)/shard_map/ppermute | solution.py:441
  (4 other events, 19.2 us)

commit v9 on v8

--- a/solution.py
+++ b/solution.py
@@ -59,7 +59,7 @@
     out_ref[...] = jnp.zeros(out_ref.shape, BF)
 
 
-def spread_kernel(cot_ref, k2_ref, blank_ref, cot_rows_ref, back_ref, one_ref, two_ref, scratch):
+def spread_kernel(cot_ref, k2_ref, blank_ref, cot_rows_ref, back_ref, scratch):
     out, depth, height, _ = cot_ref.shape
     rows = [[None] * height for _ in range(depth)]
 
@@ -71,8 +71,6 @@
     mid = k2_ref.shape[1]
     none = blank_ref[...]
     padded = [jnp.concatenate([none, *rows[d], none], axis=1) for d in range(depth)]
-    is_odd = odd("dep")
-    faces = [[], []]
     for e in range(depth + 2):
         reached = [(d, e - 1 - d) for d in range(depth) if abs(e - 1 - d) <= 1]
         w = jnp.concatenate(
@@ -89,13 +87,7 @@
             )
             y = jnp.dot(w, rhs, preferred_element_type=F32)
             back = sum(moved_along_width(y[n * mid : (n + 1) * mid], n - 1) for n in range(3))
-            if 0 < e < depth + 1:
-                back_ref[e - 1, :, j * LANES : (j + 2) * LANES] = back
-            else:
-                faces[e > 0].append(back.astype(BF))
-    low, high = (jnp.concatenate(face, axis=1) for face in faces)
-    one_ref[...] = jnp.where(is_odd, low, high)
-    two_ref[...] = jnp.where(is_odd, high, low)
+            back_ref[e, :, j * LANES : (j + 2) * LANES] = back
 
 
 def as_matrix(ref, c):
@@ -141,25 +133,6 @@
     send_two_ref[...] = jnp.where(is_odd, last, first)
 
 
-def back_rim_kernel(own_ref, one_ref, two_ref, back_ref, send_one_ref, send_two_ref):
-    before, after = sides("dep", one_ref[...], two_ref[...])
-    last = own_ref.shape[0] - 1
-    cells = back_ref.shape[2]
-    ends = []
-    for d in range(last + 1):
-        total = own_ref[d]
-        if d == 0:
-            total = total + before.astype(F32)
-        if d == last:
-            total = total + after.astype(F32)
-        back_ref[d] = total[:, LANES : LANES + cells]
-        ends.append((total[:, :LANES].astype(BF), total[:, LANES + cells :].astype(BF)))
-    is_odd = odd(HGT)
-    for d, (low, high) in enumerate(ends):
-        send_one_ref[d] = jnp.where(is_odd, low, high)
-        send_two_ref[d] = jnp.where(is_odd, high, low)
-
-
 def widened(deep_ref, one_ref, two_ref):
     left, right = sides(HGT, one_ref[...], two_ref[...])
     return [jnp.concatenate([left[d], deep_ref[d], right[d]], axis=1) for d in range(deep_ref.shape[0])]
@@ -189,11 +162,11 @@
         for half in range(halves):
             one, two = (quarter(2 * half + c) for c in range(2))
             keep_ref[part, half] = jnp.where(core, two, one)
-            send_ref[part, half] = jnp.where(core, one, two).astype(BF)
+            send_ref[part, half] = jnp.where(core, one, two)
 
 
 def hidden_kernel(
-    direct, deep_ref, one_ref, two_ref, w1_ref, moved_ref, _, hidden_ref, slope_ref, rows_ref, *grad_refs
+    direct, deep_ref, one_ref, two_ref, w1_ref, moved_ref, hidden_ref, slope_ref, rows_ref, *grad_refs
 ):
     for d, row in enumerate(widened(deep_ref, one_ref, two_ref)):
         rows_ref[d] = row
@@ -215,6 +188,7 @@
                 lanes = slice(r * LANES, (r + 1) * LANES)
                 p, q = pre[:, lanes], s[:, lanes]
                 value = (p * q).astype(BF)
+                slope = q * (1.0 + p * (1.0 - q))
                 outside = []
                 if d == 0:
                     outside.append(dep == 0)
@@ -226,10 +200,10 @@
                     outside.append(hgt == hgts - 1)
                 for far in outside:
                     value = jnp.where(far, jnp.zeros_like(value), value)
-                hidden_ref[d, :, (h + r) * LANES : (h + r + 1) * LANES] = value
-                if 0 < d < depth - 1 and 0 < h + r < height - 1:
-                    at = (h + r - 1) * LANES
-                    slope_ref[d - 1, :, at : at + LANES] = q * (1.0 + p * (1.0 - q))
+                    slope = jnp.where(far, jnp.zeros_like(slope), slope)
+                at = slice((h + r) * LANES, (h + r + 1) * LANES)
+                hidden_ref[d, :, at] = value
+                slope_ref[d, :, at] = slope
     cells = (height - 2) * LANES
     own = depth - 2
     out = moved_ref.shape[1] // 3
@@ -267,7 +241,7 @@
     pack(direct, blocks, grad_refs, units_of)
 
 
-def features_kernel(hidden_ref, k2_ref, _, out_ref, token_ref, scratch):
+def features_kernel(hidden_ref, k2_ref, out_ref, token_ref, scratch):
     out, depth, height, _ = out_ref.shape
     w2 = jnp.concatenate([as_matrix(k2_ref, c) for c in range(3)], axis=0)
     for d in range(depth):
@@ -289,18 +263,12 @@
     token_ref[...] = scratch[:8]
 
 
-def delta_kernel(direct, rows_ref, back_ref, one_ref, two_ref, slope_ref, *outs_and_scratch):
+def delta_kernel(direct, rows_ref, back_ref, slope_ref, *outs_and_scratch):
     *grad_refs, delta_ref = outs_and_scratch
-    before, after = sides(HGT, one_ref[...], two_ref[...])
-    own, mid, cells = slope_ref.shape
-    for d in range(own):
+    depth, mid, cells = slope_ref.shape
+    for d in range(depth):
         for at in range(0, cells, LANES):
-            back = back_ref[d, :, at : at + LANES]
-            if at == 0:
-                back = back + before[d].astype(F32)
-            if at == cells - LANES:
-                back = back + after[d].astype(F32)
-            delta = back * slope_ref[d, :, at : at + LANES]
+            delta = back_ref[d, :, at : at + LANES] * slope_ref[d, :, at : at + LANES]
             for n in range(3):
                 delta_ref[n * mid : (n + 1) * mid, d * cells + at : d * cells + at + LANES] = moved_along_width(
                     delta, n - 1
@@ -314,12 +282,12 @@
             [
                 jnp.concatenate(
                     [
-                        rows_ref[d + 1 + ab // 3, :, (1 + ab % 3) * LANES : (1 + ab % 3) * LANES + cells]
+                        rows_ref[d + ab // 3, :, (ab % 3) * LANES : (ab % 3) * LANES + cells]
                         for ab in group
                     ],
                     axis=0,
                 )
-                for d in range(own)
+                for d in range(depth)
             ],
             axis=1,
         )
@@ -337,13 +305,14 @@
     pack(direct, blocks, grad_refs, lambda part: [block[part * size : (part + 1) * size] for block in blocks])
 
 
-def plane_kernel(moves, keep_ref, got_ref, _, kept_ref, *send_refs):
-    part = lax.rem(lax.axis_index("dp"), keep_ref.shape[0])
+def plane_kernel(moves, *refs):
+    keep_second, got_second, keep_first, got_first, kept_ref, *send_refs = refs
+    part = lax.rem(lax.axis_index("dp"), keep_first.shape[0])
     half = lax.axis_index("y")
 
     def total(x, y):
         at = 1 - part if x else part, 1 - half if y else half
-        return keep_ref[at] + got_ref[at].astype(F32)
+        return jnp.concatenate([keep_second[at] + got_second[at], keep_first[at] + got_first[at]], axis=0)
 
     kept_ref[...] = total(0, 0)
     for (x, y), send_ref in zip(moves, send_refs, strict=True):
@@ -351,23 +320,20 @@
 
 
 def total_kernel(kept_ref, *refs):
-    *got_refs, _, out_ref = refs
+    *got_refs, out_ref = refs
     value = kept_ref[...]
     for ref in got_refs:
         value = value + ref[...].astype(F32)
     out_ref[...] = value.astype(BF)
 
 
-def depth_kernel(*refs):
-    *in_refs, out_ref = refs
-    sums = []
-    for n in range(0, len(in_refs), 4):
-        a, b, c, d = (ref[...].astype(F32) for ref in in_refs[n : n + 4])
-        sums.append((a + b) + (c + d))
-    out_ref[...] = jnp.concatenate(sums, axis=0).astype(BF)
-
-
-def order_kernel(own_ref, got_ref, _, out_ref):
+def depth_kernel(a_ref, b_ref, c_ref, d_ref, _, out_ref):
+    one = a_ref[...].astype(F32) + b_ref[...].astype(F32)
+    two = c_ref[...].astype(F32) + d_ref[...].astype(F32)
+    out_ref[...] = (one + two).astype(BF)
+
+
+def order_kernel(own_ref, got_ref, out_ref):
     mine = lax.axis_index("y")
     out_ref[mine] = own_ref[...]
     out_ref[1 - mine] = got_ref[...]
@@ -448,7 +414,7 @@
     grad = lax.psum_scatter(grad, "dp", scatter_dimension=0, tiled=True).reshape(1, halves, 2, length, LANES)
     core = lax.axis_index("core")
     keep, send = (lax.dynamic_index_in_dim(grad, at, 2, False) for at in (core, 1 - core))
-    return keep, send.astype(BF)
+    return keep, send
 
 
 def per_device(volume, kernel_first, kernel_second, cotangent):
@@ -461,13 +427,11 @@
 
     one, two = swapped(volume[0], "dep", 0), swapped(volume[0], "dep", 1)
     (blank,) = call(blank_kernel, [shape((out, 2 * width), BF)], [], flops=3_000_000_000)
-    cot_rows, back, back_one, back_two = call(
+    cot_rows, back = call(
         spread_kernel,
         [
             shape((depth, out, cells), BF),
-            shape((depth, mid, cells + 2 * width), F32),
-            shape((mid, cells + 2 * width), BF),
-            shape((mid, cells + 2 * width), BF),
+            shape((depth + 2, mid, cells + 2 * width), F32),
         ],
         [cotangent[0], k2, blank],
         [pltpu.VMEM((out * rows, width), F32)],
@@ -486,14 +450,6 @@
         [cot_rows, k1, deep],
         flops=500_000_000,
     )
-    back_one, back_two = swapped(back_one, "dep", 0), swapped(back_two, "dep", 1)
-    back, back_one, back_two = call(
-        back_rim_kernel,
-        [shape((depth, mid, cells), F32)] + [shape((depth, mid, width), BF)] * 2,
-        [back, back_one, back_two],
-    )
-    back_one, back_two = swapped(back_one, HGT, 0), swapped(back_two, HGT, 1)
-
     size = mid // parts
     direct = parts == 2 and size % 16 == 0
     halves = lax.axis_size("y")
@@ -502,24 +458,24 @@
         functools.partial(hidden_kernel, direct),
         [
             shape((depth + 2, mid, cells + 2 * width), BF),
-            shape((depth, mid, cells), F32),
+            shape((depth + 2, mid, cells + 2 * width), F32),
             shape((3 * depth, inner, cells + 4 * width), BF),
         ]
         + (
-            [shape((parts, halves, length_second, width), kind) for kind in (F32, BF)]
+            [shape((parts, halves, length_second, width), F32) for _ in range(2)]
             if direct
             else [shape((14, out, LANES), F32)]
         ),
-        [deep, one, two, w1, moved, back],
+        [deep, one, two, w1, moved],
         flops=1_500_000_000,
     )
     first = call(
         functools.partial(delta_kernel, direct),
-        [shape((parts, halves, length_first, width), kind) for kind in (F32, BF)]
+        [shape((parts, halves, length_first, width), F32) for _ in range(2)]
         if direct
         else [shape((7, mid, LANES), F32)],
-        [wide, back, back_one, back_two, slope],
-        [pltpu.VMEM((3 * mid, depth * cells), BF)],
+        [wide, back, slope],
+        [pltpu.VMEM((3 * mid, (depth + 2) * (cells + 2 * width)), BF)],
         flops=4_000_000_000,
     )
     if direct:
@@ -531,35 +487,24 @@
         units = jnp.concatenate([blocks[:, :13].reshape(parts, 26, size, LANES), tail[:, None]], axis=1)
         second = scattered(units, length_second)
         first = scattered(jnp.swapaxes(first[0].reshape(7, parts, size, LANES), 0, 1), length_first)
-    grads = []
-    after = slope
-    for keep, send in (second, first):
-        block = keep.shape[2:]
-        kept, *sends = call(
-            functools.partial(plane_kernel, moves),
-            [shape(block, F32)] + [shape(block, BF)] * len(moves),
-            [keep, across(send, ("core", 1)), after],
-        )
-        after = kept
-        grads.append((kept, [across(send, ("dp", x), ("y", y)) for send, (x, y) in zip(sends, moves, strict=True)]))
-    shares, weights, orders = [], (0, 4_000_000_000), ((1, 3, 2), (3, 2, 1))
-    for (kept, gots), weight, order in zip(grads, weights, orders, strict=True):
-        (share,) = call(total_kernel, [shape(kept.shape, BF)], [kept, *gots, after], flops=weight)
-        after = share
-        shares.append((share, [across(share, ("dep", bits)) for bits in order]))
-    (share,) = call(
-        depth_kernel,
-        [shape((length_second + length_first, width), BF)],
-        [x for share, gots in shares for x in (share, *gots)],
-    )
+    block = (length_second + length_first, width)
+    kept, *sends = call(
+        functools.partial(plane_kernel, moves),
+        [shape(block, F32)] + [shape(block, BF)] * len(moves),
+        [x for keep, send in (second, first) for x in (keep, across(send, ("core", 1)))],
+    )
+    gots = [across(send, ("dp", x), ("y", y)) for send, (x, y) in zip(sends, moves, strict=True)]
+    (share,) = call(total_kernel, [shape(block, BF)], [kept, *gots])
     features, token = call(
         features_kernel,
         [shape(cotangent.shape[1:], BF), shape((8, width), F32)],
-        [hidden, k2, share],
+        [hidden, k2],
         [pltpu.VMEM((out * rows, width), F32)],
         flops=900_000_000,
     )
-    (own,) = call(order_kernel, [shape((halves, *share.shape), BF)], [share, across(share, ("y", 1)), token])
+    gots = [across(share, ("dep", bits)) for bits in (1, 2, 3)]
+    (share,) = call(depth_kernel, [shape(block, BF)], [share, *gots, token])
+    (own,) = call(order_kernel, [shape((halves, *block), BF)], [share, across(share, ("y", 1))])
     grad_first, grad_second = call(
         functools.partial(unpack_kernel, length_second),
         [shape((27, size, inner), F32), shape((27, 2 * size, mid), F32)],

time: 48.2 us -> 43.4 us (0.900)
  starting transfers between devices: 28.4 us -> 16 us
  waiting for transfers between devices: 8.76 us -> 15.7 us
  Pallas kernels: 10 us -> 10.8 us
    ppermute x16 -> x10, starting transfers between devices: 19.1 us -> 9.79 us  [across(): lax.ppermute(x, axes, [(i, i ^ flip) for i in range(lax.axis_size(axes))])]
    ppermute x16 -> x10, waiting for transfers between devices: 7.14 us -> 11.2 us  [across(): lax.ppermute(x, axes, [(i, i ^ flip) for i in range(lax.axis_size(axes))])]
    ppermute x8 -> x4, starting transfers between devices: 9.31 us -> 6.23 us  [swapped(): return lax.ppermute(x, ('dp', *axes), list(enumerate(partner)))]
    ppermute x8 -> x4, waiting for transfers between devices: 1.63 us -> 4.43 us  [swapped(): return lax.ppermute(x, ('dp', *axes), list(enumerate(partner)))]
    pallas_call x15 -> x12, Pallas kernels: 10 us -> 10.8 us  [call(): pl.pallas_call(body, out_shape=outs, in_specs=[pl.BlockSpec(memory_space=...]
  transfers between devices with their start and end apart: 24 -> 14, of which waited for: 10 -> 10; matrix products, arithmetic and copies ran while one was open for 0% -> 0% of each run, Pallas kernels for 18% -> 15%
where the time goes in v9:
time: 43.4 us; the launch traced here: 43.2 us
  starting transfers between devices  16 us (37%)
  waiting for transfers between devices  15.7 us (36%)
  Pallas kernels  10.8 us (25%)
  between operations  0.75 us (2%)
    ppermute x10, waiting for transfers between devices, across(): lax.ppermute(x, axes, [(i, i ^ flip) for i in range(lax.axis_size(axes))])  11.2 us
    pallas_call x12, Pallas kernels, call(): pl.pallas_call(body, out_shape=outs, in_specs=[pl.BlockSpec(memory_space=...  10.8 us
    ppermute x10, starting transfers between devices, across(): lax.ppermute(x, axes, [(i, i ^ flip) for i in range(lax.axis_size(axes))])  9.79 us
    ppermute x4, starting transfers between devices, swapped(): return lax.ppermute(x, ('dp', *axes), list(enumerate(partner)))  6.23 us
    ppermute x4, waiting for transfers between devices, swapped(): return lax.ppermute(x, ('dp', *axes), list(enumerate(partner)))  4.43 us
  transfers between devices with their start and end apart: 14, of which 10 were waited for; matrix products, arithmetic and copies ran while one was open for 0% of the time, Pallas kernels for 15%

profile of v9, /device:TPU:0, one launch (start us, length us, event | category | flops | bytes accessed | tf_op | source)
XLA Modules:
  0.0 43.2 jit_solution(17195364657751504479)
XLA Ops:
  0.7 3.0 %collective-permute-start.1 = (bf16[32,2,8,128]{3,2,1,0:T(8,128)(2,1)}, bf16[32,2,8,128]{3,2,1,0:T(8,128)(2,1)S(1)}, u32[]{:S(2)}, u32[]{:S(2)}) collective-permute-start(bf16[32,2,8,128]{3,2,1,0:T(8,128)(2,1)} %bitcast.5), channel_id=1, source_target_pairs={{0,16},{4,8},{8,4},{12,28},{16,0},{20,24},{24,20},{28,12},{1,17},{... | collective-permute-start | bytes 393224 | tf_op jit(solution)/shard_map/ppermute | solution.py:399
  3.7 1.7 %collective-permute-start = (bf16[32,2,8,128]{3,2,1,0:T(8,128)(2,1)}, bf16[32,2,8,128]{3,2,1,0:T(8,128)(2,1)S(1)}, u32[]{:S(2)}, u32[]{:S(2)}) collective-permute-start(bf16[32,2,8,128]{3,2,1,0:T(8,128)(2,1)} %bitcast.6), channel_id=1, source_target_pairs={{0,4},{4,0},{8,12},{12,8},{16,20},{20,16},{24,28},{28,24},{1,5},{5... | collective-permute-start | bytes 393224 | tf_op jit(solution)/shard_map/ppermute | solution.py:399
  5.4 1.7 %shard_map.68 = (bf16[2,128,1024]{2,1,0:T(8,128)(2,1)S(1)}, f32[4,64,1280]{2,1,0:T(8,128)S(1)}) custom-call(bf16[128,2,8,128]{3,2,1,0:T(8,128)(2,1)S(1)} %bitcast.8, bf16[27,64,128]{2,1,0:T(8,128)(2,1)S(1)} %bitcast.9, bf16[128,256]{1,0:T(8,128)(2,1)S(1)} %shard_map.67.blank_ref), custom_call_target="tpu_custom_call" | custom-call | flops 1100000000 | bytes 2867200 | tf_op jit(solution)/shard_map/pallas_call | solution.py:18
  7.4 1.5 %collective-permute-done.one_ref = bf16[32,2,8,128]{3,2,1,0:T(8,128)(2,1)S(1)} collective-permute-done((bf16[32,2,8,128]{3,2,1,0:T(8,128)(2,1)}, bf16[32,2,8,128]{3,2,1,0:T(8,128)(2,1)S(1)}, u32[]{:S(2)}, u32[]{:S(2)}) %collective-permute-start) | collective-permute-done | bytes 131104 | tf_op jit(solution)/shard_map/ppermute | solution.py:399
  9.3 1.5 %collective-permute-start.3 = (bf16[6,32,256]{2,1,0:T(8,128)(2,1)S(1)}, bf16[6,32,256]{2,1,0:T(8,128)(2,1)S(1)}, u32[]{:S(2)}, u32[]{:S(2)}) collective-permute-start(bf16[6,32,256]{2,1,0:T(8,128)(2,1)S(1)} %get-tuple-element.28), channel_id=1, source_target_pairs={{0,16},{1,2},{2,1},{3,19},{16,0},{17,18},{18,17},{19,3},{4,20},{5,... | collective-permute-start | bytes 294920 | tf_op jit(solution)/shard_map/ppermute | solution.py:399
  11.3 2.7 %collective-permute-done.3.two_ref = bf16[6,32,256]{2,1,0:T(8,128)(2,1)S(1)} collective-permute-done((bf16[6,32,256]{2,1,0:T(8,128)(2,1)S(1)}, bf16[6,32,256]{2,1,0:T(8,128)(2,1)S(1)}, u32[]{:S(2)}, u32[]{:S(2)}) %collective-permute-start.3) | collective-permute-done | bytes 98336 | tf_op jit(solution)/shard_map/ppermute | solution.py:399
  14.0 2.7 %shard_map.71 = (bf16[4,64,1280]{2,1,0:T(8,128)(2,1)S(1)}, f32[4,64,1280]{2,1,0:T(8,128)S(1)}, bf16[6,32,1536]{2,1,0:T(8,128)(2,1)S(1)}, f32[2,2,216,128]{3,2,1,0:T(8,128)S(1)}, f32[2,2,216,128]{3,2,1,0:T(8,128)S(1)}) custom-call(bf16[6,32,1024]{2,1,0:T(8,128)(2,1)S(1)} %get-tuple-element.26._.deep_ref, ...), custom_call_target="tpu_custom_call" | custom-call | flops 1500000000 | bytes 5713920 | tf_op jit(solution)/shard_map/pallas_call | solution.py:18
  16.9 1.6 %shard_map.73 = (f32[2,2,56,128]{3,2,1,0:T(8,128)S(1)}, f32[2,2,56,128]{3,2,1,0:T(8,128)S(1)}) custom-call(bf16[6,32,1536]{2,1,0:T(8,128)(2,1)S(1)} %get-tuple-element.35.rows_ref, f32[4,64,1280]{2,1,0:T(8,128)S(1)} %get-tuple-element.36.back_ref, f32[4,64,1280]{2,1,0:T(8,128)S(1)} %get-tuple-element.37.slope_ref), custom_call_target="tpu_custom_call" | custom-call | flops 4000000000 | bytes 3440640 | tf_op jit(solution)/shard_map/pallas_call | solution.py:18
  18.9 1.0 %collective-permute-done.5.refs_3_ = f32[2,2,56,128]{3,2,1,0:T(8,128)S(1)} collective-permute-done((f32[2,2,56,128]{3,2,1,0:T(8,128)S(1)}, f32[2,2,56,128]{3,2,1,0:T(8,128)S(1)}, u32[]{:S(2)}, u32[]{:S(2)}) %collective-permute-start.5) | collective-permute-done | bytes 114720 | tf_op jit(solution)/shard_map/ppermute | solution.py:407
  19.9 1.5 %collective-permute-start.6 = (bf16[272,128]{1,0:T(8,128)(2,1)S(1)}, bf16[272,128]{1,0:T(8,128)(2,1)S(1)}, u32[]{:S(2)}, u32[]{:S(2)}) collective-permute-start(bf16[272,128]{1,0:T(8,128)(2,1)S(1)} %get-tuple-element.41), channel_id=1, source_target_pairs={{0,16},{2,18},{16,0},{18,2},{1,17},{3,19},{17,1},{19,3},{4,20},{6,... | collective-permute-start | bytes 208904 | tf_op jit(solution)/shard_map/ppermute | solution.py:407
  21.4 0.9 %collective-permute-start.7 = (bf16[272,128]{1,0:T(8,128)(2,1)S(1)}, bf16[272,128]{1,0:T(8,128)(2,1)S(1)}, u32[]{:S(2)}, u32[]{:S(2)}) collective-permute-start(bf16[272,128]{1,0:T(8,128)(2,1)S(1)} %get-tuple-element.42), channel_id=1, source_target_pairs={{0,2},{2,0},{16,18},{18,16},{1,3},{3,1},{17,19},{19,17},{4,6},{6,4... | collective-permute-start | bytes 208904 | tf_op jit(solution)/shard_map/ppermute | solution.py:407
  22.4 1.1 %collective-permute-start.8 = (bf16[272,128]{1,0:T(8,128)(2,1)S(1)}, bf16[272,128]{1,0:T(8,128)(2,1)S(1)}, u32[]{:S(2)}, u32[]{:S(2)}) collective-permute-start(bf16[272,128]{1,0:T(8,128)(2,1)S(1)} %get-tuple-element.43), channel_id=1, source_target_pairs={{0,18},{2,16},{16,2},{18,0},{1,19},{3,17},{17,3},{19,1},{4,22},{6,... | collective-permute-start | bytes 208904 | tf_op jit(solution)/shard_map/ppermute | solution.py:407
  23.5 0.9 %collective-permute-done.6.refs_0_ = bf16[272,128]{1,0:T(8,128)(2,1)S(1)} collective-permute-done((bf16[272,128]{1,0:T(8,128)(2,1)S(1)}, bf16[272,128]{1,0:T(8,128)(2,1)S(1)}, u32[]{:S(2)}, u32[]{:S(2)}) %collective-permute-start.6) | collective-permute-done | bytes 69664 | tf_op jit(solution)/shard_map/ppermute | solution.py:407
  24.4 1.3 %collective-permute-done.7.refs_1_ = bf16[272,128]{1,0:T(8,128)(2,1)S(1)} collective-permute-done((bf16[272,128]{1,0:T(8,128)(2,1)S(1)}, bf16[272,128]{1,0:T(8,128)(2,1)S(1)}, u32[]{:S(2)}, u32[]{:S(2)}) %collective-permute-start.7) | collective-permute-done | bytes 69664 | tf_op jit(solution)/shard_map/ppermute | solution.py:407
  25.8 1.8 %collective-permute-done.8.refs_2_ = bf16[272,128]{1,0:T(8,128)(2,1)S(1)} collective-permute-done((bf16[272,128]{1,0:T(8,128)(2,1)S(1)}, bf16[272,128]{1,0:T(8,128)(2,1)S(1)}, u32[]{:S(2)}, u32[]{:S(2)}) %collective-permute-start.8) | collective-permute-done | bytes 69664 | tf_op jit(solution)/shard_map/ppermute | solution.py:407
  27.6 2.8 %collective-permute-start.11 = (bf16[272,128]{1,0:T(8,128)(2,1)S(1)}, bf16[272,128]{1,0:T(8,128)(2,1)S(1)}, u32[]{:S(2)}, u32[]{:S(2)}) collective-permute-start(bf16[272,128]{1,0:T(8,128)(2,1)S(1)} %shard_map.75.a_ref), channel_id=1, source_target_pairs={{0,12},{4,8},{8,4},{12,0},{1,13},{5,9},{9,5},{13,1},{2,14},{6,10},... | collective-permute-start | bytes 208904 | tf_op jit(solution)/shard_map/ppermute | solution.py:407
  30.4 0.5 %collective-permute-start.10 = (bf16[272,128]{1,0:T(8,128)(2,1)S(1)}, bf16[272,128]{1,0:T(8,128)(2,1)S(1)}, u32[]{:S(2)}, u32[]{:S(2)}) collective-permute-start(bf16[272,128]{1,0:T(8,128)(2,1)S(1)} %shard_map.75.a_ref), channel_id=1, source_target_pairs={{0,8},{4,12},{8,0},{12,4},{1,9},{5,13},{9,1},{13,5},{2,10},{6,14},... | collective-permute-start | bytes 208904 | tf_op jit(solution)/shard_map/ppermute | solution.py:407
  30.9 1.2 %collective-permute-start.9 = (bf16[272,128]{1,0:T(8,128)(2,1)S(1)}, bf16[272,128]{1,0:T(8,128)(2,1)S(1)}, u32[]{:S(2)}, u32[]{:S(2)}) collective-permute-start(bf16[272,128]{1,0:T(8,128)(2,1)S(1)} %shard_map.75.a_ref), channel_id=1, source_target_pairs={{0,4},{4,0},{8,12},{12,8},{1,5},{5,1},{9,13},{13,9},{2,6},{6,2},{1... | collective-permute-start | bytes 208904 | tf_op jit(solution)/shard_map/ppermute | solution.py:407
  32.1 2.5 %shard_map.72 = (bf16[128,2,8,128]{3,2,1,0:T(8,128)(2,1)}, f32[8,128]{1,0:T(8,128)S(1)}) custom-call(bf16[4,64,1280]{2,1,0:T(8,128)(2,1)S(1)} %get-tuple-element.31.hidden_ref, bf16[27,64,128]{2,1,0:T(8,128)(2,1)S(1)} %bitcast.10), custom_call_target="tpu_custom_call" | custom-call | flops 900000000 | bytes 1626112 | tf_op jit(solution)/shard_map/pallas_call | solution.py:18
  34.6 1.5 %collective-permute-done.10.c_ref = bf16[272,128]{1,0:T(8,128)(2,1)S(1)} collective-permute-done((bf16[272,128]{1,0:T(8,128)(2,1)S(1)}, bf16[272,128]{1,0:T(8,128)(2,1)S(1)}, u32[]{:S(2)}, u32[]{:S(2)}) %collective-permute-start.10) | collective-permute-done | bytes 69664 | tf_op jit(solution)/shard_map/ppermute | solution.py:407
  36.2 1.1 %collective-permute-start.12 = (bf16[272,128]{1,0:T(8,128)(2,1)S(1)}, bf16[272,128]{1,0:T(8,128)(2,1)S(1)}, u32[]{:S(2)}, u32[]{:S(2)}) collective-permute-start(bf16[272,128]{1,0:T(8,128)(2,1)S(1)} %shard_map.76.own_ref), channel_id=1, source_target_pairs={{0,2},{2,0},{1,3},{3,1},{4,6},{6,4},{5,7},{7,5},{8,10},{10,8},{9,1... | collective-permute-start | bytes 208904 | tf_op jit(solution)/shard_map/ppermute | solution.py:407
  37.3 3.3 %collective-permute-done.12.got_ref = bf16[272,128]{1,0:T(8,128)(2,1)S(1)} collective-permute-done((bf16[272,128]{1,0:T(8,128)(2,1)S(1)}, bf16[272,128]{1,0:T(8,128)(2,1)S(1)}, u32[]{:S(2)}, u32[]{:S(2)}) %collective-permute-start.12) | collective-permute-done | bytes 69664 | tf_op jit(solution)/shard_map/ppermute | solution.py:407
  40.7 1.3 %collective-permute-done.13.got_ref = bf16[2,272,128]{2,1,0:T(8,128)(2,1)S(1)} collective-permute-done((bf16[2,272,128]{2,1,0:T(8,128)(2,1)S(1)}, bf16[2,272,128]{2,1,0:T(8,128)(2,1)S(1)}, u32[]{:S(2)}, u32[]{:S(2)}) %collective-permute-start.13) | collective-permute-done | bytes 139296 | tf_op jit(solution)/shard_map/ppermute | solution.py:407
  42.0 1.2 %shard_map.78 = (f32[27,32,32]{2,1,0:T(8,128)}, f32[27,64,64]{2,1,0:T(8,128)}) custom-call(bf16[2,272,128]{2,1,0:T(8,128)(2,1)S(1)} %shard_map.77.own_ref, bf16[2,272,128]{2,1,0:T(8,128)(2,1)S(1)} %collective-permute-done.13.got_ref), custom_call_target="tpu_custom_call" | custom-call | bytes 831488 | tf_op jit(solution)/shard_map/pallas_call | solution.py:18
  (24 shorter events, 2.1 us)
Async XLA Ops:
  0.6 4.7 %copy-start.1 = (bf16[1,128,2,8,128]{4,3,2,1,0:T(8,128)(2,1)S(1)}, bf16[1,128,2,8,128]{4,3,2,1,0:T(8,128)(2,1)}, u32[]{:S(2)}) copy-start(bf16[1,128,2,8,128]{4,3,2,1,0:T(8,128)(2,1)} %param.7) | copy-start | bytes 1572868
  0.6 4.7 %copy-start.2 = (bf16[27,128,64]{1,2,0:T(8,128)(2,1)S(1)}, bf16[27,128,64]{1,2,0:T(8,128)(2,1)}, u32[]{:S(2)}) copy-start(bf16[27,128,64]{1,2,0:T(8,128)(2,1)} %param.6) | copy-start | bytes 1327108
  0.7 6.7 %collective-permute-start.1 = (bf16[32,2,8,128]{3,2,1,0:T(8,128)(2,1)}, bf16[32,2,8,128]{3,2,1,0:T(8,128)(2,1)S(1)}, u32[]{:S(2)}, u32[]{:S(2)}) collective-permute-start(bf16[32,2,8,128]{3,2,1,0:T(8,128)(2,1)} %bitcast.5), channel_id=1, source_target_pairs={{0,16},{4,8},{8,4},{12,28},{16,0},{20,24},{24,20},{28,12},{1,17},{... | collective-permute-start | bytes 393224 | tf_op jit(solution)/shard_map/ppermute | solution.py:399
  3.7 5.2 %collective-permute-start = (bf16[32,2,8,128]{3,2,1,0:T(8,128)(2,1)}, bf16[32,2,8,128]{3,2,1,0:T(8,128)(2,1)S(1)}, u32[]{:S(2)}, u32[]{:S(2)}) collective-permute-start(bf16[32,2,8,128]{3,2,1,0:T(8,128)(2,1)} %bitcast.6), channel_id=1, source_target_pairs={{0,4},{4,0},{8,12},{12,8},{16,20},{20,16},{24,28},{28,24},{1,5},{5... | collective-permute-start | bytes 393224 | tf_op jit(solution)/shard_map/ppermute | solution.py:399
  5.3 3.5 %copy-start = (bf16[1,32,2,8,128]{4,3,2,1,0:T(8,128)(2,1)S(1)}, bf16[1,32,2,8,128]{4,3,2,1,0:T(8,128)(2,1)}, u32[]{:S(2)}) copy-start(bf16[1,32,2,8,128]{4,3,2,1,0:T(8,128)(2,1)} %param.4) | copy-start | bytes 393220
  5.3 5.5 %copy-start.3 = (bf16[27,64,32]{1,2,0:T(8,128)(2,1)S(1)}, bf16[27,64,32]{1,2,0:T(8,128)(2,1)}, u32[]{:S(2)}) copy-start(bf16[27,64,32]{1,2,0:T(8,128)(2,1)} %param.5) | copy-start | bytes 331780
  9.2 2.1 %collective-permute-start.2 = (bf16[6,32,256]{2,1,0:T(8,128)(2,1)S(1)}, bf16[6,32,256]{2,1,0:T(8,128)(2,1)S(1)}, u32[]{:S(2)}, u32[]{:S(2)}) collective-permute-start(bf16[6,32,256]{2,1,0:T(8,128)(2,1)S(1)} %get-tuple-element.27), channel_id=1, source_target_pairs={{0,1},{1,0},{2,3},{3,2},{16,17},{17,16},{18,19},{19,18},{4,5},{5,4... | collective-permute-start | bytes 294920 | tf_op jit(solution)/shard_map/ppermute | solution.py:399
  9.3 4.7 %collective-permute-start.3 = (bf16[6,32,256]{2,1,0:T(8,128)(2,1)S(1)}, bf16[6,32,256]{2,1,0:T(8,128)(2,1)S(1)}, u32[]{:S(2)}, u32[]{:S(2)}) collective-permute-start(bf16[6,32,256]{2,1,0:T(8,128)(2,1)S(1)} %get-tuple-element.28), channel_id=1, source_target_pairs={{0,16},{1,2},{2,1},{3,19},{16,0},{17,18},{18,17},{19,3},{4,20},{5,... | collective-permute-start | bytes 294920 | tf_op jit(solution)/shard_map/ppermute | solution.py:399
  16.7 3.2 %collective-permute-start.4 = (f32[2,2,216,128]{3,2,1,0:T(8,128)S(1)}, f32[2,2,216,128]{3,2,1,0:T(8,128)S(1)}, u32[]{:S(2)}, u32[]{:S(2)}) collective-permute-start(f32[2,2,216,128]{3,2,1,0:T(8,128)S(1)} %get-tuple-element.34), channel_id=1, source_target_pairs={{0,1},{1,0},{2,3},{3,2},{4,5},{5,4},{6,7},{7,6},{8,9},{9,8},{10,11... | collective-permute-start | bytes 1327112 | tf_op jit(solution)/shard_map/ppermute | solution.py:407
  18.4 1.4 %collective-permute-start.5 = (f32[2,2,56,128]{3,2,1,0:T(8,128)S(1)}, f32[2,2,56,128]{3,2,1,0:T(8,128)S(1)}, u32[]{:S(2)}, u32[]{:S(2)}) collective-permute-start(f32[2,2,56,128]{3,2,1,0:T(8,128)S(1)} %get-tuple-element.39), channel_id=1, source_target_pairs={{0,1},{1,0},{2,3},{3,2},{4,5},{5,4},{6,7},{7,6},{8,9},{9,8},{10,11... | collective-permute-start | bytes 344072 | tf_op jit(solution)/shard_map/ppermute | solution.py:407
  19.9 4.5 %collective-permute-start.6 = (bf16[272,128]{1,0:T(8,128)(2,1)S(1)}, bf16[272,128]{1,0:T(8,128)(2,1)S(1)}, u32[]{:S(2)}, u32[]{:S(2)}) collective-permute-start(bf16[272,128]{1,0:T(8,128)(2,1)S(1)} %get-tuple-element.41), channel_id=1, source_target_pairs={{0,16},{2,18},{16,0},{18,2},{1,17},{3,19},{17,1},{19,3},{4,20},{6,... | collective-permute-start | bytes 208904 | tf_op jit(solution)/shard_map/ppermute | solution.py:407
  21.4 4.3 %collective-permute-start.7 = (bf16[272,128]{1,0:T(8,128)(2,1)S(1)}, bf16[272,128]{1,0:T(8,128)(2,1)S(1)}, u32[]{:S(2)}, u32[]{:S(2)}) collective-permute-start(bf16[272,128]{1,0:T(8,128)(2,1)S(1)} %get-tuple-element.42), channel_id=1, source_target_pairs={{0,2},{2,0},{16,18},{18,16},{1,3},{3,1},{17,19},{19,17},{4,6},{6,4... | collective-permute-start | bytes 208904 | tf_op jit(solution)/shard_map/ppermute | solution.py:407
  22.4 5.2 %collective-permute-start.8 = (bf16[272,128]{1,0:T(8,128)(2,1)S(1)}, bf16[272,128]{1,0:T(8,128)(2,1)S(1)}, u32[]{:S(2)}, u32[]{:S(2)}) collective-permute-start(bf16[272,128]{1,0:T(8,128)(2,1)S(1)} %get-tuple-element.43), channel_id=1, source_target_pairs={{0,18},{2,16},{16,2},{18,0},{1,19},{3,17},{17,3},{19,1},{4,22},{6,... | collective-permute-start | bytes 208904 | tf_op jit(solution)/shard_map/ppermute | solution.py:407
  27.6 7.0 %collective-permute-start.11 = (bf16[272,128]{1,0:T(8,128)(2,1)S(1)}, bf16[272,128]{1,0:T(8,128)(2,1)S(1)}, u32[]{:S(2)}, u32[]{:S(2)}) collective-permute-start(bf16[272,128]{1,0:T(8,128)(2,1)S(1)} %shard_map.75.a_ref), channel_id=1, source_target_pairs={{0,12},{4,8},{8,4},{12,0},{1,13},{5,9},{9,5},{13,1},{2,14},{6,10},... | collective-permute-start | bytes 208904 | tf_op jit(solution)/shard_map/ppermute | solution.py:407
  30.4 5.7 %collective-permute-start.10 = (bf16[272,128]{1,0:T(8,128)(2,1)S(1)}, bf16[272,128]{1,0:T(8,128)(2,1)S(1)}, u32[]{:S(2)}, u32[]{:S(2)}) collective-permute-start(bf16[272,128]{1,0:T(8,128)(2,1)S(1)} %shard_map.75.a_ref), channel_id=1, source_target_pairs={{0,8},{4,12},{8,0},{12,4},{1,9},{5,13},{9,1},{13,5},{2,10},{6,14},... | collective-permute-start | bytes 208904 | tf_op jit(solution)/shard_map/ppermute | solution.py:407
  30.9 5.3 %collective-permute-start.9 = (bf16[272,128]{1,0:T(8,128)(2,1)S(1)}, bf16[272,128]{1,0:T(8,128)(2,1)S(1)}, u32[]{:S(2)}, u32[]{:S(2)}) collective-permute-start(bf16[272,128]{1,0:T(8,128)(2,1)S(1)} %shard_map.75.a_ref), channel_id=1, source_target_pairs={{0,4},{4,0},{8,12},{12,8},{1,5},{5,1},{9,13},{13,9},{2,6},{6,2},{1... | collective-permute-start | bytes 208904 | tf_op jit(solution)/shard_map/ppermute | solution.py:407
  36.2 4.4 %collective-permute-start.12 = (bf16[272,128]{1,0:T(8,128)(2,1)S(1)}, bf16[272,128]{1,0:T(8,128)(2,1)S(1)}, u32[]{:S(2)}, u32[]{:S(2)}) collective-permute-start(bf16[272,128]{1,0:T(8,128)(2,1)S(1)} %shard_map.76.own_ref), channel_id=1, source_target_pairs={{0,2},{2,0},{1,3},{3,1},{4,6},{6,4},{5,7},{7,5},{8,10},{10,8},{9,1... | collective-permute-start | bytes 208904 | tf_op jit(solution)/shard_map/ppermute | solution.py:407
  40.6 1.4 %collective-permute-start.13 = (bf16[2,272,128]{2,1,0:T(8,128)(2,1)S(1)}, bf16[2,272,128]{2,1,0:T(8,128)(2,1)S(1)}, u32[]{:S(2)}, u32[]{:S(2)}) collective-permute-start(bf16[2,272,128]{2,1,0:T(8,128)(2,1)S(1)} %shard_map.77.own_ref), channel_id=1, source_target_pairs={{0,1},{1,0},{2,3},{3,2},{4,5},{5,4},{6,7},{7,6},{8,9},{9,8},{10,11... | collective-permute-start | bytes 417800 | tf_op jit(solution)/shard_map/ppermute | solution.py:407

commit v10 on v9

--- a/solution.py
+++ b/solution.py
@@ -10,7 +10,7 @@
 BF, F32 = jnp.bfloat16, jnp.float32
 LANES = 128
 HGT = ("y", "core")
-VMEM_BYTES = 48 * 2**20
+VMEM_BYTES = 28 * 2**20
 
 
 def call(body, outs, args, scratch=(), flops=0, far=()):
@@ -95,7 +95,7 @@
     return stacked.astype(F32).T.astype(BF)
 
 
-def arrange_kernel(cot_rows_ref, k1_ref, _, moved_ref, w1_ref):
+def arrange_kernel(cot_rows_ref, k1_ref, moved_ref, w1_ref):
     depth, out, cells = cot_rows_ref.shape
     for d in range(depth):
         for h in range(0, cells, LANES):
@@ -165,71 +165,107 @@
             send_ref[part, half] = jnp.where(core, one, two)
 
 
-def hidden_kernel(
-    direct, deep_ref, one_ref, two_ref, w1_ref, moved_ref, hidden_ref, slope_ref, rows_ref, *grad_refs
+def activated(w1, rhs, d, depth, heights):
+    mid = w1.shape[0] // 3
+    y = jnp.dot(w1, rhs, preferred_element_type=F32)
+    pre = sum(moved_along_width(y[n * mid : (n + 1) * mid], 1 - n) for n in range(3))
+    s = 1.0 / (1.0 + jnp.exp(-pre))
+    dep, deps = lax.axis_index("dep"), lax.axis_size("dep")
+    hgt, hgts = lax.axis_index(HGT), lax.axis_size(HGT)
+    results = []
+    for n, side in enumerate(heights):
+        p, q = (x[:, n * LANES : (n + 1) * LANES] for x in (pre, s))
+        value, slope = (p * q).astype(BF), q * (1.0 + p * (1.0 - q))
+        outside = []
+        if d == 0:
+            outside.append(dep == 0)
+        if d == depth - 1:
+            outside.append(dep == deps - 1)
+        if side < 0:
+            outside.append(hgt == 0)
+        if side > 0:
+            outside.append(hgt == hgts - 1)
+        for far in outside:
+            value = jnp.where(far, jnp.zeros_like(value), value)
+            slope = jnp.where(far, jnp.zeros_like(slope), slope)
+        results.append((value, slope))
+    return results
+
+
+def neighbours(ref, d, starts, count):
+    return jnp.concatenate(
+        [
+            jnp.concatenate(
+                [ref[d + a, :, (start + b) * LANES : (start + b + count) * LANES] for start in starts], axis=1
+            )
+            for a in range(3)
+            for b in range(3)
+        ],
+        axis=0,
+    )
+
+
+def products(left, right):
+    return lax.dot_general(left, right, (((1,), (1,)), ((), ())), preferred_element_type=F32)
+
+
+def shares(delta, n_channels, ref, at):
+    for n in range(3):
+        ref[n * n_channels : (n + 1) * n_channels, at : at + LANES] = moved_along_width(delta, n - 1).astype(BF)
+
+
+def inner_kernel(deep_ref, w1_ref, moved_ref, back_ref, hidden_ref, second_ref, first_ref, delta_ref):
+    w1 = w1_ref[...]
+    depth, mid, cells = hidden_ref.shape
+    height = cells // LANES
+    for d in range(depth):
+        for h in range(0, height, 2):
+            results = activated(w1, neighbours(deep_ref, d, [h], 2), d, depth, (0, 0))
+            for n, (value, slope) in enumerate(results):
+                at = (h + n) * LANES
+                hidden_ref[d, :, at : at + LANES] = value
+                back = back_ref[d, :, at + 2 * LANES : at + 3 * LANES]
+                shares(back * slope, mid, delta_ref, d * cells + at)
+    own = depth - 2
+    count = height - 2
+    left = jnp.concatenate([moved_ref[d, :, 2 * LANES : (2 + count) * LANES] for d in range(own)], axis=1)
+    right = jnp.concatenate([neighbours(hidden_ref, d, [0], count) for d in range(own)], axis=1)
+    second_ref[...] = products(left, right)
+    right = jnp.concatenate([neighbours(deep_ref, d, [0], height) for d in range(depth)], axis=1)
+    first_ref[...] = products(delta_ref[...], right)
+
+
+def outer_kernel(
+    direct, deep_ref, one_ref, two_ref, w1_ref, moved_ref, inner_ref, second_ref,
+    hidden_ref, slope_ref, rows_ref, *grad_refs,
 ):
     for d, row in enumerate(widened(deep_ref, one_ref, two_ref)):
         rows_ref[d] = row
-    rows = rows_ref
-    mid = w1_ref.shape[0] // 3
-    dep, deps = lax.axis_index("dep"), lax.axis_size("dep")
-    hgt, hgts = lax.axis_index(HGT), lax.axis_size(HGT)
-    depth, height = hidden_ref.shape[0], hidden_ref.shape[2] // LANES
     w1 = w1_ref[...]
+    depth, mid, cells = hidden_ref.shape
+    height = cells // LANES
     for d in range(depth):
-        for h in range(0, height, 2):
-            rhs = jnp.concatenate(
-                [rows[d + a, :, (h + b) * LANES : (h + b + 2) * LANES] for a in range(3) for b in range(3)], axis=0
-            )
-            y = jnp.dot(w1, rhs, preferred_element_type=F32)
-            pre = sum(moved_along_width(y[n * mid : (n + 1) * mid], 1 - n) for n in range(3))
-            s = 1.0 / (1.0 + jnp.exp(-pre))
-            for r in range(2):
-                lanes = slice(r * LANES, (r + 1) * LANES)
-                p, q = pre[:, lanes], s[:, lanes]
-                value = (p * q).astype(BF)
-                slope = q * (1.0 + p * (1.0 - q))
-                outside = []
-                if d == 0:
-                    outside.append(dep == 0)
-                if d == depth - 1:
-                    outside.append(dep == deps - 1)
-                if h + r == 0:
-                    outside.append(hgt == 0)
-                if h + r == height - 1:
-                    outside.append(hgt == hgts - 1)
-                for far in outside:
-                    value = jnp.where(far, jnp.zeros_like(value), value)
-                    slope = jnp.where(far, jnp.zeros_like(slope), slope)
-                at = slice((h + r) * LANES, (h + r + 1) * LANES)
-                hidden_ref[d, :, at] = value
-                slope_ref[d, :, at] = slope
-    cells = (height - 2) * LANES
-    own = depth - 2
-    out = moved_ref.shape[1] // 3
-    left = jnp.concatenate([moved_ref[d] for d in range(own)], axis=1)
-    blocks, tails = [None] * 12, []
-    for first in (0, 4, 8):
-        group = range(first, min(first + 4, 9))
-        right = jnp.concatenate(
-            [
-                jnp.concatenate(
-                    [hidden_ref[d + ab // 3, :, (ab % 3) * LANES : (ab % 3) * LANES + cells] for ab in group], axis=0
-                )
-                for d in range(own)
-            ],
-            axis=1,
-        )
-        g = lax.dot_general(left, right, (((1,), (1,)), ((), ())), preferred_element_type=F32)
-        for n in range(3):
-            part = g[n * out : (n + 1) * out]
-            if first < 8:
-                for m in range(2):
-                    blocks[4 * n + first // 2 + m] = part[:, m * LANES : (m + 1) * LANES]
-            else:
-                tails.append(part)
-    tails.append(jnp.zeros_like(tails[0]))
-    blocks += [jnp.concatenate(tails[2 * m : 2 * m + 2], axis=1) for m in range(2)]
+        hidden_ref[d, :, 2 * LANES : cells - 2 * LANES] = inner_ref[d]
+        for h, sides_of in ((0, (-1, 0)), (height - 2, (0, 1))):
+            results = activated(w1, neighbours(rows_ref, d, [h], 2), d, depth, sides_of)
+            for n, (value, slope) in enumerate(results):
+                hidden_ref[d, :, (h + n) * LANES : (h + n + 1) * LANES] = value
+                at = ((2 if h else 0) + n) * LANES
+                slope_ref[d, :, at : at + LANES] = slope
+    own, last = depth - 2, height - 4
+    left = jnp.concatenate(
+        [moved_ref[d, :, at * LANES : (at + 2) * LANES] for d in range(own) for at in (0, last)], axis=1
+    )
+    right = jnp.concatenate([neighbours(hidden_ref, d, [0, last], 2) for d in range(own)], axis=1)
+    total = second_ref[...] + products(left, right)
+    out = left.shape[0] // 3
+    blocks, tails = [], []
+    for n in range(3):
+        part = total[n * out : (n + 1) * out]
+        blocks += [part[:, m * LANES : (m + 1) * LANES] for m in range(4)]
+        tails.append(part[:, 4 * LANES :])
+    blocks.append(jnp.concatenate(tails[:2], axis=1))
+    blocks.append(jnp.concatenate([tails[2], jnp.zeros_like(tails[2])], axis=1))
     size = mid // lax.axis_size("dp")
 
     def units_of(part):
@@ -263,42 +299,22 @@
     token_ref[...] = scratch[:8]
 
 
-def delta_kernel(direct, rows_ref, back_ref, slope_ref, *outs_and_scratch):
+def delta_kernel(direct, rows_ref, back_ref, slope_ref, first_ref, *outs_and_scratch):
     *grad_refs, delta_ref = outs_and_scratch
     depth, mid, cells = slope_ref.shape
+    last = back_ref.shape[2] // LANES - 2
     for d in range(depth):
-        for at in range(0, cells, LANES):
-            delta = back_ref[d, :, at : at + LANES] * slope_ref[d, :, at : at + LANES]
-            for n in range(3):
-                delta_ref[n * mid : (n + 1) * mid, d * cells + at : d * cells + at + LANES] = moved_along_width(
-                    delta, n - 1
-                ).astype(BF)
-    left = delta_ref[...]
-    blocks, tails = [None] * 6, []
+        for n, h in enumerate((0, 1, last, last + 1)):
+            delta = back_ref[d, :, h * LANES : (h + 1) * LANES] * slope_ref[d, :, n * LANES : (n + 1) * LANES]
+            shares(delta, mid, delta_ref, d * cells + n * LANES)
+    right = jnp.concatenate([neighbours(rows_ref, d, [0, last], 2) for d in range(depth)], axis=1)
+    total = first_ref[...] + products(delta_ref[...], right)
     inner = rows_ref.shape[1]
-    for first in (0, 8):
-        group = range(first, min(first + 8, 9))
-        right = jnp.concatenate(
-            [
-                jnp.concatenate(
-                    [
-                        rows_ref[d + ab // 3, :, (ab % 3) * LANES : (ab % 3) * LANES + cells]
-                        for ab in group
-                    ],
-                    axis=0,
-                )
-                for d in range(depth)
-            ],
-            axis=1,
-        )
-        g = lax.dot_general(left, right, (((1,), (1,)), ((), ())), preferred_element_type=F32)
-        for n in range(3):
-            part = g[n * mid : (n + 1) * mid]
-            if first == 0:
-                for m in range(2):
-                    blocks[2 * n + m] = part[:, m * LANES : (m + 1) * LANES]
-            else:
-                tails.append(part)
+    blocks, tails = [], []
+    for n in range(3):
+        part = total[n * mid : (n + 1) * mid]
+        blocks += [part[:, m * LANES : (m + 1) * LANES] for m in range(2)]
+        tails.append(part[:, 2 * LANES :])
     tails.append(jnp.zeros((mid, LANES - 3 * inner), F32))
     blocks.append(jnp.concatenate(tails, axis=1))
     size = mid // lax.axis_size("dp")
@@ -437,45 +453,55 @@
         [pltpu.VMEM((out * rows, width), F32)],
         flops=1_100_000_000,
     )
+    moved, w1 = call(
+        arrange_kernel,
+        [shape((depth, 3 * out, cells), BF), shape((3 * mid, 9 * inner), BF)],
+        [cot_rows, k1],
+        flops=500_000_000,
+    )
     deep, one, two = call(
         rim_kernel,
         [shape((3 * depth, inner, cells), BF)] + [shape((3 * depth, inner, 2 * width), BF)] * 2,
-        [volume[0], one, two, cot_rows],
+        [volume[0], one, two, w1],
         [pltpu.VMEM((inner * rows, width), F32)],
     )
     one, two = swapped(one, HGT, 0), swapped(two, HGT, 1)
-    moved, w1 = call(
-        arrange_kernel,
-        [shape((depth, 3 * out, cells), BF), shape((3 * mid, 9 * inner), BF)],
-        [cot_rows, k1, deep],
-        flops=500_000_000,
-    )
     size = mid // parts
     direct = parts == 2 and size % 16 == 0
     halves = lax.axis_size("y")
     length_second, length_first = (-(-units * size // (16 * halves)) * 8 for units in (27, 7))
+    rows_in, rows_out = height - 2, 4
+    inner_hidden, inner_second, inner_first = call(
+        inner_kernel,
+        [
+            shape((depth + 2, mid, rows_in * width), BF),
+            shape((3 * out, 9 * mid), F32),
+            shape((3 * mid, 9 * inner), F32),
+        ],
+        [deep, w1, moved, back],
+        [pltpu.VMEM((3 * mid, (depth + 2) * rows_in * width), BF)],
+        flops=1_500_000_000,
+    )
     hidden, slope, wide, *second = call(
-        functools.partial(hidden_kernel, direct),
+        functools.partial(outer_kernel, direct),
         [
             shape((depth + 2, mid, cells + 2 * width), BF),
-            shape((depth + 2, mid, cells + 2 * width), F32),
+            shape((depth + 2, mid, rows_out * width), F32),
             shape((3 * depth, inner, cells + 4 * width), BF),
         ]
         + (
-            [shape((parts, halves, length_second, width), F32) for _ in range(2)]
+            [shape((parts, halves, length_second, width), F32)] * 2
             if direct
             else [shape((14, out, LANES), F32)]
         ),
-        [deep, one, two, w1, moved],
-        flops=1_500_000_000,
+        [deep, one, two, w1, moved, inner_hidden, inner_second],
+        flops=1_000_000_000,
     )
     first = call(
         functools.partial(delta_kernel, direct),
-        [shape((parts, halves, length_first, width), F32) for _ in range(2)]
-        if direct
-        else [shape((7, mid, LANES), F32)],
-        [wide, back, slope],
-        [pltpu.VMEM((3 * mid, (depth + 2) * (cells + 2 * width)), BF)],
+        [shape((parts, halves, length_first, width), F32)] * 2 if direct else [shape((7, mid, LANES), F32)],
+        [wide, back, slope, inner_first],
+        [pltpu.VMEM((3 * mid, (depth + 2) * rows_out * width), BF)],
         flops=4_000_000_000,
     )
     if direct:

time: 43.4 us -> 41.4 us (0.954)
  waiting for transfers between devices: 15.7 us -> 13.5 us
    ppermute x4, waiting for transfers between devices: 4.43 us -> 2.19 us  [swapped(): return lax.ppermute(x, ('dp', *axes), list(enumerate(partner)))]
    pallas_call x12 -> x13, Pallas kernels: 10.8 us -> 11 us  [call(): pl.pallas_call(body, out_shape=outs, in_specs=[pl.BlockSpec(memory_space=...]
  transfers between devices with their start and end apart: 14 -> 14, of which waited for: 10 -> 9; matrix products, arithmetic and copies ran while one was open for 0% -> 0% of each run, Pallas kernels for 15% -> 19%
where the time goes in v10:
time: 41.4 us; the launch traced here: 41.2 us
  starting transfers between devices  16 us (39%)
  waiting for transfers between devices  13.5 us (33%)
  Pallas kernels  11 us (27%)
  between operations  0.77 us (2%)
    ppermute x10, waiting for transfers between devices, across(): lax.ppermute(x, axes, [(i, i ^ flip) for i in range(lax.axis_size(axes))])  11.3 us
    pallas_call x13, Pallas kernels, call(): pl.pallas_call(body, out_shape=outs, in_specs=[pl.BlockSpec(memory_space=...  11 us
    ppermute x10, starting transfers between devices, across(): lax.ppermute(x, axes, [(i, i ^ flip) for i in range(lax.axis_size(axes))])  9.79 us
    ppermute x4, starting transfers between devices, swapped(): return lax.ppermute(x, ('dp', *axes), list(enumerate(partner)))  6.23 us
    ppermute x4, waiting for transfers between devices, swapped(): return lax.ppermute(x, ('dp', *axes), list(enumerate(partner)))  2.19 us
  transfers between devices with their start and end apart: 14, of which 9 were waited for; matrix products, arithmetic and copies ran while one was open for 0% of the time, Pallas kernels for 19%

profile of v10, /device:TPU:0, one launch (start us, length us, event | category | flops | bytes accessed | tf_op | source)
XLA Modules:
  0.0 41.2 jit_solution(758297039501916544)
XLA Ops:
  0.7 3.0 %collective-permute-start.1 = (bf16[32,2,8,128]{3,2,1,0:T(8,128)(2,1)}, bf16[32,2,8,128]{3,2,1,0:T(8,128)(2,1)S(1)}, u32[]{:S(2)}, u32[]{:S(2)}) collective-permute-start(bf16[32,2,8,128]{3,2,1,0:T(8,128)(2,1)} %bitcast.5), channel_id=1, source_target_pairs={{0,16},{4,8},{8,4},{12,28},{16,0},{20,24},{24,20},{28,12},{1,17},{... | collective-permute-start | bytes 393224 | tf_op jit(solution)/shard_map/ppermute | solution.py:415
  3.7 1.7 %collective-permute-start = (bf16[32,2,8,128]{3,2,1,0:T(8,128)(2,1)}, bf16[32,2,8,128]{3,2,1,0:T(8,128)(2,1)S(1)}, u32[]{:S(2)}, u32[]{:S(2)}) collective-permute-start(bf16[32,2,8,128]{3,2,1,0:T(8,128)(2,1)} %bitcast.6), channel_id=1, source_target_pairs={{0,4},{4,0},{8,12},{12,8},{16,20},{20,16},{24,28},{28,24},{1,5},{5... | collective-permute-start | bytes 393224 | tf_op jit(solution)/shard_map/ppermute | solution.py:415
  5.3 1.7 %shard_map.68 = (bf16[2,128,1024]{2,1,0:T(8,128)(2,1)S(1)}, f32[4,64,1280]{2,1,0:T(8,128)S(1)}) custom-call(bf16[128,2,8,128]{3,2,1,0:T(8,128)(2,1)S(1)} %bitcast.8, bf16[27,64,128]{2,1,0:T(8,128)(2,1)S(1)} %bitcast.9, bf16[128,256]{1,0:T(8,128)(2,1)S(1)} %shard_map.67.blank_ref), custom_call_target="tpu_custom_call" | custom-call | flops 1100000000 | bytes 2867200 | tf_op jit(solution)/shard_map/pallas_call | solution.py:18
  7.6 1.2 %collective-permute-done.one_ref = bf16[32,2,8,128]{3,2,1,0:T(8,128)(2,1)S(1)} collective-permute-done((bf16[32,2,8,128]{3,2,1,0:T(8,128)(2,1)}, bf16[32,2,8,128]{3,2,1,0:T(8,128)(2,1)S(1)}, u32[]{:S(2)}, u32[]{:S(2)}) %collective-permute-start) | collective-permute-done | bytes 131104 | tf_op jit(solution)/shard_map/ppermute | solution.py:415
  9.3 1.5 %collective-permute-start.3 = (bf16[6,32,256]{2,1,0:T(8,128)(2,1)S(1)}, bf16[6,32,256]{2,1,0:T(8,128)(2,1)S(1)}, u32[]{:S(2)}, u32[]{:S(2)}) collective-permute-start(bf16[6,32,256]{2,1,0:T(8,128)(2,1)S(1)} %get-tuple-element.32), channel_id=1, source_target_pairs={{0,16},{1,2},{2,1},{3,19},{16,0},{17,18},{18,17},{19,3},{4,20},{5,... | collective-permute-start | bytes 294920 | tf_op jit(solution)/shard_map/ppermute | solution.py:415
  10.8 2.2 %shard_map.71 = (bf16[4,64,768]{2,1,0:T(8,128)(2,1)S(1)}, f32[384,576]{1,0:T(8,128)S(1)}, f32[192,288]{1,0:T(8,128)S(1)}) custom-call(bf16[6,32,1024]{2,1,0:T(8,128)(2,1)S(1)} %get-tuple-element.30.deep_ref, bf16[192,288]{1,0:T(8,128)(2,1)S(1)} %get-tuple-element.29._.w1_ref, bf16[2,384,1024]{2,1,0:T(8,128)(2,1)S(1)} %get-tuple-element.33.moved_ref, ...), custom_call_target="tpu_custom_call" | custom-call | flops 1500000000 | bytes 4886528 | tf_op jit(solution)/shard_map/pallas_call | solution.py:18
  13.0 1.0 %collective-permute-done.3.two_ref = bf16[6,32,256]{2,1,0:T(8,128)(2,1)S(1)} collective-permute-done((bf16[6,32,256]{2,1,0:T(8,128)(2,1)S(1)}, bf16[6,32,256]{2,1,0:T(8,128)(2,1)S(1)}, u32[]{:S(2)}, u32[]{:S(2)}) %collective-permute-start.3) | collective-permute-done | bytes 98336 | tf_op jit(solution)/shard_map/ppermute | solution.py:415
  14.0 1.5 %shard_map.72 = (bf16[4,64,1280]{2,1,0:T(8,128)(2,1)S(1)}, f32[4,64,512]{2,1,0:T(8,128)S(1)}, bf16[6,32,1536]{2,1,0:T(8,128)(2,1)S(1)}, f32[2,2,216,128]{3,2,1,0:T(8,128)S(1)}, f32[2,2,216,128]{3,2,1,0:T(8,128)S(1)}) custom-call(bf16[6,32,1024]{2,1,0:T(8,128)(2,1)S(1)} %get-tuple-element.30.deep_ref, bf16[6,32,256]{2,1,0:T(8,128)(2,1)S(1)} %collective-permute-done.2.one_ref, ...), custom_call_target="tpu_custom_call" | custom-call | flops 1000000000 | bytes 6205440 | tf_op jit(solution)/shard_map/pallas_call | solution.py:18
  15.7 0.8 %shard_map.74 = (f32[2,2,56,128]{3,2,1,0:T(8,128)S(1)}, f32[2,2,56,128]{3,2,1,0:T(8,128)S(1)}) custom-call(bf16[6,32,1536]{2,1,0:T(8,128)(2,1)S(1)} %get-tuple-element.41.rows_ref, f32[4,64,1280]{2,1,0:T(8,128)S(1)} %get-tuple-element.34.back_ref, f32[4,64,512]{2,1,0:T(8,128)S(1)} %get-tuple-element.42.slope_ref, f32[192,288]{1,0:T(8,128)S(1)} %get-tuple-element.43.first_ref), custom_call_target="tpu_custom_call" | custom-call | flops 4000000000 | bytes 2875392 | tf_op jit(solution)/shard_map/pallas_call | solution.py:18
  16.9 1.0 %collective-permute-done.5.refs_3_ = f32[2,2,56,128]{3,2,1,0:T(8,128)S(1)} collective-permute-done((f32[2,2,56,128]{3,2,1,0:T(8,128)S(1)}, f32[2,2,56,128]{3,2,1,0:T(8,128)S(1)}, u32[]{:S(2)}, u32[]{:S(2)}) %collective-permute-start.5) | collective-permute-done | bytes 114720 | tf_op jit(solution)/shard_map/ppermute | solution.py:423
  17.9 1.5 %collective-permute-start.6 = (bf16[272,128]{1,0:T(8,128)(2,1)S(1)}, bf16[272,128]{1,0:T(8,128)(2,1)S(1)}, u32[]{:S(2)}, u32[]{:S(2)}) collective-permute-start(bf16[272,128]{1,0:T(8,128)(2,1)S(1)} %get-tuple-element.47), channel_id=1, source_target_pairs={{0,16},{2,18},{16,0},{18,2},{1,17},{3,19},{17,1},{19,3},{4,20},{6,... | collective-permute-start | bytes 208904 | tf_op jit(solution)/shard_map/ppermute | solution.py:423
  19.4 1.0 %collective-permute-start.7 = (bf16[272,128]{1,0:T(8,128)(2,1)S(1)}, bf16[272,128]{1,0:T(8,128)(2,1)S(1)}, u32[]{:S(2)}, u32[]{:S(2)}) collective-permute-start(bf16[272,128]{1,0:T(8,128)(2,1)S(1)} %get-tuple-element.48), channel_id=1, source_target_pairs={{0,2},{2,0},{16,18},{18,16},{1,3},{3,1},{17,19},{19,17},{4,6},{6,4... | collective-permute-start | bytes 208904 | tf_op jit(solution)/shard_map/ppermute | solution.py:423
  20.4 1.1 %collective-permute-start.8 = (bf16[272,128]{1,0:T(8,128)(2,1)S(1)}, bf16[272,128]{1,0:T(8,128)(2,1)S(1)}, u32[]{:S(2)}, u32[]{:S(2)}) collective-permute-start(bf16[272,128]{1,0:T(8,128)(2,1)S(1)} %get-tuple-element.49), channel_id=1, source_target_pairs={{0,18},{2,16},{16,2},{18,0},{1,19},{3,17},{17,3},{19,1},{4,22},{6,... | collective-permute-start | bytes 208904 | tf_op jit(solution)/shard_map/ppermute | solution.py:423
  21.5 0.9 %collective-permute-done.6.refs_0_ = bf16[272,128]{1,0:T(8,128)(2,1)S(1)} collective-permute-done((bf16[272,128]{1,0:T(8,128)(2,1)S(1)}, bf16[272,128]{1,0:T(8,128)(2,1)S(1)}, u32[]{:S(2)}, u32[]{:S(2)}) %collective-permute-start.6) | collective-permute-done | bytes 69664 | tf_op jit(solution)/shard_map/ppermute | solution.py:423
  22.5 1.3 %collective-permute-done.7.refs_1_ = bf16[272,128]{1,0:T(8,128)(2,1)S(1)} collective-permute-done((bf16[272,128]{1,0:T(8,128)(2,1)S(1)}, bf16[272,128]{1,0:T(8,128)(2,1)S(1)}, u32[]{:S(2)}, u32[]{:S(2)}) %collective-permute-start.7) | collective-permute-done | bytes 69664 | tf_op jit(solution)/shard_map/ppermute | solution.py:423
  23.8 1.9 %collective-permute-done.8.refs_2_ = bf16[272,128]{1,0:T(8,128)(2,1)S(1)} collective-permute-done((bf16[272,128]{1,0:T(8,128)(2,1)S(1)}, bf16[272,128]{1,0:T(8,128)(2,1)S(1)}, u32[]{:S(2)}, u32[]{:S(2)}) %collective-permute-start.8) | collective-permute-done | bytes 69664 | tf_op jit(solution)/shard_map/ppermute | solution.py:423
  25.7 2.7 %collective-permute-start.11 = (bf16[272,128]{1,0:T(8,128)(2,1)S(1)}, bf16[272,128]{1,0:T(8,128)(2,1)S(1)}, u32[]{:S(2)}, u32[]{:S(2)}) collective-permute-start(bf16[272,128]{1,0:T(8,128)(2,1)S(1)} %shard_map.76.a_ref), channel_id=1, source_target_pairs={{0,12},{4,8},{8,4},{12,0},{1,13},{5,9},{9,5},{13,1},{2,14},{6,10},... | collective-permute-start | bytes 208904 | tf_op jit(solution)/shard_map/ppermute | solution.py:423
  28.9 1.2 %collective-permute-start.9 = (bf16[272,128]{1,0:T(8,128)(2,1)S(1)}, bf16[272,128]{1,0:T(8,128)(2,1)S(1)}, u32[]{:S(2)}, u32[]{:S(2)}) collective-permute-start(bf16[272,128]{1,0:T(8,128)(2,1)S(1)} %shard_map.76.a_ref), channel_id=1, source_target_pairs={{0,4},{4,0},{8,12},{12,8},{1,5},{5,1},{9,13},{13,9},{2,6},{6,2},{1... | collective-permute-start | bytes 208904 | tf_op jit(solution)/shard_map/ppermute | solution.py:423
  30.1 2.5 %shard_map.73 = (bf16[128,2,8,128]{3,2,1,0:T(8,128)(2,1)}, f32[8,128]{1,0:T(8,128)S(1)}) custom-call(bf16[4,64,1280]{2,1,0:T(8,128)(2,1)S(1)} %get-tuple-element.37.hidden_ref, bf16[27,64,128]{2,1,0:T(8,128)(2,1)S(1)} %bitcast.10), custom_call_target="tpu_custom_call" | custom-call | flops 900000000 | bytes 1626112 | tf_op jit(solution)/shard_map/pallas_call | solution.py:18
  32.6 1.5 %collective-permute-done.10.c_ref = bf16[272,128]{1,0:T(8,128)(2,1)S(1)} collective-permute-done((bf16[272,128]{1,0:T(8,128)(2,1)S(1)}, bf16[272,128]{1,0:T(8,128)(2,1)S(1)}, u32[]{:S(2)}, u32[]{:S(2)}) %collective-permute-start.10) | collective-permute-done | bytes 69664 | tf_op jit(solution)/shard_map/ppermute | solution.py:423
  34.2 1.1 %collective-permute-start.12 = (bf16[272,128]{1,0:T(8,128)(2,1)S(1)}, bf16[272,128]{1,0:T(8,128)(2,1)S(1)}, u32[]{:S(2)}, u32[]{:S(2)}) collective-permute-start(bf16[272,128]{1,0:T(8,128)(2,1)S(1)} %shard_map.77.own_ref), channel_id=1, source_target_pairs={{0,2},{2,0},{1,3},{3,1},{4,6},{6,4},{5,7},{7,5},{8,10},{10,8},{9,1... | collective-permute-start | bytes 208904 | tf_op jit(solution)/shard_map/ppermute | solution.py:423
  35.3 3.3 %collective-permute-done.12.got_ref = bf16[272,128]{1,0:T(8,128)(2,1)S(1)} collective-permute-done((bf16[272,128]{1,0:T(8,128)(2,1)S(1)}, bf16[272,128]{1,0:T(8,128)(2,1)S(1)}, u32[]{:S(2)}, u32[]{:S(2)}) %collective-permute-start.12) | collective-permute-done | bytes 69664 | tf_op jit(solution)/shard_map/ppermute | solution.py:423
  38.7 1.3 %collective-permute-done.13.got_ref = bf16[2,272,128]{2,1,0:T(8,128)(2,1)S(1)} collective-permute-done((bf16[2,272,128]{2,1,0:T(8,128)(2,1)S(1)}, bf16[2,272,128]{2,1,0:T(8,128)(2,1)S(1)}, u32[]{:S(2)}, u32[]{:S(2)}) %collective-permute-start.13) | collective-permute-done | bytes 139296 | tf_op jit(solution)/shard_map/ppermute | solution.py:423
  40.0 1.2 %shard_map.79 = (f32[27,32,32]{2,1,0:T(8,128)}, f32[27,64,64]{2,1,0:T(8,128)}) custom-call(bf16[2,272,128]{2,1,0:T(8,128)(2,1)S(1)} %shard_map.78.own_ref, bf16[2,272,128]{2,1,0:T(8,128)(2,1)S(1)} %collective-permute-done.13.got_ref), custom_call_target="tpu_custom_call" | custom-call | bytes 831488 | tf_op jit(solution)/shard_map/pallas_call | solution.py:18
  (25 shorter events, 2.3 us)
Async XLA Ops:
  0.6 4.7 %copy-start.1 = (bf16[1,128,2,8,128]{4,3,2,1,0:T(8,128)(2,1)S(1)}, bf16[1,128,2,8,128]{4,3,2,1,0:T(8,128)(2,1)}, u32[]{:S(2)}) copy-start(bf16[1,128,2,8,128]{4,3,2,1,0:T(8,128)(2,1)} %param.7) | copy-start | bytes 1572868
  0.6 4.7 %copy-start.2 = (bf16[27,128,64]{1,2,0:T(8,128)(2,1)S(1)}, bf16[27,128,64]{1,2,0:T(8,128)(2,1)}, u32[]{:S(2)}) copy-start(bf16[27,128,64]{1,2,0:T(8,128)(2,1)} %param.6) | copy-start | bytes 1327108
  0.7 6.9 %collective-permute-start.1 = (bf16[32,2,8,128]{3,2,1,0:T(8,128)(2,1)}, bf16[32,2,8,128]{3,2,1,0:T(8,128)(2,1)S(1)}, u32[]{:S(2)}, u32[]{:S(2)}) collective-permute-start(bf16[32,2,8,128]{3,2,1,0:T(8,128)(2,1)} %bitcast.5), channel_id=1, source_target_pairs={{0,16},{4,8},{8,4},{12,28},{16,0},{20,24},{24,20},{28,12},{1,17},{... | collective-permute-start | bytes 393224 | tf_op jit(solution)/shard_map/ppermute | solution.py:415
  3.7 5.2 %collective-permute-start = (bf16[32,2,8,128]{3,2,1,0:T(8,128)(2,1)}, bf16[32,2,8,128]{3,2,1,0:T(8,128)(2,1)S(1)}, u32[]{:S(2)}, u32[]{:S(2)}) collective-permute-start(bf16[32,2,8,128]{3,2,1,0:T(8,128)(2,1)} %bitcast.6), channel_id=1, source_target_pairs={{0,4},{4,0},{8,12},{12,8},{16,20},{20,16},{24,28},{28,24},{1,5},{5... | collective-permute-start | bytes 393224 | tf_op jit(solution)/shard_map/ppermute | solution.py:415
  5.3 1.8 %copy-start.3 = (bf16[27,64,32]{1,2,0:T(8,128)(2,1)S(1)}, bf16[27,64,32]{1,2,0:T(8,128)(2,1)}, u32[]{:S(2)}) copy-start(bf16[27,64,32]{1,2,0:T(8,128)(2,1)} %param.5) | copy-start | bytes 331780
  7.1 1.7 %copy-start = (bf16[1,32,2,8,128]{4,3,2,1,0:T(8,128)(2,1)S(1)}, bf16[1,32,2,8,128]{4,3,2,1,0:T(8,128)(2,1)}, u32[]{:S(2)}) copy-start(bf16[1,32,2,8,128]{4,3,2,1,0:T(8,128)(2,1)} %param.4) | copy-start | bytes 393220
  9.2 3.8 %collective-permute-start.2 = (bf16[6,32,256]{2,1,0:T(8,128)(2,1)S(1)}, bf16[6,32,256]{2,1,0:T(8,128)(2,1)S(1)}, u32[]{:S(2)}, u32[]{:S(2)}) collective-permute-start(bf16[6,32,256]{2,1,0:T(8,128)(2,1)S(1)} %get-tuple-element.31), channel_id=1, source_target_pairs={{0,1},{1,0},{2,3},{3,2},{16,17},{17,16},{18,19},{19,18},{4,5},{5,4... | collective-permute-start | bytes 294920 | tf_op jit(solution)/shard_map/ppermute | solution.py:415
  9.3 4.7 %collective-permute-start.3 = (bf16[6,32,256]{2,1,0:T(8,128)(2,1)S(1)}, bf16[6,32,256]{2,1,0:T(8,128)(2,1)S(1)}, u32[]{:S(2)}, u32[]{:S(2)}) collective-permute-start(bf16[6,32,256]{2,1,0:T(8,128)(2,1)S(1)} %get-tuple-element.32), channel_id=1, source_target_pairs={{0,16},{1,2},{2,1},{3,19},{16,0},{17,18},{18,17},{19,3},{4,20},{5,... | collective-permute-start | bytes 294920 | tf_op jit(solution)/shard_map/ppermute | solution.py:415
  15.5 2.4 %collective-permute-start.4 = (f32[2,2,216,128]{3,2,1,0:T(8,128)S(1)}, f32[2,2,216,128]{3,2,1,0:T(8,128)S(1)}, u32[]{:S(2)}, u32[]{:S(2)}) collective-permute-start(f32[2,2,216,128]{3,2,1,0:T(8,128)S(1)} %get-tuple-element.40), channel_id=1, source_target_pairs={{0,1},{1,0},{2,3},{3,2},{4,5},{5,4},{6,7},{7,6},{8,9},{9,8},{10,11... | collective-permute-start | bytes 1327112 | tf_op jit(solution)/shard_map/ppermute | solution.py:423
  16.5 1.4 %collective-permute-start.5 = (f32[2,2,56,128]{3,2,1,0:T(8,128)S(1)}, f32[2,2,56,128]{3,2,1,0:T(8,128)S(1)}, u32[]{:S(2)}, u32[]{:S(2)}) collective-permute-start(f32[2,2,56,128]{3,2,1,0:T(8,128)S(1)} %get-tuple-element.45), channel_id=1, source_target_pairs={{0,1},{1,0},{2,3},{3,2},{4,5},{5,4},{6,7},{7,6},{8,9},{9,8},{10,11... | collective-permute-start | bytes 344072 | tf_op jit(solution)/shard_map/ppermute | solution.py:423
  17.9 4.5 %collective-permute-start.6 = (bf16[272,128]{1,0:T(8,128)(2,1)S(1)}, bf16[272,128]{1,0:T(8,128)(2,1)S(1)}, u32[]{:S(2)}, u32[]{:S(2)}) collective-permute-start(bf16[272,128]{1,0:T(8,128)(2,1)S(1)} %get-tuple-element.47), channel_id=1, source_target_pairs={{0,16},{2,18},{16,0},{18,2},{1,17},{3,19},{17,1},{19,3},{4,20},{6,... | collective-permute-start | bytes 208904 | tf_op jit(solution)/shard_map/ppermute | solution.py:423
  19.4 4.3 %collective-permute-start.7 = (bf16[272,128]{1,0:T(8,128)(2,1)S(1)}, bf16[272,128]{1,0:T(8,128)(2,1)S(1)}, u32[]{:S(2)}, u32[]{:S(2)}) collective-permute-start(bf16[272,128]{1,0:T(8,128)(2,1)S(1)} %get-tuple-element.48), channel_id=1, source_target_pairs={{0,2},{2,0},{16,18},{18,16},{1,3},{3,1},{17,19},{19,17},{4,6},{6,4... | collective-permute-start | bytes 208904 | tf_op jit(solution)/shard_map/ppermute | solution.py:423
  20.4 5.2 %collective-permute-start.8 = (bf16[272,128]{1,0:T(8,128)(2,1)S(1)}, bf16[272,128]{1,0:T(8,128)(2,1)S(1)}, u32[]{:S(2)}, u32[]{:S(2)}) collective-permute-start(bf16[272,128]{1,0:T(8,128)(2,1)S(1)} %get-tuple-element.49), channel_id=1, source_target_pairs={{0,18},{2,16},{16,2},{18,0},{1,19},{3,17},{17,3},{19,1},{4,22},{6,... | collective-permute-start | bytes 208904 | tf_op jit(solution)/shard_map/ppermute | solution.py:423
  25.7 7.0 %collective-permute-start.11 = (bf16[272,128]{1,0:T(8,128)(2,1)S(1)}, bf16[272,128]{1,0:T(8,128)(2,1)S(1)}, u32[]{:S(2)}, u32[]{:S(2)}) collective-permute-start(bf16[272,128]{1,0:T(8,128)(2,1)S(1)} %shard_map.76.a_ref), channel_id=1, source_target_pairs={{0,12},{4,8},{8,4},{12,0},{1,13},{5,9},{9,5},{13,1},{2,14},{6,10},... | collective-permute-start | bytes 208904 | tf_op jit(solution)/shard_map/ppermute | solution.py:423
  28.4 5.8 %collective-permute-start.10 = (bf16[272,128]{1,0:T(8,128)(2,1)S(1)}, bf16[272,128]{1,0:T(8,128)(2,1)S(1)}, u32[]{:S(2)}, u32[]{:S(2)}) collective-permute-start(bf16[272,128]{1,0:T(8,128)(2,1)S(1)} %shard_map.76.a_ref), channel_id=1, source_target_pairs={{0,8},{4,12},{8,0},{12,4},{1,9},{5,13},{9,1},{13,5},{2,10},{6,14},... | collective-permute-start | bytes 208904 | tf_op jit(solution)/shard_map/ppermute | solution.py:423
  28.9 5.3 %collective-permute-start.9 = (bf16[272,128]{1,0:T(8,128)(2,1)S(1)}, bf16[272,128]{1,0:T(8,128)(2,1)S(1)}, u32[]{:S(2)}, u32[]{:S(2)}) collective-permute-start(bf16[272,128]{1,0:T(8,128)(2,1)S(1)} %shard_map.76.a_ref), channel_id=1, source_target_pairs={{0,4},{4,0},{8,12},{12,8},{1,5},{5,1},{9,13},{13,9},{2,6},{6,2},{1... | collective-permute-start | bytes 208904 | tf_op jit(solution)/shard_map/ppermute | solution.py:423
  34.2 4.4 %collective-permute-start.12 = (bf16[272,128]{1,0:T(8,128)(2,1)S(1)}, bf16[272,128]{1,0:T(8,128)(2,1)S(1)}, u32[]{:S(2)}, u32[]{:S(2)}) collective-permute-start(bf16[272,128]{1,0:T(8,128)(2,1)S(1)} %shard_map.77.own_ref), channel_id=1, source_target_pairs={{0,2},{2,0},{1,3},{3,1},{4,6},{6,4},{5,7},{7,5},{8,10},{10,8},{9,1... | collective-permute-start | bytes 208904 | tf_op jit(solution)/shard_map/ppermute | solution.py:423
  38.6 1.4 %collective-permute-start.13 = (bf16[2,272,128]{2,1,0:T(8,128)(2,1)S(1)}, bf16[2,272,128]{2,1,0:T(8,128)(2,1)S(1)}, u32[]{:S(2)}, u32[]{:S(2)}) collective-permute-start(bf16[2,272,128]{2,1,0:T(8,128)(2,1)S(1)} %shard_map.78.own_ref), channel_id=1, source_target_pairs={{0,1},{1,0},{2,3},{3,2},{4,5},{5,4},{6,7},{7,6},{8,9},{9,8},{10,11... | collective-permute-start | bytes 417800 | tf_op jit(solution)/shard_map/ppermute | solution.py:423

commit v11 on v10

--- a/solution.py
+++ b/solution.py
@@ -13,14 +13,15 @@
 VMEM_BYTES = 28 * 2**20
 
 
-def call(body, outs, args, scratch=(), flops=0, far=()):
+def call(body, outs, args, scratch=(), flops=0, far=(), far_outs=False, aliases=None):
     moved = sum(x.size * x.dtype.itemsize for x in (*outs, *args))
     return pl.pallas_call(
         body,
         out_shape=outs,
         in_specs=[pl.BlockSpec(memory_space=pl.ANY if n in far else pltpu.VMEM) for n in range(len(args))],
-        out_specs=[pl.BlockSpec(memory_space=pltpu.VMEM)] * len(outs),
+        out_specs=[pl.BlockSpec(memory_space=pl.ANY if far_outs else pltpu.VMEM)] * len(outs),
         scratch_shapes=list(scratch),
+        input_output_aliases=aliases or {},
         compiler_params=pltpu.CompilerParams(vmem_limit_bytes=VMEM_BYTES),
         cost_estimate=pl.CostEstimate(flops=flops, bytes_accessed=moved, transcendentals=0),
     )(*args)
@@ -138,7 +139,7 @@
     return [jnp.concatenate([left[d], deep_ref[d], right[d]], axis=1) for d in range(deep_ref.shape[0])]
 
 
-def pack(direct, blocks, refs, units_of):
+def pack(direct, refs, rows_of, blocks):
     if not direct:
         for j, block in enumerate(blocks):
             refs[0][j] = block
@@ -147,22 +148,16 @@
     parts, halves, length, _ = keep_ref.shape
     core = lax.axis_index("core") == 1
     for part in range(parts):
-        whole = units_of(part)
-        size = whole[0].shape[0]
-
-        def quarter(number, whole=whole, size=size):
-            values, row = [], number * length
-            while row < (number + 1) * length:
-                unit, start = divmod(row, size)
-                stop = min(size, start + (number + 1) * length - row)
-                values.append(whole[unit][start:stop])
-                row += stop - start
-            return jnp.concatenate(values, axis=0)
-
+        one, two = (jnp.concatenate(rows_of(part, c), axis=0) for c in range(2))
         for half in range(halves):
-            one, two = (quarter(2 * half + c) for c in range(2))
-            keep_ref[part, half] = jnp.where(core, two, one)
-            send_ref[part, half] = jnp.where(core, one, two)
+            at = slice(half * length, (half + 1) * length)
+            keep_ref[part, half] = jnp.where(core, two[at], one[at])
+            send_ref[part, half] = jnp.where(core, one[at], two[at])
+
+
+def folded(tail):
+    half = tail.shape[0] // 2
+    return jnp.concatenate([tail[:half], tail[half:]], axis=1)
 
 
 def activated(w1, rhs, d, depth, heights):
@@ -227,9 +222,16 @@
                 back = back_ref[d, :, at + 2 * LANES : at + 3 * LANES]
                 shares(back * slope, mid, delta_ref, d * cells + at)
     own = depth - 2
-    count = height - 2
-    left = jnp.concatenate([moved_ref[d, :, 2 * LANES : (2 + count) * LANES] for d in range(own)], axis=1)
-    right = jnp.concatenate([neighbours(hidden_ref, d, [0], count) for d in range(own)], axis=1)
+    left = jnp.concatenate(
+        [
+            jnp.concatenate([moved_ref[d, :, (2 - b) * LANES : (2 - b) * LANES + cells] for d in range(own)], axis=1)
+            for b in range(3)
+        ],
+        axis=0,
+    )
+    right = jnp.concatenate(
+        [jnp.concatenate([hidden_ref[d + a] for a in range(3)], axis=0) for d in range(own)], axis=1
+    )
     second_ref[...] = products(left, right)
     right = jnp.concatenate([neighbours(deep_ref, d, [0], height) for d in range(depth)], axis=1)
     first_ref[...] = products(delta_ref[...], right)
@@ -252,29 +254,35 @@
                 hidden_ref[d, :, (h + n) * LANES : (h + n + 1) * LANES] = value
                 at = ((2 if h else 0) + n) * LANES
                 slope_ref[d, :, at : at + LANES] = slope
-    own, last = depth - 2, height - 4
-    left = jnp.concatenate(
-        [moved_ref[d, :, at * LANES : (at + 2) * LANES] for d in range(own) for at in (0, last)], axis=1
-    )
-    right = jnp.concatenate([neighbours(hidden_ref, d, [0, last], 2) for d in range(own)], axis=1)
-    total = second_ref[...] + products(left, right)
-    out = left.shape[0] // 3
-    blocks, tails = [], []
-    for n in range(3):
-        part = total[n * out : (n + 1) * out]
-        blocks += [part[:, m * LANES : (m + 1) * LANES] for m in range(4)]
-        tails.append(part[:, 4 * LANES :])
-    blocks.append(jnp.concatenate(tails[:2], axis=1))
-    blocks.append(jnp.concatenate([tails[2], jnp.zeros_like(tails[2])], axis=1))
+    own = depth - 2
+    out = moved_ref.shape[1] // 3
+    heads, tails = [], []
+    for b in range(3):
+        far = [h for h in range(height - 2) if not 2 <= h + b <= height - 3]
+        left = jnp.concatenate(
+            [moved_ref[d, :, h * LANES : (h + 1) * LANES] for d in range(own) for h in far], axis=1
+        )
+        right = jnp.concatenate(
+            [
+                jnp.concatenate([hidden_ref[d + a, :, (h + b) * LANES : (h + b + 1) * LANES] for a in range(3)], axis=0)
+                for d in range(own)
+                for h in far
+            ],
+            axis=1,
+        )
+        total = second_ref[3 * b * out : 3 * (b + 1) * out, :] + products(left, right)
+        for c in range(3):
+            part = total[c * out : (c + 1) * out]
+            heads.append(part[:, :LANES])
+            tails.append(part[:, LANES:])
+    blocks = heads + [jnp.concatenate(tails[n : n + 2], axis=1) for n in range(0, 8, 2)]
     size = mid // lax.axis_size("dp")
 
-    def units_of(part):
-        rows = [slice((2 * part + half) * size, (2 * part + half + 1) * size) for half in range(2)]
-        return [block[at] for block in blocks[:13] for at in rows] + [
-            jnp.concatenate([tails[2][at] for at in rows], axis=1)
-        ]
-
-    pack(direct, blocks, grad_refs, units_of)
+    def rows_of(part, core):
+        at = slice((2 * part + core) * size, (2 * part + core + 1) * size)
+        return [block[at] for block in blocks] + [folded(tails[8][at])]
+
+    pack(direct, grad_refs, rows_of, [*blocks, jnp.concatenate([tails[8], jnp.zeros_like(tails[8])], axis=1)])
 
 
 def features_kernel(hidden_ref, k2_ref, out_ref, token_ref, scratch):
@@ -318,7 +326,12 @@
     tails.append(jnp.zeros((mid, LANES - 3 * inner), F32))
     blocks.append(jnp.concatenate(tails, axis=1))
     size = mid // lax.axis_size("dp")
-    pack(direct, blocks, grad_refs, lambda part: [block[part * size : (part + 1) * size] for block in blocks])
+    half = size // 2
+
+    def rows_of(part, core):
+        return [block[part * size + core * half : part * size + (core + 1) * half] for block in blocks]
+
+    pack(direct, grad_refs, rows_of, blocks)
 
 
 def plane_kernel(moves, *refs):
@@ -355,51 +368,35 @@
     out_ref[1 - mine] = got_ref[...]
 
 
-def quarters_of(own_ref, got_ref):
-    core = lax.axis_index("core") == 1
-    quarters = []
-    for n in range(own_ref.shape[0]):
-        own, got = (ref[n].astype(F32) for ref in (own_ref, got_ref))
-        quarters += [jnp.where(core, got, own), jnp.where(core, own, got)]
-    return quarters
-
-
-def units_in(quarters, size):
-    length = quarters[0].shape[0]
-
-    def get(unit):
-        values, row = [], unit * size
-        while row < (unit + 1) * size:
-            number, start = divmod(row, length)
-            stop = min(length, start + (unit + 1) * size - row)
-            values.append(quarters[number][start:stop])
-            row += stop - start
-        return values[0] if len(values) == 1 else jnp.concatenate(values, axis=0)
-
-    return get
-
-
-def unpack_kernel(length, own_ref, got_ref, first_ref, second_ref):
-    quarters = quarters_of(own_ref, got_ref)
-    size, inner = first_ref.shape[1:]
-    mid = second_ref.shape[2]
-    get = units_in([quarter[:length] for quarter in quarters], size)
+def unpack_kernel(length, theirs, in_ref, *refs):
+    first_ref, second_ref, first, second, sems = refs[-5:]
+    core = lax.axis_index("core")
+    at = 1 - core if theirs else core
+    _, size, mid = second.shape
+    whole = [in_ref[n].astype(F32) for n in range(in_ref.shape[0])]
+    rows = jnp.concatenate([x[:length] for x in whole], axis=0)
     for j in range(13):
-        for half in range(2):
-            value = get(2 * j + half)
-            for m in range(2):
-                c, ab = (j // 4, 2 * (j % 4) + m) if j < 12 else (m, 8)
-                second_ref[3 * ab + c, half * size : (half + 1) * size, :] = value[:, m * mid : (m + 1) * mid]
-    value = get(26)
-    for half in range(2):
-        second_ref[26, half * size : (half + 1) * size, :] = value[:, half * mid : (half + 1) * mid]
-    get = units_in([quarter[length:] for quarter in quarters], size)
+        value = rows[j * size : (j + 1) * size]
+        for m, k in enumerate((j, 9 + j) if j < 9 else (2 * j, 2 * j + 1)):
+            second[k] = value[:, m * mid : (m + 1) * mid]
+    value = rows[13 * size : 13 * size + size // 2]
+    second[26] = jnp.concatenate([value[:, :mid], value[:, mid:]], axis=0)
+    copies = [pltpu.make_async_copy(second, second_ref.at[:, pl.ds(pl.multiple_of(at * size, size), size), :], sems.at[1])]
+    copies[0].start()
+    _, half, inner = first.shape
+    rows = jnp.concatenate([x[length:] for x in whole], axis=0)
     for j in range(7):
-        value = get(j)
+        value = rows[j * half : (j + 1) * half]
         for m in range(4):
             c, ab = (j // 2, 4 * (j % 2) + m) if j < 6 else (m, 8)
             if c < 3:
-                first_ref[3 * ab + c] = value[:, m * inner : (m + 1) * inner]
+                first[3 * ab + c] = value[:, m * inner : (m + 1) * inner]
+    copies.append(
+        pltpu.make_async_copy(first, first_ref.at[:, pl.ds(pl.multiple_of(at * half, half), half), :], sems.at[0])
+    )
+    copies[1].start()
+    for copy in copies:
+        copy.wait()
 
 
 def swapped(x, axis, first):
@@ -423,14 +420,35 @@
     return lax.ppermute(x, axes, [(i, i ^ flip) for i in range(lax.axis_size(axes))])
 
 
-def scattered(units, length):
-    parts, halves = units.shape[0], lax.axis_size("y")
-    grad = units.reshape(parts, -1, LANES)
-    grad = jnp.pad(grad, ((0, 0), (0, 2 * halves * length - grad.shape[1]), (0, 0)))
-    grad = lax.psum_scatter(grad, "dp", scatter_dimension=0, tiled=True).reshape(1, halves, 2, length, LANES)
+def scattered(rows, length):
+    halves = lax.axis_size("y")
+    grad = jnp.pad(rows, ((0, 0), (0, 0), (0, halves * length - rows.shape[2]), (0, 0)))
+    grad = lax.psum_scatter(grad, "dp", scatter_dimension=0, tiled=True)
+    grad = grad.reshape(1, 2, halves, length, LANES)
     core = lax.axis_index("core")
-    keep, send = (lax.dynamic_index_in_dim(grad, at, 2, False) for at in (core, 1 - core))
-    return keep, send
+    return tuple(lax.dynamic_index_in_dim(grad, at, 1, False) for at in (core, 1 - core))
+
+
+def assembled(own, got, length, size, inner, mid):
+    core = lax.axis_index("core")
+    both = jnp.stack([own, got]).astype(F32)
+    both = jnp.stack([lax.dynamic_index_in_dim(both, at, 0, False) for at in (core, 1 - core)])
+    rows = both[:, :, :length].reshape(2, -1, LANES)
+    second = [None] * 27
+    for j in range(13):
+        for m, k in enumerate((j, 9 + j) if j < 9 else (2 * j, 2 * j + 1)):
+            second[k] = rows[:, j * size : (j + 1) * size, m * mid : (m + 1) * mid].reshape(2 * size, mid)
+    tail = rows[:, 13 * size : 13 * size + size // 2]
+    second[26] = jnp.concatenate([tail[:, :, :mid], tail[:, :, mid:]], axis=1).reshape(2 * size, mid)
+    rows, half = both[:, :, length:].reshape(2, -1, LANES), size // 2
+    first = [None] * 27
+    for j in range(7):
+        for m in range(4):
+            c, ab = (j // 2, 4 * (j % 2) + m) if j < 6 else (m, 8)
+            if c < 3:
+                value = rows[:, j * half : (j + 1) * half, m * inner : (m + 1) * inner]
+                first[3 * ab + c] = value.reshape(size, inner)
+    return jnp.stack(first), jnp.stack(second)
 
 
 def per_device(volume, kernel_first, kernel_second, cotangent):
@@ -475,7 +493,7 @@
         inner_kernel,
         [
             shape((depth + 2, mid, rows_in * width), BF),
-            shape((3 * out, 9 * mid), F32),
+            shape((9 * out, 3 * mid), F32),
             shape((3 * mid, 9 * inner), F32),
         ],
         [deep, w1, moved, back],
@@ -505,14 +523,16 @@
         flops=4_000_000_000,
     )
     if direct:
-        moves = [(1, 0), (0, 1), (1, 1)]
+        moves = [(1, 1), (0, 1), (1, 0)]
     else:
         moves = [(0, 1)]
-        blocks = jnp.swapaxes(second[0].reshape(14, parts, 2, size, LANES), 0, 1)
-        tail = jnp.concatenate([blocks[:, 13, half, :, :mid] for half in range(2)], axis=-1)
-        units = jnp.concatenate([blocks[:, :13].reshape(parts, 26, size, LANES), tail[:, None]], axis=1)
-        second = scattered(units, length_second)
-        first = scattered(jnp.swapaxes(first[0].reshape(7, parts, size, LANES), 0, 1), length_first)
+        blocks = second[0].reshape(14, parts, 2, size, LANES).transpose(1, 2, 0, 3, 4)
+        tail = blocks[:, :, 13, :, :mid]
+        tail = jnp.concatenate([tail[:, :, : size // 2], tail[:, :, size // 2 :]], axis=-1)
+        rows_second = jnp.concatenate([blocks[:, :, :13].reshape(parts, 2, 13 * size, LANES), tail], axis=2)
+        second = scattered(rows_second, length_second)
+        blocks = first[0].reshape(7, parts, 2, size // 2, LANES).transpose(1, 2, 0, 3, 4)
+        first = scattered(blocks.reshape(parts, 2, 7 * (size // 2), LANES), length_first)
     block = (length_second + length_first, width)
     kept, *sends = call(
         functools.partial(plane_kernel, moves),
@@ -531,11 +551,26 @@
     gots = [across(share, ("dep", bits)) for bits in (1, 2, 3)]
     (share,) = call(depth_kernel, [shape(block, BF)], [share, *gots, token])
     (own,) = call(order_kernel, [shape((halves, *block), BF)], [share, across(share, ("y", 1))])
-    grad_first, grad_second = call(
-        functools.partial(unpack_kernel, length_second),
-        [shape((27, size, inner), F32), shape((27, 2 * size, mid), F32)],
-        [own, across(own, ("core", 1))],
-    )
+    got = across(own, ("core", 1))
+    if size % 16 == 0:
+        grads = [shape((27, size, inner), F32), shape((27, 2 * size, mid), F32)]
+        scratch = [
+            pltpu.VMEM((27, size // 2, inner), F32),
+            pltpu.VMEM((27, size, mid), F32),
+            pltpu.SemaphoreType.DMA((2,)),
+        ]
+        written = call(functools.partial(unpack_kernel, length_second, False), grads, [own], scratch, far_outs=True)
+        grad_first, grad_second = call(
+            functools.partial(unpack_kernel, length_second, True),
+            grads,
+            [got, *written],
+            scratch,
+            far=(1, 2),
+            far_outs=True,
+            aliases={1: 0, 2: 1},
+        )
+    else:
+        grad_first, grad_second = assembled(own, got, length_second, size, inner, mid)
     return features[None], grad_first, grad_second
 
 

time: 41.4 us -> 41.4 us (level)
  Pallas kernels: 11 us -> 11.8 us
  waiting for transfers between devices: 13.5 us -> 12.7 us
    pallas_call x13 -> x14, Pallas kernels: 11 us -> 11.8 us  [call(): pl.pallas_call(body, out_shape=outs, in_specs=[pl.BlockSpec(memory_space=...]
  transfers between devices with their start and end apart: 14 -> 14, of which waited for: 9 -> 9; matrix products, arithmetic and copies ran while one was open for 0% -> 0% of each run, Pallas kernels for 19% -> 22%
where the time goes in v11:
time: 41.4 us; the launch traced here: 41.2 us
  starting transfers between devices  15.9 us (38%)
  waiting for transfers between devices  12.7 us (31%)
  Pallas kernels  11.8 us (29%)
  between operations  0.79 us (2%)
    pallas_call x14, Pallas kernels, call(): pl.pallas_call(body, out_shape=outs, in_specs=[pl.BlockSpec(memory_space=...  11.8 us
    ppermute x10, waiting for transfers between devices, across(): lax.ppermute(x, axes, [(i, i ^ flip) for i in range(lax.axis_size(axes))])  10.9 us
    ppermute x10, starting transfers between devices, across(): lax.ppermute(x, axes, [(i, i ^ flip) for i in range(lax.axis_size(axes))])  9.67 us
    ppermute x4, starting transfers between devices, swapped(): return lax.ppermute(x, ('dp', *axes), list(enumerate(partner)))  6.23 us
    ppermute x4, waiting for transfers between devices, swapped(): return lax.ppermute(x, ('dp', *axes), list(enumerate(partner)))  1.82 us
  transfers between devices with their start and end apart: 14, of which 9 were waited for; matrix products, arithmetic and copies ran while one was open for 0% of the time, Pallas kernels for 22%

profile of v11, /device:TPU:0, one launch (start us, length us, event | category | flops | bytes accessed | tf_op | source)
XLA Modules:
  0.0 41.2 jit_solution(15785812195757286918)
XLA Ops:
  0.7 3.0 %collective-permute-start.1 = (bf16[32,2,8,128]{3,2,1,0:T(8,128)(2,1)}, bf16[32,2,8,128]{3,2,1,0:T(8,128)(2,1)S(1)}, u32[]{:S(2)}, u32[]{:S(2)}) collective-permute-start(bf16[32,2,8,128]{3,2,1,0:T(8,128)(2,1)} %bitcast.5), channel_id=1, source_target_pairs={{0,16},{4,8},{8,4},{12,28},{16,0},{20,24},{24,20},{28,12},{1,17},{... | collective-permute-start | bytes 393224 | tf_op jit(solution)/shard_map/ppermute | solution.py:412
  3.7 1.7 %collective-permute-start = (bf16[32,2,8,128]{3,2,1,0:T(8,128)(2,1)}, bf16[32,2,8,128]{3,2,1,0:T(8,128)(2,1)S(1)}, u32[]{:S(2)}, u32[]{:S(2)}) collective-permute-start(bf16[32,2,8,128]{3,2,1,0:T(8,128)(2,1)} %bitcast.6), channel_id=1, source_target_pairs={{0,4},{4,0},{8,12},{12,8},{16,20},{20,16},{24,28},{28,24},{1,5},{5... | collective-permute-start | bytes 393224 | tf_op jit(solution)/shard_map/ppermute | solution.py:412
  5.3 1.7 %shard_map.68 = (bf16[2,128,1024]{2,1,0:T(8,128)(2,1)S(1)}, f32[4,64,1280]{2,1,0:T(8,128)S(1)}) custom-call(bf16[128,2,8,128]{3,2,1,0:T(8,128)(2,1)S(1)} %bitcast.8, bf16[27,64,128]{2,1,0:T(8,128)(2,1)S(1)} %bitcast.9, bf16[128,256]{1,0:T(8,128)(2,1)S(1)} %shard_map.67.blank_ref), custom_call_target="tpu_custom_call" | custom-call | flops 1100000000 | bytes 2867200 | tf_op jit(solution)/shard_map/pallas_call | solution.py:18
  7.1 0.5 %shard_map.69 = (bf16[2,384,1024]{2,1,0:T(8,128)(2,1)S(1)}, bf16[192,288]{1,0:T(8,128)(2,1)S(1)}) custom-call(bf16[2,128,1024]{2,1,0:T(8,128)(2,1)S(1)} %get-tuple-element.30.cot_rows_ref, bf16[27,32,64]{2,1,0:T(8,128)(2,1)S(1)} %bitcast.11), custom_call_target="tpu_custom_call" | custom-call | flops 500000000 | bytes 2318336 | tf_op jit(solution)/shard_map/pallas_call | solution.py:18
  7.6 1.2 %collective-permute-done.one_ref = bf16[32,2,8,128]{3,2,1,0:T(8,128)(2,1)S(1)} collective-permute-done((bf16[32,2,8,128]{3,2,1,0:T(8,128)(2,1)}, bf16[32,2,8,128]{3,2,1,0:T(8,128)(2,1)S(1)}, u32[]{:S(2)}, u32[]{:S(2)}) %collective-permute-start) | collective-permute-done | bytes 131104 | tf_op jit(solution)/shard_map/ppermute | solution.py:412
  9.3 1.5 %collective-permute-start.3 = (bf16[6,32,256]{2,1,0:T(8,128)(2,1)S(1)}, bf16[6,32,256]{2,1,0:T(8,128)(2,1)S(1)}, u32[]{:S(2)}, u32[]{:S(2)}) collective-permute-start(bf16[6,32,256]{2,1,0:T(8,128)(2,1)S(1)} %get-tuple-element.34), channel_id=1, source_target_pairs={{0,16},{1,2},{2,1},{3,19},{16,0},{17,18},{18,17},{19,3},{4,20},{5,... | collective-permute-start | bytes 294920 | tf_op jit(solution)/shard_map/ppermute | solution.py:412
  10.8 2.6 %shard_map.71 = (bf16[4,64,768]{2,1,0:T(8,128)(2,1)S(1)}, f32[1152,192]{1,0:T(8,128)S(1)}, f32[192,288]{1,0:T(8,128)S(1)}) custom-call(bf16[6,32,1024]{2,1,0:T(8,128)(2,1)S(1)} %get-tuple-element.32.deep_ref, bf16[192,288]{1,0:T(8,128)(2,1)S(1)} %get-tuple-element.31._.w1_ref, bf16[2,384,1024]{2,1,0:T(8,128)(2,1)S(1)} %get-tuple-element.35.moved_ref, ...), custom_call_target="tpu_custom_call" | custom-call | flops 1500000000 | bytes 4886528 | tf_op jit(solution)/shard_map/pallas_call | solution.py:18
  13.4 0.6 %collective-permute-done.3.two_ref = bf16[6,32,256]{2,1,0:T(8,128)(2,1)S(1)} collective-permute-done((bf16[6,32,256]{2,1,0:T(8,128)(2,1)S(1)}, bf16[6,32,256]{2,1,0:T(8,128)(2,1)S(1)}, u32[]{:S(2)}, u32[]{:S(2)}) %collective-permute-start.3) | collective-permute-done | bytes 98336 | tf_op jit(solution)/shard_map/ppermute | solution.py:412
  14.0 1.3 %shard_map.72 = (bf16[4,64,1280]{2,1,0:T(8,128)(2,1)S(1)}, f32[4,64,512]{2,1,0:T(8,128)S(1)}, bf16[6,32,1536]{2,1,0:T(8,128)(2,1)S(1)}, f32[2,2,216,128]{3,2,1,0:T(8,128)S(1)}, f32[2,2,216,128]{3,2,1,0:T(8,128)S(1)}) custom-call(bf16[6,32,1024]{2,1,0:T(8,128)(2,1)S(1)} %get-tuple-element.32.deep_ref, bf16[6,32,256]{2,1,0:T(8,128)(2,1)S(1)} %collective-permute-done.2.one_ref, ...), custom_call_target="tpu_custom_call" | custom-call | flops 1000000000 | bytes 6205440 | tf_op jit(solution)/shard_map/pallas_call | solution.py:18
  15.5 0.8 %shard_map.74 = (f32[2,2,56,128]{3,2,1,0:T(8,128)S(1)}, f32[2,2,56,128]{3,2,1,0:T(8,128)S(1)}) custom-call(bf16[6,32,1536]{2,1,0:T(8,128)(2,1)S(1)} %get-tuple-element.43.rows_ref, f32[4,64,1280]{2,1,0:T(8,128)S(1)} %get-tuple-element.36.back_ref, f32[4,64,512]{2,1,0:T(8,128)S(1)} %get-tuple-element.44.slope_ref, f32[192,288]{1,0:T(8,128)S(1)} %get-tuple-element.45.first_ref), custom_call_target="tpu_custom_call" | custom-call | flops 4000000000 | bytes 2875392 | tf_op jit(solution)/shard_map/pallas_call | solution.py:18
  16.7 1.0 %collective-permute-done.5.refs_3_ = f32[2,2,56,128]{3,2,1,0:T(8,128)S(1)} collective-permute-done((f32[2,2,56,128]{3,2,1,0:T(8,128)S(1)}, f32[2,2,56,128]{3,2,1,0:T(8,128)S(1)}, u32[]{:S(2)}, u32[]{:S(2)}) %collective-permute-start.5) | collective-permute-done | bytes 114720 | tf_op jit(solution)/shard_map/ppermute | solution.py:420
  17.7 1.9 %collective-permute-start.6 = (bf16[272,128]{1,0:T(8,128)(2,1)S(1)}, bf16[272,128]{1,0:T(8,128)(2,1)S(1)}, u32[]{:S(2)}, u32[]{:S(2)}) collective-permute-start(bf16[272,128]{1,0:T(8,128)(2,1)S(1)} %get-tuple-element.49), channel_id=1, source_target_pairs={{0,18},{2,16},{16,2},{18,0},{1,19},{3,17},{17,3},{19,1},{4,22},{6,... | collective-permute-start | bytes 208904 | tf_op jit(solution)/shard_map/ppermute | solution.py:420
  19.6 1.1 %collective-permute-start.7 = (bf16[272,128]{1,0:T(8,128)(2,1)S(1)}, bf16[272,128]{1,0:T(8,128)(2,1)S(1)}, u32[]{:S(2)}, u32[]{:S(2)}) collective-permute-start(bf16[272,128]{1,0:T(8,128)(2,1)S(1)} %get-tuple-element.50), channel_id=1, source_target_pairs={{0,2},{2,0},{16,18},{18,16},{1,3},{3,1},{17,19},{19,17},{4,6},{6,4... | collective-permute-start | bytes 208904 | tf_op jit(solution)/shard_map/ppermute | solution.py:420
  20.7 0.6 %collective-permute-start.8 = (bf16[272,128]{1,0:T(8,128)(2,1)S(1)}, bf16[272,128]{1,0:T(8,128)(2,1)S(1)}, u32[]{:S(2)}, u32[]{:S(2)}) collective-permute-start(bf16[272,128]{1,0:T(8,128)(2,1)S(1)} %get-tuple-element.51), channel_id=1, source_target_pairs={{0,16},{2,18},{16,0},{18,2},{1,17},{3,19},{17,1},{19,3},{4,20},{6,... | collective-permute-start | bytes 208904 | tf_op jit(solution)/shard_map/ppermute | solution.py:420
  21.3 1.9 %collective-permute-done.6.refs_0_ = bf16[272,128]{1,0:T(8,128)(2,1)S(1)} collective-permute-done((bf16[272,128]{1,0:T(8,128)(2,1)S(1)}, bf16[272,128]{1,0:T(8,128)(2,1)S(1)}, u32[]{:S(2)}, u32[]{:S(2)}) %collective-permute-start.6) | collective-permute-done | bytes 69664 | tf_op jit(solution)/shard_map/ppermute | solution.py:420
  23.2 1.4 %collective-permute-done.7.refs_1_ = bf16[272,128]{1,0:T(8,128)(2,1)S(1)} collective-permute-done((bf16[272,128]{1,0:T(8,128)(2,1)S(1)}, bf16[272,128]{1,0:T(8,128)(2,1)S(1)}, u32[]{:S(2)}, u32[]{:S(2)}) %collective-permute-start.7) | collective-permute-done | bytes 69664 | tf_op jit(solution)/shard_map/ppermute | solution.py:420
  25.1 3.0 %collective-permute-start.11 = (bf16[272,128]{1,0:T(8,128)(2,1)S(1)}, bf16[272,128]{1,0:T(8,128)(2,1)S(1)}, u32[]{:S(2)}, u32[]{:S(2)}) collective-permute-start(bf16[272,128]{1,0:T(8,128)(2,1)S(1)} %shard_map.76.a_ref), channel_id=1, source_target_pairs={{0,12},{4,8},{8,4},{12,0},{1,13},{5,9},{9,5},{13,1},{2,14},{6,10},... | collective-permute-start | bytes 208904 | tf_op jit(solution)/shard_map/ppermute | solution.py:420
  28.3 1.2 %collective-permute-start.9 = (bf16[272,128]{1,0:T(8,128)(2,1)S(1)}, bf16[272,128]{1,0:T(8,128)(2,1)S(1)}, u32[]{:S(2)}, u32[]{:S(2)}) collective-permute-start(bf16[272,128]{1,0:T(8,128)(2,1)S(1)} %shard_map.76.a_ref), channel_id=1, source_target_pairs={{0,4},{4,0},{8,12},{12,8},{1,5},{5,1},{9,13},{13,9},{2,6},{6,2},{1... | collective-permute-start | bytes 208904 | tf_op jit(solution)/shard_map/ppermute | solution.py:420
  29.5 2.5 %shard_map.73 = (bf16[128,2,8,128]{3,2,1,0:T(8,128)(2,1)}, f32[8,128]{1,0:T(8,128)S(1)}) custom-call(bf16[4,64,1280]{2,1,0:T(8,128)(2,1)S(1)} %get-tuple-element.39.hidden_ref, bf16[27,64,128]{2,1,0:T(8,128)(2,1)S(1)} %bitcast.10), custom_call_target="tpu_custom_call" | custom-call | flops 900000000 | bytes 1626112 | tf_op jit(solution)/shard_map/pallas_call | solution.py:18
  32.0 2.4 %collective-permute-done.10.c_ref = bf16[272,128]{1,0:T(8,128)(2,1)S(1)} collective-permute-done((bf16[272,128]{1,0:T(8,128)(2,1)S(1)}, bf16[272,128]{1,0:T(8,128)(2,1)S(1)}, u32[]{:S(2)}, u32[]{:S(2)}) %collective-permute-start.10) | collective-permute-done | bytes 69664 | tf_op jit(solution)/shard_map/ppermute | solution.py:420
  34.5 0.9 %collective-permute-start.12 = (bf16[272,128]{1,0:T(8,128)(2,1)S(1)}, bf16[272,128]{1,0:T(8,128)(2,1)S(1)}, u32[]{:S(2)}, u32[]{:S(2)}) collective-permute-start(bf16[272,128]{1,0:T(8,128)(2,1)S(1)} %shard_map.77.own_ref), channel_id=1, source_target_pairs={{0,2},{2,0},{1,3},{3,1},{4,6},{6,4},{5,7},{7,5},{8,10},{10,8},{9,1... | collective-permute-start | bytes 208904 | tf_op jit(solution)/shard_map/ppermute | solution.py:420
  35.4 3.5 %collective-permute-done.12.got_ref = bf16[272,128]{1,0:T(8,128)(2,1)S(1)} collective-permute-done((bf16[272,128]{1,0:T(8,128)(2,1)S(1)}, bf16[272,128]{1,0:T(8,128)(2,1)S(1)}, u32[]{:S(2)}, u32[]{:S(2)}) %collective-permute-start.12) | collective-permute-done | bytes 69664 | tf_op jit(solution)/shard_map/ppermute | solution.py:420
  38.9 0.9 %shard_map.79 = (f32[27,32,32]{2,1,0:T(8,128)}, f32[27,64,64]{2,1,0:T(8,128)}) custom-call(bf16[2,272,128]{2,1,0:T(8,128)(2,1)S(1)} %shard_map.78.in_ref), custom_call_target="tpu_custom_call" | custom-call | bytes 692224 | tf_op jit(solution)/shard_map/pallas_call | solution.py:18
  40.3 0.9 %shard_map.80 = (f32[27,32,32]{2,1,0:T(8,128)}, f32[27,64,64]{2,1,0:T(8,128)}) custom-call(bf16[2,272,128]{2,1,0:T(8,128)(2,1)S(1)} %collective-permute-done.13.in_ref, f32[27,32,32]{2,1,0:T(8,128)} %get-tuple-element.53.refs_0_, f32[27,64,64]{2,1,0:T(8,128)} %get-tuple-element.54.refs_1_), custom_call_target="tpu_custom_call", output_to_operand_aliasing={{0}: (1, {}), {1}: (2, {})} | custom-call | bytes 1245184 | tf_op jit(solution)/shard_map/pallas_call | solution.py:18
  (26 shorter events, 2.4 us)
Async XLA Ops:
  0.6 4.7 %copy-start.1 = (bf16[1,128,2,8,128]{4,3,2,1,0:T(8,128)(2,1)S(1)}, bf16[1,128,2,8,128]{4,3,2,1,0:T(8,128)(2,1)}, u32[]{:S(2)}) copy-start(bf16[1,128,2,8,128]{4,3,2,1,0:T(8,128)(2,1)} %param.7) | copy-start | bytes 1572868
  0.6 4.7 %copy-start.2 = (bf16[27,128,64]{1,2,0:T(8,128)(2,1)S(1)}, bf16[27,128,64]{1,2,0:T(8,128)(2,1)}, u32[]{:S(2)}) copy-start(bf16[27,128,64]{1,2,0:T(8,128)(2,1)} %param.6) | copy-start | bytes 1327108
  0.7 6.9 %collective-permute-start.1 = (bf16[32,2,8,128]{3,2,1,0:T(8,128)(2,1)}, bf16[32,2,8,128]{3,2,1,0:T(8,128)(2,1)S(1)}, u32[]{:S(2)}, u32[]{:S(2)}) collective-permute-start(bf16[32,2,8,128]{3,2,1,0:T(8,128)(2,1)} %bitcast.5), channel_id=1, source_target_pairs={{0,16},{4,8},{8,4},{12,28},{16,0},{20,24},{24,20},{28,12},{1,17},{... | collective-permute-start | bytes 393224 | tf_op jit(solution)/shard_map/ppermute | solution.py:412
  3.7 5.2 %collective-permute-start = (bf16[32,2,8,128]{3,2,1,0:T(8,128)(2,1)}, bf16[32,2,8,128]{3,2,1,0:T(8,128)(2,1)S(1)}, u32[]{:S(2)}, u32[]{:S(2)}) collective-permute-start(bf16[32,2,8,128]{3,2,1,0:T(8,128)(2,1)} %bitcast.6), channel_id=1, source_target_pairs={{0,4},{4,0},{8,12},{12,8},{16,20},{20,16},{24,28},{28,24},{1,5},{5... | collective-permute-start | bytes 393224 | tf_op jit(solution)/shard_map/ppermute | solution.py:412
  5.3 1.8 %copy-start.3 = (bf16[27,64,32]{1,2,0:T(8,128)(2,1)S(1)}, bf16[27,64,32]{1,2,0:T(8,128)(2,1)}, u32[]{:S(2)}) copy-start(bf16[27,64,32]{1,2,0:T(8,128)(2,1)} %param.5) | copy-start | bytes 331780
  7.1 1.7 %copy-start = (bf16[1,32,2,8,128]{4,3,2,1,0:T(8,128)(2,1)S(1)}, bf16[1,32,2,8,128]{4,3,2,1,0:T(8,128)(2,1)}, u32[]{:S(2)}) copy-start(bf16[1,32,2,8,128]{4,3,2,1,0:T(8,128)(2,1)} %param.4) | copy-start | bytes 393220
  9.2 4.2 %collective-permute-start.2 = (bf16[6,32,256]{2,1,0:T(8,128)(2,1)S(1)}, bf16[6,32,256]{2,1,0:T(8,128)(2,1)S(1)}, u32[]{:S(2)}, u32[]{:S(2)}) collective-permute-start(bf16[6,32,256]{2,1,0:T(8,128)(2,1)S(1)} %get-tuple-element.33), channel_id=1, source_target_pairs={{0,1},{1,0},{2,3},{3,2},{16,17},{17,16},{18,19},{19,18},{4,5},{5,4... | collective-permute-start | bytes 294920 | tf_op jit(solution)/shard_map/ppermute | solution.py:412
  9.3 4.7 %collective-permute-start.3 = (bf16[6,32,256]{2,1,0:T(8,128)(2,1)S(1)}, bf16[6,32,256]{2,1,0:T(8,128)(2,1)S(1)}, u32[]{:S(2)}, u32[]{:S(2)}) collective-permute-start(bf16[6,32,256]{2,1,0:T(8,128)(2,1)S(1)} %get-tuple-element.34), channel_id=1, source_target_pairs={{0,16},{1,2},{2,1},{3,19},{16,0},{17,18},{18,17},{19,3},{4,20},{5,... | collective-permute-start | bytes 294920 | tf_op jit(solution)/shard_map/ppermute | solution.py:412
  15.3 2.4 %collective-permute-start.4 = (f32[2,2,216,128]{3,2,1,0:T(8,128)S(1)}, f32[2,2,216,128]{3,2,1,0:T(8,128)S(1)}, u32[]{:S(2)}, u32[]{:S(2)}) collective-permute-start(f32[2,2,216,128]{3,2,1,0:T(8,128)S(1)} %get-tuple-element.42), channel_id=1, source_target_pairs={{0,1},{1,0},{2,3},{3,2},{4,5},{5,4},{6,7},{7,6},{8,9},{9,8},{10,11... | collective-permute-start | bytes 1327112 | tf_op jit(solution)/shard_map/ppermute | solution.py:420
  16.2 1.4 %collective-permute-start.5 = (f32[2,2,56,128]{3,2,1,0:T(8,128)S(1)}, f32[2,2,56,128]{3,2,1,0:T(8,128)S(1)}, u32[]{:S(2)}, u32[]{:S(2)}) collective-permute-start(f32[2,2,56,128]{3,2,1,0:T(8,128)S(1)} %get-tuple-element.47), channel_id=1, source_target_pairs={{0,1},{1,0},{2,3},{3,2},{4,5},{5,4},{6,7},{7,6},{8,9},{9,8},{10,11... | collective-permute-start | bytes 344072 | tf_op jit(solution)/shard_map/ppermute | solution.py:420
  17.7 5.5 %collective-permute-start.6 = (bf16[272,128]{1,0:T(8,128)(2,1)S(1)}, bf16[272,128]{1,0:T(8,128)(2,1)S(1)}, u32[]{:S(2)}, u32[]{:S(2)}) collective-permute-start(bf16[272,128]{1,0:T(8,128)(2,1)S(1)} %get-tuple-element.49), channel_id=1, source_target_pairs={{0,18},{2,16},{16,2},{18,0},{1,19},{3,17},{17,3},{19,1},{4,22},{6,... | collective-permute-start | bytes 208904 | tf_op jit(solution)/shard_map/ppermute | solution.py:420
  19.6 5.0 %collective-permute-start.7 = (bf16[272,128]{1,0:T(8,128)(2,1)S(1)}, bf16[272,128]{1,0:T(8,128)(2,1)S(1)}, u32[]{:S(2)}, u32[]{:S(2)}) collective-permute-start(bf16[272,128]{1,0:T(8,128)(2,1)S(1)} %get-tuple-element.50), channel_id=1, source_target_pairs={{0,2},{2,0},{16,18},{18,16},{1,3},{3,1},{17,19},{19,17},{4,6},{6,4... | collective-permute-start | bytes 208904 | tf_op jit(solution)/shard_map/ppermute | solution.py:420
  20.7 4.3 %collective-permute-start.8 = (bf16[272,128]{1,0:T(8,128)(2,1)S(1)}, bf16[272,128]{1,0:T(8,128)(2,1)S(1)}, u32[]{:S(2)}, u32[]{:S(2)}) collective-permute-start(bf16[272,128]{1,0:T(8,128)(2,1)S(1)} %get-tuple-element.51), channel_id=1, source_target_pairs={{0,16},{2,18},{16,0},{18,2},{1,17},{3,19},{17,1},{19,3},{4,20},{6,... | collective-permute-start | bytes 208904 | tf_op jit(solution)/shard_map/ppermute | solution.py:420
  25.1 7.0 %collective-permute-start.11 = (bf16[272,128]{1,0:T(8,128)(2,1)S(1)}, bf16[272,128]{1,0:T(8,128)(2,1)S(1)}, u32[]{:S(2)}, u32[]{:S(2)}) collective-permute-start(bf16[272,128]{1,0:T(8,128)(2,1)S(1)} %shard_map.76.a_ref), channel_id=1, source_target_pairs={{0,12},{4,8},{8,4},{12,0},{1,13},{5,9},{9,5},{13,1},{2,14},{6,10},... | collective-permute-start | bytes 208904 | tf_op jit(solution)/shard_map/ppermute | solution.py:420
  28.1 6.3 %collective-permute-start.10 = (bf16[272,128]{1,0:T(8,128)(2,1)S(1)}, bf16[272,128]{1,0:T(8,128)(2,1)S(1)}, u32[]{:S(2)}, u32[]{:S(2)}) collective-permute-start(bf16[272,128]{1,0:T(8,128)(2,1)S(1)} %shard_map.76.a_ref), channel_id=1, source_target_pairs={{0,8},{4,12},{8,0},{12,4},{1,9},{5,13},{9,1},{13,5},{2,10},{6,14},... | collective-permute-start | bytes 208904 | tf_op jit(solution)/shard_map/ppermute | solution.py:420
  28.3 6.1 %collective-permute-start.9 = (bf16[272,128]{1,0:T(8,128)(2,1)S(1)}, bf16[272,128]{1,0:T(8,128)(2,1)S(1)}, u32[]{:S(2)}, u32[]{:S(2)}) collective-permute-start(bf16[272,128]{1,0:T(8,128)(2,1)S(1)} %shard_map.76.a_ref), channel_id=1, source_target_pairs={{0,4},{4,0},{8,12},{12,8},{1,5},{5,1},{9,13},{13,9},{2,6},{6,2},{1... | collective-permute-start | bytes 208904 | tf_op jit(solution)/shard_map/ppermute | solution.py:420
  34.5 4.4 %collective-permute-start.12 = (bf16[272,128]{1,0:T(8,128)(2,1)S(1)}, bf16[272,128]{1,0:T(8,128)(2,1)S(1)}, u32[]{:S(2)}, u32[]{:S(2)}) collective-permute-start(bf16[272,128]{1,0:T(8,128)(2,1)S(1)} %shard_map.77.own_ref), channel_id=1, source_target_pairs={{0,2},{2,0},{1,3},{3,1},{4,6},{6,4},{5,7},{7,5},{8,10},{10,8},{9,1... | collective-permute-start | bytes 208904 | tf_op jit(solution)/shard_map/ppermute | solution.py:420
  38.9 1.4 %collective-permute-start.13 = (bf16[2,272,128]{2,1,0:T(8,128)(2,1)S(1)}, bf16[2,272,128]{2,1,0:T(8,128)(2,1)S(1)}, u32[]{:S(2)}, u32[]{:S(2)}) collective-permute-start(bf16[2,272,128]{2,1,0:T(8,128)(2,1)S(1)} %shard_map.78.in_ref), channel_id=1, source_target_pairs={{0,1},{1,0},{2,3},{3,2},{4,5},{5,4},{6,7},{7,6},{8,9},{9,8},{10,11... | collective-permute-start | bytes 417800 | tf_op jit(solution)/shard_map/ppermute | solution.py:420

commit v12 on v11

--- a/solution.py
+++ b/solution.py
@@ -238,7 +238,7 @@
 
 
 def outer_kernel(
-    direct, deep_ref, one_ref, two_ref, w1_ref, moved_ref, inner_ref, second_ref,
+    direct, deep_ref, two_ref, one_ref, w1_ref, moved_ref, inner_ref, second_ref,
     hidden_ref, slope_ref, rows_ref, *grad_refs,
 ):
     for d, row in enumerate(widened(deep_ref, one_ref, two_ref)):
@@ -512,7 +512,7 @@
             if direct
             else [shape((14, out, LANES), F32)]
         ),
-        [deep, one, two, w1, moved, inner_hidden, inner_second],
+        [deep, two, one, w1, moved, inner_hidden, inner_second],
         flops=1_000_000_000,
     )
     first = call(
@@ -523,7 +523,7 @@
         flops=4_000_000_000,
     )
     if direct:
-        moves = [(1, 1), (0, 1), (1, 0)]
+        moves = [(1, 0), (0, 1), (1, 1)]
     else:
         moves = [(0, 1)]
         blocks = second[0].reshape(14, parts, 2, size, LANES).transpose(1, 2, 0, 3, 4)

time: 41.4 us -> 40.8 us (0.986)
  waiting for transfers between devices: 12.7 us -> 11.9 us
    ppermute x10, waiting for transfers between devices: 10.9 us -> 10.3 us  [across(): lax.ppermute(x, axes, [(i, i ^ flip) for i in range(lax.axis_size(axes))])]
where the time goes in v12:
time: 40.8 us; the launch traced here: 40.7 us
  starting transfers between devices  16.2 us (40%)
  waiting for transfers between devices  11.9 us (29%)
  Pallas kernels  11.8 us (29%)
  between operations  0.78 us (2%)
    pallas_call x14, Pallas kernels, call(): pl.pallas_call(body, out_shape=outs, in_specs=[pl.BlockSpec(memory_space=...  11.8 us
    ppermute x10, waiting for transfers between devices, across(): lax.ppermute(x, axes, [(i, i ^ flip) for i in range(lax.axis_size(axes))])  10.3 us
    ppermute x10, starting transfers between devices, across(): lax.ppermute(x, axes, [(i, i ^ flip) for i in range(lax.axis_size(axes))])  9.8 us
    ppermute x4, starting transfers between devices, swapped(): return lax.ppermute(x, ('dp', *axes), list(enumerate(partner)))  6.36 us
    ppermute x4, waiting for transfers between devices, swapped(): return lax.ppermute(x, ('dp', *axes), list(enumerate(partner)))  1.63 us
  transfers between devices with their start and end apart: 14, of which 9 were waited for; matrix products, arithmetic and copies ran while one was open for 0% of the time, Pallas kernels for 22%

profile of v12, /device:TPU:0, one launch (start us, length us, event | category | flops | bytes accessed | tf_op | source)
XLA Modules:
  0.0 40.7 jit_solution(9969141548543348327)
XLA Ops:
  0.7 3.0 %collective-permute-start.1 = (bf16[32,2,8,128]{3,2,1,0:T(8,128)(2,1)}, bf16[32,2,8,128]{3,2,1,0:T(8,128)(2,1)S(1)}, u32[]{:S(2)}, u32[]{:S(2)}) collective-permute-start(bf16[32,2,8,128]{3,2,1,0:T(8,128)(2,1)} %bitcast.5), channel_id=1, source_target_pairs={{0,16},{4,8},{8,4},{12,28},{16,0},{20,24},{24,20},{28,12},{1,17},{... | collective-permute-start | bytes 393224 | tf_op jit(solution)/shard_map/ppermute | solution.py:412
  3.7 1.7 %collective-permute-start = (bf16[32,2,8,128]{3,2,1,0:T(8,128)(2,1)}, bf16[32,2,8,128]{3,2,1,0:T(8,128)(2,1)S(1)}, u32[]{:S(2)}, u32[]{:S(2)}) collective-permute-start(bf16[32,2,8,128]{3,2,1,0:T(8,128)(2,1)} %bitcast.6), channel_id=1, source_target_pairs={{0,4},{4,0},{8,12},{12,8},{16,20},{20,16},{24,28},{28,24},{1,5},{5... | collective-permute-start | bytes 393224 | tf_op jit(solution)/shard_map/ppermute | solution.py:412
  5.3 1.7 %shard_map.68 = (bf16[2,128,1024]{2,1,0:T(8,128)(2,1)S(1)}, f32[4,64,1280]{2,1,0:T(8,128)S(1)}) custom-call(bf16[128,2,8,128]{3,2,1,0:T(8,128)(2,1)S(1)} %bitcast.8, bf16[27,64,128]{2,1,0:T(8,128)(2,1)S(1)} %bitcast.9, bf16[128,256]{1,0:T(8,128)(2,1)S(1)} %shard_map.67.blank_ref), custom_call_target="tpu_custom_call" | custom-call | flops 1100000000 | bytes 2867200 | tf_op jit(solution)/shard_map/pallas_call | solution.py:18
  7.6 1.2 %collective-permute-done.one_ref = bf16[32,2,8,128]{3,2,1,0:T(8,128)(2,1)S(1)} collective-permute-done((bf16[32,2,8,128]{3,2,1,0:T(8,128)(2,1)}, bf16[32,2,8,128]{3,2,1,0:T(8,128)(2,1)S(1)}, u32[]{:S(2)}, u32[]{:S(2)}) %collective-permute-start) | collective-permute-done | bytes 131104 | tf_op jit(solution)/shard_map/ppermute | solution.py:412
  9.2 1.5 %collective-permute-start.2 = (bf16[6,32,256]{2,1,0:T(8,128)(2,1)S(1)}, bf16[6,32,256]{2,1,0:T(8,128)(2,1)S(1)}, u32[]{:S(2)}, u32[]{:S(2)}) collective-permute-start(bf16[6,32,256]{2,1,0:T(8,128)(2,1)S(1)} %get-tuple-element.33), channel_id=1, source_target_pairs={{0,16},{1,2},{2,1},{3,19},{16,0},{17,18},{18,17},{19,3},{4,20},{5,... | collective-permute-start | bytes 294920 | tf_op jit(solution)/shard_map/ppermute | solution.py:412
  10.9 2.6 %shard_map.71 = (bf16[4,64,768]{2,1,0:T(8,128)(2,1)S(1)}, f32[1152,192]{1,0:T(8,128)S(1)}, f32[192,288]{1,0:T(8,128)S(1)}) custom-call(bf16[6,32,1024]{2,1,0:T(8,128)(2,1)S(1)} %get-tuple-element.32.deep_ref, bf16[192,288]{1,0:T(8,128)(2,1)S(1)} %get-tuple-element.31._.w1_ref, bf16[2,384,1024]{2,1,0:T(8,128)(2,1)S(1)} %get-tuple-element.35.moved_ref, ...), custom_call_target="tpu_custom_call" | custom-call | flops 1500000000 | bytes 4886528 | tf_op jit(solution)/shard_map/pallas_call | solution.py:18
  13.9 1.3 %shard_map.72 = (bf16[4,64,1280]{2,1,0:T(8,128)(2,1)S(1)}, f32[4,64,512]{2,1,0:T(8,128)S(1)}, bf16[6,32,1536]{2,1,0:T(8,128)(2,1)S(1)}, f32[2,2,216,128]{3,2,1,0:T(8,128)S(1)}, f32[2,2,216,128]{3,2,1,0:T(8,128)S(1)}) custom-call(bf16[6,32,1024]{2,1,0:T(8,128)(2,1)S(1)} %get-tuple-element.32.deep_ref, bf16[6,32,256]{2,1,0:T(8,128)(2,1)S(1)} %collective-permute-done.2.two_ref, ...), custom_call_target="tpu_custom_call" | custom-call | flops 1000000000 | bytes 6205440 | tf_op jit(solution)/shard_map/pallas_call | solution.py:18
  15.3 0.8 %shard_map.74 = (f32[2,2,56,128]{3,2,1,0:T(8,128)S(1)}, f32[2,2,56,128]{3,2,1,0:T(8,128)S(1)}) custom-call(bf16[6,32,1536]{2,1,0:T(8,128)(2,1)S(1)} %get-tuple-element.43.rows_ref, f32[4,64,1280]{2,1,0:T(8,128)S(1)} %get-tuple-element.36.back_ref, f32[4,64,512]{2,1,0:T(8,128)S(1)} %get-tuple-element.44.slope_ref, f32[192,288]{1,0:T(8,128)S(1)} %get-tuple-element.45.first_ref), custom_call_target="tpu_custom_call" | custom-call | flops 4000000000 | bytes 2875392 | tf_op jit(solution)/shard_map/pallas_call | solution.py:18
  16.1 0.6 %collective-permute-start.5 = (f32[2,2,56,128]{3,2,1,0:T(8,128)S(1)}, f32[2,2,56,128]{3,2,1,0:T(8,128)S(1)}, u32[]{:S(2)}, u32[]{:S(2)}) collective-permute-start(f32[2,2,56,128]{3,2,1,0:T(8,128)S(1)} %get-tuple-element.47), channel_id=1, source_target_pairs={{0,1},{1,0},{2,3},{3,2},{4,5},{5,4},{6,7},{7,6},{8,9},{9,8},{10,11... | collective-permute-start | bytes 344072 | tf_op jit(solution)/shard_map/ppermute | solution.py:420
  16.6 1.0 %collective-permute-done.5.refs_3_ = f32[2,2,56,128]{3,2,1,0:T(8,128)S(1)} collective-permute-done((f32[2,2,56,128]{3,2,1,0:T(8,128)S(1)}, f32[2,2,56,128]{3,2,1,0:T(8,128)S(1)}, u32[]{:S(2)}, u32[]{:S(2)}) %collective-permute-start.5) | collective-permute-done | bytes 114720 | tf_op jit(solution)/shard_map/ppermute | solution.py:420
  17.7 1.5 %collective-permute-start.6 = (bf16[272,128]{1,0:T(8,128)(2,1)S(1)}, bf16[272,128]{1,0:T(8,128)(2,1)S(1)}, u32[]{:S(2)}, u32[]{:S(2)}) collective-permute-start(bf16[272,128]{1,0:T(8,128)(2,1)S(1)} %get-tuple-element.49), channel_id=1, source_target_pairs={{0,16},{2,18},{16,0},{18,2},{1,17},{3,19},{17,1},{19,3},{4,20},{6,... | collective-permute-start | bytes 208904 | tf_op jit(solution)/shard_map/ppermute | solution.py:420
  19.2 0.9 %collective-permute-start.7 = (bf16[272,128]{1,0:T(8,128)(2,1)S(1)}, bf16[272,128]{1,0:T(8,128)(2,1)S(1)}, u32[]{:S(2)}, u32[]{:S(2)}) collective-permute-start(bf16[272,128]{1,0:T(8,128)(2,1)S(1)} %get-tuple-element.50), channel_id=1, source_target_pairs={{0,2},{2,0},{16,18},{18,16},{1,3},{3,1},{17,19},{19,17},{4,6},{6,4... | collective-permute-start | bytes 208904 | tf_op jit(solution)/shard_map/ppermute | solution.py:420
  20.1 1.1 %collective-permute-start.8 = (bf16[272,128]{1,0:T(8,128)(2,1)S(1)}, bf16[272,128]{1,0:T(8,128)(2,1)S(1)}, u32[]{:S(2)}, u32[]{:S(2)}) collective-permute-start(bf16[272,128]{1,0:T(8,128)(2,1)S(1)} %get-tuple-element.51), channel_id=1, source_target_pairs={{0,18},{2,16},{16,2},{18,0},{1,19},{3,17},{17,3},{19,1},{4,22},{6,... | collective-permute-start | bytes 208904 | tf_op jit(solution)/shard_map/ppermute | solution.py:420
  21.2 0.9 %collective-permute-done.6.refs_0_ = bf16[272,128]{1,0:T(8,128)(2,1)S(1)} collective-permute-done((bf16[272,128]{1,0:T(8,128)(2,1)S(1)}, bf16[272,128]{1,0:T(8,128)(2,1)S(1)}, u32[]{:S(2)}, u32[]{:S(2)}) %collective-permute-start.6) | collective-permute-done | bytes 69664 | tf_op jit(solution)/shard_map/ppermute | solution.py:420
  22.2 1.3 %collective-permute-done.7.refs_1_ = bf16[272,128]{1,0:T(8,128)(2,1)S(1)} collective-permute-done((bf16[272,128]{1,0:T(8,128)(2,1)S(1)}, bf16[272,128]{1,0:T(8,128)(2,1)S(1)}, u32[]{:S(2)}, u32[]{:S(2)}) %collective-permute-start.7) | collective-permute-done | bytes 69664 | tf_op jit(solution)/shard_map/ppermute | solution.py:420
  23.5 1.8 %collective-permute-done.8.refs_2_ = bf16[272,128]{1,0:T(8,128)(2,1)S(1)} collective-permute-done((bf16[272,128]{1,0:T(8,128)(2,1)S(1)}, bf16[272,128]{1,0:T(8,128)(2,1)S(1)}, u32[]{:S(2)}, u32[]{:S(2)}) %collective-permute-start.8) | collective-permute-done | bytes 69664 | tf_op jit(solution)/shard_map/ppermute | solution.py:420
  25.4 2.8 %collective-permute-start.11 = (bf16[272,128]{1,0:T(8,128)(2,1)S(1)}, bf16[272,128]{1,0:T(8,128)(2,1)S(1)}, u32[]{:S(2)}, u32[]{:S(2)}) collective-permute-start(bf16[272,128]{1,0:T(8,128)(2,1)S(1)} %shard_map.76.a_ref), channel_id=1, source_target_pairs={{0,12},{4,8},{8,4},{12,0},{1,13},{5,9},{9,5},{13,1},{2,14},{6,10},... | collective-permute-start | bytes 208904 | tf_op jit(solution)/shard_map/ppermute | solution.py:420
  28.6 1.2 %collective-permute-start.9 = (bf16[272,128]{1,0:T(8,128)(2,1)S(1)}, bf16[272,128]{1,0:T(8,128)(2,1)S(1)}, u32[]{:S(2)}, u32[]{:S(2)}) collective-permute-start(bf16[272,128]{1,0:T(8,128)(2,1)S(1)} %shard_map.76.a_ref), channel_id=1, source_target_pairs={{0,4},{4,0},{8,12},{12,8},{1,5},{5,1},{9,13},{13,9},{2,6},{6,2},{1... | collective-permute-start | bytes 208904 | tf_op jit(solution)/shard_map/ppermute | solution.py:420
  29.8 2.5 %shard_map.73 = (bf16[128,2,8,128]{3,2,1,0:T(8,128)(2,1)}, f32[8,128]{1,0:T(8,128)S(1)}) custom-call(bf16[4,64,1280]{2,1,0:T(8,128)(2,1)S(1)} %get-tuple-element.39.hidden_ref, bf16[27,64,128]{2,1,0:T(8,128)(2,1)S(1)} %bitcast.10), custom_call_target="tpu_custom_call" | custom-call | flops 900000000 | bytes 1626112 | tf_op jit(solution)/shard_map/pallas_call | solution.py:18
  32.3 1.5 %collective-permute-done.10.c_ref = bf16[272,128]{1,0:T(8,128)(2,1)S(1)} collective-permute-done((bf16[272,128]{1,0:T(8,128)(2,1)S(1)}, bf16[272,128]{1,0:T(8,128)(2,1)S(1)}, u32[]{:S(2)}, u32[]{:S(2)}) %collective-permute-start.10) | collective-permute-done | bytes 69664 | tf_op jit(solution)/shard_map/ppermute | solution.py:420
  33.9 1.1 %collective-permute-start.12 = (bf16[272,128]{1,0:T(8,128)(2,1)S(1)}, bf16[272,128]{1,0:T(8,128)(2,1)S(1)}, u32[]{:S(2)}, u32[]{:S(2)}) collective-permute-start(bf16[272,128]{1,0:T(8,128)(2,1)S(1)} %shard_map.77.own_ref), channel_id=1, source_target_pairs={{0,2},{2,0},{1,3},{3,1},{4,6},{6,4},{5,7},{7,5},{8,10},{10,8},{9,1... | collective-permute-start | bytes 208904 | tf_op jit(solution)/shard_map/ppermute | solution.py:420
  35.0 3.3 %collective-permute-done.12.got_ref = bf16[272,128]{1,0:T(8,128)(2,1)S(1)} collective-permute-done((bf16[272,128]{1,0:T(8,128)(2,1)S(1)}, bf16[272,128]{1,0:T(8,128)(2,1)S(1)}, u32[]{:S(2)}, u32[]{:S(2)}) %collective-permute-start.12) | collective-permute-done | bytes 69664 | tf_op jit(solution)/shard_map/ppermute | solution.py:420
  38.4 0.9 %shard_map.79 = (f32[27,32,32]{2,1,0:T(8,128)}, f32[27,64,64]{2,1,0:T(8,128)}) custom-call(bf16[2,272,128]{2,1,0:T(8,128)(2,1)S(1)} %shard_map.78.in_ref), custom_call_target="tpu_custom_call" | custom-call | bytes 692224 | tf_op jit(solution)/shard_map/pallas_call | solution.py:18
  39.7 0.9 %shard_map.80 = (f32[27,32,32]{2,1,0:T(8,128)}, f32[27,64,64]{2,1,0:T(8,128)}) custom-call(bf16[2,272,128]{2,1,0:T(8,128)(2,1)S(1)} %collective-permute-done.13.in_ref, f32[27,32,32]{2,1,0:T(8,128)} %get-tuple-element.53.refs_0_, f32[27,64,64]{2,1,0:T(8,128)} %get-tuple-element.54.refs_1_), custom_call_target="tpu_custom_call", output_to_operand_aliasing={{0}: (1, {}), {1}: (2, {})} | custom-call | bytes 1245184 | tf_op jit(solution)/shard_map/pallas_call | solution.py:18
  (26 shorter events, 2.7 us)
Async XLA Ops:
  0.6 4.7 %copy-start.1 = (bf16[1,128,2,8,128]{4,3,2,1,0:T(8,128)(2,1)S(1)}, bf16[1,128,2,8,128]{4,3,2,1,0:T(8,128)(2,1)}, u32[]{:S(2)}) copy-start(bf16[1,128,2,8,128]{4,3,2,1,0:T(8,128)(2,1)} %param.7) | copy-start | bytes 1572868
  0.6 4.7 %copy-start.2 = (bf16[27,128,64]{1,2,0:T(8,128)(2,1)S(1)}, bf16[27,128,64]{1,2,0:T(8,128)(2,1)}, u32[]{:S(2)}) copy-start(bf16[27,128,64]{1,2,0:T(8,128)(2,1)} %param.6) | copy-start | bytes 1327108
  0.7 6.9 %collective-permute-start.1 = (bf16[32,2,8,128]{3,2,1,0:T(8,128)(2,1)}, bf16[32,2,8,128]{3,2,1,0:T(8,128)(2,1)S(1)}, u32[]{:S(2)}, u32[]{:S(2)}) collective-permute-start(bf16[32,2,8,128]{3,2,1,0:T(8,128)(2,1)} %bitcast.5), channel_id=1, source_target_pairs={{0,16},{4,8},{8,4},{12,28},{16,0},{20,24},{24,20},{28,12},{1,17},{... | collective-permute-start | bytes 393224 | tf_op jit(solution)/shard_map/ppermute | solution.py:412
  3.7 5.2 %collective-permute-start = (bf16[32,2,8,128]{3,2,1,0:T(8,128)(2,1)}, bf16[32,2,8,128]{3,2,1,0:T(8,128)(2,1)S(1)}, u32[]{:S(2)}, u32[]{:S(2)}) collective-permute-start(bf16[32,2,8,128]{3,2,1,0:T(8,128)(2,1)} %bitcast.6), channel_id=1, source_target_pairs={{0,4},{4,0},{8,12},{12,8},{16,20},{20,16},{24,28},{28,24},{1,5},{5... | collective-permute-start | bytes 393224 | tf_op jit(solution)/shard_map/ppermute | solution.py:412
  5.3 1.8 %copy-start.3 = (bf16[27,64,32]{1,2,0:T(8,128)(2,1)S(1)}, bf16[27,64,32]{1,2,0:T(8,128)(2,1)}, u32[]{:S(2)}) copy-start(bf16[27,64,32]{1,2,0:T(8,128)(2,1)} %param.5) | copy-start | bytes 331780
  7.1 1.7 %copy-start = (bf16[1,32,2,8,128]{4,3,2,1,0:T(8,128)(2,1)S(1)}, bf16[1,32,2,8,128]{4,3,2,1,0:T(8,128)(2,1)}, u32[]{:S(2)}) copy-start(bf16[1,32,2,8,128]{4,3,2,1,0:T(8,128)(2,1)} %param.4) | copy-start | bytes 393220
  9.2 4.7 %collective-permute-start.2 = (bf16[6,32,256]{2,1,0:T(8,128)(2,1)S(1)}, bf16[6,32,256]{2,1,0:T(8,128)(2,1)S(1)}, u32[]{:S(2)}, u32[]{:S(2)}) collective-permute-start(bf16[6,32,256]{2,1,0:T(8,128)(2,1)S(1)} %get-tuple-element.33), channel_id=1, source_target_pairs={{0,16},{1,2},{2,1},{3,19},{16,0},{17,18},{18,17},{19,3},{4,20},{5,... | collective-permute-start | bytes 294920 | tf_op jit(solution)/shard_map/ppermute | solution.py:412
  10.7 3.2 %collective-permute-start.3 = (bf16[6,32,256]{2,1,0:T(8,128)(2,1)S(1)}, bf16[6,32,256]{2,1,0:T(8,128)(2,1)S(1)}, u32[]{:S(2)}, u32[]{:S(2)}) collective-permute-start(bf16[6,32,256]{2,1,0:T(8,128)(2,1)S(1)} %get-tuple-element.34), channel_id=1, source_target_pairs={{0,1},{1,0},{2,3},{3,2},{16,17},{17,16},{18,19},{19,18},{4,5},{5,4... | collective-permute-start | bytes 294920 | tf_op jit(solution)/shard_map/ppermute | solution.py:412
  15.2 2.4 %collective-permute-start.4 = (f32[2,2,216,128]{3,2,1,0:T(8,128)S(1)}, f32[2,2,216,128]{3,2,1,0:T(8,128)S(1)}, u32[]{:S(2)}, u32[]{:S(2)}) collective-permute-start(f32[2,2,216,128]{3,2,1,0:T(8,128)S(1)} %get-tuple-element.42), channel_id=1, source_target_pairs={{0,1},{1,0},{2,3},{3,2},{4,5},{5,4},{6,7},{7,6},{8,9},{9,8},{10,11... | collective-permute-start | bytes 1327112 | tf_op jit(solution)/shard_map/ppermute | solution.py:420
  16.1 1.5 %collective-permute-start.5 = (f32[2,2,56,128]{3,2,1,0:T(8,128)S(1)}, f32[2,2,56,128]{3,2,1,0:T(8,128)S(1)}, u32[]{:S(2)}, u32[]{:S(2)}) collective-permute-start(f32[2,2,56,128]{3,2,1,0:T(8,128)S(1)} %get-tuple-element.47), channel_id=1, source_target_pairs={{0,1},{1,0},{2,3},{3,2},{4,5},{5,4},{6,7},{7,6},{8,9},{9,8},{10,11... | collective-permute-start | bytes 344072 | tf_op jit(solution)/shard_map/ppermute | solution.py:420
  17.7 4.5 %collective-permute-start.6 = (bf16[272,128]{1,0:T(8,128)(2,1)S(1)}, bf16[272,128]{1,0:T(8,128)(2,1)S(1)}, u32[]{:S(2)}, u32[]{:S(2)}) collective-permute-start(bf16[272,128]{1,0:T(8,128)(2,1)S(1)} %get-tuple-element.49), channel_id=1, source_target_pairs={{0,16},{2,18},{16,0},{18,2},{1,17},{3,19},{17,1},{19,3},{4,20},{6,... | collective-permute-start | bytes 208904 | tf_op jit(solution)/shard_map/ppermute | solution.py:420
  19.2 4.3 %collective-permute-start.7 = (bf16[272,128]{1,0:T(8,128)(2,1)S(1)}, bf16[272,128]{1,0:T(8,128)(2,1)S(1)}, u32[]{:S(2)}, u32[]{:S(2)}) collective-permute-start(bf16[272,128]{1,0:T(8,128)(2,1)S(1)} %get-tuple-element.50), channel_id=1, source_target_pairs={{0,2},{2,0},{16,18},{18,16},{1,3},{3,1},{17,19},{19,17},{4,6},{6,4... | collective-permute-start | bytes 208904 | tf_op jit(solution)/shard_map/ppermute | solution.py:420
  20.1 5.2 %collective-permute-start.8 = (bf16[272,128]{1,0:T(8,128)(2,1)S(1)}, bf16[272,128]{1,0:T(8,128)(2,1)S(1)}, u32[]{:S(2)}, u32[]{:S(2)}) collective-permute-start(bf16[272,128]{1,0:T(8,128)(2,1)S(1)} %get-tuple-element.51), channel_id=1, source_target_pairs={{0,18},{2,16},{16,2},{18,0},{1,19},{3,17},{17,3},{19,1},{4,22},{6,... | collective-permute-start | bytes 208904 | tf_op jit(solution)/shard_map/ppermute | solution.py:420
  25.4 7.0 %collective-permute-start.11 = (bf16[272,128]{1,0:T(8,128)(2,1)S(1)}, bf16[272,128]{1,0:T(8,128)(2,1)S(1)}, u32[]{:S(2)}, u32[]{:S(2)}) collective-permute-start(bf16[272,128]{1,0:T(8,128)(2,1)S(1)} %shard_map.76.a_ref), channel_id=1, source_target_pairs={{0,12},{4,8},{8,4},{12,0},{1,13},{5,9},{9,5},{13,1},{2,14},{6,10},... | collective-permute-start | bytes 208904 | tf_op jit(solution)/shard_map/ppermute | solution.py:420
  28.1 5.7 %collective-permute-start.10 = (bf16[272,128]{1,0:T(8,128)(2,1)S(1)}, bf16[272,128]{1,0:T(8,128)(2,1)S(1)}, u32[]{:S(2)}, u32[]{:S(2)}) collective-permute-start(bf16[272,128]{1,0:T(8,128)(2,1)S(1)} %shard_map.76.a_ref), channel_id=1, source_target_pairs={{0,8},{4,12},{8,0},{12,4},{1,9},{5,13},{9,1},{13,5},{2,10},{6,14},... | collective-permute-start | bytes 208904 | tf_op jit(solution)/shard_map/ppermute | solution.py:420
  28.6 5.2 %collective-permute-start.9 = (bf16[272,128]{1,0:T(8,128)(2,1)S(1)}, bf16[272,128]{1,0:T(8,128)(2,1)S(1)}, u32[]{:S(2)}, u32[]{:S(2)}) collective-permute-start(bf16[272,128]{1,0:T(8,128)(2,1)S(1)} %shard_map.76.a_ref), channel_id=1, source_target_pairs={{0,4},{4,0},{8,12},{12,8},{1,5},{5,1},{9,13},{13,9},{2,6},{6,2},{1... | collective-permute-start | bytes 208904 | tf_op jit(solution)/shard_map/ppermute | solution.py:420
  33.9 4.4 %collective-permute-start.12 = (bf16[272,128]{1,0:T(8,128)(2,1)S(1)}, bf16[272,128]{1,0:T(8,128)(2,1)S(1)}, u32[]{:S(2)}, u32[]{:S(2)}) collective-permute-start(bf16[272,128]{1,0:T(8,128)(2,1)S(1)} %shard_map.77.own_ref), channel_id=1, source_target_pairs={{0,2},{2,0},{1,3},{3,1},{4,6},{6,4},{5,7},{7,5},{8,10},{10,8},{9,1... | collective-permute-start | bytes 208904 | tf_op jit(solution)/shard_map/ppermute | solution.py:420
  38.3 1.4 %collective-permute-start.13 = (bf16[2,272,128]{2,1,0:T(8,128)(2,1)S(1)}, bf16[2,272,128]{2,1,0:T(8,128)(2,1)S(1)}, u32[]{:S(2)}, u32[]{:S(2)}) collective-permute-start(bf16[2,272,128]{2,1,0:T(8,128)(2,1)S(1)} %shard_map.78.in_ref), channel_id=1, source_target_pairs={{0,1},{1,0},{2,3},{3,2},{4,5},{5,4},{6,7},{7,6},{8,9},{9,8},{10,11... | collective-permute-start | bytes 417800 | tf_op jit(solution)/shard_map/ppermute | solution.py:420

commit v13 on v12

--- a/solution.py
+++ b/solution.py
@@ -96,7 +96,11 @@
     return stacked.astype(F32).T.astype(BF)
 
 
-def arrange_kernel(cot_rows_ref, k1_ref, moved_ref, w1_ref):
+def arrange_kernel(cot_rows_ref, k1_ref, vol_ref, moved_ref, w1_ref, own_ref, scratch):
+    def store(d, h, row):
+        own_ref[d, :, h * LANES : (h + 1) * LANES] = row.astype(BF)
+
+    by_rows(vol_ref, scratch, store)
     depth, out, cells = cot_rows_ref.shape
     for d in range(depth):
         for h in range(0, cells, LANES):
@@ -118,12 +122,12 @@
     return before, after
 
 
-def rim_kernel(own_ref, one_ref, two_ref, _, deep_ref, send_one_ref, send_two_ref, scratch):
-    depth = own_ref.shape[1]
-    before, after = sides("dep", one_ref[...], two_ref[...])
-    for n, part in enumerate((before, own_ref[...], after)):
-
-        def store(d, h, row, at=n * depth):
+def rim_kernel(own_ref, one_ref, two_ref, deep_ref, send_one_ref, send_two_ref, scratch):
+    depth = own_ref.shape[0]
+    deep_ref[depth : 2 * depth] = own_ref[...]
+    for at, part in zip((0, 2 * depth), sides("dep", one_ref[...], two_ref[...]), strict=True):
+
+        def store(d, h, row, at=at):
             deep_ref[at + d, :, h * LANES : (h + 1) * LANES] = row.astype(BF)
 
         by_rows(part, scratch, store)
@@ -152,7 +156,7 @@
         for half in range(halves):
             at = slice(half * length, (half + 1) * length)
             keep_ref[part, half] = jnp.where(core, two[at], one[at])
-            send_ref[part, half] = jnp.where(core, one[at], two[at])
+            send_ref[part, half] = jnp.where(core, one[at], two[at]).astype(send_ref.dtype)
 
 
 def folded(tail):
@@ -238,22 +242,45 @@
 
 
 def outer_kernel(
-    direct, deep_ref, two_ref, one_ref, w1_ref, moved_ref, inner_ref, second_ref,
-    hidden_ref, slope_ref, rows_ref, *grad_refs,
+    direct, deep_ref, two_ref, one_ref, w1_ref, back_ref, inner_ref, first_ref, hidden_ref, *grad_refs_and_scratch,
 ):
+    *grad_refs, rows_ref, delta_ref = grad_refs_and_scratch
     for d, row in enumerate(widened(deep_ref, one_ref, two_ref)):
         rows_ref[d] = row
     w1 = w1_ref[...]
     depth, mid, cells = hidden_ref.shape
-    height = cells // LANES
+    last = cells // LANES - 2
     for d in range(depth):
-        hidden_ref[d, :, 2 * LANES : cells - 2 * LANES] = inner_ref[d]
-        for h, sides_of in ((0, (-1, 0)), (height - 2, (0, 1))):
+        hidden_ref[d, :, 2 * LANES : last * LANES] = inner_ref[d]
+        for h, sides_of in ((0, (-1, 0)), (last, (0, 1))):
             results = activated(w1, neighbours(rows_ref, d, [h], 2), d, depth, sides_of)
             for n, (value, slope) in enumerate(results):
-                hidden_ref[d, :, (h + n) * LANES : (h + n + 1) * LANES] = value
-                at = ((2 if h else 0) + n) * LANES
-                slope_ref[d, :, at : at + LANES] = slope
+                at = (h + n) * LANES
+                hidden_ref[d, :, at : at + LANES] = value
+                delta = back_ref[d, :, at : at + LANES] * slope
+                shares(delta, mid, delta_ref, (4 * d + (2 if h else 0) + n) * LANES)
+    right = jnp.concatenate([neighbours(rows_ref, d, [0, last], 2) for d in range(depth)], axis=1)
+    total = first_ref[...] + products(delta_ref[...], right)
+    inner = rows_ref.shape[1]
+    blocks, tails = [], []
+    for n in range(3):
+        part = total[n * mid : (n + 1) * mid]
+        blocks += [part[:, m * LANES : (m + 1) * LANES] for m in range(2)]
+        tails.append(part[:, 2 * LANES :])
+    tails.append(jnp.zeros((mid, LANES - 3 * inner), F32))
+    blocks.append(jnp.concatenate(tails, axis=1))
+    size = mid // lax.axis_size("dp")
+    half = size // 2
+
+    def rows_of(part, core):
+        return [block[part * size + core * half : part * size + (core + 1) * half] for block in blocks]
+
+    pack(direct, grad_refs, rows_of, blocks)
+
+
+def second_kernel(direct, hidden_ref, moved_ref, second_ref, *grad_refs):
+    depth, mid, cells = hidden_ref.shape
+    height = cells // LANES
     own = depth - 2
     out = moved_ref.shape[1] // 3
     heads, tails = [], []
@@ -307,41 +334,14 @@
     token_ref[...] = scratch[:8]
 
 
-def delta_kernel(direct, rows_ref, back_ref, slope_ref, first_ref, *outs_and_scratch):
-    *grad_refs, delta_ref = outs_and_scratch
-    depth, mid, cells = slope_ref.shape
-    last = back_ref.shape[2] // LANES - 2
-    for d in range(depth):
-        for n, h in enumerate((0, 1, last, last + 1)):
-            delta = back_ref[d, :, h * LANES : (h + 1) * LANES] * slope_ref[d, :, n * LANES : (n + 1) * LANES]
-            shares(delta, mid, delta_ref, d * cells + n * LANES)
-    right = jnp.concatenate([neighbours(rows_ref, d, [0, last], 2) for d in range(depth)], axis=1)
-    total = first_ref[...] + products(delta_ref[...], right)
-    inner = rows_ref.shape[1]
-    blocks, tails = [], []
-    for n in range(3):
-        part = total[n * mid : (n + 1) * mid]
-        blocks += [part[:, m * LANES : (m + 1) * LANES] for m in range(2)]
-        tails.append(part[:, 2 * LANES :])
-    tails.append(jnp.zeros((mid, LANES - 3 * inner), F32))
-    blocks.append(jnp.concatenate(tails, axis=1))
-    size = mid // lax.axis_size("dp")
-    half = size // 2
-
-    def rows_of(part, core):
-        return [block[part * size + core * half : part * size + (core + 1) * half] for block in blocks]
-
-    pack(direct, grad_refs, rows_of, blocks)
-
-
 def plane_kernel(moves, *refs):
-    keep_second, got_second, keep_first, got_first, kept_ref, *send_refs = refs
+    keep_first, got_first, keep_second, got_second, kept_ref, *send_refs = refs
     part = lax.rem(lax.axis_index("dp"), keep_first.shape[0])
     half = lax.axis_index("y")
 
     def total(x, y):
         at = 1 - part if x else part, 1 - half if y else half
-        return jnp.concatenate([keep_second[at] + got_second[at], keep_first[at] + got_first[at]], axis=0)
+        return jnp.concatenate([keep_second[at] + got_second[at].astype(F32), keep_first[at] + got_first[at]], axis=0)
 
     kept_ref[...] = total(0, 0)
     for (x, y), send_ref in zip(moves, send_refs, strict=True):
@@ -471,16 +471,21 @@
         [pltpu.VMEM((out * rows, width), F32)],
         flops=1_100_000_000,
     )
-    moved, w1 = call(
+    moved, w1, vol = call(
         arrange_kernel,
-        [shape((depth, 3 * out, cells), BF), shape((3 * mid, 9 * inner), BF)],
-        [cot_rows, k1],
+        [
+            shape((depth, 3 * out, cells), BF),
+            shape((3 * mid, 9 * inner), BF),
+            shape((depth, inner, cells), BF),
+        ],
+        [cot_rows, k1, volume[0]],
+        [pltpu.VMEM((inner * rows, width), F32)],
         flops=500_000_000,
     )
     deep, one, two = call(
         rim_kernel,
         [shape((3 * depth, inner, cells), BF)] + [shape((3 * depth, inner, 2 * width), BF)] * 2,
-        [volume[0], one, two, w1],
+        [vol, one, two],
         [pltpu.VMEM((inner * rows, width), F32)],
     )
     one, two = swapped(one, HGT, 0), swapped(two, HGT, 1)
@@ -500,26 +505,23 @@
         [pltpu.VMEM((3 * mid, (depth + 2) * rows_in * width), BF)],
         flops=1_500_000_000,
     )
-    hidden, slope, wide, *second = call(
+    hidden, *first = call(
         functools.partial(outer_kernel, direct),
+        [shape((depth + 2, mid, cells + 2 * width), BF)]
+        + ([shape((parts, halves, length_first, width), F32)] * 2 if direct else [shape((7, mid, LANES), F32)]),
+        [deep, two, one, w1, back, inner_hidden, inner_first],
         [
-            shape((depth + 2, mid, cells + 2 * width), BF),
-            shape((depth + 2, mid, rows_out * width), F32),
-            shape((3 * depth, inner, cells + 4 * width), BF),
-        ]
-        + (
-            [shape((parts, halves, length_second, width), F32)] * 2
-            if direct
-            else [shape((14, out, LANES), F32)]
-        ),
-        [deep, two, one, w1, moved, inner_hidden, inner_second],
+            pltpu.VMEM((3 * depth, inner, cells + 4 * width), BF),
+            pltpu.VMEM((3 * mid, (depth + 2) * rows_out * width), BF),
+        ],
         flops=1_000_000_000,
     )
-    first = call(
-        functools.partial(delta_kernel, direct),
-        [shape((parts, halves, length_first, width), F32)] * 2 if direct else [shape((7, mid, LANES), F32)],
-        [wide, back, slope, inner_first],
-        [pltpu.VMEM((3 * mid, (depth + 2) * rows_out * width), BF)],
+    second = call(
+        functools.partial(second_kernel, direct),
+        [shape((parts, halves, length_second, width), kind) for kind in (F32, BF)]
+        if direct
+        else [shape((14, out, LANES), F32)],
+        [hidden, moved, inner_second],
         flops=4_000_000_000,
     )
     if direct:
@@ -537,7 +539,7 @@
     kept, *sends = call(
         functools.partial(plane_kernel, moves),
         [shape(block, F32)] + [shape(block, BF)] * len(moves),
-        [x for keep, send in (second, first) for x in (keep, across(send, ("core", 1)))],
+        [x for keep, send in (first, second) for x in (keep, across(send, ("core", 1)))],
     )
     gots = [across(send, ("dp", x), ("y", y)) for send, (x, y) in zip(sends, moves, strict=True)]
     (share,) = call(total_kernel, [shape(block, BF)], [kept, *gots])

time: 40.8 us -> 40.8 us (level)
  transfers between devices with their start and end apart: 14 -> 14, of which waited for: 9 -> 9; matrix products, arithmetic and copies ran while one was open for 0% -> 0% of each run, Pallas kernels for 22% -> 20%
where the time goes in v13:
time: 40.8 us; the launch traced here: 40.6 us
  starting transfers between devices  16.2 us (40%)
  waiting for transfers between devices  11.9 us (29%)
  Pallas kernels  11.8 us (29%)
  between operations  0.79 us (2%)
    pallas_call x14, Pallas kernels, call(): pl.pallas_call(body, out_shape=outs, in_specs=[pl.BlockSpec(memory_space=...  11.8 us
    ppermute x10, waiting for transfers between devices, across(): lax.ppermute(x, axes, [(i, i ^ flip) for i in range(lax.axis_size(axes))])  10.3 us
    ppermute x10, starting transfers between devices, across(): lax.ppermute(x, axes, [(i, i ^ flip) for i in range(lax.axis_size(axes))])  9.79 us
    ppermute x4, starting transfers between devices, swapped(): return lax.ppermute(x, ('dp', *axes), list(enumerate(partner)))  6.36 us
    ppermute x4, waiting for transfers between devices, swapped(): return lax.ppermute(x, ('dp', *axes), list(enumerate(partner)))  1.58 us
  transfers between devices with their start and end apart: 14, of which 9 were waited for; matrix products, arithmetic and copies ran while one was open for 0% of the time, Pallas kernels for 20%

profile of v13, /device:TPU:0, one launch (start us, length us, event | category | flops | bytes accessed | tf_op | source)
XLA Modules:
  0.0 40.6 jit_solution(3551179592852401537)
XLA Ops:
  0.7 3.0 %collective-permute-start.1 = (bf16[32,2,8,128]{3,2,1,0:T(8,128)(2,1)}, bf16[32,2,8,128]{3,2,1,0:T(8,128)(2,1)S(1)}, u32[]{:S(2)}, u32[]{:S(2)}) collective-permute-start(bf16[32,2,8,128]{3,2,1,0:T(8,128)(2,1)} %bitcast.9), channel_id=1, source_target_pairs={{0,16},{4,8},{8,4},{12,28},{16,0},{20,24},{24,20},{28,12},{1,17},{... | collective-permute-start | bytes 393224 | tf_op jit(solution)/shard_map/ppermute | solution.py:412
  3.7 1.7 %collective-permute-start = (bf16[32,2,8,128]{3,2,1,0:T(8,128)(2,1)}, bf16[32,2,8,128]{3,2,1,0:T(8,128)(2,1)S(1)}, u32[]{:S(2)}, u32[]{:S(2)}) collective-permute-start(bf16[32,2,8,128]{3,2,1,0:T(8,128)(2,1)} %bitcast.10), channel_id=1, source_target_pairs={{0,4},{4,0},{8,12},{12,8},{16,20},{20,16},{24,28},{28,24},{1,5},{5... | collective-permute-start | bytes 393224 | tf_op jit(solution)/shard_map/ppermute | solution.py:412
  5.4 1.7 %shard_map.68 = (bf16[2,128,1024]{2,1,0:T(8,128)(2,1)S(1)}, f32[4,64,1280]{2,1,0:T(8,128)S(1)}) custom-call(bf16[128,2,8,128]{3,2,1,0:T(8,128)(2,1)S(1)} %bitcast.5, bf16[27,64,128]{2,1,0:T(8,128)(2,1)S(1)} %bitcast.6, bf16[128,256]{1,0:T(8,128)(2,1)S(1)} %shard_map.67.blank_ref), custom_call_target="tpu_custom_call" | custom-call | flops 1100000000 | bytes 2867200 | tf_op jit(solution)/shard_map/pallas_call | solution.py:18
  7.1 0.5 %shard_map.69 = (bf16[2,384,1024]{2,1,0:T(8,128)(2,1)S(1)}, bf16[192,288]{1,0:T(8,128)(2,1)S(1)}, bf16[2,32,1024]{2,1,0:T(8,128)(2,1)S(1)}) custom-call(bf16[2,128,1024]{2,1,0:T(8,128)(2,1)S(1)} %get-tuple-element.29.cot_rows_ref, bf16[27,32,64]{2,1,0:T(8,128)(2,1)S(1)} %bitcast.8, bf16[32,2,8,128]{3,2,1,0:T(8,128)(2,1)S(1)} %bitcast.11), custom_call_target="tpu_custom_call" | custom-call | flops 500000000 | bytes 2580480 | tf_op jit(solution)/shard_map/pallas_call | solution.py:18
  7.6 1.2 %collective-permute-done.one_ref = bf16[32,2,8,128]{3,2,1,0:T(8,128)(2,1)S(1)} collective-permute-done((bf16[32,2,8,128]{3,2,1,0:T(8,128)(2,1)}, bf16[32,2,8,128]{3,2,1,0:T(8,128)(2,1)S(1)}, u32[]{:S(2)}, u32[]{:S(2)}) %collective-permute-start) | collective-permute-done | bytes 131104 | tf_op jit(solution)/shard_map/ppermute | solution.py:412
  9.1 1.5 %collective-permute-start.2 = (bf16[6,32,256]{2,1,0:T(8,128)(2,1)S(1)}, bf16[6,32,256]{2,1,0:T(8,128)(2,1)S(1)}, u32[]{:S(2)}, u32[]{:S(2)}) collective-permute-start(bf16[6,32,256]{2,1,0:T(8,128)(2,1)S(1)} %get-tuple-element.32), channel_id=1, source_target_pairs={{0,16},{1,2},{2,1},{3,19},{16,0},{17,18},{18,17},{19,3},{4,20},{5,... | collective-permute-start | bytes 294920 | tf_op jit(solution)/shard_map/ppermute | solution.py:412
  10.8 2.6 %shard_map.71 = (bf16[4,64,768]{2,1,0:T(8,128)(2,1)S(1)}, f32[1152,192]{1,0:T(8,128)S(1)}, f32[192,288]{1,0:T(8,128)S(1)}) custom-call(bf16[6,32,1024]{2,1,0:T(8,128)(2,1)S(1)} %get-tuple-element.31.deep_ref, bf16[192,288]{1,0:T(8,128)(2,1)S(1)} %get-tuple-element.34.w1_ref, bf16[2,384,1024]{2,1,0:T(8,128)(2,1)S(1)} %get-tuple-element.36.moved_ref, ...), custom_call_target="tpu_custom_call" | custom-call | flops 1500000000 | bytes 4886528 | tf_op jit(solution)/shard_map/pallas_call | solution.py:18
  13.8 1.5 %shard_map.72 = (bf16[4,64,1280]{2,1,0:T(8,128)(2,1)S(1)}, f32[2,2,56,128]{3,2,1,0:T(8,128)S(1)}, f32[2,2,56,128]{3,2,1,0:T(8,128)S(1)}) custom-call(bf16[6,32,1024]{2,1,0:T(8,128)(2,1)S(1)} %get-tuple-element.31.deep_ref, bf16[6,32,256]{2,1,0:T(8,128)(2,1)S(1)} %collective-permute-done.2.two_ref, bf16[6,32,256]{2,1,0:T(8,128)(2,1)S(1)} %collective-permute-done.3.one_ref, ...), custom_call_target="tpu_custom_call" | custom-call | flops 1000000000 | bytes 3510272 | tf_op jit(solution)/shard_map/pallas_call | solution.py:18
  15.4 0.6 %shard_map.74 = (f32[2,2,216,128]{3,2,1,0:T(8,128)S(1)}, bf16[2,2,216,128]{3,2,1,0:T(8,128)(2,1)S(1)}) custom-call(bf16[4,64,1280]{2,1,0:T(8,128)(2,1)S(1)} %get-tuple-element.39.hidden_ref, bf16[2,384,1024]{2,1,0:T(8,128)(2,1)S(1)} %get-tuple-element.36.moved_ref, f32[1152,192]{1,0:T(8,128)S(1)} %get-tuple-element.43.second_ref), custom_call_target="tpu_custom_call" | custom-call | flops 4000000000 | bytes 3776512 | tf_op jit(solution)/shard_map/pallas_call | solution.py:18
  16.5 1.1 %collective-permute-done.4.refs_1_ = f32[2,2,56,128]{3,2,1,0:T(8,128)S(1)} collective-permute-done((f32[2,2,56,128]{3,2,1,0:T(8,128)S(1)}, f32[2,2,56,128]{3,2,1,0:T(8,128)S(1)}, u32[]{:S(2)}, u32[]{:S(2)}) %collective-permute-start.4) | collective-permute-done | bytes 114720 | tf_op jit(solution)/shard_map/ppermute | solution.py:420
  17.7 1.5 %collective-permute-start.6 = (bf16[272,128]{1,0:T(8,128)(2,1)S(1)}, bf16[272,128]{1,0:T(8,128)(2,1)S(1)}, u32[]{:S(2)}, u32[]{:S(2)}) collective-permute-start(bf16[272,128]{1,0:T(8,128)(2,1)S(1)} %get-tuple-element.47), channel_id=1, source_target_pairs={{0,16},{2,18},{16,0},{18,2},{1,17},{3,19},{17,1},{19,3},{4,20},{6,... | collective-permute-start | bytes 208904 | tf_op jit(solution)/shard_map/ppermute | solution.py:420
  19.2 0.9 %collective-permute-start.7 = (bf16[272,128]{1,0:T(8,128)(2,1)S(1)}, bf16[272,128]{1,0:T(8,128)(2,1)S(1)}, u32[]{:S(2)}, u32[]{:S(2)}) collective-permute-start(bf16[272,128]{1,0:T(8,128)(2,1)S(1)} %get-tuple-element.48), channel_id=1, source_target_pairs={{0,2},{2,0},{16,18},{18,16},{1,3},{3,1},{17,19},{19,17},{4,6},{6,4... | collective-permute-start | bytes 208904 | tf_op jit(solution)/shard_map/ppermute | solution.py:420
  20.1 1.1 %collective-permute-start.8 = (bf16[272,128]{1,0:T(8,128)(2,1)S(1)}, bf16[272,128]{1,0:T(8,128)(2,1)S(1)}, u32[]{:S(2)}, u32[]{:S(2)}) collective-permute-start(bf16[272,128]{1,0:T(8,128)(2,1)S(1)} %get-tuple-element.49), channel_id=1, source_target_pairs={{0,18},{2,16},{16,2},{18,0},{1,19},{3,17},{17,3},{19,1},{4,22},{6,... | collective-permute-start | bytes 208904 | tf_op jit(solution)/shard_map/ppermute | solution.py:420
  21.3 0.8 %collective-permute-done.6.refs_0_ = bf16[272,128]{1,0:T(8,128)(2,1)S(1)} collective-permute-done((bf16[272,128]{1,0:T(8,128)(2,1)S(1)}, bf16[272,128]{1,0:T(8,128)(2,1)S(1)}, u32[]{:S(2)}, u32[]{:S(2)}) %collective-permute-start.6) | collective-permute-done | bytes 69664 | tf_op jit(solution)/shard_map/ppermute | solution.py:420
  22.1 2.2 %collective-permute-done.7.refs_1_ = bf16[272,128]{1,0:T(8,128)(2,1)S(1)} collective-permute-done((bf16[272,128]{1,0:T(8,128)(2,1)S(1)}, bf16[272,128]{1,0:T(8,128)(2,1)S(1)}, u32[]{:S(2)}, u32[]{:S(2)}) %collective-permute-start.7) | collective-permute-done | bytes 69664 | tf_op jit(solution)/shard_map/ppermute | solution.py:420
  24.3 1.1 %collective-permute-done.8.refs_2_ = bf16[272,128]{1,0:T(8,128)(2,1)S(1)} collective-permute-done((bf16[272,128]{1,0:T(8,128)(2,1)S(1)}, bf16[272,128]{1,0:T(8,128)(2,1)S(1)}, u32[]{:S(2)}, u32[]{:S(2)}) %collective-permute-start.8) | collective-permute-done | bytes 69664 | tf_op jit(solution)/shard_map/ppermute | solution.py:420
  25.4 2.8 %collective-permute-start.11 = (bf16[272,128]{1,0:T(8,128)(2,1)S(1)}, bf16[272,128]{1,0:T(8,128)(2,1)S(1)}, u32[]{:S(2)}, u32[]{:S(2)}) collective-permute-start(bf16[272,128]{1,0:T(8,128)(2,1)S(1)} %shard_map.76.a_ref), channel_id=1, source_target_pairs={{0,12},{4,8},{8,4},{12,0},{1,13},{5,9},{9,5},{13,1},{2,14},{6,10},... | collective-permute-start | bytes 208904 | tf_op jit(solution)/shard_map/ppermute | solution.py:420
  28.7 1.2 %collective-permute-start.9 = (bf16[272,128]{1,0:T(8,128)(2,1)S(1)}, bf16[272,128]{1,0:T(8,128)(2,1)S(1)}, u32[]{:S(2)}, u32[]{:S(2)}) collective-permute-start(bf16[272,128]{1,0:T(8,128)(2,1)S(1)} %shard_map.76.a_ref), channel_id=1, source_target_pairs={{0,4},{4,0},{8,12},{12,8},{1,5},{5,1},{9,13},{13,9},{2,6},{6,2},{1... | collective-permute-start | bytes 208904 | tf_op jit(solution)/shard_map/ppermute | solution.py:420
  29.9 2.5 %shard_map.73 = (bf16[128,2,8,128]{3,2,1,0:T(8,128)(2,1)}, f32[8,128]{1,0:T(8,128)S(1)}) custom-call(bf16[4,64,1280]{2,1,0:T(8,128)(2,1)S(1)} %get-tuple-element.39.hidden_ref, bf16[27,64,128]{2,1,0:T(8,128)(2,1)S(1)} %bitcast.7), custom_call_target="tpu_custom_call" | custom-call | flops 900000000 | bytes 1626112 | tf_op jit(solution)/shard_map/pallas_call | solution.py:18
  32.4 1.4 %collective-permute-done.10.c_ref = bf16[272,128]{1,0:T(8,128)(2,1)S(1)} collective-permute-done((bf16[272,128]{1,0:T(8,128)(2,1)S(1)}, bf16[272,128]{1,0:T(8,128)(2,1)S(1)}, u32[]{:S(2)}, u32[]{:S(2)}) %collective-permute-start.10) | collective-permute-done | bytes 69664 | tf_op jit(solution)/shard_map/ppermute | solution.py:420
  33.9 1.1 %collective-permute-start.12 = (bf16[272,128]{1,0:T(8,128)(2,1)S(1)}, bf16[272,128]{1,0:T(8,128)(2,1)S(1)}, u32[]{:S(2)}, u32[]{:S(2)}) collective-permute-start(bf16[272,128]{1,0:T(8,128)(2,1)S(1)} %shard_map.77.own_ref), channel_id=1, source_target_pairs={{0,2},{2,0},{1,3},{3,1},{4,6},{6,4},{5,7},{7,5},{8,10},{10,8},{9,1... | collective-permute-start | bytes 208904 | tf_op jit(solution)/shard_map/ppermute | solution.py:420
  35.0 3.2 %collective-permute-done.12.got_ref = bf16[272,128]{1,0:T(8,128)(2,1)S(1)} collective-permute-done((bf16[272,128]{1,0:T(8,128)(2,1)S(1)}, bf16[272,128]{1,0:T(8,128)(2,1)S(1)}, u32[]{:S(2)}, u32[]{:S(2)}) %collective-permute-start.12) | collective-permute-done | bytes 69664 | tf_op jit(solution)/shard_map/ppermute | solution.py:420
  38.3 0.9 %shard_map.79 = (f32[27,32,32]{2,1,0:T(8,128)}, f32[27,64,64]{2,1,0:T(8,128)}) custom-call(bf16[2,272,128]{2,1,0:T(8,128)(2,1)S(1)} %shard_map.78.in_ref), custom_call_target="tpu_custom_call" | custom-call | bytes 692224 | tf_op jit(solution)/shard_map/pallas_call | solution.py:18
  39.7 0.9 %shard_map.80 = (f32[27,32,32]{2,1,0:T(8,128)}, f32[27,64,64]{2,1,0:T(8,128)}) custom-call(bf16[2,272,128]{2,1,0:T(8,128)(2,1)S(1)} %collective-permute-done.13.in_ref, f32[27,32,32]{2,1,0:T(8,128)} %get-tuple-element.51.refs_0_, f32[27,64,64]{2,1,0:T(8,128)} %get-tuple-element.52.refs_1_), custom_call_target="tpu_custom_call", output_to_operand_aliasing={{0}: (1, {}), {1}: (2, {})} | custom-call | bytes 1245184 | tf_op jit(solution)/shard_map/pallas_call | solution.py:18
  (26 shorter events, 2.6 us)
Async XLA Ops:
  0.6 4.7 %copy-start = (bf16[1,128,2,8,128]{4,3,2,1,0:T(8,128)(2,1)S(1)}, bf16[1,128,2,8,128]{4,3,2,1,0:T(8,128)(2,1)}, u32[]{:S(2)}) copy-start(bf16[1,128,2,8,128]{4,3,2,1,0:T(8,128)(2,1)} %param.7) | copy-start | bytes 1572868
  0.6 4.7 %copy-start.1 = (bf16[27,128,64]{1,2,0:T(8,128)(2,1)S(1)}, bf16[27,128,64]{1,2,0:T(8,128)(2,1)}, u32[]{:S(2)}) copy-start(bf16[27,128,64]{1,2,0:T(8,128)(2,1)} %param.6) | copy-start | bytes 1327108
  0.7 7.0 %collective-permute-start.1 = (bf16[32,2,8,128]{3,2,1,0:T(8,128)(2,1)}, bf16[32,2,8,128]{3,2,1,0:T(8,128)(2,1)S(1)}, u32[]{:S(2)}, u32[]{:S(2)}) collective-permute-start(bf16[32,2,8,128]{3,2,1,0:T(8,128)(2,1)} %bitcast.9), channel_id=1, source_target_pairs={{0,16},{4,8},{8,4},{12,28},{16,0},{20,24},{24,20},{28,12},{1,17},{... | collective-permute-start | bytes 393224 | tf_op jit(solution)/shard_map/ppermute | solution.py:412
  3.7 5.2 %collective-permute-start = (bf16[32,2,8,128]{3,2,1,0:T(8,128)(2,1)}, bf16[32,2,8,128]{3,2,1,0:T(8,128)(2,1)S(1)}, u32[]{:S(2)}, u32[]{:S(2)}) collective-permute-start(bf16[32,2,8,128]{3,2,1,0:T(8,128)(2,1)} %bitcast.10), channel_id=1, source_target_pairs={{0,4},{4,0},{8,12},{12,8},{16,20},{20,16},{24,28},{28,24},{1,5},{5... | collective-permute-start | bytes 393224 | tf_op jit(solution)/shard_map/ppermute | solution.py:412
  5.3 1.8 %copy-start.2 = (bf16[27,64,32]{1,2,0:T(8,128)(2,1)S(1)}, bf16[27,64,32]{1,2,0:T(8,128)(2,1)}, u32[]{:S(2)}) copy-start(bf16[27,64,32]{1,2,0:T(8,128)(2,1)} %param.5) | copy-start | bytes 331780
  5.3 1.8 %copy-start.3 = (bf16[1,32,2,8,128]{4,3,2,1,0:T(8,128)(2,1)S(1)}, bf16[1,32,2,8,128]{4,3,2,1,0:T(8,128)(2,1)}, u32[]{:S(2)}) copy-start(bf16[1,32,2,8,128]{4,3,2,1,0:T(8,128)(2,1)} %param.4) | copy-start | bytes 393220
  9.1 4.7 %collective-permute-start.2 = (bf16[6,32,256]{2,1,0:T(8,128)(2,1)S(1)}, bf16[6,32,256]{2,1,0:T(8,128)(2,1)S(1)}, u32[]{:S(2)}, u32[]{:S(2)}) collective-permute-start(bf16[6,32,256]{2,1,0:T(8,128)(2,1)S(1)} %get-tuple-element.32), channel_id=1, source_target_pairs={{0,16},{1,2},{2,1},{3,19},{16,0},{17,18},{18,17},{19,3},{4,20},{5,... | collective-permute-start | bytes 294920 | tf_op jit(solution)/shard_map/ppermute | solution.py:412
  10.6 3.2 %collective-permute-start.3 = (bf16[6,32,256]{2,1,0:T(8,128)(2,1)S(1)}, bf16[6,32,256]{2,1,0:T(8,128)(2,1)S(1)}, u32[]{:S(2)}, u32[]{:S(2)}) collective-permute-start(bf16[6,32,256]{2,1,0:T(8,128)(2,1)S(1)} %get-tuple-element.33), channel_id=1, source_target_pairs={{0,1},{1,0},{2,3},{3,2},{16,17},{17,16},{18,19},{19,18},{4,5},{5,4... | collective-permute-start | bytes 294920 | tf_op jit(solution)/shard_map/ppermute | solution.py:412
  15.9 1.7 %collective-permute-start.5 = (bf16[2,2,216,128]{3,2,1,0:T(8,128)(2,1)S(1)}, bf16[2,2,216,128]{3,2,1,0:T(8,128)(2,1)S(1)}, u32[]{:S(2)}, u32[]{:S(2)}) collective-permute-start(bf16[2,2,216,128]{3,2,1,0:T(8,128)(2,1)S(1)} %get-tuple-element.45), channel_id=1, source_target_pairs={{0,1},{1,0},{2,3},{3,2},{4,5},{5,4},{6,7},{7,6},{8,9},{9,8},{10,11... | collective-permute-start | bytes 663560 | tf_op jit(solution)/shard_map/ppermute | solution.py:420
  16.0 1.6 %collective-permute-start.4 = (f32[2,2,56,128]{3,2,1,0:T(8,128)S(1)}, f32[2,2,56,128]{3,2,1,0:T(8,128)S(1)}, u32[]{:S(2)}, u32[]{:S(2)}) collective-permute-start(f32[2,2,56,128]{3,2,1,0:T(8,128)S(1)} %get-tuple-element.42), channel_id=1, source_target_pairs={{0,1},{1,0},{2,3},{3,2},{4,5},{5,4},{6,7},{7,6},{8,9},{9,8},{10,11... | collective-permute-start | bytes 344072 | tf_op jit(solution)/shard_map/ppermute | solution.py:420
  17.7 4.4 %collective-permute-start.6 = (bf16[272,128]{1,0:T(8,128)(2,1)S(1)}, bf16[272,128]{1,0:T(8,128)(2,1)S(1)}, u32[]{:S(2)}, u32[]{:S(2)}) collective-permute-start(bf16[272,128]{1,0:T(8,128)(2,1)S(1)} %get-tuple-element.47), channel_id=1, source_target_pairs={{0,16},{2,18},{16,0},{18,2},{1,17},{3,19},{17,1},{19,3},{4,20},{6,... | collective-permute-start | bytes 208904 | tf_op jit(solution)/shard_map/ppermute | solution.py:420
  19.2 5.1 %collective-permute-start.7 = (bf16[272,128]{1,0:T(8,128)(2,1)S(1)}, bf16[272,128]{1,0:T(8,128)(2,1)S(1)}, u32[]{:S(2)}, u32[]{:S(2)}) collective-permute-start(bf16[272,128]{1,0:T(8,128)(2,1)S(1)} %get-tuple-element.48), channel_id=1, source_target_pairs={{0,2},{2,0},{16,18},{18,16},{1,3},{3,1},{17,19},{19,17},{4,6},{6,4... | collective-permute-start | bytes 208904 | tf_op jit(solution)/shard_map/ppermute | solution.py:420
  20.1 5.2 %collective-permute-start.8 = (bf16[272,128]{1,0:T(8,128)(2,1)S(1)}, bf16[272,128]{1,0:T(8,128)(2,1)S(1)}, u32[]{:S(2)}, u32[]{:S(2)}) collective-permute-start(bf16[272,128]{1,0:T(8,128)(2,1)S(1)} %get-tuple-element.49), channel_id=1, source_target_pairs={{0,18},{2,16},{16,2},{18,0},{1,19},{3,17},{17,3},{19,1},{4,22},{6,... | collective-permute-start | bytes 208904 | tf_op jit(solution)/shard_map/ppermute | solution.py:420
  25.4 7.0 %collective-permute-start.11 = (bf16[272,128]{1,0:T(8,128)(2,1)S(1)}, bf16[272,128]{1,0:T(8,128)(2,1)S(1)}, u32[]{:S(2)}, u32[]{:S(2)}) collective-permute-start(bf16[272,128]{1,0:T(8,128)(2,1)S(1)} %shard_map.76.a_ref), channel_id=1, source_target_pairs={{0,12},{4,8},{8,4},{12,0},{1,13},{5,9},{9,5},{13,1},{2,14},{6,10},... | collective-permute-start | bytes 208904 | tf_op jit(solution)/shard_map/ppermute | solution.py:420
  28.2 5.6 %collective-permute-start.10 = (bf16[272,128]{1,0:T(8,128)(2,1)S(1)}, bf16[272,128]{1,0:T(8,128)(2,1)S(1)}, u32[]{:S(2)}, u32[]{:S(2)}) collective-permute-start(bf16[272,128]{1,0:T(8,128)(2,1)S(1)} %shard_map.76.a_ref), channel_id=1, source_target_pairs={{0,8},{4,12},{8,0},{12,4},{1,9},{5,13},{9,1},{13,5},{2,10},{6,14},... | collective-permute-start | bytes 208904 | tf_op jit(solution)/shard_map/ppermute | solution.py:420
  28.7 5.2 %collective-permute-start.9 = (bf16[272,128]{1,0:T(8,128)(2,1)S(1)}, bf16[272,128]{1,0:T(8,128)(2,1)S(1)}, u32[]{:S(2)}, u32[]{:S(2)}) collective-permute-start(bf16[272,128]{1,0:T(8,128)(2,1)S(1)} %shard_map.76.a_ref), channel_id=1, source_target_pairs={{0,4},{4,0},{8,12},{12,8},{1,5},{5,1},{9,13},{13,9},{2,6},{6,2},{1... | collective-permute-start | bytes 208904 | tf_op jit(solution)/shard_map/ppermute | solution.py:420
  33.9 4.4 %collective-permute-start.12 = (bf16[272,128]{1,0:T(8,128)(2,1)S(1)}, bf16[272,128]{1,0:T(8,128)(2,1)S(1)}, u32[]{:S(2)}, u32[]{:S(2)}) collective-permute-start(bf16[272,128]{1,0:T(8,128)(2,1)S(1)} %shard_map.77.own_ref), channel_id=1, source_target_pairs={{0,2},{2,0},{1,3},{3,1},{4,6},{6,4},{5,7},{7,5},{8,10},{10,8},{9,1... | collective-permute-start | bytes 208904 | tf_op jit(solution)/shard_map/ppermute | solution.py:420
  38.3 1.4 %collective-permute-start.13 = (bf16[2,272,128]{2,1,0:T(8,128)(2,1)S(1)}, bf16[2,272,128]{2,1,0:T(8,128)(2,1)S(1)}, u32[]{:S(2)}, u32[]{:S(2)}) collective-permute-start(bf16[2,272,128]{2,1,0:T(8,128)(2,1)S(1)} %shard_map.78.in_ref), channel_id=1, source_target_pairs={{0,1},{1,0},{2,3},{3,2},{4,5},{5,4},{6,7},{7,6},{8,9},{9,8},{10,11... | collective-permute-start | bytes 417800 | tf_op jit(solution)/shard_map/ppermute | solution.py:420

commit v14 on v13

--- a/solution.py
+++ b/solution.py
@@ -13,13 +13,13 @@
 VMEM_BYTES = 28 * 2**20
 
 
-def call(body, outs, args, scratch=(), flops=0, far=(), far_outs=False, aliases=None):
+def call(body, outs, args, scratch=(), flops=0, far=(), far_outs=(), aliases=None):
     moved = sum(x.size * x.dtype.itemsize for x in (*outs, *args))
     return pl.pallas_call(
         body,
         out_shape=outs,
         in_specs=[pl.BlockSpec(memory_space=pl.ANY if n in far else pltpu.VMEM) for n in range(len(args))],
-        out_specs=[pl.BlockSpec(memory_space=pl.ANY if far_outs else pltpu.VMEM)] * len(outs),
+        out_specs=[pl.BlockSpec(memory_space=pl.ANY if n in far_outs else pltpu.VMEM) for n in range(len(outs))],
         scratch_shapes=list(scratch),
         input_output_aliases=aliases or {},
         compiler_params=pltpu.CompilerParams(vmem_limit_bytes=VMEM_BYTES),
@@ -151,12 +151,16 @@
     keep_ref, send_ref = refs
     parts, halves, length, _ = keep_ref.shape
     core = lax.axis_index("core") == 1
+
+    def filled(rows):
+        rest = length - sum(x.shape[0] for x in rows)
+        return jnp.concatenate([*rows, jnp.zeros((rest, LANES), F32)] if rest else rows, axis=0)
+
     for part in range(parts):
-        one, two = (jnp.concatenate(rows_of(part, c), axis=0) for c in range(2))
         for half in range(halves):
-            at = slice(half * length, (half + 1) * length)
-            keep_ref[part, half] = jnp.where(core, two[at], one[at])
-            send_ref[part, half] = jnp.where(core, one[at], two[at]).astype(send_ref.dtype)
+            one, two = (filled(rows_of(part, c)[half]) for c in range(2))
+            keep_ref[part, half] = jnp.where(core, two, one)
+            send_ref[part, half] = jnp.where(core, one, two).astype(send_ref.dtype)
 
 
 def folded(tail):
@@ -273,7 +277,8 @@
     half = size // 2
 
     def rows_of(part, core):
-        return [block[part * size + core * half : part * size + (core + 1) * half] for block in blocks]
+        rows = [block[part * size + core * half : part * size + (core + 1) * half] for block in blocks]
+        return rows[:3], rows[3:]
 
     pack(direct, grad_refs, rows_of, blocks)
 
@@ -307,7 +312,8 @@
 
     def rows_of(part, core):
         at = slice((2 * part + core) * size, (2 * part + core + 1) * size)
-        return [block[at] for block in blocks] + [folded(tails[8][at])]
+        rows = [block[at] for block in blocks] + [folded(tails[8][at])]
+        return rows[:7], rows[7:]
 
     pack(direct, grad_refs, rows_of, [*blocks, jnp.concatenate([tails[8], jnp.zeros_like(tails[8])], axis=1)])
 
@@ -334,14 +340,18 @@
     token_ref[...] = scratch[:8]
 
 
-def plane_kernel(moves, *refs):
-    keep_first, got_first, keep_second, got_second, kept_ref, *send_refs = refs
-    part = lax.rem(lax.axis_index("dp"), keep_first.shape[0])
+def plane_kernel(moves, cuts, *refs):
+    sums, (kept_ref, *send_refs) = refs[: -1 - len(moves)], refs[-1 - len(moves) :]
+    part = lax.rem(lax.axis_index("dp"), sums[0].shape[0])
     half = lax.axis_index("y")
 
     def total(x, y):
         at = 1 - part if x else part, 1 - half if y else half
-        return jnp.concatenate([keep_second[at] + got_second[at].astype(F32), keep_first[at] + got_first[at]], axis=0)
+        values = [keep[at] + got[at].astype(F32) for keep, got in zip(sums[::2], sums[1::2], strict=True)]
+        if len(values) == 1:
+            return values[0]
+        one, two = (jnp.concatenate([v[:n] for v, n in zip(values, cut, strict=True)], axis=0) for cut in cuts)
+        return jnp.where(at[1] == 0, one, two)
 
     kept_ref[...] = total(0, 0)
     for (x, y), send_ref in zip(moves, send_refs, strict=True):
@@ -356,47 +366,83 @@
     out_ref[...] = value.astype(BF)
 
 
-def depth_kernel(a_ref, b_ref, c_ref, d_ref, _, out_ref):
+def depth_kernel(a_ref, b_ref, c_ref, d_ref, _, out_ref, padded_ref):
     one = a_ref[...].astype(F32) + b_ref[...].astype(F32)
     two = c_ref[...].astype(F32) + d_ref[...].astype(F32)
     out_ref[...] = (one + two).astype(BF)
-
-
-def order_kernel(own_ref, got_ref, out_ref):
-    mine = lax.axis_index("y")
-    out_ref[mine] = own_ref[...]
-    out_ref[1 - mine] = got_ref[...]
-
-
-def unpack_kernel(length, theirs, in_ref, *refs):
-    first_ref, second_ref, first, second, sems = refs[-5:]
-    core = lax.axis_index("core")
-    at = 1 - core if theirs else core
-    _, size, mid = second.shape
-    whole = [in_ref[n].astype(F32) for n in range(in_ref.shape[0])]
-    rows = jnp.concatenate([x[:length] for x in whole], axis=0)
-    for j in range(13):
-        value = rows[j * size : (j + 1) * size]
-        for m, k in enumerate((j, 9 + j) if j < 9 else (2 * j, 2 * j + 1)):
-            second[k] = value[:, m * mid : (m + 1) * mid]
-    value = rows[13 * size : 13 * size + size // 2]
-    second[26] = jnp.concatenate([value[:, :mid], value[:, mid:]], axis=0)
-    copies = [pltpu.make_async_copy(second, second_ref.at[:, pl.ds(pl.multiple_of(at * size, size), size), :], sems.at[1])]
-    copies[0].start()
-    _, half, inner = first.shape
-    rows = jnp.concatenate([x[length:] for x in whole], axis=0)
-    for j in range(7):
-        value = rows[j * half : (j + 1) * half]
-        for m in range(4):
-            c, ab = (j // 2, 4 * (j % 2) + m) if j < 6 else (m, 8)
-            if c < 3:
-                first[3 * ab + c] = value[:, m * inner : (m + 1) * inner]
-    copies.append(
-        pltpu.make_async_copy(first, first_ref.at[:, pl.ds(pl.multiple_of(at * half, half), half), :], sems.at[0])
-    )
-    copies[1].start()
-    for copy in copies:
-        copy.wait()
+    rest = jnp.zeros((padded_ref.shape[0] - out_ref.shape[0], LANES), F32)
+    padded_ref[...] = jnp.concatenate([one + two, rest], axis=0).astype(BF)
+
+
+def after_kernel(in_ref, _, out_ref):
+    out_ref[...] = in_ref[: out_ref.shape[0]]
+
+
+def write_kernel(count, wheres, *refs):
+    n_scratch = 6
+    in_refs = refs[:count]
+    first_ref, second_ref, token_ref = refs[-3 - n_scratch * count : -n_scratch * count]
+    token_ref[...] = jnp.zeros(token_ref.shape, F32)
+    scratch = refs[-n_scratch * count :]
+    core, y = lax.axis_index("core"), lax.axis_index("y")
+
+    def begun(n, half):
+        wide, last, low, high, tail, sems = scratch[n_scratch * n : n_scratch * (n + 1)]
+        own_core, _ = wheres[n]
+        at = core if own_core else 1 - core
+        rows = in_refs[n][...].astype(F32)
+        _, _, size, mid = wide.shape
+        _, small, inner = low.shape
+        here = pl.ds(pl.multiple_of(at * size, size), size)
+        count = 2 if half else 7
+        for j in range(count):
+            value = rows[j * size : (j + 1) * size]
+            for m in range(2):
+                wide[m, j] = value[:, m * mid : (m + 1) * mid]
+        pairs = [(wide.at[:, :count], second_ref.at[0:2, 7 * half : 7 * half + count, here, :])]
+        row = count * size
+        if half:
+            for j in range(4):
+                value = rows[row : row + size]
+                row += size
+                for m in range(2):
+                    last[2 * j + m] = value[:, m * mid : (m + 1) * mid]
+            value = rows[row : row + size // 2]
+            row += size // 2
+            last[8] = jnp.concatenate([value[:, :mid], value[:, mid:]], axis=0)
+            pairs.append((last, second_ref.at[2, :, here, :]))
+        copies = [pltpu.make_async_copy(src, dst, sems.at[i]) for i, (src, dst) in enumerate(pairs)]
+        for copy in copies:
+            copy.start()
+        here = pl.ds(pl.multiple_of(at * small, small), small)
+        places = [(high, 0, 4), (low, 0, 4), (low, 4, 4), (tail, 0, 3)] if half else [(low, 0, 4), (low, 4, 4), (high, 0, 4)]
+        for ref, start, number in places:
+            value = rows[row : row + small]
+            row += small
+            for m in range(number):
+                ref[start + m] = value[:, m * inner : (m + 1) * inner]
+        if half:
+            pairs = [
+                (high, first_ref.at[4:8, 1, here, :]),
+                (low, first_ref.at[0:8, 2, here, :]),
+                (tail, first_ref.at[8, :, here, :]),
+            ]
+        else:
+            pairs = [(low, first_ref.at[0:8, 0, here, :]), (high, first_ref.at[0:4, 1, here, :])]
+        more = [pltpu.make_async_copy(src, dst, sems.at[2 + i]) for i, (src, dst) in enumerate(pairs)]
+        for copy in more:
+            copy.start()
+        return copies + more
+
+    for half in range(2):
+
+        @pl.when(y == half)
+        def _(half=half):
+            copies = []
+            for n, (_, own_y) in enumerate(wheres):
+                copies += begun(n, half if own_y else 1 - half)
+            for copy in copies:
+                copy.wait()
 
 
 def swapped(x, axis, first):
@@ -420,35 +466,37 @@
     return lax.ppermute(x, axes, [(i, i ^ flip) for i in range(lax.axis_size(axes))])
 
 
-def scattered(rows, length):
-    halves = lax.axis_size("y")
-    grad = jnp.pad(rows, ((0, 0), (0, 0), (0, halves * length - rows.shape[2]), (0, 0)))
-    grad = lax.psum_scatter(grad, "dp", scatter_dimension=0, tiled=True)
-    grad = grad.reshape(1, 2, halves, length, LANES)
+def scattered(rows, cuts):
+    halves = [
+        jnp.concatenate([x[:, :, :n] if at == 0 else x[:, :, x.shape[2] - n :] for x, n in zip(rows, cut)], axis=2)
+        for at, cut in enumerate(cuts)
+    ]
+    grad = lax.psum_scatter(jnp.stack(halves, axis=2), "dp", scatter_dimension=0, tiled=True)
     core = lax.axis_index("core")
     return tuple(lax.dynamic_index_in_dim(grad, at, 1, False) for at in (core, 1 - core))
 
 
-def assembled(own, got, length, size, inner, mid):
-    core = lax.axis_index("core")
-    both = jnp.stack([own, got]).astype(F32)
-    both = jnp.stack([lax.dynamic_index_in_dim(both, at, 0, False) for at in (core, 1 - core)])
-    rows = both[:, :, :length].reshape(2, -1, LANES)
-    second = [None] * 27
-    for j in range(13):
-        for m, k in enumerate((j, 9 + j) if j < 9 else (2 * j, 2 * j + 1)):
-            second[k] = rows[:, j * size : (j + 1) * size, m * mid : (m + 1) * mid].reshape(2 * size, mid)
-    tail = rows[:, 13 * size : 13 * size + size // 2]
-    second[26] = jnp.concatenate([tail[:, :, :mid], tail[:, :, mid:]], axis=1).reshape(2 * size, mid)
-    rows, half = both[:, :, length:].reshape(2, -1, LANES), size // 2
-    first = [None] * 27
-    for j in range(7):
-        for m in range(4):
-            c, ab = (j // 2, 4 * (j % 2) + m) if j < 6 else (m, 8)
-            if c < 3:
-                value = rows[:, j * half : (j + 1) * half, m * inner : (m + 1) * inner]
-                first[3 * ab + c] = value.reshape(size, inner)
-    return jnp.stack(first), jnp.stack(second)
+def assembled(quarters, size, inner, mid):
+    first, second = ([[None, None] for _ in range(27)] for _ in range(2))
+    half = size // 2
+    for core in range(2):
+        for y in range(2):
+            rows, row = quarters[core][y].astype(F32), 0
+            for j in range(7) if y == 0 else range(7, 13):
+                for m, k in enumerate((j, 9 + j) if j < 9 else (2 * j, 2 * j + 1)):
+                    second[k][core] = rows[row : row + size, m * mid : (m + 1) * mid]
+                row += size
+            if y == 1:
+                tail = rows[row : row + half]
+                second[26][core] = jnp.concatenate([tail[:, :mid], tail[:, mid:]], axis=0)
+                row += half
+            for j in range(3) if y == 0 else range(3, 7):
+                for m in range(4):
+                    c, ab = (j // 2, 4 * (j % 2) + m) if j < 6 else (m, 8)
+                    if c < 3:
+                        first[3 * ab + c][core] = rows[row : row + half, m * inner : (m + 1) * inner]
+                row += half
+    return tuple(jnp.stack([jnp.concatenate(both, axis=0) for both in grad]) for grad in (first, second))
 
 
 def per_device(volume, kernel_first, kernel_second, cotangent):
@@ -492,7 +540,8 @@
     size = mid // parts
     direct = parts == 2 and size % 16 == 0
     halves = lax.axis_size("y")
-    length_second, length_first = (-(-units * size // (16 * halves)) * 8 for units in (27, 7))
+    cuts = ((7 * size, 3 * size // 2), (13 * size // 2, 2 * size))
+    length_second, length_first = 7 * size, 2 * size
     rows_in, rows_out = height - 2, 4
     inner_hidden, inner_second, inner_first = call(
         inner_kernel,
@@ -525,21 +574,22 @@
         flops=4_000_000_000,
     )
     if direct:
-        moves = [(1, 0), (0, 1), (1, 1)]
+        moves = [(1, 0), (1, 1), (0, 1)]
+        grads = [second, first]
     else:
         moves = [(0, 1)]
         blocks = second[0].reshape(14, parts, 2, size, LANES).transpose(1, 2, 0, 3, 4)
         tail = blocks[:, :, 13, :, :mid]
         tail = jnp.concatenate([tail[:, :, : size // 2], tail[:, :, size // 2 :]], axis=-1)
         rows_second = jnp.concatenate([blocks[:, :, :13].reshape(parts, 2, 13 * size, LANES), tail], axis=2)
-        second = scattered(rows_second, length_second)
         blocks = first[0].reshape(7, parts, 2, size // 2, LANES).transpose(1, 2, 0, 3, 4)
-        first = scattered(blocks.reshape(parts, 2, 7 * (size // 2), LANES), length_first)
-    block = (length_second + length_first, width)
+        rows_first = blocks.reshape(parts, 2, 7 * (size // 2), LANES)
+        grads = [scattered([rows_second, rows_first], cuts)]
+    block = (sum(cuts[0]), width)
     kept, *sends = call(
-        functools.partial(plane_kernel, moves),
+        functools.partial(plane_kernel, moves, cuts),
         [shape(block, F32)] + [shape(block, BF)] * len(moves),
-        [x for keep, send in (first, second) for x in (keep, across(send, ("core", 1)))],
+        [x for keep, send in grads for x in (keep, across(send, ("core", 1)))],
     )
     gots = [across(send, ("dp", x), ("y", y)) for send, (x, y) in zip(sends, moves, strict=True)]
     (share,) = call(total_kernel, [shape(block, BF)], [kept, *gots])
@@ -551,28 +601,43 @@
         flops=900_000_000,
     )
     gots = [across(share, ("dep", bits)) for bits in (1, 2, 3)]
-    (share,) = call(depth_kernel, [shape(block, BF)], [share, *gots, token])
-    (own,) = call(order_kernel, [shape((halves, *block), BF)], [share, across(share, ("y", 1))])
-    got = across(own, ("core", 1))
+    share, for_y = call(depth_kernel, [shape(block, BF), shape((block[0] + 16, width), BF)], [share, *gots, token])
+    other, far = across(share, ("core", 1)), across(for_y, ("y", 1))
     if size % 16 == 0:
-        grads = [shape((27, size, inner), F32), shape((27, 2 * size, mid), F32)]
-        scratch = [
-            pltpu.VMEM((27, size // 2, inner), F32),
-            pltpu.VMEM((27, size, mid), F32),
-            pltpu.SemaphoreType.DMA((2,)),
+        outs = [shape((9, 3, size, inner), F32), shape((3, 9, 2 * size, mid), F32)]
+
+        def written(quarters, wheres, before=()):
+            scratch = [
+                pltpu.VMEM((2, 7, size, mid), F32),
+                pltpu.VMEM((9, size, mid), F32),
+                pltpu.VMEM((8, size // 2, inner), F32),
+                pltpu.VMEM((4, size // 2, inner), F32),
+                pltpu.VMEM((3, size // 2, inner), F32),
+                pltpu.SemaphoreType.DMA((5,)),
+            ]
+            count = len(quarters)
+            return call(
+                functools.partial(write_kernel, count, wheres),
+                [*outs, shape((8, width), F32)],
+                [*quarters, *before],
+                scratch * count,
+                far=range(count, count + len(before)),
+                far_outs=(0, 1),
+                aliases={count + n: n for n in range(len(before))},
+            )
+
+        *grads, token = written([share, other], [(True, True), (False, True)])
+        (far,) = call(after_kernel, [shape(block, BF)], [far, token])
+        *grads, _ = written([far], [(True, False)], grads)
+        *grads, _ = written([across(far, ("core", 1))], [(False, False)], grads)
+        grad_first, grad_second = (grad.reshape(27, *grad.shape[2:]) for grad in grads)
+    else:
+        core, y = lax.axis_index("core"), lax.axis_index("y")
+        stacked = jnp.stack([jnp.stack([share, far[: block[0]]]), jnp.stack([other, across(far[: block[0]], ("core", 1))])])
+        quarters = [
+            [stacked[lax.bitwise_xor(core, c), lax.bitwise_xor(y, h)] for h in range(2)] for c in range(2)
         ]
-        written = call(functools.partial(unpack_kernel, length_second, False), grads, [own], scratch, far_outs=True)
-        grad_first, grad_second = call(
-            functools.partial(unpack_kernel, length_second, True),
-            grads,
-            [got, *written],
-            scratch,
-            far=(1, 2),
-            far_outs=True,
-            aliases={1: 0, 2: 1},
-        )
-    else:
-        grad_first, grad_second = assembled(own, got, length_second, size, inner, mid)
+        grad_first, grad_second = assembled(quarters, size, inner, mid)
     return features[None], grad_first, grad_second
 
 

time: 40.8 us -> 42.2 us (1.034)
  Pallas kernels: 11.8 us -> 13.8 us
  waiting for transfers between devices: 11.9 us -> 11.3 us
    pallas_call x14 -> x15, Pallas kernels: 11.8 us -> 13.8 us  [call(): pl.pallas_call(body, out_shape=outs, in_specs=[pl.BlockSpec(memory_space=...]
    ppermute x10 -> x11, waiting for transfers between devices: 10.3 us -> 9.69 us  [across(): lax.ppermute(x, axes, [(i, i ^ flip) for i in range(lax.axis_size(axes))])]
    ppermute x10 -> x11, starting transfers between devices: 9.79 us -> 9.85 us  [across(): lax.ppermute(x, axes, [(i, i ^ flip) for i in range(lax.axis_size(axes))])]
  transfers between devices with their start and end apart: 14 -> 15, of which waited for: 9 -> 9; matrix products, arithmetic and copies ran while one was open for 0% -> 0% of each run, Pallas kernels for 20% -> 23%
where the time goes in v14:
time: 42.2 us; the launch traced here: 42.1 us
  starting transfers between devices  16.2 us (38%)
  Pallas kernels  13.8 us (33%)
  waiting for transfers between devices  11.3 us (27%)
  between operations  0.8 us (2%)
    pallas_call x15, Pallas kernels, call(): pl.pallas_call(body, out_shape=outs, in_specs=[pl.BlockSpec(memory_space=...  13.8 us
    ppermute x11, starting transfers between devices, across(): lax.ppermute(x, axes, [(i, i ^ flip) for i in range(lax.axis_size(axes))])  9.85 us
    ppermute x11, waiting for transfers between devices, across(): lax.ppermute(x, axes, [(i, i ^ flip) for i in range(lax.axis_size(axes))])  9.69 us
    ppermute x4, starting transfers between devices, swapped(): return lax.ppermute(x, ('dp', *axes), list(enumerate(partner)))  6.36 us
    ppermute x4, waiting for transfers between devices, swapped(): return lax.ppermute(x, ('dp', *axes), list(enumerate(partner)))  1.58 us
  transfers between devices with their start and end apart: 15, of which 9 were waited for; matrix products, arithmetic and copies ran while one was open for 0% of the time, Pallas kernels for 23%

profile of v14, /device:TPU:0, one launch (start us, length us, event | category | flops | bytes accessed | tf_op | source)
XLA Modules:
  0.0 42.1 jit_solution(16955909009573997695)
XLA Ops:
  0.7 3.0 %collective-permute-start.1 = (bf16[32,2,8,128]{3,2,1,0:T(8,128)(2,1)}, bf16[32,2,8,128]{3,2,1,0:T(8,128)(2,1)S(1)}, u32[]{:S(2)}, u32[]{:S(2)}) collective-permute-start(bf16[32,2,8,128]{3,2,1,0:T(8,128)(2,1)} %bitcast.11), channel_id=1, source_target_pairs={{0,16},{4,8},{8,4},{12,28},{16,0},{20,24},{24,20},{28,12},{1,17},{... | collective-permute-start | bytes 393224 | tf_op jit(solution)/shard_map/ppermute | solution.py:458
  3.7 1.7 %collective-permute-start = (bf16[32,2,8,128]{3,2,1,0:T(8,128)(2,1)}, bf16[32,2,8,128]{3,2,1,0:T(8,128)(2,1)S(1)}, u32[]{:S(2)}, u32[]{:S(2)}) collective-permute-start(bf16[32,2,8,128]{3,2,1,0:T(8,128)(2,1)} %bitcast.12), channel_id=1, source_target_pairs={{0,4},{4,0},{8,12},{12,8},{16,20},{20,16},{24,28},{28,24},{1,5},{5... | collective-permute-start | bytes 393224 | tf_op jit(solution)/shard_map/ppermute | solution.py:458
  5.4 1.7 %shard_map.68 = (bf16[2,128,1024]{2,1,0:T(8,128)(2,1)S(1)}, f32[4,64,1280]{2,1,0:T(8,128)S(1)}) custom-call(bf16[128,2,8,128]{3,2,1,0:T(8,128)(2,1)S(1)} %bitcast.7, bf16[27,64,128]{2,1,0:T(8,128)(2,1)S(1)} %bitcast.8, bf16[128,256]{1,0:T(8,128)(2,1)S(1)} %shard_map.67.blank_ref), custom_call_target="tpu_custom_call" | custom-call | flops 1100000000 | bytes 2867200 | tf_op jit(solution)/shard_map/pallas_call | solution.py:18
  7.6 1.2 %collective-permute-done.one_ref = bf16[32,2,8,128]{3,2,1,0:T(8,128)(2,1)S(1)} collective-permute-done((bf16[32,2,8,128]{3,2,1,0:T(8,128)(2,1)}, bf16[32,2,8,128]{3,2,1,0:T(8,128)(2,1)S(1)}, u32[]{:S(2)}, u32[]{:S(2)}) %collective-permute-start) | collective-permute-done | bytes 131104 | tf_op jit(solution)/shard_map/ppermute | solution.py:458
  9.1 1.5 %collective-permute-start.2 = (bf16[6,32,256]{2,1,0:T(8,128)(2,1)S(1)}, bf16[6,32,256]{2,1,0:T(8,128)(2,1)S(1)}, u32[]{:S(2)}, u32[]{:S(2)}) collective-permute-start(bf16[6,32,256]{2,1,0:T(8,128)(2,1)S(1)} %get-tuple-element.37), channel_id=1, source_target_pairs={{0,16},{1,2},{2,1},{3,19},{16,0},{17,18},{18,17},{19,3},{4,20},{5,... | collective-permute-start | bytes 294920 | tf_op jit(solution)/shard_map/ppermute | solution.py:458
  10.8 2.6 %shard_map.71 = (bf16[4,64,768]{2,1,0:T(8,128)(2,1)S(1)}, f32[1152,192]{1,0:T(8,128)S(1)}, f32[192,288]{1,0:T(8,128)S(1)}) custom-call(bf16[6,32,1024]{2,1,0:T(8,128)(2,1)S(1)} %get-tuple-element.36.deep_ref, bf16[192,288]{1,0:T(8,128)(2,1)S(1)} %get-tuple-element.39.w1_ref, bf16[2,384,1024]{2,1,0:T(8,128)(2,1)S(1)} %get-tuple-element.41.moved_ref, ...), custom_call_target="tpu_custom_call" | custom-call | flops 1500000000 | bytes 4886528 | tf_op jit(solution)/shard_map/pallas_call | solution.py:18
  13.8 1.5 %shard_map.72 = (bf16[4,64,1280]{2,1,0:T(8,128)(2,1)S(1)}, f32[2,2,64,128]{3,2,1,0:T(8,128)S(1)}, f32[2,2,64,128]{3,2,1,0:T(8,128)S(1)}) custom-call(bf16[6,32,1024]{2,1,0:T(8,128)(2,1)S(1)} %get-tuple-element.36.deep_ref, bf16[6,32,256]{2,1,0:T(8,128)(2,1)S(1)} %collective-permute-done.2.two_ref, bf16[6,32,256]{2,1,0:T(8,128)(2,1)S(1)} %collective-permute-done.3.one_ref, ...), custom_call_target="tpu_custom_call" | custom-call | flops 1000000000 | bytes 3543040 | tf_op jit(solution)/shard_map/pallas_call | solution.py:18
  16.5 1.2 %collective-permute-done.5.refs_3_ = f32[2,2,64,128]{3,2,1,0:T(8,128)S(1)} collective-permute-done((f32[2,2,64,128]{3,2,1,0:T(8,128)S(1)}, f32[2,2,64,128]{3,2,1,0:T(8,128)S(1)}, u32[]{:S(2)}, u32[]{:S(2)}) %collective-permute-start.5) | collective-permute-done | bytes 131104 | tf_op jit(solution)/shard_map/ppermute | solution.py:466
  17.7 1.5 %collective-permute-start.6 = (bf16[272,128]{1,0:T(8,128)(2,1)S(1)}, bf16[272,128]{1,0:T(8,128)(2,1)S(1)}, u32[]{:S(2)}, u32[]{:S(2)}) collective-permute-start(bf16[272,128]{1,0:T(8,128)(2,1)S(1)} %get-tuple-element.52), channel_id=1, source_target_pairs={{0,16},{2,18},{16,0},{18,2},{1,17},{3,19},{17,1},{19,3},{4,20},{6,... | collective-permute-start | bytes 208904 | tf_op jit(solution)/shard_map/ppermute | solution.py:466
  19.2 1.0 %collective-permute-start.7 = (bf16[272,128]{1,0:T(8,128)(2,1)S(1)}, bf16[272,128]{1,0:T(8,128)(2,1)S(1)}, u32[]{:S(2)}, u32[]{:S(2)}) collective-permute-start(bf16[272,128]{1,0:T(8,128)(2,1)S(1)} %get-tuple-element.53), channel_id=1, source_target_pairs={{0,18},{2,16},{16,2},{18,0},{1,19},{3,17},{17,3},{19,1},{4,22},{6,... | collective-permute-start | bytes 208904 | tf_op jit(solution)/shard_map/ppermute | solution.py:466
  20.2 1.1 %collective-permute-start.8 = (bf16[272,128]{1,0:T(8,128)(2,1)S(1)}, bf16[272,128]{1,0:T(8,128)(2,1)S(1)}, u32[]{:S(2)}, u32[]{:S(2)}) collective-permute-start(bf16[272,128]{1,0:T(8,128)(2,1)S(1)} %get-tuple-element.54), channel_id=1, source_target_pairs={{0,2},{2,0},{16,18},{18,16},{1,3},{3,1},{17,19},{19,17},{4,6},{6,4... | collective-permute-start | bytes 208904 | tf_op jit(solution)/shard_map/ppermute | solution.py:466
  21.3 0.8 %collective-permute-done.6.refs_0_ = bf16[272,128]{1,0:T(8,128)(2,1)S(1)} collective-permute-done((bf16[272,128]{1,0:T(8,128)(2,1)S(1)}, bf16[272,128]{1,0:T(8,128)(2,1)S(1)}, u32[]{:S(2)}, u32[]{:S(2)}) %collective-permute-start.6) | collective-permute-done | bytes 69664 | tf_op jit(solution)/shard_map/ppermute | solution.py:466
  22.1 2.4 %collective-permute-done.7.refs_1_ = bf16[272,128]{1,0:T(8,128)(2,1)S(1)} collective-permute-done((bf16[272,128]{1,0:T(8,128)(2,1)S(1)}, bf16[272,128]{1,0:T(8,128)(2,1)S(1)}, u32[]{:S(2)}, u32[]{:S(2)}) %collective-permute-start.7) | collective-permute-done | bytes 69664 | tf_op jit(solution)/shard_map/ppermute | solution.py:466
  24.5 0.9 %collective-permute-done.8.refs_2_ = bf16[272,128]{1,0:T(8,128)(2,1)S(1)} collective-permute-done((bf16[272,128]{1,0:T(8,128)(2,1)S(1)}, bf16[272,128]{1,0:T(8,128)(2,1)S(1)}, u32[]{:S(2)}, u32[]{:S(2)}) %collective-permute-start.8) | collective-permute-done | bytes 69664 | tf_op jit(solution)/shard_map/ppermute | solution.py:466
  25.5 3.3 %collective-permute-start.11 = (bf16[272,128]{1,0:T(8,128)(2,1)S(1)}, bf16[272,128]{1,0:T(8,128)(2,1)S(1)}, u32[]{:S(2)}, u32[]{:S(2)}) collective-permute-start(bf16[272,128]{1,0:T(8,128)(2,1)S(1)} %shard_map.76.a_ref), channel_id=1, source_target_pairs={{0,12},{4,8},{8,4},{12,0},{1,13},{5,9},{9,5},{13,1},{2,14},{6,10},... | collective-permute-start | bytes 208904 | tf_op jit(solution)/shard_map/ppermute | solution.py:466
  28.8 1.1 %collective-permute-start.9 = (bf16[272,128]{1,0:T(8,128)(2,1)S(1)}, bf16[272,128]{1,0:T(8,128)(2,1)S(1)}, u32[]{:S(2)}, u32[]{:S(2)}) collective-permute-start(bf16[272,128]{1,0:T(8,128)(2,1)S(1)} %shard_map.76.a_ref), channel_id=1, source_target_pairs={{0,4},{4,0},{8,12},{12,8},{1,5},{5,1},{9,13},{13,9},{2,6},{6,2},{1... | collective-permute-start | bytes 208904 | tf_op jit(solution)/shard_map/ppermute | solution.py:466
  29.9 2.5 %shard_map.73 = (bf16[128,2,8,128]{3,2,1,0:T(8,128)(2,1)}, f32[8,128]{1,0:T(8,128)S(1)}) custom-call(bf16[4,64,1280]{2,1,0:T(8,128)(2,1)S(1)} %get-tuple-element.44.hidden_ref, bf16[27,64,128]{2,1,0:T(8,128)(2,1)S(1)} %bitcast.9), custom_call_target="tpu_custom_call" | custom-call | flops 900000000 | bytes 1626112 | tf_op jit(solution)/shard_map/pallas_call | solution.py:18
  32.4 2.2 %collective-permute-done.10.c_ref = bf16[272,128]{1,0:T(8,128)(2,1)S(1)} collective-permute-done((bf16[272,128]{1,0:T(8,128)(2,1)S(1)}, bf16[272,128]{1,0:T(8,128)(2,1)S(1)}, u32[]{:S(2)}, u32[]{:S(2)}) %collective-permute-start.10) | collective-permute-done | bytes 69664 | tf_op jit(solution)/shard_map/ppermute | solution.py:466
  34.7 1.3 %collective-permute-start.12 = (bf16[288,128]{1,0:T(8,128)(2,1)S(1)}, bf16[288,128]{1,0:T(8,128)(2,1)S(1)}, u32[]{:S(2)}, u32[]{:S(2)}) collective-permute-start(bf16[288,128]{1,0:T(8,128)(2,1)S(1)} %get-tuple-element.56), channel_id=1, source_target_pairs={{0,2},{2,0},{1,3},{3,1},{4,6},{6,4},{5,7},{7,5},{8,10},{10,8},{9,1... | collective-permute-start | bytes 221192 | tf_op jit(solution)/shard_map/ppermute | solution.py:466
  36.0 1.3 %collective-permute-done.13.refs_1_ = bf16[272,128]{1,0:T(8,128)(2,1)S(1)} collective-permute-done((bf16[272,128]{1,0:T(8,128)(2,1)S(1)}, bf16[272,128]{1,0:T(8,128)(2,1)S(1)}, u32[]{:S(2)}, u32[]{:S(2)}) %collective-permute-start.13) | collective-permute-done | bytes 69664 | tf_op jit(solution)/shard_map/ppermute | solution.py:466
  37.3 1.0 %shard_map.78 = (f32[9,3,32,32]{3,2,1,0:T(8,128)}, f32[3,9,64,64]{3,2,1,0:T(8,128)}, f32[8,128]{1,0:T(8,128)S(1)}) custom-call(bf16[272,128]{1,0:T(8,128)(2,1)S(1)} %get-tuple-element.57.refs_0_, bf16[272,128]{1,0:T(8,128)(2,1)S(1)} %collective-permute-done.13.refs_1_), custom_call_target="tpu_custom_call" | custom-call | bytes 696320 | tf_op jit(solution)/shard_map/pallas_call | solution.py:18
  38.3 0.9 %collective-permute-done.12.in_ref = bf16[288,128]{1,0:T(8,128)(2,1)S(1)} collective-permute-done((bf16[288,128]{1,0:T(8,128)(2,1)S(1)}, bf16[288,128]{1,0:T(8,128)(2,1)S(1)}, u32[]{:S(2)}, u32[]{:S(2)}) %collective-permute-start.12) | collective-permute-done | bytes 73760 | tf_op jit(solution)/shard_map/ppermute | solution.py:466
  39.2 1.4 %shard_map.80 = (f32[9,3,32,32]{3,2,1,0:T(8,128)}, f32[3,9,64,64]{3,2,1,0:T(8,128)}, f32[8,128]{1,0:T(8,128)}) custom-call(bf16[272,128]{1,0:T(8,128)(2,1)S(1)} %shard_map.79.refs_0_, f32[9,3,32,32]{3,2,1,0:T(8,128)} %get-tuple-element.59.refs_1_, f32[3,9,64,64]{3,2,1,0:T(8,128)} %get-tuple-element.60.refs_2_), custom_call_target="tpu_custom_call", output_to_operand_aliasing={{0}: (1, {}), {1}: (2, {})} | custom-call | bytes 1179648 | tf_op jit(solution)/shard_map/pallas_call | solution.py:18
  40.6 1.4 %shard_map.81 = (f32[9,3,32,32]{3,2,1,0:T(8,128)}, f32[3,9,64,64]{3,2,1,0:T(8,128)}, f32[8,128]{1,0:T(8,128)}) custom-call(bf16[272,128]{1,0:T(8,128)(2,1)S(1)} %collective-permute-done.14.refs_0_, f32[9,3,32,32]{3,2,1,0:T(8,128)} %get-tuple-element.61.refs_1_, f32[3,9,64,64]{3,2,1,0:T(8,128)} %get-tuple-element.62.refs_2_), custom_call_target="tpu_custom_call", output_to_operand_aliasing={{0}: (1, {}), {1}: (2, {})} | custom-call | bytes 1179648 | tf_op jit(solution)/shard_map/pallas_call | solution.py:18
  (29 shorter events, 2.7 us)
Async XLA Ops:
  0.6 4.7 %copy-start = (bf16[1,128,2,8,128]{4,3,2,1,0:T(8,128)(2,1)S(1)}, bf16[1,128,2,8,128]{4,3,2,1,0:T(8,128)(2,1)}, u32[]{:S(2)}) copy-start(bf16[1,128,2,8,128]{4,3,2,1,0:T(8,128)(2,1)} %param.7) | copy-start | bytes 1572868
  0.6 4.7 %copy-start.1 = (bf16[27,128,64]{1,2,0:T(8,128)(2,1)S(1)}, bf16[27,128,64]{1,2,0:T(8,128)(2,1)}, u32[]{:S(2)}) copy-start(bf16[27,128,64]{1,2,0:T(8,128)(2,1)} %param.6) | copy-start | bytes 1327108
  0.7 7.0 %collective-permute-start.1 = (bf16[32,2,8,128]{3,2,1,0:T(8,128)(2,1)}, bf16[32,2,8,128]{3,2,1,0:T(8,128)(2,1)S(1)}, u32[]{:S(2)}, u32[]{:S(2)}) collective-permute-start(bf16[32,2,8,128]{3,2,1,0:T(8,128)(2,1)} %bitcast.11), channel_id=1, source_target_pairs={{0,16},{4,8},{8,4},{12,28},{16,0},{20,24},{24,20},{28,12},{1,17},{... | collective-permute-start | bytes 393224 | tf_op jit(solution)/shard_map/ppermute | solution.py:458
  3.7 5.2 %collective-permute-start = (bf16[32,2,8,128]{3,2,1,0:T(8,128)(2,1)}, bf16[32,2,8,128]{3,2,1,0:T(8,128)(2,1)S(1)}, u32[]{:S(2)}, u32[]{:S(2)}) collective-permute-start(bf16[32,2,8,128]{3,2,1,0:T(8,128)(2,1)} %bitcast.12), channel_id=1, source_target_pairs={{0,4},{4,0},{8,12},{12,8},{16,20},{20,16},{24,28},{28,24},{1,5},{5... | collective-permute-start | bytes 393224 | tf_op jit(solution)/shard_map/ppermute | solution.py:458
  5.3 1.8 %copy-start.2 = (bf16[27,64,32]{1,2,0:T(8,128)(2,1)S(1)}, bf16[27,64,32]{1,2,0:T(8,128)(2,1)}, u32[]{:S(2)}) copy-start(bf16[27,64,32]{1,2,0:T(8,128)(2,1)} %param.5) | copy-start | bytes 331780
  5.3 1.8 %copy-start.3 = (bf16[1,32,2,8,128]{4,3,2,1,0:T(8,128)(2,1)S(1)}, bf16[1,32,2,8,128]{4,3,2,1,0:T(8,128)(2,1)}, u32[]{:S(2)}) copy-start(bf16[1,32,2,8,128]{4,3,2,1,0:T(8,128)(2,1)} %param.4) | copy-start | bytes 393220
  9.1 4.7 %collective-permute-start.2 = (bf16[6,32,256]{2,1,0:T(8,128)(2,1)S(1)}, bf16[6,32,256]{2,1,0:T(8,128)(2,1)S(1)}, u32[]{:S(2)}, u32[]{:S(2)}) collective-permute-start(bf16[6,32,256]{2,1,0:T(8,128)(2,1)S(1)} %get-tuple-element.37), channel_id=1, source_target_pairs={{0,16},{1,2},{2,1},{3,19},{16,0},{17,18},{18,17},{19,3},{4,20},{5,... | collective-permute-start | bytes 294920 | tf_op jit(solution)/shard_map/ppermute | solution.py:458
  10.6 3.2 %collective-permute-start.3 = (bf16[6,32,256]{2,1,0:T(8,128)(2,1)S(1)}, bf16[6,32,256]{2,1,0:T(8,128)(2,1)S(1)}, u32[]{:S(2)}, u32[]{:S(2)}) collective-permute-start(bf16[6,32,256]{2,1,0:T(8,128)(2,1)S(1)} %get-tuple-element.38), channel_id=1, source_target_pairs={{0,1},{1,0},{2,3},{3,2},{16,17},{17,16},{18,19},{19,18},{4,5},{5,4... | collective-permute-start | bytes 294920 | tf_op jit(solution)/shard_map/ppermute | solution.py:458
  15.9 1.7 %collective-permute-start.4 = (bf16[2,2,224,128]{3,2,1,0:T(8,128)(2,1)S(1)}, bf16[2,2,224,128]{3,2,1,0:T(8,128)(2,1)S(1)}, u32[]{:S(2)}, u32[]{:S(2)}) collective-permute-start(bf16[2,2,224,128]{3,2,1,0:T(8,128)(2,1)S(1)} %get-tuple-element.48), channel_id=1, source_target_pairs={{0,1},{1,0},{2,3},{3,2},{4,5},{5,4},{6,7},{7,6},{8,9},{9,8},{10,11... | collective-permute-start | bytes 688136 | tf_op jit(solution)/shard_map/ppermute | solution.py:466
  16.0 1.7 %collective-permute-start.5 = (f32[2,2,64,128]{3,2,1,0:T(8,128)S(1)}, f32[2,2,64,128]{3,2,1,0:T(8,128)S(1)}, u32[]{:S(2)}, u32[]{:S(2)}) collective-permute-start(f32[2,2,64,128]{3,2,1,0:T(8,128)S(1)} %get-tuple-element.50), channel_id=1, source_target_pairs={{0,1},{1,0},{2,3},{3,2},{4,5},{5,4},{6,7},{7,6},{8,9},{9,8},{10,11... | collective-permute-start | bytes 393224 | tf_op jit(solution)/shard_map/ppermute | solution.py:466
  17.7 4.4 %collective-permute-start.6 = (bf16[272,128]{1,0:T(8,128)(2,1)S(1)}, bf16[272,128]{1,0:T(8,128)(2,1)S(1)}, u32[]{:S(2)}, u32[]{:S(2)}) collective-permute-start(bf16[272,128]{1,0:T(8,128)(2,1)S(1)} %get-tuple-element.52), channel_id=1, source_target_pairs={{0,16},{2,18},{16,0},{18,2},{1,17},{3,19},{17,1},{19,3},{4,20},{6,... | collective-permute-start | bytes 208904 | tf_op jit(solution)/shard_map/ppermute | solution.py:466
  19.2 5.3 %collective-permute-start.7 = (bf16[272,128]{1,0:T(8,128)(2,1)S(1)}, bf16[272,128]{1,0:T(8,128)(2,1)S(1)}, u32[]{:S(2)}, u32[]{:S(2)}) collective-permute-start(bf16[272,128]{1,0:T(8,128)(2,1)S(1)} %get-tuple-element.53), channel_id=1, source_target_pairs={{0,18},{2,16},{16,2},{18,0},{1,19},{3,17},{17,3},{19,1},{4,22},{6,... | collective-permute-start | bytes 208904 | tf_op jit(solution)/shard_map/ppermute | solution.py:466
  20.2 5.2 %collective-permute-start.8 = (bf16[272,128]{1,0:T(8,128)(2,1)S(1)}, bf16[272,128]{1,0:T(8,128)(2,1)S(1)}, u32[]{:S(2)}, u32[]{:S(2)}) collective-permute-start(bf16[272,128]{1,0:T(8,128)(2,1)S(1)} %get-tuple-element.54), channel_id=1, source_target_pairs={{0,2},{2,0},{16,18},{18,16},{1,3},{3,1},{17,19},{19,17},{4,6},{6,4... | collective-permute-start | bytes 208904 | tf_op jit(solution)/shard_map/ppermute | solution.py:466
  25.5 7.0 %collective-permute-start.11 = (bf16[272,128]{1,0:T(8,128)(2,1)S(1)}, bf16[272,128]{1,0:T(8,128)(2,1)S(1)}, u32[]{:S(2)}, u32[]{:S(2)}) collective-permute-start(bf16[272,128]{1,0:T(8,128)(2,1)S(1)} %shard_map.76.a_ref), channel_id=1, source_target_pairs={{0,12},{4,8},{8,4},{12,0},{1,13},{5,9},{9,5},{13,1},{2,14},{6,10},... | collective-permute-start | bytes 208904 | tf_op jit(solution)/shard_map/ppermute | solution.py:466
  28.8 5.9 %collective-permute-start.10 = (bf16[272,128]{1,0:T(8,128)(2,1)S(1)}, bf16[272,128]{1,0:T(8,128)(2,1)S(1)}, u32[]{:S(2)}, u32[]{:S(2)}) collective-permute-start(bf16[272,128]{1,0:T(8,128)(2,1)S(1)} %shard_map.76.a_ref), channel_id=1, source_target_pairs={{0,8},{4,12},{8,0},{12,4},{1,9},{5,13},{9,1},{13,5},{2,10},{6,14},... | collective-permute-start | bytes 208904 | tf_op jit(solution)/shard_map/ppermute | solution.py:466
  28.8 5.9 %collective-permute-start.9 = (bf16[272,128]{1,0:T(8,128)(2,1)S(1)}, bf16[272,128]{1,0:T(8,128)(2,1)S(1)}, u32[]{:S(2)}, u32[]{:S(2)}) collective-permute-start(bf16[272,128]{1,0:T(8,128)(2,1)S(1)} %shard_map.76.a_ref), channel_id=1, source_target_pairs={{0,4},{4,0},{8,12},{12,8},{1,5},{5,1},{9,13},{13,9},{2,6},{6,2},{1... | collective-permute-start | bytes 208904 | tf_op jit(solution)/shard_map/ppermute | solution.py:466
  34.7 4.4 %collective-permute-start.12 = (bf16[288,128]{1,0:T(8,128)(2,1)S(1)}, bf16[288,128]{1,0:T(8,128)(2,1)S(1)}, u32[]{:S(2)}, u32[]{:S(2)}) collective-permute-start(bf16[288,128]{1,0:T(8,128)(2,1)S(1)} %get-tuple-element.56), channel_id=1, source_target_pairs={{0,2},{2,0},{1,3},{3,1},{4,6},{6,4},{5,7},{7,5},{8,10},{10,8},{9,1... | collective-permute-start | bytes 221192 | tf_op jit(solution)/shard_map/ppermute | solution.py:466
  36.0 1.3 %collective-permute-start.13 = (bf16[272,128]{1,0:T(8,128)(2,1)S(1)}, bf16[272,128]{1,0:T(8,128)(2,1)S(1)}, u32[]{:S(2)}, u32[]{:S(2)}) collective-permute-start(bf16[272,128]{1,0:T(8,128)(2,1)S(1)} %get-tuple-element.57.refs_0_), channel_id=1, source_target_pairs={{0,1},{1,0},{2,3},{3,2},{4,5},{5,4},{6,7},{7,6},{8,9},{9,8},{10,11... | collective-permute-start | bytes 208904 | tf_op jit(solution)/shard_map/ppermute | solution.py:466
  39.2 1.5 %collective-permute-start.14 = (bf16[272,128]{1,0:T(8,128)(2,1)S(1)}, bf16[272,128]{1,0:T(8,128)(2,1)S(1)}, u32[]{:S(2)}, u32[]{:S(2)}) collective-permute-start(bf16[272,128]{1,0:T(8,128)(2,1)S(1)} %shard_map.79.refs_0_), channel_id=1, source_target_pairs={{0,1},{1,0},{2,3},{3,2},{4,5},{5,4},{6,7},{7,6},{8,9},{9,8},{10,11... | collective-permute-start | bytes 208904 | tf_op jit(solution)/shard_map/ppermute | solution.py:466

commit v15 on v13

--- a/solution.py
+++ b/solution.py
@@ -96,7 +96,7 @@
     return stacked.astype(F32).T.astype(BF)
 
 
-def arrange_kernel(cot_rows_ref, k1_ref, vol_ref, moved_ref, w1_ref, own_ref, scratch):
+def arrange_kernel(cot_rows_ref, k1_ref, vol_ref, moved_ref, w1_ref, w1_last_ref, own_ref, scratch):
     def store(d, h, row):
         own_ref[d, :, h * LANES : (h + 1) * LANES] = row.astype(BF)
 
@@ -110,7 +110,10 @@
                 moved_ref[d, n * out : (n + 1) * out, h : h + LANES] = value
     mid = k1_ref.shape[2]
     for c in range(3):
-        w1_ref[c * mid : (c + 1) * mid, :] = as_matrix(k1_ref, c)
+        w = as_matrix(k1_ref, c)
+        split = w1_ref.shape[1]
+        w1_ref[c * mid : (c + 1) * mid, :] = w[:, :split]
+        w1_last_ref[:, c * (w.shape[1] - split) : (c + 1) * (w.shape[1] - split)] = w[:, split:]
 
 
 def sides(axis, one, two):
@@ -143,20 +146,22 @@
     return [jnp.concatenate([left[d], deep_ref[d], right[d]], axis=1) for d in range(deep_ref.shape[0])]
 
 
-def pack(direct, refs, rows_of, blocks):
-    if not direct:
-        for j, block in enumerate(blocks):
-            refs[0][j] = block
-        return
-    keep_ref, send_ref = refs
-    parts, halves, length, _ = keep_ref.shape
+def pack(keep_ref, send_ref, rows_of):
+    parts, halves, _, _ = keep_ref.shape
     core = lax.axis_index("core") == 1
     for part in range(parts):
-        one, two = (jnp.concatenate(rows_of(part, c), axis=0) for c in range(2))
+        one, two = ([jnp.concatenate(rows, axis=0) for rows in rows_of(part, c)] for c in range(2))
         for half in range(halves):
-            at = slice(half * length, (half + 1) * length)
-            keep_ref[part, half] = jnp.where(core, two[at], one[at])
-            send_ref[part, half] = jnp.where(core, one[at], two[at]).astype(send_ref.dtype)
+
+            def quarter(grads, half=half):
+                lengths = [grad.shape[0] // halves for grad in grads]
+                return jnp.concatenate(
+                    [grad[half * n : (half + 1) * n] for grad, n in zip(grads, lengths, strict=True)], axis=0
+                )
+
+            a, b = quarter(one), quarter(two)
+            keep_ref[part, half] = jnp.where(core, b, a)
+            send_ref[part, half] = jnp.where(core, a, b).astype(BF)
 
 
 def folded(tail):
@@ -164,10 +169,16 @@
     return jnp.concatenate([tail[:half], tail[half:]], axis=1)
 
 
-def activated(w1, rhs, d, depth, heights):
-    mid = w1.shape[0] // 3
-    y = jnp.dot(w1, rhs, preferred_element_type=F32)
-    pre = sum(moved_along_width(y[n * mid : (n + 1) * mid], 1 - n) for n in range(3))
+def activated(weights, ref, d, h, depth, heights):
+    w1, w1_last = weights
+    mid = w1_last.shape[0]
+    rhs = neighbours(ref, d, [h], 2)
+    n_last = ref.shape[1]
+    y = jnp.dot(w1, rhs[: rhs.shape[0] - n_last], preferred_element_type=F32)
+    last = rhs[rhs.shape[0] - n_last :].astype(F32)
+    last = jnp.concatenate([moved_along_width(last, 1 - n).astype(BF) for n in range(3)], axis=0)
+    pre = jnp.dot(w1_last, last, preferred_element_type=F32)
+    pre = sum((moved_along_width(y[n * mid : (n + 1) * mid], 1 - n) for n in range(3)), pre)
     s = 1.0 / (1.0 + jnp.exp(-pre))
     dep, deps = lax.axis_index("dep"), lax.axis_size("dep")
     hgt, hgts = lax.axis_index(HGT), lax.axis_size(HGT)
@@ -213,13 +224,13 @@
         ref[n * n_channels : (n + 1) * n_channels, at : at + LANES] = moved_along_width(delta, n - 1).astype(BF)
 
 
-def inner_kernel(deep_ref, w1_ref, moved_ref, back_ref, hidden_ref, second_ref, first_ref, delta_ref):
-    w1 = w1_ref[...]
+def inner_kernel(deep_ref, w1_ref, w1_last_ref, moved_ref, back_ref, hidden_ref, second_ref, first_ref, delta_ref):
+    weights = w1_ref[...], w1_last_ref[...]
     depth, mid, cells = hidden_ref.shape
     height = cells // LANES
     for d in range(depth):
         for h in range(0, height, 2):
-            results = activated(w1, neighbours(deep_ref, d, [h], 2), d, depth, (0, 0))
+            results = activated(weights, deep_ref, d, h, depth, (0, 0))
             for n, (value, slope) in enumerate(results):
                 at = (h + n) * LANES
                 hidden_ref[d, :, at : at + LANES] = value
@@ -238,47 +249,40 @@
     )
     second_ref[...] = products(left, right)
     right = jnp.concatenate([neighbours(deep_ref, d, [0], height) for d in range(depth)], axis=1)
-    first_ref[...] = products(delta_ref[...], right)
+    first_ref[...] = products(right, delta_ref[...])
 
 
 def outer_kernel(
-    direct, deep_ref, two_ref, one_ref, w1_ref, back_ref, inner_ref, first_ref, hidden_ref, *grad_refs_and_scratch,
+    deep_ref, two_ref, one_ref, w1_ref, w1_last_ref, back_ref, inner_ref, first_ref, hidden_ref, blocks_ref, rows_ref, delta_ref,
 ):
-    *grad_refs, rows_ref, delta_ref = grad_refs_and_scratch
     for d, row in enumerate(widened(deep_ref, one_ref, two_ref)):
         rows_ref[d] = row
-    w1 = w1_ref[...]
+    weights = w1_ref[...], w1_last_ref[...]
     depth, mid, cells = hidden_ref.shape
     last = cells // LANES - 2
     for d in range(depth):
         hidden_ref[d, :, 2 * LANES : last * LANES] = inner_ref[d]
         for h, sides_of in ((0, (-1, 0)), (last, (0, 1))):
-            results = activated(w1, neighbours(rows_ref, d, [h], 2), d, depth, sides_of)
+            results = activated(weights, rows_ref, d, h, depth, sides_of)
             for n, (value, slope) in enumerate(results):
                 at = (h + n) * LANES
                 hidden_ref[d, :, at : at + LANES] = value
                 delta = back_ref[d, :, at : at + LANES] * slope
                 shares(delta, mid, delta_ref, (4 * d + (2 if h else 0) + n) * LANES)
     right = jnp.concatenate([neighbours(rows_ref, d, [0, last], 2) for d in range(depth)], axis=1)
-    total = first_ref[...] + products(delta_ref[...], right)
+    total = (first_ref[...] + products(right, delta_ref[...])).T
     inner = rows_ref.shape[1]
-    blocks, tails = [], []
+    tails = []
     for n in range(3):
         part = total[n * mid : (n + 1) * mid]
-        blocks += [part[:, m * LANES : (m + 1) * LANES] for m in range(2)]
+        for m in range(2):
+            blocks_ref[2 * n + m] = part[:, m * LANES : (m + 1) * LANES]
         tails.append(part[:, 2 * LANES :])
     tails.append(jnp.zeros((mid, LANES - 3 * inner), F32))
-    blocks.append(jnp.concatenate(tails, axis=1))
-    size = mid // lax.axis_size("dp")
-    half = size // 2
-
-    def rows_of(part, core):
-        return [block[part * size + core * half : part * size + (core + 1) * half] for block in blocks]
-
-    pack(direct, grad_refs, rows_of, blocks)
-
-
-def second_kernel(direct, hidden_ref, moved_ref, second_ref, *grad_refs):
+    blocks_ref[6] = jnp.concatenate(tails, axis=1)
+
+
+def second_kernel(direct, hidden_ref, moved_ref, second_ref, first_ref, *grad_refs):
     depth, mid, cells = hidden_ref.shape
     height = cells // LANES
     own = depth - 2
@@ -305,11 +309,18 @@
     blocks = heads + [jnp.concatenate(tails[n : n + 2], axis=1) for n in range(0, 8, 2)]
     size = mid // lax.axis_size("dp")
 
+    if not direct:
+        for j, block in enumerate([*blocks, jnp.concatenate([tails[8], jnp.zeros_like(tails[8])], axis=1)]):
+            grad_refs[0][j] = block
+        return
+
     def rows_of(part, core):
         at = slice((2 * part + core) * size, (2 * part + core + 1) * size)
-        return [block[at] for block in blocks] + [folded(tails[8][at])]
-
-    pack(direct, grad_refs, rows_of, [*blocks, jnp.concatenate([tails[8], jnp.zeros_like(tails[8])], axis=1)])
+        second = [block[at] for block in blocks] + [folded(tails[8][at])]
+        start = part * size + core * (size // 2)
+        return second, [first_ref[j, start : start + size // 2, :] for j in range(first_ref.shape[0])]
+
+    pack(*grad_refs, rows_of)
 
 
 def features_kernel(hidden_ref, k2_ref, out_ref, token_ref, scratch):
@@ -334,14 +345,13 @@
     token_ref[...] = scratch[:8]
 
 
-def plane_kernel(moves, *refs):
-    keep_first, got_first, keep_second, got_second, kept_ref, *send_refs = refs
-    part = lax.rem(lax.axis_index("dp"), keep_first.shape[0])
+def plane_kernel(moves, keep_ref, got_ref, kept_ref, *send_refs):
+    part = lax.rem(lax.axis_index("dp"), keep_ref.shape[0])
     half = lax.axis_index("y")
 
     def total(x, y):
         at = 1 - part if x else part, 1 - half if y else half
-        return jnp.concatenate([keep_second[at] + got_second[at].astype(F32), keep_first[at] + got_first[at]], axis=0)
+        return keep_ref[at] + got_ref[at].astype(F32)
 
     kept_ref[...] = total(0, 0)
     for (x, y), send_ref in zip(moves, send_refs, strict=True):
@@ -471,11 +481,12 @@
         [pltpu.VMEM((out * rows, width), F32)],
         flops=1_100_000_000,
     )
-    moved, w1, vol = call(
+    moved, w1, w1_last, vol = call(
         arrange_kernel,
         [
             shape((depth, 3 * out, cells), BF),
-            shape((3 * mid, 9 * inner), BF),
+            shape((3 * mid, 8 * inner), BF),
+            shape((mid, 3 * inner), BF),
             shape((depth, inner, cells), BF),
         ],
         [cot_rows, k1, volume[0]],
@@ -499,47 +510,47 @@
         [
             shape((depth + 2, mid, rows_in * width), BF),
             shape((9 * out, 3 * mid), F32),
-            shape((3 * mid, 9 * inner), F32),
+            shape((9 * inner, 3 * mid), F32),
         ],
-        [deep, w1, moved, back],
+        [deep, w1, w1_last, moved, back],
         [pltpu.VMEM((3 * mid, (depth + 2) * rows_in * width), BF)],
         flops=1_500_000_000,
     )
-    hidden, *first = call(
-        functools.partial(outer_kernel, direct),
-        [shape((depth + 2, mid, cells + 2 * width), BF)]
-        + ([shape((parts, halves, length_first, width), F32)] * 2 if direct else [shape((7, mid, LANES), F32)]),
-        [deep, two, one, w1, back, inner_hidden, inner_first],
+    hidden, first = call(
+        outer_kernel,
+        [shape((depth + 2, mid, cells + 2 * width), BF), shape((7, mid, LANES), F32)],
+        [deep, two, one, w1, w1_last, back, inner_hidden, inner_first],
         [
             pltpu.VMEM((3 * depth, inner, cells + 4 * width), BF),
             pltpu.VMEM((3 * mid, (depth + 2) * rows_out * width), BF),
         ],
         flops=1_000_000_000,
     )
-    second = call(
+    block = (length_second + length_first, width)
+    grads = call(
         functools.partial(second_kernel, direct),
-        [shape((parts, halves, length_second, width), kind) for kind in (F32, BF)]
-        if direct
-        else [shape((14, out, LANES), F32)],
-        [hidden, moved, inner_second],
+        [shape((parts, halves, *block), kind) for kind in (F32, BF)] if direct else [shape((14, out, LANES), F32)],
+        [hidden, moved, inner_second, first],
         flops=4_000_000_000,
     )
     if direct:
         moves = [(1, 0), (0, 1), (1, 1)]
+        keep, send = grads
     else:
         moves = [(0, 1)]
-        blocks = second[0].reshape(14, parts, 2, size, LANES).transpose(1, 2, 0, 3, 4)
+        blocks = grads[0].reshape(14, parts, 2, size, LANES).transpose(1, 2, 0, 3, 4)
         tail = blocks[:, :, 13, :, :mid]
         tail = jnp.concatenate([tail[:, :, : size // 2], tail[:, :, size // 2 :]], axis=-1)
         rows_second = jnp.concatenate([blocks[:, :, :13].reshape(parts, 2, 13 * size, LANES), tail], axis=2)
-        second = scattered(rows_second, length_second)
-        blocks = first[0].reshape(7, parts, 2, size // 2, LANES).transpose(1, 2, 0, 3, 4)
-        first = scattered(blocks.reshape(parts, 2, 7 * (size // 2), LANES), length_first)
-    block = (length_second + length_first, width)
+        blocks = first.reshape(7, parts, 2, size // 2, LANES).transpose(1, 2, 0, 3, 4)
+        rows_first = blocks.reshape(parts, 2, 7 * (size // 2), LANES)
+        pairs = [scattered(rows, n) for rows, n in ((rows_second, length_second), (rows_first, length_first))]
+        keep, send = (jnp.concatenate(both, axis=2) for both in zip(*pairs, strict=True))
+        send = send.astype(BF)
     kept, *sends = call(
         functools.partial(plane_kernel, moves),
         [shape(block, F32)] + [shape(block, BF)] * len(moves),
-        [x for keep, send in (first, second) for x in (keep, across(send, ("core", 1)))],
+        [keep, across(send, ("core", 1))],
     )
     gots = [across(send, ("dp", x), ("y", y)) for send, (x, y) in zip(sends, moves, strict=True)]
     (share,) = call(total_kernel, [shape(block, BF)], [kept, *gots])

time: 40.8 us -> 40.7 us (level)
  starting transfers between devices: 16.2 us -> 15.7 us
  waiting for transfers between devices: 11.9 us -> 12.4 us
    ppermute x10 -> x9, starting transfers between devices: 9.79 us -> 9.3 us  [across(): lax.ppermute(x, axes, [(i, i ^ flip) for i in range(lax.axis_size(axes))])]
    ppermute x10 -> x9, waiting for transfers between devices: 10.3 us -> 10.7 us  [across(): lax.ppermute(x, axes, [(i, i ^ flip) for i in range(lax.axis_size(axes))])]
  transfers between devices with their start and end apart: 14 -> 13, of which waited for: 9 -> 9; matrix products, arithmetic and copies ran while one was open for 0% -> 0% of each run, Pallas kernels for 20% -> 20%
where the time goes in v15:
time: 40.7 us; the launch traced here: 40.6 us
  starting transfers between devices  15.7 us (39%)
  waiting for transfers between devices  12.4 us (30%)
  Pallas kernels  11.7 us (29%)
  between operations  0.79 us (2%)
    pallas_call x14, Pallas kernels, call(): pl.pallas_call(body, out_shape=outs, in_specs=[pl.BlockSpec(memory_space=...  11.7 us
    ppermute x9, waiting for transfers between devices, across(): lax.ppermute(x, axes, [(i, i ^ flip) for i in range(lax.axis_size(axes))])  10.7 us
    ppermute x9, starting transfers between devices, across(): lax.ppermute(x, axes, [(i, i ^ flip) for i in range(lax.axis_size(axes))])  9.3 us
    ppermute x4, starting transfers between devices, swapped(): return lax.ppermute(x, ('dp', *axes), list(enumerate(partner)))  6.36 us
    ppermute x4, waiting for transfers between devices, swapped(): return lax.ppermute(x, ('dp', *axes), list(enumerate(partner)))  1.73 us
  transfers between devices with their start and end apart: 13, of which 9 were waited for; matrix products, arithmetic and copies ran while one was open for 0% of the time, Pallas kernels for 20%

profile of v15, /device:TPU:0, one launch (start us, length us, event | category | flops | bytes accessed | tf_op | source)
XLA Modules:
  0.0 40.6 jit_solution(1828886547607492531)
XLA Ops:
  0.7 3.0 %collective-permute-start.1 = (bf16[32,2,8,128]{3,2,1,0:T(8,128)(2,1)}, bf16[32,2,8,128]{3,2,1,0:T(8,128)(2,1)S(1)}, u32[]{:S(2)}, u32[]{:S(2)}) collective-permute-start(bf16[32,2,8,128]{3,2,1,0:T(8,128)(2,1)} %bitcast.9), channel_id=1, source_target_pairs={{0,16},{4,8},{8,4},{12,28},{16,0},{20,24},{24,20},{28,12},{1,17},{... | collective-permute-start | bytes 393224 | tf_op jit(solution)/shard_map/ppermute | solution.py:422
  3.7 1.7 %collective-permute-start = (bf16[32,2,8,128]{3,2,1,0:T(8,128)(2,1)}, bf16[32,2,8,128]{3,2,1,0:T(8,128)(2,1)S(1)}, u32[]{:S(2)}, u32[]{:S(2)}) collective-permute-start(bf16[32,2,8,128]{3,2,1,0:T(8,128)(2,1)} %bitcast.10), channel_id=1, source_target_pairs={{0,4},{4,0},{8,12},{12,8},{16,20},{20,16},{24,28},{28,24},{1,5},{5... | collective-permute-start | bytes 393224 | tf_op jit(solution)/shard_map/ppermute | solution.py:422
  5.4 1.7 %shard_map.68 = (bf16[2,128,1024]{2,1,0:T(8,128)(2,1)S(1)}, f32[4,64,1280]{2,1,0:T(8,128)S(1)}) custom-call(bf16[128,2,8,128]{3,2,1,0:T(8,128)(2,1)S(1)} %bitcast.5, bf16[27,64,128]{2,1,0:T(8,128)(2,1)S(1)} %bitcast.6, bf16[128,256]{1,0:T(8,128)(2,1)S(1)} %shard_map.67.blank_ref), custom_call_target="tpu_custom_call" | custom-call | flops 1100000000 | bytes 2867200 | tf_op jit(solution)/shard_map/pallas_call | solution.py:18
  7.7 1.1 %collective-permute-done.one_ref = bf16[32,2,8,128]{3,2,1,0:T(8,128)(2,1)S(1)} collective-permute-done((bf16[32,2,8,128]{3,2,1,0:T(8,128)(2,1)}, bf16[32,2,8,128]{3,2,1,0:T(8,128)(2,1)S(1)}, u32[]{:S(2)}, u32[]{:S(2)}) %collective-permute-start) | collective-permute-done | bytes 131104 | tf_op jit(solution)/shard_map/ppermute | solution.py:422
  9.1 1.5 %collective-permute-start.2 = (bf16[6,32,256]{2,1,0:T(8,128)(2,1)S(1)}, bf16[6,32,256]{2,1,0:T(8,128)(2,1)S(1)}, u32[]{:S(2)}, u32[]{:S(2)}) collective-permute-start(bf16[6,32,256]{2,1,0:T(8,128)(2,1)S(1)} %get-tuple-element.32), channel_id=1, source_target_pairs={{0,16},{1,2},{2,1},{3,19},{16,0},{17,18},{18,17},{19,3},{4,20},{5,... | collective-permute-start | bytes 294920 | tf_op jit(solution)/shard_map/ppermute | solution.py:422
  10.8 2.4 %shard_map.71 = (bf16[4,64,768]{2,1,0:T(8,128)(2,1)S(1)}, f32[1152,192]{1,0:T(8,128)S(1)}, f32[288,192]{1,0:T(8,128)S(1)}) custom-call(bf16[6,32,1024]{2,1,0:T(8,128)(2,1)S(1)} %get-tuple-element.31.deep_ref, bf16[192,256]{1,0:T(8,128)(2,1)S(1)} %get-tuple-element.34.w1_ref, bf16[64,96]{1,0:T(8,128)(2,1)S(1)} %get-tuple-element.35.w1_last_ref, ...), custom_call_target="tpu_custom_call" | custom-call | flops 1500000000 | bytes 4886528 | tf_op jit(solution)/shard_map/pallas_call | solution.py:18
  13.2 0.6 %collective-permute-done.2.two_ref = bf16[6,32,256]{2,1,0:T(8,128)(2,1)S(1)} collective-permute-done((bf16[6,32,256]{2,1,0:T(8,128)(2,1)S(1)}, bf16[6,32,256]{2,1,0:T(8,128)(2,1)S(1)}, u32[]{:S(2)}, u32[]{:S(2)}) %collective-permute-start.2) | collective-permute-done | bytes 98336 | tf_op jit(solution)/shard_map/ppermute | solution.py:422
  13.8 1.6 %shard_map.72 = (bf16[4,64,1280]{2,1,0:T(8,128)(2,1)S(1)}, f32[7,64,128]{2,1,0:T(8,128)S(1)}) custom-call(bf16[6,32,1024]{2,1,0:T(8,128)(2,1)S(1)} %get-tuple-element.31.deep_ref, bf16[6,32,256]{2,1,0:T(8,128)(2,1)S(1)} %collective-permute-done.2.two_ref, bf16[6,32,256]{2,1,0:T(8,128)(2,1)S(1)} %collective-permute-done.3.one_ref, ...), custom_call_target="tpu_custom_call" | custom-call | flops 1000000000 | bytes 3510272 | tf_op jit(solution)/shard_map/pallas_call | solution.py:18
  15.4 0.6 %shard_map.74 = (f32[2,2,272,128]{3,2,1,0:T(8,128)S(1)}, bf16[2,2,272,128]{3,2,1,0:T(8,128)(2,1)S(1)}) custom-call(bf16[4,64,1280]{2,1,0:T(8,128)(2,1)S(1)} %get-tuple-element.40.hidden_ref, bf16[2,384,1024]{2,1,0:T(8,128)(2,1)S(1)} %get-tuple-element.37.moved_ref, f32[1152,192]{1,0:T(8,128)S(1)} %get-tuple-element.42.second_ref, ...), custom_call_target="tpu_custom_call" | custom-call | flops 4000000000 | bytes 4177920 | tf_op jit(solution)/shard_map/pallas_call | solution.py:18
  16.1 1.5 %collective-permute-done.4.got_ref = bf16[2,2,272,128]{3,2,1,0:T(8,128)(2,1)S(1)} collective-permute-done((bf16[2,2,272,128]{3,2,1,0:T(8,128)(2,1)S(1)}, bf16[2,2,272,128]{3,2,1,0:T(8,128)(2,1)S(1)}, u32[]{:S(2)}, u32[]{:S(2)}) %collective-permute-start.4) | collective-permute-done | bytes 278560 | tf_op jit(solution)/shard_map/ppermute | solution.py:430
  17.7 1.5 %collective-permute-start.5 = (bf16[272,128]{1,0:T(8,128)(2,1)S(1)}, bf16[272,128]{1,0:T(8,128)(2,1)S(1)}, u32[]{:S(2)}, u32[]{:S(2)}) collective-permute-start(bf16[272,128]{1,0:T(8,128)(2,1)S(1)} %get-tuple-element.47), channel_id=1, source_target_pairs={{0,16},{2,18},{16,0},{18,2},{1,17},{3,19},{17,1},{19,3},{4,20},{6,... | collective-permute-start | bytes 208904 | tf_op jit(solution)/shard_map/ppermute | solution.py:430
  19.2 0.9 %collective-permute-start.6 = (bf16[272,128]{1,0:T(8,128)(2,1)S(1)}, bf16[272,128]{1,0:T(8,128)(2,1)S(1)}, u32[]{:S(2)}, u32[]{:S(2)}) collective-permute-start(bf16[272,128]{1,0:T(8,128)(2,1)S(1)} %get-tuple-element.48), channel_id=1, source_target_pairs={{0,2},{2,0},{16,18},{18,16},{1,3},{3,1},{17,19},{19,17},{4,6},{6,4... | collective-permute-start | bytes 208904 | tf_op jit(solution)/shard_map/ppermute | solution.py:430
  20.1 1.1 %collective-permute-start.7 = (bf16[272,128]{1,0:T(8,128)(2,1)S(1)}, bf16[272,128]{1,0:T(8,128)(2,1)S(1)}, u32[]{:S(2)}, u32[]{:S(2)}) collective-permute-start(bf16[272,128]{1,0:T(8,128)(2,1)S(1)} %get-tuple-element.49), channel_id=1, source_target_pairs={{0,18},{2,16},{16,2},{18,0},{1,19},{3,17},{17,3},{19,1},{4,22},{6,... | collective-permute-start | bytes 208904 | tf_op jit(solution)/shard_map/ppermute | solution.py:430
  21.2 0.8 %collective-permute-done.5.refs_0_ = bf16[272,128]{1,0:T(8,128)(2,1)S(1)} collective-permute-done((bf16[272,128]{1,0:T(8,128)(2,1)S(1)}, bf16[272,128]{1,0:T(8,128)(2,1)S(1)}, u32[]{:S(2)}, u32[]{:S(2)}) %collective-permute-start.5) | collective-permute-done | bytes 69664 | tf_op jit(solution)/shard_map/ppermute | solution.py:430
  22.0 2.2 %collective-permute-done.6.refs_1_ = bf16[272,128]{1,0:T(8,128)(2,1)S(1)} collective-permute-done((bf16[272,128]{1,0:T(8,128)(2,1)S(1)}, bf16[272,128]{1,0:T(8,128)(2,1)S(1)}, u32[]{:S(2)}, u32[]{:S(2)}) %collective-permute-start.6) | collective-permute-done | bytes 69664 | tf_op jit(solution)/shard_map/ppermute | solution.py:430
  24.2 1.1 %collective-permute-done.7.refs_2_ = bf16[272,128]{1,0:T(8,128)(2,1)S(1)} collective-permute-done((bf16[272,128]{1,0:T(8,128)(2,1)S(1)}, bf16[272,128]{1,0:T(8,128)(2,1)S(1)}, u32[]{:S(2)}, u32[]{:S(2)}) %collective-permute-start.7) | collective-permute-done | bytes 69664 | tf_op jit(solution)/shard_map/ppermute | solution.py:430
  25.4 2.8 %collective-permute-start.10 = (bf16[272,128]{1,0:T(8,128)(2,1)S(1)}, bf16[272,128]{1,0:T(8,128)(2,1)S(1)}, u32[]{:S(2)}, u32[]{:S(2)}) collective-permute-start(bf16[272,128]{1,0:T(8,128)(2,1)S(1)} %shard_map.76.a_ref), channel_id=1, source_target_pairs={{0,12},{4,8},{8,4},{12,0},{1,13},{5,9},{9,5},{13,1},{2,14},{6,10},... | collective-permute-start | bytes 208904 | tf_op jit(solution)/shard_map/ppermute | solution.py:430
  28.6 1.2 %collective-permute-start.8 = (bf16[272,128]{1,0:T(8,128)(2,1)S(1)}, bf16[272,128]{1,0:T(8,128)(2,1)S(1)}, u32[]{:S(2)}, u32[]{:S(2)}) collective-permute-start(bf16[272,128]{1,0:T(8,128)(2,1)S(1)} %shard_map.76.a_ref), channel_id=1, source_target_pairs={{0,4},{4,0},{8,12},{12,8},{1,5},{5,1},{9,13},{13,9},{2,6},{6,2},{1... | collective-permute-start | bytes 208904 | tf_op jit(solution)/shard_map/ppermute | solution.py:430
  29.8 2.5 %shard_map.73 = (bf16[128,2,8,128]{3,2,1,0:T(8,128)(2,1)}, f32[8,128]{1,0:T(8,128)S(1)}) custom-call(bf16[4,64,1280]{2,1,0:T(8,128)(2,1)S(1)} %get-tuple-element.40.hidden_ref, bf16[27,64,128]{2,1,0:T(8,128)(2,1)S(1)} %bitcast.7), custom_call_target="tpu_custom_call" | custom-call | flops 900000000 | bytes 1626112 | tf_op jit(solution)/shard_map/pallas_call | solution.py:18
  32.3 1.4 %collective-permute-done.9.c_ref = bf16[272,128]{1,0:T(8,128)(2,1)S(1)} collective-permute-done((bf16[272,128]{1,0:T(8,128)(2,1)S(1)}, bf16[272,128]{1,0:T(8,128)(2,1)S(1)}, u32[]{:S(2)}, u32[]{:S(2)}) %collective-permute-start.9) | collective-permute-done | bytes 69664 | tf_op jit(solution)/shard_map/ppermute | solution.py:430
  33.8 1.1 %collective-permute-start.11 = (bf16[272,128]{1,0:T(8,128)(2,1)S(1)}, bf16[272,128]{1,0:T(8,128)(2,1)S(1)}, u32[]{:S(2)}, u32[]{:S(2)}) collective-permute-start(bf16[272,128]{1,0:T(8,128)(2,1)S(1)} %shard_map.77.own_ref), channel_id=1, source_target_pairs={{0,2},{2,0},{1,3},{3,1},{4,6},{6,4},{5,7},{7,5},{8,10},{10,8},{9,1... | collective-permute-start | bytes 208904 | tf_op jit(solution)/shard_map/ppermute | solution.py:430
  35.0 3.2 %collective-permute-done.11.got_ref = bf16[272,128]{1,0:T(8,128)(2,1)S(1)} collective-permute-done((bf16[272,128]{1,0:T(8,128)(2,1)S(1)}, bf16[272,128]{1,0:T(8,128)(2,1)S(1)}, u32[]{:S(2)}, u32[]{:S(2)}) %collective-permute-start.11) | collective-permute-done | bytes 69664 | tf_op jit(solution)/shard_map/ppermute | solution.py:430
  38.3 0.9 %shard_map.79 = (f32[27,32,32]{2,1,0:T(8,128)}, f32[27,64,64]{2,1,0:T(8,128)}) custom-call(bf16[2,272,128]{2,1,0:T(8,128)(2,1)S(1)} %shard_map.78.in_ref), custom_call_target="tpu_custom_call" | custom-call | bytes 692224 | tf_op jit(solution)/shard_map/pallas_call | solution.py:18
  39.6 0.9 %shard_map.80 = (f32[27,32,32]{2,1,0:T(8,128)}, f32[27,64,64]{2,1,0:T(8,128)}) custom-call(bf16[2,272,128]{2,1,0:T(8,128)(2,1)S(1)} %collective-permute-done.12.in_ref, f32[27,32,32]{2,1,0:T(8,128)} %get-tuple-element.51.refs_0_, f32[27,64,64]{2,1,0:T(8,128)} %get-tuple-element.52.refs_1_), custom_call_target="tpu_custom_call", output_to_operand_aliasing={{0}: (1, {}), {1}: (2, {})} | custom-call | bytes 1245184 | tf_op jit(solution)/shard_map/pallas_call | solution.py:18
  (24 shorter events, 2.3 us)
Async XLA Ops:
  0.6 4.7 %copy-start = (bf16[1,128,2,8,128]{4,3,2,1,0:T(8,128)(2,1)S(1)}, bf16[1,128,2,8,128]{4,3,2,1,0:T(8,128)(2,1)}, u32[]{:S(2)}) copy-start(bf16[1,128,2,8,128]{4,3,2,1,0:T(8,128)(2,1)} %param.7) | copy-start | bytes 1572868
  0.6 4.7 %copy-start.1 = (bf16[27,128,64]{1,2,0:T(8,128)(2,1)S(1)}, bf16[27,128,64]{1,2,0:T(8,128)(2,1)}, u32[]{:S(2)}) copy-start(bf16[27,128,64]{1,2,0:T(8,128)(2,1)} %param.6) | copy-start | bytes 1327108
  0.7 7.0 %collective-permute-start.1 = (bf16[32,2,8,128]{3,2,1,0:T(8,128)(2,1)}, bf16[32,2,8,128]{3,2,1,0:T(8,128)(2,1)S(1)}, u32[]{:S(2)}, u32[]{:S(2)}) collective-permute-start(bf16[32,2,8,128]{3,2,1,0:T(8,128)(2,1)} %bitcast.9), channel_id=1, source_target_pairs={{0,16},{4,8},{8,4},{12,28},{16,0},{20,24},{24,20},{28,12},{1,17},{... | collective-permute-start | bytes 393224 | tf_op jit(solution)/shard_map/ppermute | solution.py:422
  3.7 5.2 %collective-permute-start = (bf16[32,2,8,128]{3,2,1,0:T(8,128)(2,1)}, bf16[32,2,8,128]{3,2,1,0:T(8,128)(2,1)S(1)}, u32[]{:S(2)}, u32[]{:S(2)}) collective-permute-start(bf16[32,2,8,128]{3,2,1,0:T(8,128)(2,1)} %bitcast.10), channel_id=1, source_target_pairs={{0,4},{4,0},{8,12},{12,8},{16,20},{20,16},{24,28},{28,24},{1,5},{5... | collective-permute-start | bytes 393224 | tf_op jit(solution)/shard_map/ppermute | solution.py:422
  5.3 1.8 %copy-start.2 = (bf16[27,64,32]{1,2,0:T(8,128)(2,1)S(1)}, bf16[27,64,32]{1,2,0:T(8,128)(2,1)}, u32[]{:S(2)}) copy-start(bf16[27,64,32]{1,2,0:T(8,128)(2,1)} %param.5) | copy-start | bytes 331780
  5.3 1.8 %copy-start.3 = (bf16[1,32,2,8,128]{4,3,2,1,0:T(8,128)(2,1)S(1)}, bf16[1,32,2,8,128]{4,3,2,1,0:T(8,128)(2,1)}, u32[]{:S(2)}) copy-start(bf16[1,32,2,8,128]{4,3,2,1,0:T(8,128)(2,1)} %param.4) | copy-start | bytes 393220
  9.1 4.7 %collective-permute-start.2 = (bf16[6,32,256]{2,1,0:T(8,128)(2,1)S(1)}, bf16[6,32,256]{2,1,0:T(8,128)(2,1)S(1)}, u32[]{:S(2)}, u32[]{:S(2)}) collective-permute-start(bf16[6,32,256]{2,1,0:T(8,128)(2,1)S(1)} %get-tuple-element.32), channel_id=1, source_target_pairs={{0,16},{1,2},{2,1},{3,19},{16,0},{17,18},{18,17},{19,3},{4,20},{5,... | collective-permute-start | bytes 294920 | tf_op jit(solution)/shard_map/ppermute | solution.py:422
  10.6 3.2 %collective-permute-start.3 = (bf16[6,32,256]{2,1,0:T(8,128)(2,1)S(1)}, bf16[6,32,256]{2,1,0:T(8,128)(2,1)S(1)}, u32[]{:S(2)}, u32[]{:S(2)}) collective-permute-start(bf16[6,32,256]{2,1,0:T(8,128)(2,1)S(1)} %get-tuple-element.33), channel_id=1, source_target_pairs={{0,1},{1,0},{2,3},{3,2},{16,17},{17,16},{18,19},{19,18},{4,5},{5,4... | collective-permute-start | bytes 294920 | tf_op jit(solution)/shard_map/ppermute | solution.py:422
  16.0 1.6 %collective-permute-start.4 = (bf16[2,2,272,128]{3,2,1,0:T(8,128)(2,1)S(1)}, bf16[2,2,272,128]{3,2,1,0:T(8,128)(2,1)S(1)}, u32[]{:S(2)}, u32[]{:S(2)}) collective-permute-start(bf16[2,2,272,128]{3,2,1,0:T(8,128)(2,1)S(1)} %get-tuple-element.45), channel_id=1, source_target_pairs={{0,1},{1,0},{2,3},{3,2},{4,5},{5,4},{6,7},{7,6},{8,9},{9,8},{10,11... | collective-permute-start | bytes 835592 | tf_op jit(solution)/shard_map/ppermute | solution.py:430
  17.7 4.4 %collective-permute-start.5 = (bf16[272,128]{1,0:T(8,128)(2,1)S(1)}, bf16[272,128]{1,0:T(8,128)(2,1)S(1)}, u32[]{:S(2)}, u32[]{:S(2)}) collective-permute-start(bf16[272,128]{1,0:T(8,128)(2,1)S(1)} %get-tuple-element.47), channel_id=1, source_target_pairs={{0,16},{2,18},{16,0},{18,2},{1,17},{3,19},{17,1},{19,3},{4,20},{6,... | collective-permute-start | bytes 208904 | tf_op jit(solution)/shard_map/ppermute | solution.py:430
  19.2 5.1 %collective-permute-start.6 = (bf16[272,128]{1,0:T(8,128)(2,1)S(1)}, bf16[272,128]{1,0:T(8,128)(2,1)S(1)}, u32[]{:S(2)}, u32[]{:S(2)}) collective-permute-start(bf16[272,128]{1,0:T(8,128)(2,1)S(1)} %get-tuple-element.48), channel_id=1, source_target_pairs={{0,2},{2,0},{16,18},{18,16},{1,3},{3,1},{17,19},{19,17},{4,6},{6,4... | collective-permute-start | bytes 208904 | tf_op jit(solution)/shard_map/ppermute | solution.py:430
  20.1 5.2 %collective-permute-start.7 = (bf16[272,128]{1,0:T(8,128)(2,1)S(1)}, bf16[272,128]{1,0:T(8,128)(2,1)S(1)}, u32[]{:S(2)}, u32[]{:S(2)}) collective-permute-start(bf16[272,128]{1,0:T(8,128)(2,1)S(1)} %get-tuple-element.49), channel_id=1, source_target_pairs={{0,18},{2,16},{16,2},{18,0},{1,19},{3,17},{17,3},{19,1},{4,22},{6,... | collective-permute-start | bytes 208904 | tf_op jit(solution)/shard_map/ppermute | solution.py:430
  25.4 7.0 %collective-permute-start.10 = (bf16[272,128]{1,0:T(8,128)(2,1)S(1)}, bf16[272,128]{1,0:T(8,128)(2,1)S(1)}, u32[]{:S(2)}, u32[]{:S(2)}) collective-permute-start(bf16[272,128]{1,0:T(8,128)(2,1)S(1)} %shard_map.76.a_ref), channel_id=1, source_target_pairs={{0,12},{4,8},{8,4},{12,0},{1,13},{5,9},{9,5},{13,1},{2,14},{6,10},... | collective-permute-start | bytes 208904 | tf_op jit(solution)/shard_map/ppermute | solution.py:430
  28.1 5.6 %collective-permute-start.9 = (bf16[272,128]{1,0:T(8,128)(2,1)S(1)}, bf16[272,128]{1,0:T(8,128)(2,1)S(1)}, u32[]{:S(2)}, u32[]{:S(2)}) collective-permute-start(bf16[272,128]{1,0:T(8,128)(2,1)S(1)} %shard_map.76.a_ref), channel_id=1, source_target_pairs={{0,8},{4,12},{8,0},{12,4},{1,9},{5,13},{9,1},{13,5},{2,10},{6,14},... | collective-permute-start | bytes 208904 | tf_op jit(solution)/shard_map/ppermute | solution.py:430
  28.6 5.2 %collective-permute-start.8 = (bf16[272,128]{1,0:T(8,128)(2,1)S(1)}, bf16[272,128]{1,0:T(8,128)(2,1)S(1)}, u32[]{:S(2)}, u32[]{:S(2)}) collective-permute-start(bf16[272,128]{1,0:T(8,128)(2,1)S(1)} %shard_map.76.a_ref), channel_id=1, source_target_pairs={{0,4},{4,0},{8,12},{12,8},{1,5},{5,1},{9,13},{13,9},{2,6},{6,2},{1... | collective-permute-start | bytes 208904 | tf_op jit(solution)/shard_map/ppermute | solution.py:430
  33.8 4.4 %collective-permute-start.11 = (bf16[272,128]{1,0:T(8,128)(2,1)S(1)}, bf16[272,128]{1,0:T(8,128)(2,1)S(1)}, u32[]{:S(2)}, u32[]{:S(2)}) collective-permute-start(bf16[272,128]{1,0:T(8,128)(2,1)S(1)} %shard_map.77.own_ref), channel_id=1, source_target_pairs={{0,2},{2,0},{1,3},{3,1},{4,6},{6,4},{5,7},{7,5},{8,10},{10,8},{9,1... | collective-permute-start | bytes 208904 | tf_op jit(solution)/shard_map/ppermute | solution.py:430
  38.2 1.4 %collective-permute-start.12 = (bf16[2,272,128]{2,1,0:T(8,128)(2,1)S(1)}, bf16[2,272,128]{2,1,0:T(8,128)(2,1)S(1)}, u32[]{:S(2)}, u32[]{:S(2)}) collective-permute-start(bf16[2,272,128]{2,1,0:T(8,128)(2,1)S(1)} %shard_map.78.in_ref), channel_id=1, source_target_pairs={{0,1},{1,0},{2,3},{3,2},{4,5},{5,4},{6,7},{7,6},{8,9},{9,8},{10,11... | collective-permute-start | bytes 417800 | tf_op jit(solution)/shard_map/ppermute | solution.py:430

commit v16 on v13

--- a/solution.py
+++ b/solution.py
@@ -550,7 +550,7 @@
         [pltpu.VMEM((out * rows, width), F32)],
         flops=900_000_000,
     )
-    gots = [across(share, ("dep", bits)) for bits in (1, 2, 3)]
+    gots = [across(share, ("dep", bits)) for bits in (1, 3, 2)]
     (share,) = call(depth_kernel, [shape(block, BF)], [share, *gots, token])
     (own,) = call(order_kernel, [shape((halves, *block), BF)], [share, across(share, ("y", 1))])
     got = across(own, ("core", 1))

time: 40.8 us -> 40.9 us (level)
  transfers between devices with their start and end apart: 14 -> 14, of which waited for: 9 -> 10; matrix products, arithmetic and copies ran while one was open for 0% -> 0% of each run, Pallas kernels for 20% -> 20%
where the time goes in v16:
time: 40.9 us; the launch traced here: 40.7 us
  starting transfers between devices  15.9 us (39%)
  waiting for transfers between devices  12.2 us (30%)
  Pallas kernels  11.8 us (29%)
  between operations  0.79 us (2%)
    pallas_call x14, Pallas kernels, call(): pl.pallas_call(body, out_shape=outs, in_specs=[pl.BlockSpec(memory_space=...  11.8 us
    ppermute x10, waiting for transfers between devices, across(): lax.ppermute(x, axes, [(i, i ^ flip) for i in range(lax.axis_size(axes))])  10.7 us
    ppermute x10, starting transfers between devices, across(): lax.ppermute(x, axes, [(i, i ^ flip) for i in range(lax.axis_size(axes))])  9.54 us
    ppermute x4, starting transfers between devices, swapped(): return lax.ppermute(x, ('dp', *axes), list(enumerate(partner)))  6.36 us
    ppermute x4, waiting for transfers between devices, swapped(): return lax.ppermute(x, ('dp', *axes), list(enumerate(partner)))  1.58 us
  transfers between devices with their start and end apart: 14, of which 10 were waited for; matrix products, arithmetic and copies ran while one was open for 0% of the time, Pallas kernels for 20%

profile of v16, /device:TPU:0, one launch (start us, length us, event | category | flops | bytes accessed | tf_op | source)
XLA Modules:
  0.0 40.7 jit_solution(17498772454111146195)
XLA Ops:
  0.7 3.0 %collective-permute-start.1 = (bf16[32,2,8,128]{3,2,1,0:T(8,128)(2,1)}, bf16[32,2,8,128]{3,2,1,0:T(8,128)(2,1)S(1)}, u32[]{:S(2)}, u32[]{:S(2)}) collective-permute-start(bf16[32,2,8,128]{3,2,1,0:T(8,128)(2,1)} %bitcast.9), channel_id=1, source_target_pairs={{0,16},{4,8},{8,4},{12,28},{16,0},{20,24},{24,20},{28,12},{1,17},{... | collective-permute-start | bytes 393224 | tf_op jit(solution)/shard_map/ppermute | solution.py:412
  3.7 1.7 %collective-permute-start = (bf16[32,2,8,128]{3,2,1,0:T(8,128)(2,1)}, bf16[32,2,8,128]{3,2,1,0:T(8,128)(2,1)S(1)}, u32[]{:S(2)}, u32[]{:S(2)}) collective-permute-start(bf16[32,2,8,128]{3,2,1,0:T(8,128)(2,1)} %bitcast.10), channel_id=1, source_target_pairs={{0,4},{4,0},{8,12},{12,8},{16,20},{20,16},{24,28},{28,24},{1,5},{5... | collective-permute-start | bytes 393224 | tf_op jit(solution)/shard_map/ppermute | solution.py:412
  5.4 1.7 %shard_map.68 = (bf16[2,128,1024]{2,1,0:T(8,128)(2,1)S(1)}, f32[4,64,1280]{2,1,0:T(8,128)S(1)}) custom-call(bf16[128,2,8,128]{3,2,1,0:T(8,128)(2,1)S(1)} %bitcast.5, bf16[27,64,128]{2,1,0:T(8,128)(2,1)S(1)} %bitcast.6, bf16[128,256]{1,0:T(8,128)(2,1)S(1)} %shard_map.67.blank_ref), custom_call_target="tpu_custom_call" | custom-call | flops 1100000000 | bytes 2867200 | tf_op jit(solution)/shard_map/pallas_call | solution.py:18
  7.6 1.2 %collective-permute-done.one_ref = bf16[32,2,8,128]{3,2,1,0:T(8,128)(2,1)S(1)} collective-permute-done((bf16[32,2,8,128]{3,2,1,0:T(8,128)(2,1)}, bf16[32,2,8,128]{3,2,1,0:T(8,128)(2,1)S(1)}, u32[]{:S(2)}, u32[]{:S(2)}) %collective-permute-start) | collective-permute-done | bytes 131104 | tf_op jit(solution)/shard_map/ppermute | solution.py:412
  9.1 1.5 %collective-permute-start.2 = (bf16[6,32,256]{2,1,0:T(8,128)(2,1)S(1)}, bf16[6,32,256]{2,1,0:T(8,128)(2,1)S(1)}, u32[]{:S(2)}, u32[]{:S(2)}) collective-permute-start(bf16[6,32,256]{2,1,0:T(8,128)(2,1)S(1)} %get-tuple-element.32), channel_id=1, source_target_pairs={{0,16},{1,2},{2,1},{3,19},{16,0},{17,18},{18,17},{19,3},{4,20},{5,... | collective-permute-start | bytes 294920 | tf_op jit(solution)/shard_map/ppermute | solution.py:412
  10.8 2.6 %shard_map.71 = (bf16[4,64,768]{2,1,0:T(8,128)(2,1)S(1)}, f32[1152,192]{1,0:T(8,128)S(1)}, f32[192,288]{1,0:T(8,128)S(1)}) custom-call(bf16[6,32,1024]{2,1,0:T(8,128)(2,1)S(1)} %get-tuple-element.31.deep_ref, bf16[192,288]{1,0:T(8,128)(2,1)S(1)} %get-tuple-element.34.w1_ref, bf16[2,384,1024]{2,1,0:T(8,128)(2,1)S(1)} %get-tuple-element.36.moved_ref, ...), custom_call_target="tpu_custom_call" | custom-call | flops 1500000000 | bytes 4886528 | tf_op jit(solution)/shard_map/pallas_call | solution.py:18
  13.8 1.5 %shard_map.72 = (bf16[4,64,1280]{2,1,0:T(8,128)(2,1)S(1)}, f32[2,2,56,128]{3,2,1,0:T(8,128)S(1)}, f32[2,2,56,128]{3,2,1,0:T(8,128)S(1)}) custom-call(bf16[6,32,1024]{2,1,0:T(8,128)(2,1)S(1)} %get-tuple-element.31.deep_ref, bf16[6,32,256]{2,1,0:T(8,128)(2,1)S(1)} %collective-permute-done.2.two_ref, bf16[6,32,256]{2,1,0:T(8,128)(2,1)S(1)} %collective-permute-done.3.one_ref, ...), custom_call_target="tpu_custom_call" | custom-call | flops 1000000000 | bytes 3510272 | tf_op jit(solution)/shard_map/pallas_call | solution.py:18
  15.4 0.6 %shard_map.74 = (f32[2,2,216,128]{3,2,1,0:T(8,128)S(1)}, bf16[2,2,216,128]{3,2,1,0:T(8,128)(2,1)S(1)}) custom-call(bf16[4,64,1280]{2,1,0:T(8,128)(2,1)S(1)} %get-tuple-element.39.hidden_ref, bf16[2,384,1024]{2,1,0:T(8,128)(2,1)S(1)} %get-tuple-element.36.moved_ref, f32[1152,192]{1,0:T(8,128)S(1)} %get-tuple-element.43.second_ref), custom_call_target="tpu_custom_call" | custom-call | flops 4000000000 | bytes 3776512 | tf_op jit(solution)/shard_map/pallas_call | solution.py:18
  16.5 1.1 %collective-permute-done.4.refs_1_ = f32[2,2,56,128]{3,2,1,0:T(8,128)S(1)} collective-permute-done((f32[2,2,56,128]{3,2,1,0:T(8,128)S(1)}, f32[2,2,56,128]{3,2,1,0:T(8,128)S(1)}, u32[]{:S(2)}, u32[]{:S(2)}) %collective-permute-start.4) | collective-permute-done | bytes 114720 | tf_op jit(solution)/shard_map/ppermute | solution.py:420
  17.7 1.5 %collective-permute-start.6 = (bf16[272,128]{1,0:T(8,128)(2,1)S(1)}, bf16[272,128]{1,0:T(8,128)(2,1)S(1)}, u32[]{:S(2)}, u32[]{:S(2)}) collective-permute-start(bf16[272,128]{1,0:T(8,128)(2,1)S(1)} %get-tuple-element.47), channel_id=1, source_target_pairs={{0,16},{2,18},{16,0},{18,2},{1,17},{3,19},{17,1},{19,3},{4,20},{6,... | collective-permute-start | bytes 208904 | tf_op jit(solution)/shard_map/ppermute | solution.py:420
  19.2 0.9 %collective-permute-start.7 = (bf16[272,128]{1,0:T(8,128)(2,1)S(1)}, bf16[272,128]{1,0:T(8,128)(2,1)S(1)}, u32[]{:S(2)}, u32[]{:S(2)}) collective-permute-start(bf16[272,128]{1,0:T(8,128)(2,1)S(1)} %get-tuple-element.48), channel_id=1, source_target_pairs={{0,2},{2,0},{16,18},{18,16},{1,3},{3,1},{17,19},{19,17},{4,6},{6,4... | collective-permute-start | bytes 208904 | tf_op jit(solution)/shard_map/ppermute | solution.py:420
  20.1 1.1 %collective-permute-start.8 = (bf16[272,128]{1,0:T(8,128)(2,1)S(1)}, bf16[272,128]{1,0:T(8,128)(2,1)S(1)}, u32[]{:S(2)}, u32[]{:S(2)}) collective-permute-start(bf16[272,128]{1,0:T(8,128)(2,1)S(1)} %get-tuple-element.49), channel_id=1, source_target_pairs={{0,18},{2,16},{16,2},{18,0},{1,19},{3,17},{17,3},{19,1},{4,22},{6,... | collective-permute-start | bytes 208904 | tf_op jit(solution)/shard_map/ppermute | solution.py:420
  21.3 0.8 %collective-permute-done.6.refs_0_ = bf16[272,128]{1,0:T(8,128)(2,1)S(1)} collective-permute-done((bf16[272,128]{1,0:T(8,128)(2,1)S(1)}, bf16[272,128]{1,0:T(8,128)(2,1)S(1)}, u32[]{:S(2)}, u32[]{:S(2)}) %collective-permute-start.6) | collective-permute-done | bytes 69664 | tf_op jit(solution)/shard_map/ppermute | solution.py:420
  22.1 2.2 %collective-permute-done.7.refs_1_ = bf16[272,128]{1,0:T(8,128)(2,1)S(1)} collective-permute-done((bf16[272,128]{1,0:T(8,128)(2,1)S(1)}, bf16[272,128]{1,0:T(8,128)(2,1)S(1)}, u32[]{:S(2)}, u32[]{:S(2)}) %collective-permute-start.7) | collective-permute-done | bytes 69664 | tf_op jit(solution)/shard_map/ppermute | solution.py:420
  24.3 1.1 %collective-permute-done.8.refs_2_ = bf16[272,128]{1,0:T(8,128)(2,1)S(1)} collective-permute-done((bf16[272,128]{1,0:T(8,128)(2,1)S(1)}, bf16[272,128]{1,0:T(8,128)(2,1)S(1)}, u32[]{:S(2)}, u32[]{:S(2)}) %collective-permute-start.8) | collective-permute-done | bytes 69664 | tf_op jit(solution)/shard_map/ppermute | solution.py:420
  25.4 1.7 %collective-permute-start.11 = (bf16[272,128]{1,0:T(8,128)(2,1)S(1)}, bf16[272,128]{1,0:T(8,128)(2,1)S(1)}, u32[]{:S(2)}, u32[]{:S(2)}) collective-permute-start(bf16[272,128]{1,0:T(8,128)(2,1)S(1)} %shard_map.76.a_ref), channel_id=1, source_target_pairs={{0,8},{4,12},{8,0},{12,4},{1,9},{5,13},{9,1},{13,5},{2,10},{6,14},... | collective-permute-start | bytes 208904 | tf_op jit(solution)/shard_map/ppermute | solution.py:420
  27.1 2.5 %collective-permute-start.10 = (bf16[272,128]{1,0:T(8,128)(2,1)S(1)}, bf16[272,128]{1,0:T(8,128)(2,1)S(1)}, u32[]{:S(2)}, u32[]{:S(2)}) collective-permute-start(bf16[272,128]{1,0:T(8,128)(2,1)S(1)} %shard_map.76.a_ref), channel_id=1, source_target_pairs={{0,12},{4,8},{8,4},{12,0},{1,13},{5,9},{9,5},{13,1},{2,14},{6,10},... | collective-permute-start | bytes 208904 | tf_op jit(solution)/shard_map/ppermute | solution.py:420
  29.6 2.5 %shard_map.73 = (bf16[128,2,8,128]{3,2,1,0:T(8,128)(2,1)}, f32[8,128]{1,0:T(8,128)S(1)}) custom-call(bf16[4,64,1280]{2,1,0:T(8,128)(2,1)S(1)} %get-tuple-element.39.hidden_ref, bf16[27,64,128]{2,1,0:T(8,128)(2,1)S(1)} %bitcast.7), custom_call_target="tpu_custom_call" | custom-call | flops 900000000 | bytes 1626112 | tf_op jit(solution)/shard_map/pallas_call | solution.py:18
  32.1 1.1 %collective-permute-done.11.d_ref = bf16[272,128]{1,0:T(8,128)(2,1)S(1)} collective-permute-done((bf16[272,128]{1,0:T(8,128)(2,1)S(1)}, bf16[272,128]{1,0:T(8,128)(2,1)S(1)}, u32[]{:S(2)}, u32[]{:S(2)}) %collective-permute-start.11) | collective-permute-done | bytes 69664 | tf_op jit(solution)/shard_map/ppermute | solution.py:420
  33.2 0.7 %collective-permute-done.9.b_ref = bf16[272,128]{1,0:T(8,128)(2,1)S(1)} collective-permute-done((bf16[272,128]{1,0:T(8,128)(2,1)S(1)}, bf16[272,128]{1,0:T(8,128)(2,1)S(1)}, u32[]{:S(2)}, u32[]{:S(2)}) %collective-permute-start.9) | collective-permute-done | bytes 69664 | tf_op jit(solution)/shard_map/ppermute | solution.py:420
  34.0 1.2 %collective-permute-start.12 = (bf16[272,128]{1,0:T(8,128)(2,1)S(1)}, bf16[272,128]{1,0:T(8,128)(2,1)S(1)}, u32[]{:S(2)}, u32[]{:S(2)}) collective-permute-start(bf16[272,128]{1,0:T(8,128)(2,1)S(1)} %shard_map.77.own_ref), channel_id=1, source_target_pairs={{0,2},{2,0},{1,3},{3,1},{4,6},{6,4},{5,7},{7,5},{8,10},{10,8},{9,1... | collective-permute-start | bytes 208904 | tf_op jit(solution)/shard_map/ppermute | solution.py:420
  35.2 3.2 %collective-permute-done.12.got_ref = bf16[272,128]{1,0:T(8,128)(2,1)S(1)} collective-permute-done((bf16[272,128]{1,0:T(8,128)(2,1)S(1)}, bf16[272,128]{1,0:T(8,128)(2,1)S(1)}, u32[]{:S(2)}, u32[]{:S(2)}) %collective-permute-start.12) | collective-permute-done | bytes 69664 | tf_op jit(solution)/shard_map/ppermute | solution.py:420
  38.5 0.9 %shard_map.79 = (f32[27,32,32]{2,1,0:T(8,128)}, f32[27,64,64]{2,1,0:T(8,128)}) custom-call(bf16[2,272,128]{2,1,0:T(8,128)(2,1)S(1)} %shard_map.78.in_ref), custom_call_target="tpu_custom_call" | custom-call | bytes 692224 | tf_op jit(solution)/shard_map/pallas_call | solution.py:18
  39.8 0.9 %shard_map.80 = (f32[27,32,32]{2,1,0:T(8,128)}, f32[27,64,64]{2,1,0:T(8,128)}) custom-call(bf16[2,272,128]{2,1,0:T(8,128)(2,1)S(1)} %collective-permute-done.13.in_ref, f32[27,32,32]{2,1,0:T(8,128)} %get-tuple-element.51.refs_0_, f32[27,64,64]{2,1,0:T(8,128)} %get-tuple-element.52.refs_1_), custom_call_target="tpu_custom_call", output_to_operand_aliasing={{0}: (1, {}), {1}: (2, {})} | custom-call | bytes 1245184 | tf_op jit(solution)/shard_map/pallas_call | solution.py:18
  (26 shorter events, 2.6 us)
Async XLA Ops:
  0.6 4.7 %copy-start = (bf16[1,128,2,8,128]{4,3,2,1,0:T(8,128)(2,1)S(1)}, bf16[1,128,2,8,128]{4,3,2,1,0:T(8,128)(2,1)}, u32[]{:S(2)}) copy-start(bf16[1,128,2,8,128]{4,3,2,1,0:T(8,128)(2,1)} %param.7) | copy-start | bytes 1572868
  0.6 4.7 %copy-start.1 = (bf16[27,128,64]{1,2,0:T(8,128)(2,1)S(1)}, bf16[27,128,64]{1,2,0:T(8,128)(2,1)}, u32[]{:S(2)}) copy-start(bf16[27,128,64]{1,2,0:T(8,128)(2,1)} %param.6) | copy-start | bytes 1327108
  0.7 7.0 %collective-permute-start.1 = (bf16[32,2,8,128]{3,2,1,0:T(8,128)(2,1)}, bf16[32,2,8,128]{3,2,1,0:T(8,128)(2,1)S(1)}, u32[]{:S(2)}, u32[]{:S(2)}) collective-permute-start(bf16[32,2,8,128]{3,2,1,0:T(8,128)(2,1)} %bitcast.9), channel_id=1, source_target_pairs={{0,16},{4,8},{8,4},{12,28},{16,0},{20,24},{24,20},{28,12},{1,17},{... | collective-permute-start | bytes 393224 | tf_op jit(solution)/shard_map/ppermute | solution.py:412
  3.7 5.2 %collective-permute-start = (bf16[32,2,8,128]{3,2,1,0:T(8,128)(2,1)}, bf16[32,2,8,128]{3,2,1,0:T(8,128)(2,1)S(1)}, u32[]{:S(2)}, u32[]{:S(2)}) collective-permute-start(bf16[32,2,8,128]{3,2,1,0:T(8,128)(2,1)} %bitcast.10), channel_id=1, source_target_pairs={{0,4},{4,0},{8,12},{12,8},{16,20},{20,16},{24,28},{28,24},{1,5},{5... | collective-permute-start | bytes 393224 | tf_op jit(solution)/shard_map/ppermute | solution.py:412
  5.3 1.8 %copy-start.2 = (bf16[27,64,32]{1,2,0:T(8,128)(2,1)S(1)}, bf16[27,64,32]{1,2,0:T(8,128)(2,1)}, u32[]{:S(2)}) copy-start(bf16[27,64,32]{1,2,0:T(8,128)(2,1)} %param.5) | copy-start | bytes 331780
  5.3 1.8 %copy-start.3 = (bf16[1,32,2,8,128]{4,3,2,1,0:T(8,128)(2,1)S(1)}, bf16[1,32,2,8,128]{4,3,2,1,0:T(8,128)(2,1)}, u32[]{:S(2)}) copy-start(bf16[1,32,2,8,128]{4,3,2,1,0:T(8,128)(2,1)} %param.4) | copy-start | bytes 393220
  9.1 4.7 %collective-permute-start.2 = (bf16[6,32,256]{2,1,0:T(8,128)(2,1)S(1)}, bf16[6,32,256]{2,1,0:T(8,128)(2,1)S(1)}, u32[]{:S(2)}, u32[]{:S(2)}) collective-permute-start(bf16[6,32,256]{2,1,0:T(8,128)(2,1)S(1)} %get-tuple-element.32), channel_id=1, source_target_pairs={{0,16},{1,2},{2,1},{3,19},{16,0},{17,18},{18,17},{19,3},{4,20},{5,... | collective-permute-start | bytes 294920 | tf_op jit(solution)/shard_map/ppermute | solution.py:412
  10.6 3.2 %collective-permute-start.3 = (bf16[6,32,256]{2,1,0:T(8,128)(2,1)S(1)}, bf16[6,32,256]{2,1,0:T(8,128)(2,1)S(1)}, u32[]{:S(2)}, u32[]{:S(2)}) collective-permute-start(bf16[6,32,256]{2,1,0:T(8,128)(2,1)S(1)} %get-tuple-element.33), channel_id=1, source_target_pairs={{0,1},{1,0},{2,3},{3,2},{16,17},{17,16},{18,19},{19,18},{4,5},{5,4... | collective-permute-start | bytes 294920 | tf_op jit(solution)/shard_map/ppermute | solution.py:412
  15.9 1.7 %collective-permute-start.5 = (bf16[2,2,216,128]{3,2,1,0:T(8,128)(2,1)S(1)}, bf16[2,2,216,128]{3,2,1,0:T(8,128)(2,1)S(1)}, u32[]{:S(2)}, u32[]{:S(2)}) collective-permute-start(bf16[2,2,216,128]{3,2,1,0:T(8,128)(2,1)S(1)} %get-tuple-element.45), channel_id=1, source_target_pairs={{0,1},{1,0},{2,3},{3,2},{4,5},{5,4},{6,7},{7,6},{8,9},{9,8},{10,11... | collective-permute-start | bytes 663560 | tf_op jit(solution)/shard_map/ppermute | solution.py:420
  16.0 1.6 %collective-permute-start.4 = (f32[2,2,56,128]{3,2,1,0:T(8,128)S(1)}, f32[2,2,56,128]{3,2,1,0:T(8,128)S(1)}, u32[]{:S(2)}, u32[]{:S(2)}) collective-permute-start(f32[2,2,56,128]{3,2,1,0:T(8,128)S(1)} %get-tuple-element.42), channel_id=1, source_target_pairs={{0,1},{1,0},{2,3},{3,2},{4,5},{5,4},{6,7},{7,6},{8,9},{9,8},{10,11... | collective-permute-start | bytes 344072 | tf_op jit(solution)/shard_map/ppermute | solution.py:420
  17.7 4.4 %collective-permute-start.6 = (bf16[272,128]{1,0:T(8,128)(2,1)S(1)}, bf16[272,128]{1,0:T(8,128)(2,1)S(1)}, u32[]{:S(2)}, u32[]{:S(2)}) collective-permute-start(bf16[272,128]{1,0:T(8,128)(2,1)S(1)} %get-tuple-element.47), channel_id=1, source_target_pairs={{0,16},{2,18},{16,0},{18,2},{1,17},{3,19},{17,1},{19,3},{4,20},{6,... | collective-permute-start | bytes 208904 | tf_op jit(solution)/shard_map/ppermute | solution.py:420
  19.2 5.1 %collective-permute-start.7 = (bf16[272,128]{1,0:T(8,128)(2,1)S(1)}, bf16[272,128]{1,0:T(8,128)(2,1)S(1)}, u32[]{:S(2)}, u32[]{:S(2)}) collective-permute-start(bf16[272,128]{1,0:T(8,128)(2,1)S(1)} %get-tuple-element.48), channel_id=1, source_target_pairs={{0,2},{2,0},{16,18},{18,16},{1,3},{3,1},{17,19},{19,17},{4,6},{6,4... | collective-permute-start | bytes 208904 | tf_op jit(solution)/shard_map/ppermute | solution.py:420
  20.1 5.2 %collective-permute-start.8 = (bf16[272,128]{1,0:T(8,128)(2,1)S(1)}, bf16[272,128]{1,0:T(8,128)(2,1)S(1)}, u32[]{:S(2)}, u32[]{:S(2)}) collective-permute-start(bf16[272,128]{1,0:T(8,128)(2,1)S(1)} %get-tuple-element.49), channel_id=1, source_target_pairs={{0,18},{2,16},{16,2},{18,0},{1,19},{3,17},{17,3},{19,1},{4,22},{6,... | collective-permute-start | bytes 208904 | tf_op jit(solution)/shard_map/ppermute | solution.py:420
  25.4 7.8 %collective-permute-start.11 = (bf16[272,128]{1,0:T(8,128)(2,1)S(1)}, bf16[272,128]{1,0:T(8,128)(2,1)S(1)}, u32[]{:S(2)}, u32[]{:S(2)}) collective-permute-start(bf16[272,128]{1,0:T(8,128)(2,1)S(1)} %shard_map.76.a_ref), channel_id=1, source_target_pairs={{0,8},{4,12},{8,0},{12,4},{1,9},{5,13},{9,1},{13,5},{2,10},{6,14},... | collective-permute-start | bytes 208904 | tf_op jit(solution)/shard_map/ppermute | solution.py:420
  27.1 6.1 %collective-permute-start.10 = (bf16[272,128]{1,0:T(8,128)(2,1)S(1)}, bf16[272,128]{1,0:T(8,128)(2,1)S(1)}, u32[]{:S(2)}, u32[]{:S(2)}) collective-permute-start(bf16[272,128]{1,0:T(8,128)(2,1)S(1)} %shard_map.76.a_ref), channel_id=1, source_target_pairs={{0,12},{4,8},{8,4},{12,0},{1,13},{5,9},{9,5},{13,1},{2,14},{6,10},... | collective-permute-start | bytes 208904 | tf_op jit(solution)/shard_map/ppermute | solution.py:420
  29.6 4.4 %collective-permute-start.9 = (bf16[272,128]{1,0:T(8,128)(2,1)S(1)}, bf16[272,128]{1,0:T(8,128)(2,1)S(1)}, u32[]{:S(2)}, u32[]{:S(2)}) collective-permute-start(bf16[272,128]{1,0:T(8,128)(2,1)S(1)} %shard_map.76.a_ref), channel_id=1, source_target_pairs={{0,4},{4,0},{8,12},{12,8},{1,5},{5,1},{9,13},{13,9},{2,6},{6,2},{1... | collective-permute-start | bytes 208904 | tf_op jit(solution)/shard_map/ppermute | solution.py:420
  34.0 4.4 %collective-permute-start.12 = (bf16[272,128]{1,0:T(8,128)(2,1)S(1)}, bf16[272,128]{1,0:T(8,128)(2,1)S(1)}, u32[]{:S(2)}, u32[]{:S(2)}) collective-permute-start(bf16[272,128]{1,0:T(8,128)(2,1)S(1)} %shard_map.77.own_ref), channel_id=1, source_target_pairs={{0,2},{2,0},{1,3},{3,1},{4,6},{6,4},{5,7},{7,5},{8,10},{10,8},{9,1... | collective-permute-start | bytes 208904 | tf_op jit(solution)/shard_map/ppermute | solution.py:420
  38.4 1.4 %collective-permute-start.13 = (bf16[2,272,128]{2,1,0:T(8,128)(2,1)S(1)}, bf16[2,272,128]{2,1,0:T(8,128)(2,1)S(1)}, u32[]{:S(2)}, u32[]{:S(2)}) collective-permute-start(bf16[2,272,128]{2,1,0:T(8,128)(2,1)S(1)} %shard_map.78.in_ref), channel_id=1, source_target_pairs={{0,1},{1,0},{2,3},{3,2},{4,5},{5,4},{6,7},{7,6},{8,9},{9,8},{10,11... | collective-permute-start | bytes 417800 | tf_op jit(solution)/shard_map/ppermute | solution.py:420

commit v17 on v15

--- a/solution.py
+++ b/solution.py
@@ -60,7 +60,14 @@
     out_ref[...] = jnp.zeros(out_ref.shape, BF)
 
 
-def spread_kernel(cot_ref, k2_ref, blank_ref, cot_rows_ref, back_ref, scratch):
+def own_kernel(vol_ref, _, out_ref, scratch):
+    def store(d, h, row):
+        out_ref[d, :, h * LANES : (h + 1) * LANES] = row.astype(BF)
+
+    by_rows(vol_ref, scratch, store)
+
+
+def spread_kernel(cot_ref, k2_ref, blank_ref, _, cot_rows_ref, back_ref, scratch):
     out, depth, height, _ = cot_ref.shape
     rows = [[None] * height for _ in range(depth)]
 
@@ -96,11 +103,7 @@
     return stacked.astype(F32).T.astype(BF)
 
 
-def arrange_kernel(cot_rows_ref, k1_ref, vol_ref, moved_ref, w1_ref, w1_last_ref, own_ref, scratch):
-    def store(d, h, row):
-        own_ref[d, :, h * LANES : (h + 1) * LANES] = row.astype(BF)
-
-    by_rows(vol_ref, scratch, store)
+def arrange_kernel(cot_rows_ref, k1_ref, _, moved_ref, w1_ref, w1_last_ref):
     depth, out, cells = cot_rows_ref.shape
     for d in range(depth):
         for h in range(0, cells, LANES):
@@ -125,20 +128,45 @@
     return before, after
 
 
-def rim_kernel(own_ref, one_ref, two_ref, deep_ref, send_one_ref, send_two_ref, scratch):
+def extend(deep_ref, one_ref, two_ref, scratch):
+    depth = deep_ref.shape[0] // 3
+    for at, part in zip((0, 2 * depth), sides("dep", one_ref[...], two_ref[...]), strict=True):
+
+        def store(d, h, row, at=at):
+            deep_ref[at + d, :, h * LANES : (h + 1) * LANES] = row.astype(BF)
+
+        by_rows(part, scratch, store)
+
+
+def edges(deep_ref, n):
+    cells = deep_ref.shape[2]
+    return deep_ref[:, :, :n], deep_ref[:, :, cells - n :]
+
+
+def inside():
+    hgt, hgts = lax.axis_index(HGT), lax.axis_size(HGT)
+    return jnp.logical_and(hgt > 0, hgt < hgts - 1)
+
+
+def early_rim_kernel(own_ref, one_ref, two_ref, _, deep_ref, send_ref, scratch):
     depth = own_ref.shape[0]
     deep_ref[depth : 2 * depth] = own_ref[...]
-    for at, part in zip((0, 2 * depth), sides("dep", one_ref[...], two_ref[...]), strict=True):
-
-        def store(d, h, row, at=at):
-            deep_ref[at + d, :, h * LANES : (h + 1) * LANES] = row.astype(BF)
-
-        by_rows(part, scratch, store)
-    n, cells = send_one_ref.shape[2], deep_ref.shape[2]
-    first, last = deep_ref[:, :, :n], deep_ref[:, :, cells - n :]
-    is_odd = odd(HGT)
-    send_one_ref[...] = jnp.where(is_odd, first, last)
-    send_two_ref[...] = jnp.where(is_odd, last, first)
+    extend(deep_ref, one_ref, two_ref, scratch)
+    first, last = edges(deep_ref, send_ref.shape[2])
+    send_ref[...] = jnp.where(odd(HGT), last, first)
+
+
+def late_rim_kernel(early_ref, one_ref, two_ref, _, deep_ref, send_ref):
+    deep_ref[...] = early_ref[...]
+
+    depth = one_ref.shape[0]
+
+    @pl.when(jnp.logical_not(inside()))
+    def _():
+        deep_ref[:depth], deep_ref[2 * depth :] = sides("dep", one_ref[...], two_ref[...])
+
+    first, last = edges(deep_ref, send_ref.shape[2])
+    send_ref[...] = jnp.where(odd(HGT), first, last)
 
 
 def widened(deep_ref, one_ref, two_ref):
@@ -422,6 +450,19 @@
     return lax.ppermute(x, ("dp", *axes), list(enumerate(partner)))
 
 
+def along_depth(x, first, inner):
+    parts, deps, hgts = (lax.axis_size(axis) for axis in ("dp", "dep", HGT))
+    partner = list(range(parts * deps * hgts))
+    for i in partner:
+        part, at = divmod(i, deps * hgts)
+        z, h = divmod(at, hgts)
+        if (0 < h < hgts - 1) == inner and first <= z < deps - (deps - first) % 2:
+            partner[i] = (part * deps + (z - first ^ 1) + first) * hgts + h
+        elif parts % 2 == 0:
+            partner[i] = ((part ^ 1) * deps + z) * hgts + h
+    return lax.ppermute(x, ("dp", "dep", *HGT), list(enumerate(partner)))
+
+
 def across(x, *moves):
     axes = tuple(axis for axis, _ in moves)
     flip = 0
@@ -469,37 +510,39 @@
     k1, k2 = jnp.swapaxes(kernel_first, 1, 2), jnp.swapaxes(kernel_second, 1, 2)
     rows = depth * height
 
-    one, two = swapped(volume[0], "dep", 0), swapped(volume[0], "dep", 1)
+    early = [along_depth(volume[0], first, True) for first in range(2)]
     (blank,) = call(blank_kernel, [shape((out, 2 * width), BF)], [], flops=3_000_000_000)
+    (vol,) = call(
+        own_kernel,
+        [shape((depth, inner, cells), BF)],
+        [volume[0], blank],
+        [pltpu.VMEM((inner * rows, width), F32)],
+    )
+    late = [along_depth(vol, first, False) for first in range(2)]
     cot_rows, back = call(
         spread_kernel,
         [
             shape((depth, out, cells), BF),
             shape((depth + 2, mid, cells + 2 * width), F32),
         ],
-        [cotangent[0], k2, blank],
+        [cotangent[0], k2, blank, vol],
         [pltpu.VMEM((out * rows, width), F32)],
-        flops=1_100_000_000,
-    )
-    moved, w1, w1_last, vol = call(
+        flops=300_000_000,
+    )
+    extended = shape((3 * depth, inner, cells), BF)
+    edge = shape((3 * depth, inner, 2 * width), BF)
+    scratch = [pltpu.VMEM((inner * rows, width), F32)]
+    deep, two = call(early_rim_kernel, [extended, edge], [vol, *early, cot_rows], scratch)
+    moved, w1, w1_last = call(
         arrange_kernel,
-        [
-            shape((depth, 3 * out, cells), BF),
-            shape((3 * mid, 8 * inner), BF),
-            shape((mid, 3 * inner), BF),
-            shape((depth, inner, cells), BF),
-        ],
-        [cot_rows, k1, volume[0]],
-        [pltpu.VMEM((inner * rows, width), F32)],
+        [shape((depth, 3 * out, cells), BF), shape((3 * mid, 8 * inner), BF), shape((mid, 3 * inner), BF)],
+        [cot_rows, k1, deep],
         flops=500_000_000,
     )
-    deep, one, two = call(
-        rim_kernel,
-        [shape((3 * depth, inner, cells), BF)] + [shape((3 * depth, inner, 2 * width), BF)] * 2,
-        [vol, one, two],
-        [pltpu.VMEM((inner * rows, width), F32)],
-    )
-    one, two = swapped(one, HGT, 0), swapped(two, HGT, 1)
+    two = swapped(two, HGT, 1)
+    deep, one = call(late_rim_kernel, [extended, edge], [deep, *late, w1])
+    one = swapped(one, HGT, 0)
+
     size = mid // parts
     direct = parts == 2 and size % 16 == 0
     halves = lax.axis_size("y")

time: 40.7 us -> 44.9 us (1.10)
  starting transfers between devices: 15.7 us -> 18.7 us
  waiting for transfers between devices: 12.4 us -> 13.5 us
    ppermute x0 -> x4, starting transfers between devices: none -> 6.76 us  [along_depth(): return lax.ppermute(x, ('dp', 'dep', *HGT), list(enumerate(partner)))]
    ppermute x4 -> x2, starting transfers between devices: 6.36 us -> 1.97 us  [swapped(): return lax.ppermute(x, ('dp', *axes), list(enumerate(partner)))]
    ppermute x9, waiting for transfers between devices: 10.7 us -> 12.5 us  [across(): lax.ppermute(x, axes, [(i, i ^ flip) for i in range(lax.axis_size(axes))])]
    ppermute x4 -> x2, waiting for transfers between devices: 1.73 us -> 0.01 us  [swapped(): return lax.ppermute(x, ('dp', *axes), list(enumerate(partner)))]
    ppermute x0 -> x4, waiting for transfers between devices: none -> 1.04 us  [along_depth(): return lax.ppermute(x, ('dp', 'dep', *HGT), list(enumerate(partner)))]
    ppermute x9, starting transfers between devices: 9.3 us -> 9.93 us  [across(): lax.ppermute(x, axes, [(i, i ^ flip) for i in range(lax.axis_size(axes))])]
    pallas_call x14 -> x16, Pallas kernels: 11.7 us -> 11.8 us  [call(): pl.pallas_call(body, out_shape=outs, in_specs=[pl.BlockSpec(memory_space=...]
  transfers between devices with their start and end apart: 13 -> 15, of which waited for: 9 -> 10; matrix products, arithmetic and copies ran while one was open for 0% -> 0% of each run, Pallas kernels for 20% -> 19%
where the time goes in v17:
time: 44.9 us; the launch traced here: 44.7 us
  starting transfers between devices  18.7 us (42%)
  waiting for transfers between devices  13.5 us (30%)
  Pallas kernels  11.8 us (26%)
  between operations  0.78 us (2%)
    ppermute x9, waiting for transfers between devices, across(): lax.ppermute(x, axes, [(i, i ^ flip) for i in range(lax.axis_size(axes))])  12.5 us
    pallas_call x16, Pallas kernels, call(): pl.pallas_call(body, out_shape=outs, in_specs=[pl.BlockSpec(memory_space=...  11.8 us
    ppermute x9, starting transfers between devices, across(): lax.ppermute(x, axes, [(i, i ^ flip) for i in range(lax.axis_size(axes))])  9.93 us
    ppermute x4, starting transfers between devices, along_depth(): return lax.ppermute(x, ('dp', 'dep', *HGT), list(enumerate(partner)))  6.76 us
    ppermute x2, starting transfers between devices, swapped(): return lax.ppermute(x, ('dp', *axes), list(enumerate(partner)))  1.97 us
    ppermute x4, waiting for transfers between devices, along_depth(): return lax.ppermute(x, ('dp', 'dep', *HGT), list(enumerate(partner)))  1.04 us
  transfers between devices with their start and end apart: 15, of which 10 were waited for; matrix products, arithmetic and copies ran while one was open for 0% of the time, Pallas kernels for 19%

profile of v17, /device:TPU:0, one launch (start us, length us, event | category | flops | bytes accessed | tf_op | source)
XLA Modules:
  0.0 44.7 jit_solution(292023551310369277)
XLA Ops:
  0.7 3.0 %collective-permute-start.1 = (bf16[32,2,8,128]{3,2,1,0:T(8,128)(2,1)}, bf16[32,2,8,128]{3,2,1,0:T(8,128)(2,1)S(1)}, u32[]{:S(2)}, u32[]{:S(2)}) collective-permute-start(bf16[32,2,8,128]{3,2,1,0:T(8,128)(2,1)} %bitcast.8), channel_id=1, source_target_pairs={{0,16},{1,17},{2,18},{3,19},{4,20},{5,9},{6,10},{7,23},{8,24},{9,5... | collective-permute-start | bytes 393224 | tf_op jit(solution)/shard_map/ppermute | solution.py:463
  3.9 2.0 %collective-permute-start.3 = (bf16[2,32,1024]{2,1,0:T(8,128)(2,1)S(1)}, bf16[2,32,1024]{2,1,0:T(8,128)(2,1)S(1)}, u32[]{:S(2)}, u32[]{:S(2)}) collective-permute-start(bf16[2,32,1024]{2,1,0:T(8,128)(2,1)S(1)} %shard_map.68._.own_ref), channel_id=1, source_target_pairs={{0,16},{1,17},{2,18},{3,19},{4,8},{5,21},{6,22},{7,11},{8,4},{9,25... | collective-permute-start | bytes 393224 | tf_op jit(solution)/shard_map/ppermute | solution.py:463
  5.9 1.7 %collective-permute-start.2 = (bf16[2,32,1024]{2,1,0:T(8,128)(2,1)S(1)}, bf16[2,32,1024]{2,1,0:T(8,128)(2,1)S(1)}, u32[]{:S(2)}, u32[]{:S(2)}) collective-permute-start(bf16[2,32,1024]{2,1,0:T(8,128)(2,1)S(1)} %shard_map.68._.own_ref), channel_id=1, source_target_pairs={{0,4},{1,17},{2,18},{3,7},{4,0},{5,21},{6,22},{7,3},{8,12},{9,25},... | collective-permute-start | bytes 393224 | tf_op jit(solution)/shard_map/ppermute | solution.py:463
  7.6 1.7 %shard_map.69 = (bf16[2,128,1024]{2,1,0:T(8,128)(2,1)S(1)}, f32[4,64,1280]{2,1,0:T(8,128)S(1)}) custom-call(bf16[128,2,8,128]{3,2,1,0:T(8,128)(2,1)S(1)} %bitcast.5, bf16[27,64,128]{2,1,0:T(8,128)(2,1)S(1)} %bitcast.6, bf16[128,256]{1,0:T(8,128)(2,1)S(1)} %shard_map.67._.blank_ref, bf16[2,32,1024]{2,1,0:T(8,128)(2,1)S(1)} %shard_map.68._.own_ref), custom_call_target="tpu_custom_call" | custom-call | flops 300000000 | bytes 2998272 | tf_op jit(solution)/shard_map/pallas_call | solution.py:18
  9.3 0.9 %collective-permute-done.one_ref = bf16[32,2,8,128]{3,2,1,0:T(8,128)(2,1)S(1)} collective-permute-done((bf16[32,2,8,128]{3,2,1,0:T(8,128)(2,1)}, bf16[32,2,8,128]{3,2,1,0:T(8,128)(2,1)S(1)}, u32[]{:S(2)}, u32[]{:S(2)}) %collective-permute-start) | collective-permute-done | bytes 131104 | tf_op jit(solution)/shard_map/ppermute | solution.py:463
  10.6 1.9 %collective-permute-start.4 = (bf16[6,32,256]{2,1,0:T(8,128)(2,1)S(1)}, bf16[6,32,256]{2,1,0:T(8,128)(2,1)S(1)}, u32[]{:S(2)}, u32[]{:S(2)}) collective-permute-start(bf16[6,32,256]{2,1,0:T(8,128)(2,1)S(1)} %get-tuple-element.33), channel_id=1, source_target_pairs={{0,16},{1,2},{2,1},{3,19},{16,0},{17,18},{18,17},{19,3},{4,20},{5,... | collective-permute-start | bytes 294920 | tf_op jit(solution)/shard_map/ppermute | solution.py:450
  12.4 0.5 %shard_map.71 = (bf16[2,384,1024]{2,1,0:T(8,128)(2,1)S(1)}, bf16[192,256]{1,0:T(8,128)(2,1)S(1)}, bf16[64,96]{1,0:T(8,128)(2,1)S(1)}) custom-call(bf16[2,128,1024]{2,1,0:T(8,128)(2,1)S(1)} %get-tuple-element.29._.cot_rows_ref, bf16[27,32,64]{2,1,0:T(8,128)(2,1)S(1)} %bitcast.11, bf16[6,32,1024]{2,1,0:T(8,128)(2,1)S(1)} %get-tuple-element.30._.early_ref), custom_call_target="tpu_custom_call" | custom-call | flops 500000000 | bytes 2711552 | tf_op jit(solution)/shard_map/pallas_call | solution.py:18
  13.2 2.4 %shard_map.73 = (bf16[4,64,768]{2,1,0:T(8,128)(2,1)S(1)}, f32[1152,192]{1,0:T(8,128)S(1)}, f32[288,192]{1,0:T(8,128)S(1)}) custom-call(bf16[6,32,1024]{2,1,0:T(8,128)(2,1)S(1)} %get-tuple-element.32.deep_ref, bf16[192,256]{1,0:T(8,128)(2,1)S(1)} %get-tuple-element.31._.w1_ref, bf16[64,96]{1,0:T(8,128)(2,1)S(1)} %get-tuple-element.35.w1_last_ref, ...), custom_call_target="tpu_custom_call" | custom-call | flops 1500000000 | bytes 4886528 | tf_op jit(solution)/shard_map/pallas_call | solution.py:18
  15.6 1.6 %shard_map.74 = (bf16[4,64,1280]{2,1,0:T(8,128)(2,1)S(1)}, f32[7,64,128]{2,1,0:T(8,128)S(1)}) custom-call(bf16[6,32,1024]{2,1,0:T(8,128)(2,1)S(1)} %get-tuple-element.32.deep_ref, bf16[6,32,256]{2,1,0:T(8,128)(2,1)S(1)} %collective-permute-done.4.two_ref, bf16[6,32,256]{2,1,0:T(8,128)(2,1)S(1)} %collective-permute-done.5.one_ref, ...), custom_call_target="tpu_custom_call" | custom-call | flops 1000000000 | bytes 3510272 | tf_op jit(solution)/shard_map/pallas_call | solution.py:18
  17.2 0.6 %shard_map.76 = (f32[2,2,272,128]{3,2,1,0:T(8,128)S(1)}, bf16[2,2,272,128]{3,2,1,0:T(8,128)(2,1)S(1)}) custom-call(bf16[4,64,1280]{2,1,0:T(8,128)(2,1)S(1)} %get-tuple-element.40.hidden_ref, bf16[2,384,1024]{2,1,0:T(8,128)(2,1)S(1)} %get-tuple-element.37.moved_ref, f32[1152,192]{1,0:T(8,128)S(1)} %get-tuple-element.42.second_ref, ...), custom_call_target="tpu_custom_call" | custom-call | flops 4000000000 | bytes 4177920 | tf_op jit(solution)/shard_map/pallas_call | solution.py:18
  17.7 0.5 %collective-permute-start.6 = (bf16[2,2,272,128]{3,2,1,0:T(8,128)(2,1)S(1)}, bf16[2,2,272,128]{3,2,1,0:T(8,128)(2,1)S(1)}, u32[]{:S(2)}, u32[]{:S(2)}) collective-permute-start(bf16[2,2,272,128]{3,2,1,0:T(8,128)(2,1)S(1)} %get-tuple-element.45), channel_id=1, source_target_pairs={{0,1},{1,0},{2,3},{3,2},{4,5},{5,4},{6,7},{7,6},{8,9},{9,8},{10,11... | collective-permute-start | bytes 835592 | tf_op jit(solution)/shard_map/ppermute | solution.py:471
  18.3 1.2 %collective-permute-done.6.got_ref = bf16[2,2,272,128]{3,2,1,0:T(8,128)(2,1)S(1)} collective-permute-done((bf16[2,2,272,128]{3,2,1,0:T(8,128)(2,1)S(1)}, bf16[2,2,272,128]{3,2,1,0:T(8,128)(2,1)S(1)}, u32[]{:S(2)}, u32[]{:S(2)}) %collective-permute-start.6) | collective-permute-done | bytes 278560 | tf_op jit(solution)/shard_map/ppermute | solution.py:471
  19.5 1.8 %collective-permute-start.7 = (bf16[272,128]{1,0:T(8,128)(2,1)S(1)}, bf16[272,128]{1,0:T(8,128)(2,1)S(1)}, u32[]{:S(2)}, u32[]{:S(2)}) collective-permute-start(bf16[272,128]{1,0:T(8,128)(2,1)S(1)} %get-tuple-element.47), channel_id=1, source_target_pairs={{0,16},{2,18},{16,0},{18,2},{1,17},{3,19},{17,1},{19,3},{4,20},{6,... | collective-permute-start | bytes 208904 | tf_op jit(solution)/shard_map/ppermute | solution.py:471
  21.3 2.5 %collective-permute-start.8 = (bf16[272,128]{1,0:T(8,128)(2,1)S(1)}, bf16[272,128]{1,0:T(8,128)(2,1)S(1)}, u32[]{:S(2)}, u32[]{:S(2)}) collective-permute-start(bf16[272,128]{1,0:T(8,128)(2,1)S(1)} %get-tuple-element.48), channel_id=1, source_target_pairs={{0,2},{2,0},{16,18},{18,16},{1,3},{3,1},{17,19},{19,17},{4,6},{6,4... | collective-permute-start | bytes 208904 | tf_op jit(solution)/shard_map/ppermute | solution.py:471
  24.1 3.2 %collective-permute-done.8.refs_1_ = bf16[272,128]{1,0:T(8,128)(2,1)S(1)} collective-permute-done((bf16[272,128]{1,0:T(8,128)(2,1)S(1)}, bf16[272,128]{1,0:T(8,128)(2,1)S(1)}, u32[]{:S(2)}, u32[]{:S(2)}) %collective-permute-start.8) | collective-permute-done | bytes 69664 | tf_op jit(solution)/shard_map/ppermute | solution.py:471
  27.2 1.9 %collective-permute-done.9.refs_2_ = bf16[272,128]{1,0:T(8,128)(2,1)S(1)} collective-permute-done((bf16[272,128]{1,0:T(8,128)(2,1)S(1)}, bf16[272,128]{1,0:T(8,128)(2,1)S(1)}, u32[]{:S(2)}, u32[]{:S(2)}) %collective-permute-start.9) | collective-permute-done | bytes 69664 | tf_op jit(solution)/shard_map/ppermute | solution.py:471
  29.1 3.4 %collective-permute-start.12 = (bf16[272,128]{1,0:T(8,128)(2,1)S(1)}, bf16[272,128]{1,0:T(8,128)(2,1)S(1)}, u32[]{:S(2)}, u32[]{:S(2)}) collective-permute-start(bf16[272,128]{1,0:T(8,128)(2,1)S(1)} %shard_map.78.a_ref), channel_id=1, source_target_pairs={{0,12},{4,8},{8,4},{12,0},{1,13},{5,9},{9,5},{13,1},{2,14},{6,10},... | collective-permute-start | bytes 208904 | tf_op jit(solution)/shard_map/ppermute | solution.py:471
  32.6 1.0 %collective-permute-start.10 = (bf16[272,128]{1,0:T(8,128)(2,1)S(1)}, bf16[272,128]{1,0:T(8,128)(2,1)S(1)}, u32[]{:S(2)}, u32[]{:S(2)}) collective-permute-start(bf16[272,128]{1,0:T(8,128)(2,1)S(1)} %shard_map.78.a_ref), channel_id=1, source_target_pairs={{0,4},{4,0},{8,12},{12,8},{1,5},{5,1},{9,13},{13,9},{2,6},{6,2},{1... | collective-permute-start | bytes 208904 | tf_op jit(solution)/shard_map/ppermute | solution.py:471
  33.6 2.5 %shard_map.75 = (bf16[128,2,8,128]{3,2,1,0:T(8,128)(2,1)}, f32[8,128]{1,0:T(8,128)S(1)}) custom-call(bf16[4,64,1280]{2,1,0:T(8,128)(2,1)S(1)} %get-tuple-element.40.hidden_ref, bf16[27,64,128]{2,1,0:T(8,128)(2,1)S(1)} %bitcast.7), custom_call_target="tpu_custom_call" | custom-call | flops 900000000 | bytes 1626112 | tf_op jit(solution)/shard_map/pallas_call | solution.py:18
  36.1 1.7 %collective-permute-done.11.c_ref = bf16[272,128]{1,0:T(8,128)(2,1)S(1)} collective-permute-done((bf16[272,128]{1,0:T(8,128)(2,1)S(1)}, bf16[272,128]{1,0:T(8,128)(2,1)S(1)}, u32[]{:S(2)}, u32[]{:S(2)}) %collective-permute-start.11) | collective-permute-done | bytes 69664 | tf_op jit(solution)/shard_map/ppermute | solution.py:471
  38.0 0.5 %collective-permute-start.13 = (bf16[272,128]{1,0:T(8,128)(2,1)S(1)}, bf16[272,128]{1,0:T(8,128)(2,1)S(1)}, u32[]{:S(2)}, u32[]{:S(2)}) collective-permute-start(bf16[272,128]{1,0:T(8,128)(2,1)S(1)} %shard_map.79.own_ref), channel_id=1, source_target_pairs={{0,2},{2,0},{1,3},{3,1},{4,6},{6,4},{5,7},{7,5},{8,10},{10,8},{9,1... | collective-permute-start | bytes 208904 | tf_op jit(solution)/shard_map/ppermute | solution.py:471
  38.5 3.9 %collective-permute-done.13.got_ref = bf16[272,128]{1,0:T(8,128)(2,1)S(1)} collective-permute-done((bf16[272,128]{1,0:T(8,128)(2,1)S(1)}, bf16[272,128]{1,0:T(8,128)(2,1)S(1)}, u32[]{:S(2)}, u32[]{:S(2)}) %collective-permute-start.13) | collective-permute-done | bytes 69664 | tf_op jit(solution)/shard_map/ppermute | solution.py:471
  42.4 0.9 %shard_map.81 = (f32[27,32,32]{2,1,0:T(8,128)}, f32[27,64,64]{2,1,0:T(8,128)}) custom-call(bf16[2,272,128]{2,1,0:T(8,128)(2,1)S(1)} %shard_map.80.in_ref), custom_call_target="tpu_custom_call" | custom-call | bytes 692224 | tf_op jit(solution)/shard_map/pallas_call | solution.py:18
  43.8 0.9 %shard_map.82 = (f32[27,32,32]{2,1,0:T(8,128)}, f32[27,64,64]{2,1,0:T(8,128)}) custom-call(bf16[2,272,128]{2,1,0:T(8,128)(2,1)S(1)} %collective-permute-done.14.in_ref, f32[27,32,32]{2,1,0:T(8,128)} %get-tuple-element.51.refs_0_, f32[27,64,64]{2,1,0:T(8,128)} %get-tuple-element.52.refs_1_), custom_call_target="tpu_custom_call", output_to_operand_aliasing={{0}: (1, {}), {1}: (2, {})} | custom-call | bytes 1245184 | tf_op jit(solution)/shard_map/pallas_call | solution.py:18
  (30 shorter events, 1.7 us)
Async XLA Ops:
  0.6 3.1 %copy-start.2 = (bf16[1,32,2,8,128]{4,3,2,1,0:T(8,128)(2,1)S(1)}, bf16[1,32,2,8,128]{4,3,2,1,0:T(8,128)(2,1)}, u32[]{:S(2)}) copy-start(bf16[1,32,2,8,128]{4,3,2,1,0:T(8,128)(2,1)} %param.4) | copy-start | bytes 393220
  0.6 6.9 %copy-start = (bf16[1,128,2,8,128]{4,3,2,1,0:T(8,128)(2,1)S(1)}, bf16[1,128,2,8,128]{4,3,2,1,0:T(8,128)(2,1)}, u32[]{:S(2)}) copy-start(bf16[1,128,2,8,128]{4,3,2,1,0:T(8,128)(2,1)} %param.7) | copy-start | bytes 1572868
  0.7 6.9 %copy-start.1 = (bf16[27,128,64]{1,2,0:T(8,128)(2,1)S(1)}, bf16[27,128,64]{1,2,0:T(8,128)(2,1)}, u32[]{:S(2)}) copy-start(bf16[27,128,64]{1,2,0:T(8,128)(2,1)} %param.6) | copy-start | bytes 1327108
  0.7 8.6 %collective-permute-start.1 = (bf16[32,2,8,128]{3,2,1,0:T(8,128)(2,1)}, bf16[32,2,8,128]{3,2,1,0:T(8,128)(2,1)S(1)}, u32[]{:S(2)}, u32[]{:S(2)}) collective-permute-start(bf16[32,2,8,128]{3,2,1,0:T(8,128)(2,1)} %bitcast.8), channel_id=1, source_target_pairs={{0,16},{1,17},{2,18},{3,19},{4,20},{5,9},{6,10},{7,23},{8,24},{9,5... | collective-permute-start | bytes 393224 | tf_op jit(solution)/shard_map/ppermute | solution.py:463
  3.7 6.6 %collective-permute-start = (bf16[32,2,8,128]{3,2,1,0:T(8,128)(2,1)}, bf16[32,2,8,128]{3,2,1,0:T(8,128)(2,1)S(1)}, u32[]{:S(2)}, u32[]{:S(2)}) collective-permute-start(bf16[32,2,8,128]{3,2,1,0:T(8,128)(2,1)} %bitcast.9), channel_id=1, source_target_pairs={{0,16},{1,5},{2,6},{3,19},{4,20},{5,1},{6,2},{7,23},{8,24},{9,13},... | collective-permute-start | bytes 393224 | tf_op jit(solution)/shard_map/ppermute | solution.py:463
  3.8 8.7 %copy-start.3 = (bf16[27,64,32]{1,2,0:T(8,128)(2,1)S(1)}, bf16[27,64,32]{1,2,0:T(8,128)(2,1)}, u32[]{:S(2)}) copy-start(bf16[27,64,32]{1,2,0:T(8,128)(2,1)} %param.5) | copy-start | bytes 331780
  3.9 9.1 %collective-permute-start.3 = (bf16[2,32,1024]{2,1,0:T(8,128)(2,1)S(1)}, bf16[2,32,1024]{2,1,0:T(8,128)(2,1)S(1)}, u32[]{:S(2)}, u32[]{:S(2)}) collective-permute-start(bf16[2,32,1024]{2,1,0:T(8,128)(2,1)S(1)} %shard_map.68._.own_ref), channel_id=1, source_target_pairs={{0,16},{1,17},{2,18},{3,19},{4,8},{5,21},{6,22},{7,11},{8,4},{9,25... | collective-permute-start | bytes 393224 | tf_op jit(solution)/shard_map/ppermute | solution.py:463
  5.9 7.1 %collective-permute-start.2 = (bf16[2,32,1024]{2,1,0:T(8,128)(2,1)S(1)}, bf16[2,32,1024]{2,1,0:T(8,128)(2,1)S(1)}, u32[]{:S(2)}, u32[]{:S(2)}) collective-permute-start(bf16[2,32,1024]{2,1,0:T(8,128)(2,1)S(1)} %shard_map.68._.own_ref), channel_id=1, source_target_pairs={{0,4},{1,17},{2,18},{3,7},{4,0},{5,21},{6,22},{7,3},{8,12},{9,25},... | collective-permute-start | bytes 393224 | tf_op jit(solution)/shard_map/ppermute | solution.py:463
  10.6 5.0 %collective-permute-start.4 = (bf16[6,32,256]{2,1,0:T(8,128)(2,1)S(1)}, bf16[6,32,256]{2,1,0:T(8,128)(2,1)S(1)}, u32[]{:S(2)}, u32[]{:S(2)}) collective-permute-start(bf16[6,32,256]{2,1,0:T(8,128)(2,1)S(1)} %get-tuple-element.33), channel_id=1, source_target_pairs={{0,16},{1,2},{2,1},{3,19},{16,0},{17,18},{18,17},{19,3},{4,20},{5,... | collective-permute-start | bytes 294920 | tf_op jit(solution)/shard_map/ppermute | solution.py:450
  13.1 2.5 %collective-permute-start.5 = (bf16[6,32,256]{2,1,0:T(8,128)(2,1)S(1)}, bf16[6,32,256]{2,1,0:T(8,128)(2,1)S(1)}, u32[]{:S(2)}, u32[]{:S(2)}) collective-permute-start(bf16[6,32,256]{2,1,0:T(8,128)(2,1)S(1)} %get-tuple-element.34), channel_id=1, source_target_pairs={{0,1},{1,0},{2,3},{3,2},{16,17},{17,16},{18,19},{19,18},{4,5},{5,4... | collective-permute-start | bytes 294920 | tf_op jit(solution)/shard_map/ppermute | solution.py:450
  17.7 1.7 %collective-permute-start.6 = (bf16[2,2,272,128]{3,2,1,0:T(8,128)(2,1)S(1)}, bf16[2,2,272,128]{3,2,1,0:T(8,128)(2,1)S(1)}, u32[]{:S(2)}, u32[]{:S(2)}) collective-permute-start(bf16[2,2,272,128]{3,2,1,0:T(8,128)(2,1)S(1)} %get-tuple-element.45), channel_id=1, source_target_pairs={{0,1},{1,0},{2,3},{3,2},{4,5},{5,4},{6,7},{7,6},{8,9},{9,8},{10,11... | collective-permute-start | bytes 835592 | tf_op jit(solution)/shard_map/ppermute | solution.py:471
  19.5 4.5 %collective-permute-start.7 = (bf16[272,128]{1,0:T(8,128)(2,1)S(1)}, bf16[272,128]{1,0:T(8,128)(2,1)S(1)}, u32[]{:S(2)}, u32[]{:S(2)}) collective-permute-start(bf16[272,128]{1,0:T(8,128)(2,1)S(1)} %get-tuple-element.47), channel_id=1, source_target_pairs={{0,16},{2,18},{16,0},{18,2},{1,17},{3,19},{17,1},{19,3},{4,20},{6,... | collective-permute-start | bytes 208904 | tf_op jit(solution)/shard_map/ppermute | solution.py:471
  21.3 5.9 %collective-permute-start.8 = (bf16[272,128]{1,0:T(8,128)(2,1)S(1)}, bf16[272,128]{1,0:T(8,128)(2,1)S(1)}, u32[]{:S(2)}, u32[]{:S(2)}) collective-permute-start(bf16[272,128]{1,0:T(8,128)(2,1)S(1)} %get-tuple-element.48), channel_id=1, source_target_pairs={{0,2},{2,0},{16,18},{18,16},{1,3},{3,1},{17,19},{19,17},{4,6},{6,4... | collective-permute-start | bytes 208904 | tf_op jit(solution)/shard_map/ppermute | solution.py:471
  23.9 5.2 %collective-permute-start.9 = (bf16[272,128]{1,0:T(8,128)(2,1)S(1)}, bf16[272,128]{1,0:T(8,128)(2,1)S(1)}, u32[]{:S(2)}, u32[]{:S(2)}) collective-permute-start(bf16[272,128]{1,0:T(8,128)(2,1)S(1)} %get-tuple-element.49), channel_id=1, source_target_pairs={{0,18},{2,16},{16,2},{18,0},{1,19},{3,17},{17,3},{19,1},{4,22},{6,... | collective-permute-start | bytes 208904 | tf_op jit(solution)/shard_map/ppermute | solution.py:471
  29.1 7.0 %collective-permute-start.12 = (bf16[272,128]{1,0:T(8,128)(2,1)S(1)}, bf16[272,128]{1,0:T(8,128)(2,1)S(1)}, u32[]{:S(2)}, u32[]{:S(2)}) collective-permute-start(bf16[272,128]{1,0:T(8,128)(2,1)S(1)} %shard_map.78.a_ref), channel_id=1, source_target_pairs={{0,12},{4,8},{8,4},{12,0},{1,13},{5,9},{9,5},{13,1},{2,14},{6,10},... | collective-permute-start | bytes 208904 | tf_op jit(solution)/shard_map/ppermute | solution.py:471
  32.6 5.3 %collective-permute-start.11 = (bf16[272,128]{1,0:T(8,128)(2,1)S(1)}, bf16[272,128]{1,0:T(8,128)(2,1)S(1)}, u32[]{:S(2)}, u32[]{:S(2)}) collective-permute-start(bf16[272,128]{1,0:T(8,128)(2,1)S(1)} %shard_map.78.a_ref), channel_id=1, source_target_pairs={{0,8},{4,12},{8,0},{12,4},{1,9},{5,13},{9,1},{13,5},{2,10},{6,14},... | collective-permute-start | bytes 208904 | tf_op jit(solution)/shard_map/ppermute | solution.py:471
  32.6 5.4 %collective-permute-start.10 = (bf16[272,128]{1,0:T(8,128)(2,1)S(1)}, bf16[272,128]{1,0:T(8,128)(2,1)S(1)}, u32[]{:S(2)}, u32[]{:S(2)}) collective-permute-start(bf16[272,128]{1,0:T(8,128)(2,1)S(1)} %shard_map.78.a_ref), channel_id=1, source_target_pairs={{0,4},{4,0},{8,12},{12,8},{1,5},{5,1},{9,13},{13,9},{2,6},{6,2},{1... | collective-permute-start | bytes 208904 | tf_op jit(solution)/shard_map/ppermute | solution.py:471
  38.0 4.4 %collective-permute-start.13 = (bf16[272,128]{1,0:T(8,128)(2,1)S(1)}, bf16[272,128]{1,0:T(8,128)(2,1)S(1)}, u32[]{:S(2)}, u32[]{:S(2)}) collective-permute-start(bf16[272,128]{1,0:T(8,128)(2,1)S(1)} %shard_map.79.own_ref), channel_id=1, source_target_pairs={{0,2},{2,0},{1,3},{3,1},{4,6},{6,4},{5,7},{7,5},{8,10},{10,8},{9,1... | collective-permute-start | bytes 208904 | tf_op jit(solution)/shard_map/ppermute | solution.py:471
  42.4 1.4 %collective-permute-start.14 = (bf16[2,272,128]{2,1,0:T(8,128)(2,1)S(1)}, bf16[2,272,128]{2,1,0:T(8,128)(2,1)S(1)}, u32[]{:S(2)}, u32[]{:S(2)}) collective-permute-start(bf16[2,272,128]{2,1,0:T(8,128)(2,1)S(1)} %shard_map.80.in_ref), channel_id=1, source_target_pairs={{0,1},{1,0},{2,3},{3,2},{4,5},{5,4},{6,7},{7,6},{8,9},{9,8},{10,11... | collective-permute-start | bytes 417800 | tf_op jit(solution)/shard_map/ppermute | solution.py:471

commit v18 on v14

--- a/solution.py
+++ b/solution.py
@@ -381,9 +381,12 @@
 def write_kernel(count, wheres, *refs):
     n_scratch = 6
     in_refs = refs[:count]
-    first_ref, second_ref, token_ref = refs[-3 - n_scratch * count : -n_scratch * count]
-    token_ref[...] = jnp.zeros(token_ref.shape, F32)
-    scratch = refs[-n_scratch * count :]
+    out_refs, scratch = refs[: -n_scratch * count], refs[-n_scratch * count :]
+    if wheres[0][1]:
+        first_ref, second_ref, token_ref = out_refs[-3:]
+        token_ref[...] = jnp.zeros(token_ref.shape, F32)
+    else:
+        first_ref, second_ref = out_refs[-2:]
     core, y = lax.axis_index("core"), lax.axis_index("y")
 
     def begun(n, half):
@@ -574,7 +577,7 @@
         flops=4_000_000_000,
     )
     if direct:
-        moves = [(1, 0), (1, 1), (0, 1)]
+        moves = [(1, 0), (0, 1), (1, 1)]
         grads = [second, first]
     else:
         moves = [(0, 1)]
@@ -618,7 +621,7 @@
             count = len(quarters)
             return call(
                 functools.partial(write_kernel, count, wheres),
-                [*outs, shape((8, width), F32)],
+                outs if before else [*outs, shape((8, width), F32)],
                 [*quarters, *before],
                 scratch * count,
                 far=range(count, count + len(before)),
@@ -628,8 +631,7 @@
 
         *grads, token = written([share, other], [(True, True), (False, True)])
         (far,) = call(after_kernel, [shape(block, BF)], [far, token])
-        *grads, _ = written([far], [(True, False)], grads)
-        *grads, _ = written([across(far, ("core", 1))], [(False, False)], grads)
+        grads = written([far, across(far, ("core", 1))], [(True, False), (False, False)], grads)
         grad_first, grad_second = (grad.reshape(27, *grad.shape[2:]) for grad in grads)
     else:
         core, y = lax.axis_index("core"), lax.axis_index("y")

time: 42.2 us -> 40.7 us (0.964)
  Pallas kernels: 13.8 us -> 11.9 us
  waiting for transfers between devices: 11.3 us -> 11.8 us
    pallas_call x15 -> x14, Pallas kernels: 13.8 us -> 11.9 us  [call(): pl.pallas_call(body, out_shape=outs, in_specs=[pl.BlockSpec(memory_space=...]
    ppermute x11, waiting for transfers between devices: 9.69 us -> 10.2 us  [across(): lax.ppermute(x, axes, [(i, i ^ flip) for i in range(lax.axis_size(axes))])]
  transfers between devices with their start and end apart: 15 -> 15, of which waited for: 9 -> 10; matrix products, arithmetic and copies ran while one was open for 0% -> 0% of each run, Pallas kernels for 23% -> 21%
where the time goes in v18:
time: 40.7 us; the launch traced here: 40.6 us
  starting transfers between devices  16.1 us (40%)
  Pallas kernels  11.9 us (29%)
  waiting for transfers between devices  11.8 us (29%)
  between operations  0.79 us (2%)
    pallas_call x14, Pallas kernels, call(): pl.pallas_call(body, out_shape=outs, in_specs=[pl.BlockSpec(memory_space=...  11.9 us
    ppermute x11, waiting for transfers between devices, across(): lax.ppermute(x, axes, [(i, i ^ flip) for i in range(lax.axis_size(axes))])  10.2 us
    ppermute x11, starting transfers between devices, across(): lax.ppermute(x, axes, [(i, i ^ flip) for i in range(lax.axis_size(axes))])  9.72 us
    ppermute x4, starting transfers between devices, swapped(): return lax.ppermute(x, ('dp', *axes), list(enumerate(partner)))  6.36 us
    ppermute x4, waiting for transfers between devices, swapped(): return lax.ppermute(x, ('dp', *axes), list(enumerate(partner)))  1.58 us
  transfers between devices with their start and end apart: 15, of which 10 were waited for; matrix products, arithmetic and copies ran while one was open for 0% of the time, Pallas kernels for 21%

profile of v18, /device:TPU:0, one launch (start us, length us, event | category | flops | bytes accessed | tf_op | source)
XLA Modules:
  0.0 40.6 jit_solution(4410590541341304345)
XLA Ops:
  0.7 3.0 %collective-permute-start.1 = (bf16[32,2,8,128]{3,2,1,0:T(8,128)(2,1)}, bf16[32,2,8,128]{3,2,1,0:T(8,128)(2,1)S(1)}, u32[]{:S(2)}, u32[]{:S(2)}) collective-permute-start(bf16[32,2,8,128]{3,2,1,0:T(8,128)(2,1)} %bitcast.11), channel_id=1, source_target_pairs={{0,16},{4,8},{8,4},{12,28},{16,0},{20,24},{24,20},{28,12},{1,17},{... | collective-permute-start | bytes 393224 | tf_op jit(solution)/shard_map/ppermute | solution.py:461
  3.7 1.7 %collective-permute-start = (bf16[32,2,8,128]{3,2,1,0:T(8,128)(2,1)}, bf16[32,2,8,128]{3,2,1,0:T(8,128)(2,1)S(1)}, u32[]{:S(2)}, u32[]{:S(2)}) collective-permute-start(bf16[32,2,8,128]{3,2,1,0:T(8,128)(2,1)} %bitcast.12), channel_id=1, source_target_pairs={{0,4},{4,0},{8,12},{12,8},{16,20},{20,16},{24,28},{28,24},{1,5},{5... | collective-permute-start | bytes 393224 | tf_op jit(solution)/shard_map/ppermute | solution.py:461
  5.4 1.7 %shard_map.68 = (bf16[2,128,1024]{2,1,0:T(8,128)(2,1)S(1)}, f32[4,64,1280]{2,1,0:T(8,128)S(1)}) custom-call(bf16[128,2,8,128]{3,2,1,0:T(8,128)(2,1)S(1)} %bitcast.7, bf16[27,64,128]{2,1,0:T(8,128)(2,1)S(1)} %bitcast.8, bf16[128,256]{1,0:T(8,128)(2,1)S(1)} %shard_map.67.blank_ref), custom_call_target="tpu_custom_call" | custom-call | flops 1100000000 | bytes 2867200 | tf_op jit(solution)/shard_map/pallas_call | solution.py:18
  7.6 1.2 %collective-permute-done.one_ref = bf16[32,2,8,128]{3,2,1,0:T(8,128)(2,1)S(1)} collective-permute-done((bf16[32,2,8,128]{3,2,1,0:T(8,128)(2,1)}, bf16[32,2,8,128]{3,2,1,0:T(8,128)(2,1)S(1)}, u32[]{:S(2)}, u32[]{:S(2)}) %collective-permute-start) | collective-permute-done | bytes 131104 | tf_op jit(solution)/shard_map/ppermute | solution.py:461
  9.1 1.5 %collective-permute-start.2 = (bf16[6,32,256]{2,1,0:T(8,128)(2,1)S(1)}, bf16[6,32,256]{2,1,0:T(8,128)(2,1)S(1)}, u32[]{:S(2)}, u32[]{:S(2)}) collective-permute-start(bf16[6,32,256]{2,1,0:T(8,128)(2,1)S(1)} %get-tuple-element.35), channel_id=1, source_target_pairs={{0,16},{1,2},{2,1},{3,19},{16,0},{17,18},{18,17},{19,3},{4,20},{5,... | collective-permute-start | bytes 294920 | tf_op jit(solution)/shard_map/ppermute | solution.py:461
  10.8 2.6 %shard_map.71 = (bf16[4,64,768]{2,1,0:T(8,128)(2,1)S(1)}, f32[1152,192]{1,0:T(8,128)S(1)}, f32[192,288]{1,0:T(8,128)S(1)}) custom-call(bf16[6,32,1024]{2,1,0:T(8,128)(2,1)S(1)} %get-tuple-element.34.deep_ref, bf16[192,288]{1,0:T(8,128)(2,1)S(1)} %get-tuple-element.37.w1_ref, bf16[2,384,1024]{2,1,0:T(8,128)(2,1)S(1)} %get-tuple-element.39.moved_ref, ...), custom_call_target="tpu_custom_call" | custom-call | flops 1500000000 | bytes 4886528 | tf_op jit(solution)/shard_map/pallas_call | solution.py:18
  13.8 1.5 %shard_map.72 = (bf16[4,64,1280]{2,1,0:T(8,128)(2,1)S(1)}, f32[2,2,64,128]{3,2,1,0:T(8,128)S(1)}, f32[2,2,64,128]{3,2,1,0:T(8,128)S(1)}) custom-call(bf16[6,32,1024]{2,1,0:T(8,128)(2,1)S(1)} %get-tuple-element.34.deep_ref, bf16[6,32,256]{2,1,0:T(8,128)(2,1)S(1)} %collective-permute-done.2.two_ref, bf16[6,32,256]{2,1,0:T(8,128)(2,1)S(1)} %collective-permute-done.3.one_ref, ...), custom_call_target="tpu_custom_call" | custom-call | flops 1000000000 | bytes 3543040 | tf_op jit(solution)/shard_map/pallas_call | solution.py:18
  16.5 1.2 %collective-permute-done.5.refs_3_ = f32[2,2,64,128]{3,2,1,0:T(8,128)S(1)} collective-permute-done((f32[2,2,64,128]{3,2,1,0:T(8,128)S(1)}, f32[2,2,64,128]{3,2,1,0:T(8,128)S(1)}, u32[]{:S(2)}, u32[]{:S(2)}) %collective-permute-start.5) | collective-permute-done | bytes 131104 | tf_op jit(solution)/shard_map/ppermute | solution.py:469
  17.7 1.5 %collective-permute-start.6 = (bf16[272,128]{1,0:T(8,128)(2,1)S(1)}, bf16[272,128]{1,0:T(8,128)(2,1)S(1)}, u32[]{:S(2)}, u32[]{:S(2)}) collective-permute-start(bf16[272,128]{1,0:T(8,128)(2,1)S(1)} %get-tuple-element.50), channel_id=1, source_target_pairs={{0,16},{2,18},{16,0},{18,2},{1,17},{3,19},{17,1},{19,3},{4,20},{6,... | collective-permute-start | bytes 208904 | tf_op jit(solution)/shard_map/ppermute | solution.py:469
  19.2 0.9 %collective-permute-start.7 = (bf16[272,128]{1,0:T(8,128)(2,1)S(1)}, bf16[272,128]{1,0:T(8,128)(2,1)S(1)}, u32[]{:S(2)}, u32[]{:S(2)}) collective-permute-start(bf16[272,128]{1,0:T(8,128)(2,1)S(1)} %get-tuple-element.51), channel_id=1, source_target_pairs={{0,2},{2,0},{16,18},{18,16},{1,3},{3,1},{17,19},{19,17},{4,6},{6,4... | collective-permute-start | bytes 208904 | tf_op jit(solution)/shard_map/ppermute | solution.py:469
  20.2 1.1 %collective-permute-start.8 = (bf16[272,128]{1,0:T(8,128)(2,1)S(1)}, bf16[272,128]{1,0:T(8,128)(2,1)S(1)}, u32[]{:S(2)}, u32[]{:S(2)}) collective-permute-start(bf16[272,128]{1,0:T(8,128)(2,1)S(1)} %get-tuple-element.52), channel_id=1, source_target_pairs={{0,18},{2,16},{16,2},{18,0},{1,19},{3,17},{17,3},{19,1},{4,22},{6,... | collective-permute-start | bytes 208904 | tf_op jit(solution)/shard_map/ppermute | solution.py:469
  21.3 0.8 %collective-permute-done.6.refs_0_ = bf16[272,128]{1,0:T(8,128)(2,1)S(1)} collective-permute-done((bf16[272,128]{1,0:T(8,128)(2,1)S(1)}, bf16[272,128]{1,0:T(8,128)(2,1)S(1)}, u32[]{:S(2)}, u32[]{:S(2)}) %collective-permute-start.6) | collective-permute-done | bytes 69664 | tf_op jit(solution)/shard_map/ppermute | solution.py:469
  22.1 2.2 %collective-permute-done.7.refs_1_ = bf16[272,128]{1,0:T(8,128)(2,1)S(1)} collective-permute-done((bf16[272,128]{1,0:T(8,128)(2,1)S(1)}, bf16[272,128]{1,0:T(8,128)(2,1)S(1)}, u32[]{:S(2)}, u32[]{:S(2)}) %collective-permute-start.7) | collective-permute-done | bytes 69664 | tf_op jit(solution)/shard_map/ppermute | solution.py:469
  24.3 1.1 %collective-permute-done.8.refs_2_ = bf16[272,128]{1,0:T(8,128)(2,1)S(1)} collective-permute-done((bf16[272,128]{1,0:T(8,128)(2,1)S(1)}, bf16[272,128]{1,0:T(8,128)(2,1)S(1)}, u32[]{:S(2)}, u32[]{:S(2)}) %collective-permute-start.8) | collective-permute-done | bytes 69664 | tf_op jit(solution)/shard_map/ppermute | solution.py:469
  25.4 2.8 %collective-permute-start.11 = (bf16[272,128]{1,0:T(8,128)(2,1)S(1)}, bf16[272,128]{1,0:T(8,128)(2,1)S(1)}, u32[]{:S(2)}, u32[]{:S(2)}) collective-permute-start(bf16[272,128]{1,0:T(8,128)(2,1)S(1)} %shard_map.76.a_ref), channel_id=1, source_target_pairs={{0,12},{4,8},{8,4},{12,0},{1,13},{5,9},{9,5},{13,1},{2,14},{6,10},... | collective-permute-start | bytes 208904 | tf_op jit(solution)/shard_map/ppermute | solution.py:469
  28.7 1.2 %collective-permute-start.9 = (bf16[272,128]{1,0:T(8,128)(2,1)S(1)}, bf16[272,128]{1,0:T(8,128)(2,1)S(1)}, u32[]{:S(2)}, u32[]{:S(2)}) collective-permute-start(bf16[272,128]{1,0:T(8,128)(2,1)S(1)} %shard_map.76.a_ref), channel_id=1, source_target_pairs={{0,4},{4,0},{8,12},{12,8},{1,5},{5,1},{9,13},{13,9},{2,6},{6,2},{1... | collective-permute-start | bytes 208904 | tf_op jit(solution)/shard_map/ppermute | solution.py:469
  29.9 2.5 %shard_map.73 = (bf16[128,2,8,128]{3,2,1,0:T(8,128)(2,1)}, f32[8,128]{1,0:T(8,128)S(1)}) custom-call(bf16[4,64,1280]{2,1,0:T(8,128)(2,1)S(1)} %get-tuple-element.42.hidden_ref, bf16[27,64,128]{2,1,0:T(8,128)(2,1)S(1)} %bitcast.9), custom_call_target="tpu_custom_call" | custom-call | flops 900000000 | bytes 1626112 | tf_op jit(solution)/shard_map/pallas_call | solution.py:18
  32.4 1.4 %collective-permute-done.10.c_ref = bf16[272,128]{1,0:T(8,128)(2,1)S(1)} collective-permute-done((bf16[272,128]{1,0:T(8,128)(2,1)S(1)}, bf16[272,128]{1,0:T(8,128)(2,1)S(1)}, u32[]{:S(2)}, u32[]{:S(2)}) %collective-permute-start.10) | collective-permute-done | bytes 69664 | tf_op jit(solution)/shard_map/ppermute | solution.py:469
  33.9 1.1 %collective-permute-start.12 = (bf16[288,128]{1,0:T(8,128)(2,1)S(1)}, bf16[288,128]{1,0:T(8,128)(2,1)S(1)}, u32[]{:S(2)}, u32[]{:S(2)}) collective-permute-start(bf16[288,128]{1,0:T(8,128)(2,1)S(1)} %get-tuple-element.54), channel_id=1, source_target_pairs={{0,2},{2,0},{1,3},{3,1},{4,6},{6,4},{5,7},{7,5},{8,10},{10,8},{9,1... | collective-permute-start | bytes 221192 | tf_op jit(solution)/shard_map/ppermute | solution.py:469
  35.0 1.3 %collective-permute-done.13.refs_1_ = bf16[272,128]{1,0:T(8,128)(2,1)S(1)} collective-permute-done((bf16[272,128]{1,0:T(8,128)(2,1)S(1)}, bf16[272,128]{1,0:T(8,128)(2,1)S(1)}, u32[]{:S(2)}, u32[]{:S(2)}) %collective-permute-start.13) | collective-permute-done | bytes 69664 | tf_op jit(solution)/shard_map/ppermute | solution.py:469
  36.3 1.0 %shard_map.78 = (f32[9,3,32,32]{3,2,1,0:T(8,128)}, f32[3,9,64,64]{3,2,1,0:T(8,128)}, f32[8,128]{1,0:T(8,128)S(1)}) custom-call(bf16[272,128]{1,0:T(8,128)(2,1)S(1)} %get-tuple-element.55.refs_0_, bf16[272,128]{1,0:T(8,128)(2,1)S(1)} %collective-permute-done.13.refs_1_), custom_call_target="tpu_custom_call" | custom-call | bytes 696320 | tf_op jit(solution)/shard_map/pallas_call | solution.py:18
  37.3 1.0 %collective-permute-done.12.in_ref = bf16[288,128]{1,0:T(8,128)(2,1)S(1)} collective-permute-done((bf16[288,128]{1,0:T(8,128)(2,1)S(1)}, bf16[288,128]{1,0:T(8,128)(2,1)S(1)}, u32[]{:S(2)}, u32[]{:S(2)}) %collective-permute-start.12) | collective-permute-done | bytes 73760 | tf_op jit(solution)/shard_map/ppermute | solution.py:469
  38.3 1.3 %collective-permute-done.14.refs_1_ = bf16[272,128]{1,0:T(8,128)(2,1)S(1)} collective-permute-done((bf16[272,128]{1,0:T(8,128)(2,1)S(1)}, bf16[272,128]{1,0:T(8,128)(2,1)S(1)}, u32[]{:S(2)}, u32[]{:S(2)}) %collective-permute-start.14) | collective-permute-done | bytes 69664 | tf_op jit(solution)/shard_map/ppermute | solution.py:469
  39.6 1.0 %shard_map.80 = (f32[9,3,32,32]{3,2,1,0:T(8,128)}, f32[3,9,64,64]{3,2,1,0:T(8,128)}) custom-call(bf16[272,128]{1,0:T(8,128)(2,1)S(1)} %shard_map.79.refs_0_, bf16[272,128]{1,0:T(8,128)(2,1)S(1)} %collective-permute-done.14.refs_1_, f32[9,3,32,32]{3,2,1,0:T(8,128)} %get-tuple-element.57.refs_2_, ...), custom_call_target="tpu_custom_call", output_to_operand_aliasing={{0}: (2, {}), {1}: (3, {})} | custom-call | bytes 1245184 | tf_op jit(solution)/shard_map/pallas_call | solution.py:18
  (28 shorter events, 3.2 us)
Async XLA Ops:
  0.6 4.7 %copy-start = (bf16[1,128,2,8,128]{4,3,2,1,0:T(8,128)(2,1)S(1)}, bf16[1,128,2,8,128]{4,3,2,1,0:T(8,128)(2,1)}, u32[]{:S(2)}) copy-start(bf16[1,128,2,8,128]{4,3,2,1,0:T(8,128)(2,1)} %param.7) | copy-start | bytes 1572868
  0.6 4.7 %copy-start.1 = (bf16[27,128,64]{1,2,0:T(8,128)(2,1)S(1)}, bf16[27,128,64]{1,2,0:T(8,128)(2,1)}, u32[]{:S(2)}) copy-start(bf16[27,128,64]{1,2,0:T(8,128)(2,1)} %param.6) | copy-start | bytes 1327108
  0.7 7.0 %collective-permute-start.1 = (bf16[32,2,8,128]{3,2,1,0:T(8,128)(2,1)}, bf16[32,2,8,128]{3,2,1,0:T(8,128)(2,1)S(1)}, u32[]{:S(2)}, u32[]{:S(2)}) collective-permute-start(bf16[32,2,8,128]{3,2,1,0:T(8,128)(2,1)} %bitcast.11), channel_id=1, source_target_pairs={{0,16},{4,8},{8,4},{12,28},{16,0},{20,24},{24,20},{28,12},{1,17},{... | collective-permute-start | bytes 393224 | tf_op jit(solution)/shard_map/ppermute | solution.py:461
  3.7 5.2 %collective-permute-start = (bf16[32,2,8,128]{3,2,1,0:T(8,128)(2,1)}, bf16[32,2,8,128]{3,2,1,0:T(8,128)(2,1)S(1)}, u32[]{:S(2)}, u32[]{:S(2)}) collective-permute-start(bf16[32,2,8,128]{3,2,1,0:T(8,128)(2,1)} %bitcast.12), channel_id=1, source_target_pairs={{0,4},{4,0},{8,12},{12,8},{16,20},{20,16},{24,28},{28,24},{1,5},{5... | collective-permute-start | bytes 393224 | tf_op jit(solution)/shard_map/ppermute | solution.py:461
  5.3 1.8 %copy-start.2 = (bf16[27,64,32]{1,2,0:T(8,128)(2,1)S(1)}, bf16[27,64,32]{1,2,0:T(8,128)(2,1)}, u32[]{:S(2)}) copy-start(bf16[27,64,32]{1,2,0:T(8,128)(2,1)} %param.5) | copy-start | bytes 331780
  5.3 1.8 %copy-start.3 = (bf16[1,32,2,8,128]{4,3,2,1,0:T(8,128)(2,1)S(1)}, bf16[1,32,2,8,128]{4,3,2,1,0:T(8,128)(2,1)}, u32[]{:S(2)}) copy-start(bf16[1,32,2,8,128]{4,3,2,1,0:T(8,128)(2,1)} %param.4) | copy-start | bytes 393220
  9.1 4.7 %collective-permute-start.2 = (bf16[6,32,256]{2,1,0:T(8,128)(2,1)S(1)}, bf16[6,32,256]{2,1,0:T(8,128)(2,1)S(1)}, u32[]{:S(2)}, u32[]{:S(2)}) collective-permute-start(bf16[6,32,256]{2,1,0:T(8,128)(2,1)S(1)} %get-tuple-element.35), channel_id=1, source_target_pairs={{0,16},{1,2},{2,1},{3,19},{16,0},{17,18},{18,17},{19,3},{4,20},{5,... | collective-permute-start | bytes 294920 | tf_op jit(solution)/shard_map/ppermute | solution.py:461
  10.6 3.2 %collective-permute-start.3 = (bf16[6,32,256]{2,1,0:T(8,128)(2,1)S(1)}, bf16[6,32,256]{2,1,0:T(8,128)(2,1)S(1)}, u32[]{:S(2)}, u32[]{:S(2)}) collective-permute-start(bf16[6,32,256]{2,1,0:T(8,128)(2,1)S(1)} %get-tuple-element.36), channel_id=1, source_target_pairs={{0,1},{1,0},{2,3},{3,2},{16,17},{17,16},{18,19},{19,18},{4,5},{5,4... | collective-permute-start | bytes 294920 | tf_op jit(solution)/shard_map/ppermute | solution.py:461
  15.9 1.7 %collective-permute-start.4 = (bf16[2,2,224,128]{3,2,1,0:T(8,128)(2,1)S(1)}, bf16[2,2,224,128]{3,2,1,0:T(8,128)(2,1)S(1)}, u32[]{:S(2)}, u32[]{:S(2)}) collective-permute-start(bf16[2,2,224,128]{3,2,1,0:T(8,128)(2,1)S(1)} %get-tuple-element.46), channel_id=1, source_target_pairs={{0,1},{1,0},{2,3},{3,2},{4,5},{5,4},{6,7},{7,6},{8,9},{9,8},{10,11... | collective-permute-start | bytes 688136 | tf_op jit(solution)/shard_map/ppermute | solution.py:469
  16.0 1.7 %collective-permute-start.5 = (f32[2,2,64,128]{3,2,1,0:T(8,128)S(1)}, f32[2,2,64,128]{3,2,1,0:T(8,128)S(1)}, u32[]{:S(2)}, u32[]{:S(2)}) collective-permute-start(f32[2,2,64,128]{3,2,1,0:T(8,128)S(1)} %get-tuple-element.48), channel_id=1, source_target_pairs={{0,1},{1,0},{2,3},{3,2},{4,5},{5,4},{6,7},{7,6},{8,9},{9,8},{10,11... | collective-permute-start | bytes 393224 | tf_op jit(solution)/shard_map/ppermute | solution.py:469
  17.7 4.4 %collective-permute-start.6 = (bf16[272,128]{1,0:T(8,128)(2,1)S(1)}, bf16[272,128]{1,0:T(8,128)(2,1)S(1)}, u32[]{:S(2)}, u32[]{:S(2)}) collective-permute-start(bf16[272,128]{1,0:T(8,128)(2,1)S(1)} %get-tuple-element.50), channel_id=1, source_target_pairs={{0,16},{2,18},{16,0},{18,2},{1,17},{3,19},{17,1},{19,3},{4,20},{6,... | collective-permute-start | bytes 208904 | tf_op jit(solution)/shard_map/ppermute | solution.py:469
  19.2 5.1 %collective-permute-start.7 = (bf16[272,128]{1,0:T(8,128)(2,1)S(1)}, bf16[272,128]{1,0:T(8,128)(2,1)S(1)}, u32[]{:S(2)}, u32[]{:S(2)}) collective-permute-start(bf16[272,128]{1,0:T(8,128)(2,1)S(1)} %get-tuple-element.51), channel_id=1, source_target_pairs={{0,2},{2,0},{16,18},{18,16},{1,3},{3,1},{17,19},{19,17},{4,6},{6,4... | collective-permute-start | bytes 208904 | tf_op jit(solution)/shard_map/ppermute | solution.py:469
  20.2 5.2 %collective-permute-start.8 = (bf16[272,128]{1,0:T(8,128)(2,1)S(1)}, bf16[272,128]{1,0:T(8,128)(2,1)S(1)}, u32[]{:S(2)}, u32[]{:S(2)}) collective-permute-start(bf16[272,128]{1,0:T(8,128)(2,1)S(1)} %get-tuple-element.52), channel_id=1, source_target_pairs={{0,18},{2,16},{16,2},{18,0},{1,19},{3,17},{17,3},{19,1},{4,22},{6,... | collective-permute-start | bytes 208904 | tf_op jit(solution)/shard_map/ppermute | solution.py:469
  25.4 7.0 %collective-permute-start.11 = (bf16[272,128]{1,0:T(8,128)(2,1)S(1)}, bf16[272,128]{1,0:T(8,128)(2,1)S(1)}, u32[]{:S(2)}, u32[]{:S(2)}) collective-permute-start(bf16[272,128]{1,0:T(8,128)(2,1)S(1)} %shard_map.76.a_ref), channel_id=1, source_target_pairs={{0,12},{4,8},{8,4},{12,0},{1,13},{5,9},{9,5},{13,1},{2,14},{6,10},... | collective-permute-start | bytes 208904 | tf_op jit(solution)/shard_map/ppermute | solution.py:469
  28.2 5.6 %collective-permute-start.10 = (bf16[272,128]{1,0:T(8,128)(2,1)S(1)}, bf16[272,128]{1,0:T(8,128)(2,1)S(1)}, u32[]{:S(2)}, u32[]{:S(2)}) collective-permute-start(bf16[272,128]{1,0:T(8,128)(2,1)S(1)} %shard_map.76.a_ref), channel_id=1, source_target_pairs={{0,8},{4,12},{8,0},{12,4},{1,9},{5,13},{9,1},{13,5},{2,10},{6,14},... | collective-permute-start | bytes 208904 | tf_op jit(solution)/shard_map/ppermute | solution.py:469
  28.7 5.2 %collective-permute-start.9 = (bf16[272,128]{1,0:T(8,128)(2,1)S(1)}, bf16[272,128]{1,0:T(8,128)(2,1)S(1)}, u32[]{:S(2)}, u32[]{:S(2)}) collective-permute-start(bf16[272,128]{1,0:T(8,128)(2,1)S(1)} %shard_map.76.a_ref), channel_id=1, source_target_pairs={{0,4},{4,0},{8,12},{12,8},{1,5},{5,1},{9,13},{13,9},{2,6},{6,2},{1... | collective-permute-start | bytes 208904 | tf_op jit(solution)/shard_map/ppermute | solution.py:469
  33.9 4.4 %collective-permute-start.12 = (bf16[288,128]{1,0:T(8,128)(2,1)S(1)}, bf16[288,128]{1,0:T(8,128)(2,1)S(1)}, u32[]{:S(2)}, u32[]{:S(2)}) collective-permute-start(bf16[288,128]{1,0:T(8,128)(2,1)S(1)} %get-tuple-element.54), channel_id=1, source_target_pairs={{0,2},{2,0},{1,3},{3,1},{4,6},{6,4},{5,7},{7,5},{8,10},{10,8},{9,1... | collective-permute-start | bytes 221192 | tf_op jit(solution)/shard_map/ppermute | solution.py:469
  35.0 1.3 %collective-permute-start.13 = (bf16[272,128]{1,0:T(8,128)(2,1)S(1)}, bf16[272,128]{1,0:T(8,128)(2,1)S(1)}, u32[]{:S(2)}, u32[]{:S(2)}) collective-permute-start(bf16[272,128]{1,0:T(8,128)(2,1)S(1)} %get-tuple-element.55.refs_0_), channel_id=1, source_target_pairs={{0,1},{1,0},{2,3},{3,2},{4,5},{5,4},{6,7},{7,6},{8,9},{9,8},{10,11... | collective-permute-start | bytes 208904 | tf_op jit(solution)/shard_map/ppermute | solution.py:469
  38.3 1.3 %collective-permute-start.14 = (bf16[272,128]{1,0:T(8,128)(2,1)S(1)}, bf16[272,128]{1,0:T(8,128)(2,1)S(1)}, u32[]{:S(2)}, u32[]{:S(2)}) collective-permute-start(bf16[272,128]{1,0:T(8,128)(2,1)S(1)} %shard_map.79.refs_0_), channel_id=1, source_target_pairs={{0,1},{1,0},{2,3},{3,2},{4,5},{5,4},{6,7},{7,6},{8,9},{9,8},{10,11... | collective-permute-start | bytes 208904 | tf_op jit(solution)/shard_map/ppermute | solution.py:469

commit v19 on v13

--- a/solution.py
+++ b/solution.py
@@ -46,7 +46,7 @@
 def by_rows(ref, scratch, store):
     channels, depth, height, width = ref.shape
     rows = depth * height
-    scratch[...] = ref[...].astype(F32).reshape(channels * rows, width)
+    scratch[: channels * rows] = ref[...].astype(F32).reshape(channels * rows, width)
     for d in range(depth):
         for h in range(height):
             store(d, h, scratch[pl.ds(d * height + h, channels, stride=rows), :])
@@ -330,7 +330,7 @@
             for r in range(2):
                 row = total[:, r * LANES : (r + 1) * LANES]
                 scratch[pl.ds(d * height + h + r, out, stride=depth * height), :] = row
-    out_ref[...] = scratch[...].reshape(out_ref.shape).astype(BF)
+    out_ref[...] = scratch[: out * depth * height].reshape(out_ref.shape).astype(BF)
     token_ref[...] = scratch[:8]
 
 
@@ -468,7 +468,7 @@
             shape((depth + 2, mid, cells + 2 * width), F32),
         ],
         [cotangent[0], k2, blank],
-        [pltpu.VMEM((out * rows, width), F32)],
+        [pltpu.VMEM(((out + 1) * rows, width), F32)],
         flops=1_100_000_000,
     )
     moved, w1, vol = call(
@@ -479,14 +479,14 @@
             shape((depth, inner, cells), BF),
         ],
         [cot_rows, k1, volume[0]],
-        [pltpu.VMEM((inner * rows, width), F32)],
+        [pltpu.VMEM(((inner + 1) * rows, width), F32)],
         flops=500_000_000,
     )
     deep, one, two = call(
         rim_kernel,
         [shape((3 * depth, inner, cells), BF)] + [shape((3 * depth, inner, 2 * width), BF)] * 2,
         [vol, one, two],
-        [pltpu.VMEM((inner * rows, width), F32)],
+        [pltpu.VMEM(((inner + 1) * rows, width), F32)],
     )
     one, two = swapped(one, HGT, 0), swapped(two, HGT, 1)
     size = mid // parts
@@ -547,7 +547,7 @@
         features_kernel,
         [shape(cotangent.shape[1:], BF), shape((8, width), F32)],
         [hidden, k2],
-        [pltpu.VMEM((out * rows, width), F32)],
+        [pltpu.VMEM(((out + 1) * rows, width), F32)],
         flops=900_000_000,
     )
     gots = [across(share, ("dep", bits)) for bits in (1, 2, 3)]

time: 40.8 us -> 40.8 us (level)
  no operation moved by 1% of the time
where the time goes in v19:
time: 40.8 us; the launch traced here: 40.6 us
  starting transfers between devices  16.2 us (40%)
  waiting for transfers between devices  11.9 us (29%)
  Pallas kernels  11.8 us (29%)
  between operations  0.79 us (2%)
    pallas_call x14, Pallas kernels, call(): pl.pallas_call(body, out_shape=outs, in_specs=[pl.BlockSpec(memory_space=...  11.8 us
    ppermute x10, waiting for transfers between devices, across(): lax.ppermute(x, axes, [(i, i ^ flip) for i in range(lax.axis_size(axes))])  10.3 us
    ppermute x10, starting transfers between devices, across(): lax.ppermute(x, axes, [(i, i ^ flip) for i in range(lax.axis_size(axes))])  9.79 us
    ppermute x4, starting transfers between devices, swapped(): return lax.ppermute(x, ('dp', *axes), list(enumerate(partner)))  6.36 us
    ppermute x4, waiting for transfers between devices, swapped(): return lax.ppermute(x, ('dp', *axes), list(enumerate(partner)))  1.58 us
  transfers between devices with their start and end apart: 14, of which 9 were waited for; matrix products, arithmetic and copies ran while one was open for 0% of the time, Pallas kernels for 20%

profile of v19, /device:TPU:0, one launch (start us, length us, event | category | flops | bytes accessed | tf_op | source)
XLA Modules:
  0.0 40.6 jit_solution(14206971888408594885)
XLA Ops:
  0.7 3.0 %collective-permute-start.1 = (bf16[32,2,8,128]{3,2,1,0:T(8,128)(2,1)}, bf16[32,2,8,128]{3,2,1,0:T(8,128)(2,1)S(1)}, u32[]{:S(2)}, u32[]{:S(2)}) collective-permute-start(bf16[32,2,8,128]{3,2,1,0:T(8,128)(2,1)} %bitcast.9), channel_id=1, source_target_pairs={{0,16},{4,8},{8,4},{12,28},{16,0},{20,24},{24,20},{28,12},{1,17},{... | collective-permute-start | bytes 393224 | tf_op jit(solution)/shard_map/ppermute | solution.py:412
  3.7 1.7 %collective-permute-start = (bf16[32,2,8,128]{3,2,1,0:T(8,128)(2,1)}, bf16[32,2,8,128]{3,2,1,0:T(8,128)(2,1)S(1)}, u32[]{:S(2)}, u32[]{:S(2)}) collective-permute-start(bf16[32,2,8,128]{3,2,1,0:T(8,128)(2,1)} %bitcast.10), channel_id=1, source_target_pairs={{0,4},{4,0},{8,12},{12,8},{16,20},{20,16},{24,28},{28,24},{1,5},{5... | collective-permute-start | bytes 393224 | tf_op jit(solution)/shard_map/ppermute | solution.py:412
  5.4 1.7 %shard_map.68 = (bf16[2,128,1024]{2,1,0:T(8,128)(2,1)S(1)}, f32[4,64,1280]{2,1,0:T(8,128)S(1)}) custom-call(bf16[128,2,8,128]{3,2,1,0:T(8,128)(2,1)S(1)} %bitcast.5, bf16[27,64,128]{2,1,0:T(8,128)(2,1)S(1)} %bitcast.6, bf16[128,256]{1,0:T(8,128)(2,1)S(1)} %shard_map.67.blank_ref), custom_call_target="tpu_custom_call" | custom-call | flops 1100000000 | bytes 2867200 | tf_op jit(solution)/shard_map/pallas_call | solution.py:18
  7.1 0.5 %shard_map.69 = (bf16[2,384,1024]{2,1,0:T(8,128)(2,1)S(1)}, bf16[192,288]{1,0:T(8,128)(2,1)S(1)}, bf16[2,32,1024]{2,1,0:T(8,128)(2,1)S(1)}) custom-call(bf16[2,128,1024]{2,1,0:T(8,128)(2,1)S(1)} %get-tuple-element.29.cot_rows_ref, bf16[27,32,64]{2,1,0:T(8,128)(2,1)S(1)} %bitcast.8, bf16[32,2,8,128]{3,2,1,0:T(8,128)(2,1)S(1)} %bitcast.11), custom_call_target="tpu_custom_call" | custom-call | flops 500000000 | bytes 2580480 | tf_op jit(solution)/shard_map/pallas_call | solution.py:18
  7.6 1.2 %collective-permute-done.one_ref = bf16[32,2,8,128]{3,2,1,0:T(8,128)(2,1)S(1)} collective-permute-done((bf16[32,2,8,128]{3,2,1,0:T(8,128)(2,1)}, bf16[32,2,8,128]{3,2,1,0:T(8,128)(2,1)S(1)}, u32[]{:S(2)}, u32[]{:S(2)}) %collective-permute-start) | collective-permute-done | bytes 131104 | tf_op jit(solution)/shard_map/ppermute | solution.py:412
  9.1 1.5 %collective-permute-start.2 = (bf16[6,32,256]{2,1,0:T(8,128)(2,1)S(1)}, bf16[6,32,256]{2,1,0:T(8,128)(2,1)S(1)}, u32[]{:S(2)}, u32[]{:S(2)}) collective-permute-start(bf16[6,32,256]{2,1,0:T(8,128)(2,1)S(1)} %get-tuple-element.32), channel_id=1, source_target_pairs={{0,16},{1,2},{2,1},{3,19},{16,0},{17,18},{18,17},{19,3},{4,20},{5,... | collective-permute-start | bytes 294920 | tf_op jit(solution)/shard_map/ppermute | solution.py:412
  10.8 2.6 %shard_map.71 = (bf16[4,64,768]{2,1,0:T(8,128)(2,1)S(1)}, f32[1152,192]{1,0:T(8,128)S(1)}, f32[192,288]{1,0:T(8,128)S(1)}) custom-call(bf16[6,32,1024]{2,1,0:T(8,128)(2,1)S(1)} %get-tuple-element.31.deep_ref, bf16[192,288]{1,0:T(8,128)(2,1)S(1)} %get-tuple-element.34.w1_ref, bf16[2,384,1024]{2,1,0:T(8,128)(2,1)S(1)} %get-tuple-element.36.moved_ref, ...), custom_call_target="tpu_custom_call" | custom-call | flops 1500000000 | bytes 4886528 | tf_op jit(solution)/shard_map/pallas_call | solution.py:18
  13.8 1.5 %shard_map.72 = (bf16[4,64,1280]{2,1,0:T(8,128)(2,1)S(1)}, f32[2,2,56,128]{3,2,1,0:T(8,128)S(1)}, f32[2,2,56,128]{3,2,1,0:T(8,128)S(1)}) custom-call(bf16[6,32,1024]{2,1,0:T(8,128)(2,1)S(1)} %get-tuple-element.31.deep_ref, bf16[6,32,256]{2,1,0:T(8,128)(2,1)S(1)} %collective-permute-done.2.two_ref, bf16[6,32,256]{2,1,0:T(8,128)(2,1)S(1)} %collective-permute-done.3.one_ref, ...), custom_call_target="tpu_custom_call" | custom-call | flops 1000000000 | bytes 3510272 | tf_op jit(solution)/shard_map/pallas_call | solution.py:18
  15.4 0.6 %shard_map.74 = (f32[2,2,216,128]{3,2,1,0:T(8,128)S(1)}, bf16[2,2,216,128]{3,2,1,0:T(8,128)(2,1)S(1)}) custom-call(bf16[4,64,1280]{2,1,0:T(8,128)(2,1)S(1)} %get-tuple-element.39.hidden_ref, bf16[2,384,1024]{2,1,0:T(8,128)(2,1)S(1)} %get-tuple-element.36.moved_ref, f32[1152,192]{1,0:T(8,128)S(1)} %get-tuple-element.43.second_ref), custom_call_target="tpu_custom_call" | custom-call | flops 4000000000 | bytes 3776512 | tf_op jit(solution)/shard_map/pallas_call | solution.py:18
  16.5 1.1 %collective-permute-done.4.refs_1_ = f32[2,2,56,128]{3,2,1,0:T(8,128)S(1)} collective-permute-done((f32[2,2,56,128]{3,2,1,0:T(8,128)S(1)}, f32[2,2,56,128]{3,2,1,0:T(8,128)S(1)}, u32[]{:S(2)}, u32[]{:S(2)}) %collective-permute-start.4) | collective-permute-done | bytes 114720 | tf_op jit(solution)/shard_map/ppermute | solution.py:420
  17.7 1.5 %collective-permute-start.6 = (bf16[272,128]{1,0:T(8,128)(2,1)S(1)}, bf16[272,128]{1,0:T(8,128)(2,1)S(1)}, u32[]{:S(2)}, u32[]{:S(2)}) collective-permute-start(bf16[272,128]{1,0:T(8,128)(2,1)S(1)} %get-tuple-element.47), channel_id=1, source_target_pairs={{0,16},{2,18},{16,0},{18,2},{1,17},{3,19},{17,1},{19,3},{4,20},{6,... | collective-permute-start | bytes 208904 | tf_op jit(solution)/shard_map/ppermute | solution.py:420
  19.2 0.9 %collective-permute-start.7 = (bf16[272,128]{1,0:T(8,128)(2,1)S(1)}, bf16[272,128]{1,0:T(8,128)(2,1)S(1)}, u32[]{:S(2)}, u32[]{:S(2)}) collective-permute-start(bf16[272,128]{1,0:T(8,128)(2,1)S(1)} %get-tuple-element.48), channel_id=1, source_target_pairs={{0,2},{2,0},{16,18},{18,16},{1,3},{3,1},{17,19},{19,17},{4,6},{6,4... | collective-permute-start | bytes 208904 | tf_op jit(solution)/shard_map/ppermute | solution.py:420
  20.1 1.1 %collective-permute-start.8 = (bf16[272,128]{1,0:T(8,128)(2,1)S(1)}, bf16[272,128]{1,0:T(8,128)(2,1)S(1)}, u32[]{:S(2)}, u32[]{:S(2)}) collective-permute-start(bf16[272,128]{1,0:T(8,128)(2,1)S(1)} %get-tuple-element.49), channel_id=1, source_target_pairs={{0,18},{2,16},{16,2},{18,0},{1,19},{3,17},{17,3},{19,1},{4,22},{6,... | collective-permute-start | bytes 208904 | tf_op jit(solution)/shard_map/ppermute | solution.py:420
  21.3 0.8 %collective-permute-done.6.refs_0_ = bf16[272,128]{1,0:T(8,128)(2,1)S(1)} collective-permute-done((bf16[272,128]{1,0:T(8,128)(2,1)S(1)}, bf16[272,128]{1,0:T(8,128)(2,1)S(1)}, u32[]{:S(2)}, u32[]{:S(2)}) %collective-permute-start.6) | collective-permute-done | bytes 69664 | tf_op jit(solution)/shard_map/ppermute | solution.py:420
  22.1 2.2 %collective-permute-done.7.refs_1_ = bf16[272,128]{1,0:T(8,128)(2,1)S(1)} collective-permute-done((bf16[272,128]{1,0:T(8,128)(2,1)S(1)}, bf16[272,128]{1,0:T(8,128)(2,1)S(1)}, u32[]{:S(2)}, u32[]{:S(2)}) %collective-permute-start.7) | collective-permute-done | bytes 69664 | tf_op jit(solution)/shard_map/ppermute | solution.py:420
  24.3 1.1 %collective-permute-done.8.refs_2_ = bf16[272,128]{1,0:T(8,128)(2,1)S(1)} collective-permute-done((bf16[272,128]{1,0:T(8,128)(2,1)S(1)}, bf16[272,128]{1,0:T(8,128)(2,1)S(1)}, u32[]{:S(2)}, u32[]{:S(2)}) %collective-permute-start.8) | collective-permute-done | bytes 69664 | tf_op jit(solution)/shard_map/ppermute | solution.py:420
  25.4 2.8 %collective-permute-start.11 = (bf16[272,128]{1,0:T(8,128)(2,1)S(1)}, bf16[272,128]{1,0:T(8,128)(2,1)S(1)}, u32[]{:S(2)}, u32[]{:S(2)}) collective-permute-start(bf16[272,128]{1,0:T(8,128)(2,1)S(1)} %shard_map.76.a_ref), channel_id=1, source_target_pairs={{0,12},{4,8},{8,4},{12,0},{1,13},{5,9},{9,5},{13,1},{2,14},{6,10},... | collective-permute-start | bytes 208904 | tf_op jit(solution)/shard_map/ppermute | solution.py:420
  28.7 1.2 %collective-permute-start.9 = (bf16[272,128]{1,0:T(8,128)(2,1)S(1)}, bf16[272,128]{1,0:T(8,128)(2,1)S(1)}, u32[]{:S(2)}, u32[]{:S(2)}) collective-permute-start(bf16[272,128]{1,0:T(8,128)(2,1)S(1)} %shard_map.76.a_ref), channel_id=1, source_target_pairs={{0,4},{4,0},{8,12},{12,8},{1,5},{5,1},{9,13},{13,9},{2,6},{6,2},{1... | collective-permute-start | bytes 208904 | tf_op jit(solution)/shard_map/ppermute | solution.py:420
  29.9 2.5 %shard_map.73 = (bf16[128,2,8,128]{3,2,1,0:T(8,128)(2,1)}, f32[8,128]{1,0:T(8,128)S(1)}) custom-call(bf16[4,64,1280]{2,1,0:T(8,128)(2,1)S(1)} %get-tuple-element.39.hidden_ref, bf16[27,64,128]{2,1,0:T(8,128)(2,1)S(1)} %bitcast.7), custom_call_target="tpu_custom_call" | custom-call | flops 900000000 | bytes 1626112 | tf_op jit(solution)/shard_map/pallas_call | solution.py:18
  32.4 1.4 %collective-permute-done.10.c_ref = bf16[272,128]{1,0:T(8,128)(2,1)S(1)} collective-permute-done((bf16[272,128]{1,0:T(8,128)(2,1)S(1)}, bf16[272,128]{1,0:T(8,128)(2,1)S(1)}, u32[]{:S(2)}, u32[]{:S(2)}) %collective-permute-start.10) | collective-permute-done | bytes 69664 | tf_op jit(solution)/shard_map/ppermute | solution.py:420
  33.9 1.1 %collective-permute-start.12 = (bf16[272,128]{1,0:T(8,128)(2,1)S(1)}, bf16[272,128]{1,0:T(8,128)(2,1)S(1)}, u32[]{:S(2)}, u32[]{:S(2)}) collective-permute-start(bf16[272,128]{1,0:T(8,128)(2,1)S(1)} %shard_map.77.own_ref), channel_id=1, source_target_pairs={{0,2},{2,0},{1,3},{3,1},{4,6},{6,4},{5,7},{7,5},{8,10},{10,8},{9,1... | collective-permute-start | bytes 208904 | tf_op jit(solution)/shard_map/ppermute | solution.py:420
  35.0 3.2 %collective-permute-done.12.got_ref = bf16[272,128]{1,0:T(8,128)(2,1)S(1)} collective-permute-done((bf16[272,128]{1,0:T(8,128)(2,1)S(1)}, bf16[272,128]{1,0:T(8,128)(2,1)S(1)}, u32[]{:S(2)}, u32[]{:S(2)}) %collective-permute-start.12) | collective-permute-done | bytes 69664 | tf_op jit(solution)/shard_map/ppermute | solution.py:420
  38.3 0.9 %shard_map.79 = (f32[27,32,32]{2,1,0:T(8,128)}, f32[27,64,64]{2,1,0:T(8,128)}) custom-call(bf16[2,272,128]{2,1,0:T(8,128)(2,1)S(1)} %shard_map.78.in_ref), custom_call_target="tpu_custom_call" | custom-call | bytes 692224 | tf_op jit(solution)/shard_map/pallas_call | solution.py:18
  39.7 0.9 %shard_map.80 = (f32[27,32,32]{2,1,0:T(8,128)}, f32[27,64,64]{2,1,0:T(8,128)}) custom-call(bf16[2,272,128]{2,1,0:T(8,128)(2,1)S(1)} %collective-permute-done.13.in_ref, f32[27,32,32]{2,1,0:T(8,128)} %get-tuple-element.51.refs_0_, f32[27,64,64]{2,1,0:T(8,128)} %get-tuple-element.52.refs_1_), custom_call_target="tpu_custom_call", output_to_operand_aliasing={{0}: (1, {}), {1}: (2, {})} | custom-call | bytes 1245184 | tf_op jit(solution)/shard_map/pallas_call | solution.py:18
  (26 shorter events, 2.6 us)
Async XLA Ops:
  0.6 4.7 %copy-start = (bf16[1,128,2,8,128]{4,3,2,1,0:T(8,128)(2,1)S(1)}, bf16[1,128,2,8,128]{4,3,2,1,0:T(8,128)(2,1)}, u32[]{:S(2)}) copy-start(bf16[1,128,2,8,128]{4,3,2,1,0:T(8,128)(2,1)} %param.7) | copy-start | bytes 1572868
  0.6 4.7 %copy-start.1 = (bf16[27,128,64]{1,2,0:T(8,128)(2,1)S(1)}, bf16[27,128,64]{1,2,0:T(8,128)(2,1)}, u32[]{:S(2)}) copy-start(bf16[27,128,64]{1,2,0:T(8,128)(2,1)} %param.6) | copy-start | bytes 1327108
  0.7 7.0 %collective-permute-start.1 = (bf16[32,2,8,128]{3,2,1,0:T(8,128)(2,1)}, bf16[32,2,8,128]{3,2,1,0:T(8,128)(2,1)S(1)}, u32[]{:S(2)}, u32[]{:S(2)}) collective-permute-start(bf16[32,2,8,128]{3,2,1,0:T(8,128)(2,1)} %bitcast.9), channel_id=1, source_target_pairs={{0,16},{4,8},{8,4},{12,28},{16,0},{20,24},{24,20},{28,12},{1,17},{... | collective-permute-start | bytes 393224 | tf_op jit(solution)/shard_map/ppermute | solution.py:412
  3.7 5.2 %collective-permute-start = (bf16[32,2,8,128]{3,2,1,0:T(8,128)(2,1)}, bf16[32,2,8,128]{3,2,1,0:T(8,128)(2,1)S(1)}, u32[]{:S(2)}, u32[]{:S(2)}) collective-permute-start(bf16[32,2,8,128]{3,2,1,0:T(8,128)(2,1)} %bitcast.10), channel_id=1, source_target_pairs={{0,4},{4,0},{8,12},{12,8},{16,20},{20,16},{24,28},{28,24},{1,5},{5... | collective-permute-start | bytes 393224 | tf_op jit(solution)/shard_map/ppermute | solution.py:412
  5.3 1.8 %copy-start.2 = (bf16[27,64,32]{1,2,0:T(8,128)(2,1)S(1)}, bf16[27,64,32]{1,2,0:T(8,128)(2,1)}, u32[]{:S(2)}) copy-start(bf16[27,64,32]{1,2,0:T(8,128)(2,1)} %param.5) | copy-start | bytes 331780
  5.3 1.8 %copy-start.3 = (bf16[1,32,2,8,128]{4,3,2,1,0:T(8,128)(2,1)S(1)}, bf16[1,32,2,8,128]{4,3,2,1,0:T(8,128)(2,1)}, u32[]{:S(2)}) copy-start(bf16[1,32,2,8,128]{4,3,2,1,0:T(8,128)(2,1)} %param.4) | copy-start | bytes 393220
  9.1 4.7 %collective-permute-start.2 = (bf16[6,32,256]{2,1,0:T(8,128)(2,1)S(1)}, bf16[6,32,256]{2,1,0:T(8,128)(2,1)S(1)}, u32[]{:S(2)}, u32[]{:S(2)}) collective-permute-start(bf16[6,32,256]{2,1,0:T(8,128)(2,1)S(1)} %get-tuple-element.32), channel_id=1, source_target_pairs={{0,16},{1,2},{2,1},{3,19},{16,0},{17,18},{18,17},{19,3},{4,20},{5,... | collective-permute-start | bytes 294920 | tf_op jit(solution)/shard_map/ppermute | solution.py:412
  10.6 3.2 %collective-permute-start.3 = (bf16[6,32,256]{2,1,0:T(8,128)(2,1)S(1)}, bf16[6,32,256]{2,1,0:T(8,128)(2,1)S(1)}, u32[]{:S(2)}, u32[]{:S(2)}) collective-permute-start(bf16[6,32,256]{2,1,0:T(8,128)(2,1)S(1)} %get-tuple-element.33), channel_id=1, source_target_pairs={{0,1},{1,0},{2,3},{3,2},{16,17},{17,16},{18,19},{19,18},{4,5},{5,4... | collective-permute-start | bytes 294920 | tf_op jit(solution)/shard_map/ppermute | solution.py:412
  15.9 1.7 %collective-permute-start.5 = (bf16[2,2,216,128]{3,2,1,0:T(8,128)(2,1)S(1)}, bf16[2,2,216,128]{3,2,1,0:T(8,128)(2,1)S(1)}, u32[]{:S(2)}, u32[]{:S(2)}) collective-permute-start(bf16[2,2,216,128]{3,2,1,0:T(8,128)(2,1)S(1)} %get-tuple-element.45), channel_id=1, source_target_pairs={{0,1},{1,0},{2,3},{3,2},{4,5},{5,4},{6,7},{7,6},{8,9},{9,8},{10,11... | collective-permute-start | bytes 663560 | tf_op jit(solution)/shard_map/ppermute | solution.py:420
  16.0 1.6 %collective-permute-start.4 = (f32[2,2,56,128]{3,2,1,0:T(8,128)S(1)}, f32[2,2,56,128]{3,2,1,0:T(8,128)S(1)}, u32[]{:S(2)}, u32[]{:S(2)}) collective-permute-start(f32[2,2,56,128]{3,2,1,0:T(8,128)S(1)} %get-tuple-element.42), channel_id=1, source_target_pairs={{0,1},{1,0},{2,3},{3,2},{4,5},{5,4},{6,7},{7,6},{8,9},{9,8},{10,11... | collective-permute-start | bytes 344072 | tf_op jit(solution)/shard_map/ppermute | solution.py:420
  17.7 4.4 %collective-permute-start.6 = (bf16[272,128]{1,0:T(8,128)(2,1)S(1)}, bf16[272,128]{1,0:T(8,128)(2,1)S(1)}, u32[]{:S(2)}, u32[]{:S(2)}) collective-permute-start(bf16[272,128]{1,0:T(8,128)(2,1)S(1)} %get-tuple-element.47), channel_id=1, source_target_pairs={{0,16},{2,18},{16,0},{18,2},{1,17},{3,19},{17,1},{19,3},{4,20},{6,... | collective-permute-start | bytes 208904 | tf_op jit(solution)/shard_map/ppermute | solution.py:420
  19.2 5.1 %collective-permute-start.7 = (bf16[272,128]{1,0:T(8,128)(2,1)S(1)}, bf16[272,128]{1,0:T(8,128)(2,1)S(1)}, u32[]{:S(2)}, u32[]{:S(2)}) collective-permute-start(bf16[272,128]{1,0:T(8,128)(2,1)S(1)} %get-tuple-element.48), channel_id=1, source_target_pairs={{0,2},{2,0},{16,18},{18,16},{1,3},{3,1},{17,19},{19,17},{4,6},{6,4... | collective-permute-start | bytes 208904 | tf_op jit(solution)/shard_map/ppermute | solution.py:420
  20.1 5.2 %collective-permute-start.8 = (bf16[272,128]{1,0:T(8,128)(2,1)S(1)}, bf16[272,128]{1,0:T(8,128)(2,1)S(1)}, u32[]{:S(2)}, u32[]{:S(2)}) collective-permute-start(bf16[272,128]{1,0:T(8,128)(2,1)S(1)} %get-tuple-element.49), channel_id=1, source_target_pairs={{0,18},{2,16},{16,2},{18,0},{1,19},{3,17},{17,3},{19,1},{4,22},{6,... | collective-permute-start | bytes 208904 | tf_op jit(solution)/shard_map/ppermute | solution.py:420
  25.4 7.0 %collective-permute-start.11 = (bf16[272,128]{1,0:T(8,128)(2,1)S(1)}, bf16[272,128]{1,0:T(8,128)(2,1)S(1)}, u32[]{:S(2)}, u32[]{:S(2)}) collective-permute-start(bf16[272,128]{1,0:T(8,128)(2,1)S(1)} %shard_map.76.a_ref), channel_id=1, source_target_pairs={{0,12},{4,8},{8,4},{12,0},{1,13},{5,9},{9,5},{13,1},{2,14},{6,10},... | collective-permute-start | bytes 208904 | tf_op jit(solution)/shard_map/ppermute | solution.py:420
  28.2 5.6 %collective-permute-start.10 = (bf16[272,128]{1,0:T(8,128)(2,1)S(1)}, bf16[272,128]{1,0:T(8,128)(2,1)S(1)}, u32[]{:S(2)}, u32[]{:S(2)}) collective-permute-start(bf16[272,128]{1,0:T(8,128)(2,1)S(1)} %shard_map.76.a_ref), channel_id=1, source_target_pairs={{0,8},{4,12},{8,0},{12,4},{1,9},{5,13},{9,1},{13,5},{2,10},{6,14},... | collective-permute-start | bytes 208904 | tf_op jit(solution)/shard_map/ppermute | solution.py:420
  28.7 5.2 %collective-permute-start.9 = (bf16[272,128]{1,0:T(8,128)(2,1)S(1)}, bf16[272,128]{1,0:T(8,128)(2,1)S(1)}, u32[]{:S(2)}, u32[]{:S(2)}) collective-permute-start(bf16[272,128]{1,0:T(8,128)(2,1)S(1)} %shard_map.76.a_ref), channel_id=1, source_target_pairs={{0,4},{4,0},{8,12},{12,8},{1,5},{5,1},{9,13},{13,9},{2,6},{6,2},{1... | collective-permute-start | bytes 208904 | tf_op jit(solution)/shard_map/ppermute | solution.py:420
  33.9 4.4 %collective-permute-start.12 = (bf16[272,128]{1,0:T(8,128)(2,1)S(1)}, bf16[272,128]{1,0:T(8,128)(2,1)S(1)}, u32[]{:S(2)}, u32[]{:S(2)}) collective-permute-start(bf16[272,128]{1,0:T(8,128)(2,1)S(1)} %shard_map.77.own_ref), channel_id=1, source_target_pairs={{0,2},{2,0},{1,3},{3,1},{4,6},{6,4},{5,7},{7,5},{8,10},{10,8},{9,1... | collective-permute-start | bytes 208904 | tf_op jit(solution)/shard_map/ppermute | solution.py:420
  38.3 1.4 %collective-permute-start.13 = (bf16[2,272,128]{2,1,0:T(8,128)(2,1)S(1)}, bf16[2,272,128]{2,1,0:T(8,128)(2,1)S(1)}, u32[]{:S(2)}, u32[]{:S(2)}) collective-permute-start(bf16[2,272,128]{2,1,0:T(8,128)(2,1)S(1)} %shard_map.78.in_ref), channel_id=1, source_target_pairs={{0,1},{1,0},{2,3},{3,2},{4,5},{5,4},{6,7},{7,6},{8,9},{9,8},{10,11... | collective-permute-start | bytes 417800 | tf_op jit(solution)/shard_map/ppermute | solution.py:420

commit v20 on v18

--- a/solution.py
+++ b/solution.py
@@ -46,7 +46,7 @@
 def by_rows(ref, scratch, store):
     channels, depth, height, width = ref.shape
     rows = depth * height
-    scratch[...] = ref[...].astype(F32).reshape(channels * rows, width)
+    scratch[: channels * rows] = ref[...].astype(F32).reshape(channels * rows, width)
     for d in range(depth):
         for h in range(height):
             store(d, h, scratch[pl.ds(d * height + h, channels, stride=rows), :])
@@ -336,7 +336,7 @@
             for r in range(2):
                 row = total[:, r * LANES : (r + 1) * LANES]
                 scratch[pl.ds(d * height + h + r, out, stride=depth * height), :] = row
-    out_ref[...] = scratch[...].reshape(out_ref.shape).astype(BF)
+    out_ref[...] = scratch[: out * depth * height].reshape(out_ref.shape).astype(BF)
     token_ref[...] = scratch[:8]
 
 
@@ -372,10 +372,6 @@
     out_ref[...] = (one + two).astype(BF)
     rest = jnp.zeros((padded_ref.shape[0] - out_ref.shape[0], LANES), F32)
     padded_ref[...] = jnp.concatenate([one + two, rest], axis=0).astype(BF)
-
-
-def after_kernel(in_ref, _, out_ref):
-    out_ref[...] = in_ref[: out_ref.shape[0]]
 
 
 def write_kernel(count, wheres, *refs):
@@ -519,7 +515,7 @@
             shape((depth + 2, mid, cells + 2 * width), F32),
         ],
         [cotangent[0], k2, blank],
-        [pltpu.VMEM((out * rows, width), F32)],
+        [pltpu.VMEM(((out + 1) * rows, width), F32)],
         flops=1_100_000_000,
     )
     moved, w1, vol = call(
@@ -530,14 +526,14 @@
             shape((depth, inner, cells), BF),
         ],
         [cot_rows, k1, volume[0]],
-        [pltpu.VMEM((inner * rows, width), F32)],
+        [pltpu.VMEM(((inner + 1) * rows, width), F32)],
         flops=500_000_000,
     )
     deep, one, two = call(
         rim_kernel,
         [shape((3 * depth, inner, cells), BF)] + [shape((3 * depth, inner, 2 * width), BF)] * 2,
         [vol, one, two],
-        [pltpu.VMEM((inner * rows, width), F32)],
+        [pltpu.VMEM(((inner + 1) * rows, width), F32)],
     )
     one, two = swapped(one, HGT, 0), swapped(two, HGT, 1)
     size = mid // parts
@@ -600,12 +596,13 @@
         features_kernel,
         [shape(cotangent.shape[1:], BF), shape((8, width), F32)],
         [hidden, k2],
-        [pltpu.VMEM((out * rows, width), F32)],
+        [pltpu.VMEM(((out + 1) * rows, width), F32)],
         flops=900_000_000,
     )
     gots = [across(share, ("dep", bits)) for bits in (1, 2, 3)]
     share, for_y = call(depth_kernel, [shape(block, BF), shape((block[0] + 16, width), BF)], [share, *gots, token])
     other, far = across(share, ("core", 1)), across(for_y, ("y", 1))
+    far_other = across(for_y, ("y", 1), ("core", 1))
     if size % 16 == 0:
         outs = [shape((9, 3, size, inner), F32), shape((3, 9, 2 * size, mid), F32)]
 
@@ -629,13 +626,12 @@
                 aliases={count + n: n for n in range(len(before))},
             )
 
-        *grads, token = written([share, other], [(True, True), (False, True)])
-        (far,) = call(after_kernel, [shape(block, BF)], [far, token])
-        grads = written([far, across(far, ("core", 1))], [(True, False), (False, False)], grads)
+        *grads, _ = written([share, other], [(True, True), (False, True)])
+        grads = written([far_other, far], [(False, False), (True, False)], grads)
         grad_first, grad_second = (grad.reshape(27, *grad.shape[2:]) for grad in grads)
     else:
         core, y = lax.axis_index("core"), lax.axis_index("y")
-        stacked = jnp.stack([jnp.stack([share, far[: block[0]]]), jnp.stack([other, across(far[: block[0]], ("core", 1))])])
+        stacked = jnp.stack([jnp.stack([share, far[: block[0]]]), jnp.stack([other, far_other[: block[0]]])])
         quarters = [
             [stacked[lax.bitwise_xor(core, c), lax.bitwise_xor(y, h)] for h in range(2)] for c in range(2)
         ]

time: 40.7 us -> 40.7 us (level)
  waiting for transfers between devices: 11.8 us -> 10.1 us
  starting transfers between devices: 16.1 us -> 17.1 us
  Pallas kernels: 11.9 us -> 12.5 us
    ppermute x11, waiting for transfers between devices: 10.2 us -> 8.55 us  [across(): lax.ppermute(x, axes, [(i, i ^ flip) for i in range(lax.axis_size(axes))])]
    ppermute x11, starting transfers between devices: 9.72 us -> 10.8 us  [across(): lax.ppermute(x, axes, [(i, i ^ flip) for i in range(lax.axis_size(axes))])]
    pallas_call x14 -> x13, Pallas kernels: 11.9 us -> 12.5 us  [call(): pl.pallas_call(body, out_shape=outs, in_specs=[pl.BlockSpec(memory_space=...]
  transfers between devices with their start and end apart: 15 -> 15, of which waited for: 10 -> 10; matrix products, arithmetic and copies ran while one was open for 0% -> 0% of each run, Pallas kernels for 21% -> 22%
where the time goes in v20:
time: 40.7 us; the launch traced here: 40.5 us
  starting transfers between devices  17.1 us (42%)
  Pallas kernels  12.5 us (31%)
  waiting for transfers between devices  10.1 us (25%)
  between operations  0.78 us (2%)
    pallas_call x13, Pallas kernels, call(): pl.pallas_call(body, out_shape=outs, in_specs=[pl.BlockSpec(memory_space=...  12.5 us
    ppermute x11, starting transfers between devices, across(): lax.ppermute(x, axes, [(i, i ^ flip) for i in range(lax.axis_size(axes))])  10.8 us
    ppermute x11, waiting for transfers between devices, across(): lax.ppermute(x, axes, [(i, i ^ flip) for i in range(lax.axis_size(axes))])  8.55 us
    ppermute x4, starting transfers between devices, swapped(): return lax.ppermute(x, ('dp', *axes), list(enumerate(partner)))  6.36 us
    ppermute x4, waiting for transfers between devices, swapped(): return lax.ppermute(x, ('dp', *axes), list(enumerate(partner)))  1.58 us
  transfers between devices with their start and end apart: 15, of which 10 were waited for; matrix products, arithmetic and copies ran while one was open for 0% of the time, Pallas kernels for 22%

profile of v20, /device:TPU:0, one launch (start us, length us, event | category | flops | bytes accessed | tf_op | source)
XLA Modules:
  0.0 40.5 jit_solution(15492551520392117882)
XLA Ops:
  0.7 3.0 %collective-permute-start.1 = (bf16[32,2,8,128]{3,2,1,0:T(8,128)(2,1)}, bf16[32,2,8,128]{3,2,1,0:T(8,128)(2,1)S(1)}, u32[]{:S(2)}, u32[]{:S(2)}) collective-permute-start(bf16[32,2,8,128]{3,2,1,0:T(8,128)(2,1)} %bitcast.11), channel_id=1, source_target_pairs={{0,16},{4,8},{8,4},{12,28},{16,0},{20,24},{24,20},{28,12},{1,17},{... | collective-permute-start | bytes 393224 | tf_op jit(solution)/shard_map/ppermute | solution.py:457
  3.7 1.7 %collective-permute-start = (bf16[32,2,8,128]{3,2,1,0:T(8,128)(2,1)}, bf16[32,2,8,128]{3,2,1,0:T(8,128)(2,1)S(1)}, u32[]{:S(2)}, u32[]{:S(2)}) collective-permute-start(bf16[32,2,8,128]{3,2,1,0:T(8,128)(2,1)} %bitcast.12), channel_id=1, source_target_pairs={{0,4},{4,0},{8,12},{12,8},{16,20},{20,16},{24,28},{28,24},{1,5},{5... | collective-permute-start | bytes 393224 | tf_op jit(solution)/shard_map/ppermute | solution.py:457
  5.4 1.7 %shard_map.68 = (bf16[2,128,1024]{2,1,0:T(8,128)(2,1)S(1)}, f32[4,64,1280]{2,1,0:T(8,128)S(1)}) custom-call(bf16[128,2,8,128]{3,2,1,0:T(8,128)(2,1)S(1)} %bitcast.7, bf16[27,64,128]{2,1,0:T(8,128)(2,1)S(1)} %bitcast.8, bf16[128,256]{1,0:T(8,128)(2,1)S(1)} %shard_map.67.blank_ref), custom_call_target="tpu_custom_call" | custom-call | flops 1100000000 | bytes 2867200 | tf_op jit(solution)/shard_map/pallas_call | solution.py:18
  7.6 1.2 %collective-permute-done.one_ref = bf16[32,2,8,128]{3,2,1,0:T(8,128)(2,1)S(1)} collective-permute-done((bf16[32,2,8,128]{3,2,1,0:T(8,128)(2,1)}, bf16[32,2,8,128]{3,2,1,0:T(8,128)(2,1)S(1)}, u32[]{:S(2)}, u32[]{:S(2)}) %collective-permute-start) | collective-permute-done | bytes 131104 | tf_op jit(solution)/shard_map/ppermute | solution.py:457
  9.1 1.5 %collective-permute-start.2 = (bf16[6,32,256]{2,1,0:T(8,128)(2,1)S(1)}, bf16[6,32,256]{2,1,0:T(8,128)(2,1)S(1)}, u32[]{:S(2)}, u32[]{:S(2)}) collective-permute-start(bf16[6,32,256]{2,1,0:T(8,128)(2,1)S(1)} %get-tuple-element.34), channel_id=1, source_target_pairs={{0,16},{1,2},{2,1},{3,19},{16,0},{17,18},{18,17},{19,3},{4,20},{5,... | collective-permute-start | bytes 294920 | tf_op jit(solution)/shard_map/ppermute | solution.py:457
  10.8 2.6 %shard_map.71 = (bf16[4,64,768]{2,1,0:T(8,128)(2,1)S(1)}, f32[1152,192]{1,0:T(8,128)S(1)}, f32[192,288]{1,0:T(8,128)S(1)}) custom-call(bf16[6,32,1024]{2,1,0:T(8,128)(2,1)S(1)} %get-tuple-element.33.deep_ref, bf16[192,288]{1,0:T(8,128)(2,1)S(1)} %get-tuple-element.36.w1_ref, bf16[2,384,1024]{2,1,0:T(8,128)(2,1)S(1)} %get-tuple-element.38.moved_ref, ...), custom_call_target="tpu_custom_call" | custom-call | flops 1500000000 | bytes 4886528 | tf_op jit(solution)/shard_map/pallas_call | solution.py:18
  13.8 1.5 %shard_map.72 = (bf16[4,64,1280]{2,1,0:T(8,128)(2,1)S(1)}, f32[2,2,64,128]{3,2,1,0:T(8,128)S(1)}, f32[2,2,64,128]{3,2,1,0:T(8,128)S(1)}) custom-call(bf16[6,32,1024]{2,1,0:T(8,128)(2,1)S(1)} %get-tuple-element.33.deep_ref, bf16[6,32,256]{2,1,0:T(8,128)(2,1)S(1)} %collective-permute-done.2.two_ref, bf16[6,32,256]{2,1,0:T(8,128)(2,1)S(1)} %collective-permute-done.3.one_ref, ...), custom_call_target="tpu_custom_call" | custom-call | flops 1000000000 | bytes 3543040 | tf_op jit(solution)/shard_map/pallas_call | solution.py:18
  16.5 1.2 %collective-permute-done.5.refs_3_ = f32[2,2,64,128]{3,2,1,0:T(8,128)S(1)} collective-permute-done((f32[2,2,64,128]{3,2,1,0:T(8,128)S(1)}, f32[2,2,64,128]{3,2,1,0:T(8,128)S(1)}, u32[]{:S(2)}, u32[]{:S(2)}) %collective-permute-start.5) | collective-permute-done | bytes 131104 | tf_op jit(solution)/shard_map/ppermute | solution.py:465
  17.7 1.5 %collective-permute-start.6 = (bf16[272,128]{1,0:T(8,128)(2,1)S(1)}, bf16[272,128]{1,0:T(8,128)(2,1)S(1)}, u32[]{:S(2)}, u32[]{:S(2)}) collective-permute-start(bf16[272,128]{1,0:T(8,128)(2,1)S(1)} %get-tuple-element.49), channel_id=1, source_target_pairs={{0,16},{2,18},{16,0},{18,2},{1,17},{3,19},{17,1},{19,3},{4,20},{6,... | collective-permute-start | bytes 208904 | tf_op jit(solution)/shard_map/ppermute | solution.py:465
  19.2 0.9 %collective-permute-start.7 = (bf16[272,128]{1,0:T(8,128)(2,1)S(1)}, bf16[272,128]{1,0:T(8,128)(2,1)S(1)}, u32[]{:S(2)}, u32[]{:S(2)}) collective-permute-start(bf16[272,128]{1,0:T(8,128)(2,1)S(1)} %get-tuple-element.50), channel_id=1, source_target_pairs={{0,2},{2,0},{16,18},{18,16},{1,3},{3,1},{17,19},{19,17},{4,6},{6,4... | collective-permute-start | bytes 208904 | tf_op jit(solution)/shard_map/ppermute | solution.py:465
  20.2 1.1 %collective-permute-start.8 = (bf16[272,128]{1,0:T(8,128)(2,1)S(1)}, bf16[272,128]{1,0:T(8,128)(2,1)S(1)}, u32[]{:S(2)}, u32[]{:S(2)}) collective-permute-start(bf16[272,128]{1,0:T(8,128)(2,1)S(1)} %get-tuple-element.51), channel_id=1, source_target_pairs={{0,18},{2,16},{16,2},{18,0},{1,19},{3,17},{17,3},{19,1},{4,22},{6,... | collective-permute-start | bytes 208904 | tf_op jit(solution)/shard_map/ppermute | solution.py:465
  21.3 0.8 %collective-permute-done.6.refs_0_ = bf16[272,128]{1,0:T(8,128)(2,1)S(1)} collective-permute-done((bf16[272,128]{1,0:T(8,128)(2,1)S(1)}, bf16[272,128]{1,0:T(8,128)(2,1)S(1)}, u32[]{:S(2)}, u32[]{:S(2)}) %collective-permute-start.6) | collective-permute-done | bytes 69664 | tf_op jit(solution)/shard_map/ppermute | solution.py:465
  22.1 2.2 %collective-permute-done.7.refs_1_ = bf16[272,128]{1,0:T(8,128)(2,1)S(1)} collective-permute-done((bf16[272,128]{1,0:T(8,128)(2,1)S(1)}, bf16[272,128]{1,0:T(8,128)(2,1)S(1)}, u32[]{:S(2)}, u32[]{:S(2)}) %collective-permute-start.7) | collective-permute-done | bytes 69664 | tf_op jit(solution)/shard_map/ppermute | solution.py:465
  24.3 1.1 %collective-permute-done.8.refs_2_ = bf16[272,128]{1,0:T(8,128)(2,1)S(1)} collective-permute-done((bf16[272,128]{1,0:T(8,128)(2,1)S(1)}, bf16[272,128]{1,0:T(8,128)(2,1)S(1)}, u32[]{:S(2)}, u32[]{:S(2)}) %collective-permute-start.8) | collective-permute-done | bytes 69664 | tf_op jit(solution)/shard_map/ppermute | solution.py:465
  25.4 2.8 %collective-permute-start.11 = (bf16[272,128]{1,0:T(8,128)(2,1)S(1)}, bf16[272,128]{1,0:T(8,128)(2,1)S(1)}, u32[]{:S(2)}, u32[]{:S(2)}) collective-permute-start(bf16[272,128]{1,0:T(8,128)(2,1)S(1)} %shard_map.76.a_ref), channel_id=1, source_target_pairs={{0,12},{4,8},{8,4},{12,0},{1,13},{5,9},{9,5},{13,1},{2,14},{6,10},... | collective-permute-start | bytes 208904 | tf_op jit(solution)/shard_map/ppermute | solution.py:465
  28.7 1.2 %collective-permute-start.9 = (bf16[272,128]{1,0:T(8,128)(2,1)S(1)}, bf16[272,128]{1,0:T(8,128)(2,1)S(1)}, u32[]{:S(2)}, u32[]{:S(2)}) collective-permute-start(bf16[272,128]{1,0:T(8,128)(2,1)S(1)} %shard_map.76.a_ref), channel_id=1, source_target_pairs={{0,4},{4,0},{8,12},{12,8},{1,5},{5,1},{9,13},{13,9},{2,6},{6,2},{1... | collective-permute-start | bytes 208904 | tf_op jit(solution)/shard_map/ppermute | solution.py:465
  29.9 2.5 %shard_map.73 = (bf16[128,2,8,128]{3,2,1,0:T(8,128)(2,1)}, f32[8,128]{1,0:T(8,128)S(1)}) custom-call(bf16[4,64,1280]{2,1,0:T(8,128)(2,1)S(1)} %get-tuple-element.41.hidden_ref, bf16[27,64,128]{2,1,0:T(8,128)(2,1)S(1)} %bitcast.9), custom_call_target="tpu_custom_call" | custom-call | flops 900000000 | bytes 1626112 | tf_op jit(solution)/shard_map/pallas_call | solution.py:18
  32.4 1.4 %collective-permute-done.10.c_ref = bf16[272,128]{1,0:T(8,128)(2,1)S(1)} collective-permute-done((bf16[272,128]{1,0:T(8,128)(2,1)S(1)}, bf16[272,128]{1,0:T(8,128)(2,1)S(1)}, u32[]{:S(2)}, u32[]{:S(2)}) %collective-permute-start.10) | collective-permute-done | bytes 69664 | tf_op jit(solution)/shard_map/ppermute | solution.py:465
  33.9 1.1 %collective-permute-start.13 = (bf16[288,128]{1,0:T(8,128)(2,1)S(1)}, bf16[288,128]{1,0:T(8,128)(2,1)S(1)}, u32[]{:S(2)}, u32[]{:S(2)}) collective-permute-start(bf16[288,128]{1,0:T(8,128)(2,1)S(1)} %get-tuple-element.53), channel_id=1, source_target_pairs={{0,2},{2,0},{1,3},{3,1},{4,6},{6,4},{5,7},{7,5},{8,10},{10,8},{9,1... | collective-permute-start | bytes 221192 | tf_op jit(solution)/shard_map/ppermute | solution.py:465
  35.0 1.1 %collective-permute-start.14 = (bf16[272,128]{1,0:T(8,128)(2,1)S(1)}, bf16[272,128]{1,0:T(8,128)(2,1)S(1)}, u32[]{:S(2)}, u32[]{:S(2)}) collective-permute-start(bf16[272,128]{1,0:T(8,128)(2,1)S(1)} %get-tuple-element.54.refs_0_), channel_id=1, source_target_pairs={{0,1},{1,0},{2,3},{3,2},{4,5},{5,4},{6,7},{7,6},{8,9},{9,8},{10,11... | collective-permute-start | bytes 208904 | tf_op jit(solution)/shard_map/ppermute | solution.py:465
  36.1 0.9 %collective-permute-done.14.refs_1_ = bf16[272,128]{1,0:T(8,128)(2,1)S(1)} collective-permute-done((bf16[272,128]{1,0:T(8,128)(2,1)S(1)}, bf16[272,128]{1,0:T(8,128)(2,1)S(1)}, u32[]{:S(2)}, u32[]{:S(2)}) %collective-permute-start.14) | collective-permute-done | bytes 69664 | tf_op jit(solution)/shard_map/ppermute | solution.py:465
  37.0 1.6 %shard_map.78 = (f32[9,3,32,32]{3,2,1,0:T(8,128)}, f32[3,9,64,64]{3,2,1,0:T(8,128)}, f32[8,128]{1,0:T(8,128)}) custom-call(bf16[272,128]{1,0:T(8,128)(2,1)S(1)} %get-tuple-element.54.refs_0_, bf16[272,128]{1,0:T(8,128)(2,1)S(1)} %collective-permute-done.14.refs_1_), custom_call_target="tpu_custom_call" | custom-call | bytes 696320 | tf_op jit(solution)/shard_map/pallas_call | solution.py:18
  38.7 0.9 %collective-permute-done.12.refs_0_ = bf16[288,128]{1,0:T(8,128)(2,1)S(1)} collective-permute-done((bf16[288,128]{1,0:T(8,128)(2,1)S(1)}, bf16[288,128]{1,0:T(8,128)(2,1)S(1)}, u32[]{:S(2)}, u32[]{:S(2)}) %collective-permute-start.12) | collective-permute-done | bytes 73760 | tf_op jit(solution)/shard_map/ppermute | solution.py:465
  39.5 1.0 %shard_map.79 = (f32[9,3,32,32]{3,2,1,0:T(8,128)}, f32[3,9,64,64]{3,2,1,0:T(8,128)}) custom-call(bf16[288,128]{1,0:T(8,128)(2,1)S(1)} %collective-permute-done.12.refs_0_, bf16[288,128]{1,0:T(8,128)(2,1)S(1)} %collective-permute-done.13.refs_1_, f32[9,3,32,32]{3,2,1,0:T(8,128)} %get-tuple-element.55.refs_2_, ...), custom_call_target="tpu_custom_call", output_to_operand_aliasing={{0}: (2, {}), {1}: (3, {})} | custom-call | bytes 1253376 | tf_op jit(solution)/shard_map/pallas_call | solution.py:18
  (27 shorter events, 3.3 us)
Async XLA Ops:
  0.6 4.7 %copy-start = (bf16[1,128,2,8,128]{4,3,2,1,0:T(8,128)(2,1)S(1)}, bf16[1,128,2,8,128]{4,3,2,1,0:T(8,128)(2,1)}, u32[]{:S(2)}) copy-start(bf16[1,128,2,8,128]{4,3,2,1,0:T(8,128)(2,1)} %param.7) | copy-start | bytes 1572868
  0.6 4.7 %copy-start.1 = (bf16[27,128,64]{1,2,0:T(8,128)(2,1)S(1)}, bf16[27,128,64]{1,2,0:T(8,128)(2,1)}, u32[]{:S(2)}) copy-start(bf16[27,128,64]{1,2,0:T(8,128)(2,1)} %param.6) | copy-start | bytes 1327108
  0.7 7.0 %collective-permute-start.1 = (bf16[32,2,8,128]{3,2,1,0:T(8,128)(2,1)}, bf16[32,2,8,128]{3,2,1,0:T(8,128)(2,1)S(1)}, u32[]{:S(2)}, u32[]{:S(2)}) collective-permute-start(bf16[32,2,8,128]{3,2,1,0:T(8,128)(2,1)} %bitcast.11), channel_id=1, source_target_pairs={{0,16},{4,8},{8,4},{12,28},{16,0},{20,24},{24,20},{28,12},{1,17},{... | collective-permute-start | bytes 393224 | tf_op jit(solution)/shard_map/ppermute | solution.py:457
  3.7 5.2 %collective-permute-start = (bf16[32,2,8,128]{3,2,1,0:T(8,128)(2,1)}, bf16[32,2,8,128]{3,2,1,0:T(8,128)(2,1)S(1)}, u32[]{:S(2)}, u32[]{:S(2)}) collective-permute-start(bf16[32,2,8,128]{3,2,1,0:T(8,128)(2,1)} %bitcast.12), channel_id=1, source_target_pairs={{0,4},{4,0},{8,12},{12,8},{16,20},{20,16},{24,28},{28,24},{1,5},{5... | collective-permute-start | bytes 393224 | tf_op jit(solution)/shard_map/ppermute | solution.py:457
  5.3 1.8 %copy-start.2 = (bf16[27,64,32]{1,2,0:T(8,128)(2,1)S(1)}, bf16[27,64,32]{1,2,0:T(8,128)(2,1)}, u32[]{:S(2)}) copy-start(bf16[27,64,32]{1,2,0:T(8,128)(2,1)} %param.5) | copy-start | bytes 331780
  5.3 1.8 %copy-start.3 = (bf16[1,32,2,8,128]{4,3,2,1,0:T(8,128)(2,1)S(1)}, bf16[1,32,2,8,128]{4,3,2,1,0:T(8,128)(2,1)}, u32[]{:S(2)}) copy-start(bf16[1,32,2,8,128]{4,3,2,1,0:T(8,128)(2,1)} %param.4) | copy-start | bytes 393220
  9.1 4.7 %collective-permute-start.2 = (bf16[6,32,256]{2,1,0:T(8,128)(2,1)S(1)}, bf16[6,32,256]{2,1,0:T(8,128)(2,1)S(1)}, u32[]{:S(2)}, u32[]{:S(2)}) collective-permute-start(bf16[6,32,256]{2,1,0:T(8,128)(2,1)S(1)} %get-tuple-element.34), channel_id=1, source_target_pairs={{0,16},{1,2},{2,1},{3,19},{16,0},{17,18},{18,17},{19,3},{4,20},{5,... | collective-permute-start | bytes 294920 | tf_op jit(solution)/shard_map/ppermute | solution.py:457
  10.6 3.2 %collective-permute-start.3 = (bf16[6,32,256]{2,1,0:T(8,128)(2,1)S(1)}, bf16[6,32,256]{2,1,0:T(8,128)(2,1)S(1)}, u32[]{:S(2)}, u32[]{:S(2)}) collective-permute-start(bf16[6,32,256]{2,1,0:T(8,128)(2,1)S(1)} %get-tuple-element.35), channel_id=1, source_target_pairs={{0,1},{1,0},{2,3},{3,2},{16,17},{17,16},{18,19},{19,18},{4,5},{5,4... | collective-permute-start | bytes 294920 | tf_op jit(solution)/shard_map/ppermute | solution.py:457
  15.9 1.7 %collective-permute-start.4 = (bf16[2,2,224,128]{3,2,1,0:T(8,128)(2,1)S(1)}, bf16[2,2,224,128]{3,2,1,0:T(8,128)(2,1)S(1)}, u32[]{:S(2)}, u32[]{:S(2)}) collective-permute-start(bf16[2,2,224,128]{3,2,1,0:T(8,128)(2,1)S(1)} %get-tuple-element.45), channel_id=1, source_target_pairs={{0,1},{1,0},{2,3},{3,2},{4,5},{5,4},{6,7},{7,6},{8,9},{9,8},{10,11... | collective-permute-start | bytes 688136 | tf_op jit(solution)/shard_map/ppermute | solution.py:465
  16.0 1.7 %collective-permute-start.5 = (f32[2,2,64,128]{3,2,1,0:T(8,128)S(1)}, f32[2,2,64,128]{3,2,1,0:T(8,128)S(1)}, u32[]{:S(2)}, u32[]{:S(2)}) collective-permute-start(f32[2,2,64,128]{3,2,1,0:T(8,128)S(1)} %get-tuple-element.47), channel_id=1, source_target_pairs={{0,1},{1,0},{2,3},{3,2},{4,5},{5,4},{6,7},{7,6},{8,9},{9,8},{10,11... | collective-permute-start | bytes 393224 | tf_op jit(solution)/shard_map/ppermute | solution.py:465
  17.7 4.4 %collective-permute-start.6 = (bf16[272,128]{1,0:T(8,128)(2,1)S(1)}, bf16[272,128]{1,0:T(8,128)(2,1)S(1)}, u32[]{:S(2)}, u32[]{:S(2)}) collective-permute-start(bf16[272,128]{1,0:T(8,128)(2,1)S(1)} %get-tuple-element.49), channel_id=1, source_target_pairs={{0,16},{2,18},{16,0},{18,2},{1,17},{3,19},{17,1},{19,3},{4,20},{6,... | collective-permute-start | bytes 208904 | tf_op jit(solution)/shard_map/ppermute | solution.py:465
  19.2 5.1 %collective-permute-start.7 = (bf16[272,128]{1,0:T(8,128)(2,1)S(1)}, bf16[272,128]{1,0:T(8,128)(2,1)S(1)}, u32[]{:S(2)}, u32[]{:S(2)}) collective-permute-start(bf16[272,128]{1,0:T(8,128)(2,1)S(1)} %get-tuple-element.50), channel_id=1, source_target_pairs={{0,2},{2,0},{16,18},{18,16},{1,3},{3,1},{17,19},{19,17},{4,6},{6,4... | collective-permute-start | bytes 208904 | tf_op jit(solution)/shard_map/ppermute | solution.py:465
  20.2 5.2 %collective-permute-start.8 = (bf16[272,128]{1,0:T(8,128)(2,1)S(1)}, bf16[272,128]{1,0:T(8,128)(2,1)S(1)}, u32[]{:S(2)}, u32[]{:S(2)}) collective-permute-start(bf16[272,128]{1,0:T(8,128)(2,1)S(1)} %get-tuple-element.51), channel_id=1, source_target_pairs={{0,18},{2,16},{16,2},{18,0},{1,19},{3,17},{17,3},{19,1},{4,22},{6,... | collective-permute-start | bytes 208904 | tf_op jit(solution)/shard_map/ppermute | solution.py:465
  25.4 7.0 %collective-permute-start.11 = (bf16[272,128]{1,0:T(8,128)(2,1)S(1)}, bf16[272,128]{1,0:T(8,128)(2,1)S(1)}, u32[]{:S(2)}, u32[]{:S(2)}) collective-permute-start(bf16[272,128]{1,0:T(8,128)(2,1)S(1)} %shard_map.76.a_ref), channel_id=1, source_target_pairs={{0,12},{4,8},{8,4},{12,0},{1,13},{5,9},{9,5},{13,1},{2,14},{6,10},... | collective-permute-start | bytes 208904 | tf_op jit(solution)/shard_map/ppermute | solution.py:465
  28.2 5.6 %collective-permute-start.10 = (bf16[272,128]{1,0:T(8,128)(2,1)S(1)}, bf16[272,128]{1,0:T(8,128)(2,1)S(1)}, u32[]{:S(2)}, u32[]{:S(2)}) collective-permute-start(bf16[272,128]{1,0:T(8,128)(2,1)S(1)} %shard_map.76.a_ref), channel_id=1, source_target_pairs={{0,8},{4,12},{8,0},{12,4},{1,9},{5,13},{9,1},{13,5},{2,10},{6,14},... | collective-permute-start | bytes 208904 | tf_op jit(solution)/shard_map/ppermute | solution.py:465
  28.7 5.2 %collective-permute-start.9 = (bf16[272,128]{1,0:T(8,128)(2,1)S(1)}, bf16[272,128]{1,0:T(8,128)(2,1)S(1)}, u32[]{:S(2)}, u32[]{:S(2)}) collective-permute-start(bf16[272,128]{1,0:T(8,128)(2,1)S(1)} %shard_map.76.a_ref), channel_id=1, source_target_pairs={{0,4},{4,0},{8,12},{12,8},{1,5},{5,1},{9,13},{13,9},{2,6},{6,2},{1... | collective-permute-start | bytes 208904 | tf_op jit(solution)/shard_map/ppermute | solution.py:465
  33.9 4.8 %collective-permute-start.13 = (bf16[288,128]{1,0:T(8,128)(2,1)S(1)}, bf16[288,128]{1,0:T(8,128)(2,1)S(1)}, u32[]{:S(2)}, u32[]{:S(2)}) collective-permute-start(bf16[288,128]{1,0:T(8,128)(2,1)S(1)} %get-tuple-element.53), channel_id=1, source_target_pairs={{0,2},{2,0},{1,3},{3,1},{4,6},{6,4},{5,7},{7,5},{8,10},{10,8},{9,1... | collective-permute-start | bytes 221192 | tf_op jit(solution)/shard_map/ppermute | solution.py:465
  35.0 4.5 %collective-permute-start.12 = (bf16[288,128]{1,0:T(8,128)(2,1)S(1)}, bf16[288,128]{1,0:T(8,128)(2,1)S(1)}, u32[]{:S(2)}, u32[]{:S(2)}) collective-permute-start(bf16[288,128]{1,0:T(8,128)(2,1)S(1)} %get-tuple-element.53), channel_id=1, source_target_pairs={{0,3},{1,2},{2,1},{3,0},{4,7},{5,6},{6,5},{7,4},{8,11},{9,10},{10,... | collective-permute-start | bytes 221192 | tf_op jit(solution)/shard_map/ppermute | solution.py:465
  35.0 2.0 %collective-permute-start.14 = (bf16[272,128]{1,0:T(8,128)(2,1)S(1)}, bf16[272,128]{1,0:T(8,128)(2,1)S(1)}, u32[]{:S(2)}, u32[]{:S(2)}) collective-permute-start(bf16[272,128]{1,0:T(8,128)(2,1)S(1)} %get-tuple-element.54.refs_0_), channel_id=1, source_target_pairs={{0,1},{1,0},{2,3},{3,2},{4,5},{5,4},{6,7},{7,6},{8,9},{9,8},{10,11... | collective-permute-start | bytes 208904 | tf_op jit(solution)/shard_map/ppermute | solution.py:465

commit v21 on v20

--- a/solution.py
+++ b/solution.py
@@ -378,11 +378,7 @@
     n_scratch = 6
     in_refs = refs[:count]
     out_refs, scratch = refs[: -n_scratch * count], refs[-n_scratch * count :]
-    if wheres[0][1]:
-        first_ref, second_ref, token_ref = out_refs[-3:]
-        token_ref[...] = jnp.zeros(token_ref.shape, F32)
-    else:
-        first_ref, second_ref = out_refs[-2:]
+    first_ref, second_ref = out_refs[-2:]
     core, y = lax.axis_index("core"), lax.axis_index("y")
 
     def begun(n, half):
@@ -618,7 +614,7 @@
             count = len(quarters)
             return call(
                 functools.partial(write_kernel, count, wheres),
-                outs if before else [*outs, shape((8, width), F32)],
+                outs,
                 [*quarters, *before],
                 scratch * count,
                 far=range(count, count + len(before)),
@@ -626,7 +622,7 @@
                 aliases={count + n: n for n in range(len(before))},
             )
 
-        *grads, _ = written([share, other], [(True, True), (False, True)])
+        grads = written([share, other], [(True, True), (False, True)])
         grads = written([far_other, far], [(False, False), (True, False)], grads)
         grad_first, grad_second = (grad.reshape(27, *grad.shape[2:]) for grad in grads)
     else:

time: 40.7 us -> 40.7 us (level)
  Pallas kernels: 12.5 us -> 11.9 us
  waiting for transfers between devices: 10.1 us -> 10.7 us
    ppermute x11, waiting for transfers between devices: 8.55 us -> 9.14 us  [across(): lax.ppermute(x, axes, [(i, i ^ flip) for i in range(lax.axis_size(axes))])]
    pallas_call x13, Pallas kernels: 12.5 us -> 11.9 us  [call(): pl.pallas_call(body, out_shape=outs, in_specs=[pl.BlockSpec(memory_space=...]
  transfers between devices with their start and end apart: 15 -> 15, of which waited for: 10 -> 10; matrix products, arithmetic and copies ran while one was open for 0% -> 0% of each run, Pallas kernels for 22% -> 21%
where the time goes in v21:
time: 40.7 us; the launch traced here: 40.5 us
  starting transfers between devices  17.1 us (42%)
  Pallas kernels  11.9 us (29%)
  waiting for transfers between devices  10.7 us (26%)
  between operations  0.78 us (2%)
    pallas_call x13, Pallas kernels, call(): pl.pallas_call(body, out_shape=outs, in_specs=[pl.BlockSpec(memory_space=...  11.9 us
    ppermute x11, starting transfers between devices, across(): lax.ppermute(x, axes, [(i, i ^ flip) for i in range(lax.axis_size(axes))])  10.8 us
    ppermute x11, waiting for transfers between devices, across(): lax.ppermute(x, axes, [(i, i ^ flip) for i in range(lax.axis_size(axes))])  9.14 us
    ppermute x4, starting transfers between devices, swapped(): return lax.ppermute(x, ('dp', *axes), list(enumerate(partner)))  6.36 us
    ppermute x4, waiting for transfers between devices, swapped(): return lax.ppermute(x, ('dp', *axes), list(enumerate(partner)))  1.58 us
  transfers between devices with their start and end apart: 15, of which 10 were waited for; matrix products, arithmetic and copies ran while one was open for 0% of the time, Pallas kernels for 21%

profile of v21, /device:TPU:0, one launch (start us, length us, event | category | flops | bytes accessed | tf_op | source)
XLA Modules:
  0.0 40.5 jit_solution(3182382244251109267)
XLA Ops:
  0.7 3.0 %collective-permute-start.1 = (bf16[32,2,8,128]{3,2,1,0:T(8,128)(2,1)}, bf16[32,2,8,128]{3,2,1,0:T(8,128)(2,1)S(1)}, u32[]{:S(2)}, u32[]{:S(2)}) collective-permute-start(bf16[32,2,8,128]{3,2,1,0:T(8,128)(2,1)} %bitcast.11), channel_id=1, source_target_pairs={{0,16},{4,8},{8,4},{12,28},{16,0},{20,24},{24,20},{28,12},{1,17},{... | collective-permute-start | bytes 393224 | tf_op jit(solution)/shard_map/ppermute | solution.py:453
  3.7 1.7 %collective-permute-start = (bf16[32,2,8,128]{3,2,1,0:T(8,128)(2,1)}, bf16[32,2,8,128]{3,2,1,0:T(8,128)(2,1)S(1)}, u32[]{:S(2)}, u32[]{:S(2)}) collective-permute-start(bf16[32,2,8,128]{3,2,1,0:T(8,128)(2,1)} %bitcast.12), channel_id=1, source_target_pairs={{0,4},{4,0},{8,12},{12,8},{16,20},{20,16},{24,28},{28,24},{1,5},{5... | collective-permute-start | bytes 393224 | tf_op jit(solution)/shard_map/ppermute | solution.py:453
  5.4 1.7 %shard_map.68 = (bf16[2,128,1024]{2,1,0:T(8,128)(2,1)S(1)}, f32[4,64,1280]{2,1,0:T(8,128)S(1)}) custom-call(bf16[128,2,8,128]{3,2,1,0:T(8,128)(2,1)S(1)} %bitcast.7, bf16[27,64,128]{2,1,0:T(8,128)(2,1)S(1)} %bitcast.8, bf16[128,256]{1,0:T(8,128)(2,1)S(1)} %shard_map.67.blank_ref), custom_call_target="tpu_custom_call" | custom-call | flops 1100000000 | bytes 2867200 | tf_op jit(solution)/shard_map/pallas_call | solution.py:18
  7.6 1.2 %collective-permute-done.one_ref = bf16[32,2,8,128]{3,2,1,0:T(8,128)(2,1)S(1)} collective-permute-done((bf16[32,2,8,128]{3,2,1,0:T(8,128)(2,1)}, bf16[32,2,8,128]{3,2,1,0:T(8,128)(2,1)S(1)}, u32[]{:S(2)}, u32[]{:S(2)}) %collective-permute-start) | collective-permute-done | bytes 131104 | tf_op jit(solution)/shard_map/ppermute | solution.py:453
  9.1 1.5 %collective-permute-start.2 = (bf16[6,32,256]{2,1,0:T(8,128)(2,1)S(1)}, bf16[6,32,256]{2,1,0:T(8,128)(2,1)S(1)}, u32[]{:S(2)}, u32[]{:S(2)}) collective-permute-start(bf16[6,32,256]{2,1,0:T(8,128)(2,1)S(1)} %get-tuple-element.34), channel_id=1, source_target_pairs={{0,16},{1,2},{2,1},{3,19},{16,0},{17,18},{18,17},{19,3},{4,20},{5,... | collective-permute-start | bytes 294920 | tf_op jit(solution)/shard_map/ppermute | solution.py:453
  10.8 2.6 %shard_map.71 = (bf16[4,64,768]{2,1,0:T(8,128)(2,1)S(1)}, f32[1152,192]{1,0:T(8,128)S(1)}, f32[192,288]{1,0:T(8,128)S(1)}) custom-call(bf16[6,32,1024]{2,1,0:T(8,128)(2,1)S(1)} %get-tuple-element.33.deep_ref, bf16[192,288]{1,0:T(8,128)(2,1)S(1)} %get-tuple-element.36.w1_ref, bf16[2,384,1024]{2,1,0:T(8,128)(2,1)S(1)} %get-tuple-element.38.moved_ref, ...), custom_call_target="tpu_custom_call" | custom-call | flops 1500000000 | bytes 4886528 | tf_op jit(solution)/shard_map/pallas_call | solution.py:18
  13.8 1.5 %shard_map.72 = (bf16[4,64,1280]{2,1,0:T(8,128)(2,1)S(1)}, f32[2,2,64,128]{3,2,1,0:T(8,128)S(1)}, f32[2,2,64,128]{3,2,1,0:T(8,128)S(1)}) custom-call(bf16[6,32,1024]{2,1,0:T(8,128)(2,1)S(1)} %get-tuple-element.33.deep_ref, bf16[6,32,256]{2,1,0:T(8,128)(2,1)S(1)} %collective-permute-done.2.two_ref, bf16[6,32,256]{2,1,0:T(8,128)(2,1)S(1)} %collective-permute-done.3.one_ref, ...), custom_call_target="tpu_custom_call" | custom-call | flops 1000000000 | bytes 3543040 | tf_op jit(solution)/shard_map/pallas_call | solution.py:18
  16.5 1.2 %collective-permute-done.5.refs_3_ = f32[2,2,64,128]{3,2,1,0:T(8,128)S(1)} collective-permute-done((f32[2,2,64,128]{3,2,1,0:T(8,128)S(1)}, f32[2,2,64,128]{3,2,1,0:T(8,128)S(1)}, u32[]{:S(2)}, u32[]{:S(2)}) %collective-permute-start.5) | collective-permute-done | bytes 131104 | tf_op jit(solution)/shard_map/ppermute | solution.py:461
  17.7 1.5 %collective-permute-start.6 = (bf16[272,128]{1,0:T(8,128)(2,1)S(1)}, bf16[272,128]{1,0:T(8,128)(2,1)S(1)}, u32[]{:S(2)}, u32[]{:S(2)}) collective-permute-start(bf16[272,128]{1,0:T(8,128)(2,1)S(1)} %get-tuple-element.49), channel_id=1, source_target_pairs={{0,16},{2,18},{16,0},{18,2},{1,17},{3,19},{17,1},{19,3},{4,20},{6,... | collective-permute-start | bytes 208904 | tf_op jit(solution)/shard_map/ppermute | solution.py:461
  19.2 0.9 %collective-permute-start.7 = (bf16[272,128]{1,0:T(8,128)(2,1)S(1)}, bf16[272,128]{1,0:T(8,128)(2,1)S(1)}, u32[]{:S(2)}, u32[]{:S(2)}) collective-permute-start(bf16[272,128]{1,0:T(8,128)(2,1)S(1)} %get-tuple-element.50), channel_id=1, source_target_pairs={{0,2},{2,0},{16,18},{18,16},{1,3},{3,1},{17,19},{19,17},{4,6},{6,4... | collective-permute-start | bytes 208904 | tf_op jit(solution)/shard_map/ppermute | solution.py:461
  20.2 1.1 %collective-permute-start.8 = (bf16[272,128]{1,0:T(8,128)(2,1)S(1)}, bf16[272,128]{1,0:T(8,128)(2,1)S(1)}, u32[]{:S(2)}, u32[]{:S(2)}) collective-permute-start(bf16[272,128]{1,0:T(8,128)(2,1)S(1)} %get-tuple-element.51), channel_id=1, source_target_pairs={{0,18},{2,16},{16,2},{18,0},{1,19},{3,17},{17,3},{19,1},{4,22},{6,... | collective-permute-start | bytes 208904 | tf_op jit(solution)/shard_map/ppermute | solution.py:461
  21.3 0.8 %collective-permute-done.6.refs_0_ = bf16[272,128]{1,0:T(8,128)(2,1)S(1)} collective-permute-done((bf16[272,128]{1,0:T(8,128)(2,1)S(1)}, bf16[272,128]{1,0:T(8,128)(2,1)S(1)}, u32[]{:S(2)}, u32[]{:S(2)}) %collective-permute-start.6) | collective-permute-done | bytes 69664 | tf_op jit(solution)/shard_map/ppermute | solution.py:461
  22.1 2.2 %collective-permute-done.7.refs_1_ = bf16[272,128]{1,0:T(8,128)(2,1)S(1)} collective-permute-done((bf16[272,128]{1,0:T(8,128)(2,1)S(1)}, bf16[272,128]{1,0:T(8,128)(2,1)S(1)}, u32[]{:S(2)}, u32[]{:S(2)}) %collective-permute-start.7) | collective-permute-done | bytes 69664 | tf_op jit(solution)/shard_map/ppermute | solution.py:461
  24.3 1.1 %collective-permute-done.8.refs_2_ = bf16[272,128]{1,0:T(8,128)(2,1)S(1)} collective-permute-done((bf16[272,128]{1,0:T(8,128)(2,1)S(1)}, bf16[272,128]{1,0:T(8,128)(2,1)S(1)}, u32[]{:S(2)}, u32[]{:S(2)}) %collective-permute-start.8) | collective-permute-done | bytes 69664 | tf_op jit(solution)/shard_map/ppermute | solution.py:461
  25.4 2.8 %collective-permute-start.11 = (bf16[272,128]{1,0:T(8,128)(2,1)S(1)}, bf16[272,128]{1,0:T(8,128)(2,1)S(1)}, u32[]{:S(2)}, u32[]{:S(2)}) collective-permute-start(bf16[272,128]{1,0:T(8,128)(2,1)S(1)} %shard_map.76.a_ref), channel_id=1, source_target_pairs={{0,12},{4,8},{8,4},{12,0},{1,13},{5,9},{9,5},{13,1},{2,14},{6,10},... | collective-permute-start | bytes 208904 | tf_op jit(solution)/shard_map/ppermute | solution.py:461
  28.7 1.2 %collective-permute-start.9 = (bf16[272,128]{1,0:T(8,128)(2,1)S(1)}, bf16[272,128]{1,0:T(8,128)(2,1)S(1)}, u32[]{:S(2)}, u32[]{:S(2)}) collective-permute-start(bf16[272,128]{1,0:T(8,128)(2,1)S(1)} %shard_map.76.a_ref), channel_id=1, source_target_pairs={{0,4},{4,0},{8,12},{12,8},{1,5},{5,1},{9,13},{13,9},{2,6},{6,2},{1... | collective-permute-start | bytes 208904 | tf_op jit(solution)/shard_map/ppermute | solution.py:461
  29.9 2.5 %shard_map.73 = (bf16[128,2,8,128]{3,2,1,0:T(8,128)(2,1)}, f32[8,128]{1,0:T(8,128)S(1)}) custom-call(bf16[4,64,1280]{2,1,0:T(8,128)(2,1)S(1)} %get-tuple-element.41.hidden_ref, bf16[27,64,128]{2,1,0:T(8,128)(2,1)S(1)} %bitcast.9), custom_call_target="tpu_custom_call" | custom-call | flops 900000000 | bytes 1626112 | tf_op jit(solution)/shard_map/pallas_call | solution.py:18
  32.4 1.4 %collective-permute-done.10.c_ref = bf16[272,128]{1,0:T(8,128)(2,1)S(1)} collective-permute-done((bf16[272,128]{1,0:T(8,128)(2,1)S(1)}, bf16[272,128]{1,0:T(8,128)(2,1)S(1)}, u32[]{:S(2)}, u32[]{:S(2)}) %collective-permute-start.10) | collective-permute-done | bytes 69664 | tf_op jit(solution)/shard_map/ppermute | solution.py:461
  33.9 1.1 %collective-permute-start.13 = (bf16[288,128]{1,0:T(8,128)(2,1)S(1)}, bf16[288,128]{1,0:T(8,128)(2,1)S(1)}, u32[]{:S(2)}, u32[]{:S(2)}) collective-permute-start(bf16[288,128]{1,0:T(8,128)(2,1)S(1)} %get-tuple-element.53), channel_id=1, source_target_pairs={{0,2},{2,0},{1,3},{3,1},{4,6},{6,4},{5,7},{7,5},{8,10},{10,8},{9,1... | collective-permute-start | bytes 221192 | tf_op jit(solution)/shard_map/ppermute | solution.py:461
  35.0 1.1 %collective-permute-start.14 = (bf16[272,128]{1,0:T(8,128)(2,1)S(1)}, bf16[272,128]{1,0:T(8,128)(2,1)S(1)}, u32[]{:S(2)}, u32[]{:S(2)}) collective-permute-start(bf16[272,128]{1,0:T(8,128)(2,1)S(1)} %get-tuple-element.54.refs_0_), channel_id=1, source_target_pairs={{0,1},{1,0},{2,3},{3,2},{4,5},{5,4},{6,7},{7,6},{8,9},{9,8},{10,11... | collective-permute-start | bytes 208904 | tf_op jit(solution)/shard_map/ppermute | solution.py:461
  36.1 0.9 %collective-permute-done.14.refs_1_ = bf16[272,128]{1,0:T(8,128)(2,1)S(1)} collective-permute-done((bf16[272,128]{1,0:T(8,128)(2,1)S(1)}, bf16[272,128]{1,0:T(8,128)(2,1)S(1)}, u32[]{:S(2)}, u32[]{:S(2)}) %collective-permute-start.14) | collective-permute-done | bytes 69664 | tf_op jit(solution)/shard_map/ppermute | solution.py:461
  37.0 1.0 %shard_map.78 = (f32[9,3,32,32]{3,2,1,0:T(8,128)}, f32[3,9,64,64]{3,2,1,0:T(8,128)}) custom-call(bf16[272,128]{1,0:T(8,128)(2,1)S(1)} %get-tuple-element.54.refs_0_, bf16[272,128]{1,0:T(8,128)(2,1)S(1)} %collective-permute-done.14.refs_1_), custom_call_target="tpu_custom_call" | custom-call | bytes 692224 | tf_op jit(solution)/shard_map/pallas_call | solution.py:18
  38.7 0.9 %collective-permute-done.12.refs_0_ = bf16[288,128]{1,0:T(8,128)(2,1)S(1)} collective-permute-done((bf16[288,128]{1,0:T(8,128)(2,1)S(1)}, bf16[288,128]{1,0:T(8,128)(2,1)S(1)}, u32[]{:S(2)}, u32[]{:S(2)}) %collective-permute-start.12) | collective-permute-done | bytes 73760 | tf_op jit(solution)/shard_map/ppermute | solution.py:461
  39.5 1.0 %shard_map.79 = (f32[9,3,32,32]{3,2,1,0:T(8,128)}, f32[3,9,64,64]{3,2,1,0:T(8,128)}) custom-call(bf16[288,128]{1,0:T(8,128)(2,1)S(1)} %collective-permute-done.12.refs_0_, bf16[288,128]{1,0:T(8,128)(2,1)S(1)} %collective-permute-done.13.refs_1_, f32[9,3,32,32]{3,2,1,0:T(8,128)} %get-tuple-element.55.refs_2_, ...), custom_call_target="tpu_custom_call", output_to_operand_aliasing={{0}: (2, {}), {1}: (3, {})} | custom-call | bytes 1253376 | tf_op jit(solution)/shard_map/pallas_call | solution.py:18
  (27 shorter events, 3.9 us)
Async XLA Ops:
  0.6 4.7 %copy-start = (bf16[1,128,2,8,128]{4,3,2,1,0:T(8,128)(2,1)S(1)}, bf16[1,128,2,8,128]{4,3,2,1,0:T(8,128)(2,1)}, u32[]{:S(2)}) copy-start(bf16[1,128,2,8,128]{4,3,2,1,0:T(8,128)(2,1)} %param.7) | copy-start | bytes 1572868
  0.6 4.7 %copy-start.1 = (bf16[27,128,64]{1,2,0:T(8,128)(2,1)S(1)}, bf16[27,128,64]{1,2,0:T(8,128)(2,1)}, u32[]{:S(2)}) copy-start(bf16[27,128,64]{1,2,0:T(8,128)(2,1)} %param.6) | copy-start | bytes 1327108
  0.7 7.0 %collective-permute-start.1 = (bf16[32,2,8,128]{3,2,1,0:T(8,128)(2,1)}, bf16[32,2,8,128]{3,2,1,0:T(8,128)(2,1)S(1)}, u32[]{:S(2)}, u32[]{:S(2)}) collective-permute-start(bf16[32,2,8,128]{3,2,1,0:T(8,128)(2,1)} %bitcast.11), channel_id=1, source_target_pairs={{0,16},{4,8},{8,4},{12,28},{16,0},{20,24},{24,20},{28,12},{1,17},{... | collective-permute-start | bytes 393224 | tf_op jit(solution)/shard_map/ppermute | solution.py:453
  3.7 5.2 %collective-permute-start = (bf16[32,2,8,128]{3,2,1,0:T(8,128)(2,1)}, bf16[32,2,8,128]{3,2,1,0:T(8,128)(2,1)S(1)}, u32[]{:S(2)}, u32[]{:S(2)}) collective-permute-start(bf16[32,2,8,128]{3,2,1,0:T(8,128)(2,1)} %bitcast.12), channel_id=1, source_target_pairs={{0,4},{4,0},{8,12},{12,8},{16,20},{20,16},{24,28},{28,24},{1,5},{5... | collective-permute-start | bytes 393224 | tf_op jit(solution)/shard_map/ppermute | solution.py:453
  5.3 1.8 %copy-start.2 = (bf16[27,64,32]{1,2,0:T(8,128)(2,1)S(1)}, bf16[27,64,32]{1,2,0:T(8,128)(2,1)}, u32[]{:S(2)}) copy-start(bf16[27,64,32]{1,2,0:T(8,128)(2,1)} %param.5) | copy-start | bytes 331780
  5.3 1.8 %copy-start.3 = (bf16[1,32,2,8,128]{4,3,2,1,0:T(8,128)(2,1)S(1)}, bf16[1,32,2,8,128]{4,3,2,1,0:T(8,128)(2,1)}, u32[]{:S(2)}) copy-start(bf16[1,32,2,8,128]{4,3,2,1,0:T(8,128)(2,1)} %param.4) | copy-start | bytes 393220
  9.1 4.7 %collective-permute-start.2 = (bf16[6,32,256]{2,1,0:T(8,128)(2,1)S(1)}, bf16[6,32,256]{2,1,0:T(8,128)(2,1)S(1)}, u32[]{:S(2)}, u32[]{:S(2)}) collective-permute-start(bf16[6,32,256]{2,1,0:T(8,128)(2,1)S(1)} %get-tuple-element.34), channel_id=1, source_target_pairs={{0,16},{1,2},{2,1},{3,19},{16,0},{17,18},{18,17},{19,3},{4,20},{5,... | collective-permute-start | bytes 294920 | tf_op jit(solution)/shard_map/ppermute | solution.py:453
  10.6 3.2 %collective-permute-start.3 = (bf16[6,32,256]{2,1,0:T(8,128)(2,1)S(1)}, bf16[6,32,256]{2,1,0:T(8,128)(2,1)S(1)}, u32[]{:S(2)}, u32[]{:S(2)}) collective-permute-start(bf16[6,32,256]{2,1,0:T(8,128)(2,1)S(1)} %get-tuple-element.35), channel_id=1, source_target_pairs={{0,1},{1,0},{2,3},{3,2},{16,17},{17,16},{18,19},{19,18},{4,5},{5,4... | collective-permute-start | bytes 294920 | tf_op jit(solution)/shard_map/ppermute | solution.py:453
  15.9 1.7 %collective-permute-start.4 = (bf16[2,2,224,128]{3,2,1,0:T(8,128)(2,1)S(1)}, bf16[2,2,224,128]{3,2,1,0:T(8,128)(2,1)S(1)}, u32[]{:S(2)}, u32[]{:S(2)}) collective-permute-start(bf16[2,2,224,128]{3,2,1,0:T(8,128)(2,1)S(1)} %get-tuple-element.45), channel_id=1, source_target_pairs={{0,1},{1,0},{2,3},{3,2},{4,5},{5,4},{6,7},{7,6},{8,9},{9,8},{10,11... | collective-permute-start | bytes 688136 | tf_op jit(solution)/shard_map/ppermute | solution.py:461
  16.0 1.7 %collective-permute-start.5 = (f32[2,2,64,128]{3,2,1,0:T(8,128)S(1)}, f32[2,2,64,128]{3,2,1,0:T(8,128)S(1)}, u32[]{:S(2)}, u32[]{:S(2)}) collective-permute-start(f32[2,2,64,128]{3,2,1,0:T(8,128)S(1)} %get-tuple-element.47), channel_id=1, source_target_pairs={{0,1},{1,0},{2,3},{3,2},{4,5},{5,4},{6,7},{7,6},{8,9},{9,8},{10,11... | collective-permute-start | bytes 393224 | tf_op jit(solution)/shard_map/ppermute | solution.py:461
  17.7 4.4 %collective-permute-start.6 = (bf16[272,128]{1,0:T(8,128)(2,1)S(1)}, bf16[272,128]{1,0:T(8,128)(2,1)S(1)}, u32[]{:S(2)}, u32[]{:S(2)}) collective-permute-start(bf16[272,128]{1,0:T(8,128)(2,1)S(1)} %get-tuple-element.49), channel_id=1, source_target_pairs={{0,16},{2,18},{16,0},{18,2},{1,17},{3,19},{17,1},{19,3},{4,20},{6,... | collective-permute-start | bytes 208904 | tf_op jit(solution)/shard_map/ppermute | solution.py:461
  19.2 5.1 %collective-permute-start.7 = (bf16[272,128]{1,0:T(8,128)(2,1)S(1)}, bf16[272,128]{1,0:T(8,128)(2,1)S(1)}, u32[]{:S(2)}, u32[]{:S(2)}) collective-permute-start(bf16[272,128]{1,0:T(8,128)(2,1)S(1)} %get-tuple-element.50), channel_id=1, source_target_pairs={{0,2},{2,0},{16,18},{18,16},{1,3},{3,1},{17,19},{19,17},{4,6},{6,4... | collective-permute-start | bytes 208904 | tf_op jit(solution)/shard_map/ppermute | solution.py:461
  20.2 5.2 %collective-permute-start.8 = (bf16[272,128]{1,0:T(8,128)(2,1)S(1)}, bf16[272,128]{1,0:T(8,128)(2,1)S(1)}, u32[]{:S(2)}, u32[]{:S(2)}) collective-permute-start(bf16[272,128]{1,0:T(8,128)(2,1)S(1)} %get-tuple-element.51), channel_id=1, source_target_pairs={{0,18},{2,16},{16,2},{18,0},{1,19},{3,17},{17,3},{19,1},{4,22},{6,... | collective-permute-start | bytes 208904 | tf_op jit(solution)/shard_map/ppermute | solution.py:461
  25.4 7.0 %collective-permute-start.11 = (bf16[272,128]{1,0:T(8,128)(2,1)S(1)}, bf16[272,128]{1,0:T(8,128)(2,1)S(1)}, u32[]{:S(2)}, u32[]{:S(2)}) collective-permute-start(bf16[272,128]{1,0:T(8,128)(2,1)S(1)} %shard_map.76.a_ref), channel_id=1, source_target_pairs={{0,12},{4,8},{8,4},{12,0},{1,13},{5,9},{9,5},{13,1},{2,14},{6,10},... | collective-permute-start | bytes 208904 | tf_op jit(solution)/shard_map/ppermute | solution.py:461
  28.2 5.6 %collective-permute-start.10 = (bf16[272,128]{1,0:T(8,128)(2,1)S(1)}, bf16[272,128]{1,0:T(8,128)(2,1)S(1)}, u32[]{:S(2)}, u32[]{:S(2)}) collective-permute-start(bf16[272,128]{1,0:T(8,128)(2,1)S(1)} %shard_map.76.a_ref), channel_id=1, source_target_pairs={{0,8},{4,12},{8,0},{12,4},{1,9},{5,13},{9,1},{13,5},{2,10},{6,14},... | collective-permute-start | bytes 208904 | tf_op jit(solution)/shard_map/ppermute | solution.py:461
  28.7 5.2 %collective-permute-start.9 = (bf16[272,128]{1,0:T(8,128)(2,1)S(1)}, bf16[272,128]{1,0:T(8,128)(2,1)S(1)}, u32[]{:S(2)}, u32[]{:S(2)}) collective-permute-start(bf16[272,128]{1,0:T(8,128)(2,1)S(1)} %shard_map.76.a_ref), channel_id=1, source_target_pairs={{0,4},{4,0},{8,12},{12,8},{1,5},{5,1},{9,13},{13,9},{2,6},{6,2},{1... | collective-permute-start | bytes 208904 | tf_op jit(solution)/shard_map/ppermute | solution.py:461
  33.9 4.8 %collective-permute-start.13 = (bf16[288,128]{1,0:T(8,128)(2,1)S(1)}, bf16[288,128]{1,0:T(8,128)(2,1)S(1)}, u32[]{:S(2)}, u32[]{:S(2)}) collective-permute-start(bf16[288,128]{1,0:T(8,128)(2,1)S(1)} %get-tuple-element.53), channel_id=1, source_target_pairs={{0,2},{2,0},{1,3},{3,1},{4,6},{6,4},{5,7},{7,5},{8,10},{10,8},{9,1... | collective-permute-start | bytes 221192 | tf_op jit(solution)/shard_map/ppermute | solution.py:461
  35.0 4.5 %collective-permute-start.12 = (bf16[288,128]{1,0:T(8,128)(2,1)S(1)}, bf16[288,128]{1,0:T(8,128)(2,1)S(1)}, u32[]{:S(2)}, u32[]{:S(2)}) collective-permute-start(bf16[288,128]{1,0:T(8,128)(2,1)S(1)} %get-tuple-element.53), channel_id=1, source_target_pairs={{0,3},{1,2},{2,1},{3,0},{4,7},{5,6},{6,5},{7,4},{8,11},{9,10},{10,... | collective-permute-start | bytes 221192 | tf_op jit(solution)/shard_map/ppermute | solution.py:461
  35.0 2.0 %collective-permute-start.14 = (bf16[272,128]{1,0:T(8,128)(2,1)S(1)}, bf16[272,128]{1,0:T(8,128)(2,1)S(1)}, u32[]{:S(2)}, u32[]{:S(2)}) collective-permute-start(bf16[272,128]{1,0:T(8,128)(2,1)S(1)} %get-tuple-element.54.refs_0_), channel_id=1, source_target_pairs={{0,1},{1,0},{2,3},{3,2},{4,5},{5,4},{6,7},{7,6},{8,9},{9,8},{10,11... | collective-permute-start | bytes 208904 | tf_op jit(solution)/shard_map/ppermute | solution.py:461

commit v22 on v21

--- a/solution.py
+++ b/solution.py
@@ -122,7 +122,7 @@
     return before, after
 
 
-def rim_kernel(own_ref, one_ref, two_ref, deep_ref, send_one_ref, send_two_ref, scratch):
+def rim_kernel(own_ref, two_ref, one_ref, deep_ref, send_one_ref, send_two_ref, scratch):
     depth = own_ref.shape[0]
     deep_ref[depth : 2 * depth] = own_ref[...]
     for at, part in zip((0, 2 * depth), sides("dep", one_ref[...], two_ref[...]), strict=True):
@@ -528,7 +528,7 @@
     deep, one, two = call(
         rim_kernel,
         [shape((3 * depth, inner, cells), BF)] + [shape((3 * depth, inner, 2 * width), BF)] * 2,
-        [vol, one, two],
+        [vol, two, one],
         [pltpu.VMEM(((inner + 1) * rows, width), F32)],
     )
     one, two = swapped(one, HGT, 0), swapped(two, HGT, 1)

time: 40.7 us -> 41.2 us (1.012)
  waiting for transfers between devices: 10.7 us -> 11.4 us
    ppermute x11, waiting for transfers between devices: 9.14 us -> 9.59 us  [across(): lax.ppermute(x, axes, [(i, i ^ flip) for i in range(lax.axis_size(axes))])]
  transfers between devices with their start and end apart: 15 -> 15, of which waited for: 10 -> 10; matrix products, arithmetic and copies ran while one was open for 0% -> 0% of each run, Pallas kernels for 21% -> 20%
where the time goes in v22:
time: 41.2 us; the launch traced here: 41.1 us
  starting transfers between devices  17.1 us (42%)
  Pallas kernels  11.9 us (29%)
  waiting for transfers between devices  11.4 us (28%)
  between operations  0.78 us (2%)
    pallas_call x13, Pallas kernels, call(): pl.pallas_call(body, out_shape=outs, in_specs=[pl.BlockSpec(memory_space=...  11.9 us
    ppermute x11, starting transfers between devices, across(): lax.ppermute(x, axes, [(i, i ^ flip) for i in range(lax.axis_size(axes))])  10.8 us
    ppermute x11, waiting for transfers between devices, across(): lax.ppermute(x, axes, [(i, i ^ flip) for i in range(lax.axis_size(axes))])  9.59 us
    ppermute x4, starting transfers between devices, swapped(): return lax.ppermute(x, ('dp', *axes), list(enumerate(partner)))  6.28 us
    ppermute x4, waiting for transfers between devices, swapped(): return lax.ppermute(x, ('dp', *axes), list(enumerate(partner)))  1.76 us
  transfers between devices with their start and end apart: 15, of which 10 were waited for; matrix products, arithmetic and copies ran while one was open for 0% of the time, Pallas kernels for 20%

profile of v22, /device:TPU:0, one launch (start us, length us, event | category | flops | bytes accessed | tf_op | source)
XLA Modules:
  0.0 41.1 jit_solution(9174695113504620887)
XLA Ops:
  0.7 3.1 %collective-permute-start.1 = (bf16[32,2,8,128]{3,2,1,0:T(8,128)(2,1)}, bf16[32,2,8,128]{3,2,1,0:T(8,128)(2,1)S(1)}, u32[]{:S(2)}, u32[]{:S(2)}) collective-permute-start(bf16[32,2,8,128]{3,2,1,0:T(8,128)(2,1)} %bitcast.11), channel_id=1, source_target_pairs={{0,4},{4,0},{8,12},{12,8},{16,20},{20,16},{24,28},{28,24},{1,5},{5... | collective-permute-start | bytes 393224 | tf_op jit(solution)/shard_map/ppermute | solution.py:453
  3.7 1.5 %collective-permute-start = (bf16[32,2,8,128]{3,2,1,0:T(8,128)(2,1)}, bf16[32,2,8,128]{3,2,1,0:T(8,128)(2,1)S(1)}, u32[]{:S(2)}, u32[]{:S(2)}) collective-permute-start(bf16[32,2,8,128]{3,2,1,0:T(8,128)(2,1)} %bitcast.12), channel_id=1, source_target_pairs={{0,16},{4,8},{8,4},{12,28},{16,0},{20,24},{24,20},{28,12},{1,17},{... | collective-permute-start | bytes 393224 | tf_op jit(solution)/shard_map/ppermute | solution.py:453
  5.3 1.7 %shard_map.68 = (bf16[2,128,1024]{2,1,0:T(8,128)(2,1)S(1)}, f32[4,64,1280]{2,1,0:T(8,128)S(1)}) custom-call(bf16[128,2,8,128]{3,2,1,0:T(8,128)(2,1)S(1)} %bitcast.7, bf16[27,64,128]{2,1,0:T(8,128)(2,1)S(1)} %bitcast.8, bf16[128,256]{1,0:T(8,128)(2,1)S(1)} %shard_map.67.blank_ref), custom_call_target="tpu_custom_call" | custom-call | flops 1100000000 | bytes 2867200 | tf_op jit(solution)/shard_map/pallas_call | solution.py:18
  7.6 1.4 %collective-permute-done.two_ref = bf16[32,2,8,128]{3,2,1,0:T(8,128)(2,1)S(1)} collective-permute-done((bf16[32,2,8,128]{3,2,1,0:T(8,128)(2,1)}, bf16[32,2,8,128]{3,2,1,0:T(8,128)(2,1)S(1)}, u32[]{:S(2)}, u32[]{:S(2)}) %collective-permute-start) | collective-permute-done | bytes 131104 | tf_op jit(solution)/shard_map/ppermute | solution.py:453
  9.2 1.6 %collective-permute-start.2 = (bf16[6,32,256]{2,1,0:T(8,128)(2,1)S(1)}, bf16[6,32,256]{2,1,0:T(8,128)(2,1)S(1)}, u32[]{:S(2)}, u32[]{:S(2)}) collective-permute-start(bf16[6,32,256]{2,1,0:T(8,128)(2,1)S(1)} %get-tuple-element.34), channel_id=1, source_target_pairs={{0,16},{1,2},{2,1},{3,19},{16,0},{17,18},{18,17},{19,3},{4,20},{5,... | collective-permute-start | bytes 294920 | tf_op jit(solution)/shard_map/ppermute | solution.py:453
  10.9 2.6 %shard_map.71 = (bf16[4,64,768]{2,1,0:T(8,128)(2,1)S(1)}, f32[1152,192]{1,0:T(8,128)S(1)}, f32[192,288]{1,0:T(8,128)S(1)}) custom-call(bf16[6,32,1024]{2,1,0:T(8,128)(2,1)S(1)} %get-tuple-element.33.deep_ref, bf16[192,288]{1,0:T(8,128)(2,1)S(1)} %get-tuple-element.36.w1_ref, bf16[2,384,1024]{2,1,0:T(8,128)(2,1)S(1)} %get-tuple-element.38.moved_ref, ...), custom_call_target="tpu_custom_call" | custom-call | flops 1500000000 | bytes 4886528 | tf_op jit(solution)/shard_map/pallas_call | solution.py:18
  13.9 1.5 %shard_map.72 = (bf16[4,64,1280]{2,1,0:T(8,128)(2,1)S(1)}, f32[2,2,64,128]{3,2,1,0:T(8,128)S(1)}, f32[2,2,64,128]{3,2,1,0:T(8,128)S(1)}) custom-call(bf16[6,32,1024]{2,1,0:T(8,128)(2,1)S(1)} %get-tuple-element.33.deep_ref, bf16[6,32,256]{2,1,0:T(8,128)(2,1)S(1)} %collective-permute-done.2.two_ref, bf16[6,32,256]{2,1,0:T(8,128)(2,1)S(1)} %collective-permute-done.3.one_ref, ...), custom_call_target="tpu_custom_call" | custom-call | flops 1000000000 | bytes 3543040 | tf_op jit(solution)/shard_map/pallas_call | solution.py:18
  16.6 1.2 %collective-permute-done.5.refs_3_ = f32[2,2,64,128]{3,2,1,0:T(8,128)S(1)} collective-permute-done((f32[2,2,64,128]{3,2,1,0:T(8,128)S(1)}, f32[2,2,64,128]{3,2,1,0:T(8,128)S(1)}, u32[]{:S(2)}, u32[]{:S(2)}) %collective-permute-start.5) | collective-permute-done | bytes 131104 | tf_op jit(solution)/shard_map/ppermute | solution.py:461
  17.8 1.6 %collective-permute-start.6 = (bf16[272,128]{1,0:T(8,128)(2,1)S(1)}, bf16[272,128]{1,0:T(8,128)(2,1)S(1)}, u32[]{:S(2)}, u32[]{:S(2)}) collective-permute-start(bf16[272,128]{1,0:T(8,128)(2,1)S(1)} %get-tuple-element.49), channel_id=1, source_target_pairs={{0,16},{2,18},{16,0},{18,2},{1,17},{3,19},{17,1},{19,3},{4,20},{6,... | collective-permute-start | bytes 208904 | tf_op jit(solution)/shard_map/ppermute | solution.py:461
  19.4 0.9 %collective-permute-start.7 = (bf16[272,128]{1,0:T(8,128)(2,1)S(1)}, bf16[272,128]{1,0:T(8,128)(2,1)S(1)}, u32[]{:S(2)}, u32[]{:S(2)}) collective-permute-start(bf16[272,128]{1,0:T(8,128)(2,1)S(1)} %get-tuple-element.50), channel_id=1, source_target_pairs={{0,2},{2,0},{16,18},{18,16},{1,3},{3,1},{17,19},{19,17},{4,6},{6,4... | collective-permute-start | bytes 208904 | tf_op jit(solution)/shard_map/ppermute | solution.py:461
  20.3 1.1 %collective-permute-start.8 = (bf16[272,128]{1,0:T(8,128)(2,1)S(1)}, bf16[272,128]{1,0:T(8,128)(2,1)S(1)}, u32[]{:S(2)}, u32[]{:S(2)}) collective-permute-start(bf16[272,128]{1,0:T(8,128)(2,1)S(1)} %get-tuple-element.51), channel_id=1, source_target_pairs={{0,18},{2,16},{16,2},{18,0},{1,19},{3,17},{17,3},{19,1},{4,22},{6,... | collective-permute-start | bytes 208904 | tf_op jit(solution)/shard_map/ppermute | solution.py:461
  21.4 0.8 %collective-permute-done.6.refs_0_ = bf16[272,128]{1,0:T(8,128)(2,1)S(1)} collective-permute-done((bf16[272,128]{1,0:T(8,128)(2,1)S(1)}, bf16[272,128]{1,0:T(8,128)(2,1)S(1)}, u32[]{:S(2)}, u32[]{:S(2)}) %collective-permute-start.6) | collective-permute-done | bytes 69664 | tf_op jit(solution)/shard_map/ppermute | solution.py:461
  22.2 2.2 %collective-permute-done.7.refs_1_ = bf16[272,128]{1,0:T(8,128)(2,1)S(1)} collective-permute-done((bf16[272,128]{1,0:T(8,128)(2,1)S(1)}, bf16[272,128]{1,0:T(8,128)(2,1)S(1)}, u32[]{:S(2)}, u32[]{:S(2)}) %collective-permute-start.7) | collective-permute-done | bytes 69664 | tf_op jit(solution)/shard_map/ppermute | solution.py:461
  24.4 1.1 %collective-permute-done.8.refs_2_ = bf16[272,128]{1,0:T(8,128)(2,1)S(1)} collective-permute-done((bf16[272,128]{1,0:T(8,128)(2,1)S(1)}, bf16[272,128]{1,0:T(8,128)(2,1)S(1)}, u32[]{:S(2)}, u32[]{:S(2)}) %collective-permute-start.8) | collective-permute-done | bytes 69664 | tf_op jit(solution)/shard_map/ppermute | solution.py:461
  25.6 2.5 %collective-permute-start.11 = (bf16[272,128]{1,0:T(8,128)(2,1)S(1)}, bf16[272,128]{1,0:T(8,128)(2,1)S(1)}, u32[]{:S(2)}, u32[]{:S(2)}) collective-permute-start(bf16[272,128]{1,0:T(8,128)(2,1)S(1)} %shard_map.76.a_ref), channel_id=1, source_target_pairs={{0,12},{4,8},{8,4},{12,0},{1,13},{5,9},{9,5},{13,1},{2,14},{6,10},... | collective-permute-start | bytes 208904 | tf_op jit(solution)/shard_map/ppermute | solution.py:461
  28.5 1.5 %collective-permute-start.9 = (bf16[272,128]{1,0:T(8,128)(2,1)S(1)}, bf16[272,128]{1,0:T(8,128)(2,1)S(1)}, u32[]{:S(2)}, u32[]{:S(2)}) collective-permute-start(bf16[272,128]{1,0:T(8,128)(2,1)S(1)} %shard_map.76.a_ref), channel_id=1, source_target_pairs={{0,4},{4,0},{8,12},{12,8},{1,5},{5,1},{9,13},{13,9},{2,6},{6,2},{1... | collective-permute-start | bytes 208904 | tf_op jit(solution)/shard_map/ppermute | solution.py:461
  30.0 2.5 %shard_map.73 = (bf16[128,2,8,128]{3,2,1,0:T(8,128)(2,1)}, f32[8,128]{1,0:T(8,128)S(1)}) custom-call(bf16[4,64,1280]{2,1,0:T(8,128)(2,1)S(1)} %get-tuple-element.41.hidden_ref, bf16[27,64,128]{2,1,0:T(8,128)(2,1)S(1)} %bitcast.9), custom_call_target="tpu_custom_call" | custom-call | flops 900000000 | bytes 1626112 | tf_op jit(solution)/shard_map/pallas_call | solution.py:18
  32.5 1.8 %collective-permute-done.10.c_ref = bf16[272,128]{1,0:T(8,128)(2,1)S(1)} collective-permute-done((bf16[272,128]{1,0:T(8,128)(2,1)S(1)}, bf16[272,128]{1,0:T(8,128)(2,1)S(1)}, u32[]{:S(2)}, u32[]{:S(2)}) %collective-permute-start.10) | collective-permute-done | bytes 69664 | tf_op jit(solution)/shard_map/ppermute | solution.py:461
  34.4 1.1 %collective-permute-start.13 = (bf16[288,128]{1,0:T(8,128)(2,1)S(1)}, bf16[288,128]{1,0:T(8,128)(2,1)S(1)}, u32[]{:S(2)}, u32[]{:S(2)}) collective-permute-start(bf16[288,128]{1,0:T(8,128)(2,1)S(1)} %get-tuple-element.53), channel_id=1, source_target_pairs={{0,2},{2,0},{1,3},{3,1},{4,6},{6,4},{5,7},{7,5},{8,10},{10,8},{9,1... | collective-permute-start | bytes 221192 | tf_op jit(solution)/shard_map/ppermute | solution.py:461
  35.6 1.1 %collective-permute-start.14 = (bf16[272,128]{1,0:T(8,128)(2,1)S(1)}, bf16[272,128]{1,0:T(8,128)(2,1)S(1)}, u32[]{:S(2)}, u32[]{:S(2)}) collective-permute-start(bf16[272,128]{1,0:T(8,128)(2,1)S(1)} %get-tuple-element.54.refs_0_), channel_id=1, source_target_pairs={{0,1},{1,0},{2,3},{3,2},{4,5},{5,4},{6,7},{7,6},{8,9},{9,8},{10,11... | collective-permute-start | bytes 208904 | tf_op jit(solution)/shard_map/ppermute | solution.py:461
  36.6 0.9 %collective-permute-done.14.refs_1_ = bf16[272,128]{1,0:T(8,128)(2,1)S(1)} collective-permute-done((bf16[272,128]{1,0:T(8,128)(2,1)S(1)}, bf16[272,128]{1,0:T(8,128)(2,1)S(1)}, u32[]{:S(2)}, u32[]{:S(2)}) %collective-permute-start.14) | collective-permute-done | bytes 69664 | tf_op jit(solution)/shard_map/ppermute | solution.py:461
  37.5 1.0 %shard_map.78 = (f32[9,3,32,32]{3,2,1,0:T(8,128)}, f32[3,9,64,64]{3,2,1,0:T(8,128)}) custom-call(bf16[272,128]{1,0:T(8,128)(2,1)S(1)} %get-tuple-element.54.refs_0_, bf16[272,128]{1,0:T(8,128)(2,1)S(1)} %collective-permute-done.14.refs_1_), custom_call_target="tpu_custom_call" | custom-call | bytes 692224 | tf_op jit(solution)/shard_map/pallas_call | solution.py:18
  39.2 0.9 %collective-permute-done.12.refs_0_ = bf16[288,128]{1,0:T(8,128)(2,1)S(1)} collective-permute-done((bf16[288,128]{1,0:T(8,128)(2,1)S(1)}, bf16[288,128]{1,0:T(8,128)(2,1)S(1)}, u32[]{:S(2)}, u32[]{:S(2)}) %collective-permute-start.12) | collective-permute-done | bytes 73760 | tf_op jit(solution)/shard_map/ppermute | solution.py:461
  40.1 1.0 %shard_map.79 = (f32[9,3,32,32]{3,2,1,0:T(8,128)}, f32[3,9,64,64]{3,2,1,0:T(8,128)}) custom-call(bf16[288,128]{1,0:T(8,128)(2,1)S(1)} %collective-permute-done.12.refs_0_, bf16[288,128]{1,0:T(8,128)(2,1)S(1)} %collective-permute-done.13.refs_1_, f32[9,3,32,32]{3,2,1,0:T(8,128)} %get-tuple-element.55.refs_2_, ...), custom_call_target="tpu_custom_call", output_to_operand_aliasing={{0}: (2, {}), {1}: (3, {})} | custom-call | bytes 1253376 | tf_op jit(solution)/shard_map/pallas_call | solution.py:18
  (27 shorter events, 3.7 us)
Async XLA Ops:
  0.6 4.6 %copy-start = (bf16[1,128,2,8,128]{4,3,2,1,0:T(8,128)(2,1)S(1)}, bf16[1,128,2,8,128]{4,3,2,1,0:T(8,128)(2,1)}, u32[]{:S(2)}) copy-start(bf16[1,128,2,8,128]{4,3,2,1,0:T(8,128)(2,1)} %param.7) | copy-start | bytes 1572868
  0.6 4.6 %copy-start.1 = (bf16[27,128,64]{1,2,0:T(8,128)(2,1)S(1)}, bf16[27,128,64]{1,2,0:T(8,128)(2,1)}, u32[]{:S(2)}) copy-start(bf16[27,128,64]{1,2,0:T(8,128)(2,1)} %param.6) | copy-start | bytes 1327108
  0.7 6.9 %collective-permute-start.1 = (bf16[32,2,8,128]{3,2,1,0:T(8,128)(2,1)}, bf16[32,2,8,128]{3,2,1,0:T(8,128)(2,1)S(1)}, u32[]{:S(2)}, u32[]{:S(2)}) collective-permute-start(bf16[32,2,8,128]{3,2,1,0:T(8,128)(2,1)} %bitcast.11), channel_id=1, source_target_pairs={{0,4},{4,0},{8,12},{12,8},{16,20},{20,16},{24,28},{28,24},{1,5},{5... | collective-permute-start | bytes 393224 | tf_op jit(solution)/shard_map/ppermute | solution.py:453
  3.7 5.2 %collective-permute-start = (bf16[32,2,8,128]{3,2,1,0:T(8,128)(2,1)}, bf16[32,2,8,128]{3,2,1,0:T(8,128)(2,1)S(1)}, u32[]{:S(2)}, u32[]{:S(2)}) collective-permute-start(bf16[32,2,8,128]{3,2,1,0:T(8,128)(2,1)} %bitcast.12), channel_id=1, source_target_pairs={{0,16},{4,8},{8,4},{12,28},{16,0},{20,24},{24,20},{28,12},{1,17},{... | collective-permute-start | bytes 393224 | tf_op jit(solution)/shard_map/ppermute | solution.py:453
  5.3 1.8 %copy-start.2 = (bf16[27,64,32]{1,2,0:T(8,128)(2,1)S(1)}, bf16[27,64,32]{1,2,0:T(8,128)(2,1)}, u32[]{:S(2)}) copy-start(bf16[27,64,32]{1,2,0:T(8,128)(2,1)} %param.5) | copy-start | bytes 331780
  5.3 1.8 %copy-start.3 = (bf16[1,32,2,8,128]{4,3,2,1,0:T(8,128)(2,1)S(1)}, bf16[1,32,2,8,128]{4,3,2,1,0:T(8,128)(2,1)}, u32[]{:S(2)}) copy-start(bf16[1,32,2,8,128]{4,3,2,1,0:T(8,128)(2,1)} %param.4) | copy-start | bytes 393220
  9.2 4.7 %collective-permute-start.2 = (bf16[6,32,256]{2,1,0:T(8,128)(2,1)S(1)}, bf16[6,32,256]{2,1,0:T(8,128)(2,1)S(1)}, u32[]{:S(2)}, u32[]{:S(2)}) collective-permute-start(bf16[6,32,256]{2,1,0:T(8,128)(2,1)S(1)} %get-tuple-element.34), channel_id=1, source_target_pairs={{0,16},{1,2},{2,1},{3,19},{16,0},{17,18},{18,17},{19,3},{4,20},{5,... | collective-permute-start | bytes 294920 | tf_op jit(solution)/shard_map/ppermute | solution.py:453
  10.8 3.1 %collective-permute-start.3 = (bf16[6,32,256]{2,1,0:T(8,128)(2,1)S(1)}, bf16[6,32,256]{2,1,0:T(8,128)(2,1)S(1)}, u32[]{:S(2)}, u32[]{:S(2)}) collective-permute-start(bf16[6,32,256]{2,1,0:T(8,128)(2,1)S(1)} %get-tuple-element.35), channel_id=1, source_target_pairs={{0,1},{1,0},{2,3},{3,2},{16,17},{17,16},{18,19},{19,18},{4,5},{5,4... | collective-permute-start | bytes 294920 | tf_op jit(solution)/shard_map/ppermute | solution.py:453
  16.0 1.7 %collective-permute-start.4 = (bf16[2,2,224,128]{3,2,1,0:T(8,128)(2,1)S(1)}, bf16[2,2,224,128]{3,2,1,0:T(8,128)(2,1)S(1)}, u32[]{:S(2)}, u32[]{:S(2)}) collective-permute-start(bf16[2,2,224,128]{3,2,1,0:T(8,128)(2,1)S(1)} %get-tuple-element.45), channel_id=1, source_target_pairs={{0,1},{1,0},{2,3},{3,2},{4,5},{5,4},{6,7},{7,6},{8,9},{9,8},{10,11... | collective-permute-start | bytes 688136 | tf_op jit(solution)/shard_map/ppermute | solution.py:461
  16.1 1.7 %collective-permute-start.5 = (f32[2,2,64,128]{3,2,1,0:T(8,128)S(1)}, f32[2,2,64,128]{3,2,1,0:T(8,128)S(1)}, u32[]{:S(2)}, u32[]{:S(2)}) collective-permute-start(f32[2,2,64,128]{3,2,1,0:T(8,128)S(1)} %get-tuple-element.47), channel_id=1, source_target_pairs={{0,1},{1,0},{2,3},{3,2},{4,5},{5,4},{6,7},{7,6},{8,9},{9,8},{10,11... | collective-permute-start | bytes 393224 | tf_op jit(solution)/shard_map/ppermute | solution.py:461
  17.8 4.4 %collective-permute-start.6 = (bf16[272,128]{1,0:T(8,128)(2,1)S(1)}, bf16[272,128]{1,0:T(8,128)(2,1)S(1)}, u32[]{:S(2)}, u32[]{:S(2)}) collective-permute-start(bf16[272,128]{1,0:T(8,128)(2,1)S(1)} %get-tuple-element.49), channel_id=1, source_target_pairs={{0,16},{2,18},{16,0},{18,2},{1,17},{3,19},{17,1},{19,3},{4,20},{6,... | collective-permute-start | bytes 208904 | tf_op jit(solution)/shard_map/ppermute | solution.py:461
  19.4 5.1 %collective-permute-start.7 = (bf16[272,128]{1,0:T(8,128)(2,1)S(1)}, bf16[272,128]{1,0:T(8,128)(2,1)S(1)}, u32[]{:S(2)}, u32[]{:S(2)}) collective-permute-start(bf16[272,128]{1,0:T(8,128)(2,1)S(1)} %get-tuple-element.50), channel_id=1, source_target_pairs={{0,2},{2,0},{16,18},{18,16},{1,3},{3,1},{17,19},{19,17},{4,6},{6,4... | collective-permute-start | bytes 208904 | tf_op jit(solution)/shard_map/ppermute | solution.py:461
  20.3 5.2 %collective-permute-start.8 = (bf16[272,128]{1,0:T(8,128)(2,1)S(1)}, bf16[272,128]{1,0:T(8,128)(2,1)S(1)}, u32[]{:S(2)}, u32[]{:S(2)}) collective-permute-start(bf16[272,128]{1,0:T(8,128)(2,1)S(1)} %get-tuple-element.51), channel_id=1, source_target_pairs={{0,18},{2,16},{16,2},{18,0},{1,19},{3,17},{17,3},{19,1},{4,22},{6,... | collective-permute-start | bytes 208904 | tf_op jit(solution)/shard_map/ppermute | solution.py:461
  25.6 7.0 %collective-permute-start.11 = (bf16[272,128]{1,0:T(8,128)(2,1)S(1)}, bf16[272,128]{1,0:T(8,128)(2,1)S(1)}, u32[]{:S(2)}, u32[]{:S(2)}) collective-permute-start(bf16[272,128]{1,0:T(8,128)(2,1)S(1)} %shard_map.76.a_ref), channel_id=1, source_target_pairs={{0,12},{4,8},{8,4},{12,0},{1,13},{5,9},{9,5},{13,1},{2,14},{6,10},... | collective-permute-start | bytes 208904 | tf_op jit(solution)/shard_map/ppermute | solution.py:461
  28.1 6.3 %collective-permute-start.10 = (bf16[272,128]{1,0:T(8,128)(2,1)S(1)}, bf16[272,128]{1,0:T(8,128)(2,1)S(1)}, u32[]{:S(2)}, u32[]{:S(2)}) collective-permute-start(bf16[272,128]{1,0:T(8,128)(2,1)S(1)} %shard_map.76.a_ref), channel_id=1, source_target_pairs={{0,8},{4,12},{8,0},{12,4},{1,9},{5,13},{9,1},{13,5},{2,10},{6,14},... | collective-permute-start | bytes 208904 | tf_op jit(solution)/shard_map/ppermute | solution.py:461
  28.5 5.8 %collective-permute-start.9 = (bf16[272,128]{1,0:T(8,128)(2,1)S(1)}, bf16[272,128]{1,0:T(8,128)(2,1)S(1)}, u32[]{:S(2)}, u32[]{:S(2)}) collective-permute-start(bf16[272,128]{1,0:T(8,128)(2,1)S(1)} %shard_map.76.a_ref), channel_id=1, source_target_pairs={{0,4},{4,0},{8,12},{12,8},{1,5},{5,1},{9,13},{13,9},{2,6},{6,2},{1... | collective-permute-start | bytes 208904 | tf_op jit(solution)/shard_map/ppermute | solution.py:461
  34.4 4.8 %collective-permute-start.13 = (bf16[288,128]{1,0:T(8,128)(2,1)S(1)}, bf16[288,128]{1,0:T(8,128)(2,1)S(1)}, u32[]{:S(2)}, u32[]{:S(2)}) collective-permute-start(bf16[288,128]{1,0:T(8,128)(2,1)S(1)} %get-tuple-element.53), channel_id=1, source_target_pairs={{0,2},{2,0},{1,3},{3,1},{4,6},{6,4},{5,7},{7,5},{8,10},{10,8},{9,1... | collective-permute-start | bytes 221192 | tf_op jit(solution)/shard_map/ppermute | solution.py:461
  35.6 4.5 %collective-permute-start.12 = (bf16[288,128]{1,0:T(8,128)(2,1)S(1)}, bf16[288,128]{1,0:T(8,128)(2,1)S(1)}, u32[]{:S(2)}, u32[]{:S(2)}) collective-permute-start(bf16[288,128]{1,0:T(8,128)(2,1)S(1)} %get-tuple-element.53), channel_id=1, source_target_pairs={{0,3},{1,2},{2,1},{3,0},{4,7},{5,6},{6,5},{7,4},{8,11},{9,10},{10,... | collective-permute-start | bytes 221192 | tf_op jit(solution)/shard_map/ppermute | solution.py:461
  35.6 2.0 %collective-permute-start.14 = (bf16[272,128]{1,0:T(8,128)(2,1)S(1)}, bf16[272,128]{1,0:T(8,128)(2,1)S(1)}, u32[]{:S(2)}, u32[]{:S(2)}) collective-permute-start(bf16[272,128]{1,0:T(8,128)(2,1)S(1)} %get-tuple-element.54.refs_0_), channel_id=1, source_target_pairs={{0,1},{1,0},{2,3},{3,2},{4,5},{5,4},{6,7},{7,6},{8,9},{9,8},{10,11... | collective-permute-start | bytes 208904 | tf_op jit(solution)/shard_map/ppermute | solution.py:461

commit v23 on v21

--- a/solution.py
+++ b/solution.py
@@ -569,7 +569,7 @@
         flops=4_000_000_000,
     )
     if direct:
-        moves = [(1, 0), (0, 1), (1, 1)]
+        moves = [(0, 1), (1, 0), (1, 1)]
         grads = [second, first]
     else:
         moves = [(0, 1)]

time: 40.7 us -> 40.9 us (level)
  transfers between devices with their start and end apart: 15 -> 15, of which waited for: 10 -> 10; matrix products, arithmetic and copies ran while one was open for 0% -> 0% of each run, Pallas kernels for 21% -> 20%
where the time goes in v23:
time: 40.9 us; the launch traced here: 40.7 us
  starting transfers between devices  17.1 us (42%)
  Pallas kernels  11.9 us (29%)
  waiting for transfers between devices  10.9 us (27%)
  between operations  0.78 us (2%)
    pallas_call x13, Pallas kernels, call(): pl.pallas_call(body, out_shape=outs, in_specs=[pl.BlockSpec(memory_space=...  11.9 us
    ppermute x11, starting transfers between devices, across(): lax.ppermute(x, axes, [(i, i ^ flip) for i in range(lax.axis_size(axes))])  10.8 us
    ppermute x11, waiting for transfers between devices, across(): lax.ppermute(x, axes, [(i, i ^ flip) for i in range(lax.axis_size(axes))])  9.32 us
    ppermute x4, starting transfers between devices, swapped(): return lax.ppermute(x, ('dp', *axes), list(enumerate(partner)))  6.36 us
    ppermute x4, waiting for transfers between devices, swapped(): return lax.ppermute(x, ('dp', *axes), list(enumerate(partner)))  1.58 us
  transfers between devices with their start and end apart: 15, of which 10 were waited for; matrix products, arithmetic and copies ran while one was open for 0% of the time, Pallas kernels for 20%

profile of v23, /device:TPU:0, one launch (start us, length us, event | category | flops | bytes accessed | tf_op | source)
XLA Modules:
  0.0 40.7 jit_solution(3133660543130717424)
XLA Ops:
  0.7 3.0 %collective-permute-start.1 = (bf16[32,2,8,128]{3,2,1,0:T(8,128)(2,1)}, bf16[32,2,8,128]{3,2,1,0:T(8,128)(2,1)S(1)}, u32[]{:S(2)}, u32[]{:S(2)}) collective-permute-start(bf16[32,2,8,128]{3,2,1,0:T(8,128)(2,1)} %bitcast.11), channel_id=1, source_target_pairs={{0,16},{4,8},{8,4},{12,28},{16,0},{20,24},{24,20},{28,12},{1,17},{... | collective-permute-start | bytes 393224 | tf_op jit(solution)/shard_map/ppermute | solution.py:453
  3.7 1.7 %collective-permute-start = (bf16[32,2,8,128]{3,2,1,0:T(8,128)(2,1)}, bf16[32,2,8,128]{3,2,1,0:T(8,128)(2,1)S(1)}, u32[]{:S(2)}, u32[]{:S(2)}) collective-permute-start(bf16[32,2,8,128]{3,2,1,0:T(8,128)(2,1)} %bitcast.12), channel_id=1, source_target_pairs={{0,4},{4,0},{8,12},{12,8},{16,20},{20,16},{24,28},{28,24},{1,5},{5... | collective-permute-start | bytes 393224 | tf_op jit(solution)/shard_map/ppermute | solution.py:453
  5.4 1.7 %shard_map.68 = (bf16[2,128,1024]{2,1,0:T(8,128)(2,1)S(1)}, f32[4,64,1280]{2,1,0:T(8,128)S(1)}) custom-call(bf16[128,2,8,128]{3,2,1,0:T(8,128)(2,1)S(1)} %bitcast.7, bf16[27,64,128]{2,1,0:T(8,128)(2,1)S(1)} %bitcast.8, bf16[128,256]{1,0:T(8,128)(2,1)S(1)} %shard_map.67.blank_ref), custom_call_target="tpu_custom_call" | custom-call | flops 1100000000 | bytes 2867200 | tf_op jit(solution)/shard_map/pallas_call | solution.py:18
  7.6 1.2 %collective-permute-done.one_ref = bf16[32,2,8,128]{3,2,1,0:T(8,128)(2,1)S(1)} collective-permute-done((bf16[32,2,8,128]{3,2,1,0:T(8,128)(2,1)}, bf16[32,2,8,128]{3,2,1,0:T(8,128)(2,1)S(1)}, u32[]{:S(2)}, u32[]{:S(2)}) %collective-permute-start) | collective-permute-done | bytes 131104 | tf_op jit(solution)/shard_map/ppermute | solution.py:453
  9.1 1.5 %collective-permute-start.2 = (bf16[6,32,256]{2,1,0:T(8,128)(2,1)S(1)}, bf16[6,32,256]{2,1,0:T(8,128)(2,1)S(1)}, u32[]{:S(2)}, u32[]{:S(2)}) collective-permute-start(bf16[6,32,256]{2,1,0:T(8,128)(2,1)S(1)} %get-tuple-element.34), channel_id=1, source_target_pairs={{0,16},{1,2},{2,1},{3,19},{16,0},{17,18},{18,17},{19,3},{4,20},{5,... | collective-permute-start | bytes 294920 | tf_op jit(solution)/shard_map/ppermute | solution.py:453
  10.8 2.6 %shard_map.71 = (bf16[4,64,768]{2,1,0:T(8,128)(2,1)S(1)}, f32[1152,192]{1,0:T(8,128)S(1)}, f32[192,288]{1,0:T(8,128)S(1)}) custom-call(bf16[6,32,1024]{2,1,0:T(8,128)(2,1)S(1)} %get-tuple-element.33.deep_ref, bf16[192,288]{1,0:T(8,128)(2,1)S(1)} %get-tuple-element.36.w1_ref, bf16[2,384,1024]{2,1,0:T(8,128)(2,1)S(1)} %get-tuple-element.38.moved_ref, ...), custom_call_target="tpu_custom_call" | custom-call | flops 1500000000 | bytes 4886528 | tf_op jit(solution)/shard_map/pallas_call | solution.py:18
  13.8 1.5 %shard_map.72 = (bf16[4,64,1280]{2,1,0:T(8,128)(2,1)S(1)}, f32[2,2,64,128]{3,2,1,0:T(8,128)S(1)}, f32[2,2,64,128]{3,2,1,0:T(8,128)S(1)}) custom-call(bf16[6,32,1024]{2,1,0:T(8,128)(2,1)S(1)} %get-tuple-element.33.deep_ref, bf16[6,32,256]{2,1,0:T(8,128)(2,1)S(1)} %collective-permute-done.2.two_ref, bf16[6,32,256]{2,1,0:T(8,128)(2,1)S(1)} %collective-permute-done.3.one_ref, ...), custom_call_target="tpu_custom_call" | custom-call | flops 1000000000 | bytes 3543040 | tf_op jit(solution)/shard_map/pallas_call | solution.py:18
  16.5 1.2 %collective-permute-done.5.refs_3_ = f32[2,2,64,128]{3,2,1,0:T(8,128)S(1)} collective-permute-done((f32[2,2,64,128]{3,2,1,0:T(8,128)S(1)}, f32[2,2,64,128]{3,2,1,0:T(8,128)S(1)}, u32[]{:S(2)}, u32[]{:S(2)}) %collective-permute-start.5) | collective-permute-done | bytes 131104 | tf_op jit(solution)/shard_map/ppermute | solution.py:461
  17.7 1.0 %collective-permute-start.6 = (bf16[272,128]{1,0:T(8,128)(2,1)S(1)}, bf16[272,128]{1,0:T(8,128)(2,1)S(1)}, u32[]{:S(2)}, u32[]{:S(2)}) collective-permute-start(bf16[272,128]{1,0:T(8,128)(2,1)S(1)} %get-tuple-element.49), channel_id=1, source_target_pairs={{0,2},{2,0},{16,18},{18,16},{1,3},{3,1},{17,19},{19,17},{4,6},{6,4... | collective-permute-start | bytes 208904 | tf_op jit(solution)/shard_map/ppermute | solution.py:461
  18.8 1.4 %collective-permute-start.7 = (bf16[272,128]{1,0:T(8,128)(2,1)S(1)}, bf16[272,128]{1,0:T(8,128)(2,1)S(1)}, u32[]{:S(2)}, u32[]{:S(2)}) collective-permute-start(bf16[272,128]{1,0:T(8,128)(2,1)S(1)} %get-tuple-element.50), channel_id=1, source_target_pairs={{0,16},{2,18},{16,0},{18,2},{1,17},{3,19},{17,1},{19,3},{4,20},{6,... | collective-permute-start | bytes 208904 | tf_op jit(solution)/shard_map/ppermute | solution.py:461
  20.2 1.1 %collective-permute-start.8 = (bf16[272,128]{1,0:T(8,128)(2,1)S(1)}, bf16[272,128]{1,0:T(8,128)(2,1)S(1)}, u32[]{:S(2)}, u32[]{:S(2)}) collective-permute-start(bf16[272,128]{1,0:T(8,128)(2,1)S(1)} %get-tuple-element.51), channel_id=1, source_target_pairs={{0,18},{2,16},{16,2},{18,0},{1,19},{3,17},{17,3},{19,1},{4,22},{6,... | collective-permute-start | bytes 208904 | tf_op jit(solution)/shard_map/ppermute | solution.py:461
  21.3 0.8 %collective-permute-done.6.refs_0_ = bf16[272,128]{1,0:T(8,128)(2,1)S(1)} collective-permute-done((bf16[272,128]{1,0:T(8,128)(2,1)S(1)}, bf16[272,128]{1,0:T(8,128)(2,1)S(1)}, u32[]{:S(2)}, u32[]{:S(2)}) %collective-permute-start.6) | collective-permute-done | bytes 69664 | tf_op jit(solution)/shard_map/ppermute | solution.py:461
  22.1 1.2 %collective-permute-done.7.refs_1_ = bf16[272,128]{1,0:T(8,128)(2,1)S(1)} collective-permute-done((bf16[272,128]{1,0:T(8,128)(2,1)S(1)}, bf16[272,128]{1,0:T(8,128)(2,1)S(1)}, u32[]{:S(2)}, u32[]{:S(2)}) %collective-permute-start.7) | collective-permute-done | bytes 69664 | tf_op jit(solution)/shard_map/ppermute | solution.py:461
  23.3 2.1 %collective-permute-done.8.refs_2_ = bf16[272,128]{1,0:T(8,128)(2,1)S(1)} collective-permute-done((bf16[272,128]{1,0:T(8,128)(2,1)S(1)}, bf16[272,128]{1,0:T(8,128)(2,1)S(1)}, u32[]{:S(2)}, u32[]{:S(2)}) %collective-permute-start.8) | collective-permute-done | bytes 69664 | tf_op jit(solution)/shard_map/ppermute | solution.py:461
  25.4 3.0 %collective-permute-start.11 = (bf16[272,128]{1,0:T(8,128)(2,1)S(1)}, bf16[272,128]{1,0:T(8,128)(2,1)S(1)}, u32[]{:S(2)}, u32[]{:S(2)}) collective-permute-start(bf16[272,128]{1,0:T(8,128)(2,1)S(1)} %shard_map.76.a_ref), channel_id=1, source_target_pairs={{0,12},{4,8},{8,4},{12,0},{1,13},{5,9},{9,5},{13,1},{2,14},{6,10},... | collective-permute-start | bytes 208904 | tf_op jit(solution)/shard_map/ppermute | solution.py:461
  28.7 1.2 %collective-permute-start.9 = (bf16[272,128]{1,0:T(8,128)(2,1)S(1)}, bf16[272,128]{1,0:T(8,128)(2,1)S(1)}, u32[]{:S(2)}, u32[]{:S(2)}) collective-permute-start(bf16[272,128]{1,0:T(8,128)(2,1)S(1)} %shard_map.76.a_ref), channel_id=1, source_target_pairs={{0,4},{4,0},{8,12},{12,8},{1,5},{5,1},{9,13},{13,9},{2,6},{6,2},{1... | collective-permute-start | bytes 208904 | tf_op jit(solution)/shard_map/ppermute | solution.py:461
  29.9 2.5 %shard_map.73 = (bf16[128,2,8,128]{3,2,1,0:T(8,128)(2,1)}, f32[8,128]{1,0:T(8,128)S(1)}) custom-call(bf16[4,64,1280]{2,1,0:T(8,128)(2,1)S(1)} %get-tuple-element.41.hidden_ref, bf16[27,64,128]{2,1,0:T(8,128)(2,1)S(1)} %bitcast.9), custom_call_target="tpu_custom_call" | custom-call | flops 900000000 | bytes 1626112 | tf_op jit(solution)/shard_map/pallas_call | solution.py:18
  32.4 1.7 %collective-permute-done.10.c_ref = bf16[272,128]{1,0:T(8,128)(2,1)S(1)} collective-permute-done((bf16[272,128]{1,0:T(8,128)(2,1)S(1)}, bf16[272,128]{1,0:T(8,128)(2,1)S(1)}, u32[]{:S(2)}, u32[]{:S(2)}) %collective-permute-start.10) | collective-permute-done | bytes 69664 | tf_op jit(solution)/shard_map/ppermute | solution.py:461
  34.1 1.1 %collective-permute-start.13 = (bf16[288,128]{1,0:T(8,128)(2,1)S(1)}, bf16[288,128]{1,0:T(8,128)(2,1)S(1)}, u32[]{:S(2)}, u32[]{:S(2)}) collective-permute-start(bf16[288,128]{1,0:T(8,128)(2,1)S(1)} %get-tuple-element.53), channel_id=1, source_target_pairs={{0,2},{2,0},{1,3},{3,1},{4,6},{6,4},{5,7},{7,5},{8,10},{10,8},{9,1... | collective-permute-start | bytes 221192 | tf_op jit(solution)/shard_map/ppermute | solution.py:461
  35.2 1.1 %collective-permute-start.14 = (bf16[272,128]{1,0:T(8,128)(2,1)S(1)}, bf16[272,128]{1,0:T(8,128)(2,1)S(1)}, u32[]{:S(2)}, u32[]{:S(2)}) collective-permute-start(bf16[272,128]{1,0:T(8,128)(2,1)S(1)} %get-tuple-element.54.refs_0_), channel_id=1, source_target_pairs={{0,1},{1,0},{2,3},{3,2},{4,5},{5,4},{6,7},{7,6},{8,9},{9,8},{10,11... | collective-permute-start | bytes 208904 | tf_op jit(solution)/shard_map/ppermute | solution.py:461
  36.3 0.9 %collective-permute-done.14.refs_1_ = bf16[272,128]{1,0:T(8,128)(2,1)S(1)} collective-permute-done((bf16[272,128]{1,0:T(8,128)(2,1)S(1)}, bf16[272,128]{1,0:T(8,128)(2,1)S(1)}, u32[]{:S(2)}, u32[]{:S(2)}) %collective-permute-start.14) | collective-permute-done | bytes 69664 | tf_op jit(solution)/shard_map/ppermute | solution.py:461
  37.2 1.0 %shard_map.78 = (f32[9,3,32,32]{3,2,1,0:T(8,128)}, f32[3,9,64,64]{3,2,1,0:T(8,128)}) custom-call(bf16[272,128]{1,0:T(8,128)(2,1)S(1)} %get-tuple-element.54.refs_0_, bf16[272,128]{1,0:T(8,128)(2,1)S(1)} %collective-permute-done.14.refs_1_), custom_call_target="tpu_custom_call" | custom-call | bytes 692224 | tf_op jit(solution)/shard_map/pallas_call | solution.py:18
  38.9 0.8 %collective-permute-done.12.refs_0_ = bf16[288,128]{1,0:T(8,128)(2,1)S(1)} collective-permute-done((bf16[288,128]{1,0:T(8,128)(2,1)S(1)}, bf16[288,128]{1,0:T(8,128)(2,1)S(1)}, u32[]{:S(2)}, u32[]{:S(2)}) %collective-permute-start.12) | collective-permute-done | bytes 73760 | tf_op jit(solution)/shard_map/ppermute | solution.py:461
  39.7 1.0 %shard_map.79 = (f32[9,3,32,32]{3,2,1,0:T(8,128)}, f32[3,9,64,64]{3,2,1,0:T(8,128)}) custom-call(bf16[288,128]{1,0:T(8,128)(2,1)S(1)} %collective-permute-done.12.refs_0_, bf16[288,128]{1,0:T(8,128)(2,1)S(1)} %collective-permute-done.13.refs_1_, f32[9,3,32,32]{3,2,1,0:T(8,128)} %get-tuple-element.55.refs_2_, ...), custom_call_target="tpu_custom_call", output_to_operand_aliasing={{0}: (2, {}), {1}: (3, {})} | custom-call | bytes 1253376 | tf_op jit(solution)/shard_map/pallas_call | solution.py:18
  (27 shorter events, 3.6 us)
Async XLA Ops:
  0.6 4.7 %copy-start = (bf16[1,128,2,8,128]{4,3,2,1,0:T(8,128)(2,1)S(1)}, bf16[1,128,2,8,128]{4,3,2,1,0:T(8,128)(2,1)}, u32[]{:S(2)}) copy-start(bf16[1,128,2,8,128]{4,3,2,1,0:T(8,128)(2,1)} %param.7) | copy-start | bytes 1572868
  0.6 4.7 %copy-start.1 = (bf16[27,128,64]{1,2,0:T(8,128)(2,1)S(1)}, bf16[27,128,64]{1,2,0:T(8,128)(2,1)}, u32[]{:S(2)}) copy-start(bf16[27,128,64]{1,2,0:T(8,128)(2,1)} %param.6) | copy-start | bytes 1327108
  0.7 7.0 %collective-permute-start.1 = (bf16[32,2,8,128]{3,2,1,0:T(8,128)(2,1)}, bf16[32,2,8,128]{3,2,1,0:T(8,128)(2,1)S(1)}, u32[]{:S(2)}, u32[]{:S(2)}) collective-permute-start(bf16[32,2,8,128]{3,2,1,0:T(8,128)(2,1)} %bitcast.11), channel_id=1, source_target_pairs={{0,16},{4,8},{8,4},{12,28},{16,0},{20,24},{24,20},{28,12},{1,17},{... | collective-permute-start | bytes 393224 | tf_op jit(solution)/shard_map/ppermute | solution.py:453
  3.7 5.2 %collective-permute-start = (bf16[32,2,8,128]{3,2,1,0:T(8,128)(2,1)}, bf16[32,2,8,128]{3,2,1,0:T(8,128)(2,1)S(1)}, u32[]{:S(2)}, u32[]{:S(2)}) collective-permute-start(bf16[32,2,8,128]{3,2,1,0:T(8,128)(2,1)} %bitcast.12), channel_id=1, source_target_pairs={{0,4},{4,0},{8,12},{12,8},{16,20},{20,16},{24,28},{28,24},{1,5},{5... | collective-permute-start | bytes 393224 | tf_op jit(solution)/shard_map/ppermute | solution.py:453
  5.3 1.8 %copy-start.2 = (bf16[27,64,32]{1,2,0:T(8,128)(2,1)S(1)}, bf16[27,64,32]{1,2,0:T(8,128)(2,1)}, u32[]{:S(2)}) copy-start(bf16[27,64,32]{1,2,0:T(8,128)(2,1)} %param.5) | copy-start | bytes 331780
  5.3 1.8 %copy-start.3 = (bf16[1,32,2,8,128]{4,3,2,1,0:T(8,128)(2,1)S(1)}, bf16[1,32,2,8,128]{4,3,2,1,0:T(8,128)(2,1)}, u32[]{:S(2)}) copy-start(bf16[1,32,2,8,128]{4,3,2,1,0:T(8,128)(2,1)} %param.4) | copy-start | bytes 393220
  9.1 4.7 %collective-permute-start.2 = (bf16[6,32,256]{2,1,0:T(8,128)(2,1)S(1)}, bf16[6,32,256]{2,1,0:T(8,128)(2,1)S(1)}, u32[]{:S(2)}, u32[]{:S(2)}) collective-permute-start(bf16[6,32,256]{2,1,0:T(8,128)(2,1)S(1)} %get-tuple-element.34), channel_id=1, source_target_pairs={{0,16},{1,2},{2,1},{3,19},{16,0},{17,18},{18,17},{19,3},{4,20},{5,... | collective-permute-start | bytes 294920 | tf_op jit(solution)/shard_map/ppermute | solution.py:453
  10.6 3.2 %collective-permute-start.3 = (bf16[6,32,256]{2,1,0:T(8,128)(2,1)S(1)}, bf16[6,32,256]{2,1,0:T(8,128)(2,1)S(1)}, u32[]{:S(2)}, u32[]{:S(2)}) collective-permute-start(bf16[6,32,256]{2,1,0:T(8,128)(2,1)S(1)} %get-tuple-element.35), channel_id=1, source_target_pairs={{0,1},{1,0},{2,3},{3,2},{16,17},{17,16},{18,19},{19,18},{4,5},{5,4... | collective-permute-start | bytes 294920 | tf_op jit(solution)/shard_map/ppermute | solution.py:453
  15.9 1.7 %collective-permute-start.4 = (bf16[2,2,224,128]{3,2,1,0:T(8,128)(2,1)S(1)}, bf16[2,2,224,128]{3,2,1,0:T(8,128)(2,1)S(1)}, u32[]{:S(2)}, u32[]{:S(2)}) collective-permute-start(bf16[2,2,224,128]{3,2,1,0:T(8,128)(2,1)S(1)} %get-tuple-element.45), channel_id=1, source_target_pairs={{0,1},{1,0},{2,3},{3,2},{4,5},{5,4},{6,7},{7,6},{8,9},{9,8},{10,11... | collective-permute-start | bytes 688136 | tf_op jit(solution)/shard_map/ppermute | solution.py:461
  16.0 1.7 %collective-permute-start.5 = (f32[2,2,64,128]{3,2,1,0:T(8,128)S(1)}, f32[2,2,64,128]{3,2,1,0:T(8,128)S(1)}, u32[]{:S(2)}, u32[]{:S(2)}) collective-permute-start(f32[2,2,64,128]{3,2,1,0:T(8,128)S(1)} %get-tuple-element.47), channel_id=1, source_target_pairs={{0,1},{1,0},{2,3},{3,2},{4,5},{5,4},{6,7},{7,6},{8,9},{9,8},{10,11... | collective-permute-start | bytes 393224 | tf_op jit(solution)/shard_map/ppermute | solution.py:461
  17.7 4.4 %collective-permute-start.6 = (bf16[272,128]{1,0:T(8,128)(2,1)S(1)}, bf16[272,128]{1,0:T(8,128)(2,1)S(1)}, u32[]{:S(2)}, u32[]{:S(2)}) collective-permute-start(bf16[272,128]{1,0:T(8,128)(2,1)S(1)} %get-tuple-element.49), channel_id=1, source_target_pairs={{0,2},{2,0},{16,18},{18,16},{1,3},{3,1},{17,19},{19,17},{4,6},{6,4... | collective-permute-start | bytes 208904 | tf_op jit(solution)/shard_map/ppermute | solution.py:461
  18.8 4.5 %collective-permute-start.7 = (bf16[272,128]{1,0:T(8,128)(2,1)S(1)}, bf16[272,128]{1,0:T(8,128)(2,1)S(1)}, u32[]{:S(2)}, u32[]{:S(2)}) collective-permute-start(bf16[272,128]{1,0:T(8,128)(2,1)S(1)} %get-tuple-element.50), channel_id=1, source_target_pairs={{0,16},{2,18},{16,0},{18,2},{1,17},{3,19},{17,1},{19,3},{4,20},{6,... | collective-permute-start | bytes 208904 | tf_op jit(solution)/shard_map/ppermute | solution.py:461
  20.2 5.2 %collective-permute-start.8 = (bf16[272,128]{1,0:T(8,128)(2,1)S(1)}, bf16[272,128]{1,0:T(8,128)(2,1)S(1)}, u32[]{:S(2)}, u32[]{:S(2)}) collective-permute-start(bf16[272,128]{1,0:T(8,128)(2,1)S(1)} %get-tuple-element.51), channel_id=1, source_target_pairs={{0,18},{2,16},{16,2},{18,0},{1,19},{3,17},{17,3},{19,1},{4,22},{6,... | collective-permute-start | bytes 208904 | tf_op jit(solution)/shard_map/ppermute | solution.py:461
  25.4 7.0 %collective-permute-start.11 = (bf16[272,128]{1,0:T(8,128)(2,1)S(1)}, bf16[272,128]{1,0:T(8,128)(2,1)S(1)}, u32[]{:S(2)}, u32[]{:S(2)}) collective-permute-start(bf16[272,128]{1,0:T(8,128)(2,1)S(1)} %shard_map.76.a_ref), channel_id=1, source_target_pairs={{0,12},{4,8},{8,4},{12,0},{1,13},{5,9},{9,5},{13,1},{2,14},{6,10},... | collective-permute-start | bytes 208904 | tf_op jit(solution)/shard_map/ppermute | solution.py:461
  28.5 5.6 %collective-permute-start.10 = (bf16[272,128]{1,0:T(8,128)(2,1)S(1)}, bf16[272,128]{1,0:T(8,128)(2,1)S(1)}, u32[]{:S(2)}, u32[]{:S(2)}) collective-permute-start(bf16[272,128]{1,0:T(8,128)(2,1)S(1)} %shard_map.76.a_ref), channel_id=1, source_target_pairs={{0,8},{4,12},{8,0},{12,4},{1,9},{5,13},{9,1},{13,5},{2,10},{6,14},... | collective-permute-start | bytes 208904 | tf_op jit(solution)/shard_map/ppermute | solution.py:461
  28.7 5.4 %collective-permute-start.9 = (bf16[272,128]{1,0:T(8,128)(2,1)S(1)}, bf16[272,128]{1,0:T(8,128)(2,1)S(1)}, u32[]{:S(2)}, u32[]{:S(2)}) collective-permute-start(bf16[272,128]{1,0:T(8,128)(2,1)S(1)} %shard_map.76.a_ref), channel_id=1, source_target_pairs={{0,4},{4,0},{8,12},{12,8},{1,5},{5,1},{9,13},{13,9},{2,6},{6,2},{1... | collective-permute-start | bytes 208904 | tf_op jit(solution)/shard_map/ppermute | solution.py:461
  34.1 4.8 %collective-permute-start.13 = (bf16[288,128]{1,0:T(8,128)(2,1)S(1)}, bf16[288,128]{1,0:T(8,128)(2,1)S(1)}, u32[]{:S(2)}, u32[]{:S(2)}) collective-permute-start(bf16[288,128]{1,0:T(8,128)(2,1)S(1)} %get-tuple-element.53), channel_id=1, source_target_pairs={{0,2},{2,0},{1,3},{3,1},{4,6},{6,4},{5,7},{7,5},{8,10},{10,8},{9,1... | collective-permute-start | bytes 221192 | tf_op jit(solution)/shard_map/ppermute | solution.py:461
  35.2 4.5 %collective-permute-start.12 = (bf16[288,128]{1,0:T(8,128)(2,1)S(1)}, bf16[288,128]{1,0:T(8,128)(2,1)S(1)}, u32[]{:S(2)}, u32[]{:S(2)}) collective-permute-start(bf16[288,128]{1,0:T(8,128)(2,1)S(1)} %get-tuple-element.53), channel_id=1, source_target_pairs={{0,3},{1,2},{2,1},{3,0},{4,7},{5,6},{6,5},{7,4},{8,11},{9,10},{10,... | collective-permute-start | bytes 221192 | tf_op jit(solution)/shard_map/ppermute | solution.py:461
  35.2 2.0 %collective-permute-start.14 = (bf16[272,128]{1,0:T(8,128)(2,1)S(1)}, bf16[272,128]{1,0:T(8,128)(2,1)S(1)}, u32[]{:S(2)}, u32[]{:S(2)}) collective-permute-start(bf16[272,128]{1,0:T(8,128)(2,1)S(1)} %get-tuple-element.54.refs_0_), channel_id=1, source_target_pairs={{0,1},{1,0},{2,3},{3,2},{4,5},{5,4},{6,7},{7,6},{8,9},{9,8},{10,11... | collective-permute-start | bytes 208904 | tf_op jit(solution)/shard_map/ppermute | solution.py:461

commit v24 on v21

--- a/solution.py
+++ b/solution.py
@@ -536,7 +536,7 @@
     direct = parts == 2 and size % 16 == 0
     halves = lax.axis_size("y")
     cuts = ((7 * size, 3 * size // 2), (13 * size // 2, 2 * size))
-    length_second, length_first = 7 * size, 2 * size
+    length_second, length_first = 7 * size, 4 * size
     rows_in, rows_out = height - 2, 4
     inner_hidden, inner_second, inner_first = call(
         inner_kernel,

time: 40.7 us -> 40.7 us (level)
  transfers between devices with their start and end apart: 15 -> 15, of which waited for: 10 -> 10; matrix products, arithmetic and copies ran while one was open for 0% -> 0% of each run, Pallas kernels for 21% -> 22%
where the time goes in v24:
time: 40.7 us; the launch traced here: 40.6 us
  starting transfers between devices  17.2 us (42%)
  Pallas kernels  11.9 us (29%)
  waiting for transfers between devices  10.7 us (26%)
  between operations  0.78 us (2%)
    pallas_call x13, Pallas kernels, call(): pl.pallas_call(body, out_shape=outs, in_specs=[pl.BlockSpec(memory_space=...  11.9 us
    ppermute x11, starting transfers between devices, across(): lax.ppermute(x, axes, [(i, i ^ flip) for i in range(lax.axis_size(axes))])  10.9 us
    ppermute x11, waiting for transfers between devices, across(): lax.ppermute(x, axes, [(i, i ^ flip) for i in range(lax.axis_size(axes))])  9.11 us
    ppermute x4, starting transfers between devices, swapped(): return lax.ppermute(x, ('dp', *axes), list(enumerate(partner)))  6.36 us
    ppermute x4, waiting for transfers between devices, swapped(): return lax.ppermute(x, ('dp', *axes), list(enumerate(partner)))  1.58 us
  transfers between devices with their start and end apart: 15, of which 10 were waited for; matrix products, arithmetic and copies ran while one was open for 0% of the time, Pallas kernels for 22%

profile of v24, /device:TPU:0, one launch (start us, length us, event | category | flops | bytes accessed | tf_op | source)
XLA Modules:
  0.0 40.6 jit_solution(9332042600348456500)
XLA Ops:
  0.7 3.0 %collective-permute-start.1 = (bf16[32,2,8,128]{3,2,1,0:T(8,128)(2,1)}, bf16[32,2,8,128]{3,2,1,0:T(8,128)(2,1)S(1)}, u32[]{:S(2)}, u32[]{:S(2)}) collective-permute-start(bf16[32,2,8,128]{3,2,1,0:T(8,128)(2,1)} %bitcast.11), channel_id=1, source_target_pairs={{0,16},{4,8},{8,4},{12,28},{16,0},{20,24},{24,20},{28,12},{1,17},{... | collective-permute-start | bytes 393224 | tf_op jit(solution)/shard_map/ppermute | solution.py:453
  3.7 1.7 %collective-permute-start = (bf16[32,2,8,128]{3,2,1,0:T(8,128)(2,1)}, bf16[32,2,8,128]{3,2,1,0:T(8,128)(2,1)S(1)}, u32[]{:S(2)}, u32[]{:S(2)}) collective-permute-start(bf16[32,2,8,128]{3,2,1,0:T(8,128)(2,1)} %bitcast.12), channel_id=1, source_target_pairs={{0,4},{4,0},{8,12},{12,8},{16,20},{20,16},{24,28},{28,24},{1,5},{5... | collective-permute-start | bytes 393224 | tf_op jit(solution)/shard_map/ppermute | solution.py:453
  5.4 1.7 %shard_map.68 = (bf16[2,128,1024]{2,1,0:T(8,128)(2,1)S(1)}, f32[4,64,1280]{2,1,0:T(8,128)S(1)}) custom-call(bf16[128,2,8,128]{3,2,1,0:T(8,128)(2,1)S(1)} %bitcast.7, bf16[27,64,128]{2,1,0:T(8,128)(2,1)S(1)} %bitcast.8, bf16[128,256]{1,0:T(8,128)(2,1)S(1)} %shard_map.67.blank_ref), custom_call_target="tpu_custom_call" | custom-call | flops 1100000000 | bytes 2867200 | tf_op jit(solution)/shard_map/pallas_call | solution.py:18
  7.6 1.2 %collective-permute-done.one_ref = bf16[32,2,8,128]{3,2,1,0:T(8,128)(2,1)S(1)} collective-permute-done((bf16[32,2,8,128]{3,2,1,0:T(8,128)(2,1)}, bf16[32,2,8,128]{3,2,1,0:T(8,128)(2,1)S(1)}, u32[]{:S(2)}, u32[]{:S(2)}) %collective-permute-start) | collective-permute-done | bytes 131104 | tf_op jit(solution)/shard_map/ppermute | solution.py:453
  9.1 1.5 %collective-permute-start.2 = (bf16[6,32,256]{2,1,0:T(8,128)(2,1)S(1)}, bf16[6,32,256]{2,1,0:T(8,128)(2,1)S(1)}, u32[]{:S(2)}, u32[]{:S(2)}) collective-permute-start(bf16[6,32,256]{2,1,0:T(8,128)(2,1)S(1)} %get-tuple-element.34), channel_id=1, source_target_pairs={{0,16},{1,2},{2,1},{3,19},{16,0},{17,18},{18,17},{19,3},{4,20},{5,... | collective-permute-start | bytes 294920 | tf_op jit(solution)/shard_map/ppermute | solution.py:453
  10.8 2.6 %shard_map.71 = (bf16[4,64,768]{2,1,0:T(8,128)(2,1)S(1)}, f32[1152,192]{1,0:T(8,128)S(1)}, f32[192,288]{1,0:T(8,128)S(1)}) custom-call(bf16[6,32,1024]{2,1,0:T(8,128)(2,1)S(1)} %get-tuple-element.33.deep_ref, bf16[192,288]{1,0:T(8,128)(2,1)S(1)} %get-tuple-element.36.w1_ref, bf16[2,384,1024]{2,1,0:T(8,128)(2,1)S(1)} %get-tuple-element.38.moved_ref, ...), custom_call_target="tpu_custom_call" | custom-call | flops 1500000000 | bytes 4886528 | tf_op jit(solution)/shard_map/pallas_call | solution.py:18
  13.8 1.5 %shard_map.72 = (bf16[4,64,1280]{2,1,0:T(8,128)(2,1)S(1)}, f32[2,2,128,128]{3,2,1,0:T(8,128)S(1)}, f32[2,2,128,128]{3,2,1,0:T(8,128)S(1)}) custom-call(bf16[6,32,1024]{2,1,0:T(8,128)(2,1)S(1)} %get-tuple-element.33.deep_ref, bf16[6,32,256]{2,1,0:T(8,128)(2,1)S(1)} %collective-permute-done.2.two_ref, bf16[6,32,256]{2,1,0:T(8,128)(2,1)S(1)} %collective-permute-done.3.one_ref, ...), custom_call_target="tpu_custom_call" | custom-call | flops 1000000000 | bytes 3805184 | tf_op jit(solution)/shard_map/pallas_call | solution.py:18
  16.6 1.1 %collective-permute-done.4.refs_1_ = bf16[2,2,224,128]{3,2,1,0:T(8,128)(2,1)S(1)} collective-permute-done((bf16[2,2,224,128]{3,2,1,0:T(8,128)(2,1)S(1)}, bf16[2,2,224,128]{3,2,1,0:T(8,128)(2,1)S(1)}, u32[]{:S(2)}, u32[]{:S(2)}) %collective-permute-start.4) | collective-permute-done | bytes 229408 | tf_op jit(solution)/shard_map/ppermute | solution.py:461
  17.8 1.5 %collective-permute-start.6 = (bf16[272,128]{1,0:T(8,128)(2,1)S(1)}, bf16[272,128]{1,0:T(8,128)(2,1)S(1)}, u32[]{:S(2)}, u32[]{:S(2)}) collective-permute-start(bf16[272,128]{1,0:T(8,128)(2,1)S(1)} %get-tuple-element.49), channel_id=1, source_target_pairs={{0,16},{2,18},{16,0},{18,2},{1,17},{3,19},{17,1},{19,3},{4,20},{6,... | collective-permute-start | bytes 208904 | tf_op jit(solution)/shard_map/ppermute | solution.py:461
  19.3 0.9 %collective-permute-start.7 = (bf16[272,128]{1,0:T(8,128)(2,1)S(1)}, bf16[272,128]{1,0:T(8,128)(2,1)S(1)}, u32[]{:S(2)}, u32[]{:S(2)}) collective-permute-start(bf16[272,128]{1,0:T(8,128)(2,1)S(1)} %get-tuple-element.50), channel_id=1, source_target_pairs={{0,2},{2,0},{16,18},{18,16},{1,3},{3,1},{17,19},{19,17},{4,6},{6,4... | collective-permute-start | bytes 208904 | tf_op jit(solution)/shard_map/ppermute | solution.py:461
  20.2 1.1 %collective-permute-start.8 = (bf16[272,128]{1,0:T(8,128)(2,1)S(1)}, bf16[272,128]{1,0:T(8,128)(2,1)S(1)}, u32[]{:S(2)}, u32[]{:S(2)}) collective-permute-start(bf16[272,128]{1,0:T(8,128)(2,1)S(1)} %get-tuple-element.51), channel_id=1, source_target_pairs={{0,18},{2,16},{16,2},{18,0},{1,19},{3,17},{17,3},{19,1},{4,22},{6,... | collective-permute-start | bytes 208904 | tf_op jit(solution)/shard_map/ppermute | solution.py:461
  21.3 1.0 %collective-permute-done.6.refs_0_ = bf16[272,128]{1,0:T(8,128)(2,1)S(1)} collective-permute-done((bf16[272,128]{1,0:T(8,128)(2,1)S(1)}, bf16[272,128]{1,0:T(8,128)(2,1)S(1)}, u32[]{:S(2)}, u32[]{:S(2)}) %collective-permute-start.6) | collective-permute-done | bytes 69664 | tf_op jit(solution)/shard_map/ppermute | solution.py:461
  22.3 1.3 %collective-permute-done.7.refs_1_ = bf16[272,128]{1,0:T(8,128)(2,1)S(1)} collective-permute-done((bf16[272,128]{1,0:T(8,128)(2,1)S(1)}, bf16[272,128]{1,0:T(8,128)(2,1)S(1)}, u32[]{:S(2)}, u32[]{:S(2)}) %collective-permute-start.7) | collective-permute-done | bytes 69664 | tf_op jit(solution)/shard_map/ppermute | solution.py:461
  23.6 1.8 %collective-permute-done.8.refs_2_ = bf16[272,128]{1,0:T(8,128)(2,1)S(1)} collective-permute-done((bf16[272,128]{1,0:T(8,128)(2,1)S(1)}, bf16[272,128]{1,0:T(8,128)(2,1)S(1)}, u32[]{:S(2)}, u32[]{:S(2)}) %collective-permute-start.8) | collective-permute-done | bytes 69664 | tf_op jit(solution)/shard_map/ppermute | solution.py:461
  25.5 2.8 %collective-permute-start.11 = (bf16[272,128]{1,0:T(8,128)(2,1)S(1)}, bf16[272,128]{1,0:T(8,128)(2,1)S(1)}, u32[]{:S(2)}, u32[]{:S(2)}) collective-permute-start(bf16[272,128]{1,0:T(8,128)(2,1)S(1)} %shard_map.76.a_ref), channel_id=1, source_target_pairs={{0,12},{4,8},{8,4},{12,0},{1,13},{5,9},{9,5},{13,1},{2,14},{6,10},... | collective-permute-start | bytes 208904 | tf_op jit(solution)/shard_map/ppermute | solution.py:461
  28.7 1.2 %collective-permute-start.9 = (bf16[272,128]{1,0:T(8,128)(2,1)S(1)}, bf16[272,128]{1,0:T(8,128)(2,1)S(1)}, u32[]{:S(2)}, u32[]{:S(2)}) collective-permute-start(bf16[272,128]{1,0:T(8,128)(2,1)S(1)} %shard_map.76.a_ref), channel_id=1, source_target_pairs={{0,4},{4,0},{8,12},{12,8},{1,5},{5,1},{9,13},{13,9},{2,6},{6,2},{1... | collective-permute-start | bytes 208904 | tf_op jit(solution)/shard_map/ppermute | solution.py:461
  29.9 2.5 %shard_map.73 = (bf16[128,2,8,128]{3,2,1,0:T(8,128)(2,1)}, f32[8,128]{1,0:T(8,128)S(1)}) custom-call(bf16[4,64,1280]{2,1,0:T(8,128)(2,1)S(1)} %get-tuple-element.41.hidden_ref, bf16[27,64,128]{2,1,0:T(8,128)(2,1)S(1)} %bitcast.9), custom_call_target="tpu_custom_call" | custom-call | flops 900000000 | bytes 1626112 | tf_op jit(solution)/shard_map/pallas_call | solution.py:18
  32.4 1.5 %collective-permute-done.10.c_ref = bf16[272,128]{1,0:T(8,128)(2,1)S(1)} collective-permute-done((bf16[272,128]{1,0:T(8,128)(2,1)S(1)}, bf16[272,128]{1,0:T(8,128)(2,1)S(1)}, u32[]{:S(2)}, u32[]{:S(2)}) %collective-permute-start.10) | collective-permute-done | bytes 69664 | tf_op jit(solution)/shard_map/ppermute | solution.py:461
  34.0 1.1 %collective-permute-start.13 = (bf16[288,128]{1,0:T(8,128)(2,1)S(1)}, bf16[288,128]{1,0:T(8,128)(2,1)S(1)}, u32[]{:S(2)}, u32[]{:S(2)}) collective-permute-start(bf16[288,128]{1,0:T(8,128)(2,1)S(1)} %get-tuple-element.53), channel_id=1, source_target_pairs={{0,2},{2,0},{1,3},{3,1},{4,6},{6,4},{5,7},{7,5},{8,10},{10,8},{9,1... | collective-permute-start | bytes 221192 | tf_op jit(solution)/shard_map/ppermute | solution.py:461
  35.1 1.1 %collective-permute-start.14 = (bf16[272,128]{1,0:T(8,128)(2,1)S(1)}, bf16[272,128]{1,0:T(8,128)(2,1)S(1)}, u32[]{:S(2)}, u32[]{:S(2)}) collective-permute-start(bf16[272,128]{1,0:T(8,128)(2,1)S(1)} %get-tuple-element.54.refs_0_), channel_id=1, source_target_pairs={{0,1},{1,0},{2,3},{3,2},{4,5},{5,4},{6,7},{7,6},{8,9},{9,8},{10,11... | collective-permute-start | bytes 208904 | tf_op jit(solution)/shard_map/ppermute | solution.py:461
  36.2 0.9 %collective-permute-done.14.refs_1_ = bf16[272,128]{1,0:T(8,128)(2,1)S(1)} collective-permute-done((bf16[272,128]{1,0:T(8,128)(2,1)S(1)}, bf16[272,128]{1,0:T(8,128)(2,1)S(1)}, u32[]{:S(2)}, u32[]{:S(2)}) %collective-permute-start.14) | collective-permute-done | bytes 69664 | tf_op jit(solution)/shard_map/ppermute | solution.py:461
  37.1 1.0 %shard_map.78 = (f32[9,3,32,32]{3,2,1,0:T(8,128)}, f32[3,9,64,64]{3,2,1,0:T(8,128)}) custom-call(bf16[272,128]{1,0:T(8,128)(2,1)S(1)} %get-tuple-element.54.refs_0_, bf16[272,128]{1,0:T(8,128)(2,1)S(1)} %collective-permute-done.14.refs_1_), custom_call_target="tpu_custom_call" | custom-call | bytes 692224 | tf_op jit(solution)/shard_map/pallas_call | solution.py:18
  38.1 0.7 %collective-permute-done.13.refs_1_ = bf16[288,128]{1,0:T(8,128)(2,1)S(1)} collective-permute-done((bf16[288,128]{1,0:T(8,128)(2,1)S(1)}, bf16[288,128]{1,0:T(8,128)(2,1)S(1)}, u32[]{:S(2)}, u32[]{:S(2)}) %collective-permute-start.13) | collective-permute-done | bytes 73760 | tf_op jit(solution)/shard_map/ppermute | solution.py:461
  39.6 1.0 %shard_map.79 = (f32[9,3,32,32]{3,2,1,0:T(8,128)}, f32[3,9,64,64]{3,2,1,0:T(8,128)}) custom-call(bf16[288,128]{1,0:T(8,128)(2,1)S(1)} %collective-permute-done.12.refs_0_, bf16[288,128]{1,0:T(8,128)(2,1)S(1)} %collective-permute-done.13.refs_1_, f32[9,3,32,32]{3,2,1,0:T(8,128)} %get-tuple-element.55.refs_2_, ...), custom_call_target="tpu_custom_call", output_to_operand_aliasing={{0}: (2, {}), {1}: (3, {})} | custom-call | bytes 1253376 | tf_op jit(solution)/shard_map/pallas_call | solution.py:18
  (27 shorter events, 4.0 us)
Async XLA Ops:
  0.6 4.7 %copy-start = (bf16[1,128,2,8,128]{4,3,2,1,0:T(8,128)(2,1)S(1)}, bf16[1,128,2,8,128]{4,3,2,1,0:T(8,128)(2,1)}, u32[]{:S(2)}) copy-start(bf16[1,128,2,8,128]{4,3,2,1,0:T(8,128)(2,1)} %param.7) | copy-start | bytes 1572868
  0.6 4.7 %copy-start.1 = (bf16[27,128,64]{1,2,0:T(8,128)(2,1)S(1)}, bf16[27,128,64]{1,2,0:T(8,128)(2,1)}, u32[]{:S(2)}) copy-start(bf16[27,128,64]{1,2,0:T(8,128)(2,1)} %param.6) | copy-start | bytes 1327108
  0.7 7.0 %collective-permute-start.1 = (bf16[32,2,8,128]{3,2,1,0:T(8,128)(2,1)}, bf16[32,2,8,128]{3,2,1,0:T(8,128)(2,1)S(1)}, u32[]{:S(2)}, u32[]{:S(2)}) collective-permute-start(bf16[32,2,8,128]{3,2,1,0:T(8,128)(2,1)} %bitcast.11), channel_id=1, source_target_pairs={{0,16},{4,8},{8,4},{12,28},{16,0},{20,24},{24,20},{28,12},{1,17},{... | collective-permute-start | bytes 393224 | tf_op jit(solution)/shard_map/ppermute | solution.py:453
  3.7 5.2 %collective-permute-start = (bf16[32,2,8,128]{3,2,1,0:T(8,128)(2,1)}, bf16[32,2,8,128]{3,2,1,0:T(8,128)(2,1)S(1)}, u32[]{:S(2)}, u32[]{:S(2)}) collective-permute-start(bf16[32,2,8,128]{3,2,1,0:T(8,128)(2,1)} %bitcast.12), channel_id=1, source_target_pairs={{0,4},{4,0},{8,12},{12,8},{16,20},{20,16},{24,28},{28,24},{1,5},{5... | collective-permute-start | bytes 393224 | tf_op jit(solution)/shard_map/ppermute | solution.py:453
  5.3 1.8 %copy-start.2 = (bf16[27,64,32]{1,2,0:T(8,128)(2,1)S(1)}, bf16[27,64,32]{1,2,0:T(8,128)(2,1)}, u32[]{:S(2)}) copy-start(bf16[27,64,32]{1,2,0:T(8,128)(2,1)} %param.5) | copy-start | bytes 331780
  5.3 1.8 %copy-start.3 = (bf16[1,32,2,8,128]{4,3,2,1,0:T(8,128)(2,1)S(1)}, bf16[1,32,2,8,128]{4,3,2,1,0:T(8,128)(2,1)}, u32[]{:S(2)}) copy-start(bf16[1,32,2,8,128]{4,3,2,1,0:T(8,128)(2,1)} %param.4) | copy-start | bytes 393220
  9.1 4.7 %collective-permute-start.2 = (bf16[6,32,256]{2,1,0:T(8,128)(2,1)S(1)}, bf16[6,32,256]{2,1,0:T(8,128)(2,1)S(1)}, u32[]{:S(2)}, u32[]{:S(2)}) collective-permute-start(bf16[6,32,256]{2,1,0:T(8,128)(2,1)S(1)} %get-tuple-element.34), channel_id=1, source_target_pairs={{0,16},{1,2},{2,1},{3,19},{16,0},{17,18},{18,17},{19,3},{4,20},{5,... | collective-permute-start | bytes 294920 | tf_op jit(solution)/shard_map/ppermute | solution.py:453
  10.6 3.2 %collective-permute-start.3 = (bf16[6,32,256]{2,1,0:T(8,128)(2,1)S(1)}, bf16[6,32,256]{2,1,0:T(8,128)(2,1)S(1)}, u32[]{:S(2)}, u32[]{:S(2)}) collective-permute-start(bf16[6,32,256]{2,1,0:T(8,128)(2,1)S(1)} %get-tuple-element.35), channel_id=1, source_target_pairs={{0,1},{1,0},{2,3},{3,2},{16,17},{17,16},{18,19},{19,18},{4,5},{5,4... | collective-permute-start | bytes 294920 | tf_op jit(solution)/shard_map/ppermute | solution.py:453
  15.4 2.3 %collective-permute-start.5 = (f32[2,2,128,128]{3,2,1,0:T(8,128)S(1)}, f32[2,2,128,128]{3,2,1,0:T(8,128)S(1)}, u32[]{:S(2)}, u32[]{:S(2)}) collective-permute-start(f32[2,2,128,128]{3,2,1,0:T(8,128)S(1)} %get-tuple-element.47), channel_id=1, source_target_pairs={{0,1},{1,0},{2,3},{3,2},{4,5},{5,4},{6,7},{7,6},{8,9},{9,8},{10,11... | collective-permute-start | bytes 786440 | tf_op jit(solution)/shard_map/ppermute | solution.py:461
  16.0 1.7 %collective-permute-start.4 = (bf16[2,2,224,128]{3,2,1,0:T(8,128)(2,1)S(1)}, bf16[2,2,224,128]{3,2,1,0:T(8,128)(2,1)S(1)}, u32[]{:S(2)}, u32[]{:S(2)}) collective-permute-start(bf16[2,2,224,128]{3,2,1,0:T(8,128)(2,1)S(1)} %get-tuple-element.45), channel_id=1, source_target_pairs={{0,1},{1,0},{2,3},{3,2},{4,5},{5,4},{6,7},{7,6},{8,9},{9,8},{10,11... | collective-permute-start | bytes 688136 | tf_op jit(solution)/shard_map/ppermute | solution.py:461
  17.8 4.5 %collective-permute-start.6 = (bf16[272,128]{1,0:T(8,128)(2,1)S(1)}, bf16[272,128]{1,0:T(8,128)(2,1)S(1)}, u32[]{:S(2)}, u32[]{:S(2)}) collective-permute-start(bf16[272,128]{1,0:T(8,128)(2,1)S(1)} %get-tuple-element.49), channel_id=1, source_target_pairs={{0,16},{2,18},{16,0},{18,2},{1,17},{3,19},{17,1},{19,3},{4,20},{6,... | collective-permute-start | bytes 208904 | tf_op jit(solution)/shard_map/ppermute | solution.py:461
  19.3 4.3 %collective-permute-start.7 = (bf16[272,128]{1,0:T(8,128)(2,1)S(1)}, bf16[272,128]{1,0:T(8,128)(2,1)S(1)}, u32[]{:S(2)}, u32[]{:S(2)}) collective-permute-start(bf16[272,128]{1,0:T(8,128)(2,1)S(1)} %get-tuple-element.50), channel_id=1, source_target_pairs={{0,2},{2,0},{16,18},{18,16},{1,3},{3,1},{17,19},{19,17},{4,6},{6,4... | collective-permute-start | bytes 208904 | tf_op jit(solution)/shard_map/ppermute | solution.py:461
  20.2 5.2 %collective-permute-start.8 = (bf16[272,128]{1,0:T(8,128)(2,1)S(1)}, bf16[272,128]{1,0:T(8,128)(2,1)S(1)}, u32[]{:S(2)}, u32[]{:S(2)}) collective-permute-start(bf16[272,128]{1,0:T(8,128)(2,1)S(1)} %get-tuple-element.51), channel_id=1, source_target_pairs={{0,18},{2,16},{16,2},{18,0},{1,19},{3,17},{17,3},{19,1},{4,22},{6,... | collective-permute-start | bytes 208904 | tf_op jit(solution)/shard_map/ppermute | solution.py:461
  25.5 7.0 %collective-permute-start.11 = (bf16[272,128]{1,0:T(8,128)(2,1)S(1)}, bf16[272,128]{1,0:T(8,128)(2,1)S(1)}, u32[]{:S(2)}, u32[]{:S(2)}) collective-permute-start(bf16[272,128]{1,0:T(8,128)(2,1)S(1)} %shard_map.76.a_ref), channel_id=1, source_target_pairs={{0,12},{4,8},{8,4},{12,0},{1,13},{5,9},{9,5},{13,1},{2,14},{6,10},... | collective-permute-start | bytes 208904 | tf_op jit(solution)/shard_map/ppermute | solution.py:461
  28.2 5.7 %collective-permute-start.10 = (bf16[272,128]{1,0:T(8,128)(2,1)S(1)}, bf16[272,128]{1,0:T(8,128)(2,1)S(1)}, u32[]{:S(2)}, u32[]{:S(2)}) collective-permute-start(bf16[272,128]{1,0:T(8,128)(2,1)S(1)} %shard_map.76.a_ref), channel_id=1, source_target_pairs={{0,8},{4,12},{8,0},{12,4},{1,9},{5,13},{9,1},{13,5},{2,10},{6,14},... | collective-permute-start | bytes 208904 | tf_op jit(solution)/shard_map/ppermute | solution.py:461
  28.7 5.3 %collective-permute-start.9 = (bf16[272,128]{1,0:T(8,128)(2,1)S(1)}, bf16[272,128]{1,0:T(8,128)(2,1)S(1)}, u32[]{:S(2)}, u32[]{:S(2)}) collective-permute-start(bf16[272,128]{1,0:T(8,128)(2,1)S(1)} %shard_map.76.a_ref), channel_id=1, source_target_pairs={{0,4},{4,0},{8,12},{12,8},{1,5},{5,1},{9,13},{13,9},{2,6},{6,2},{1... | collective-permute-start | bytes 208904 | tf_op jit(solution)/shard_map/ppermute | solution.py:461
  34.0 4.9 %collective-permute-start.13 = (bf16[288,128]{1,0:T(8,128)(2,1)S(1)}, bf16[288,128]{1,0:T(8,128)(2,1)S(1)}, u32[]{:S(2)}, u32[]{:S(2)}) collective-permute-start(bf16[288,128]{1,0:T(8,128)(2,1)S(1)} %get-tuple-element.53), channel_id=1, source_target_pairs={{0,2},{2,0},{1,3},{3,1},{4,6},{6,4},{5,7},{7,5},{8,10},{10,8},{9,1... | collective-permute-start | bytes 221192 | tf_op jit(solution)/shard_map/ppermute | solution.py:461
  35.1 4.5 %collective-permute-start.12 = (bf16[288,128]{1,0:T(8,128)(2,1)S(1)}, bf16[288,128]{1,0:T(8,128)(2,1)S(1)}, u32[]{:S(2)}, u32[]{:S(2)}) collective-permute-start(bf16[288,128]{1,0:T(8,128)(2,1)S(1)} %get-tuple-element.53), channel_id=1, source_target_pairs={{0,3},{1,2},{2,1},{3,0},{4,7},{5,6},{6,5},{7,4},{8,11},{9,10},{10,... | collective-permute-start | bytes 221192 | tf_op jit(solution)/shard_map/ppermute | solution.py:461
  35.1 2.0 %collective-permute-start.14 = (bf16[272,128]{1,0:T(8,128)(2,1)S(1)}, bf16[272,128]{1,0:T(8,128)(2,1)S(1)}, u32[]{:S(2)}, u32[]{:S(2)}) collective-permute-start(bf16[272,128]{1,0:T(8,128)(2,1)S(1)} %get-tuple-element.54.refs_0_), channel_id=1, source_target_pairs={{0,1},{1,0},{2,3},{3,2},{4,5},{5,4},{6,7},{7,6},{8,9},{9,8},{10,11... | collective-permute-start | bytes 208904 | tf_op jit(solution)/shard_map/ppermute | solution.py:461

commit v25 on v23

--- a/solution.py
+++ b/solution.py
@@ -354,8 +354,9 @@
         return jnp.where(at[1] == 0, one, two)
 
     kept_ref[...] = total(0, 0)
-    for (x, y), send_ref in zip(moves, send_refs, strict=True):
-        send_ref[...] = total(x, y).astype(BF)
+    core = lax.axis_index("core") == 1
+    for (one, two), send_ref in zip(moves, send_refs, strict=True):
+        send_ref[...] = jnp.where(core, total(*two), total(*one)).astype(BF)
 
 
 def total_kernel(kept_ref, *refs):
@@ -453,6 +454,17 @@
     return lax.ppermute(x, ("dp", *axes), list(enumerate(partner)))
 
 
+def across_plane(x, move):
+    parts, halves = lax.axis_size("dp"), lax.axis_size("y")
+    partner = [
+        ((part ^ move[core][0]) * halves + (y ^ move[core][1])) * 2 + core
+        for part in range(parts)
+        for y in range(halves)
+        for core in range(2)
+    ]
+    return lax.ppermute(x, ("dp", "y", "core"), list(enumerate(partner)))
+
+
 def across(x, *moves):
     axes = tuple(axis for axis, _ in moves)
     flip = 0
@@ -569,10 +581,10 @@
         flops=4_000_000_000,
     )
     if direct:
-        moves = [(0, 1), (1, 0), (1, 1)]
+        moves = [((0, 1), (1, 0)), ((1, 0), (0, 1)), ((1, 1), (1, 1))]
         grads = [second, first]
     else:
-        moves = [(0, 1)]
+        moves = [((0, 1), (0, 1))]
         blocks = second[0].reshape(14, parts, 2, size, LANES).transpose(1, 2, 0, 3, 4)
         tail = blocks[:, :, 13, :, :mid]
         tail = jnp.concatenate([tail[:, :, : size // 2], tail[:, :, size // 2 :]], axis=-1)
@@ -586,7 +598,7 @@
         [shape(block, F32)] + [shape(block, BF)] * len(moves),
         [x for keep, send in grads for x in (keep, across(send, ("core", 1)))],
     )
-    gots = [across(send, ("dp", x), ("y", y)) for send, (x, y) in zip(sends, moves, strict=True)]
+    gots = [across_plane(send, move) for send, move in zip(sends, moves, strict=True)]
     (share,) = call(total_kernel, [shape(block, BF)], [kept, *gots])
     features, token = call(
         features_kernel,

time: 40.9 us -> 40.9 us (level)
    ppermute x0 -> x3, waiting for transfers between devices: none -> 4.1 us  [across_plane(): return lax.ppermute(x, ('dp', 'y', 'core'), list(enumerate(partner)))]
    ppermute x11 -> x8, waiting for transfers between devices: 9.32 us -> 5.24 us  [across(): lax.ppermute(x, axes, [(i, i ^ flip) for i in range(lax.axis_size(axes))])]
    ppermute x0 -> x3, starting transfers between devices: none -> 3.55 us  [across_plane(): return lax.ppermute(x, ('dp', 'y', 'core'), list(enumerate(partner)))]
    ppermute x11 -> x8, starting transfers between devices: 10.8 us -> 7.23 us  [across(): lax.ppermute(x, axes, [(i, i ^ flip) for i in range(lax.axis_size(axes))])]
where the time goes in v25:
time: 40.9 us; the launch traced here: 40.7 us
  starting transfers between devices  17.1 us (42%)
  Pallas kernels  11.9 us (29%)
  waiting for transfers between devices  10.9 us (27%)
  between operations  0.78 us (2%)
    pallas_call x13, Pallas kernels, call(): pl.pallas_call(body, out_shape=outs, in_specs=[pl.BlockSpec(memory_space=...  11.9 us
    ppermute x8, starting transfers between devices, across(): lax.ppermute(x, axes, [(i, i ^ flip) for i in range(lax.axis_size(axes))])  7.23 us
    ppermute x4, starting transfers between devices, swapped(): return lax.ppermute(x, ('dp', *axes), list(enumerate(partner)))  6.36 us
    ppermute x8, waiting for transfers between devices, across(): lax.ppermute(x, axes, [(i, i ^ flip) for i in range(lax.axis_size(axes))])  5.24 us
    ppermute x3, waiting for transfers between devices, across_plane(): return lax.ppermute(x, ('dp', 'y', 'core'), list(enumerate(partner)))  4.1 us
    ppermute x3, starting transfers between devices, across_plane(): return lax.ppermute(x, ('dp', 'y', 'core'), list(enumerate(partner)))  3.55 us
    ppermute x4, waiting for transfers between devices, swapped(): return lax.ppermute(x, ('dp', *axes), list(enumerate(partner)))  1.58 us
  transfers between devices with their start and end apart: 15, of which 10 were waited for; matrix products, arithmetic and copies ran while one was open for 0% of the time, Pallas kernels for 20%

profile of v25, /device:TPU:0, one launch (start us, length us, event | category | flops | bytes accessed | tf_op | source)
XLA Modules:
  0.0 40.7 jit_solution(8257672758273649655)
XLA Ops:
  0.7 3.0 %collective-permute-start.1 = (bf16[32,2,8,128]{3,2,1,0:T(8,128)(2,1)}, bf16[32,2,8,128]{3,2,1,0:T(8,128)(2,1)S(1)}, u32[]{:S(2)}, u32[]{:S(2)}) collective-permute-start(bf16[32,2,8,128]{3,2,1,0:T(8,128)(2,1)} %bitcast.11), channel_id=1, source_target_pairs={{0,16},{4,8},{8,4},{12,28},{16,0},{20,24},{24,20},{28,12},{1,17},{... | collective-permute-start | bytes 393224 | tf_op jit(solution)/shard_map/ppermute | solution.py:454
  3.7 1.7 %collective-permute-start = (bf16[32,2,8,128]{3,2,1,0:T(8,128)(2,1)}, bf16[32,2,8,128]{3,2,1,0:T(8,128)(2,1)S(1)}, u32[]{:S(2)}, u32[]{:S(2)}) collective-permute-start(bf16[32,2,8,128]{3,2,1,0:T(8,128)(2,1)} %bitcast.12), channel_id=1, source_target_pairs={{0,4},{4,0},{8,12},{12,8},{16,20},{20,16},{24,28},{28,24},{1,5},{5... | collective-permute-start | bytes 393224 | tf_op jit(solution)/shard_map/ppermute | solution.py:454
  5.4 1.7 %shard_map.68 = (bf16[2,128,1024]{2,1,0:T(8,128)(2,1)S(1)}, f32[4,64,1280]{2,1,0:T(8,128)S(1)}) custom-call(bf16[128,2,8,128]{3,2,1,0:T(8,128)(2,1)S(1)} %bitcast.7, bf16[27,64,128]{2,1,0:T(8,128)(2,1)S(1)} %bitcast.8, bf16[128,256]{1,0:T(8,128)(2,1)S(1)} %shard_map.67.blank_ref), custom_call_target="tpu_custom_call" | custom-call | flops 1100000000 | bytes 2867200 | tf_op jit(solution)/shard_map/pallas_call | solution.py:18
  7.6 1.2 %collective-permute-done.one_ref = bf16[32,2,8,128]{3,2,1,0:T(8,128)(2,1)S(1)} collective-permute-done((bf16[32,2,8,128]{3,2,1,0:T(8,128)(2,1)}, bf16[32,2,8,128]{3,2,1,0:T(8,128)(2,1)S(1)}, u32[]{:S(2)}, u32[]{:S(2)}) %collective-permute-start) | collective-permute-done | bytes 131104 | tf_op jit(solution)/shard_map/ppermute | solution.py:454
  9.1 1.5 %collective-permute-start.2 = (bf16[6,32,256]{2,1,0:T(8,128)(2,1)S(1)}, bf16[6,32,256]{2,1,0:T(8,128)(2,1)S(1)}, u32[]{:S(2)}, u32[]{:S(2)}) collective-permute-start(bf16[6,32,256]{2,1,0:T(8,128)(2,1)S(1)} %get-tuple-element.34), channel_id=1, source_target_pairs={{0,16},{1,2},{2,1},{3,19},{16,0},{17,18},{18,17},{19,3},{4,20},{5,... | collective-permute-start | bytes 294920 | tf_op jit(solution)/shard_map/ppermute | solution.py:454
  10.8 2.6 %shard_map.71 = (bf16[4,64,768]{2,1,0:T(8,128)(2,1)S(1)}, f32[1152,192]{1,0:T(8,128)S(1)}, f32[192,288]{1,0:T(8,128)S(1)}) custom-call(bf16[6,32,1024]{2,1,0:T(8,128)(2,1)S(1)} %get-tuple-element.33.deep_ref, bf16[192,288]{1,0:T(8,128)(2,1)S(1)} %get-tuple-element.36.w1_ref, bf16[2,384,1024]{2,1,0:T(8,128)(2,1)S(1)} %get-tuple-element.38.moved_ref, ...), custom_call_target="tpu_custom_call" | custom-call | flops 1500000000 | bytes 4886528 | tf_op jit(solution)/shard_map/pallas_call | solution.py:18
  13.8 1.5 %shard_map.72 = (bf16[4,64,1280]{2,1,0:T(8,128)(2,1)S(1)}, f32[2,2,64,128]{3,2,1,0:T(8,128)S(1)}, f32[2,2,64,128]{3,2,1,0:T(8,128)S(1)}) custom-call(bf16[6,32,1024]{2,1,0:T(8,128)(2,1)S(1)} %get-tuple-element.33.deep_ref, bf16[6,32,256]{2,1,0:T(8,128)(2,1)S(1)} %collective-permute-done.2.two_ref, bf16[6,32,256]{2,1,0:T(8,128)(2,1)S(1)} %collective-permute-done.3.one_ref, ...), custom_call_target="tpu_custom_call" | custom-call | flops 1000000000 | bytes 3543040 | tf_op jit(solution)/shard_map/pallas_call | solution.py:18
  16.5 1.2 %collective-permute-done.5.refs_3_ = f32[2,2,64,128]{3,2,1,0:T(8,128)S(1)} collective-permute-done((f32[2,2,64,128]{3,2,1,0:T(8,128)S(1)}, f32[2,2,64,128]{3,2,1,0:T(8,128)S(1)}, u32[]{:S(2)}, u32[]{:S(2)}) %collective-permute-start.5) | collective-permute-done | bytes 131104 | tf_op jit(solution)/shard_map/ppermute | solution.py:473
  17.7 1.0 %collective-permute-start.6 = (bf16[272,128]{1,0:T(8,128)(2,1)S(1)}, bf16[272,128]{1,0:T(8,128)(2,1)S(1)}, u32[]{:S(2)}, u32[]{:S(2)}) collective-permute-start(bf16[272,128]{1,0:T(8,128)(2,1)S(1)} %get-tuple-element.49), channel_id=1, source_target_pairs={{0,2},{1,17},{2,0},{3,19},{16,18},{17,1},{18,16},{19,3},{4,6},{5,2... | collective-permute-start | bytes 208904 | tf_op jit(solution)/shard_map/ppermute | solution.py:465
  18.8 1.4 %collective-permute-start.7 = (bf16[272,128]{1,0:T(8,128)(2,1)S(1)}, bf16[272,128]{1,0:T(8,128)(2,1)S(1)}, u32[]{:S(2)}, u32[]{:S(2)}) collective-permute-start(bf16[272,128]{1,0:T(8,128)(2,1)S(1)} %get-tuple-element.50), channel_id=1, source_target_pairs={{0,16},{1,3},{2,18},{3,1},{16,0},{17,19},{18,2},{19,17},{4,20},{5,... | collective-permute-start | bytes 208904 | tf_op jit(solution)/shard_map/ppermute | solution.py:465
  20.2 1.1 %collective-permute-start.8 = (bf16[272,128]{1,0:T(8,128)(2,1)S(1)}, bf16[272,128]{1,0:T(8,128)(2,1)S(1)}, u32[]{:S(2)}, u32[]{:S(2)}) collective-permute-start(bf16[272,128]{1,0:T(8,128)(2,1)S(1)} %get-tuple-element.51), channel_id=1, source_target_pairs={{0,18},{1,19},{2,16},{3,17},{16,2},{17,3},{18,0},{19,1},{4,22},{5,... | collective-permute-start | bytes 208904 | tf_op jit(solution)/shard_map/ppermute | solution.py:465
  21.3 1.3 %collective-permute-done.6.refs_0_ = bf16[272,128]{1,0:T(8,128)(2,1)S(1)} collective-permute-done((bf16[272,128]{1,0:T(8,128)(2,1)S(1)}, bf16[272,128]{1,0:T(8,128)(2,1)S(1)}, u32[]{:S(2)}, u32[]{:S(2)}) %collective-permute-start.6) | collective-permute-done | bytes 69664 | tf_op jit(solution)/shard_map/ppermute | solution.py:465
  22.6 0.7 %collective-permute-done.7.refs_1_ = bf16[272,128]{1,0:T(8,128)(2,1)S(1)} collective-permute-done((bf16[272,128]{1,0:T(8,128)(2,1)S(1)}, bf16[272,128]{1,0:T(8,128)(2,1)S(1)}, u32[]{:S(2)}, u32[]{:S(2)}) %collective-permute-start.7) | collective-permute-done | bytes 69664 | tf_op jit(solution)/shard_map/ppermute | solution.py:465
  23.3 2.1 %collective-permute-done.8.refs_2_ = bf16[272,128]{1,0:T(8,128)(2,1)S(1)} collective-permute-done((bf16[272,128]{1,0:T(8,128)(2,1)S(1)}, bf16[272,128]{1,0:T(8,128)(2,1)S(1)}, u32[]{:S(2)}, u32[]{:S(2)}) %collective-permute-start.8) | collective-permute-done | bytes 69664 | tf_op jit(solution)/shard_map/ppermute | solution.py:465
  25.4 2.9 %collective-permute-start.11 = (bf16[272,128]{1,0:T(8,128)(2,1)S(1)}, bf16[272,128]{1,0:T(8,128)(2,1)S(1)}, u32[]{:S(2)}, u32[]{:S(2)}) collective-permute-start(bf16[272,128]{1,0:T(8,128)(2,1)S(1)} %shard_map.76.a_ref), channel_id=1, source_target_pairs={{0,12},{4,8},{8,4},{12,0},{1,13},{5,9},{9,5},{13,1},{2,14},{6,10},... | collective-permute-start | bytes 208904 | tf_op jit(solution)/shard_map/ppermute | solution.py:473
  28.7 1.2 %collective-permute-start.9 = (bf16[272,128]{1,0:T(8,128)(2,1)S(1)}, bf16[272,128]{1,0:T(8,128)(2,1)S(1)}, u32[]{:S(2)}, u32[]{:S(2)}) collective-permute-start(bf16[272,128]{1,0:T(8,128)(2,1)S(1)} %shard_map.76.a_ref), channel_id=1, source_target_pairs={{0,4},{4,0},{8,12},{12,8},{1,5},{5,1},{9,13},{13,9},{2,6},{6,2},{1... | collective-permute-start | bytes 208904 | tf_op jit(solution)/shard_map/ppermute | solution.py:473
  29.9 2.5 %shard_map.73 = (bf16[128,2,8,128]{3,2,1,0:T(8,128)(2,1)}, f32[8,128]{1,0:T(8,128)S(1)}) custom-call(bf16[4,64,1280]{2,1,0:T(8,128)(2,1)S(1)} %get-tuple-element.41.hidden_ref, bf16[27,64,128]{2,1,0:T(8,128)(2,1)S(1)} %bitcast.9), custom_call_target="tpu_custom_call" | custom-call | flops 900000000 | bytes 1626112 | tf_op jit(solution)/shard_map/pallas_call | solution.py:18
  32.4 1.6 %collective-permute-done.10.c_ref = bf16[272,128]{1,0:T(8,128)(2,1)S(1)} collective-permute-done((bf16[272,128]{1,0:T(8,128)(2,1)S(1)}, bf16[272,128]{1,0:T(8,128)(2,1)S(1)}, u32[]{:S(2)}, u32[]{:S(2)}) %collective-permute-start.10) | collective-permute-done | bytes 69664 | tf_op jit(solution)/shard_map/ppermute | solution.py:473
  34.1 1.2 %collective-permute-start.13 = (bf16[288,128]{1,0:T(8,128)(2,1)S(1)}, bf16[288,128]{1,0:T(8,128)(2,1)S(1)}, u32[]{:S(2)}, u32[]{:S(2)}) collective-permute-start(bf16[288,128]{1,0:T(8,128)(2,1)S(1)} %get-tuple-element.53), channel_id=1, source_target_pairs={{0,2},{2,0},{1,3},{3,1},{4,6},{6,4},{5,7},{7,5},{8,10},{10,8},{9,1... | collective-permute-start | bytes 221192 | tf_op jit(solution)/shard_map/ppermute | solution.py:473
  35.2 1.0 %collective-permute-start.14 = (bf16[272,128]{1,0:T(8,128)(2,1)S(1)}, bf16[272,128]{1,0:T(8,128)(2,1)S(1)}, u32[]{:S(2)}, u32[]{:S(2)}) collective-permute-start(bf16[272,128]{1,0:T(8,128)(2,1)S(1)} %get-tuple-element.54.refs_0_), channel_id=1, source_target_pairs={{0,1},{1,0},{2,3},{3,2},{4,5},{5,4},{6,7},{7,6},{8,9},{9,8},{10,11... | collective-permute-start | bytes 208904 | tf_op jit(solution)/shard_map/ppermute | solution.py:473
  36.3 0.9 %collective-permute-done.14.refs_1_ = bf16[272,128]{1,0:T(8,128)(2,1)S(1)} collective-permute-done((bf16[272,128]{1,0:T(8,128)(2,1)S(1)}, bf16[272,128]{1,0:T(8,128)(2,1)S(1)}, u32[]{:S(2)}, u32[]{:S(2)}) %collective-permute-start.14) | collective-permute-done | bytes 69664 | tf_op jit(solution)/shard_map/ppermute | solution.py:473
  37.2 1.0 %shard_map.78 = (f32[9,3,32,32]{3,2,1,0:T(8,128)}, f32[3,9,64,64]{3,2,1,0:T(8,128)}) custom-call(bf16[272,128]{1,0:T(8,128)(2,1)S(1)} %get-tuple-element.54.refs_0_, bf16[272,128]{1,0:T(8,128)(2,1)S(1)} %collective-permute-done.14.refs_1_), custom_call_target="tpu_custom_call" | custom-call | bytes 692224 | tf_op jit(solution)/shard_map/pallas_call | solution.py:18
  38.8 0.9 %collective-permute-done.12.refs_0_ = bf16[288,128]{1,0:T(8,128)(2,1)S(1)} collective-permute-done((bf16[288,128]{1,0:T(8,128)(2,1)S(1)}, bf16[288,128]{1,0:T(8,128)(2,1)S(1)}, u32[]{:S(2)}, u32[]{:S(2)}) %collective-permute-start.12) | collective-permute-done | bytes 73760 | tf_op jit(solution)/shard_map/ppermute | solution.py:473
  39.7 1.0 %shard_map.79 = (f32[9,3,32,32]{3,2,1,0:T(8,128)}, f32[3,9,64,64]{3,2,1,0:T(8,128)}) custom-call(bf16[288,128]{1,0:T(8,128)(2,1)S(1)} %collective-permute-done.12.refs_0_, bf16[288,128]{1,0:T(8,128)(2,1)S(1)} %collective-permute-done.13.refs_1_, f32[9,3,32,32]{3,2,1,0:T(8,128)} %get-tuple-element.55.refs_2_, ...), custom_call_target="tpu_custom_call", output_to_operand_aliasing={{0}: (2, {}), {1}: (3, {})} | custom-call | bytes 1253376 | tf_op jit(solution)/shard_map/pallas_call | solution.py:18
  (27 shorter events, 3.7 us)
Async XLA Ops:
  0.6 4.7 %copy-start = (bf16[1,128,2,8,128]{4,3,2,1,0:T(8,128)(2,1)S(1)}, bf16[1,128,2,8,128]{4,3,2,1,0:T(8,128)(2,1)}, u32[]{:S(2)}) copy-start(bf16[1,128,2,8,128]{4,3,2,1,0:T(8,128)(2,1)} %param.7) | copy-start | bytes 1572868
  0.6 4.7 %copy-start.1 = (bf16[27,128,64]{1,2,0:T(8,128)(2,1)S(1)}, bf16[27,128,64]{1,2,0:T(8,128)(2,1)}, u32[]{:S(2)}) copy-start(bf16[27,128,64]{1,2,0:T(8,128)(2,1)} %param.6) | copy-start | bytes 1327108
  0.7 7.0 %collective-permute-start.1 = (bf16[32,2,8,128]{3,2,1,0:T(8,128)(2,1)}, bf16[32,2,8,128]{3,2,1,0:T(8,128)(2,1)S(1)}, u32[]{:S(2)}, u32[]{:S(2)}) collective-permute-start(bf16[32,2,8,128]{3,2,1,0:T(8,128)(2,1)} %bitcast.11), channel_id=1, source_target_pairs={{0,16},{4,8},{8,4},{12,28},{16,0},{20,24},{24,20},{28,12},{1,17},{... | collective-permute-start | bytes 393224 | tf_op jit(solution)/shard_map/ppermute | solution.py:454
  3.7 5.2 %collective-permute-start = (bf16[32,2,8,128]{3,2,1,0:T(8,128)(2,1)}, bf16[32,2,8,128]{3,2,1,0:T(8,128)(2,1)S(1)}, u32[]{:S(2)}, u32[]{:S(2)}) collective-permute-start(bf16[32,2,8,128]{3,2,1,0:T(8,128)(2,1)} %bitcast.12), channel_id=1, source_target_pairs={{0,4},{4,0},{8,12},{12,8},{16,20},{20,16},{24,28},{28,24},{1,5},{5... | collective-permute-start | bytes 393224 | tf_op jit(solution)/shard_map/ppermute | solution.py:454
  5.3 1.8 %copy-start.2 = (bf16[27,64,32]{1,2,0:T(8,128)(2,1)S(1)}, bf16[27,64,32]{1,2,0:T(8,128)(2,1)}, u32[]{:S(2)}) copy-start(bf16[27,64,32]{1,2,0:T(8,128)(2,1)} %param.5) | copy-start | bytes 331780
  5.3 1.8 %copy-start.3 = (bf16[1,32,2,8,128]{4,3,2,1,0:T(8,128)(2,1)S(1)}, bf16[1,32,2,8,128]{4,3,2,1,0:T(8,128)(2,1)}, u32[]{:S(2)}) copy-start(bf16[1,32,2,8,128]{4,3,2,1,0:T(8,128)(2,1)} %param.4) | copy-start | bytes 393220
  9.1 4.7 %collective-permute-start.2 = (bf16[6,32,256]{2,1,0:T(8,128)(2,1)S(1)}, bf16[6,32,256]{2,1,0:T(8,128)(2,1)S(1)}, u32[]{:S(2)}, u32[]{:S(2)}) collective-permute-start(bf16[6,32,256]{2,1,0:T(8,128)(2,1)S(1)} %get-tuple-element.34), channel_id=1, source_target_pairs={{0,16},{1,2},{2,1},{3,19},{16,0},{17,18},{18,17},{19,3},{4,20},{5,... | collective-permute-start | bytes 294920 | tf_op jit(solution)/shard_map/ppermute | solution.py:454
  10.6 3.2 %collective-permute-start.3 = (bf16[6,32,256]{2,1,0:T(8,128)(2,1)S(1)}, bf16[6,32,256]{2,1,0:T(8,128)(2,1)S(1)}, u32[]{:S(2)}, u32[]{:S(2)}) collective-permute-start(bf16[6,32,256]{2,1,0:T(8,128)(2,1)S(1)} %get-tuple-element.35), channel_id=1, source_target_pairs={{0,1},{1,0},{2,3},{3,2},{16,17},{17,16},{18,19},{19,18},{4,5},{5,4... | collective-permute-start | bytes 294920 | tf_op jit(solution)/shard_map/ppermute | solution.py:454
  15.9 1.7 %collective-permute-start.4 = (bf16[2,2,224,128]{3,2,1,0:T(8,128)(2,1)S(1)}, bf16[2,2,224,128]{3,2,1,0:T(8,128)(2,1)S(1)}, u32[]{:S(2)}, u32[]{:S(2)}) collective-permute-start(bf16[2,2,224,128]{3,2,1,0:T(8,128)(2,1)S(1)} %get-tuple-element.45), channel_id=1, source_target_pairs={{0,1},{1,0},{2,3},{3,2},{4,5},{5,4},{6,7},{7,6},{8,9},{9,8},{10,11... | collective-permute-start | bytes 688136 | tf_op jit(solution)/shard_map/ppermute | solution.py:473
  16.0 1.7 %collective-permute-start.5 = (f32[2,2,64,128]{3,2,1,0:T(8,128)S(1)}, f32[2,2,64,128]{3,2,1,0:T(8,128)S(1)}, u32[]{:S(2)}, u32[]{:S(2)}) collective-permute-start(f32[2,2,64,128]{3,2,1,0:T(8,128)S(1)} %get-tuple-element.47), channel_id=1, source_target_pairs={{0,1},{1,0},{2,3},{3,2},{4,5},{5,4},{6,7},{7,6},{8,9},{9,8},{10,11... | collective-permute-start | bytes 393224 | tf_op jit(solution)/shard_map/ppermute | solution.py:473
  17.7 4.8 %collective-permute-start.6 = (bf16[272,128]{1,0:T(8,128)(2,1)S(1)}, bf16[272,128]{1,0:T(8,128)(2,1)S(1)}, u32[]{:S(2)}, u32[]{:S(2)}) collective-permute-start(bf16[272,128]{1,0:T(8,128)(2,1)S(1)} %get-tuple-element.49), channel_id=1, source_target_pairs={{0,2},{1,17},{2,0},{3,19},{16,18},{17,1},{18,16},{19,3},{4,6},{5,2... | collective-permute-start | bytes 208904 | tf_op jit(solution)/shard_map/ppermute | solution.py:465
  18.8 4.5 %collective-permute-start.7 = (bf16[272,128]{1,0:T(8,128)(2,1)S(1)}, bf16[272,128]{1,0:T(8,128)(2,1)S(1)}, u32[]{:S(2)}, u32[]{:S(2)}) collective-permute-start(bf16[272,128]{1,0:T(8,128)(2,1)S(1)} %get-tuple-element.50), channel_id=1, source_target_pairs={{0,16},{1,3},{2,18},{3,1},{16,0},{17,19},{18,2},{19,17},{4,20},{5,... | collective-permute-start | bytes 208904 | tf_op jit(solution)/shard_map/ppermute | solution.py:465
  20.2 5.2 %collective-permute-start.8 = (bf16[272,128]{1,0:T(8,128)(2,1)S(1)}, bf16[272,128]{1,0:T(8,128)(2,1)S(1)}, u32[]{:S(2)}, u32[]{:S(2)}) collective-permute-start(bf16[272,128]{1,0:T(8,128)(2,1)S(1)} %get-tuple-element.51), channel_id=1, source_target_pairs={{0,18},{1,19},{2,16},{3,17},{16,2},{17,3},{18,0},{19,1},{4,22},{5,... | collective-permute-start | bytes 208904 | tf_op jit(solution)/shard_map/ppermute | solution.py:465
  25.4 7.0 %collective-permute-start.11 = (bf16[272,128]{1,0:T(8,128)(2,1)S(1)}, bf16[272,128]{1,0:T(8,128)(2,1)S(1)}, u32[]{:S(2)}, u32[]{:S(2)}) collective-permute-start(bf16[272,128]{1,0:T(8,128)(2,1)S(1)} %shard_map.76.a_ref), channel_id=1, source_target_pairs={{0,12},{4,8},{8,4},{12,0},{1,13},{5,9},{9,5},{13,1},{2,14},{6,10},... | collective-permute-start | bytes 208904 | tf_op jit(solution)/shard_map/ppermute | solution.py:473
  28.4 5.6 %collective-permute-start.10 = (bf16[272,128]{1,0:T(8,128)(2,1)S(1)}, bf16[272,128]{1,0:T(8,128)(2,1)S(1)}, u32[]{:S(2)}, u32[]{:S(2)}) collective-permute-start(bf16[272,128]{1,0:T(8,128)(2,1)S(1)} %shard_map.76.a_ref), channel_id=1, source_target_pairs={{0,8},{4,12},{8,0},{12,4},{1,9},{5,13},{9,1},{13,5},{2,10},{6,14},... | collective-permute-start | bytes 208904 | tf_op jit(solution)/shard_map/ppermute | solution.py:473
  28.7 5.3 %collective-permute-start.9 = (bf16[272,128]{1,0:T(8,128)(2,1)S(1)}, bf16[272,128]{1,0:T(8,128)(2,1)S(1)}, u32[]{:S(2)}, u32[]{:S(2)}) collective-permute-start(bf16[272,128]{1,0:T(8,128)(2,1)S(1)} %shard_map.76.a_ref), channel_id=1, source_target_pairs={{0,4},{4,0},{8,12},{12,8},{1,5},{5,1},{9,13},{13,9},{2,6},{6,2},{1... | collective-permute-start | bytes 208904 | tf_op jit(solution)/shard_map/ppermute | solution.py:473
  34.1 4.7 %collective-permute-start.13 = (bf16[288,128]{1,0:T(8,128)(2,1)S(1)}, bf16[288,128]{1,0:T(8,128)(2,1)S(1)}, u32[]{:S(2)}, u32[]{:S(2)}) collective-permute-start(bf16[288,128]{1,0:T(8,128)(2,1)S(1)} %get-tuple-element.53), channel_id=1, source_target_pairs={{0,2},{2,0},{1,3},{3,1},{4,6},{6,4},{5,7},{7,5},{8,10},{10,8},{9,1... | collective-permute-start | bytes 221192 | tf_op jit(solution)/shard_map/ppermute | solution.py:473
  35.2 4.5 %collective-permute-start.12 = (bf16[288,128]{1,0:T(8,128)(2,1)S(1)}, bf16[288,128]{1,0:T(8,128)(2,1)S(1)}, u32[]{:S(2)}, u32[]{:S(2)}) collective-permute-start(bf16[288,128]{1,0:T(8,128)(2,1)S(1)} %get-tuple-element.53), channel_id=1, source_target_pairs={{0,3},{1,2},{2,1},{3,0},{4,7},{5,6},{6,5},{7,4},{8,11},{9,10},{10,... | collective-permute-start | bytes 221192 | tf_op jit(solution)/shard_map/ppermute | solution.py:473
  35.2 1.9 %collective-permute-start.14 = (bf16[272,128]{1,0:T(8,128)(2,1)S(1)}, bf16[272,128]{1,0:T(8,128)(2,1)S(1)}, u32[]{:S(2)}, u32[]{:S(2)}) collective-permute-start(bf16[272,128]{1,0:T(8,128)(2,1)S(1)} %get-tuple-element.54.refs_0_), channel_id=1, source_target_pairs={{0,1},{1,0},{2,3},{3,2},{4,5},{5,4},{6,7},{7,6},{8,9},{9,8},{10,11... | collective-permute-start | bytes 208904 | tf_op jit(solution)/shard_map/ppermute | solution.py:473

commit v26 on v21

--- a/solution.py
+++ b/solution.py
@@ -595,7 +595,7 @@
         [pltpu.VMEM(((out + 1) * rows, width), F32)],
         flops=900_000_000,
     )
-    gots = [across(share, ("dep", bits)) for bits in (1, 2, 3)]
+    gots = [across(share, ("dep", bits)) for bits in (1, 3, 2)]
     share, for_y = call(depth_kernel, [shape(block, BF), shape((block[0] + 16, width), BF)], [share, *gots, token])
     other, far = across(share, ("core", 1)), across(for_y, ("y", 1))
     far_other = across(for_y, ("y", 1), ("core", 1))

time: 40.7 us -> 40.8 us (level)
  waiting for transfers between devices: 10.7 us -> 11.2 us
    ppermute x11, waiting for transfers between devices: 9.14 us -> 9.61 us  [across(): lax.ppermute(x, axes, [(i, i ^ flip) for i in range(lax.axis_size(axes))])]
  transfers between devices with their start and end apart: 15 -> 15, of which waited for: 10 -> 12; matrix products, arithmetic and copies ran while one was open for 0% -> 0% of each run, Pallas kernels for 21% -> 20%
where the time goes in v26:
time: 40.8 us; the launch traced here: 40.7 us
  starting transfers between devices  16.8 us (41%)
  Pallas kernels  11.9 us (29%)
  waiting for transfers between devices  11.2 us (27%)
  between operations  0.78 us (2%)
    pallas_call x13, Pallas kernels, call(): pl.pallas_call(body, out_shape=outs, in_specs=[pl.BlockSpec(memory_space=...  11.9 us
    ppermute x11, starting transfers between devices, across(): lax.ppermute(x, axes, [(i, i ^ flip) for i in range(lax.axis_size(axes))])  10.5 us
    ppermute x11, waiting for transfers between devices, across(): lax.ppermute(x, axes, [(i, i ^ flip) for i in range(lax.axis_size(axes))])  9.61 us
    ppermute x4, starting transfers between devices, swapped(): return lax.ppermute(x, ('dp', *axes), list(enumerate(partner)))  6.36 us
    ppermute x4, waiting for transfers between devices, swapped(): return lax.ppermute(x, ('dp', *axes), list(enumerate(partner)))  1.58 us
  transfers between devices with their start and end apart: 15, of which 12 were waited for; matrix products, arithmetic and copies ran while one was open for 0% of the time, Pallas kernels for 20%

profile of v26, /device:TPU:0, one launch (start us, length us, event | category | flops | bytes accessed | tf_op | source)
XLA Modules:
  0.0 40.7 jit_solution(7230335467942973204)
XLA Ops:
  0.7 3.0 %collective-permute-start.1 = (bf16[32,2,8,128]{3,2,1,0:T(8,128)(2,1)}, bf16[32,2,8,128]{3,2,1,0:T(8,128)(2,1)S(1)}, u32[]{:S(2)}, u32[]{:S(2)}) collective-permute-start(bf16[32,2,8,128]{3,2,1,0:T(8,128)(2,1)} %bitcast.11), channel_id=1, source_target_pairs={{0,16},{4,8},{8,4},{12,28},{16,0},{20,24},{24,20},{28,12},{1,17},{... | collective-permute-start | bytes 393224 | tf_op jit(solution)/shard_map/ppermute | solution.py:453
  3.7 1.7 %collective-permute-start = (bf16[32,2,8,128]{3,2,1,0:T(8,128)(2,1)}, bf16[32,2,8,128]{3,2,1,0:T(8,128)(2,1)S(1)}, u32[]{:S(2)}, u32[]{:S(2)}) collective-permute-start(bf16[32,2,8,128]{3,2,1,0:T(8,128)(2,1)} %bitcast.12), channel_id=1, source_target_pairs={{0,4},{4,0},{8,12},{12,8},{16,20},{20,16},{24,28},{28,24},{1,5},{5... | collective-permute-start | bytes 393224 | tf_op jit(solution)/shard_map/ppermute | solution.py:453
  5.4 1.7 %shard_map.68 = (bf16[2,128,1024]{2,1,0:T(8,128)(2,1)S(1)}, f32[4,64,1280]{2,1,0:T(8,128)S(1)}) custom-call(bf16[128,2,8,128]{3,2,1,0:T(8,128)(2,1)S(1)} %bitcast.7, bf16[27,64,128]{2,1,0:T(8,128)(2,1)S(1)} %bitcast.8, bf16[128,256]{1,0:T(8,128)(2,1)S(1)} %shard_map.67.blank_ref), custom_call_target="tpu_custom_call" | custom-call | flops 1100000000 | bytes 2867200 | tf_op jit(solution)/shard_map/pallas_call | solution.py:18
  7.6 1.2 %collective-permute-done.one_ref = bf16[32,2,8,128]{3,2,1,0:T(8,128)(2,1)S(1)} collective-permute-done((bf16[32,2,8,128]{3,2,1,0:T(8,128)(2,1)}, bf16[32,2,8,128]{3,2,1,0:T(8,128)(2,1)S(1)}, u32[]{:S(2)}, u32[]{:S(2)}) %collective-permute-start) | collective-permute-done | bytes 131104 | tf_op jit(solution)/shard_map/ppermute | solution.py:453
  9.1 1.5 %collective-permute-start.2 = (bf16[6,32,256]{2,1,0:T(8,128)(2,1)S(1)}, bf16[6,32,256]{2,1,0:T(8,128)(2,1)S(1)}, u32[]{:S(2)}, u32[]{:S(2)}) collective-permute-start(bf16[6,32,256]{2,1,0:T(8,128)(2,1)S(1)} %get-tuple-element.34), channel_id=1, source_target_pairs={{0,16},{1,2},{2,1},{3,19},{16,0},{17,18},{18,17},{19,3},{4,20},{5,... | collective-permute-start | bytes 294920 | tf_op jit(solution)/shard_map/ppermute | solution.py:453
  10.8 2.6 %shard_map.71 = (bf16[4,64,768]{2,1,0:T(8,128)(2,1)S(1)}, f32[1152,192]{1,0:T(8,128)S(1)}, f32[192,288]{1,0:T(8,128)S(1)}) custom-call(bf16[6,32,1024]{2,1,0:T(8,128)(2,1)S(1)} %get-tuple-element.33.deep_ref, bf16[192,288]{1,0:T(8,128)(2,1)S(1)} %get-tuple-element.36.w1_ref, bf16[2,384,1024]{2,1,0:T(8,128)(2,1)S(1)} %get-tuple-element.38.moved_ref, ...), custom_call_target="tpu_custom_call" | custom-call | flops 1500000000 | bytes 4886528 | tf_op jit(solution)/shard_map/pallas_call | solution.py:18
  13.8 1.5 %shard_map.72 = (bf16[4,64,1280]{2,1,0:T(8,128)(2,1)S(1)}, f32[2,2,64,128]{3,2,1,0:T(8,128)S(1)}, f32[2,2,64,128]{3,2,1,0:T(8,128)S(1)}) custom-call(bf16[6,32,1024]{2,1,0:T(8,128)(2,1)S(1)} %get-tuple-element.33.deep_ref, bf16[6,32,256]{2,1,0:T(8,128)(2,1)S(1)} %collective-permute-done.2.two_ref, bf16[6,32,256]{2,1,0:T(8,128)(2,1)S(1)} %collective-permute-done.3.one_ref, ...), custom_call_target="tpu_custom_call" | custom-call | flops 1000000000 | bytes 3543040 | tf_op jit(solution)/shard_map/pallas_call | solution.py:18
  16.5 1.2 %collective-permute-done.5.refs_3_ = f32[2,2,64,128]{3,2,1,0:T(8,128)S(1)} collective-permute-done((f32[2,2,64,128]{3,2,1,0:T(8,128)S(1)}, f32[2,2,64,128]{3,2,1,0:T(8,128)S(1)}, u32[]{:S(2)}, u32[]{:S(2)}) %collective-permute-start.5) | collective-permute-done | bytes 131104 | tf_op jit(solution)/shard_map/ppermute | solution.py:461
  17.7 1.5 %collective-permute-start.6 = (bf16[272,128]{1,0:T(8,128)(2,1)S(1)}, bf16[272,128]{1,0:T(8,128)(2,1)S(1)}, u32[]{:S(2)}, u32[]{:S(2)}) collective-permute-start(bf16[272,128]{1,0:T(8,128)(2,1)S(1)} %get-tuple-element.49), channel_id=1, source_target_pairs={{0,16},{2,18},{16,0},{18,2},{1,17},{3,19},{17,1},{19,3},{4,20},{6,... | collective-permute-start | bytes 208904 | tf_op jit(solution)/shard_map/ppermute | solution.py:461
  19.2 0.9 %collective-permute-start.7 = (bf16[272,128]{1,0:T(8,128)(2,1)S(1)}, bf16[272,128]{1,0:T(8,128)(2,1)S(1)}, u32[]{:S(2)}, u32[]{:S(2)}) collective-permute-start(bf16[272,128]{1,0:T(8,128)(2,1)S(1)} %get-tuple-element.50), channel_id=1, source_target_pairs={{0,2},{2,0},{16,18},{18,16},{1,3},{3,1},{17,19},{19,17},{4,6},{6,4... | collective-permute-start | bytes 208904 | tf_op jit(solution)/shard_map/ppermute | solution.py:461
  20.2 1.1 %collective-permute-start.8 = (bf16[272,128]{1,0:T(8,128)(2,1)S(1)}, bf16[272,128]{1,0:T(8,128)(2,1)S(1)}, u32[]{:S(2)}, u32[]{:S(2)}) collective-permute-start(bf16[272,128]{1,0:T(8,128)(2,1)S(1)} %get-tuple-element.51), channel_id=1, source_target_pairs={{0,18},{2,16},{16,2},{18,0},{1,19},{3,17},{17,3},{19,1},{4,22},{6,... | collective-permute-start | bytes 208904 | tf_op jit(solution)/shard_map/ppermute | solution.py:461
  21.3 0.8 %collective-permute-done.6.refs_0_ = bf16[272,128]{1,0:T(8,128)(2,1)S(1)} collective-permute-done((bf16[272,128]{1,0:T(8,128)(2,1)S(1)}, bf16[272,128]{1,0:T(8,128)(2,1)S(1)}, u32[]{:S(2)}, u32[]{:S(2)}) %collective-permute-start.6) | collective-permute-done | bytes 69664 | tf_op jit(solution)/shard_map/ppermute | solution.py:461
  22.1 2.2 %collective-permute-done.7.refs_1_ = bf16[272,128]{1,0:T(8,128)(2,1)S(1)} collective-permute-done((bf16[272,128]{1,0:T(8,128)(2,1)S(1)}, bf16[272,128]{1,0:T(8,128)(2,1)S(1)}, u32[]{:S(2)}, u32[]{:S(2)}) %collective-permute-start.7) | collective-permute-done | bytes 69664 | tf_op jit(solution)/shard_map/ppermute | solution.py:461
  24.3 1.1 %collective-permute-done.8.refs_2_ = bf16[272,128]{1,0:T(8,128)(2,1)S(1)} collective-permute-done((bf16[272,128]{1,0:T(8,128)(2,1)S(1)}, bf16[272,128]{1,0:T(8,128)(2,1)S(1)}, u32[]{:S(2)}, u32[]{:S(2)}) %collective-permute-start.8) | collective-permute-done | bytes 69664 | tf_op jit(solution)/shard_map/ppermute | solution.py:461
  25.4 1.7 %collective-permute-start.11 = (bf16[272,128]{1,0:T(8,128)(2,1)S(1)}, bf16[272,128]{1,0:T(8,128)(2,1)S(1)}, u32[]{:S(2)}, u32[]{:S(2)}) collective-permute-start(bf16[272,128]{1,0:T(8,128)(2,1)S(1)} %shard_map.76.a_ref), channel_id=1, source_target_pairs={{0,8},{4,12},{8,0},{12,4},{1,9},{5,13},{9,1},{13,5},{2,10},{6,14},... | collective-permute-start | bytes 208904 | tf_op jit(solution)/shard_map/ppermute | solution.py:461
  27.1 2.5 %collective-permute-start.10 = (bf16[272,128]{1,0:T(8,128)(2,1)S(1)}, bf16[272,128]{1,0:T(8,128)(2,1)S(1)}, u32[]{:S(2)}, u32[]{:S(2)}) collective-permute-start(bf16[272,128]{1,0:T(8,128)(2,1)S(1)} %shard_map.76.a_ref), channel_id=1, source_target_pairs={{0,12},{4,8},{8,4},{12,0},{1,13},{5,9},{9,5},{13,1},{2,14},{6,10},... | collective-permute-start | bytes 208904 | tf_op jit(solution)/shard_map/ppermute | solution.py:461
  29.6 2.5 %shard_map.73 = (bf16[128,2,8,128]{3,2,1,0:T(8,128)(2,1)}, f32[8,128]{1,0:T(8,128)S(1)}) custom-call(bf16[4,64,1280]{2,1,0:T(8,128)(2,1)S(1)} %get-tuple-element.41.hidden_ref, bf16[27,64,128]{2,1,0:T(8,128)(2,1)S(1)} %bitcast.9), custom_call_target="tpu_custom_call" | custom-call | flops 900000000 | bytes 1626112 | tf_op jit(solution)/shard_map/pallas_call | solution.py:18
  32.5 0.8 %collective-permute-done.10.c_ref = bf16[272,128]{1,0:T(8,128)(2,1)S(1)} collective-permute-done((bf16[272,128]{1,0:T(8,128)(2,1)S(1)}, bf16[272,128]{1,0:T(8,128)(2,1)S(1)}, u32[]{:S(2)}, u32[]{:S(2)}) %collective-permute-start.10) | collective-permute-done | bytes 69664 | tf_op jit(solution)/shard_map/ppermute | solution.py:461
  34.1 1.1 %collective-permute-start.13 = (bf16[288,128]{1,0:T(8,128)(2,1)S(1)}, bf16[288,128]{1,0:T(8,128)(2,1)S(1)}, u32[]{:S(2)}, u32[]{:S(2)}) collective-permute-start(bf16[288,128]{1,0:T(8,128)(2,1)S(1)} %get-tuple-element.53), channel_id=1, source_target_pairs={{0,2},{2,0},{1,3},{3,1},{4,6},{6,4},{5,7},{7,5},{8,10},{10,8},{9,1... | collective-permute-start | bytes 221192 | tf_op jit(solution)/shard_map/ppermute | solution.py:461
  35.2 1.1 %collective-permute-start.14 = (bf16[272,128]{1,0:T(8,128)(2,1)S(1)}, bf16[272,128]{1,0:T(8,128)(2,1)S(1)}, u32[]{:S(2)}, u32[]{:S(2)}) collective-permute-start(bf16[272,128]{1,0:T(8,128)(2,1)S(1)} %get-tuple-element.54.refs_0_), channel_id=1, source_target_pairs={{0,1},{1,0},{2,3},{3,2},{4,5},{5,4},{6,7},{7,6},{8,9},{9,8},{10,11... | collective-permute-start | bytes 208904 | tf_op jit(solution)/shard_map/ppermute | solution.py:461
  36.3 0.9 %collective-permute-done.14.refs_1_ = bf16[272,128]{1,0:T(8,128)(2,1)S(1)} collective-permute-done((bf16[272,128]{1,0:T(8,128)(2,1)S(1)}, bf16[272,128]{1,0:T(8,128)(2,1)S(1)}, u32[]{:S(2)}, u32[]{:S(2)}) %collective-permute-start.14) | collective-permute-done | bytes 69664 | tf_op jit(solution)/shard_map/ppermute | solution.py:461
  37.2 1.0 %shard_map.78 = (f32[9,3,32,32]{3,2,1,0:T(8,128)}, f32[3,9,64,64]{3,2,1,0:T(8,128)}) custom-call(bf16[272,128]{1,0:T(8,128)(2,1)S(1)} %get-tuple-element.54.refs_0_, bf16[272,128]{1,0:T(8,128)(2,1)S(1)} %collective-permute-done.14.refs_1_), custom_call_target="tpu_custom_call" | custom-call | bytes 692224 | tf_op jit(solution)/shard_map/pallas_call | solution.py:18
  38.8 0.9 %collective-permute-done.12.refs_0_ = bf16[288,128]{1,0:T(8,128)(2,1)S(1)} collective-permute-done((bf16[288,128]{1,0:T(8,128)(2,1)S(1)}, bf16[288,128]{1,0:T(8,128)(2,1)S(1)}, u32[]{:S(2)}, u32[]{:S(2)}) %collective-permute-start.12) | collective-permute-done | bytes 73760 | tf_op jit(solution)/shard_map/ppermute | solution.py:461
  39.7 1.0 %shard_map.79 = (f32[9,3,32,32]{3,2,1,0:T(8,128)}, f32[3,9,64,64]{3,2,1,0:T(8,128)}) custom-call(bf16[288,128]{1,0:T(8,128)(2,1)S(1)} %collective-permute-done.12.refs_0_, bf16[288,128]{1,0:T(8,128)(2,1)S(1)} %collective-permute-done.13.refs_1_, f32[9,3,32,32]{3,2,1,0:T(8,128)} %get-tuple-element.55.refs_2_, ...), custom_call_target="tpu_custom_call", output_to_operand_aliasing={{0}: (2, {}), {1}: (3, {})} | custom-call | bytes 1253376 | tf_op jit(solution)/shard_map/pallas_call | solution.py:18
  (27 shorter events, 4.5 us)
Async XLA Ops:
  0.6 4.7 %copy-start = (bf16[1,128,2,8,128]{4,3,2,1,0:T(8,128)(2,1)S(1)}, bf16[1,128,2,8,128]{4,3,2,1,0:T(8,128)(2,1)}, u32[]{:S(2)}) copy-start(bf16[1,128,2,8,128]{4,3,2,1,0:T(8,128)(2,1)} %param.7) | copy-start | bytes 1572868
  0.6 4.7 %copy-start.1 = (bf16[27,128,64]{1,2,0:T(8,128)(2,1)S(1)}, bf16[27,128,64]{1,2,0:T(8,128)(2,1)}, u32[]{:S(2)}) copy-start(bf16[27,128,64]{1,2,0:T(8,128)(2,1)} %param.6) | copy-start | bytes 1327108
  0.7 7.0 %collective-permute-start.1 = (bf16[32,2,8,128]{3,2,1,0:T(8,128)(2,1)}, bf16[32,2,8,128]{3,2,1,0:T(8,128)(2,1)S(1)}, u32[]{:S(2)}, u32[]{:S(2)}) collective-permute-start(bf16[32,2,8,128]{3,2,1,0:T(8,128)(2,1)} %bitcast.11), channel_id=1, source_target_pairs={{0,16},{4,8},{8,4},{12,28},{16,0},{20,24},{24,20},{28,12},{1,17},{... | collective-permute-start | bytes 393224 | tf_op jit(solution)/shard_map/ppermute | solution.py:453
  3.7 5.2 %collective-permute-start = (bf16[32,2,8,128]{3,2,1,0:T(8,128)(2,1)}, bf16[32,2,8,128]{3,2,1,0:T(8,128)(2,1)S(1)}, u32[]{:S(2)}, u32[]{:S(2)}) collective-permute-start(bf16[32,2,8,128]{3,2,1,0:T(8,128)(2,1)} %bitcast.12), channel_id=1, source_target_pairs={{0,4},{4,0},{8,12},{12,8},{16,20},{20,16},{24,28},{28,24},{1,5},{5... | collective-permute-start | bytes 393224 | tf_op jit(solution)/shard_map/ppermute | solution.py:453
  5.3 1.8 %copy-start.2 = (bf16[27,64,32]{1,2,0:T(8,128)(2,1)S(1)}, bf16[27,64,32]{1,2,0:T(8,128)(2,1)}, u32[]{:S(2)}) copy-start(bf16[27,64,32]{1,2,0:T(8,128)(2,1)} %param.5) | copy-start | bytes 331780
  5.3 1.8 %copy-start.3 = (bf16[1,32,2,8,128]{4,3,2,1,0:T(8,128)(2,1)S(1)}, bf16[1,32,2,8,128]{4,3,2,1,0:T(8,128)(2,1)}, u32[]{:S(2)}) copy-start(bf16[1,32,2,8,128]{4,3,2,1,0:T(8,128)(2,1)} %param.4) | copy-start | bytes 393220
  9.1 4.7 %collective-permute-start.2 = (bf16[6,32,256]{2,1,0:T(8,128)(2,1)S(1)}, bf16[6,32,256]{2,1,0:T(8,128)(2,1)S(1)}, u32[]{:S(2)}, u32[]{:S(2)}) collective-permute-start(bf16[6,32,256]{2,1,0:T(8,128)(2,1)S(1)} %get-tuple-element.34), channel_id=1, source_target_pairs={{0,16},{1,2},{2,1},{3,19},{16,0},{17,18},{18,17},{19,3},{4,20},{5,... | collective-permute-start | bytes 294920 | tf_op jit(solution)/shard_map/ppermute | solution.py:453
  10.6 3.2 %collective-permute-start.3 = (bf16[6,32,256]{2,1,0:T(8,128)(2,1)S(1)}, bf16[6,32,256]{2,1,0:T(8,128)(2,1)S(1)}, u32[]{:S(2)}, u32[]{:S(2)}) collective-permute-start(bf16[6,32,256]{2,1,0:T(8,128)(2,1)S(1)} %get-tuple-element.35), channel_id=1, source_target_pairs={{0,1},{1,0},{2,3},{3,2},{16,17},{17,16},{18,19},{19,18},{4,5},{5,4... | collective-permute-start | bytes 294920 | tf_op jit(solution)/shard_map/ppermute | solution.py:453
  15.9 1.7 %collective-permute-start.4 = (bf16[2,2,224,128]{3,2,1,0:T(8,128)(2,1)S(1)}, bf16[2,2,224,128]{3,2,1,0:T(8,128)(2,1)S(1)}, u32[]{:S(2)}, u32[]{:S(2)}) collective-permute-start(bf16[2,2,224,128]{3,2,1,0:T(8,128)(2,1)S(1)} %get-tuple-element.45), channel_id=1, source_target_pairs={{0,1},{1,0},{2,3},{3,2},{4,5},{5,4},{6,7},{7,6},{8,9},{9,8},{10,11... | collective-permute-start | bytes 688136 | tf_op jit(solution)/shard_map/ppermute | solution.py:461
  16.0 1.7 %collective-permute-start.5 = (f32[2,2,64,128]{3,2,1,0:T(8,128)S(1)}, f32[2,2,64,128]{3,2,1,0:T(8,128)S(1)}, u32[]{:S(2)}, u32[]{:S(2)}) collective-permute-start(f32[2,2,64,128]{3,2,1,0:T(8,128)S(1)} %get-tuple-element.47), channel_id=1, source_target_pairs={{0,1},{1,0},{2,3},{3,2},{4,5},{5,4},{6,7},{7,6},{8,9},{9,8},{10,11... | collective-permute-start | bytes 393224 | tf_op jit(solution)/shard_map/ppermute | solution.py:461
  17.7 4.4 %collective-permute-start.6 = (bf16[272,128]{1,0:T(8,128)(2,1)S(1)}, bf16[272,128]{1,0:T(8,128)(2,1)S(1)}, u32[]{:S(2)}, u32[]{:S(2)}) collective-permute-start(bf16[272,128]{1,0:T(8,128)(2,1)S(1)} %get-tuple-element.49), channel_id=1, source_target_pairs={{0,16},{2,18},{16,0},{18,2},{1,17},{3,19},{17,1},{19,3},{4,20},{6,... | collective-permute-start | bytes 208904 | tf_op jit(solution)/shard_map/ppermute | solution.py:461
  19.2 5.1 %collective-permute-start.7 = (bf16[272,128]{1,0:T(8,128)(2,1)S(1)}, bf16[272,128]{1,0:T(8,128)(2,1)S(1)}, u32[]{:S(2)}, u32[]{:S(2)}) collective-permute-start(bf16[272,128]{1,0:T(8,128)(2,1)S(1)} %get-tuple-element.50), channel_id=1, source_target_pairs={{0,2},{2,0},{16,18},{18,16},{1,3},{3,1},{17,19},{19,17},{4,6},{6,4... | collective-permute-start | bytes 208904 | tf_op jit(solution)/shard_map/ppermute | solution.py:461
  20.2 5.2 %collective-permute-start.8 = (bf16[272,128]{1,0:T(8,128)(2,1)S(1)}, bf16[272,128]{1,0:T(8,128)(2,1)S(1)}, u32[]{:S(2)}, u32[]{:S(2)}) collective-permute-start(bf16[272,128]{1,0:T(8,128)(2,1)S(1)} %get-tuple-element.51), channel_id=1, source_target_pairs={{0,18},{2,16},{16,2},{18,0},{1,19},{3,17},{17,3},{19,1},{4,22},{6,... | collective-permute-start | bytes 208904 | tf_op jit(solution)/shard_map/ppermute | solution.py:461
  25.4 7.0 %collective-permute-start.11 = (bf16[272,128]{1,0:T(8,128)(2,1)S(1)}, bf16[272,128]{1,0:T(8,128)(2,1)S(1)}, u32[]{:S(2)}, u32[]{:S(2)}) collective-permute-start(bf16[272,128]{1,0:T(8,128)(2,1)S(1)} %shard_map.76.a_ref), channel_id=1, source_target_pairs={{0,8},{4,12},{8,0},{12,4},{1,9},{5,13},{9,1},{13,5},{2,10},{6,14},... | collective-permute-start | bytes 208904 | tf_op jit(solution)/shard_map/ppermute | solution.py:461
  27.1 6.2 %collective-permute-start.10 = (bf16[272,128]{1,0:T(8,128)(2,1)S(1)}, bf16[272,128]{1,0:T(8,128)(2,1)S(1)}, u32[]{:S(2)}, u32[]{:S(2)}) collective-permute-start(bf16[272,128]{1,0:T(8,128)(2,1)S(1)} %shard_map.76.a_ref), channel_id=1, source_target_pairs={{0,12},{4,8},{8,4},{12,0},{1,13},{5,9},{9,5},{13,1},{2,14},{6,10},... | collective-permute-start | bytes 208904 | tf_op jit(solution)/shard_map/ppermute | solution.py:461
  29.6 4.4 %collective-permute-start.9 = (bf16[272,128]{1,0:T(8,128)(2,1)S(1)}, bf16[272,128]{1,0:T(8,128)(2,1)S(1)}, u32[]{:S(2)}, u32[]{:S(2)}) collective-permute-start(bf16[272,128]{1,0:T(8,128)(2,1)S(1)} %shard_map.76.a_ref), channel_id=1, source_target_pairs={{0,4},{4,0},{8,12},{12,8},{1,5},{5,1},{9,13},{13,9},{2,6},{6,2},{1... | collective-permute-start | bytes 208904 | tf_op jit(solution)/shard_map/ppermute | solution.py:461
  34.1 4.8 %collective-permute-start.13 = (bf16[288,128]{1,0:T(8,128)(2,1)S(1)}, bf16[288,128]{1,0:T(8,128)(2,1)S(1)}, u32[]{:S(2)}, u32[]{:S(2)}) collective-permute-start(bf16[288,128]{1,0:T(8,128)(2,1)S(1)} %get-tuple-element.53), channel_id=1, source_target_pairs={{0,2},{2,0},{1,3},{3,1},{4,6},{6,4},{5,7},{7,5},{8,10},{10,8},{9,1... | collective-permute-start | bytes 221192 | tf_op jit(solution)/shard_map/ppermute | solution.py:461
  35.2 4.5 %collective-permute-start.12 = (bf16[288,128]{1,0:T(8,128)(2,1)S(1)}, bf16[288,128]{1,0:T(8,128)(2,1)S(1)}, u32[]{:S(2)}, u32[]{:S(2)}) collective-permute-start(bf16[288,128]{1,0:T(8,128)(2,1)S(1)} %get-tuple-element.53), channel_id=1, source_target_pairs={{0,3},{1,2},{2,1},{3,0},{4,7},{5,6},{6,5},{7,4},{8,11},{9,10},{10,... | collective-permute-start | bytes 221192 | tf_op jit(solution)/shard_map/ppermute | solution.py:461
  35.2 2.0 %collective-permute-start.14 = (bf16[272,128]{1,0:T(8,128)(2,1)S(1)}, bf16[272,128]{1,0:T(8,128)(2,1)S(1)}, u32[]{:S(2)}, u32[]{:S(2)}) collective-permute-start(bf16[272,128]{1,0:T(8,128)(2,1)S(1)} %get-tuple-element.54.refs_0_), channel_id=1, source_target_pairs={{0,1},{1,0},{2,3},{3,2},{4,5},{5,4},{6,7},{7,6},{8,9},{9,8},{10,11... | collective-permute-start | bytes 208904 | tf_op jit(solution)/shard_map/ppermute | solution.py:461
